TPU v7x, 32 devices: a whole 2x2x4 slice. The times are simulated.
32 devices in a mesh: groups: 2 (over y), replica: 16 (over z, x, core).
Axes of the slice: x: 2, y: 2, z: 4, core: 2. Of those that a mesh axis runs over, the one named last changes fastest.
Arguments:
- hidden_state_input: bfloat16 [32, 8192], P(('groups', 'replica')), parts along dimension 0, may hold values from -6 to 6
- attention_norm_scale: bfloat16 [8192], replicated, may hold values from 0.099609375 to 1.8984375
- query_weight: bfloat16 [8192, 8192], P(None, 'replica'), may hold values from -0.0625 to 0.0625
- key_value_weight: bfloat16 [8192, 2048], P(None, 'replica'), may hold values from -0.0625 to 0.0625
- output_weight: bfloat16 [8192, 8192], P('replica'), may hold values from -0.0625 to 0.0625
- adapter_down_weight: bfloat16 [32, 8192, 64], P('replica'), may hold values from -0.0625 to 0.0625
- adapter_up_weight: bfloat16 [32, 64, 8192], P(None, None, 'replica'), may hold values from -0.75 to 0.75
- row_adapter_index: int32 [32], P(('groups', 'replica')), parts along dimension 0, may hold values from 0 to 31
- adapter_storage_index: int32 [32], replicated, may hold values from 0 to 31, each once
- cache_length_per_row: int32 [32], P(('groups', 'replica')), parts along dimension 0, may hold values from 32 to 512, as said below
- key_value_cache: bfloat16 [32, 2, 512, 1024], P(('groups', 'replica')), parts along dimension 0
Outputs:
- layer_out: bfloat16 [2, 32, 8192], P(None, ('groups', 'replica')), parts along dimension 1
There are 2 independent parts, one for each index of `groups`. A program takes and returns all parts, laid end to end along the dimension named above; an argument that names none is the same for every part. Nothing has to cross between parts.
Inputs may be any that keep to these rules, and one draw needn't show every extreme that they name: `cache_length_per_row`: some row uses exactly 512 positions. `adapter_storage_index`: each storage index appears once.
All inputs are finite; a program needn't handle non-finite values.
Results may differ from a plain program's by a relative error of at most 0.033.
Values may be sent and summed in bfloat16 or wider, within the bound.
No kernel may reach another device: no remote copies, remote signals or barrier semaphores. Data moves between devices by JAX's collectives and lax.ppermute only.
A program may use at most 128 MiB of HBM per device.

v0:
```python
import math

import jax
import jax.numpy as jnp
from jax import lax
from jax.sharding import PartitionSpec as P

H = 64
KVH = 8
HD = 128
CACHE = 512
STEPS = 2
BLOCK = 16


def rms_normed(hidden, attention_norm_scale):
    widened = hidden.astype(jnp.float32)
    factor = lax.rsqrt(jnp.mean(widened * widened, axis=-1, keepdims=True) + 1e-05)
    return (widened * factor * attention_norm_scale.astype(jnp.float32)).astype(jnp.bfloat16)


def down_projected(gathered_row_inputs, gathered_storage_index, owner_offset, adapter_down_weight):
    total_row_count = gathered_row_inputs.shape[0]
    current_hidden = jnp.zeros((total_row_count, adapter_down_weight.shape[2]), jnp.float32)
    for kept_storage_index in range(adapter_down_weight.shape[0]):
        member = gathered_storage_index == owner_offset + kept_storage_index
        kept_down_weight = adapter_down_weight[kept_storage_index]
        member_count = jnp.sum(member.astype(jnp.int32))
        sorted_rows = jnp.argsort(jnp.where(member, 0, 1).astype(jnp.int32), stable=True)
        block_turns = (member_count + BLOCK - 1) // BLOCK

        def add_block(
            block_index,
            carried,
            sorted_rows=sorted_rows,
            member_count=member_count,
            kept_down_weight=kept_down_weight,
        ):
            first_row = block_index * BLOCK
            picked = lax.dynamic_slice_in_dim(sorted_rows, first_row, BLOCK)
            live_mask = first_row + jnp.arange(BLOCK, dtype=jnp.int32) < member_count
            block_part = jnp.dot(
                gathered_row_inputs[picked], kept_down_weight, preferred_element_type=jnp.float32
            )
            return carried.at[picked].add(jnp.where(live_mask[:, None], block_part, 0.0))

        current_hidden = lax.fori_loop(0, block_turns, add_block, current_hidden)
    return current_hidden


def attend(queries, key_value_cache, cache_length_per_row, recent_keys, recent_values):
    total_row_count = queries.shape[0]
    score_scale = 1.0 / math.sqrt(HD)
    grouped_q = queries.reshape(total_row_count, KVH, H // KVH, HD)
    cache_keys = key_value_cache[:, 0].reshape(total_row_count, CACHE, KVH, HD)
    cache_values = key_value_cache[:, 1].reshape(total_row_count, CACHE, KVH, HD)
    new_keys = recent_keys.reshape(total_row_count, -1, KVH, HD)
    new_values = recent_values.reshape(total_row_count, -1, KVH, HD)
    cached_scores = (
        jnp.einsum("rhgd,rchd->rhgc", grouped_q, cache_keys, preferred_element_type=jnp.float32)
        * score_scale
    )
    in_cache = jnp.arange(CACHE, dtype=jnp.int32)[None, :] < cache_length_per_row[:, None]
    cached_scores = jnp.where(in_cache[:, None, None, :], cached_scores, -jnp.inf)
    new_scores = (
        jnp.einsum("rhgd,rnhd->rhgn", grouped_q, new_keys, preferred_element_type=jnp.float32)
        * score_scale
    )
    scores = jnp.concatenate([cached_scores, new_scores], axis=-1)
    peak = jnp.max(scores, axis=-1, keepdims=True)
    exp_scores = jnp.exp(scores - peak)
    weights = (exp_scores / jnp.sum(exp_scores, axis=-1, keepdims=True)).astype(jnp.bfloat16)
    mixed = jnp.einsum(
        "rhgc,rchd->rhgd", weights[..., :CACHE], cache_values, preferred_element_type=jnp.float32
    )
    mixed = mixed + jnp.einsum(
        "rhgn,rnhd->rhgd", weights[..., CACHE:], new_values, preferred_element_type=jnp.float32
    )
    return mixed.reshape(total_row_count, H * HD).astype(jnp.bfloat16)


def shards(
    hidden_state_input,
    attention_norm_scale,
    query_weight,
    key_value_weight,
    output_weight,
    adapter_down_weight,
    adapter_up_weight,
    row_adapter_index,
    adapter_storage_index,
    cache_length_per_row,
    key_value_cache,
):
    owner_offset = lax.axis_index("replica") * adapter_down_weight.shape[0]
    gathered_adapter_index = lax.all_gather(row_adapter_index, "replica", axis=0, tiled=True)
    table_index = jnp.arange(adapter_storage_index.shape[0], dtype=jnp.int32)
    gathered_storage_index = jnp.sum(
        jnp.where(
            gathered_adapter_index[:, None] == table_index[None, :],
            adapter_storage_index[None, :],
            0,
        ),
        axis=1,
    )
    up_projection_parts = adapter_up_weight[gathered_adapter_index]
    w_o_cols = lax.all_to_all(output_weight, "replica", split_axis=1, concat_axis=0, tiled=True)
    hidden = hidden_state_input
    keys_new = []
    values_new = []
    results = []
    for decode_step in range(STEPS):
        normalized_hidden = rms_normed(hidden, attention_norm_scale)
        gathered_row_inputs = lax.all_gather(normalized_hidden, "replica", axis=0, tiled=True)
        base_q = jnp.dot(gathered_row_inputs, query_weight, preferred_element_type=jnp.float32)
        kv_cols = jnp.dot(
            gathered_row_inputs, key_value_weight, preferred_element_type=jnp.float32
        ).astype(jnp.bfloat16)
        partial_rank_terms = down_projected(
            gathered_row_inputs, gathered_storage_index, owner_offset, adapter_down_weight
        )
        rank_projected = lax.psum(partial_rank_terms, "replica").astype(jnp.bfloat16)
        up_projected = jnp.einsum(
            "rk,rkc->rc", rank_projected, up_projection_parts, preferred_element_type=jnp.float32
        )
        query_cols = (base_q + up_projected).astype(jnp.bfloat16)
        queries, fresh_kv = (
            lax.all_to_all(query_cols, "replica", split_axis=0, concat_axis=1, tiled=True),
            lax.all_to_all(kv_cols, "replica", split_axis=0, concat_axis=1, tiled=True),
        )
        half_width = fresh_kv.shape[1] // 2
        keys_new.append(fresh_kv[:, :half_width])
        values_new.append(fresh_kv[:, half_width:])
        attended = attend(
            queries,
            key_value_cache,
            cache_length_per_row,
            jnp.stack(keys_new, axis=1),
            jnp.stack(values_new, axis=1),
        )
        out_cols = jnp.dot(
            lax.all_gather(attended, "replica", axis=0, tiled=True),
            w_o_cols,
            preferred_element_type=jnp.float32,
        ).astype(jnp.bfloat16)
        output = lax.all_to_all(out_cols, "replica", split_axis=0, concat_axis=1, tiled=True)
        hidden = (hidden.astype(jnp.float32) + output.astype(jnp.float32)).astype(jnp.bfloat16)
        results.append(hidden)
    return jnp.stack(results)


def solution(mesh):
    in_specs = (
        P(("groups", "replica"), None),
        P(),
        P(None, "replica"),
        P(None, "replica"),
        P("replica", None),
        P("replica", None, None),
        P(None, None, "replica"),
        P(("groups", "replica")),
        P(),
        P(("groups", "replica")),
        P(("groups", "replica"), None, None, None),
    )
    out_specs = P(None, ("groups", "replica"), None)
    return jax.shard_map(shards, mesh=mesh, in_specs=in_specs, out_specs=out_specs, check_vma=False)
```

profile of v0, /device:TPU:0, one launch (start us, length us, event | category | flops | bytes accessed | tf_op | source)
XLA Modules:
  0.0 462.9 jit_solution(16276279545043468038)
XLA Ops:
  3.8 24.6 %all-gather = bf16[16,1,8192]{2,1,0:T(2,128)(2,1)S(1)} all-gather(bf16[1,1,8192]{2,1,0:T(2,128)(2,1)S(1)} %convert_bitcast_fusion.1), channel_id=1, replica_groups=mesh['groups'=2,'replica'=16] {'replica'}, dimensions={0}, use_global_device_ids=true | all-gather | bytes 278528 | tf_op jit(solution)/shard_map/all_gather | solution.py:114
  28.7 2.0 fusion.30
  31.3 3.5 all-to-all-start.1
  36.8 12.3 %all-reduce = s32[16]{0:T(128)S(1)} all-reduce(s32[16]{0:T(128)S(1)} %dynamic-update-slice), channel_id=1, replica_groups=mesh['groups'=2,'replica'=16] {'replica'}, use_global_device_ids=true, to_apply=%add | all-reduce | flops 16 | bytes 128
  53.4 1.6 fusion.38
  57.0 1.6 fusion.34
  58.6 30.0 %psum.14 = bf16[16,64]{1,0:T(8,128)(2,1)S(1)} all-reduce(f32[16,64]{1,0:T(8,128)S(1)} %get-tuple-element.346), channel_id=1, replica_groups=mesh['groups'=2,'replica'=16] {'replica'}, use_global_device_ids=true, to_apply=%region_12.13 | all-reduce | flops 1024 | bytes 6144 | tf_op jit(solution)/shard_map/psum | solution.py:122
  89.4 4.6 fusion.29
  96.0 3.5 all-to-all-start
  99.5 12.0 %copy.90 = bf16[512,8192]{0,1:T(8,128)(2,1)} copy(bf16[512,8192]{1,0:T(8,128)(2,1)} %param.23) | data formatting | bytes 16777216 | tf_op args[4]
  111.4 6.0 %all-to-all-start.2 = ((bf16[512,16,512]{0,2,1:T(8,128)(2,1)}), bf16[512,16,512]{0,2,1:T(8,128)(2,1)}, u32[]{:S(2)}, u32[]{:S(2)}) async-start(bf16[512,16,512]{0,2,1:T(8,128)(2,1)} %bitcast.168), calls=%async_computation.2 | async-start | bytes 16777216 | tf_op jit(solution)/shard_map/all_to_all | solution.py:107
  117.5 3.1 fusion.72
  120.5 2.3 copy.121
  122.8 2.3 copy.120
  126.1 1.6 fusion.73
  128.1 1.6 fusion.23
  129.8 156.2 %all-gather.1 = bf16[16,1,8192]{2,1,0:T(2,128)(2,1)} all-gather(bf16[1,1,8192]{2,1,0:T(2,128)(2,1)S(1)} %reshape.566), channel_id=1, replica_groups=mesh['groups'=2,'replica'=16] {'replica'}, dimensions={0}, use_global_device_ids=true | all-gather | bytes 278528 | tf_op jit(solution)/shard_map/all_gather | solution.py:142
  286.0 12.3 %copy.91 = bf16[16,512,512]{2,1,0:T(8,128)(2,1)} copy(bf16[16,512,512]{1,2,0:T(8,128)(2,1)} %bitcast.29) | data formatting | bytes 16777216 | tf_op jit(solution)/shard_map/all_to_all | solution.py:107
  298.3 4.8 %fusion.26 = bf16[16,1,512]{2,0,1:T(8,128)(2,1)S(1)} fusion(bf16[8192,512]{1,0:T(8,128)(2,1)} %bitcast.166, bf16[16,1,8192]{2,1,0:T(2,128)(2,1)} %all-gather.1), kind=kOutput, calls=%fused_computation.51 | convolution fusion | flops 134225920 | bytes 8667136 | tf_op jit(solution)/shard_map/dot_general | solution.py:141
  304.4 31.3 %all-to-all-start.3 = ((bf16[16,2,256]{2,1,0:T(2,128)(2,1)}), bf16[16,2,256]{2,1,0:T(2,128)(2,1)S(1)}, u32[]{:S(2)}, u32[]{:S(2)}) async-start(bf16[16,2,256]{2,1,0:T(2,128)(2,1)} %reshape.596), calls=%async_computation.3 | async-start | bytes 32768 | tf_op jit(solution)/shard_map/all_to_all | solution.py:146
  335.7 6.5 %all-to-all-done.3 = bf16[16,2,256]{2,1,0:T(2,128)(2,1)S(1)} async-done(((bf16[16,2,256]{2,1,0:T(2,128)(2,1)}), bf16[16,2,256]{2,1,0:T(2,128)(2,1)S(1)}, u32[]{:S(2)}, u32[]{:S(2)}) %all-to-all-start.3) | async-done | bytes 16416 | tf_op jit(solution)/shard_map/all_to_all | solution.py:146
  343.6 19.1 %all-gather.2 = bf16[16,1,8192]{2,1,0:T(2,128)(2,1)S(1)} all-gather(bf16[1,1,8192]{2,1,0:T(2,128)(2,1)S(1)} %convert_bitcast_fusion), channel_id=1, replica_groups=mesh['groups'=2,'replica'=16] {'replica'}, dimensions={0}, use_global_device_ids=true | all-gather | bytes 278528 | tf_op jit(solution)/shard_map/all_gather | solution.py:114
  365.8 2.1 fusion.31
  368.4 1.7 fusion.32
  370.1 32.8 %psum.15 = bf16[16,64]{1,0:T(8,128)(2,1)S(1)} all-reduce(f32[16,64]{1,0:T(8,128)S(1)} %get-tuple-element.348), channel_id=1, replica_groups=mesh['groups'=2,'replica'=16] {'replica'}, use_global_device_ids=true, to_apply=%region_22.23 | all-reduce | flops 1024 | bytes 6144 | tf_op jit(solution)/shard_map/psum | solution.py:122
  403.8 3.4 all-to-all-start.5
  407.2 4.7 %fusion.28 = bf16[16,1,512]{2,0,1:T(8,128)(2,1)S(1)} fusion(bf16[16,8192]{1,0:T(8,128)(2,1)S(1)} %bitcast.165, bf16[8192,512]{1,0:T(8,128)(2,1)} %param.21, f32[16,1,512]{2,1,0:T(1,128)S(1)} %fusion.56), kind=kOutput, calls=%fused_computation.53 | convolution fusion | flops 134234112 | bytes 8699904 | tf_op jit(solution)/shard_map/dot_general | solution.py:115
  413.6 5.6 %all-to-all-start.4 = ((bf16[16,2,256]{2,1,0:T(2,128)(2,1)}), bf16[16,2,256]{2,1,0:T(2,128)(2,1)S(1)}, u32[]{:S(2)}, u32[]{:S(2)}) async-start(bf16[16,2,256]{2,1,0:T(2,128)(2,1)} %reshape.598), calls=%async_computation.4 | async-start | bytes 32768 | tf_op jit(solution)/shard_map/all_to_all | solution.py:128
  419.2 6.5 %all-to-all-done.4 = bf16[16,2,256]{2,1,0:T(2,128)(2,1)S(1)} async-done(((bf16[16,2,256]{2,1,0:T(2,128)(2,1)}), bf16[16,2,256]{2,1,0:T(2,128)(2,1)S(1)}, u32[]{:S(2)}, u32[]{:S(2)}) %all-to-all-start.4) | async-done | bytes 16416 | tf_op jit(solution)/shard_map/all_to_all | solution.py:128
  428.5 19.1 %all-gather.3 = bf16[16,1,8192]{2,1,0:T(2,128)(2,1)S(1)} all-gather(bf16[1,1,8192]{2,1,0:T(2,128)(2,1)S(1)} %reshape.570), channel_id=1, replica_groups=mesh['groups'=2,'replica'=16] {'replica'}, dimensions={0}, use_global_device_ids=true | all-gather | bytes 278528 | tf_op jit(solution)/shard_map/all_gather | solution.py:142
  447.6 4.6 fusion.27
  452.9 9.2 %all_to_all.103 = bf16[16,2,256]{2,1,0:T(2,128)(2,1)S(1)} all-to-all(bf16[16,2,256]{2,1,0:T(2,128)(2,1)S(1)} %reshape.600), channel_id=1, replica_groups=mesh['groups'=2,'replica'=16] {'replica'}, dimensions={0} | all-to-all | bytes 32768 | tf_op jit(solution)/shard_map/all_to_all | solution.py:146
  (94 shorter events, 26.3 us)
Async XLA Ops:
  0.0 88.6 %copy-start = (bf16[32,64,512]{2,1,0:T(8,128)(2,1)S(1)}, bf16[32,64,512]{2,1,0:T(8,128)(2,1)}, u32[]{:S(2)}) copy-start(bf16[32,64,512]{2,1,0:T(8,128)(2,1)} %param.25) | copy-start | bytes 6291460
  0.0 35.5 %copy-start.6 = (u32[32]{0:T(128)S(1)}, u32[32]{0:T(128)}, u32[]{:S(2)}) copy-start(u32[32]{0:T(128)} %constant.153) | copy-start | bytes 388
  0.0 49.1 %copy-start.5 = (s32[32]{0:T(128)S(1)}, s32[32]{0:T(128)}, u32[]{:S(2)}) copy-start(s32[32]{0:T(128)} %param.27) | copy-start | bytes 388
  31.3 64.7 %all-to-all-start.1 = ((bf16[16,1,128]{2,1,0:T(2,128)(2,1)}), bf16[16,1,128]{2,1,0:T(2,128)(2,1)S(1)}, u32[]{:S(2)}, u32[]{:S(2)}) async-start(bf16[16,1,128]{2,1,0:T(2,128)(2,1)} %copy.86), calls=%async_computation.1 | async-start | bytes 16384 | tf_op jit(solution)/shard_map/all_to_all | solution.py:129
  96.0 15.5 %all-to-all-start = ((bf16[16,2,256]{2,1,0:T(2,128)(2,1)}), bf16[16,2,256]{2,1,0:T(2,128)(2,1)S(1)}, u32[]{:S(2)}, u32[]{:S(2)}) async-start(bf16[16,2,256]{2,1,0:T(2,128)(2,1)} %reshape.594), calls=%async_computation | async-start | bytes 32768 | tf_op jit(solution)/shard_map/all_to_all | solution.py:128
  111.4 174.6 %all-to-all-start.2 = ((bf16[512,16,512]{0,2,1:T(8,128)(2,1)}), bf16[512,16,512]{0,2,1:T(8,128)(2,1)}, u32[]{:S(2)}, u32[]{:S(2)}) async-start(bf16[512,16,512]{0,2,1:T(8,128)(2,1)} %bitcast.168), calls=%async_computation.2 | async-start | bytes 16777216 | tf_op jit(solution)/shard_map/all_to_all | solution.py:107
  298.3 43.9 %copy-start.4 = (bf16[1,8192]{1,0:T(2,128)(2,1)S(1)}, bf16[1,8192]{1,0:T(2,128)(2,1)}, u32[]{:S(2)}) copy-start(bf16[1,8192]{1,0:T(2,128)(2,1)} %param.19) | copy-start | bytes 49156
  304.4 37.8 %all-to-all-start.3 = ((bf16[16,2,256]{2,1,0:T(2,128)(2,1)}), bf16[16,2,256]{2,1,0:T(2,128)(2,1)S(1)}, u32[]{:S(2)}, u32[]{:S(2)}) async-start(bf16[16,2,256]{2,1,0:T(2,128)(2,1)} %reshape.596), calls=%async_computation.3 | async-start | bytes 32768 | tf_op jit(solution)/shard_map/all_to_all | solution.py:146
  365.8 2.2 copy-start.2
  365.8 2.2 copy-start.3
  403.8 9.7 %all-to-all-start.5 = ((bf16[16,1,128]{2,1,0:T(2,128)(2,1)}), bf16[16,1,128]{2,1,0:T(2,128)(2,1)S(1)}, u32[]{:S(2)}, u32[]{:S(2)}) async-start(bf16[16,1,128]{2,1,0:T(2,128)(2,1)} %copy.95), calls=%async_computation.5 | async-start | bytes 16384 | tf_op jit(solution)/shard_map/all_to_all | solution.py:129
  407.2 20.7 %copy-start.1 = (bf16[1,1,512,1024]{2,3,1,0:T(8,128)(2,1)S(1)}, bf16[1,1,512,1024]{2,3,1,0:T(8,128)(2,1)}, u32[]{:S(2)}) copy-start(bf16[1,1,512,1024]{2,3,1,0:T(8,128)(2,1)} %copy.121) | copy-start | bytes 3145732
  413.6 12.1 %all-to-all-start.4 = ((bf16[16,2,256]{2,1,0:T(2,128)(2,1)}), bf16[16,2,256]{2,1,0:T(2,128)(2,1)S(1)}, u32[]{:S(2)}, u32[]{:S(2)}) async-start(bf16[16,2,256]{2,1,0:T(2,128)(2,1)} %reshape.598), calls=%async_computation.4 | async-start | bytes 32768 | tf_op jit(solution)/shard_map/all_to_all | solution.py:128
where the time goes:
time: 465 us; the launch traced here: 463 us
  blocking collectives  303 us (65%)
  starting transfers between devices  53.3 us (11%)
  local copies, waits for them, and re-layouts  43 us (9%)
  matrix products  33.9 us (7%)
  waiting for transfers between devices  13.3 us (3%)
  other arithmetic  11.7 us (3%)
    all_gather x2, blocking collectives, shards(): lax.all_gather(attended, 'replica', axis=0, tiled=True)  175 us
    psum x2, blocking collectives, shards(): lax.psum(partial_rank_terms, 'replica').astype(jnp.bfloat16)  62.8 us
    all_gather x2, blocking collectives, shards(): lax.all_gather(normalized_hidden, 'replica', axis=0, tiled=True)  43.7 us
    all_to_all x1, starting transfers between devices, shards(): lax.all_to_all(out_cols, 'replica', split_axis=0, concat_axis=1, tiled=True)  31.3 us
    unnamed x32, local copies, waits for them, and re-layouts  20.6 us
    unnamed x1, blocking collectives  12.3 us
    all_to_all x1, local copies, waits for them, and re-layouts, shards(): lax.all_to_all(output_weight, 'replica', split_axis=1, concat_axis=0, til...  12.3 us
    dot_general x2, matrix products, shards(): jnp.dot(lax.all_gather(attended, 'replica', axis=0, tiled=True), w_o_cols...  9.33 us
  transfers between devices with their start and end apart: 6, of which 3 were waited for; matrix products, arithmetic and copies ran while one was open for 10% of the time, Pallas kernels for 0%

commit v1 on v0

v1 whole, which is shorter than its diff:
```python
import functools
import math

import jax
import jax.numpy as jnp
from jax import lax
from jax.experimental import pallas as pl
from jax.experimental.pallas import tpu as pltpu
from jax.sharding import PartitionSpec as P

H = 64
KVH = 8
HD = 128
CACHE = 512
STEPS = 2
GROUP = H // KVH
NEW = 8
AXIS = "replica"


def rms_normed(hidden, attention_norm_scale):
    widened = hidden.astype(jnp.float32)
    factor = lax.rsqrt(jnp.mean(widened * widened, axis=-1, keepdims=True) + 1e-05)
    return (widened * factor * attention_norm_scale.astype(jnp.float32)).astype(jnp.bfloat16)


def everyone(block, count):
    spread = jnp.broadcast_to(block, (count,) + block.shape[1:])
    return lax.all_to_all(spread, AXIS, split_axis=0, concat_axis=0, tiled=True)


def swap(blocks):
    return lax.all_to_all(blocks, AXIS, split_axis=0, concat_axis=0, tiled=True)


def attend_kernel(fresh, length_ref, query_ref, cache_ref, new_keys_ref, new_values_ref, out_ref):
    length = length_ref[0]
    in_cache = lax.broadcasted_iota(jnp.int32, (GROUP, CACHE), 1) < length
    is_new = lax.broadcasted_iota(jnp.int32, (GROUP, NEW), 1) < fresh
    contract_last = (((1,), (1,)), ((), ()))
    for head in range(KVH):
        lanes = slice(head * HD, (head + 1) * HD)
        rows = slice(head * GROUP, (head + 1) * GROUP)
        query = query_ref[rows, :].astype(jnp.bfloat16)
        old = lax.dot_general(
            query, cache_ref[0, 0, :, lanes], contract_last, preferred_element_type=jnp.float32
        ) * (1.0 / math.sqrt(HD))
        new = lax.dot_general(
            query,
            new_keys_ref[:, lanes].astype(jnp.bfloat16),
            contract_last,
            preferred_element_type=jnp.float32,
        ) * (1.0 / math.sqrt(HD))
        old = jnp.where(in_cache, old, -jnp.inf)
        new = jnp.where(is_new, new, -jnp.inf)
        peak = jnp.maximum(
            jnp.max(old, axis=-1, keepdims=True), jnp.max(new, axis=-1, keepdims=True)
        )
        old = jnp.exp(old - peak)
        new = jnp.exp(new - peak)
        total = jnp.sum(old, axis=-1, keepdims=True) + jnp.sum(new, axis=-1, keepdims=True)
        old = (old / total).astype(jnp.bfloat16)
        new = (new / total).astype(jnp.bfloat16)
        out_ref[rows, :] = jnp.dot(
            old, cache_ref[0, 1, :, lanes], preferred_element_type=jnp.float32
        ) + jnp.dot(
            new, new_values_ref[:, lanes].astype(jnp.bfloat16), preferred_element_type=jnp.float32
        )


def attend(queries, key_value_cache, cache_length, new_keys, new_values, fresh):
    return pl.pallas_call(
        functools.partial(attend_kernel, fresh),
        out_shape=jax.ShapeDtypeStruct((H, HD), jnp.float32),
        in_specs=[pl.BlockSpec(memory_space=pltpu.SMEM)]
        + [pl.BlockSpec(memory_space=pltpu.VMEM)] * 4,
        out_specs=pl.BlockSpec(memory_space=pltpu.VMEM),
        compiler_params=pltpu.CompilerParams(vmem_limit_bytes=16 << 20),
        cost_estimate=pl.CostEstimate(flops=4 * H * CACHE * HD, bytes_accessed=2 << 20, transcendentals=0),
        name="attend",
    )(cache_length, queries, key_value_cache, new_keys, new_values)


def shards(
    hidden_state_input,
    attention_norm_scale,
    query_weight,
    key_value_weight,
    output_weight,
    adapter_down_weight,
    adapter_up_weight,
    row_adapter_index,
    adapter_storage_index,
    cache_length_per_row,
    key_value_cache,
):
    count = lax.axis_size(AXIS)
    kept, width, rank = adapter_down_weight.shape
    columns = query_weight.shape[1]
    owner_offset = lax.axis_index(AXIS) * kept

    adapter_of = everyone(jnp.broadcast_to(row_adapter_index[:, None], (1, 128)), count)[:, 0]
    storage_of = adapter_storage_index[adapter_of]
    up_of = adapter_up_weight[adapter_of].reshape(count * rank, columns)
    own_row = jnp.arange(count, dtype=jnp.int32)

    hidden = hidden_state_input
    new_keys = jnp.zeros((NEW, key_value_cache.shape[3]), jnp.float32)
    new_values = new_keys
    results = []
    for step in range(STEPS):
        normed = rms_normed(hidden, attention_norm_scale)
        rows = everyone(normed, count)

        low = jnp.zeros((count, rank), jnp.float32)
        for index in range(kept):
            part = jnp.dot(rows, adapter_down_weight[index], preferred_element_type=jnp.float32)
            low = jnp.where((storage_of == owner_offset + index)[:, None], part, low)
        low = jnp.broadcast_to(low.astype(jnp.bfloat16)[None], (count, count, rank))
        low = jnp.sum(swap(low).astype(jnp.float32), axis=0).astype(jnp.bfloat16)

        query = jnp.dot(rows, query_weight, preferred_element_type=jnp.float32)
        fresh = jnp.dot(rows, key_value_weight, preferred_element_type=jnp.float32)
        spread = jnp.where(
            own_row[:, None, None] == own_row[None, :, None], low[:, None, :], 0
        ).reshape(count, count * rank)
        query = query + jnp.dot(spread, up_of, preferred_element_type=jnp.float32)

        mine = swap(jnp.concatenate([query, fresh], axis=1).astype(jnp.bfloat16))
        query = mine[:, :columns].reshape(H, HD).astype(jnp.float32)
        fresh = mine[:, columns:].reshape(2, -1).astype(jnp.float32)
        new_keys = new_keys.at[step].set(fresh[0])
        new_values = new_values.at[step].set(fresh[1])

        attended = attend(
            query, key_value_cache, cache_length_per_row, new_keys, new_values, step + 1
        )
        features = swap(attended.astype(jnp.bfloat16).reshape(count, columns))
        partial = jnp.dot(features, output_weight, preferred_element_type=jnp.float32)
        parts = swap(partial.astype(jnp.bfloat16))
        out = jnp.sum(parts.astype(jnp.float32), axis=0, keepdims=True).astype(jnp.bfloat16)
        hidden = (hidden.astype(jnp.float32) + out.astype(jnp.float32)).astype(jnp.bfloat16)
        results.append(hidden)
    return jnp.stack(results)


def solution(mesh):
    in_specs = (
        P(("groups", "replica"), None),
        P(),
        P(None, "replica"),
        P(None, "replica"),
        P("replica", None),
        P("replica", None, None),
        P(None, None, "replica"),
        P(("groups", "replica")),
        P(),
        P(("groups", "replica")),
        P(("groups", "replica"), None, None, None),
    )
    out_specs = P(None, ("groups", "replica"), None)
    return jax.shard_map(shards, mesh=mesh, in_specs=in_specs, out_specs=out_specs, check_vma=False)
```

time: 465 us -> 195 us (0.42)
  blocking collectives: 303 us -> 67.1 us
  starting transfers between devices: 53.3 us -> 24.5 us
  local copies, waits for them, and re-layouts: 43 us -> 22.7 us
  waiting for transfers between devices: 13.3 us -> 23.7 us
  other arithmetic: 11.7 us -> 18.6 us
  matrix products: 33.9 us -> 27.3 us
  Pallas kernels: 0 us -> 5.68 us
    all_gather x4 -> x0, blocking collectives: 219 us -> none  [the longest x2 175 us: shards(): lax.all_gather(attended, 'replica', axis=0, tiled=True)]
    psum x2 -> x0, blocking collectives: 62.8 us -> none  [shards(): lax.psum(partial_rank_terms, 'replica').astype(jnp.bfloat16)]
    all_to_all x1 -> x6, blocking collectives: 9.21 us -> 67.1 us  [the longest x5 53.4 us: swap(): return lax.all_to_all(blocks, AXIS, split_axis=0, concat_axis=0, tiled=True)]
    all_to_all x6 -> x5, starting transfers between devices: 53.3 us -> 24.5 us  [the longest x2 13.4 us: everyone(): return lax.all_to_all(spread, AXIS, split_axis=0, concat_axis=0, tiled=True)]
    all_to_all x4 -> x2, local copies, waits for them, and re-layouts: 14.1 us -> 0.04 us  [swap(): return lax.all_to_all(blocks, AXIS, split_axis=0, concat_axis=0, tiled=True)]
    unnamed x1 -> x0, blocking collectives: 12.3 us -> none
    all_to_all x6 -> x5, waiting for transfers between devices: 13.3 us -> 23.7 us  [the longest x3 15.2 us: swap(): return lax.all_to_all(blocks, AXIS, split_axis=0, concat_axis=0, tiled=True)]
    dot_general x19 -> x12, matrix products: 33.9 us -> 27.3 us  [the longest x2 9.45 us: shards(): query = jnp.dot(rows, query_weight, preferred_element_type=jnp.float32)]
  transfers between devices with their start and end apart: 6 -> 5, of which waited for: 3 -> 4; matrix products, arithmetic and copies ran while one was open for 10% -> 7% of each run, Pallas kernels for 0% -> 0%
where the time goes in v1:
time: 195 us; the launch traced here: 193 us
  blocking collectives  67.1 us (34%)
  matrix products  27.3 us (14%)
  starting transfers between devices  24.5 us (13%)
  waiting for transfers between devices  23.7 us (12%)
  local copies, waits for them, and re-layouts  22.7 us (12%)
  other arithmetic  18.6 us (10%)
  Pallas kernels  5.68 us (3%)
  between operations  3.28 us (2%)
    all_to_all x5, blocking collectives, swap(): return lax.all_to_all(blocks, AXIS, split_axis=0, concat_axis=0, tiled=True)  53.4 us
    unnamed x40, local copies, waits for them, and re-layouts  17.7 us
    all_to_all x3, waiting for transfers between devices, swap(): return lax.all_to_all(blocks, AXIS, split_axis=0, concat_axis=0, tiled=True)  15.2 us
    all_to_all x1, blocking collectives, everyone(): return lax.all_to_all(spread, AXIS, split_axis=0, concat_axis=0, tiled=True)  13.7 us
    all_to_all x2, starting transfers between devices, everyone(): return lax.all_to_all(spread, AXIS, split_axis=0, concat_axis=0, tiled=True)  13.4 us
    all_to_all x3, starting transfers between devices, swap(): return lax.all_to_all(blocks, AXIS, split_axis=0, concat_axis=0, tiled=True)  11.1 us
    dot_general x2, matrix products, shards(): query = jnp.dot(rows, query_weight, preferred_element_type=jnp.float32)  9.45 us
    dot_general x2, matrix products, shards(): jnp.dot(features, output_weight, preferred_element_type=jnp.float32)  9.17 us
  transfers between devices with their start and end apart: 5, of which 4 were waited for; matrix products, arithmetic and copies ran while one was open for 7% of the time, Pallas kernels for 0%

profile of v1, /device:TPU:0, one launch (start us, length us, event | category | flops | bytes accessed | tf_op | source)
XLA Modules:
  0.0 192.9 jit_solution(5086586941506083320)
XLA Ops:
  1.4 7.4 %all-to-all-start.1 = ((s32[16,1,128]{2,1,0:T(1,128)}), s32[16,1,128]{2,1,0:T(1,128)S(1)}, u32[]{:S(2)}, u32[]{:S(2)}) async-start(s32[16,1,128]{2,1,0:T(1,128)} %broadcast_in_dim_broadcast_in_dim.8), calls=%async_computation.1 | async-start | bytes 16384 | tf_op jit(solution)/shard_map/all_to_all | solution.py:29
  14.1 2.3 %reduce.22 = bf16[16,8192]{1,0:T(8,128)(2,1)S(1)} reduce(bf16[16,1,8192]{2,1,0:T(2,128)(2,1)S(1)} %broadcast_in_dim.99, bf16[]{:T(256)} %broadcast.120), dimensions={1}, to_apply=%broadcast_in_dim.99.reduce_sub_computation | reduce | bytes 524290 | tf_op jit(solution)/shard_map/broadcast_in_dim | solution.py:28
  17.3 6.0 %all-to-all-start = ((bf16[16,2,4096]{2,1,0:T(2,128)(2,1)}), bf16[16,2,4096]{2,1,0:T(2,128)(2,1)S(1)}, u32[]{:S(2)}, u32[]{:S(2)}) async-start(bf16[16,2,4096]{2,1,0:T(2,128)(2,1)} %reshape.308), calls=%async_computation | async-start | bytes 524288 | tf_op jit(solution)/shard_map/all_to_all | solution.py:29
  24.8 8.6 %all-to-all-done = bf16[16,2,4096]{2,1,0:T(2,128)(2,1)S(1)} async-done(((bf16[16,2,4096]{2,1,0:T(2,128)(2,1)}), bf16[16,2,4096]{2,1,0:T(2,128)(2,1)S(1)}, u32[]{:S(2)}, u32[]{:S(2)}) %all-to-all-start) | async-done | bytes 262176 | tf_op jit(solution)/shard_map/all_to_all | solution.py:29
  35.6 1.6 fusion.18
  37.2 4.7 %fusion.32 = f32[16,512]{1,0:T(8,128)S(1)} fusion(bf16[8192,512]{1,0:T(8,128)(2,1)} %param.21, bf16[16,1,8192]{2,0,1:T(8,128)(2,1)S(1)} %copy.30), kind=kOutput, calls=%fused_computation.42 | convolution fusion | flops 134217728 | bytes 8683520 | tf_op jit(solution)/shard_map/dot_general | solution.py:122
  43.1 3.5 %all-to-all-start.2 = ((bf16[16,2,512]{2,1,0:T(2,128)(2,1)}), bf16[16,2,512]{2,1,0:T(2,128)(2,1)S(1)}, u32[]{:S(2)}, u32[]{:S(2)}) async-start(bf16[16,2,512]{2,1,0:T(2,128)(2,1)} %reshape.310), calls=%async_computation.2 | async-start | bytes 65536 | tf_op jit(solution)/shard_map/all_to_all | solution.py:33
  46.6 2.0 %fusion.12 = bf16[16,1,128]{2,0,1:T(8,128)(2,1)S(1)} fusion(bf16[8192,128]{1,0:T(8,128)(2,1)} %param.22, bf16[16,1,8192]{2,0,1:T(8,128)(2,1)S(1)} %copy.30), kind=kOutput, calls=%fused_computation.22 | convolution fusion | flops 33556480 | bytes 2363392 | tf_op jit(solution)/shard_map/dot_general | solution.py:123
  48.6 4.6 %all-to-all-done.2 = bf16[16,2,512]{2,1,0:T(2,128)(2,1)S(1)} async-done(((bf16[16,2,512]{2,1,0:T(2,128)(2,1)}), bf16[16,2,512]{2,1,0:T(2,128)(2,1)S(1)}, u32[]{:S(2)}, u32[]{:S(2)}) %all-to-all-start.2) | async-done | bytes 32800 | tf_op jit(solution)/shard_map/all_to_all | solution.py:33
  55.1 3.5 %all-to-all-start.3 = ((bf16[16,2,320]{2,1,0:T(2,128)(2,1)}), bf16[16,2,320]{2,1,0:T(2,128)(2,1)S(1)}, u32[]{:S(2)}, u32[]{:S(2)}) async-start(bf16[16,2,320]{2,1,0:T(2,128)(2,1)} %reshape.312), calls=%async_computation.3 | async-start | bytes 49152 | tf_op jit(solution)/shard_map/all_to_all | solution.py:33
  59.3 5.9 %all-to-all-done.3 = bf16[16,2,320]{2,1,0:T(2,128)(2,1)S(1)} async-done(((bf16[16,2,320]{2,1,0:T(2,128)(2,1)}), bf16[16,2,320]{2,1,0:T(2,128)(2,1)S(1)}, u32[]{:S(2)}, u32[]{:S(2)}) %all-to-all-start.3) | async-done | bytes 20512 | tf_op jit(solution)/shard_map/all_to_all | solution.py:33
  65.4 1.6 copy-done.1
  66.9 2.8 %attend.2 = f32[64,128]{1,0:T(8,128)S(1)} custom-call(s32[1]{0:T(128)S(6)} %copy.55.length_ref, f32[64,128]{1,0:T(8,128)S(1)} %reshape.283.query_ref, bf16[1,2,512,1024]{3,2,1,0:T(8,128)(2,1)S(1)} %copy-done.1, f32[8,1024]{1,0:T(8,128)S(1)} %scatter.14.new_keys_ref, f32[8,1024]{1,0:T(8,128)S(1)} %scatter.15.new_values_ref), custom_call_target="tpu_custom_call" | custom-call | flops 16777216 | bytes 2097152 | tf_op jit(solution)/shard_map/attend/pallas_call | solution.py:72
  70.6 9.1 %all_to_all.99 = bf16[16,2,256]{2,1,0:T(2,128)(2,1)S(1)} all-to-all(bf16[16,2,256]{2,1,0:T(2,128)(2,1)S(1)} %reshape.314), channel_id=1, replica_groups=mesh['groups'=2,'replica'=16] {'replica'}, dimensions={0} | all-to-all | bytes 32768 | tf_op jit(solution)/shard_map/all_to_all | solution.py:33
  79.7 4.6 %fusion = bf16[16,1,8192]{2,0,1:T(8,128)(2,1)S(1)} fusion(bf16[512,8192]{1,0:T(8,128)(2,1)} %param.23, bf16[16,1,512]{2,1,0:T(2,128)(2,1)S(1)} %reshape.315), kind=kOutput, calls=%fused_computation.4 | convolution fusion | flops 134348800 | bytes 8667136 | tf_op jit(solution)/shard_map/dot_general | solution.py:139
  84.3 1.5 reduce.25
  85.8 1.8 reshape.316
  87.7 13.5 %all_to_all.100 = bf16[16,2,4096]{2,1,0:T(2,128)(2,1)S(1)} all-to-all(bf16[16,2,4096]{2,1,0:T(2,128)(2,1)} %reshape.316), channel_id=1, replica_groups=mesh['groups'=2,'replica'=16] {'replica'}, dimensions={0} | all-to-all | bytes 524288 | tf_op jit(solution)/shard_map/all_to_all | solution.py:33
  107.2 3.2 %reduce.26 = bf16[16,8192]{1,0:T(8,128)(2,1)S(1)} reduce(bf16[16,1,8192]{2,1,0:T(2,128)(2,1)} %broadcast_in_dim.106, bf16[]{:T(256)} %broadcast.120), dimensions={1}, to_apply=%broadcast_in_dim.106.reduce_sub_computation | reduce | bytes 524290 | tf_op jit(solution)/shard_map/broadcast_in_dim | solution.py:28
  111.4 13.7 %all_to_all.101 = bf16[16,2,4096]{2,1,0:T(2,128)(2,1)S(1)} all-to-all(bf16[16,2,4096]{2,1,0:T(2,128)(2,1)} %reshape.318), channel_id=1, replica_groups=mesh['groups'=2,'replica'=16] {'replica'}, dimensions={0} | all-to-all | bytes 524288 | tf_op jit(solution)/shard_map/all_to_all | solution.py:29
  127.4 1.6 fusion.16
  129.0 4.7 %fusion.27 = f32[16,512]{1,0:T(8,128)S(1)} fusion(bf16[8192,512]{1,0:T(8,128)(2,1)} %param.21, bf16[16,1,8192]{2,0,1:T(8,128)(2,1)S(1)} %copy.33), kind=kOutput, calls=%fused_computation.37 | convolution fusion | flops 134217728 | bytes 8683520 | tf_op jit(solution)/shard_map/dot_general | solution.py:122
  134.7 1.6 reshape.320
  136.3 4.2 %all-to-all-start.7 = ((bf16[16,2,512]{2,1,0:T(2,128)(2,1)}), bf16[16,2,512]{2,1,0:T(2,128)(2,1)}, u32[]{:S(2)}, u32[]{:S(2)}) async-start(bf16[16,2,512]{2,1,0:T(2,128)(2,1)} %reshape.320), calls=%async_computation.7 | async-start | bytes 65536 | tf_op jit(solution)/shard_map/all_to_all | solution.py:33
  140.5 2.0 %fusion.13 = bf16[16,1,128]{2,0,1:T(8,128)(2,1)S(1)} fusion(bf16[8192,128]{1,0:T(8,128)(2,1)} %param.22, bf16[16,1,8192]{2,0,1:T(8,128)(2,1)S(1)} %copy.33), kind=kOutput, calls=%fused_computation.23 | convolution fusion | flops 33556480 | bytes 2363392 | tf_op jit(solution)/shard_map/dot_general | solution.py:123
  142.4 4.7 %all-to-all-done.7 = bf16[16,2,512]{2,1,0:T(2,128)(2,1)} async-done(((bf16[16,2,512]{2,1,0:T(2,128)(2,1)}), bf16[16,2,512]{2,1,0:T(2,128)(2,1)}, u32[]{:S(2)}, u32[]{:S(2)}) %all-to-all-start.7) | async-done | bytes 32800 | tf_op jit(solution)/shard_map/all_to_all | solution.py:33
  149.2 9.1 %all_to_all.102 = bf16[16,2,320]{2,1,0:T(2,128)(2,1)S(1)} all-to-all(bf16[16,2,320]{2,1,0:T(2,128)(2,1)S(1)} %reshape.322), channel_id=1, replica_groups=mesh['groups'=2,'replica'=16] {'replica'}, dimensions={0} | all-to-all | bytes 40960 | tf_op jit(solution)/shard_map/all_to_all | solution.py:33
  158.7 1.6 copy-done.2
  160.3 2.8 %attend.3 = f32[64,128]{1,0:T(8,128)S(1)} custom-call(s32[1]{0:T(128)S(6)} %copy.55.length_ref, f32[64,128]{1,0:T(8,128)S(1)} %reshape.285.query_ref, bf16[1,2,512,1024]{3,2,1,0:T(8,128)(2,1)S(1)} %copy-done.2, f32[8,1024]{1,0:T(8,128)S(1)} %scatter.16.new_keys_ref, f32[8,1024]{1,0:T(8,128)S(1)} %scatter.19.new_values_ref), custom_call_target="tpu_custom_call" | custom-call | flops 16777216 | bytes 2097152 | tf_op jit(solution)/shard_map/attend/pallas_call | solution.py:72
  164.0 9.1 %all_to_all.103 = bf16[16,2,256]{2,1,0:T(2,128)(2,1)S(1)} all-to-all(bf16[16,2,256]{2,1,0:T(2,128)(2,1)S(1)} %reshape.324), channel_id=1, replica_groups=mesh['groups'=2,'replica'=16] {'replica'}, dimensions={0} | all-to-all | bytes 32768 | tf_op jit(solution)/shard_map/all_to_all | solution.py:33
  173.1 4.6 %fusion.1 = bf16[16,1,8192]{2,0,1:T(8,128)(2,1)S(1)} fusion(bf16[512,8192]{1,0:T(8,128)(2,1)} %param.23, bf16[16,1,512]{2,1,0:T(2,128)(2,1)S(1)} %reshape.325), kind=kOutput, calls=%fused_computation.5 | convolution fusion | flops 134348800 | bytes 8667136 | tf_op jit(solution)/shard_map/dot_general | solution.py:139
  178.7 12.6 %all_to_all.104 = bf16[16,2,4096]{2,1,0:T(2,128)(2,1)S(1)} all-to-all(bf16[16,2,4096]{2,1,0:T(2,128)(2,1)S(1)} %reshape.326), channel_id=1, replica_groups=mesh['groups'=2,'replica'=16] {'replica'}, dimensions={0} | all-to-all | bytes 524288 | tf_op jit(solution)/shard_map/all_to_all | solution.py:33
  (89 shorter events, 29.2 us)
Async XLA Ops:
  0.0 24.1 %copy-start = (bf16[32,64,512]{2,1,0:T(8,128)(2,1)S(1)}, bf16[32,64,512]{2,1,0:T(8,128)(2,1)}, u32[]{:S(2)}) copy-start(bf16[32,64,512]{2,1,0:T(8,128)(2,1)} %param.25) | copy-start | bytes 6291460
  0.0 23.4 %copy-start.3 = (s32[32]{0:T(128)S(1)}, s32[32]{0:T(128)}, u32[]{:S(2)}) copy-start(s32[32]{0:T(128)} %param.27) | copy-start | bytes 388
  1.4 15.9 %all-to-all-start.1 = ((s32[16,1,128]{2,1,0:T(1,128)}), s32[16,1,128]{2,1,0:T(1,128)S(1)}, u32[]{:S(2)}, u32[]{:S(2)}) async-start(s32[16,1,128]{2,1,0:T(1,128)} %broadcast_in_dim_broadcast_in_dim.8), calls=%async_computation.1 | async-start | bytes 16384 | tf_op jit(solution)/shard_map/all_to_all | solution.py:29
  11.6 0.6 copy-start.7
  17.3 16.1 %all-to-all-start = ((bf16[16,2,4096]{2,1,0:T(2,128)(2,1)}), bf16[16,2,4096]{2,1,0:T(2,128)(2,1)S(1)}, u32[]{:S(2)}, u32[]{:S(2)}) async-start(bf16[16,2,4096]{2,1,0:T(2,128)(2,1)} %reshape.308), calls=%async_computation | async-start | bytes 524288 | tf_op jit(solution)/shard_map/all_to_all | solution.py:29
  37.2 4.7 %copy-start.4 = (bf16[2,8192,64]{1,2,0:T(8,128)(2,1)S(1)}, bf16[2,8192,64]{1,2,0:T(8,128)(2,1)}, u32[]{:S(2)}) copy-start(bf16[2,8192,64]{1,2,0:T(8,128)(2,1)} %param.24) | copy-start | bytes 6291460
  43.1 10.1 %all-to-all-start.2 = ((bf16[16,2,512]{2,1,0:T(2,128)(2,1)}), bf16[16,2,512]{2,1,0:T(2,128)(2,1)S(1)}, u32[]{:S(2)}, u32[]{:S(2)}) async-start(bf16[16,2,512]{2,1,0:T(2,128)(2,1)} %reshape.310), calls=%async_computation.2 | async-start | bytes 65536 | tf_op jit(solution)/shard_map/all_to_all | solution.py:33
  55.1 10.0 %all-to-all-start.3 = ((bf16[16,2,320]{2,1,0:T(2,128)(2,1)}), bf16[16,2,320]{2,1,0:T(2,128)(2,1)S(1)}, u32[]{:S(2)}, u32[]{:S(2)}) async-start(bf16[16,2,320]{2,1,0:T(2,128)(2,1)} %reshape.312), calls=%async_computation.3 | async-start | bytes 49152 | tf_op jit(solution)/shard_map/all_to_all | solution.py:33
  65.3 1.6 copy-start.1
  84.3 19.4 %copy-start.6 = (bf16[1,8192]{1,0:T(2,128)(2,1)S(1)}, bf16[1,8192]{1,0:T(2,128)(2,1)}, u32[]{:S(2)}) copy-start(bf16[1,8192]{1,0:T(2,128)(2,1)} %param.19) | copy-start | bytes 49156
  129.0 4.7 %copy-start.5 = (bf16[2,8192,64]{1,2,0:T(8,128)(2,1)S(1)}, bf16[2,8192,64]{1,2,0:T(8,128)(2,1)}, u32[]{:S(2)}) copy-start(bf16[2,8192,64]{1,2,0:T(8,128)(2,1)} %param.24) | copy-start | bytes 6291460
  136.3 10.8 %all-to-all-start.7 = ((bf16[16,2,512]{2,1,0:T(2,128)(2,1)}), bf16[16,2,512]{2,1,0:T(2,128)(2,1)}, u32[]{:S(2)}, u32[]{:S(2)}) async-start(bf16[16,2,512]{2,1,0:T(2,128)(2,1)} %reshape.320), calls=%async_computation.7 | async-start | bytes 65536 | tf_op jit(solution)/shard_map/all_to_all | solution.py:33
  158.7 1.6 copy-start.2

commit v2 on v1

v2 whole, which is shorter than its diff:
```python
import functools
import math

import jax
import jax.numpy as jnp
from jax import lax
from jax.experimental import pallas as pl
from jax.experimental.pallas import tpu as pltpu
from jax.sharding import PartitionSpec as P

H = 64
KVH = 8
HD = 128
STEPS = 2
GROUP = H // KVH
EPS = 1e-05
AXIS = "replica"
LANES = 128
LAST = (((1,), (1,)), ((), ()))
FIRST = (((0,), (0,)), ((), ()))


def split_of(count):
    far = 1 << (count.bit_length() // 2)
    return far, count // far


def shift(block, distance, count):
    return lax.ppermute(block, AXIS, [(i, i ^ distance) for i in range(count)])


def across_far(blocks, near, count):
    return [blocks[0]] + [shift(b, k * near, count) for k, b in enumerate(blocks) if k]


def across_near(blocks, count):
    return [blocks[0]] + [shift(b, k, count) for k, b in enumerate(blocks) if k]


def call(body, outs, name, scratch=(), vmem=24 << 20, flops=1 << 20, moved=1 << 18):
    def run(*operands, specs=None):
        specs = specs or [pltpu.VMEM] * len(operands)
        return pl.pallas_call(
            body,
            out_shape=outs,
            in_specs=[pl.BlockSpec(memory_space=s) for s in specs],
            out_specs=jax.tree.map(lambda _: pl.BlockSpec(memory_space=pltpu.VMEM), outs),
            scratch_shapes=list(scratch),
            compiler_params=pltpu.CompilerParams(vmem_limit_bytes=vmem),
            cost_estimate=pl.CostEstimate(flops=flops, bytes_accessed=moved, transcendentals=0),
            name=name,
        )(*operands)

    return run


def shape(dims, dtype=jnp.bfloat16):
    return jax.ShapeDtypeStruct(dims, dtype)


def iota(dims, axis):
    return lax.broadcasted_iota(jnp.int32, dims, axis)


def dot(a, b, contract=(((1,), (0,)), ((), ()))):
    return lax.dot_general(a, b, contract, preferred_element_type=jnp.float32)


def normalized(hidden, scale):
    factor = lax.rsqrt(jnp.mean(hidden * hidden, axis=-1, keepdims=True) + EPS)
    return (hidden * factor * scale).astype(jnp.bfloat16)


def first_kernel(hidden_ref, scale_ref, adapter_ref, out_ref):
    width = hidden_ref.shape[1]
    hidden = hidden_ref[...].astype(jnp.float32)
    out_ref[:, :width] = normalized(hidden, scale_ref[...].astype(jnp.float32))
    digit = iota((1, LANES), 1)
    adapter = adapter_ref[0]
    high, low = adapter // 256, adapter % 256
    out_ref[:, width:] = jnp.where(digit == 0, low, jnp.where(digit == 1, high, 0)).astype(
        jnp.float32
    ).astype(jnp.bfloat16)


def stacked_kernel(count_in, *refs):
    for k, ref in enumerate(refs[:count_in]):
        refs[count_in][k : k + 1, :] = ref[...]


def low_kernel(near, far, width, *refs):
    pieces, refs = refs[:near], refs[near:]
    me_ref, member_ref, down_ref, rows_ref, low_ref, held = refs
    count = near * far
    for l in range(near):
        held[l * far : (l + 1) * far, :] = pieces[l][:, :width].astype(jnp.float32)
    rows = held[...].astype(jnp.bfloat16)
    rows_ref[...] = rows
    kept = down_ref.shape[0]
    low = jnp.zeros((count, down_ref.shape[1]), jnp.float32)
    for index in range(kept):
        part = dot(rows, down_ref[index], LAST)
        low = jnp.where(member_ref[:, index : index + 1] > 0, part, low)
    slot = iota((count, count), 1)
    origin = me_ref[0] ^ ((slot % far) * near + slot // far)
    order = (iota((count, count), 0) == origin).astype(jnp.bfloat16)
    low_ref[...] = dot(order, low.astype(jnp.bfloat16)).astype(jnp.bfloat16)


def member_kernel(near, far, width, *refs):
    pieces, (me_ref, storage_ref, member_ref, adapter_ref, held) = refs[:near], refs[near:]
    kept = member_ref.shape[1]
    count = near * far
    for l in range(near):
        held[l * far : (l + 1) * far, :] = pieces[l][:, width:].astype(jnp.float32)
    adapter = (held[:, 0:1] + 256.0 * held[:, 1:2]).astype(jnp.int32)
    adapter_ref[...] = adapter
    table = storage_ref.shape[1]
    chosen = jnp.where(iota((count, table), 1) == adapter, storage_ref[...], 0)
    storage = jnp.sum(chosen.astype(jnp.float32), axis=1, keepdims=True).astype(jnp.int32)
    member_ref[...] = (storage - me_ref[0] * kept == iota((count, kept), 1)).astype(jnp.int32)


def project_kernel(rows_ref, query_hbm, fresh_hbm, query_ref, fresh_ref, query_w, fresh_w, sems):
    chunks = sems.shape[1]
    deep = query_w.shape[0] // chunks
    copies = []
    for c in range(chunks):
        part = pl.ds(c * deep, deep)
        copies.append(
            (
                pltpu.make_async_copy(query_hbm.at[part], query_w.at[part], sems.at[0, c]),
                pltpu.make_async_copy(fresh_hbm.at[part], fresh_w.at[part], sems.at[1, c]),
            )
        )
    for pair in copies:
        for copy in pair:
            copy.start()
    query = jnp.zeros(query_ref.shape, jnp.float32)
    fresh = jnp.zeros(fresh_ref.shape, jnp.float32)
    for c, pair in enumerate(copies):
        for copy in pair:
            copy.wait()
        part = slice(c * deep, (c + 1) * deep)
        rows = rows_ref[:, part]
        query = query + dot(rows, query_w[part, :])
        fresh = fresh + dot(rows, fresh_w[part, :])
    query_ref[...] = query
    fresh_ref[...] = fresh


def up_kernel(near, far, *refs):
    lows, refs = refs[:near], refs[near:]
    me_ref, query_ref, fresh_ref, up_ref = refs[:4]
    outs = refs[4:]
    count = near * far
    rank = lows[0].shape[1]
    columns = query_ref.shape[1]
    low = lows[0][...].astype(jnp.float32)
    for ref in lows[1:]:
        low = low + ref[...].astype(jnp.float32)
    slot = iota((count, count), 0)
    origin = me_ref[0] ^ ((slot % far) * near + slot // far)
    order = (iota((count, count), 1) == origin).astype(jnp.bfloat16)
    low = dot(order, low.astype(jnp.bfloat16)).astype(jnp.bfloat16)
    wide = count * rank
    repeat = (iota((rank, wide), 1) % rank == iota((rank, wide), 0)).astype(jnp.bfloat16)
    spread = jnp.where(
        iota((count, wide), 1) // rank == iota((count, wide), 0), dot(low, repeat), 0.0
    ).astype(jnp.bfloat16)
    query = query_ref[...] + dot(spread, up_ref[...])
    fresh = fresh_ref[...]
    for l in range(near):
        part = slice(l * far, (l + 1) * far)
        outs[l][:, :columns] = query[part].astype(jnp.bfloat16)
        outs[l][:, columns:] = fresh[part].astype(jnp.bfloat16)


def turn_kernel(near, far, *refs):
    pieces, outs, held = refs[:near], refs[near : near + far], refs[-1]
    for l in range(near):
        held[l * far : (l + 1) * far, :] = pieces[l][...].astype(jnp.float32)
    rows = held[...]
    for k in range(far):
        outs[k][...] = jnp.concatenate(
            [rows[l * far + k : l * far + k + 1] for l in range(near)], axis=0
        ).astype(jnp.bfloat16)


def pieces_of(slots, select, whole, size):
    if size >= whole:
        each = size // whole
        total = None
        for c in range(each):
            part = dot(select(each, c), slots[:, c * whole : (c + 1) * whole])
            total = part if total is None else total + part
        return total
    return jnp.concatenate([dot(select(0, p), slots) for p in range(whole // size)], axis=1)


def attend_kernel(near, far, columns, fresh_columns, first, *refs):
    pieces, refs = refs[:far], refs[far:]
    length_ref, me_ref, cache_ref = refs[:3]
    refs = refs[3:]
    if not first:
        past, refs = refs[:2], refs[2:]
    outs, refs = refs[:near], refs[near:]
    if first:
        keep, refs = refs[:2], refs[2:]
    held, scores = refs
    count = near * far
    cache = cache_ref.shape[2]
    me = me_ref[0]
    for k in range(far):
        held[k * near : (k + 1) * near, :] = pieces[k][...].astype(jnp.float32)
    slots = held[...].astype(jnp.bfloat16)
    origin = me ^ iota((H, count), 1)
    head = iota((H, count), 0)

    def query_pick(each, c):
        if each:
            return (head == origin * each + c).astype(jnp.bfloat16)
        return (head * (HD // columns) + c == origin).astype(jnp.bfloat16)

    def fresh_pick(offset):
        def pick(each, c):
            want = head // GROUP + offset
            if each:
                return (want == origin * each + c).astype(jnp.bfloat16)
            return (want * (HD // fresh_columns) + c == origin).astype(jnp.bfloat16)

        return pick

    query = pieces_of(slots[:, :columns], query_pick, HD, columns)
    fresh = slots[:, columns:]
    new = [
        (
            pieces_of(fresh, fresh_pick(0), HD, fresh_columns),
            pieces_of(fresh, fresh_pick(KVH), HD, fresh_columns),
        )
    ]
    if first:
        keep[0][...], keep[1][...] = new[0]
    else:
        new.insert(0, (past[0][...], past[1][...]))
    scale = 1.0 / math.sqrt(HD)
    for j in range(KVH):
        rows = slice(j * GROUP, (j + 1) * GROUP)
        scores[rows, :] = dot(
            query[rows].astype(jnp.bfloat16), cache_ref[0, 0, :, j * HD : (j + 1) * HD], LAST
        )
    in_cache = iota((H, cache), 1) < length_ref[0]
    old = jnp.where(in_cache, scores[...] * scale, -jnp.inf)
    news = [jnp.sum(query * keys, axis=1, keepdims=True) * scale for keys, _ in new]
    peak = jnp.max(old, axis=1, keepdims=True)
    for score in news:
        peak = jnp.maximum(peak, score)
    old = jnp.exp(old - peak)
    news = [jnp.exp(score - peak) for score in news]
    total = jnp.sum(old, axis=1, keepdims=True)
    for score in news:
        total = total + score
    old = old / total
    extra = jnp.zeros((H, HD), jnp.float32)
    for score, (_, values) in zip(news, new):
        extra = extra + (score / total).astype(jnp.bfloat16).astype(jnp.float32) * values
    mixed = jnp.concatenate(
        [
            dot(
                old[j * GROUP : (j + 1) * GROUP].astype(jnp.bfloat16),
                cache_ref[0, 1, :, j * HD : (j + 1) * HD],
            )
            for j in range(KVH)
        ],
        axis=0,
    )
    mixed = (mixed + extra).astype(jnp.bfloat16)
    slot = iota((count, H), 0)
    target = me ^ ((slot % far) * near + slot // far)
    head = iota((count, H), 1)
    if columns >= HD:
        each = columns // HD
        out = [dot((head == target * each + c).astype(jnp.bfloat16), mixed) for c in range(each)]
        out = out[0] if each == 1 else jnp.concatenate(out, axis=1)
    else:
        parts = HD // columns
        out = jnp.zeros((count, columns), jnp.float32)
        for p in range(parts):
            pick = (head * parts + p == target).astype(jnp.bfloat16)
            out = out + dot(pick, mixed[:, p * columns : (p + 1) * columns])
    for l in range(near):
        outs[l][...] = out[l * far : (l + 1) * far].astype(jnp.bfloat16)


def output_kernel(near, far, *refs):
    pieces, refs = refs[:far], refs[far:]
    weight_hbm, refs = refs[0], refs[1:]
    outs, (held, weight, sems) = refs[:near], refs[near:]
    chunks = sems.shape[0]
    wide = weight.shape[1] // chunks
    copies = [
        pltpu.make_async_copy(
            weight_hbm.at[:, pl.ds(c * wide, wide)], weight.at[:, pl.ds(c * wide, wide)], sems.at[c]
        )
        for c in range(chunks)
    ]
    for copy in copies:
        copy.start()
    for k in range(far):
        piece = pieces[k][...].astype(jnp.float32)
        for l in range(near):
            held[l * far + k : l * far + k + 1, :] = piece[l : l + 1]
    rows = held[...].astype(jnp.bfloat16)
    for c, copy in enumerate(copies):
        copy.wait()
        part = slice(c * wide, (c + 1) * wide)
        out = dot(rows, weight[:, part])
        for l in range(near):
            outs[l][:, part] = out[l * far : (l + 1) * far].astype(jnp.bfloat16)


def partial_kernel(near, far, *refs):
    pieces, outs = refs[:near], refs[near:]
    total = pieces[0][...].astype(jnp.float32)
    for ref in pieces[1:]:
        total = total + ref[...].astype(jnp.float32)
    for k in range(far):
        outs[k][...] = total[k : k + 1].astype(jnp.bfloat16)


def finish_kernel(far, last, *refs):
    pieces, refs = refs[:far], refs[far:]
    hidden_ref, scale_ref, out_ref = refs[:3]
    total = pieces[0][...].astype(jnp.float32)
    for ref in pieces[1:]:
        total = total + ref[...].astype(jnp.float32)
    total = total.astype(jnp.bfloat16).astype(jnp.float32)
    hidden = (hidden_ref[...].astype(jnp.float32) + total).astype(jnp.bfloat16)
    out_ref[...] = hidden
    if not last:
        refs[3][...] = normalized(hidden.astype(jnp.float32), scale_ref[...].astype(jnp.float32))


def shards(
    hidden_state_input,
    attention_norm_scale,
    query_weight,
    key_value_weight,
    output_weight,
    adapter_down_weight,
    adapter_up_weight,
    row_adapter_index,
    adapter_storage_index,
    cache_length_per_row,
    key_value_cache,
):
    count = lax.axis_size(AXIS)
    far, near = split_of(count)
    kept, width, rank = adapter_down_weight.shape
    columns = query_weight.shape[1]
    fresh_columns = key_value_weight.shape[1]
    message = columns + fresh_columns
    smem, vmem = pltpu.SMEM, pltpu.VMEM
    me = lax.axis_index(AXIS).astype(jnp.int32).reshape(1)
    down = adapter_down_weight.transpose(0, 2, 1)
    scale = attention_norm_scale[None]
    storage = adapter_storage_index[None]

    hidden = hidden_state_input
    carried = call(first_kernel, shape((1, width + LANES)), "first")(
        hidden, scale, row_adapter_index, specs=[vmem, vmem, smem]
    )
    results = []
    past = ()
    for step in range(STEPS):
        first, last = step == 0, step == STEPS - 1
        carried = across_far([carried] * far, near, count)
        carried = jnp.concatenate(carried, axis=0)
        pieces = across_near([carried] * near, count)
        if first:
            member, adapter = call(
                functools.partial(member_kernel, near, far, width),
                [shape((count, kept), jnp.int32), shape((count, 1), jnp.int32)],
                "member",
                [pltpu.VMEM((count, LANES), jnp.float32)],
            )(*pieces, me, storage, specs=[vmem] * near + [smem, vmem])
            up_of = adapter_up_weight[adapter[:, 0]].reshape(count * rank, columns)
        rows, low = call(
            functools.partial(low_kernel, near, far, width),
            [shape((count, width)), shape((count, rank))],
            "low",
            [pltpu.VMEM((count, width), jnp.float32)],
            moved=2 << 20,
        )(*pieces, me, member, down, specs=[vmem] * near + [smem, vmem, vmem])
        low = across_far([low] * far, near, count)
        low = functools.reduce(lambda a, b: a + b, [x.astype(jnp.float32) for x in low])
        low = low.astype(jnp.bfloat16)
        lows = across_near([low] * near, count)
        chunks = 8
        query, fresh = call(
            project_kernel,
            [shape((count, columns), jnp.float32), shape((count, fresh_columns), jnp.float32)],
            "project",
            [
                pltpu.VMEM((width, columns), jnp.bfloat16),
                pltpu.VMEM((width, fresh_columns), jnp.bfloat16),
                pltpu.SemaphoreType.DMA((2, chunks)),
            ],
            flops=2 * count * width * message,
            moved=2 * width * message,
        )(rows, query_weight, key_value_weight, specs=[vmem, pl.ANY, pl.ANY])
        blocks = call(
            functools.partial(up_kernel, near, far), [shape((far, message))] * near, "up"
        )(*lows, me, query, fresh, up_of, specs=[vmem] * near + [smem, vmem, vmem, vmem])

        turn = functools.partial(turn_kernel, near, far)
        blocks = across_near(blocks, count)
        blocks = call(
            turn, [shape((near, message))] * far, "turn", [pltpu.VMEM((count, message), jnp.float32)]
        )(*blocks)
        blocks = across_far(blocks, near, count)
        outs = [shape((far, columns))] * near
        if first:
            outs = outs + [shape((H, HD), jnp.float32)] * 2
        blocks = call(
            functools.partial(attend_kernel, near, far, columns, fresh_columns, first),
            outs,
            "attend",
            [
                pltpu.VMEM((count, message), jnp.float32),
                pltpu.VMEM((H, key_value_cache.shape[2]), jnp.float32),
            ],
            moved=2 << 20,
        )(
            *blocks,
            cache_length_per_row,
            me,
            key_value_cache,
            *past,
            specs=[vmem] * far + [smem, smem, vmem] + [vmem] * len(past),
        )
        if first:
            past = tuple(blocks[near:])
            blocks = blocks[:near]

        blocks = across_near(blocks, count)
        blocks = call(
            turn, [shape((near, columns))] * far, "turn", [pltpu.VMEM((count, columns), jnp.float32)]
        )(*blocks)
        blocks = across_far(blocks, near, count)
        chunks = 8
        blocks = call(
            functools.partial(output_kernel, near, far),
            [shape((far, width))] * near,
            "output",
            [
                pltpu.VMEM((count, columns), jnp.float32),
                pltpu.VMEM((columns, width), jnp.bfloat16),
                pltpu.SemaphoreType.DMA((chunks,)),
            ],
            flops=2 * count * width * columns,
            moved=2 * width * columns,
        )(*blocks, output_weight, specs=[vmem] * far + [pl.ANY])

        blocks = across_near(blocks, count)
        blocks = call(
            functools.partial(partial_kernel, near, far), [shape((1, width))] * far, "partial"
        )(*blocks)
        blocks = across_far(blocks, near, count)
        outs = [shape((1, width))] * (1 if last else 2)
        outs = call(functools.partial(finish_kernel, far, last), outs, "finish")(
            *blocks, hidden, scale
        )
        hidden = outs[0]
        results.append(hidden)
        if not last:
            carried = outs[1]
    return jnp.stack(results)


def solution(mesh):
    in_specs = (
        P(("groups", "replica"), None),
        P(),
        P(None, "replica"),
        P(None, "replica"),
        P("replica", None),
        P("replica", None, None),
        P(None, None, "replica"),
        P(("groups", "replica")),
        P(),
        P(("groups", "replica")),
        P(("groups", "replica"), None, None, None),
    )
    out_specs = P(None, ("groups", "replica"), None)
    return jax.shard_map(shards, mesh=mesh, in_specs=in_specs, out_specs=out_specs, check_vma=False)
```

time: 195 us -> 157 us (0.81); the launches traced: 193 us -> 157 us
  blocking collectives: 67.1 us -> 0 us
  starting transfers between devices: 24.5 us -> 64.7 us
  waiting for transfers between devices: 23.7 us -> 54.9 us
  matrix products: 27.3 us -> 0 us
  other arithmetic: 18.6 us -> 1.16 us
  Pallas kernels: 5.68 us -> 18.4 us
  local copies, waits for them, and re-layouts: 22.7 us -> 16.1 us
    all_to_all x6 -> x0, blocking collectives: 67.1 us -> none  [the longest x5 53.4 us: swap(): return lax.all_to_all(blocks, AXIS, split_axis=0, concat_axis=0, tiled=True)]
    ppermute x0 -> x60, starting transfers between devices: none -> 64.7 us  [shift(): return lax.ppermute(block, AXIS, [(i, i ^ distance) for i in range(count)])]
    ppermute x0 -> x60, waiting for transfers between devices: none -> 54.9 us  [shift(): return lax.ppermute(block, AXIS, [(i, i ^ distance) for i in range(count)])]
    dot_general x12 -> x0, matrix products: 27.3 us -> none  [the longest x2 9.45 us: shards(): query = jnp.dot(rows, query_weight, preferred_element_type=jnp.float32)]
    all_to_all x5 -> x0, starting transfers between devices: 24.5 us -> none  [the longest x2 13.4 us: everyone(): return lax.all_to_all(spread, AXIS, split_axis=0, concat_axis=0, tiled=True)]
    all_to_all x5 -> x0, waiting for transfers between devices: 23.7 us -> none  [the longest x3 15.2 us: swap(): return lax.all_to_all(blocks, AXIS, split_axis=0, concat_axis=0, tiled=True)]
    pallas_call x2 -> x20, Pallas kernels: 5.68 us -> 18.4 us  [run(): pl.pallas_call(body, out_shape=outs, in_specs=[pl.BlockSpec(memory_space=...]
    broadcast_in_dim x3 -> x0, other arithmetic: 6.25 us -> none  [the longest x2 5.53 us: everyone(): spread = jnp.broadcast_to(block, (count,) + block.shape[1:])]
  transfers between devices with their start and end apart: 5 -> 60, of which waited for: 4 -> 38; matrix products, arithmetic and copies ran while one was open for 7% -> 0% of each run, Pallas kernels for 0% -> 4%
where the time goes in v2:
time: 157 us
  starting transfers between devices  64.7 us (41%)
  waiting for transfers between devices  54.9 us (35%)
  Pallas kernels  18.4 us (12%)
  local copies, waits for them, and re-layouts  16.1 us (10%)
  between operations  1.78 us (1%)
    ppermute x60, starting transfers between devices, shift(): return lax.ppermute(block, AXIS, [(i, i ^ distance) for i in range(count)])  64.7 us
    ppermute x60, waiting for transfers between devices, shift(): return lax.ppermute(block, AXIS, [(i, i ^ distance) for i in range(count)])  54.9 us
    pallas_call x20, Pallas kernels, run(): pl.pallas_call(body, out_shape=outs, in_specs=[pl.BlockSpec(memory_space=...  18.4 us
    unnamed x30, local copies, waits for them, and re-layouts  14.8 us
  transfers between devices with their start and end apart: 60, of which 38 were waited for; matrix products, arithmetic and copies ran while one was open for 0% of the time, Pallas kernels for 4%

profile of v2, /device:TPU:0, one launch (start us, length us, event | category | flops | bytes accessed | tf_op | source)
XLA Modules:
  0.0 157.0 jit_solution(11496158582265760341)
XLA Ops:
  2.5 5.1 %collective-permute-start.2 = (bf16[1,8320]{1,0:T(2,128)(2,1)S(1)}, bf16[1,8320]{1,0:T(2,128)(2,1)S(1)}, u32[]{:S(2)}, u32[]{:S(2)}) collective-permute-start(bf16[1,8320]{1,0:T(2,128)(2,1)S(1)} %first.1), channel_id=1, source_target_pairs={{0,12},{1,13},{2,14},{3,15},{4,8},{5,9},{6,10},{7,11},{8,4},{9,5},... | collective-permute-start | bytes 49928 | tf_op jit(solution)/shard_map/ppermute | solution.py:29
  9.5 2.9 %collective-permute-done.1 = bf16[1,8320]{1,0:T(2,128)(2,1)S(1)} collective-permute-done((bf16[1,8320]{1,0:T(2,128)(2,1)S(1)}, bf16[1,8320]{1,0:T(2,128)(2,1)S(1)}, u32[]{:S(2)}, u32[]{:S(2)}) %collective-permute-start.1) | collective-permute-done | bytes 16672 | tf_op jit(solution)/shard_map/ppermute | solution.py:29
  14.5 2.5 %collective-permute-done.5.refs_3_ = bf16[4,8320]{1,0:T(4,128)(2,1)S(1)} collective-permute-done((bf16[4,8320]{1,0:T(4,128)(2,1)S(1)}, bf16[4,8320]{1,0:T(4,128)(2,1)S(1)}, u32[]{:S(2)}, u32[]{:S(2)}) %collective-permute-start.5) | collective-permute-done | bytes 66592 | tf_op jit(solution)/shard_map/ppermute | solution.py:29
  23.9 2.4 %collective-permute-start.6 = (bf16[16,64]{1,0:T(8,128)(2,1)S(1)}, bf16[16,64]{1,0:T(8,128)(2,1)S(1)}, u32[]{:S(2)}, u32[]{:S(2)}) collective-permute-start(bf16[16,64]{1,0:T(8,128)(2,1)S(1)} %get-tuple-element.68), channel_id=1, source_target_pairs={{0,4},{1,5},{2,6},{3,7},{4,0},{5,1},{6,2},{7,3},{8,12},{9,13},{10,... | collective-permute-start | bytes 6152 | tf_op jit(solution)/shard_map/ppermute | solution.py:29
  29.8 3.4 %copy-done.1 = bf16[8192,512]{1,0:T(8,128)(2,1)S(1)} copy-done((bf16[8192,512]{1,0:T(8,128)(2,1)S(1)}, bf16[8192,512]{1,0:T(8,128)(2,1)}, u32[]{:S(2)}) %copy-start.1) | copy-done | bytes 8388632
  33.1 3.2 %project.2 = (f32[16,512]{1,0:T(8,128)S(1)}, f32[16,128]{1,0:T(8,128)S(1)}) custom-call(bf16[16,8192]{1,0:T(8,128)(2,1)S(1)} %get-tuple-element.69.rows_ref, bf16[8192,512]{1,0:T(8,128)(2,1)S(1)} %copy-done.1, bf16[8192,128]{1,0:T(8,128)(2,1)S(1)} %copy-done.8), custom_call_target="tpu_custom_call" | custom-call | flops 167772160 | bytes 10485760 | tf_op jit(solution)/shard_map/project/pallas_call | solution.py:43
  39.3 1.8 %collective-permute-done.13.refs_2_ = bf16[4,640]{1,0:T(4,128)(2,1)S(1)} collective-permute-done((bf16[4,640]{1,0:T(4,128)(2,1)S(1)}, bf16[4,640]{1,0:T(4,128)(2,1)S(1)}, u32[]{:S(2)}, u32[]{:S(2)}) %collective-permute-start.13) | collective-permute-done | bytes 5152 | tf_op jit(solution)/shard_map/ppermute | solution.py:29
  41.3 2.0 %collective-permute-start.15 = (bf16[4,640]{1,0:T(4,128)(2,1)S(1)}, bf16[4,640]{1,0:T(4,128)(2,1)S(1)}, u32[]{:S(2)}, u32[]{:S(2)}) collective-permute-start(bf16[4,640]{1,0:T(4,128)(2,1)S(1)} %get-tuple-element.78), channel_id=1, source_target_pairs={{0,4},{1,5},{2,6},{3,7},{4,0},{5,1},{6,2},{7,3},{8,12},{9,13},{10,... | collective-permute-start | bytes 15368 | tf_op jit(solution)/shard_map/ppermute | solution.py:29
  47.8 2.0 %collective-permute-done.17.refs_3_ = bf16[4,640]{1,0:T(4,128)(2,1)S(1)} collective-permute-done((bf16[4,640]{1,0:T(4,128)(2,1)S(1)}, bf16[4,640]{1,0:T(4,128)(2,1)S(1)}, u32[]{:S(2)}, u32[]{:S(2)}) %collective-permute-start.17) | collective-permute-done | bytes 5152 | tf_op jit(solution)/shard_map/ppermute | solution.py:29
  56.9 1.9 %collective-permute-start.22 = (bf16[4,512]{1,0:T(4,128)(2,1)S(1)}, bf16[4,512]{1,0:T(4,128)(2,1)S(1)}, u32[]{:S(2)}, u32[]{:S(2)}) collective-permute-start(bf16[4,512]{1,0:T(4,128)(2,1)S(1)} %get-tuple-element.87), channel_id=1, source_target_pairs={{0,8},{1,9},{2,10},{3,11},{4,12},{5,13},{6,14},{7,15},{8,0},{9,1},... | collective-permute-start | bytes 12296 | tf_op jit(solution)/shard_map/ppermute | solution.py:29
  58.8 2.5 %collective-permute-start.23 = (bf16[4,512]{1,0:T(4,128)(2,1)S(1)}, bf16[4,512]{1,0:T(4,128)(2,1)S(1)}, u32[]{:S(2)}, u32[]{:S(2)}) collective-permute-start(bf16[4,512]{1,0:T(4,128)(2,1)S(1)} %get-tuple-element.88), channel_id=1, source_target_pairs={{0,12},{1,13},{2,14},{3,15},{4,8},{5,9},{6,10},{7,11},{8,4},{9,5},... | collective-permute-start | bytes 12296 | tf_op jit(solution)/shard_map/ppermute | solution.py:29
  61.5 2.7 %collective-permute-done.23.refs_3_ = bf16[4,512]{1,0:T(4,128)(2,1)S(1)} collective-permute-done((bf16[4,512]{1,0:T(4,128)(2,1)S(1)}, bf16[4,512]{1,0:T(4,128)(2,1)S(1)}, u32[]{:S(2)}, u32[]{:S(2)}) %collective-permute-start.23) | collective-permute-done | bytes 4128 | tf_op jit(solution)/shard_map/ppermute | solution.py:29
  64.2 3.4 %copy-done.3 = bf16[512,8192]{1,0:T(8,128)(2,1)S(1)} copy-done((bf16[512,8192]{1,0:T(8,128)(2,1)S(1)}, bf16[512,8192]{1,0:T(8,128)(2,1)}, u32[]{:S(2)}) %copy-start.3) | copy-done | bytes 8388632
  67.6 3.2 %output.2 = (bf16[4,8192]{1,0:T(4,128)(2,1)S(1)}, bf16[4,8192]{1,0:T(4,128)(2,1)S(1)}, bf16[4,8192]{1,0:T(4,128)(2,1)S(1)}, bf16[4,8192]{1,0:T(4,128)(2,1)S(1)}) custom-call(bf16[4,512]{1,0:T(4,128)(2,1)S(1)} %get-tuple-element.85.refs_0_, bf16[4,512]{1,0:T(4,128)(2,1)S(1)} %collective-permute-done.21.refs_1_, ...), custom_call_target="tpu_custom_call" | custom-call | flops 134217728 | bytes 8388608 | tf_op jit(solution)/shard_map/output/pallas_call | solution.py:43
  72.8 3.1 %collective-permute-done.25.refs_2_ = bf16[4,8192]{1,0:T(4,128)(2,1)S(1)} collective-permute-done((bf16[4,8192]{1,0:T(4,128)(2,1)S(1)}, bf16[4,8192]{1,0:T(4,128)(2,1)S(1)}, u32[]{:S(2)}, u32[]{:S(2)}) %collective-permute-start.25) | collective-permute-done | bytes 65568 | tf_op jit(solution)/shard_map/ppermute | solution.py:29
  76.6 3.1 %collective-permute-start.28 = (bf16[1,8192]{1,0:T(2,128)(2,1)S(1)}, bf16[1,8192]{1,0:T(2,128)(2,1)S(1)}, u32[]{:S(2)}, u32[]{:S(2)}) collective-permute-start(bf16[1,8192]{1,0:T(2,128)(2,1)S(1)} %get-tuple-element.95), channel_id=1, source_target_pairs={{0,8},{1,9},{2,10},{3,11},{4,12},{5,13},{6,14},{7,15},{8,0},{9,1},... | collective-permute-start | bytes 49160 | tf_op jit(solution)/shard_map/ppermute | solution.py:29
  81.5 3.8 %collective-permute-done.29.refs_3_ = bf16[1,8192]{1,0:T(2,128)(2,1)S(1)} collective-permute-done((bf16[1,8192]{1,0:T(2,128)(2,1)S(1)}, bf16[1,8192]{1,0:T(2,128)(2,1)S(1)}, u32[]{:S(2)}, u32[]{:S(2)}) %collective-permute-start.29) | collective-permute-done | bytes 16416 | tf_op jit(solution)/shard_map/ppermute | solution.py:29
  87.0 3.1 %collective-permute-start.30 = (bf16[1,8192]{1,0:T(2,128)(2,1)S(1)}, bf16[1,8192]{1,0:T(2,128)(2,1)S(1)}, u32[]{:S(2)}, u32[]{:S(2)}) collective-permute-start(bf16[1,8192]{1,0:T(2,128)(2,1)S(1)} %get-tuple-element.98), channel_id=1, source_target_pairs={{0,4},{1,5},{2,6},{3,7},{4,0},{5,1},{6,2},{7,3},{8,12},{9,13},{10,... | collective-permute-start | bytes 49160 | tf_op jit(solution)/shard_map/ppermute | solution.py:29
  94.5 2.3 %collective-permute-done.35.refs_3_ = bf16[4,8192]{1,0:T(4,128)(2,1)S(1)} collective-permute-done((bf16[4,8192]{1,0:T(4,128)(2,1)S(1)}, bf16[4,8192]{1,0:T(4,128)(2,1)S(1)}, u32[]{:S(2)}, u32[]{:S(2)}) %collective-permute-start.35) | collective-permute-done | bytes 65568 | tf_op jit(solution)/shard_map/ppermute | solution.py:29
  98.4 2.0 %collective-permute-start.38 = (bf16[16,64]{1,0:T(8,128)(2,1)S(1)}, bf16[16,64]{1,0:T(8,128)(2,1)S(1)}, u32[]{:S(2)}, u32[]{:S(2)}) collective-permute-start(bf16[16,64]{1,0:T(8,128)(2,1)S(1)} %get-tuple-element.99), channel_id=1, source_target_pairs={{0,12},{1,13},{2,14},{3,15},{4,8},{5,9},{6,10},{7,11},{8,4},{9,5},... | collective-permute-start | bytes 6152 | tf_op jit(solution)/shard_map/ppermute | solution.py:29
  107.1 3.4 %copy-done.2 = bf16[8192,512]{1,0:T(8,128)(2,1)S(1)} copy-done((bf16[8192,512]{1,0:T(8,128)(2,1)S(1)}, bf16[8192,512]{1,0:T(8,128)(2,1)}, u32[]{:S(2)}) %copy-start.2) | copy-done | bytes 8388632
  110.5 3.2 %project.3 = (f32[16,512]{1,0:T(8,128)S(1)}, f32[16,128]{1,0:T(8,128)S(1)}) custom-call(bf16[16,8192]{1,0:T(8,128)(2,1)S(1)} %get-tuple-element.100.rows_ref, bf16[8192,512]{1,0:T(8,128)(2,1)S(1)} %copy-done.2, bf16[8192,128]{1,0:T(8,128)(2,1)S(1)} %copy-done.9), custom_call_target="tpu_custom_call" | custom-call | flops 167772160 | bytes 10485760 | tf_op jit(solution)/shard_map/project/pallas_call | solution.py:43
  116.0 1.8 %collective-permute-done.43.refs_2_ = bf16[4,640]{1,0:T(4,128)(2,1)S(1)} collective-permute-done((bf16[4,640]{1,0:T(4,128)(2,1)S(1)}, bf16[4,640]{1,0:T(4,128)(2,1)S(1)}, u32[]{:S(2)}, u32[]{:S(2)}) %collective-permute-start.43) | collective-permute-done | bytes 5152 | tf_op jit(solution)/shard_map/ppermute | solution.py:29
  120.6 2.2 %collective-permute-start.47 = (bf16[4,640]{1,0:T(4,128)(2,1)S(1)}, bf16[4,640]{1,0:T(4,128)(2,1)S(1)}, u32[]{:S(2)}, u32[]{:S(2)}) collective-permute-start(bf16[4,640]{1,0:T(4,128)(2,1)S(1)} %get-tuple-element.110), channel_id=1, source_target_pairs={{0,12},{1,13},{2,14},{3,15},{4,8},{5,9},{6,10},{7,11},{8,4},{9,5},... | collective-permute-start | bytes 15368 | tf_op jit(solution)/shard_map/ppermute | solution.py:29
  124.1 1.9 %collective-permute-done.47.refs_3_ = bf16[4,640]{1,0:T(4,128)(2,1)S(1)} collective-permute-done((bf16[4,640]{1,0:T(4,128)(2,1)S(1)}, bf16[4,640]{1,0:T(4,128)(2,1)S(1)}, u32[]{:S(2)}, u32[]{:S(2)}) %collective-permute-start.47) | collective-permute-done | bytes 5152 | tf_op jit(solution)/shard_map/ppermute | solution.py:29
  131.2 2.7 %collective-permute-start.52 = (bf16[4,512]{1,0:T(4,128)(2,1)S(1)}, bf16[4,512]{1,0:T(4,128)(2,1)S(1)}, u32[]{:S(2)}, u32[]{:S(2)}) collective-permute-start(bf16[4,512]{1,0:T(4,128)(2,1)S(1)} %get-tuple-element.119), channel_id=1, source_target_pairs={{0,8},{1,9},{2,10},{3,11},{4,12},{5,13},{6,14},{7,15},{8,0},{9,1},... | collective-permute-start | bytes 12296 | tf_op jit(solution)/shard_map/ppermute | solution.py:29
  135.7 3.6 %collective-permute-done.53.refs_3_ = bf16[4,512]{1,0:T(4,128)(2,1)S(1)} collective-permute-done((bf16[4,512]{1,0:T(4,128)(2,1)S(1)}, bf16[4,512]{1,0:T(4,128)(2,1)S(1)}, u32[]{:S(2)}, u32[]{:S(2)}) %collective-permute-start.53) | collective-permute-done | bytes 4128 | tf_op jit(solution)/shard_map/ppermute | solution.py:29
  139.3 3.2 %output.3 = (bf16[4,8192]{1,0:T(4,128)(2,1)S(1)}, bf16[4,8192]{1,0:T(4,128)(2,1)S(1)}, bf16[4,8192]{1,0:T(4,128)(2,1)S(1)}, bf16[4,8192]{1,0:T(4,128)(2,1)S(1)}) custom-call(bf16[4,512]{1,0:T(4,128)(2,1)S(1)} %get-tuple-element.117.refs_0_, bf16[4,512]{1,0:T(4,128)(2,1)S(1)} %collective-permute-done.51.refs_1_, ...), custom_call_target="tpu_custom_call" | custom-call | flops 134217728 | bytes 8388608 | tf_op jit(solution)/shard_map/output/pallas_call | solution.py:43
  144.5 3.0 %collective-permute-done.55.refs_2_ = bf16[4,8192]{1,0:T(4,128)(2,1)S(1)} collective-permute-done((bf16[4,8192]{1,0:T(4,128)(2,1)S(1)}, bf16[4,8192]{1,0:T(4,128)(2,1)S(1)}, u32[]{:S(2)}, u32[]{:S(2)}) %collective-permute-start.55) | collective-permute-done | bytes 65568 | tf_op jit(solution)/shard_map/ppermute | solution.py:29
  148.3 2.2 %collective-permute-start.58 = (bf16[1,8192]{1,0:T(2,128)(2,1)S(1)}, bf16[1,8192]{1,0:T(2,128)(2,1)S(1)}, u32[]{:S(2)}, u32[]{:S(2)}) collective-permute-start(bf16[1,8192]{1,0:T(2,128)(2,1)S(1)} %get-tuple-element.127), channel_id=1, source_target_pairs={{0,8},{1,9},{2,10},{3,11},{4,12},{5,13},{6,14},{7,15},{8,0},{9,1},... | collective-permute-start | bytes 49160 | tf_op jit(solution)/shard_map/ppermute | solution.py:29
  150.5 2.2 %collective-permute-start.59 = (bf16[1,8192]{1,0:T(2,128)(2,1)S(1)}, bf16[1,8192]{1,0:T(2,128)(2,1)S(1)}, u32[]{:S(2)}, u32[]{:S(2)}) collective-permute-start(bf16[1,8192]{1,0:T(2,128)(2,1)S(1)} %get-tuple-element.128), channel_id=1, source_target_pairs={{0,12},{1,13},{2,14},{3,15},{4,8},{5,9},{6,10},{7,11},{8,4},{9,5},... | collective-permute-start | bytes 49160 | tf_op jit(solution)/shard_map/ppermute | solution.py:29
  153.3 2.9 %collective-permute-done.59.refs_3_ = bf16[1,8192]{1,0:T(2,128)(2,1)S(1)} collective-permute-done((bf16[1,8192]{1,0:T(2,128)(2,1)S(1)}, bf16[1,8192]{1,0:T(2,128)(2,1)S(1)}, u32[]{:S(2)}, u32[]{:S(2)}) %collective-permute-start.59) | collective-permute-done | bytes 16416 | tf_op jit(solution)/shard_map/ppermute | solution.py:29
  (148 shorter events, 66.6 us)
Async XLA Ops:
  2.5 7.0 %collective-permute-start.2 = (bf16[1,8320]{1,0:T(2,128)(2,1)S(1)}, bf16[1,8320]{1,0:T(2,128)(2,1)S(1)}, u32[]{:S(2)}, u32[]{:S(2)}) collective-permute-start(bf16[1,8320]{1,0:T(2,128)(2,1)S(1)} %first.1), channel_id=1, source_target_pairs={{0,12},{1,13},{2,14},{3,15},{4,8},{5,9},{6,10},{7,11},{8,4},{9,5},... | collective-permute-start | bytes 49928 | tf_op jit(solution)/shard_map/ppermute | solution.py:29
  7.6 4.8 %collective-permute-start.1 = (bf16[1,8320]{1,0:T(2,128)(2,1)S(1)}, bf16[1,8320]{1,0:T(2,128)(2,1)S(1)}, u32[]{:S(2)}, u32[]{:S(2)}) collective-permute-start(bf16[1,8320]{1,0:T(2,128)(2,1)S(1)} %first.1), channel_id=1, source_target_pairs={{0,8},{1,9},{2,10},{3,11},{4,12},{5,13},{6,14},{7,15},{8,0},{9,1},... | collective-permute-start | bytes 49928 | tf_op jit(solution)/shard_map/ppermute | solution.py:29
  7.6 4.8 %collective-permute-start = (bf16[1,8320]{1,0:T(2,128)(2,1)S(1)}, bf16[1,8320]{1,0:T(2,128)(2,1)S(1)}, u32[]{:S(2)}, u32[]{:S(2)}) collective-permute-start(bf16[1,8320]{1,0:T(2,128)(2,1)S(1)} %first.1), channel_id=1, source_target_pairs={{0,4},{1,5},{2,6},{3,7},{4,0},{5,1},{6,2},{7,3},{8,12},{9,13},{10,... | collective-permute-start | bytes 49928 | tf_op jit(solution)/shard_map/ppermute | solution.py:29
  12.7 5.8 %collective-permute-start.4 = (bf16[4,8320]{1,0:T(4,128)(2,1)S(1)}, bf16[4,8320]{1,0:T(4,128)(2,1)S(1)}, u32[]{:S(2)}, u32[]{:S(2)}) collective-permute-start(bf16[4,8320]{1,0:T(4,128)(2,1)S(1)} %pad_maximum_fusion.refs_0_), channel_id=1, source_target_pairs={{0,2},{1,3},{2,0},{3,1},{4,6},{5,7},{6,4},{7,5},{8,10},{9,11},{10,... | collective-permute-start | bytes 199688 | tf_op jit(solution)/shard_map/ppermute | solution.py:29
  21.8 5.4 %collective-permute-start.8 = (bf16[16,64]{1,0:T(8,128)(2,1)S(1)}, bf16[16,64]{1,0:T(8,128)(2,1)S(1)}, u32[]{:S(2)}, u32[]{:S(2)}) collective-permute-start(bf16[16,64]{1,0:T(8,128)(2,1)S(1)} %get-tuple-element.68), channel_id=1, source_target_pairs={{0,12},{1,13},{2,14},{3,15},{4,8},{5,9},{6,10},{7,11},{8,4},{9,5},... | collective-permute-start | bytes 6152 | tf_op jit(solution)/shard_map/ppermute | solution.py:29
  27.9 9.1 %collective-permute-start.11 = (bf16[16,64]{1,0:T(8,128)(2,1)S(1)}, bf16[16,64]{1,0:T(8,128)(2,1)S(1)}, u32[]{:S(2)}, u32[]{:S(2)}) collective-permute-start(bf16[16,64]{1,0:T(8,128)(2,1)S(1)} %add_convert_fusion.1.refs_0_), channel_id=1, source_target_pairs={{0,3},{1,2},{2,1},{3,0},{4,7},{5,6},{6,5},{7,4},{8,11},{9,10},{10,... | collective-permute-start | bytes 6152 | tf_op jit(solution)/shard_map/ppermute | solution.py:29
  27.9 9.0 %collective-permute-start.10 = (bf16[16,64]{1,0:T(8,128)(2,1)S(1)}, bf16[16,64]{1,0:T(8,128)(2,1)S(1)}, u32[]{:S(2)}, u32[]{:S(2)}) collective-permute-start(bf16[16,64]{1,0:T(8,128)(2,1)S(1)} %add_convert_fusion.1.refs_0_), channel_id=1, source_target_pairs={{0,2},{1,3},{2,0},{3,1},{4,6},{5,7},{6,4},{7,5},{8,10},{9,11},{10,... | collective-permute-start | bytes 6152 | tf_op jit(solution)/shard_map/ppermute | solution.py:29
  28.6 8.3 %collective-permute-start.9 = (bf16[16,64]{1,0:T(8,128)(2,1)S(1)}, bf16[16,64]{1,0:T(8,128)(2,1)S(1)}, u32[]{:S(2)}, u32[]{:S(2)}) collective-permute-start(bf16[16,64]{1,0:T(8,128)(2,1)S(1)} %add_convert_fusion.1.refs_0_), channel_id=1, source_target_pairs={{0,1},{1,0},{2,3},{3,2},{4,5},{5,4},{6,7},{7,6},{8,9},{9,8},{10,11... | collective-permute-start | bytes 6152 | tf_op jit(solution)/shard_map/ppermute | solution.py:29
  41.3 5.1 %collective-permute-start.15 = (bf16[4,640]{1,0:T(4,128)(2,1)S(1)}, bf16[4,640]{1,0:T(4,128)(2,1)S(1)}, u32[]{:S(2)}, u32[]{:S(2)}) collective-permute-start(bf16[4,640]{1,0:T(4,128)(2,1)S(1)} %get-tuple-element.78), channel_id=1, source_target_pairs={{0,4},{1,5},{2,6},{3,7},{4,0},{5,1},{6,2},{7,3},{8,12},{9,13},{10,... | collective-permute-start | bytes 15368 | tf_op jit(solution)/shard_map/ppermute | solution.py:29
  43.3 4.5 %collective-permute-start.16 = (bf16[4,640]{1,0:T(4,128)(2,1)S(1)}, bf16[4,640]{1,0:T(4,128)(2,1)S(1)}, u32[]{:S(2)}, u32[]{:S(2)}) collective-permute-start(bf16[4,640]{1,0:T(4,128)(2,1)S(1)} %get-tuple-element.79), channel_id=1, source_target_pairs={{0,8},{1,9},{2,10},{3,11},{4,12},{5,13},{6,14},{7,15},{8,0},{9,1},... | collective-permute-start | bytes 15368 | tf_op jit(solution)/shard_map/ppermute | solution.py:29
  44.4 5.4 %collective-permute-start.17 = (bf16[4,640]{1,0:T(4,128)(2,1)S(1)}, bf16[4,640]{1,0:T(4,128)(2,1)S(1)}, u32[]{:S(2)}, u32[]{:S(2)}) collective-permute-start(bf16[4,640]{1,0:T(4,128)(2,1)S(1)} %get-tuple-element.80), channel_id=1, source_target_pairs={{0,12},{1,13},{2,14},{3,15},{4,8},{5,9},{6,10},{7,11},{8,4},{9,5},... | collective-permute-start | bytes 15368 | tf_op jit(solution)/shard_map/ppermute | solution.py:29
  56.9 4.6 %collective-permute-start.22 = (bf16[4,512]{1,0:T(4,128)(2,1)S(1)}, bf16[4,512]{1,0:T(4,128)(2,1)S(1)}, u32[]{:S(2)}, u32[]{:S(2)}) collective-permute-start(bf16[4,512]{1,0:T(4,128)(2,1)S(1)} %get-tuple-element.87), channel_id=1, source_target_pairs={{0,8},{1,9},{2,10},{3,11},{4,12},{5,13},{6,14},{7,15},{8,0},{9,1},... | collective-permute-start | bytes 12296 | tf_op jit(solution)/shard_map/ppermute | solution.py:29
  58.8 5.4 %collective-permute-start.23 = (bf16[4,512]{1,0:T(4,128)(2,1)S(1)}, bf16[4,512]{1,0:T(4,128)(2,1)S(1)}, u32[]{:S(2)}, u32[]{:S(2)}) collective-permute-start(bf16[4,512]{1,0:T(4,128)(2,1)S(1)} %get-tuple-element.88), channel_id=1, source_target_pairs={{0,12},{1,13},{2,14},{3,15},{4,8},{5,9},{6,10},{7,11},{8,4},{9,5},... | collective-permute-start | bytes 12296 | tf_op jit(solution)/shard_map/ppermute | solution.py:29
  70.9 5.0 %collective-permute-start.25 = (bf16[4,8192]{1,0:T(4,128)(2,1)S(1)}, bf16[4,8192]{1,0:T(4,128)(2,1)S(1)}, u32[]{:S(2)}, u32[]{:S(2)}) collective-permute-start(bf16[4,8192]{1,0:T(4,128)(2,1)S(1)} %get-tuple-element.91), channel_id=1, source_target_pairs={{0,2},{1,3},{2,0},{3,1},{4,6},{5,7},{6,4},{7,5},{8,10},{9,11},{10,... | collective-permute-start | bytes 196616 | tf_op jit(solution)/shard_map/ppermute | solution.py:29
  71.7 4.7 %collective-permute-start.26 = (bf16[4,8192]{1,0:T(4,128)(2,1)S(1)}, bf16[4,8192]{1,0:T(4,128)(2,1)S(1)}, u32[]{:S(2)}, u32[]{:S(2)}) collective-permute-start(bf16[4,8192]{1,0:T(4,128)(2,1)S(1)} %get-tuple-element.92), channel_id=1, source_target_pairs={{0,3},{1,2},{2,1},{3,0},{4,7},{5,6},{6,5},{7,4},{8,11},{9,10},{10,... | collective-permute-start | bytes 196616 | tf_op jit(solution)/shard_map/ppermute | solution.py:29
  76.6 5.0 %collective-permute-start.28 = (bf16[1,8192]{1,0:T(2,128)(2,1)S(1)}, bf16[1,8192]{1,0:T(2,128)(2,1)S(1)}, u32[]{:S(2)}, u32[]{:S(2)}) collective-permute-start(bf16[1,8192]{1,0:T(2,128)(2,1)S(1)} %get-tuple-element.95), channel_id=1, source_target_pairs={{0,8},{1,9},{2,10},{3,11},{4,12},{5,13},{6,14},{7,15},{8,0},{9,1},... | collective-permute-start | bytes 49160 | tf_op jit(solution)/shard_map/ppermute | solution.py:29
  79.6 5.7 %collective-permute-start.29 = (bf16[1,8192]{1,0:T(2,128)(2,1)S(1)}, bf16[1,8192]{1,0:T(2,128)(2,1)S(1)}, u32[]{:S(2)}, u32[]{:S(2)}) collective-permute-start(bf16[1,8192]{1,0:T(2,128)(2,1)S(1)} %get-tuple-element.96), channel_id=1, source_target_pairs={{0,12},{1,13},{2,14},{3,15},{4,8},{5,9},{6,10},{7,11},{8,4},{9,5},... | collective-permute-start | bytes 49160 | tf_op jit(solution)/shard_map/ppermute | solution.py:29
  85.7 5.8 %collective-permute-start.32 = (bf16[1,8192]{1,0:T(2,128)(2,1)S(1)}, bf16[1,8192]{1,0:T(2,128)(2,1)S(1)}, u32[]{:S(2)}, u32[]{:S(2)}) collective-permute-start(bf16[1,8192]{1,0:T(2,128)(2,1)S(1)} %get-tuple-element.98), channel_id=1, source_target_pairs={{0,12},{1,13},{2,14},{3,15},{4,8},{5,9},{6,10},{7,11},{8,4},{9,5},... | collective-permute-start | bytes 49160 | tf_op jit(solution)/shard_map/ppermute | solution.py:29
  87.0 5.2 %collective-permute-start.31 = (bf16[1,8192]{1,0:T(2,128)(2,1)S(1)}, bf16[1,8192]{1,0:T(2,128)(2,1)S(1)}, u32[]{:S(2)}, u32[]{:S(2)}) collective-permute-start(bf16[1,8192]{1,0:T(2,128)(2,1)S(1)} %get-tuple-element.98), channel_id=1, source_target_pairs={{0,8},{1,9},{2,10},{3,11},{4,12},{5,13},{6,14},{7,15},{8,0},{9,1},... | collective-permute-start | bytes 49160 | tf_op jit(solution)/shard_map/ppermute | solution.py:29
  87.0 5.3 %collective-permute-start.30 = (bf16[1,8192]{1,0:T(2,128)(2,1)S(1)}, bf16[1,8192]{1,0:T(2,128)(2,1)S(1)}, u32[]{:S(2)}, u32[]{:S(2)}) collective-permute-start(bf16[1,8192]{1,0:T(2,128)(2,1)S(1)} %get-tuple-element.98), channel_id=1, source_target_pairs={{0,4},{1,5},{2,6},{3,7},{4,0},{5,1},{6,2},{7,3},{8,12},{9,13},{10,... | collective-permute-start | bytes 49160 | tf_op jit(solution)/shard_map/ppermute | solution.py:29
  92.6 5.0 %collective-permute-start.34 = (bf16[4,8192]{1,0:T(4,128)(2,1)S(1)}, bf16[4,8192]{1,0:T(4,128)(2,1)S(1)}, u32[]{:S(2)}, u32[]{:S(2)}) collective-permute-start(bf16[4,8192]{1,0:T(4,128)(2,1)S(1)} %pad_maximum_fusion.1.refs_0_), channel_id=1, source_target_pairs={{0,2},{1,3},{2,0},{3,1},{4,6},{5,7},{6,4},{7,5},{8,10},{9,11},{10,... | collective-permute-start | bytes 196616 | tf_op jit(solution)/shard_map/ppermute | solution.py:29
  98.4 5.5 %collective-permute-start.38 = (bf16[16,64]{1,0:T(8,128)(2,1)S(1)}, bf16[16,64]{1,0:T(8,128)(2,1)S(1)}, u32[]{:S(2)}, u32[]{:S(2)}) collective-permute-start(bf16[16,64]{1,0:T(8,128)(2,1)S(1)} %get-tuple-element.99), channel_id=1, source_target_pairs={{0,12},{1,13},{2,14},{3,15},{4,8},{5,9},{6,10},{7,11},{8,4},{9,5},... | collective-permute-start | bytes 6152 | tf_op jit(solution)/shard_map/ppermute | solution.py:29
  105.2 8.4 %collective-permute-start.41 = (bf16[16,64]{1,0:T(8,128)(2,1)S(1)}, bf16[16,64]{1,0:T(8,128)(2,1)S(1)}, u32[]{:S(2)}, u32[]{:S(2)}) collective-permute-start(bf16[16,64]{1,0:T(8,128)(2,1)S(1)} %add_convert_fusion.refs_0_), channel_id=1, source_target_pairs={{0,3},{1,2},{2,1},{3,0},{4,7},{5,6},{6,5},{7,4},{8,11},{9,10},{10,... | collective-permute-start | bytes 6152 | tf_op jit(solution)/shard_map/ppermute | solution.py:29
  105.2 8.4 %collective-permute-start.40 = (bf16[16,64]{1,0:T(8,128)(2,1)S(1)}, bf16[16,64]{1,0:T(8,128)(2,1)S(1)}, u32[]{:S(2)}, u32[]{:S(2)}) collective-permute-start(bf16[16,64]{1,0:T(8,128)(2,1)S(1)} %add_convert_fusion.refs_0_), channel_id=1, source_target_pairs={{0,2},{1,3},{2,0},{3,1},{4,6},{5,7},{6,4},{7,5},{8,10},{9,11},{10,... | collective-permute-start | bytes 6152 | tf_op jit(solution)/shard_map/ppermute | solution.py:29
  106.3 7.3 %collective-permute-start.39 = (bf16[16,64]{1,0:T(8,128)(2,1)S(1)}, bf16[16,64]{1,0:T(8,128)(2,1)S(1)}, u32[]{:S(2)}, u32[]{:S(2)}) collective-permute-start(bf16[16,64]{1,0:T(8,128)(2,1)S(1)} %add_convert_fusion.refs_0_), channel_id=1, source_target_pairs={{0,1},{1,0},{2,3},{3,2},{4,5},{5,4},{6,7},{7,6},{8,9},{9,8},{10,11... | collective-permute-start | bytes 6152 | tf_op jit(solution)/shard_map/ppermute | solution.py:29
  119.6 4.5 %collective-permute-start.46 = (bf16[4,640]{1,0:T(4,128)(2,1)S(1)}, bf16[4,640]{1,0:T(4,128)(2,1)S(1)}, u32[]{:S(2)}, u32[]{:S(2)}) collective-permute-start(bf16[4,640]{1,0:T(4,128)(2,1)S(1)} %get-tuple-element.109), channel_id=1, source_target_pairs={{0,8},{1,9},{2,10},{3,11},{4,12},{5,13},{6,14},{7,15},{8,0},{9,1},... | collective-permute-start | bytes 15368 | tf_op jit(solution)/shard_map/ppermute | solution.py:29
  120.6 5.4 %collective-permute-start.47 = (bf16[4,640]{1,0:T(4,128)(2,1)S(1)}, bf16[4,640]{1,0:T(4,128)(2,1)S(1)}, u32[]{:S(2)}, u32[]{:S(2)}) collective-permute-start(bf16[4,640]{1,0:T(4,128)(2,1)S(1)} %get-tuple-element.110), channel_id=1, source_target_pairs={{0,12},{1,13},{2,14},{3,15},{4,8},{5,9},{6,10},{7,11},{8,4},{9,5},... | collective-permute-start | bytes 15368 | tf_op jit(solution)/shard_map/ppermute | solution.py:29
  131.2 4.6 %collective-permute-start.52 = (bf16[4,512]{1,0:T(4,128)(2,1)S(1)}, bf16[4,512]{1,0:T(4,128)(2,1)S(1)}, u32[]{:S(2)}, u32[]{:S(2)}) collective-permute-start(bf16[4,512]{1,0:T(4,128)(2,1)S(1)} %get-tuple-element.119), channel_id=1, source_target_pairs={{0,8},{1,9},{2,10},{3,11},{4,12},{5,13},{6,14},{7,15},{8,0},{9,1},... | collective-permute-start | bytes 12296 | tf_op jit(solution)/shard_map/ppermute | solution.py:29
  133.9 5.4 %collective-permute-start.53 = (bf16[4,512]{1,0:T(4,128)(2,1)S(1)}, bf16[4,512]{1,0:T(4,128)(2,1)S(1)}, u32[]{:S(2)}, u32[]{:S(2)}) collective-permute-start(bf16[4,512]{1,0:T(4,128)(2,1)S(1)} %get-tuple-element.120), channel_id=1, source_target_pairs={{0,12},{1,13},{2,14},{3,15},{4,8},{5,9},{6,10},{7,11},{8,4},{9,5},... | collective-permute-start | bytes 12296 | tf_op jit(solution)/shard_map/ppermute | solution.py:29
  142.6 4.9 %collective-permute-start.55 = (bf16[4,8192]{1,0:T(4,128)(2,1)S(1)}, bf16[4,8192]{1,0:T(4,128)(2,1)S(1)}, u32[]{:S(2)}, u32[]{:S(2)}) collective-permute-start(bf16[4,8192]{1,0:T(4,128)(2,1)S(1)} %get-tuple-element.123), channel_id=1, source_target_pairs={{0,2},{1,3},{2,0},{3,1},{4,6},{5,7},{6,4},{7,5},{8,10},{9,11},{10,... | collective-permute-start | bytes 196616 | tf_op jit(solution)/shard_map/ppermute | solution.py:29
  148.3 5.0 %collective-permute-start.58 = (bf16[1,8192]{1,0:T(2,128)(2,1)S(1)}, bf16[1,8192]{1,0:T(2,128)(2,1)S(1)}, u32[]{:S(2)}, u32[]{:S(2)}) collective-permute-start(bf16[1,8192]{1,0:T(2,128)(2,1)S(1)} %get-tuple-element.127), channel_id=1, source_target_pairs={{0,8},{1,9},{2,10},{3,11},{4,12},{5,13},{6,14},{7,15},{8,0},{9,1},... | collective-permute-start | bytes 49160 | tf_op jit(solution)/shard_map/ppermute | solution.py:29
  150.5 5.7 %collective-permute-start.59 = (bf16[1,8192]{1,0:T(2,128)(2,1)S(1)}, bf16[1,8192]{1,0:T(2,128)(2,1)S(1)}, u32[]{:S(2)}, u32[]{:S(2)}) collective-permute-start(bf16[1,8192]{1,0:T(2,128)(2,1)S(1)} %get-tuple-element.128), channel_id=1, source_target_pairs={{0,12},{1,13},{2,14},{3,15},{4,8},{5,9},{6,10},{7,11},{8,4},{9,5},... | collective-permute-start | bytes 49160 | tf_op jit(solution)/shard_map/ppermute | solution.py:29
  (43 other events, 358.5 us)

commit v3 on v2

v3 whole, which is shorter than its diff:
```python
import functools
import math

import jax
import jax.numpy as jnp
from jax import lax
from jax.experimental import pallas as pl
from jax.experimental.pallas import tpu as pltpu
from jax.sharding import PartitionSpec as P

H = 64
KVH = 8
HD = 128
STEPS = 2
GROUP = H // KVH
EPS = 1e-05
AXIS = "replica"
LANES = 128
LAST = (((1,), (1,)), ((), ()))
FIRST = (((0,), (0,)), ((), ()))

CORES = 2


def sibling(block, count):
    return lax.ppermute(block, AXIS, [(i, i ^ 1) for i in range(count)])


def chips_swap(blocks, count):
    groups = [[i for i in range(count) if i % CORES == c] for c in range(CORES)]
    return lax.all_to_all(
        blocks, AXIS, split_axis=0, concat_axis=0, axis_index_groups=groups, tiled=True
    )


def call(body, outs, name, scratch=(), vmem=32 << 20, flops=1 << 20, moved=1 << 18):
    def run(*operands, specs=None):
        specs = specs or [pltpu.VMEM] * len(operands)
        return pl.pallas_call(
            body,
            out_shape=outs,
            in_specs=[pl.BlockSpec(memory_space=s) for s in specs],
            out_specs=jax.tree.map(lambda _: pl.BlockSpec(memory_space=pltpu.VMEM), outs),
            scratch_shapes=list(scratch),
            compiler_params=pltpu.CompilerParams(vmem_limit_bytes=vmem),
            cost_estimate=pl.CostEstimate(flops=flops, bytes_accessed=moved, transcendentals=0),
            name=name,
        )(*operands)

    return run


def shape(dims, dtype=jnp.bfloat16):
    return jax.ShapeDtypeStruct(dims, dtype)


def iota(dims, axis):
    return lax.broadcasted_iota(jnp.int32, dims, axis)


def dot(a, b, contract=(((1,), (0,)), ((), ()))):
    return lax.dot_general(a, b, contract, preferred_element_type=jnp.float32)


def normalized(hidden, scale):
    factor = lax.rsqrt(jnp.mean(hidden * hidden, axis=-1, keepdims=True) + EPS)
    return (hidden * factor * scale).astype(jnp.bfloat16)


FOLD = 8


def folded(out_ref, row):
    wide = row.shape[1] // FOLD
    for k in range(out_ref.shape[0]):
        for i in range(FOLD):
            out_ref[k, i : i + 1, :wide] = row[:, i * wide : (i + 1) * wide].astype(out_ref.dtype)


def unfolded(held, ref, start, chips, wide):
    for k in range(chips):
        block = ref[k, :, :wide].astype(jnp.float32)
        for i in range(FOLD):
            held[start + k : start + k + 1, i * wide : (i + 1) * wide] = block[i : i + 1]


def slot_origin(core, dims, axis):
    slot = iota(dims, axis)
    chips = dims[axis] // CORES
    return (slot % chips) * CORES + (core ^ (slot // chips))


def pair_origin(core, dims, axis):
    slot = iota(dims, axis)
    return slot ^ core


def first_kernel(hidden_ref, scale_ref, adapter_ref, out_ref):
    hidden = hidden_ref[...].astype(jnp.float32)
    folded(out_ref, normalized(hidden, scale_ref[...].astype(jnp.float32)).astype(jnp.float32))
    digit = iota((FOLD, LANES), 1)
    adapter = adapter_ref[0]
    high, low = adapter // 256, adapter % 256
    digits = jnp.where(digit == 0, low, jnp.where(digit == 1, high, 0)).astype(jnp.float32)
    wide = hidden_ref.shape[1] // FOLD
    for k in range(out_ref.shape[0]):
        out_ref[k, :, wide:] = digits.astype(jnp.bfloat16)


def low_kernel(chips, own_ref, other_ref, me_ref, member_ref, down_ref, rows_ref, low_ref, away_ref, held):
    count = chips * CORES
    wide = rows_ref.shape[1] // FOLD
    unfolded(held, own_ref, 0, chips, wide)
    unfolded(held, other_ref, chips, chips, wide)
    rows = held[...].astype(jnp.bfloat16)
    rows_ref[...] = rows
    kept = down_ref.shape[0]
    low = jnp.zeros((count, down_ref.shape[1]), jnp.float32)
    for index in range(kept):
        part = dot(rows, down_ref[index], LAST)
        low = jnp.where(member_ref[:, index : index + 1] > 0, part, low)
    low_ref[...] = low.astype(jnp.bfloat16)
    away_ref[...] = jnp.concatenate([low[chips:], low[:chips]], axis=0).astype(jnp.bfloat16)


def member_kernel(chips, own_ref, other_ref, me_ref, storage_ref, member_ref, adapter_ref, held):
    kept = member_ref.shape[1]
    count = chips * CORES
    wide = own_ref.shape[2] - LANES
    for k in range(chips):
        held[k : k + 1, :] = own_ref[k, :, wide:].astype(jnp.float32)[0:1]
        held[chips + k : chips + k + 1, :] = other_ref[k, :, wide:].astype(jnp.float32)[0:1]
    adapter = (held[:, 0:1] + 256.0 * held[:, 1:2]).astype(jnp.int32)
    adapter_ref[...] = adapter
    table = storage_ref.shape[1]
    chosen = jnp.where(iota((count, table), 1) == adapter, storage_ref[...], 0)
    storage = jnp.sum(chosen.astype(jnp.float32), axis=1, keepdims=True).astype(jnp.int32)
    member_ref[...] = (storage - me_ref[0] * kept == iota((count, kept), 1)).astype(jnp.int32)


def spread_kernel(own_ref, other_ref, out_ref):
    total = own_ref[...].astype(jnp.float32) + other_ref[...].astype(jnp.float32)
    for k in range(out_ref.shape[0]):
        out_ref[k] = total.astype(out_ref.dtype)


def project_kernel(rows_ref, query_hbm, fresh_hbm, query_ref, fresh_ref, query_w, fresh_w, sems):
    chunks = sems.shape[1]
    deep = query_w.shape[0] // chunks
    copies = []
    for c in range(chunks):
        part = pl.ds(c * deep, deep)
        copies.append(
            (
                pltpu.make_async_copy(query_hbm.at[part], query_w.at[part], sems.at[0, c]),
                pltpu.make_async_copy(fresh_hbm.at[part], fresh_w.at[part], sems.at[1, c]),
            )
        )
    for pair in copies:
        for copy in pair:
            copy.start()
    query = jnp.zeros(query_ref.shape, jnp.float32)
    fresh = jnp.zeros(fresh_ref.shape, jnp.float32)
    for c, pair in enumerate(copies):
        for copy in pair:
            copy.wait()
        part = slice(c * deep, (c + 1) * deep)
        rows = rows_ref[:, part]
        query = query + dot(rows, query_w[part, :])
        fresh = fresh + dot(rows, fresh_w[part, :])
    query_ref[...] = query
    fresh_ref[...] = fresh


def up_kernel(chips, low_ref, query_ref, fresh_ref, up_ref, own_ref, away_ref):
    count = chips * CORES
    rank = low_ref.shape[2]
    columns = query_ref.shape[1]
    low = low_ref[0].astype(jnp.float32)
    for k in range(1, chips):
        low = low + low_ref[k].astype(jnp.float32)
    low = low.astype(jnp.bfloat16)
    wide = count * rank
    repeat = (iota((rank, wide), 1) % rank == iota((rank, wide), 0)).astype(jnp.bfloat16)
    spread = jnp.where(
        iota((count, wide), 1) // rank == iota((count, wide), 0), dot(low, repeat), 0.0
    ).astype(jnp.bfloat16)
    query = query_ref[...] + dot(spread, up_ref[...])
    fresh = fresh_ref[...]
    for ref, part in ((own_ref, slice(0, chips)), (away_ref, slice(chips, count))):
        ref[:, :columns] = query[part].astype(jnp.bfloat16)
        ref[:, columns:] = fresh[part].astype(jnp.bfloat16)


def pair_kernel(own_ref, other_ref, out_ref):
    own, other = own_ref[...].astype(jnp.float32), other_ref[...].astype(jnp.float32)
    for k in range(out_ref.shape[0]):
        out_ref[k] = jnp.concatenate([own[k : k + 1], other[k : k + 1]], axis=0).astype(out_ref.dtype)


def pieces_of(slots, select, whole, size):
    if size >= whole:
        each = size // whole
        total = None
        for c in range(each):
            part = dot(select(each, c), slots[:, c * whole : (c + 1) * whole])
            total = part if total is None else total + part
        return total
    return jnp.concatenate([dot(select(0, p), slots) for p in range(whole // size)], axis=1)


def attend_kernel(chips, columns, fresh_columns, first, *refs):
    pairs_ref, length_ref, me_ref, cache_hbm = refs[:4]
    refs = refs[4:]
    if not first:
        past, refs = refs[:2], refs[2:]
    own_ref, away_ref = refs[:2]
    refs = refs[2:]
    if first:
        keep, refs = refs[:2], refs[2:]
    held, scores, cache_ref, sems = refs
    copies = [
        pltpu.make_async_copy(cache_hbm.at[0, i], cache_ref.at[0, i], sems.at[i]) for i in range(2)
    ]
    for copy in copies:
        copy.start()
    count = chips * CORES
    cache = cache_ref.shape[2]
    core = me_ref[0] % CORES
    for k in range(chips):
        held[k * CORES : (k + 1) * CORES, :] = pairs_ref[k].astype(jnp.float32)
    slots = held[...].astype(jnp.bfloat16)
    origin = pair_origin(core, (H, count), 1)
    head = iota((H, count), 0)

    def query_pick(each, c):
        if each:
            return (head == origin * each + c).astype(jnp.bfloat16)
        return (head * (HD // columns) + c == origin).astype(jnp.bfloat16)

    def fresh_pick(offset):
        def pick(each, c):
            want = head // GROUP + offset
            if each:
                return (want == origin * each + c).astype(jnp.bfloat16)
            return (want * (HD // fresh_columns) + c == origin).astype(jnp.bfloat16)

        return pick

    query = pieces_of(slots[:, :columns], query_pick, HD, columns)
    fresh = slots[:, columns:]
    new = [
        (
            pieces_of(fresh, fresh_pick(0), HD, fresh_columns),
            pieces_of(fresh, fresh_pick(KVH), HD, fresh_columns),
        )
    ]
    if first:
        keep[0][...], keep[1][...] = new[0]
    else:
        new.insert(0, (past[0][...], past[1][...]))
    scale = 1.0 / math.sqrt(HD)
    copies[0].wait()
    for j in range(KVH):
        rows = slice(j * GROUP, (j + 1) * GROUP)
        scores[rows, :] = dot(
            query[rows].astype(jnp.bfloat16), cache_ref[0, 0, :, j * HD : (j + 1) * HD], LAST
        )
    in_cache = iota((H, cache), 1) < length_ref[0]
    old = jnp.where(in_cache, scores[...] * scale, -jnp.inf)
    news = [jnp.sum(query * keys, axis=1, keepdims=True) * scale for keys, _ in new]
    peak = jnp.max(old, axis=1, keepdims=True)
    for score in news:
        peak = jnp.maximum(peak, score)
    old = jnp.exp(old - peak)
    news = [jnp.exp(score - peak) for score in news]
    total = jnp.sum(old, axis=1, keepdims=True)
    for score in news:
        total = total + score
    old = old / total
    extra = jnp.zeros((H, HD), jnp.float32)
    for score, (_, values) in zip(news, new):
        extra = extra + (score / total).astype(jnp.bfloat16).astype(jnp.float32) * values
    copies[1].wait()
    mixed = jnp.concatenate(
        [
            dot(
                old[j * GROUP : (j + 1) * GROUP].astype(jnp.bfloat16),
                cache_ref[0, 1, :, j * HD : (j + 1) * HD],
            )
            for j in range(KVH)
        ],
        axis=0,
    )
    mixed = (mixed + extra).astype(jnp.bfloat16)
    target = slot_origin(core, (count, H), 0)
    head = iota((count, H), 1)
    if columns >= HD:
        each = columns // HD
        out = [dot((head == target * each + c).astype(jnp.bfloat16), mixed) for c in range(each)]
        out = out[0] if each == 1 else jnp.concatenate(out, axis=1)
    else:
        parts = HD // columns
        out = jnp.zeros((count, columns), jnp.float32)
        for p in range(parts):
            pick = (head * parts + p == target).astype(jnp.bfloat16)
            out = out + dot(pick, mixed[:, p * columns : (p + 1) * columns])
    own_ref[...] = out[:chips].astype(jnp.bfloat16)
    away_ref[...] = out[chips:].astype(jnp.bfloat16)


def output_kernel(chips, pairs_ref, weight_hbm, own_ref, away_ref, held, weight, sems):
    chunks = sems.shape[0]
    wide = weight.shape[1] // chunks
    copies = [
        pltpu.make_async_copy(
            weight_hbm.at[:, pl.ds(c * wide, wide)], weight.at[:, pl.ds(c * wide, wide)], sems.at[c]
        )
        for c in range(chunks)
    ]
    for copy in copies:
        copy.start()
    for k in range(chips):
        pair = pairs_ref[k].astype(jnp.float32)
        for l in range(CORES):
            held[l * chips + k : l * chips + k + 1, :] = pair[l : l + 1]
    rows = held[...].astype(jnp.bfloat16)
    for c, copy in enumerate(copies):
        copy.wait()
        part = slice(c * wide, (c + 1) * wide)
        out = dot(rows, weight[:, part])
        own_ref[:, part] = out[:chips]
        away_ref[:, part] = out[chips:].astype(jnp.bfloat16)


def partial_kernel(own_ref, other_ref, out_ref):
    total = own_ref[...] + other_ref[...].astype(jnp.float32)
    wide = out_ref.shape[2]
    for k in range(out_ref.shape[0]):
        for i in range(FOLD):
            out_ref[k, i : i + 1, :] = total[k : k + 1, i * wide : (i + 1) * wide].astype(
                out_ref.dtype
            )


def finish_kernel(last, parts_ref, hidden_ref, scale_ref, out_ref, *spread):
    total = parts_ref[0].astype(jnp.float32)
    for k in range(1, parts_ref.shape[0]):
        total = total + parts_ref[k].astype(jnp.float32)
    wide = parts_ref.shape[2]
    total = jnp.concatenate([total[i : i + 1] for i in range(FOLD)], axis=1)
    total = total.astype(jnp.bfloat16).astype(jnp.float32)
    hidden = (hidden_ref[...].astype(jnp.float32) + total).astype(jnp.bfloat16)
    out_ref[...] = hidden
    if not last:
        hidden = normalized(hidden.astype(jnp.float32), scale_ref[...].astype(jnp.float32))
        folded(spread[0], hidden.astype(jnp.float32))


def shards(
    hidden_state_input,
    attention_norm_scale,
    query_weight,
    key_value_weight,
    output_weight,
    adapter_down_weight,
    adapter_up_weight,
    row_adapter_index,
    adapter_storage_index,
    cache_length_per_row,
    key_value_cache,
):
    count = lax.axis_size(AXIS)
    chips = count // CORES
    kept, width, rank = adapter_down_weight.shape
    columns = query_weight.shape[1]
    fresh_columns = key_value_weight.shape[1]
    message = columns + fresh_columns
    smem, vmem = pltpu.SMEM, pltpu.VMEM
    large = 52 << 20
    me = lax.axis_index(AXIS).astype(jnp.int32).reshape(1)
    down = adapter_down_weight.transpose(0, 2, 1)
    scale = attention_norm_scale[None]
    storage = adapter_storage_index[None]

    def exchange(own, away):
        wide = own.shape[1]
        other = sibling(away, count)
        pairs = call(pair_kernel, shape((chips, CORES, wide)), "pair")(own, other)
        return chips_swap(pairs, count)

    hidden = hidden_state_input
    carried = call(first_kernel, shape((chips, FOLD, width // FOLD + LANES)), "first")(
        hidden, scale, row_adapter_index, specs=[vmem, vmem, smem]
    )
    results = []
    past = ()
    for step in range(STEPS):
        first, last = step == 0, step == STEPS - 1
        own = chips_swap(carried, count)
        other = sibling(own, count)
        if first:
            member, adapter = call(
                functools.partial(member_kernel, chips),
                [shape((count, kept), jnp.int32), shape((count, 1), jnp.int32)],
                "member",
                [pltpu.VMEM((count, LANES), jnp.float32)],
            )(own, other, me, storage, specs=[vmem, vmem, smem, vmem])
            up_of = adapter_up_weight[adapter[:, 0]].reshape(count * rank, columns)
        rows, low, away = call(
            functools.partial(low_kernel, chips),
            [shape((count, width)), shape((count, rank)), shape((count, rank))],
            "low",
            [pltpu.VMEM((count, width), jnp.float32)],
            moved=2 << 20,
        )(own, other, me, member, down, specs=[vmem, vmem, smem, vmem, vmem])
        low = call(spread_kernel, shape((chips, count, rank)), "spread")(low, sibling(away, count))
        low = chips_swap(low, count)
        chunks = 8
        query, fresh = call(
            project_kernel,
            [shape((count, columns), jnp.float32), shape((count, fresh_columns), jnp.float32)],
            "project",
            [
                pltpu.VMEM((width, columns), jnp.bfloat16),
                pltpu.VMEM((width, fresh_columns), jnp.bfloat16),
                pltpu.SemaphoreType.DMA((2, chunks)),
            ],
            vmem=large,
            flops=2 * count * width * message,
            moved=2 * width * message,
        )(rows, query_weight, key_value_weight, specs=[vmem, pl.ANY, pl.ANY])
        own, away = call(
            functools.partial(up_kernel, chips), [shape((chips, message))] * 2, "up"
        )(low, query, fresh, up_of)

        pairs = exchange(own, away)
        outs = [shape((chips, columns))] * 2
        if first:
            outs = outs + [shape((H, HD), jnp.float32)] * 2
        outs = call(
            functools.partial(attend_kernel, chips, columns, fresh_columns, first),
            outs,
            "attend",
            [
                pltpu.VMEM((count, message), jnp.float32),
                pltpu.VMEM((H, key_value_cache.shape[2]), jnp.float32),
                pltpu.VMEM(key_value_cache.shape, jnp.bfloat16),
                pltpu.SemaphoreType.DMA((2,)),
            ],
            vmem=large,
            moved=2 << 20,
        )(
            pairs,
            cache_length_per_row,
            me,
            key_value_cache,
            *past,
            specs=[vmem, smem, smem, pl.ANY] + [vmem] * len(past),
        )
        if first:
            past = tuple(outs[2:])

        pairs = exchange(outs[0], outs[1])
        chunks = 8
        own, away = call(
            functools.partial(output_kernel, chips),
            [shape((chips, width), jnp.float32), shape((chips, width))],
            "output",
            [
                pltpu.VMEM((count, columns), jnp.float32),
                pltpu.VMEM((columns, width), jnp.bfloat16),
                pltpu.SemaphoreType.DMA((chunks,)),
            ],
            vmem=large,
            flops=2 * count * width * columns,
            moved=2 * width * columns,
        )(pairs, output_weight, specs=[vmem, pl.ANY])

        parts = call(partial_kernel, shape((chips, FOLD, width // FOLD)), "partial")(
            own, sibling(away, count)
        )
        parts = chips_swap(parts, count)
        outs = [shape((1, width))]
        if not last:
            outs = outs + [shape((chips, FOLD, width // FOLD))]
        outs = call(functools.partial(finish_kernel, last), outs, "finish")(parts, hidden, scale)
        hidden = outs[0]
        results.append(hidden)
        if not last:
            carried = outs[1]
    return jnp.stack(results)


def solution(mesh):
    in_specs = (
        P(("groups", "replica"), None),
        P(),
        P(None, "replica"),
        P(None, "replica"),
        P("replica", None),
        P("replica", None, None),
        P(None, None, "replica"),
        P(("groups", "replica")),
        P(),
        P(("groups", "replica")),
        P(("groups", "replica"), None, None, None),
    )
    out_specs = P(None, ("groups", "replica"), None)
    return jax.shard_map(shards, mesh=mesh, in_specs=in_specs, out_specs=out_specs, check_vma=False)
```

time: 157 us -> 143 us (0.911)
  blocking collectives: 0 us -> 72.9 us
  starting transfers between devices: 64.7 us -> 12.4 us
  waiting for transfers between devices: 54.9 us -> 21 us
  local copies, waits for them, and re-layouts: 16.1 us -> 8.03 us
  Pallas kernels: 18.4 us -> 25.1 us
    all_to_all x0 -> x7, blocking collectives: none -> 72.9 us  [chips_swap(): lax.all_to_all(blocks, AXIS, split_axis=0, concat_axis=0, axis_index_grou...]
    ppermute x60 -> x10, starting transfers between devices: 64.7 us -> 0.64 us  [sibling(): return lax.ppermute(block, AXIS, [(i, i ^ 1) for i in range(count)])]
    ppermute x60 -> x10, waiting for transfers between devices: 54.9 us -> 12 us  [sibling(): return lax.ppermute(block, AXIS, [(i, i ^ 1) for i in range(count)])]
    all_to_all x0 -> x3, starting transfers between devices: none -> 11.7 us  [chips_swap(): lax.all_to_all(blocks, AXIS, split_axis=0, concat_axis=0, axis_index_grou...]
    all_to_all x0 -> x3, waiting for transfers between devices: none -> 9.01 us  [chips_swap(): lax.all_to_all(blocks, AXIS, split_axis=0, concat_axis=0, axis_index_grou...]
    unnamed x30 -> x24, local copies, waits for them, and re-layouts: 14.8 us -> 6.68 us
    pallas_call x20 -> x22, Pallas kernels: 18.4 us -> 25.1 us  [run(): pl.pallas_call(body, out_shape=outs, in_specs=[pl.BlockSpec(memory_space=...]
  transfers between devices with their start and end apart: 60 -> 13, of which waited for: 38 -> 13; matrix products, arithmetic and copies ran while one was open for 0% -> 1% of each run, Pallas kernels for 4% -> 6%
where the time goes in v3:
time: 143 us; the launch traced here: 142 us
  blocking collectives  72.9 us (51%)
  Pallas kernels  25.1 us (18%)
  waiting for transfers between devices  21 us (15%)
  starting transfers between devices  12.4 us (9%)
  local copies, waits for them, and re-layouts  8.03 us (6%)
  between operations  1.68 us (1%)
    all_to_all x7, blocking collectives, chips_swap(): lax.all_to_all(blocks, AXIS, split_axis=0, concat_axis=0, axis_index_grou...  72.9 us
    pallas_call x22, Pallas kernels, run(): pl.pallas_call(body, out_shape=outs, in_specs=[pl.BlockSpec(memory_space=...  25.1 us
    ppermute x10, waiting for transfers between devices, sibling(): return lax.ppermute(block, AXIS, [(i, i ^ 1) for i in range(count)])  12 us
    all_to_all x3, starting transfers between devices, chips_swap(): lax.all_to_all(blocks, AXIS, split_axis=0, concat_axis=0, axis_index_grou...  11.7 us
    all_to_all x3, waiting for transfers between devices, chips_swap(): lax.all_to_all(blocks, AXIS, split_axis=0, concat_axis=0, axis_index_grou...  9.01 us
    unnamed x24, local copies, waits for them, and re-layouts  6.68 us
  transfers between devices with their start and end apart: 13, of which 13 were waited for; matrix products, arithmetic and copies ran while one was open for 1% of the time, Pallas kernels for 6%

profile of v3, /device:TPU:0, one launch (start us, length us, event | category | flops | bytes accessed | tf_op | source)
XLA Modules:
  0.0 141.8 jit_solution(16974405145766442129)
XLA Ops:
  2.6 14.5 %all_to_all.50.own_ref = bf16[8,8,1152]{2,1,0:T(8,128)(2,1)S(1)} all-to-all(bf16[8,8,1152]{2,1,0:T(8,128)(2,1)S(1)} %first.1), channel_id=1, replica_groups={{0,2,4,6,8,10,12,14},{1,3,5,7,9,11,13,15},{16,18,20,22,24,26,28,30},{17..., dimensions={0} | all-to-all | bytes 294912 | tf_op jit(solution)/shard_map/all_to_all | solution.py:31
  17.1 1.4 collective-permute-done.other_ref
  19.3 1.6 %copy-done.1 = bf16[2,8192,64]{1,2,0:T(8,128)(2,1)S(1)} copy-done((bf16[2,8192,64]{1,2,0:T(8,128)(2,1)S(1)}, bf16[2,8192,64]{1,2,0:T(8,128)(2,1)}, u32[]{:S(2)}) %copy-start.1) | copy-done | bytes 2097176
  21.9 0.9 collective-permute-done.1.other_ref
  23.6 3.3 %all-to-all-start.1 = ((bf16[8,2,512]{2,1,0:T(2,128)(2,1)}), bf16[8,2,512]{2,1,0:T(2,128)(2,1)S(1)}, u32[]{:S(2)}, u32[]{:S(2)}) async-start(bf16[8,2,512]{2,1,0:T(2,128)(2,1)} %reshape.17), calls=%async_computation.1 | async-start | bytes 32768 | tf_op jit(solution)/shard_map/all_to_all | solution.py:31
  27.6 4.4 %project.2 = (f32[16,512]{1,0:T(8,128)S(1)}, f32[16,128]{1,0:T(8,128)S(1)}) custom-call(bf16[16,8192]{1,0:T(8,128)(2,1)S(1)} %get-tuple-element.36.rows_ref, bf16[8192,512]{1,0:T(8,128)(2,1)} %query_hbm.3, bf16[8192,128]{1,0:T(8,128)(2,1)} %fresh_hbm.3), custom_call_target="tpu_custom_call" | custom-call | flops 167772160 | bytes 10485760 | tf_op jit(solution)/shard_map/project/pallas_call | solution.py:39
  31.9 1.5 %all-to-all-done.1 = bf16[8,2,512]{2,1,0:T(2,128)(2,1)S(1)} async-done(((bf16[8,2,512]{2,1,0:T(2,128)(2,1)}), bf16[8,2,512]{2,1,0:T(2,128)(2,1)S(1)}, u32[]{:S(2)}, u32[]{:S(2)}) %all-to-all-start.1) | async-done | bytes 16416 | tf_op jit(solution)/shard_map/all_to_all | solution.py:31
  33.9 1.2 collective-permute-done.2.other_ref
  35.7 4.5 %all-to-all-start.2 = ((bf16[8,2,640]{2,1,0:T(2,128)(2,1)}), bf16[8,2,640]{2,1,0:T(2,128)(2,1)S(1)}, u32[]{:S(2)}, u32[]{:S(2)}) async-start(bf16[8,2,640]{2,1,0:T(2,128)(2,1)} %pair.4), calls=%async_computation.2 | async-start | bytes 40960 | tf_op jit(solution)/shard_map/all_to_all | solution.py:31
  40.8 6.0 %all-to-all-done.2.refs_0_ = bf16[8,2,640]{2,1,0:T(2,128)(2,1)S(1)} async-done(((bf16[8,2,640]{2,1,0:T(2,128)(2,1)}), bf16[8,2,640]{2,1,0:T(2,128)(2,1)S(1)}, u32[]{:S(2)}, u32[]{:S(2)}) %all-to-all-start.2) | async-done | bytes 20512 | tf_op jit(solution)/shard_map/all_to_all | solution.py:31
  46.7 2.3 %attend.2 = (bf16[8,512]{1,0:T(8,128)(2,1)S(1)}, bf16[8,512]{1,0:T(8,128)(2,1)S(1)}, f32[64,128]{1,0:T(8,128)S(1)}, f32[64,128]{1,0:T(8,128)S(1)}) custom-call(bf16[8,2,640]{2,1,0:T(2,128)(2,1)S(1)} %all-to-all-done.2.refs_0_, s32[1]{0:T(128)S(6)} %copy.13.refs_1_, s32[1]{0:T(128)} %bitcast.me_ref.refs_2_, bf16[1,2,512,1024]{3,2,1,0:T(8,128)(2,1)} %refs_3_.3), custom_call_target="tpu_custom_call" | custom-call | flops 1048576 | bytes 2097152 | tf_op jit(solution)/shard_map/attend/pallas_call | solution.py:39
  49.1 1.2 collective-permute-done.3.other_ref
  50.3 8.9 %all_to_all.51.pairs_ref = bf16[8,2,512]{2,1,0:T(2,128)(2,1)S(1)} all-to-all(bf16[8,2,512]{2,1,0:T(2,128)(2,1)S(1)} %pair.5), channel_id=1, replica_groups={{0,2,4,6,8,10,12,14},{1,3,5,7,9,11,13,15},{16,18,20,22,24,26,28,30},{17..., dimensions={0} | all-to-all | bytes 32768 | tf_op jit(solution)/shard_map/all_to_all | solution.py:31
  59.2 3.9 %output.2 = (f32[8,8192]{1,0:T(8,128)S(1)}, bf16[8,8192]{1,0:T(8,128)(2,1)S(1)}) custom-call(bf16[8,2,512]{2,1,0:T(2,128)(2,1)S(1)} %all_to_all.51.pairs_ref, bf16[512,8192]{1,0:T(8,128)(2,1)} %weight_hbm.3), custom_call_target="tpu_custom_call" | custom-call | flops 134217728 | bytes 8388608 | tf_op jit(solution)/shard_map/output/pallas_call | solution.py:39
  63.2 1.3 collective-permute-done.4.other_ref
  64.7 10.0 %all_to_all.52.parts_ref = bf16[8,8,1024]{2,1,0:T(8,128)(2,1)S(1)} all-to-all(bf16[8,8,1024]{2,1,0:T(8,128)(2,1)S(1)} %partial.2), channel_id=1, replica_groups={{0,2,4,6,8,10,12,14},{1,3,5,7,9,11,13,15},{16,18,20,22,24,26,28,30},{17..., dimensions={0} | all-to-all | bytes 262144 | tf_op jit(solution)/shard_map/all_to_all | solution.py:31
  75.1 9.8 %all_to_all.53.own_ref = bf16[8,8,1024]{2,1,0:T(8,128)(2,1)S(1)} all-to-all(bf16[8,8,1024]{2,1,0:T(8,128)(2,1)S(1)} %get-tuple-element.47), channel_id=1, replica_groups={{0,2,4,6,8,10,12,14},{1,3,5,7,9,11,13,15},{16,18,20,22,24,26,28,30},{17..., dimensions={0} | all-to-all | bytes 262144 | tf_op jit(solution)/shard_map/all_to_all | solution.py:31
  84.9 1.3 collective-permute-done.5.other_ref
  87.2 1.0 collective-permute-done.6.other_ref
  88.9 3.9 %all-to-all-start.6 = ((bf16[8,2,512]{2,1,0:T(2,128)(2,1)}), bf16[8,2,512]{2,1,0:T(2,128)(2,1)}, u32[]{:S(2)}, u32[]{:S(2)}) async-start(bf16[8,2,512]{2,1,0:T(2,128)(2,1)} %reshape.19), calls=%async_computation.6 | async-start | bytes 32768 | tf_op jit(solution)/shard_map/all_to_all | solution.py:31
  92.8 4.4 %project.3 = (f32[16,512]{1,0:T(8,128)S(1)}, f32[16,128]{1,0:T(8,128)S(1)}) custom-call(bf16[16,8192]{1,0:T(8,128)(2,1)S(1)} %get-tuple-element.50.rows_ref, bf16[8192,512]{1,0:T(8,128)(2,1)} %query_hbm.3, bf16[8192,128]{1,0:T(8,128)(2,1)} %fresh_hbm.3), custom_call_target="tpu_custom_call" | custom-call | flops 167772160 | bytes 10485760 | tf_op jit(solution)/shard_map/project/pallas_call | solution.py:39
  97.8 1.6 %all-to-all-done.6 = bf16[8,2,512]{2,1,0:T(2,128)(2,1)} async-done(((bf16[8,2,512]{2,1,0:T(2,128)(2,1)}), bf16[8,2,512]{2,1,0:T(2,128)(2,1)}, u32[]{:S(2)}, u32[]{:S(2)}) %all-to-all-start.6) | async-done | bytes 16416 | tf_op jit(solution)/shard_map/all_to_all | solution.py:31
  99.4 0.8 reshape.20.low_ref
  100.2 0.7 copy-done.8
  101.3 1.2 collective-permute-done.7.other_ref
  102.5 10.7 %all_to_all.54.refs_0_ = bf16[8,2,640]{2,1,0:T(2,128)(2,1)S(1)} all-to-all(bf16[8,2,640]{2,1,0:T(2,128)(2,1)S(1)} %pair.6), channel_id=1, replica_groups={{0,2,4,6,8,10,12,14},{1,3,5,7,9,11,13,15},{16,18,20,22,24,26,28,30},{17..., dimensions={0} | all-to-all | bytes 40960 | tf_op jit(solution)/shard_map/all_to_all | solution.py:31
  113.3 2.3 %attend.3 = (bf16[8,512]{1,0:T(8,128)(2,1)S(1)}, bf16[8,512]{1,0:T(8,128)(2,1)S(1)}) custom-call(bf16[8,2,640]{2,1,0:T(2,128)(2,1)S(1)} %all_to_all.54.refs_0_, s32[1]{0:T(128)S(6)} %copy.13.refs_1_, s32[1]{0:T(128)} %bitcast.me_ref.refs_2_, bf16[1,2,512,1024]{3,2,1,0:T(8,128)(2,1)} %refs_3_.3, f32[64,128]{1,0:T(8,128)S(1)} %get-tuple-element.55.refs_4_, ...), custom_call_target="tpu_custom_call" | custom-call | flops 1048576 | bytes 2097152 | tf_op jit(solution)/shard_map/attend/pallas_call | solution.py:39
  115.6 1.2 collective-permute-done.8.other_ref
  116.8 8.9 %all_to_all.55.pairs_ref = bf16[8,2,512]{2,1,0:T(2,128)(2,1)S(1)} all-to-all(bf16[8,2,512]{2,1,0:T(2,128)(2,1)S(1)} %pair.7), channel_id=1, replica_groups={{0,2,4,6,8,10,12,14},{1,3,5,7,9,11,13,15},{16,18,20,22,24,26,28,30},{17..., dimensions={0} | all-to-all | bytes 32768 | tf_op jit(solution)/shard_map/all_to_all | solution.py:31
  125.8 3.8 %output.3 = (f32[8,8192]{1,0:T(8,128)S(1)}, bf16[8,8192]{1,0:T(8,128)(2,1)S(1)}) custom-call(bf16[8,2,512]{2,1,0:T(2,128)(2,1)S(1)} %all_to_all.55.pairs_ref, bf16[512,8192]{1,0:T(8,128)(2,1)} %weight_hbm.3), custom_call_target="tpu_custom_call" | custom-call | flops 134217728 | bytes 8388608 | tf_op jit(solution)/shard_map/output/pallas_call | solution.py:39
  129.6 1.3 collective-permute-done.9.other_ref
  131.1 10.0 %all_to_all.56.parts_ref = bf16[8,8,1024]{2,1,0:T(8,128)(2,1)S(1)} all-to-all(bf16[8,8,1024]{2,1,0:T(8,128)(2,1)S(1)} %partial.3), channel_id=1, replica_groups={{0,2,4,6,8,10,12,14},{1,3,5,7,9,11,13,15},{16,18,20,22,24,26,28,30},{17..., dimensions={0} | all-to-all | bytes 262144 | tf_op jit(solution)/shard_map/all_to_all | solution.py:31
  (52 shorter events, 10.4 us)
Async XLA Ops:
  0.0 26.9 %copy-start = (bf16[32,64,512]{2,1,0:T(8,128)(2,1)S(1)}, bf16[32,64,512]{2,1,0:T(8,128)(2,1)}, u32[]{:S(2)}) copy-start(bf16[32,64,512]{2,1,0:T(8,128)(2,1)} %param.17) | copy-start | bytes 6291460
  1.5 0.8 copy-start.3
  17.1 1.4 collective-permute-start
  18.5 0.7 copy-start.9
  19.3 1.6 %copy-start.1 = (bf16[2,8192,64]{1,2,0:T(8,128)(2,1)S(1)}, bf16[2,8192,64]{1,2,0:T(8,128)(2,1)}, u32[]{:S(2)}) copy-start(bf16[2,8192,64]{1,2,0:T(8,128)(2,1)} %param.16) | copy-start | bytes 6291460
  21.7 1.2 collective-permute-start.1
  23.6 9.9 %all-to-all-start.1 = ((bf16[8,2,512]{2,1,0:T(2,128)(2,1)}), bf16[8,2,512]{2,1,0:T(2,128)(2,1)S(1)}, u32[]{:S(2)}, u32[]{:S(2)}) async-start(bf16[8,2,512]{2,1,0:T(2,128)(2,1)} %reshape.17), calls=%async_computation.1 | async-start | bytes 32768 | tf_op jit(solution)/shard_map/all_to_all | solution.py:31
  33.9 1.2 collective-permute-start.2
  35.7 11.1 %all-to-all-start.2 = ((bf16[8,2,640]{2,1,0:T(2,128)(2,1)}), bf16[8,2,640]{2,1,0:T(2,128)(2,1)S(1)}, u32[]{:S(2)}, u32[]{:S(2)}) async-start(bf16[8,2,640]{2,1,0:T(2,128)(2,1)} %pair.4), calls=%async_computation.2 | async-start | bytes 40960 | tf_op jit(solution)/shard_map/all_to_all | solution.py:31
  49.0 14.1 %copy-start.5 = (f32[64,128]{1,0:T(8,128)}, f32[64,128]{1,0:T(8,128)S(1)}, u32[]{:S(2)}) copy-start(f32[64,128]{1,0:T(8,128)S(1)} %get-tuple-element.56.refs_5_) | copy-start | bytes 98308
  49.0 1.2 collective-permute-start.3
  59.2 15.5 %copy-start.4 = (bf16[1,8192]{1,0:T(2,128)(2,1)S(1)}, bf16[1,8192]{1,0:T(2,128)(2,1)}, u32[]{:S(2)}) copy-start(bf16[1,8192]{1,0:T(2,128)(2,1)} %hidden_ref.3) | copy-start | bytes 49156
  59.2 27.0 %copy-start.2 = (bf16[2,8192,64]{1,2,0:T(8,128)(2,1)S(1)}, bf16[2,8192,64]{1,2,0:T(8,128)(2,1)}, u32[]{:S(2)}) copy-start(bf16[2,8192,64]{1,2,0:T(8,128)(2,1)} %param.16) | copy-start | bytes 6291460
  63.2 1.4 collective-permute-start.4
  84.9 1.3 collective-permute-start.5
  87.0 1.2 collective-permute-start.6
  88.9 10.5 %all-to-all-start.6 = ((bf16[8,2,512]{2,1,0:T(2,128)(2,1)}), bf16[8,2,512]{2,1,0:T(2,128)(2,1)}, u32[]{:S(2)}, u32[]{:S(2)}) async-start(bf16[8,2,512]{2,1,0:T(2,128)(2,1)} %reshape.19), calls=%async_computation.6 | async-start | bytes 32768 | tf_op jit(solution)/shard_map/all_to_all | solution.py:31
  92.8 20.4 %copy-start.6 = (f32[64,128]{1,0:T(8,128)S(1)}, f32[64,128]{1,0:T(8,128)}, u32[]{:S(2)}) copy-start(f32[64,128]{1,0:T(8,128)} %copy-done.5) | copy-start | bytes 98308
  97.2 0.6 copy-start.7
  100.2 0.8 copy-start.8
  101.3 1.2 collective-permute-start.7
  115.5 1.2 collective-permute-start.8
  129.5 1.4 collective-permute-start.9

commit v4 on v3

v4 whole, which is shorter than its diff:
```python
import functools
import math

import jax
import jax.numpy as jnp
from jax import lax
from jax.experimental import pallas as pl
from jax.experimental.pallas import tpu as pltpu
from jax.sharding import PartitionSpec as P

H = 64
KVH = 8
HD = 128
STEPS = 2
GROUP = H // KVH
EPS = 1e-05
AXIS = "replica"
LANES = 128
LAST = (((1,), (1,)), ((), ()))
FIRST = (((0,), (0,)), ((), ()))

CORES = 2
FOLD = 8


def split_of(count):
    far = 1 << (count.bit_length() // 2)
    return far, count // far


def shift(block, distance, count):
    return lax.ppermute(block, AXIS, [(i, i ^ distance) for i in range(count)])


def across(block, strides, count):
    return [block] + [shift(block, d, count) for d in strides]


def swap(blocks):
    return lax.all_to_all(blocks, AXIS, split_axis=0, concat_axis=0, tiled=True)


def chips_swap(blocks, count):
    groups = [[i for i in range(count) if i % CORES == c] for c in range(CORES)]
    return lax.all_to_all(
        blocks, AXIS, split_axis=0, concat_axis=0, axis_index_groups=groups, tiled=True
    )


def call(body, outs, name, scratch=(), vmem=20 << 20, flops=1 << 20, moved=1 << 18):
    def run(*operands, specs=None):
        specs = specs or [pltpu.VMEM] * len(operands)
        return pl.pallas_call(
            body,
            out_shape=outs,
            in_specs=[pl.BlockSpec(memory_space=s) for s in specs],
            out_specs=[pl.BlockSpec(memory_space=pltpu.VMEM)] * len(outs),
            scratch_shapes=list(scratch),
            compiler_params=pltpu.CompilerParams(vmem_limit_bytes=vmem),
            cost_estimate=pl.CostEstimate(flops=flops, bytes_accessed=moved, transcendentals=0),
            name=name,
        )(*operands)

    return run


def shape(dims, dtype=jnp.bfloat16):
    return jax.ShapeDtypeStruct(dims, dtype)


def iota(dims, axis):
    return lax.broadcasted_iota(jnp.int32, dims, axis)


def dot(a, b, contract=(((1,), (0,)), ((), ()))):
    return lax.dot_general(a, b, contract, preferred_element_type=jnp.float32)


def normalized(hidden, scale):
    factor = lax.rsqrt(jnp.mean(hidden * hidden, axis=-1, keepdims=True) + EPS)
    return (hidden * factor * scale).astype(jnp.bfloat16)


def folded(out_ref, row):
    wide = row.shape[1] // FOLD
    for k in range(out_ref.shape[0]):
        for i in range(FOLD):
            out_ref[k, i : i + 1, :wide] = row[:, i * wide : (i + 1) * wide].astype(out_ref.dtype)


def first_kernel(hidden_ref, scale_ref, adapter_ref, out_ref):
    width = hidden_ref.shape[1]
    hidden = hidden_ref[...].astype(jnp.float32)
    out_ref[:, :width] = normalized(hidden, scale_ref[...].astype(jnp.float32))
    digit = iota((1, LANES), 1)
    adapter = adapter_ref[0]
    high, low = adapter // 256, adapter % 256
    digits = jnp.where(digit == 0, low, jnp.where(digit == 1, high, 0)).astype(jnp.float32)
    out_ref[:, width:] = digits.astype(jnp.bfloat16)


def stash_kernel(amount, token_ref, *refs):
    sources, refs = refs[:amount], refs[amount:]
    outs, out_token, sems = refs[:amount], refs[amount], refs[-1]
    copies = [
        pltpu.make_async_copy(sources[i], outs[i], sems.at[i]) for i in range(amount)
    ]
    for copy in copies:
        copy.start()
    out_token[...] = token_ref[...] * 0.0
    for copy in copies:
        copy.wait()


def member_kernel(near, far, width, *refs):
    pieces, refs = refs[:near], refs[near:]
    me_ref, storage_ref, up_hbm, member_ref, up_ref, held, sems = refs
    kept = member_ref.shape[1]
    count = near * far
    me = me_ref[0]
    for l in range(near):
        digits = pieces[l][:, width:].astype(jnp.float32)
        for k in range(far):
            held[pl.ds(me ^ (k * near + l), 1), :] = digits[k : k + 1]
    adapter = held[:, 0:1] + 256.0 * held[:, 1:2]
    row = iota((count, 1), 0)
    copies = []
    for r in range(count):
        index = jnp.sum(jnp.where(row == r, adapter, 0.0)).astype(jnp.int32)
        copies.append(pltpu.make_async_copy(up_hbm.at[index], up_ref.at[r], sems.at[r]))
        copies[-1].start()
    table = storage_ref.shape[1]
    chosen = jnp.where(iota((count, table), 1) == adapter.astype(jnp.int32), storage_ref[...], 0)
    storage = jnp.sum(chosen.astype(jnp.float32), axis=1, keepdims=True).astype(jnp.int32)
    member_ref[...] = (storage - me * kept == iota((count, kept), 1)).astype(jnp.int32)
    for copy in copies:
        copy.wait()


def low_terms(held, member_ref, down_ref, rows_ref, low_ref):
    rows = held[...].astype(jnp.bfloat16)
    rows_ref[...] = rows
    low = jnp.zeros(low_ref.shape, jnp.float32)
    for index in range(down_ref.shape[0]):
        part = dot(rows, down_ref[index], LAST)
        low = jnp.where(member_ref[:, index : index + 1] > 0, part, low)
    low_ref[...] = low.astype(jnp.bfloat16)


def low_first_kernel(near, far, *refs):
    pieces, refs = refs[:near], refs[near:]
    me_ref, member_ref, down_ref, rows_ref, low_ref, held = refs
    width = held.shape[1]
    for l in range(near):
        block = pieces[l][:, :width].astype(jnp.float32)
        for k in range(far):
            held[pl.ds(me_ref[0] ^ (k * near + l), 1), :] = block[k : k + 1]
    low_terms(held, member_ref, down_ref, rows_ref, low_ref)


def low_later_kernel(own_ref, other_ref, me_ref, member_ref, down_ref, rows_ref, low_ref, held):
    core = me_ref[0] % CORES
    for ref, flip in ((own_ref, 0), (other_ref, 1)):
        wide = ref.shape[2]
        for k in range(ref.shape[0]):
            block = ref[k].astype(jnp.float32)
            row = pl.ds(k * CORES + (core ^ flip), 1)
            for i in range(FOLD):
                held[row, i * wide : (i + 1) * wide] = block[i : i + 1]
    low_terms(held, member_ref, down_ref, rows_ref, low_ref)


def sum_kernel(*refs):
    total = refs[0][...].astype(jnp.float32)
    for ref in refs[1:-1]:
        total = total + ref[...].astype(jnp.float32)
    refs[-1][...] = total.astype(refs[-1].dtype)


def project_kernel(rows_ref, query_w, fresh_w, query_ref, fresh_ref):
    query_ref[...] = dot(rows_ref[...], query_w[...])
    fresh_ref[...] = dot(rows_ref[...], fresh_w[...])


def up_kernel(parts, *refs):
    lows, (query_ref, fresh_ref, up_ref, out_ref, held) = refs[:parts], refs[parts:]
    count, columns = query_ref.shape
    rank = lows[0].shape[1]
    low = lows[0][...].astype(jnp.float32)
    for ref in lows[1:]:
        low = low + ref[...].astype(jnp.float32)
    low = low.astype(jnp.bfloat16)
    wide = count * rank
    repeat = (iota((rank, wide), 1) % rank == iota((rank, wide), 0)).astype(jnp.bfloat16)
    spread = jnp.where(
        iota((count, wide), 1) // rank == iota((count, wide), 0), dot(low, repeat), 0.0
    ).astype(jnp.bfloat16)
    query = query_ref[...]
    for r in range(count // 2):
        part = slice(2 * r * rank, 2 * (r + 1) * rank)
        query = query + dot(
            spread[:, part],
            jnp.concatenate([up_ref[2 * r], up_ref[2 * r + 1]], axis=0),
        )
    line = out_ref.shape[2]
    lines = columns // line
    held[...] = jnp.zeros(held.shape, jnp.float32)
    for c in range(lines):
        held[:, c, :] = query[:, c * line : (c + 1) * line]
    fresh = fresh_ref[...]
    if fresh.shape[1] < line:
        fresh = jnp.concatenate(
            [fresh, jnp.zeros((count, line - fresh.shape[1]), jnp.float32)], axis=1
        )
    held[:, lines, :] = fresh
    for k in range(count):
        out_ref[k] = held[k].astype(jnp.bfloat16)


def pieces_of(lines, select, whole, size):
    if size >= whole:
        total = dot(select(len(lines), 0), lines[0])
        for c in range(1, len(lines)):
            total = total + dot(select(len(lines), c), lines[c])
        return total
    return jnp.concatenate([dot(select(0, p), lines[0]) for p in range(whole // size)], axis=1)


def attend_kernel(columns, fresh_columns, first, *refs):
    lines_ref, length_ref, cache_ref = refs[:3]
    refs = refs[3:]
    if not first:
        past, refs = refs[:2], refs[2:]
    out_ref, refs = refs[0], refs[1:]
    if first:
        keep, refs = refs[:2], refs[2:]
    held, scores = refs
    count, _, line = lines_ref.shape
    cache = cache_ref.shape[2]
    for k in range(count):
        held[k] = lines_ref[k].astype(jnp.float32)
    each = columns // line
    lines = [held[:, c, :].astype(jnp.bfloat16) for c in range(each + 1)]
    origin = iota((H, count), 1)
    head = iota((H, count), 0)

    def query_pick(each, c):
        if each:
            return (head == origin * each + c).astype(jnp.bfloat16)
        return (head * (HD // columns) + c == origin).astype(jnp.bfloat16)

    def fresh_pick(offset):
        def pick(each, c):
            want = head // GROUP + offset
            if each:
                return (want == origin * each + c).astype(jnp.bfloat16)
            return (want * (HD // fresh_columns) + c == origin).astype(jnp.bfloat16)

        return pick

    query = pieces_of(lines[:each], query_pick, HD, columns)
    fresh = [lines[each][:, :fresh_columns]]
    new = [
        (
            pieces_of(fresh, fresh_pick(0), HD, fresh_columns),
            pieces_of(fresh, fresh_pick(KVH), HD, fresh_columns),
        )
    ]
    if first:
        keep[0][...], keep[1][...] = new[0]
    else:
        new.insert(0, (past[0][...], past[1][...]))
    scale = 1.0 / math.sqrt(HD)
    for j in range(KVH):
        rows = slice(j * GROUP, (j + 1) * GROUP)
        scores[rows, :] = dot(
            query[rows].astype(jnp.bfloat16), cache_ref[0, 0, :, j * HD : (j + 1) * HD], LAST
        )
    in_cache = iota((H, cache), 1) < length_ref[0]
    old = jnp.where(in_cache, scores[...] * scale, -jnp.inf)
    news = [jnp.sum(query * keys, axis=1, keepdims=True) * scale for keys, _ in new]
    peak = jnp.max(old, axis=1, keepdims=True)
    for score in news:
        peak = jnp.maximum(peak, score)
    old = jnp.exp(old - peak)
    news = [jnp.exp(score - peak) for score in news]
    total = jnp.sum(old, axis=1, keepdims=True)
    for score in news:
        total = total + score
    old = old / total
    extra = jnp.zeros((H, HD), jnp.float32)
    for score, (_, values) in zip(news, new):
        extra = extra + (score / total).astype(jnp.bfloat16).astype(jnp.float32) * values
    mixed = jnp.concatenate(
        [
            dot(
                old[j * GROUP : (j + 1) * GROUP].astype(jnp.bfloat16),
                cache_ref[0, 1, :, j * HD : (j + 1) * HD],
            )
            for j in range(KVH)
        ],
        axis=0,
    )
    mixed = mixed + extra
    if columns >= HD:
        for k in range(count):
            out_ref[k] = mixed[k * each : (k + 1) * each].astype(jnp.bfloat16)
    else:
        parts = HD // columns
        out = jnp.zeros((count, columns), jnp.float32)
        for p in range(parts):
            pick = (iota((count, H), 1) * parts + p == iota((count, H), 0)).astype(jnp.bfloat16)
            out = out + dot(pick, mixed[:, p * columns : (p + 1) * columns].astype(jnp.bfloat16))
        for k in range(count):
            out_ref[k] = out[k : k + 1].astype(jnp.bfloat16)


def output_kernel(lines_ref, me_ref, weight_ref, own_ref, away_ref, held):
    count, each, line = lines_ref.shape
    chips = count // CORES
    for k in range(count):
        held[k, :each, :] = lines_ref[k].astype(jnp.float32)
    slot = iota((count, count), 0)
    origin = (slot % chips) * CORES + ((me_ref[0] % CORES) ^ (slot // chips))
    order = (iota((count, count), 1) == origin).astype(jnp.bfloat16)
    rows = jnp.concatenate(
        [dot(order, held[:, c, :].astype(jnp.bfloat16)).astype(jnp.bfloat16) for c in range(each)],
        axis=1,
    )
    width = weight_ref.shape[1]
    wide = width // 8
    for c in range(8):
        part = slice(c * wide, (c + 1) * wide)
        out = dot(rows, weight_ref[:, part])
        own_ref[:, part] = out[:chips]
        away_ref[:, part] = out[chips:].astype(jnp.bfloat16)


def partial_kernel(own_ref, other_ref, out_ref):
    total = own_ref[...] + other_ref[...].astype(jnp.float32)
    wide = out_ref.shape[2]
    for k in range(out_ref.shape[0]):
        for i in range(FOLD):
            out_ref[k, i : i + 1, :] = total[k : k + 1, i * wide : (i + 1) * wide].astype(
                out_ref.dtype
            )


def finish_kernel(last, parts_ref, hidden_ref, scale_ref, out_ref, *spread):
    total = parts_ref[0].astype(jnp.float32)
    for k in range(1, parts_ref.shape[0]):
        total = total + parts_ref[k].astype(jnp.float32)
    total = jnp.concatenate([total[i : i + 1] for i in range(FOLD)], axis=1)
    total = total.astype(jnp.bfloat16).astype(jnp.float32)
    before = hidden_ref[...].astype(jnp.float32)
    hidden = (before + total).astype(jnp.bfloat16).astype(jnp.float32)
    if last:
        out_ref[...] = jnp.concatenate([before, hidden], axis=0).astype(jnp.bfloat16)
    else:
        out_ref[...] = hidden.astype(jnp.bfloat16)
        folded(spread[0], normalized(hidden, scale_ref[...].astype(jnp.float32)).astype(jnp.float32))


def shards(
    hidden_state_input,
    attention_norm_scale,
    query_weight,
    key_value_weight,
    output_weight,
    adapter_down_weight,
    adapter_up_weight,
    row_adapter_index,
    adapter_storage_index,
    cache_length_per_row,
    key_value_cache,
):
    count = lax.axis_size(AXIS)
    chips = count // CORES
    far, near = split_of(count)
    far_steps = [k * near for k in range(1, far)]
    near_steps = list(range(1, near))
    kept, width, rank = adapter_down_weight.shape
    columns = query_weight.shape[1]
    fresh_columns = key_value_weight.shape[1]
    line = min(HD, columns)
    smem, vmem = pltpu.SMEM, pltpu.VMEM
    me = lax.axis_index(AXIS).astype(jnp.int32).reshape(1)
    down = adapter_down_weight.transpose(0, 2, 1)
    scale = attention_norm_scale[None]
    storage = adapter_storage_index[None]

    def stash(token, arrays, limit):
        outs = call(
            functools.partial(stash_kernel, len(arrays)),
            [pltpu.VMEM(a.shape, a.dtype) for a in arrays] + [shape((8, LANES), jnp.float32)],
            "stash",
            [pltpu.SemaphoreType.DMA((len(arrays),))],
            vmem=limit,
            moved=sum(2 * a.size for a in arrays),
        )(token, *arrays, specs=[vmem] + [pl.ANY] * len(arrays))
        return outs[:-1], outs[-1]

    hidden = hidden_state_input
    (carried,) = call(first_kernel, [shape((1, width + LANES))], "first")(
        hidden, scale, row_adapter_index, specs=[vmem, vmem, smem]
    )
    past = ()
    for step in range(STEPS):
        first, last = step == 0, step == STEPS - 1
        outs = [shape((count, width)), shape((count, rank))]
        scratch = [pltpu.VMEM((count, width), jnp.float32)]
        if first:
            token = jnp.zeros((8, LANES), jnp.float32)
            (query_w, output_w, fresh_w, down_w, cache), token = stash(
                token,
                [query_weight, output_weight, key_value_weight, down, key_value_cache],
                41 << 20,
            )
            pieces = lax.optimization_barrier((*across(carried, far_steps, count), token))
            carried = jnp.concatenate(pieces[:-1], axis=0)
            pieces = across(carried, near_steps, count)
            member, up_of = call(
                functools.partial(member_kernel, near, far, width),
                [shape((count, kept), jnp.int32), pltpu.VMEM((count, rank, columns), jnp.bfloat16)],
                "member",
                [pltpu.VMEM((count, LANES), jnp.float32), pltpu.SemaphoreType.DMA((count,))],
                vmem=16 << 20,
            )(*pieces, me, storage, adapter_up_weight, specs=[vmem] * near + [smem, vmem, pl.ANY])
            rows, low = call(
                functools.partial(low_first_kernel, near, far), outs, "low", scratch
            )(*pieces, me, member, down_w, specs=[vmem] * near + [smem, vmem, vmem])
        else:
            own = chips_swap(carried, count)
            rows, low = call(low_later_kernel, outs, "low", scratch)(
                own, shift(own, 1, count), me, member, down_w, specs=[vmem, vmem, smem, vmem, vmem]
            )
        (low,) = call(sum_kernel, [shape((count, rank))], "sum")(*across(low, near_steps, count))
        lows = across(low, far_steps, count)
        query, fresh = call(
            project_kernel,
            [shape((count, columns), jnp.float32), shape((count, fresh_columns), jnp.float32)],
            "project",
            flops=2 * count * width * (columns + fresh_columns),
            moved=2 * width * (columns + fresh_columns),
        )(rows, query_w, fresh_w)
        (lines,) = call(
            functools.partial(up_kernel, far),
            [shape((count, 8, line))],
            "up",
            [pltpu.VMEM((count, 8, line), jnp.float32)],
        )(*lows, query, fresh, up_of)

        lines = swap(lines)
        outs = [shape((count, columns // line, line))]
        if first:
            outs = outs + [shape((H, HD), jnp.float32)] * 2
        outs = call(
            functools.partial(attend_kernel, columns, fresh_columns, first),
            outs,
            "attend",
            [
                pltpu.VMEM((count, 8, line), jnp.float32),
                pltpu.VMEM((H, key_value_cache.shape[2]), jnp.float32),
            ],
            moved=2 << 20,
        )(
            lines,
            cache_length_per_row,
            cache,
            *past,
            specs=[vmem, smem, vmem] + [vmem] * len(past),
        )
        if first:
            past = tuple(outs[1:])

        lines = swap(outs[0])
        own, away = call(
            output_kernel,
            [shape((chips, width), jnp.float32), shape((chips, width))],
            "output",
            [pltpu.VMEM((count, 8, line), jnp.float32)],
            flops=2 * count * width * columns,
            moved=2 * width * columns,
        )(lines, me, output_w, specs=[vmem, smem, vmem])

        (parts,) = call(partial_kernel, [shape((chips, FOLD, width // FOLD))], "partial")(
            own, shift(away, 1, count)
        )
        parts = chips_swap(parts, count)
        outs = [shape((2 if last else 1, width))]
        if not last:
            outs = outs + [shape((chips, FOLD, width // FOLD))]
        outs = call(functools.partial(finish_kernel, last), outs, "finish")(parts, hidden, scale)
        if last:
            return outs[0].reshape(STEPS, 1, width)
        hidden, carried = outs


def solution(mesh):
    in_specs = (
        P(("groups", "replica"), None),
        P(),
        P(None, "replica"),
        P(None, "replica"),
        P("replica", None),
        P("replica", None, None),
        P(None, None, "replica"),
        P(("groups", "replica")),
        P(),
        P(("groups", "replica")),
        P(("groups", "replica"), None, None, None),
    )
    out_specs = P(None, ("groups", "replica"), None)
    return jax.shard_map(shards, mesh=mesh, in_specs=in_specs, out_specs=out_specs, check_vma=False)
```

time: 143 us -> 144 us (level)
  blocking collectives: 72.9 us -> 59.2 us
  starting transfers between devices: 12.4 us -> 23.9 us
  local copies, waits for them, and re-layouts: 8.03 us -> 15.1 us
  waiting for transfers between devices: 21 us -> 19 us
    all_to_all x7 -> x3, blocking collectives: 72.9 us -> 29.8 us  [chips_swap(): lax.all_to_all(blocks, AXIS, split_axis=0, concat_axis=0, axis_index_grou...]
    all_to_all x0 -> x3, blocking collectives: none -> 29.4 us  [swap(): return lax.all_to_all(blocks, AXIS, split_axis=0, concat_axis=0, tiled=True)]
    ppermute x10 -> x21, starting transfers between devices: 0.64 us -> 20.4 us  [shift(): return lax.ppermute(block, AXIS, [(i, i ^ distance) for i in range(count)])]
    all_to_all x3 -> x1, starting transfers between devices: 11.7 us -> 3.5 us  [swap(): return lax.all_to_all(blocks, AXIS, split_axis=0, concat_axis=0, tiled=True)]
    unnamed x24 -> x32, local copies, waits for them, and re-layouts: 6.68 us -> 13.8 us
    all_to_all x3 -> x1, waiting for transfers between devices: 9.01 us -> 5.95 us  [swap(): return lax.all_to_all(blocks, AXIS, split_axis=0, concat_axis=0, tiled=True)]
    ppermute x10 -> x21, waiting for transfers between devices: 12 us -> 13.1 us  [shift(): return lax.ppermute(block, AXIS, [(i, i ^ distance) for i in range(count)])]
    pallas_call x22 -> x19, Pallas kernels: 25.1 us -> 24.2 us  [run(): pl.pallas_call(body, out_shape=outs, in_specs=[pl.BlockSpec(memory_space=...]
  transfers between devices with their start and end apart: 13 -> 22, of which waited for: 13 -> 11; matrix products, arithmetic and copies ran while one was open for 1% -> 0% of each run, Pallas kernels for 6% -> 8%
where the time goes in v4:
time: 144 us; the launch traced here: 143 us
  blocking collectives  59.2 us (41%)
  Pallas kernels  24.2 us (17%)
  starting transfers between devices  23.9 us (17%)
  waiting for transfers between devices  19 us (13%)
  local copies, waits for them, and re-layouts  15.1 us (10%)
  between operations  1.49 us (1%)
    all_to_all x3, blocking collectives, chips_swap(): lax.all_to_all(blocks, AXIS, split_axis=0, concat_axis=0, axis_index_grou...  29.8 us
    all_to_all x3, blocking collectives, swap(): return lax.all_to_all(blocks, AXIS, split_axis=0, concat_axis=0, tiled=True)  29.4 us
    pallas_call x19, Pallas kernels, run(): pl.pallas_call(body, out_shape=outs, in_specs=[pl.BlockSpec(memory_space=...  24.2 us
    ppermute x21, starting transfers between devices, shift(): return lax.ppermute(block, AXIS, [(i, i ^ distance) for i in range(count)])  20.4 us
    unnamed x32, local copies, waits for them, and re-layouts  13.8 us
    ppermute x21, waiting for transfers between devices, shift(): return lax.ppermute(block, AXIS, [(i, i ^ distance) for i in range(count)])  13.1 us
    all_to_all x1, waiting for transfers between devices, swap(): return lax.all_to_all(blocks, AXIS, split_axis=0, concat_axis=0, tiled=True)  5.95 us
    all_to_all x1, starting transfers between devices, swap(): return lax.all_to_all(blocks, AXIS, split_axis=0, concat_axis=0, tiled=True)  3.5 us
  transfers between devices with their start and end apart: 22, of which 11 were waited for; matrix products, arithmetic and copies ran while one was open for 0% of the time, Pallas kernels for 8%

profile of v4, /device:TPU:0, one launch (start us, length us, event | category | flops | bytes accessed | tf_op | source)
XLA Modules:
  0.0 143.1 jit_solution(1931600257545931053)
XLA Ops:
  2.3 5.1 %collective-permute-start.2 = (bf16[1,8320]{1,0:T(2,128)(2,1)S(1)}, bf16[1,8320]{1,0:T(2,128)(2,1)S(1)}, u32[]{:S(2)}, u32[]{:S(2)}) collective-permute-start(bf16[1,8320]{1,0:T(2,128)(2,1)S(1)} %first.1), channel_id=1, source_target_pairs={{0,12},{1,13},{2,14},{3,15},{4,8},{5,9},{6,10},{7,11},{8,4},{9,5},... | collective-permute-start | bytes 49928 | tf_op jit(solution)/shard_map/ppermute | solution.py:32
  8.1 1.3 collective-permute-done.2
  9.4 2.9 %collective-permute-done.1 = bf16[1,8320]{1,0:T(2,128)(2,1)S(1)} collective-permute-done((bf16[1,8320]{1,0:T(2,128)(2,1)S(1)}, bf16[1,8320]{1,0:T(2,128)(2,1)S(1)}, u32[]{:S(2)}, u32[]{:S(2)}) %collective-permute-start.1) | collective-permute-done | bytes 16672 | tf_op jit(solution)/shard_map/ppermute | solution.py:32
  12.5 1.6 %collective-permute-start.4 = (bf16[4,8320]{1,0:T(4,128)(2,1)S(1)}, bf16[4,8320]{1,0:T(4,128)(2,1)S(1)}, u32[]{:S(2)}, u32[]{:S(2)}) collective-permute-start(bf16[4,8320]{1,0:T(4,128)(2,1)S(1)} %pad_maximum_fusion.refs_0_), channel_id=1, source_target_pairs={{0,2},{1,3},{2,0},{3,1},{4,6},{5,7},{6,4},{7,5},{8,10},{9,11},{10,... | collective-permute-start | bytes 199688 | tf_op jit(solution)/shard_map/ppermute | solution.py:32
  15.0 8.9 %stash.1 = (bf16[8192,512]{1,0:T(8,128)(2,1)S(1)}, bf16[512,8192]{1,0:T(8,128)(2,1)S(1)}, bf16[8192,128]{1,0:T(8,128)(2,1)S(1)}, bf16[2,64,8192]{2,1,0:T(8,128)(...) custom-call(f32[8,128]{1,0:T(8,128)} %broadcast_in_dim.11.token_ref, bf16[8192,512]{1,0:T(8,128)(2,1)} %refs_0_.1, ...), custom_call_target="tpu_custom_call" | custom-call | flops 1048576 | bytes 23068672 | tf_op jit(solution)/shard_map/stash/pallas_call | solution.py:53
  23.9 3.3 %copy-done = bf16[512,8192]{1,0:T(8,128)(2,1)} copy-done((bf16[512,8192]{1,0:T(8,128)(2,1)}, bf16[512,8192]{1,0:T(8,128)(2,1)S(1)}, u32[]{:S(2)}) %copy-start) | copy-done | bytes 8388632
  27.2 3.1 %copy-done.10 = bf16[32,64,512]{2,1,0:T(8,128)(2,1)S(1)} copy-done((bf16[32,64,512]{2,1,0:T(8,128)(2,1)S(1)}, bf16[32,64,512]{2,1,0:T(8,128)(2,1)}, u32[]{:S(2)}) %copy-start.10) | copy-done | bytes 2097176
  30.3 3.7 %member.1 = (s32[16,2]{1,0:T(8,128)S(1)}, bf16[16,64,512]{2,1,0:T(8,128)(2,1)S(1)}) custom-call(bf16[4,8320]{1,0:T(4,128)(2,1)S(1)} %pad_maximum_fusion.refs_0_, bf16[4,8320]{1,0:T(4,128)(2,1)S(1)} %collective-permute-done.3.refs_1_, bf16[4,8320]{1,0:T(4,128)(2,1)S(1)} %collective-permute-done.4.refs_2_, bf16[4,8320]{1,0:T(4,128)(2,1)S(1)} %collective-permute-done.5.refs_3_, ...), custom_call_target="tpu_custom_call" | custom-call | flops 1048576 | bytes 262144 | tf_op jit(solution)/shard_map/member/pallas_call | solution.py:53
  36.6 1.2 collective-permute-done.8.refs_3_
  37.8 1.7 %collective-permute-done.7.refs_2_ = bf16[16,64]{1,0:T(8,128)(2,1)S(1)} collective-permute-done((bf16[16,64]{1,0:T(8,128)(2,1)S(1)}, bf16[16,64]{1,0:T(8,128)(2,1)S(1)}, u32[]{:S(2)}, u32[]{:S(2)}) %collective-permute-start.7) | collective-permute-done | bytes 2080 | tf_op jit(solution)/shard_map/ppermute | solution.py:32
  39.5 1.5 %collective-permute-start.11 = (bf16[16,64]{1,0:T(8,128)(2,1)S(1)}, bf16[16,64]{1,0:T(8,128)(2,1)S(1)}, u32[]{:S(2)}, u32[]{:S(2)}) collective-permute-start(bf16[16,64]{1,0:T(8,128)(2,1)S(1)} %sum.2.refs_0_), channel_id=1, source_target_pairs={{0,12},{1,13},{2,14},{3,15},{4,8},{5,9},{6,10},{7,11},{8,4},{9,5},... | collective-permute-start | bytes 6152 | tf_op jit(solution)/shard_map/ppermute | solution.py:32
  41.6 2.3 %collective-permute-start.9 = (bf16[16,64]{1,0:T(8,128)(2,1)S(1)}, bf16[16,64]{1,0:T(8,128)(2,1)S(1)}, u32[]{:S(2)}, u32[]{:S(2)}) collective-permute-start(bf16[16,64]{1,0:T(8,128)(2,1)S(1)} %sum.2.refs_0_), channel_id=1, source_target_pairs={{0,4},{1,5},{2,6},{3,7},{4,0},{5,1},{6,2},{7,3},{8,12},{9,13},{10,... | collective-permute-start | bytes 6152 | tf_op jit(solution)/shard_map/ppermute | solution.py:32
  43.9 1.4 %project.2 = (f32[16,512]{1,0:T(8,128)S(1)}, f32[16,128]{1,0:T(8,128)S(1)}) custom-call(bf16[16,8192]{1,0:T(8,128)(2,1)S(1)} %get-tuple-element.40.rows_ref, bf16[8192,512]{1,0:T(8,128)(2,1)S(1)} %get-tuple-element.41.query_w, bf16[8192,128]{1,0:T(8,128)(2,1)S(1)} %get-tuple-element.42.fresh_w), custom_call_target="tpu_custom_call" | custom-call | flops 167772160 | bytes 10485760 | tf_op jit(solution)/shard_map/project/pallas_call | solution.py:53
  45.4 3.3 %copy-done.2 = bf16[8192,512]{1,0:T(8,128)(2,1)} copy-done((bf16[8192,512]{1,0:T(8,128)(2,1)}, bf16[8192,512]{1,0:T(8,128)(2,1)S(1)}, u32[]{:S(2)}) %copy-start.2) | copy-done | bytes 8388632
  49.7 3.5 %all-to-all-start = ((bf16[16,8,128]{2,1,0:T(8,128)(2,1)}), bf16[16,8,128]{2,1,0:T(8,128)(2,1)S(1)}, u32[]{:S(2)}, u32[]{:S(2)}) async-start(bf16[16,8,128]{2,1,0:T(8,128)(2,1)} %up.2), calls=%async_computation | async-start | bytes 65536 | tf_op jit(solution)/shard_map/all_to_all | solution.py:40
  53.8 5.9 %all-to-all-done.refs_0_ = bf16[16,8,128]{2,1,0:T(8,128)(2,1)S(1)} async-done(((bf16[16,8,128]{2,1,0:T(8,128)(2,1)}), bf16[16,8,128]{2,1,0:T(8,128)(2,1)S(1)}, u32[]{:S(2)}, u32[]{:S(2)}) %all-to-all-start) | async-done | bytes 32800 | tf_op jit(solution)/shard_map/all_to_all | solution.py:40
  60.6 9.1 %all_to_all.35.lines_ref = bf16[16,4,128]{2,1,0:T(4,128)(2,1)S(1)} all-to-all(bf16[16,4,128]{2,1,0:T(4,128)(2,1)S(1)} %get-tuple-element.47), channel_id=1, replica_groups=mesh['groups'=2,'replica'=16] {'replica'}, dimensions={0} | all-to-all | bytes 32768 | tf_op jit(solution)/shard_map/all_to_all | solution.py:40
  69.7 3.4 %copy-done.1 = bf16[512,8192]{1,0:T(8,128)(2,1)S(1)} copy-done((bf16[512,8192]{1,0:T(8,128)(2,1)S(1)}, bf16[512,8192]{1,0:T(8,128)(2,1)}, u32[]{:S(2)}) %copy-start.1) | copy-done | bytes 8388632
  73.1 1.3 output.2
  74.4 1.3 collective-permute-done.12.other_ref
  75.9 10.0 %all_to_all.36.parts_ref = bf16[8,8,1024]{2,1,0:T(8,128)(2,1)S(1)} all-to-all(bf16[8,8,1024]{2,1,0:T(8,128)(2,1)S(1)} %partial.2), channel_id=1, replica_groups={{0,2,4,6,8,10,12,14},{1,3,5,7,9,11,13,15},{16,18,20,22,24,26,28,30},{17..., dimensions={0} | all-to-all | bytes 262144 | tf_op jit(solution)/shard_map/all_to_all | solution.py:45
  86.2 9.8 %all_to_all.37.own_ref = bf16[8,8,1024]{2,1,0:T(8,128)(2,1)S(1)} all-to-all(bf16[8,8,1024]{2,1,0:T(8,128)(2,1)S(1)} %get-tuple-element.51), channel_id=1, replica_groups={{0,2,4,6,8,10,12,14},{1,3,5,7,9,11,13,15},{16,18,20,22,24,26,28,30},{17..., dimensions={0} | all-to-all | bytes 262144 | tf_op jit(solution)/shard_map/all_to_all | solution.py:45
  96.1 1.3 collective-permute-done.13.other_ref
  98.2 1.8 %collective-permute-start.15 = (bf16[16,64]{1,0:T(8,128)(2,1)S(1)}, bf16[16,64]{1,0:T(8,128)(2,1)S(1)}, u32[]{:S(2)}, u32[]{:S(2)}) collective-permute-start(bf16[16,64]{1,0:T(8,128)(2,1)S(1)} %get-tuple-element.52.refs_0_), channel_id=1, source_target_pairs={{0,2},{1,3},{2,0},{3,1},{4,6},{5,7},{6,4},{7,5},{8,10},{9,11},{10,... | collective-permute-start | bytes 6152 | tf_op jit(solution)/shard_map/ppermute | solution.py:32
  101.9 1.4 %collective-permute-start.19 = (bf16[16,64]{1,0:T(8,128)(2,1)S(1)}, bf16[16,64]{1,0:T(8,128)(2,1)S(1)}, u32[]{:S(2)}, u32[]{:S(2)}) collective-permute-start(bf16[16,64]{1,0:T(8,128)(2,1)S(1)} %sum.3.refs_0_), channel_id=1, source_target_pairs={{0,12},{1,13},{2,14},{3,15},{4,8},{5,9},{6,10},{7,11},{8,4},{9,5},... | collective-permute-start | bytes 6152 | tf_op jit(solution)/shard_map/ppermute | solution.py:32
  104.5 1.9 %collective-permute-start.17 = (bf16[16,64]{1,0:T(8,128)(2,1)S(1)}, bf16[16,64]{1,0:T(8,128)(2,1)S(1)}, u32[]{:S(2)}, u32[]{:S(2)}) collective-permute-start(bf16[16,64]{1,0:T(8,128)(2,1)S(1)} %sum.3.refs_0_), channel_id=1, source_target_pairs={{0,4},{1,5},{2,6},{3,7},{4,0},{5,1},{6,2},{7,3},{8,12},{9,13},{10,... | collective-permute-start | bytes 6152 | tf_op jit(solution)/shard_map/ppermute | solution.py:32
  106.4 1.5 %project.3 = (f32[16,512]{1,0:T(8,128)S(1)}, f32[16,128]{1,0:T(8,128)S(1)}) custom-call(bf16[16,8192]{1,0:T(8,128)(2,1)S(1)} %get-tuple-element.53.rows_ref, bf16[8192,512]{1,0:T(8,128)(2,1)S(1)} %copy-done.3, bf16[8192,128]{1,0:T(8,128)(2,1)S(1)} %copy-done.7), custom_call_target="tpu_custom_call" | custom-call | flops 167772160 | bytes 10485760 | tf_op jit(solution)/shard_map/project/pallas_call | solution.py:53
  108.5 11.2 %all_to_all.38.refs_0_ = bf16[16,8,128]{2,1,0:T(8,128)(2,1)S(1)} all-to-all(bf16[16,8,128]{2,1,0:T(8,128)(2,1)S(1)} %up.3), channel_id=1, replica_groups=mesh['groups'=2,'replica'=16] {'replica'}, dimensions={0} | all-to-all | bytes 65536 | tf_op jit(solution)/shard_map/all_to_all | solution.py:40
  120.5 9.1 %all_to_all.39.lines_ref = bf16[16,4,128]{2,1,0:T(4,128)(2,1)S(1)} all-to-all(bf16[16,4,128]{2,1,0:T(4,128)(2,1)S(1)} %attend.3), channel_id=1, replica_groups=mesh['groups'=2,'replica'=16] {'replica'}, dimensions={0} | all-to-all | bytes 32768 | tf_op jit(solution)/shard_map/all_to_all | solution.py:40
  129.6 1.3 output.3
  130.9 1.4 collective-permute-done.20.other_ref
  132.4 10.0 %all_to_all.40.parts_ref = bf16[8,8,1024]{2,1,0:T(8,128)(2,1)S(1)} all-to-all(bf16[8,8,1024]{2,1,0:T(8,128)(2,1)S(1)} %partial.3), channel_id=1, replica_groups={{0,2,4,6,8,10,12,14},{1,3,5,7,9,11,13,15},{16,18,20,22,24,26,28,30},{17..., dimensions={0} | all-to-all | bytes 262144 | tf_op jit(solution)/shard_map/all_to_all | solution.py:45
  (73 shorter events, 15.3 us)
Async XLA Ops:
  2.3 7.0 %collective-permute-start.2 = (bf16[1,8320]{1,0:T(2,128)(2,1)S(1)}, bf16[1,8320]{1,0:T(2,128)(2,1)S(1)}, u32[]{:S(2)}, u32[]{:S(2)}) collective-permute-start(bf16[1,8320]{1,0:T(2,128)(2,1)S(1)} %first.1), channel_id=1, source_target_pairs={{0,12},{1,13},{2,14},{3,15},{4,8},{5,9},{6,10},{7,11},{8,4},{9,5},... | collective-permute-start | bytes 49928 | tf_op jit(solution)/shard_map/ppermute | solution.py:32
  7.5 4.8 %collective-permute-start.1 = (bf16[1,8320]{1,0:T(2,128)(2,1)S(1)}, bf16[1,8320]{1,0:T(2,128)(2,1)S(1)}, u32[]{:S(2)}, u32[]{:S(2)}) collective-permute-start(bf16[1,8320]{1,0:T(2,128)(2,1)S(1)} %first.1), channel_id=1, source_target_pairs={{0,8},{1,9},{2,10},{3,11},{4,12},{5,13},{6,14},{7,15},{8,0},{9,1},... | collective-permute-start | bytes 49928 | tf_op jit(solution)/shard_map/ppermute | solution.py:32
  7.5 4.8 %collective-permute-start = (bf16[1,8320]{1,0:T(2,128)(2,1)S(1)}, bf16[1,8320]{1,0:T(2,128)(2,1)S(1)}, u32[]{:S(2)}, u32[]{:S(2)}) collective-permute-start(bf16[1,8320]{1,0:T(2,128)(2,1)S(1)} %first.1), channel_id=1, source_target_pairs={{0,4},{1,5},{2,6},{3,7},{4,0},{5,1},{6,2},{7,3},{8,12},{9,13},{10,... | collective-permute-start | bytes 49928 | tf_op jit(solution)/shard_map/ppermute | solution.py:32
  12.4 14.7 %collective-permute-start.5 = (bf16[4,8320]{1,0:T(4,128)(2,1)S(1)}, bf16[4,8320]{1,0:T(4,128)(2,1)S(1)}, u32[]{:S(2)}, u32[]{:S(2)}) collective-permute-start(bf16[4,8320]{1,0:T(4,128)(2,1)S(1)} %pad_maximum_fusion.refs_0_), channel_id=1, source_target_pairs={{0,3},{1,2},{2,1},{3,0},{4,7},{5,6},{6,5},{7,4},{8,11},{9,10},{10,... | collective-permute-start | bytes 199688 | tf_op jit(solution)/shard_map/ppermute | solution.py:32
  12.5 14.6 %collective-permute-start.4 = (bf16[4,8320]{1,0:T(4,128)(2,1)S(1)}, bf16[4,8320]{1,0:T(4,128)(2,1)S(1)}, u32[]{:S(2)}, u32[]{:S(2)}) collective-permute-start(bf16[4,8320]{1,0:T(4,128)(2,1)S(1)} %pad_maximum_fusion.refs_0_), channel_id=1, source_target_pairs={{0,2},{1,3},{2,0},{3,1},{4,6},{5,7},{6,4},{7,5},{8,10},{9,11},{10,... | collective-permute-start | bytes 199688 | tf_op jit(solution)/shard_map/ppermute | solution.py:32
  14.1 13.1 %collective-permute-start.3 = (bf16[4,8320]{1,0:T(4,128)(2,1)S(1)}, bf16[4,8320]{1,0:T(4,128)(2,1)S(1)}, u32[]{:S(2)}, u32[]{:S(2)}) collective-permute-start(bf16[4,8320]{1,0:T(4,128)(2,1)S(1)} %pad_maximum_fusion.refs_0_), channel_id=1, source_target_pairs={{0,1},{1,0},{2,3},{3,2},{4,5},{5,4},{6,7},{7,6},{8,9},{9,8},{10,11... | collective-permute-start | bytes 199688 | tf_op jit(solution)/shard_map/ppermute | solution.py:32
  15.0 12.2 %copy-start.13 = (s32[32]{0:T(128)S(1)}, s32[32]{0:T(128)}, u32[]{:S(2)}) copy-start(s32[32]{0:T(128)} %param.19) | copy-start | bytes 388
  27.2 7.6 %copy-start.4 = (bf16[2,64,8192]{2,1,0:T(8,128)(2,1)}, bf16[2,64,8192]{2,1,0:T(8,128)(2,1)S(1)}, u32[]{:S(2)}) copy-start(bf16[2,64,8192]{2,1,0:T(8,128)(2,1)S(1)} %get-tuple-element.38.refs_6_.down_ref) | copy-start | bytes 6291460
  27.2 16.8 %copy-start.6 = (bf16[8192,128]{1,0:T(8,128)(2,1)}, bf16[8192,128]{1,0:T(8,128)(2,1)S(1)}, u32[]{:S(2)}) copy-start(bf16[8192,128]{1,0:T(8,128)(2,1)S(1)} %get-tuple-element.42.fresh_w) | copy-start | bytes 6291460
  34.0 14.7 %copy-start.8 = (bf16[16,64,512]{2,1,0:T(8,128)(2,1)}, bf16[16,64,512]{2,1,0:T(8,128)(2,1)S(1)}, u32[]{:S(2)}) copy-start(bf16[16,64,512]{2,1,0:T(8,128)(2,1)S(1)} %get-tuple-element.45.refs_6_) | copy-start | bytes 3145732
  34.7 3.1 %collective-permute-start.8 = (bf16[16,64]{1,0:T(8,128)(2,1)S(1)}, bf16[16,64]{1,0:T(8,128)(2,1)S(1)}, u32[]{:S(2)}, u32[]{:S(2)}) collective-permute-start(bf16[16,64]{1,0:T(8,128)(2,1)S(1)} %get-tuple-element.39.refs_0_), channel_id=1, source_target_pairs={{0,3},{1,2},{2,1},{3,0},{4,7},{5,6},{6,5},{7,4},{8,11},{9,10},{10,... | collective-permute-start | bytes 6152 | tf_op jit(solution)/shard_map/ppermute | solution.py:32
  35.9 3.6 %collective-permute-start.7 = (bf16[16,64]{1,0:T(8,128)(2,1)S(1)}, bf16[16,64]{1,0:T(8,128)(2,1)S(1)}, u32[]{:S(2)}, u32[]{:S(2)}) collective-permute-start(bf16[16,64]{1,0:T(8,128)(2,1)S(1)} %get-tuple-element.39.refs_0_), channel_id=1, source_target_pairs={{0,2},{1,3},{2,0},{3,1},{4,6},{5,7},{6,4},{7,5},{8,10},{9,11},{10,... | collective-permute-start | bytes 6152 | tf_op jit(solution)/shard_map/ppermute | solution.py:32
  36.6 2.9 %collective-permute-start.6 = (bf16[16,64]{1,0:T(8,128)(2,1)S(1)}, bf16[16,64]{1,0:T(8,128)(2,1)S(1)}, u32[]{:S(2)}, u32[]{:S(2)}) collective-permute-start(bf16[16,64]{1,0:T(8,128)(2,1)S(1)} %get-tuple-element.39.refs_0_), channel_id=1, source_target_pairs={{0,1},{1,0},{2,3},{3,2},{4,5},{5,4},{6,7},{7,6},{8,9},{9,8},{10,11... | collective-permute-start | bytes 6152 | tf_op jit(solution)/shard_map/ppermute | solution.py:32
  39.5 9.2 %collective-permute-start.11 = (bf16[16,64]{1,0:T(8,128)(2,1)S(1)}, bf16[16,64]{1,0:T(8,128)(2,1)S(1)}, u32[]{:S(2)}, u32[]{:S(2)}) collective-permute-start(bf16[16,64]{1,0:T(8,128)(2,1)S(1)} %sum.2.refs_0_), channel_id=1, source_target_pairs={{0,12},{1,13},{2,14},{3,15},{4,8},{5,9},{6,10},{7,11},{8,4},{9,5},... | collective-permute-start | bytes 6152 | tf_op jit(solution)/shard_map/ppermute | solution.py:32
  41.0 7.7 %collective-permute-start.10 = (bf16[16,64]{1,0:T(8,128)(2,1)S(1)}, bf16[16,64]{1,0:T(8,128)(2,1)S(1)}, u32[]{:S(2)}, u32[]{:S(2)}) collective-permute-start(bf16[16,64]{1,0:T(8,128)(2,1)S(1)} %sum.2.refs_0_), channel_id=1, source_target_pairs={{0,8},{1,9},{2,10},{3,11},{4,12},{5,13},{6,14},{7,15},{8,0},{9,1},... | collective-permute-start | bytes 6152 | tf_op jit(solution)/shard_map/ppermute | solution.py:32
  41.6 7.0 %collective-permute-start.9 = (bf16[16,64]{1,0:T(8,128)(2,1)S(1)}, bf16[16,64]{1,0:T(8,128)(2,1)S(1)}, u32[]{:S(2)}, u32[]{:S(2)}) collective-permute-start(bf16[16,64]{1,0:T(8,128)(2,1)S(1)} %sum.2.refs_0_), channel_id=1, source_target_pairs={{0,4},{1,5},{2,6},{3,7},{4,0},{5,1},{6,2},{7,3},{8,12},{9,13},{10,... | collective-permute-start | bytes 6152 | tf_op jit(solution)/shard_map/ppermute | solution.py:32
  49.7 10.1 %all-to-all-start = ((bf16[16,8,128]{2,1,0:T(8,128)(2,1)}), bf16[16,8,128]{2,1,0:T(8,128)(2,1)S(1)}, u32[]{:S(2)}, u32[]{:S(2)}) async-start(bf16[16,8,128]{2,1,0:T(8,128)(2,1)} %up.2), calls=%async_computation | async-start | bytes 65536 | tf_op jit(solution)/shard_map/all_to_all | solution.py:40
  59.8 37.7 %copy-start.5 = (bf16[2,64,8192]{2,1,0:T(8,128)(2,1)S(1)}, bf16[2,64,8192]{2,1,0:T(8,128)(2,1)}, u32[]{:S(2)}) copy-start(bf16[2,64,8192]{2,1,0:T(8,128)(2,1)} %copy-done.4) | copy-start | bytes 6291460
  73.1 12.8 %copy-start.12 = (bf16[1,8192]{1,0:T(2,128)(2,1)S(1)}, bf16[1,8192]{1,0:T(2,128)(2,1)}, u32[]{:S(2)}) copy-start(bf16[1,8192]{1,0:T(2,128)(2,1)} %hidden_ref.3) | copy-start | bytes 49156
  73.1 33.3 %copy-start.3 = (bf16[8192,512]{1,0:T(8,128)(2,1)S(1)}, bf16[8192,512]{1,0:T(8,128)(2,1)}, u32[]{:S(2)}) copy-start(bf16[8192,512]{1,0:T(8,128)(2,1)} %copy-done.2) | copy-start | bytes 25165828
  74.4 32.0 %copy-start.7 = (bf16[8192,128]{1,0:T(8,128)(2,1)S(1)}, bf16[8192,128]{1,0:T(8,128)(2,1)}, u32[]{:S(2)}) copy-start(bf16[8192,128]{1,0:T(8,128)(2,1)} %copy-done.6) | copy-start | bytes 6291460
  74.4 1.4 collective-permute-start.12
  96.1 1.3 collective-permute-start.13
  97.4 32.2 %slice-start = ((s8[8388608]{0:T(1024)(128)(4,1)}), s8[4194304]{0:T(1024)(128)(4,1)S(1)}, s32[]{:S(2)}) async-start(s8[8388608]{0:T(1024)(128)(4,1)} %bitcast.4), calls=%async_computation.7 | async-start | bytes 8388608
  98.2 3.1 %collective-permute-start.16 = (bf16[16,64]{1,0:T(8,128)(2,1)S(1)}, bf16[16,64]{1,0:T(8,128)(2,1)S(1)}, u32[]{:S(2)}, u32[]{:S(2)}) collective-permute-start(bf16[16,64]{1,0:T(8,128)(2,1)S(1)} %get-tuple-element.52.refs_0_), channel_id=1, source_target_pairs={{0,3},{1,2},{2,1},{3,0},{4,7},{5,6},{6,5},{7,4},{8,11},{9,10},{10,... | collective-permute-start | bytes 6152 | tf_op jit(solution)/shard_map/ppermute | solution.py:32
  98.2 3.7 %collective-permute-start.15 = (bf16[16,64]{1,0:T(8,128)(2,1)S(1)}, bf16[16,64]{1,0:T(8,128)(2,1)S(1)}, u32[]{:S(2)}, u32[]{:S(2)}) collective-permute-start(bf16[16,64]{1,0:T(8,128)(2,1)S(1)} %get-tuple-element.52.refs_0_), channel_id=1, source_target_pairs={{0,2},{1,3},{2,0},{3,1},{4,6},{5,7},{6,4},{7,5},{8,10},{9,11},{10,... | collective-permute-start | bytes 6152 | tf_op jit(solution)/shard_map/ppermute | solution.py:32
  100.0 1.9 %collective-permute-start.14 = (bf16[16,64]{1,0:T(8,128)(2,1)S(1)}, bf16[16,64]{1,0:T(8,128)(2,1)S(1)}, u32[]{:S(2)}, u32[]{:S(2)}) collective-permute-start(bf16[16,64]{1,0:T(8,128)(2,1)S(1)} %get-tuple-element.52.refs_0_), channel_id=1, source_target_pairs={{0,1},{1,0},{2,3},{3,2},{4,5},{5,4},{6,7},{7,6},{8,9},{9,8},{10,11... | collective-permute-start | bytes 6152 | tf_op jit(solution)/shard_map/ppermute | solution.py:32
  101.9 5.9 %collective-permute-start.19 = (bf16[16,64]{1,0:T(8,128)(2,1)S(1)}, bf16[16,64]{1,0:T(8,128)(2,1)S(1)}, u32[]{:S(2)}, u32[]{:S(2)}) collective-permute-start(bf16[16,64]{1,0:T(8,128)(2,1)S(1)} %sum.3.refs_0_), channel_id=1, source_target_pairs={{0,12},{1,13},{2,14},{3,15},{4,8},{5,9},{6,10},{7,11},{8,4},{9,5},... | collective-permute-start | bytes 6152 | tf_op jit(solution)/shard_map/ppermute | solution.py:32
  103.3 4.5 %collective-permute-start.18 = (bf16[16,64]{1,0:T(8,128)(2,1)S(1)}, bf16[16,64]{1,0:T(8,128)(2,1)S(1)}, u32[]{:S(2)}, u32[]{:S(2)}) collective-permute-start(bf16[16,64]{1,0:T(8,128)(2,1)S(1)} %sum.3.refs_0_), channel_id=1, source_target_pairs={{0,8},{1,9},{2,10},{3,11},{4,12},{5,13},{6,14},{7,15},{8,0},{9,1},... | collective-permute-start | bytes 6152 | tf_op jit(solution)/shard_map/ppermute | solution.py:32
  104.5 3.6 %collective-permute-start.17 = (bf16[16,64]{1,0:T(8,128)(2,1)S(1)}, bf16[16,64]{1,0:T(8,128)(2,1)S(1)}, u32[]{:S(2)}, u32[]{:S(2)}) collective-permute-start(bf16[16,64]{1,0:T(8,128)(2,1)S(1)} %sum.3.refs_0_), channel_id=1, source_target_pairs={{0,4},{1,5},{2,6},{3,7},{4,0},{5,1},{6,2},{7,3},{8,12},{9,13},{10,... | collective-permute-start | bytes 6152 | tf_op jit(solution)/shard_map/ppermute | solution.py:32
  106.4 23.2 %slice-start.1 = ((s8[8388608]{0:T(1024)(128)(4,1)}), s8[4194304]{0:T(1024)(128)(4,1)S(1)}, s32[]{:S(2)}) async-start(s8[8388608]{0:T(1024)(128)(4,1)} %bitcast.4), calls=%async_computation.8 | async-start | bytes 8388608
  130.9 1.4 collective-permute-start.20
  (6 other events, 15.5 us)

commit v5 on v4

--- a/solution.py
+++ b/solution.py
@@ -88,7 +88,8 @@
             out_ref[k, i : i + 1, :wide] = row[:, i * wide : (i + 1) * wide].astype(out_ref.dtype)
 
 
-def first_kernel(hidden_ref, scale_ref, adapter_ref, out_ref):
+def first_kernel(hidden_ref, scale_ref, adapter_ref, length_ref, out_ref, length_out):
+    length_out[...] = jnp.full(length_out.shape, length_ref[0], jnp.int32)
     width = hidden_ref.shape[1]
     hidden = hidden_ref[...].astype(jnp.float32)
     out_ref[:, :width] = normalized(hidden, scale_ref[...].astype(jnp.float32))
@@ -114,7 +115,7 @@
 
 def member_kernel(near, far, width, *refs):
     pieces, refs = refs[:near], refs[near:]
-    me_ref, storage_ref, up_hbm, member_ref, up_ref, held, sems = refs
+    me_ref, storage_ref, member_ref, adapter_ref, held = refs
     kept = member_ref.shape[1]
     count = near * far
     me = me_ref[0]
@@ -122,19 +123,12 @@
         digits = pieces[l][:, width:].astype(jnp.float32)
         for k in range(far):
             held[pl.ds(me ^ (k * near + l), 1), :] = digits[k : k + 1]
-    adapter = held[:, 0:1] + 256.0 * held[:, 1:2]
-    row = iota((count, 1), 0)
-    copies = []
-    for r in range(count):
-        index = jnp.sum(jnp.where(row == r, adapter, 0.0)).astype(jnp.int32)
-        copies.append(pltpu.make_async_copy(up_hbm.at[index], up_ref.at[r], sems.at[r]))
-        copies[-1].start()
+    adapter = (held[:, 0:1] + 256.0 * held[:, 1:2]).astype(jnp.int32)
+    adapter_ref[...] = adapter
     table = storage_ref.shape[1]
-    chosen = jnp.where(iota((count, table), 1) == adapter.astype(jnp.int32), storage_ref[...], 0)
+    chosen = jnp.where(iota((count, table), 1) == adapter, storage_ref[...], 0)
     storage = jnp.sum(chosen.astype(jnp.float32), axis=1, keepdims=True).astype(jnp.int32)
     member_ref[...] = (storage - me * kept == iota((count, kept), 1)).astype(jnp.int32)
-    for copy in copies:
-        copy.wait()
 
 
 def low_terms(held, member_ref, down_ref, rows_ref, low_ref):
@@ -183,25 +177,23 @@
 
 
 def up_kernel(parts, *refs):
-    lows, (query_ref, fresh_ref, up_ref, out_ref, held) = refs[:parts], refs[parts:]
+    lows, (query_ref, fresh_ref, adapter_ref, up_ref, out_ref, held) = refs[:parts], refs[parts:]
     count, columns = query_ref.shape
     rank = lows[0].shape[1]
     low = lows[0][...].astype(jnp.float32)
     for ref in lows[1:]:
         low = low + ref[...].astype(jnp.float32)
     low = low.astype(jnp.bfloat16)
-    wide = count * rank
+    query = query_ref[...]
+    table = up_ref.shape[0]
+    some = min(table, 32)
+    wide = some * rank
     repeat = (iota((rank, wide), 1) % rank == iota((rank, wide), 0)).astype(jnp.bfloat16)
-    spread = jnp.where(
-        iota((count, wide), 1) // rank == iota((count, wide), 0), dot(low, repeat), 0.0
-    ).astype(jnp.bfloat16)
-    query = query_ref[...]
-    for r in range(count // 2):
-        part = slice(2 * r * rank, 2 * (r + 1) * rank)
-        query = query + dot(
-            spread[:, part],
-            jnp.concatenate([up_ref[2 * r], up_ref[2 * r + 1]], axis=0),
-        )
+    wide_low = dot(low, repeat)
+    place = iota((count, wide), 1) // rank
+    for start in range(0, table, some):
+        spread = jnp.where(place + start == adapter_ref[...], wide_low, 0.0).astype(jnp.bfloat16)
+        query = query + dot(spread, up_ref[start : start + some].reshape(wide, columns))
     line = out_ref.shape[2]
     lines = columns // line
     held[...] = jnp.zeros(held.shape, jnp.float32)
@@ -276,7 +268,7 @@
         scores[rows, :] = dot(
             query[rows].astype(jnp.bfloat16), cache_ref[0, 0, :, j * HD : (j + 1) * HD], LAST
         )
-    in_cache = iota((H, cache), 1) < length_ref[0]
+    in_cache = iota((H, cache), 1) < length_ref[0:1, 0:1]
     old = jnp.where(in_cache, scores[...] * scale, -jnp.inf)
     news = [jnp.sum(query * keys, axis=1, keepdims=True) * scale for keys, _ in new]
     peak = jnp.max(old, axis=1, keepdims=True)
@@ -401,9 +393,9 @@
         return outs[:-1], outs[-1]
 
     hidden = hidden_state_input
-    (carried,) = call(first_kernel, [shape((1, width + LANES))], "first")(
-        hidden, scale, row_adapter_index, specs=[vmem, vmem, smem]
-    )
+    carried, length = call(
+        first_kernel, [shape((1, width + LANES)), shape((8, LANES), jnp.int32)], "first"
+    )(hidden, scale, row_adapter_index, cache_length_per_row, specs=[vmem, vmem, smem, smem])
     past = ()
     for step in range(STEPS):
         first, last = step == 0, step == STEPS - 1
@@ -411,21 +403,20 @@
         scratch = [pltpu.VMEM((count, width), jnp.float32)]
         if first:
             token = jnp.zeros((8, LANES), jnp.float32)
-            (query_w, output_w, fresh_w, down_w, cache), token = stash(
+            (query_w, output_w, fresh_w, down_w, cache, up_w), token = stash(
                 token,
-                [query_weight, output_weight, key_value_weight, down, key_value_cache],
-                41 << 20,
+                [query_weight, output_weight, key_value_weight, down, key_value_cache, adapter_up_weight],
+                38 << 20,
             )
             pieces = lax.optimization_barrier((*across(carried, far_steps, count), token))
             carried = jnp.concatenate(pieces[:-1], axis=0)
             pieces = across(carried, near_steps, count)
-            member, up_of = call(
+            member, adapter = call(
                 functools.partial(member_kernel, near, far, width),
-                [shape((count, kept), jnp.int32), pltpu.VMEM((count, rank, columns), jnp.bfloat16)],
+                [shape((count, kept), jnp.int32), shape((count, 1), jnp.int32)],
                 "member",
-                [pltpu.VMEM((count, LANES), jnp.float32), pltpu.SemaphoreType.DMA((count,))],
-                vmem=16 << 20,
-            )(*pieces, me, storage, adapter_up_weight, specs=[vmem] * near + [smem, vmem, pl.ANY])
+                [pltpu.VMEM((count, LANES), jnp.float32)],
+            )(*pieces, me, storage, specs=[vmem] * near + [smem, vmem])
             rows, low = call(
                 functools.partial(low_first_kernel, near, far), outs, "low", scratch
             )(*pieces, me, member, down_w, specs=[vmem] * near + [smem, vmem, vmem])
@@ -448,7 +439,7 @@
             [shape((count, 8, line))],
             "up",
             [pltpu.VMEM((count, 8, line), jnp.float32)],
-        )(*lows, query, fresh, up_of)
+        )(*lows, query, fresh, adapter, up_w)
 
         lines = swap(lines)
         outs = [shape((count, columns // line, line))]
@@ -465,10 +456,10 @@
             moved=2 << 20,
         )(
             lines,
-            cache_length_per_row,
+            length,
             cache,
             *past,
-            specs=[vmem, smem, vmem] + [vmem] * len(past),
+            specs=[vmem] * (3 + len(past)),
         )
         if first:
             past = tuple(outs[1:])

time: 144 us -> 129 us (0.90)
  local copies, waits for them, and re-layouts: 15.1 us -> 2.09 us
  blocking collectives: 59.2 us -> 69.7 us
  waiting for transfers between devices: 19 us -> 13.3 us
  starting transfers between devices: 23.9 us -> 20.4 us
  Pallas kernels: 24.2 us -> 21.1 us
    unnamed x32 -> x6, local copies, waits for them, and re-layouts: 13.8 us -> 0.76 us
    all_to_all x3 -> x4, blocking collectives: 29.4 us -> 39.9 us  [swap(): return lax.all_to_all(blocks, AXIS, split_axis=0, concat_axis=0, tiled=True)]
    all_to_all x1 -> x0, waiting for transfers between devices: 5.95 us -> none  [swap(): return lax.all_to_all(blocks, AXIS, split_axis=0, concat_axis=0, tiled=True)]
    all_to_all x1 -> x0, starting transfers between devices: 3.5 us -> none  [swap(): return lax.all_to_all(blocks, AXIS, split_axis=0, concat_axis=0, tiled=True)]
    pallas_call x19, Pallas kernels: 24.2 us -> 21.1 us  [run(): pl.pallas_call(body, out_shape=outs, in_specs=[pl.BlockSpec(memory_space=...]
  transfers between devices with their start and end apart: 22 -> 21, of which waited for: 11 -> 11; matrix products, arithmetic and copies ran while one was open for 0% -> 0% of each run, Pallas kernels for 8% -> 10%
where the time goes in v5:
time: 129 us; the launch traced here: 128 us
  blocking collectives  69.7 us (54%)
  Pallas kernels  21.1 us (16%)
  starting transfers between devices  20.4 us (16%)
  waiting for transfers between devices  13.3 us (10%)
  local copies, waits for them, and re-layouts  2.09 us (2%)
  between operations  1.44 us (1%)
    all_to_all x4, blocking collectives, swap(): return lax.all_to_all(blocks, AXIS, split_axis=0, concat_axis=0, tiled=True)  39.9 us
    all_to_all x3, blocking collectives, chips_swap(): lax.all_to_all(blocks, AXIS, split_axis=0, concat_axis=0, axis_index_grou...  29.8 us
    pallas_call x19, Pallas kernels, run(): pl.pallas_call(body, out_shape=outs, in_specs=[pl.BlockSpec(memory_space=...  21.1 us
    ppermute x21, starting transfers between devices, shift(): return lax.ppermute(block, AXIS, [(i, i ^ distance) for i in range(count)])  20.4 us
    ppermute x21, waiting for transfers between devices, shift(): return lax.ppermute(block, AXIS, [(i, i ^ distance) for i in range(count)])  13.3 us
  transfers between devices with their start and end apart: 21, of which 11 were waited for; matrix products, arithmetic and copies ran while one was open for 0% of the time, Pallas kernels for 10%

profile of v5, /device:TPU:0, one launch (start us, length us, event | category | flops | bytes accessed | tf_op | source)
XLA Modules:
  0.0 128.1 jit_solution(3851016044519665385)
XLA Ops:
  3.0 5.1 %collective-permute-start.2 = (bf16[1,8320]{1,0:T(2,128)(2,1)S(1)}, bf16[1,8320]{1,0:T(2,128)(2,1)S(1)}, u32[]{:S(2)}, u32[]{:S(2)}) collective-permute-start(bf16[1,8320]{1,0:T(2,128)(2,1)S(1)} %get-tuple-element.37), channel_id=1, source_target_pairs={{0,12},{1,13},{2,14},{3,15},{4,8},{5,9},{6,10},{7,11},{8,4},{9,5},... | collective-permute-start | bytes 49928 | tf_op jit(solution)/shard_map/ppermute | solution.py:32
  8.7 1.3 collective-permute-done.2
  10.0 2.9 %collective-permute-done.1 = bf16[1,8320]{1,0:T(2,128)(2,1)S(1)} collective-permute-done((bf16[1,8320]{1,0:T(2,128)(2,1)S(1)}, bf16[1,8320]{1,0:T(2,128)(2,1)S(1)}, u32[]{:S(2)}, u32[]{:S(2)}) %collective-permute-start.1) | collective-permute-done | bytes 16672 | tf_op jit(solution)/shard_map/ppermute | solution.py:32
  13.2 1.6 %collective-permute-start.4 = (bf16[4,8320]{1,0:T(4,128)(2,1)S(1)}, bf16[4,8320]{1,0:T(4,128)(2,1)S(1)}, u32[]{:S(2)}, u32[]{:S(2)}) collective-permute-start(bf16[4,8320]{1,0:T(4,128)(2,1)S(1)} %pad_maximum_fusion.refs_0_), channel_id=1, source_target_pairs={{0,2},{1,3},{2,0},{3,1},{4,6},{5,7},{6,4},{7,5},{8,10},{9,11},{10,... | collective-permute-start | bytes 199688 | tf_op jit(solution)/shard_map/ppermute | solution.py:32
  15.6 9.5 %stash.1 = (bf16[8192,512]{1,0:T(8,128)(2,1)S(1)}, bf16[512,8192]{1,0:T(8,128)(2,1)S(1)}, bf16[8192,128]{1,0:T(8,128)(2,1)S(1)}, bf16[2,64,8192]{2,1,0:T(8,128)(...) custom-call(f32[8,128]{1,0:T(8,128)} %broadcast_in_dim.11.token_ref, ...), custom_call_target="tpu_custom_call" | custom-call | flops 1048576 | bytes 25165824 | tf_op jit(solution)/shard_map/stash/pallas_call | solution.py:53
  26.2 1.1 collective-permute-start.8
  28.0 1.2 collective-permute-done.8.refs_3_
  29.2 1.7 %collective-permute-done.7.refs_2_ = bf16[16,64]{1,0:T(8,128)(2,1)S(1)} collective-permute-done((bf16[16,64]{1,0:T(8,128)(2,1)S(1)}, bf16[16,64]{1,0:T(8,128)(2,1)S(1)}, u32[]{:S(2)}, u32[]{:S(2)}) %collective-permute-start.7) | collective-permute-done | bytes 2080 | tf_op jit(solution)/shard_map/ppermute | solution.py:32
  30.9 1.5 %collective-permute-start.11 = (bf16[16,64]{1,0:T(8,128)(2,1)S(1)}, bf16[16,64]{1,0:T(8,128)(2,1)S(1)}, u32[]{:S(2)}, u32[]{:S(2)}) collective-permute-start(bf16[16,64]{1,0:T(8,128)(2,1)S(1)} %sum.2.refs_0_), channel_id=1, source_target_pairs={{0,12},{1,13},{2,14},{3,15},{4,8},{5,9},{6,10},{7,11},{8,4},{9,5},... | collective-permute-start | bytes 6152 | tf_op jit(solution)/shard_map/ppermute | solution.py:32
  33.1 2.3 %collective-permute-start.9 = (bf16[16,64]{1,0:T(8,128)(2,1)S(1)}, bf16[16,64]{1,0:T(8,128)(2,1)S(1)}, u32[]{:S(2)}, u32[]{:S(2)}) collective-permute-start(bf16[16,64]{1,0:T(8,128)(2,1)S(1)} %sum.2.refs_0_), channel_id=1, source_target_pairs={{0,4},{1,5},{2,6},{3,7},{4,0},{5,1},{6,2},{7,3},{8,12},{9,13},{10,... | collective-permute-start | bytes 6152 | tf_op jit(solution)/shard_map/ppermute | solution.py:32
  35.4 1.5 %project.2 = (f32[16,512]{1,0:T(8,128)S(1)}, f32[16,128]{1,0:T(8,128)S(1)}) custom-call(bf16[16,8192]{1,0:T(8,128)(2,1)S(1)} %get-tuple-element.44.rows_ref, bf16[8192,512]{1,0:T(8,128)(2,1)S(1)} %get-tuple-element.45.query_w, bf16[8192,128]{1,0:T(8,128)(2,1)S(1)} %get-tuple-element.46.fresh_w), custom_call_target="tpu_custom_call" | custom-call | flops 167772160 | bytes 10485760 | tf_op jit(solution)/shard_map/project/pallas_call | solution.py:53
  37.5 10.5 %all_to_all.35.refs_0_ = bf16[16,8,128]{2,1,0:T(8,128)(2,1)S(1)} all-to-all(bf16[16,8,128]{2,1,0:T(8,128)(2,1)S(1)} %up.2), channel_id=1, replica_groups=mesh['groups'=2,'replica'=16] {'replica'}, dimensions={0} | all-to-all | bytes 65536 | tf_op jit(solution)/shard_map/all_to_all | solution.py:40
  48.0 0.8 attend.2
  48.9 9.1 %all_to_all.36.lines_ref = bf16[16,4,128]{2,1,0:T(4,128)(2,1)S(1)} all-to-all(bf16[16,4,128]{2,1,0:T(4,128)(2,1)S(1)} %get-tuple-element.53), channel_id=1, replica_groups=mesh['groups'=2,'replica'=16] {'replica'}, dimensions={0} | all-to-all | bytes 32768 | tf_op jit(solution)/shard_map/all_to_all | solution.py:40
  57.9 1.3 %output.2 = (f32[8,8192]{1,0:T(8,128)S(1)}, bf16[8,8192]{1,0:T(8,128)(2,1)S(1)}) custom-call(bf16[16,4,128]{2,1,0:T(4,128)(2,1)S(1)} %all_to_all.36.lines_ref, s32[1]{0:T(128)} %bitcast.refs_4_.me_ref, bf16[512,8192]{1,0:T(8,128)(2,1)S(1)} %get-tuple-element.54.weight_ref), custom_call_target="tpu_custom_call" | custom-call | flops 134217728 | bytes 8388608 | tf_op jit(solution)/shard_map/output/pallas_call | solution.py:53
  59.3 1.4 %collective-permute-done.12.other_ref = bf16[8,8192]{1,0:T(8,128)(2,1)S(1)} collective-permute-done((bf16[8,8192]{1,0:T(8,128)(2,1)S(1)}, bf16[8,8192]{1,0:T(8,128)(2,1)S(1)}, u32[]{:S(2)}, u32[]{:S(2)}) %collective-permute-start.12) | collective-permute-done | bytes 131104 | tf_op jit(solution)/shard_map/ppermute | solution.py:32
  60.8 10.0 %all_to_all.37.parts_ref = bf16[8,8,1024]{2,1,0:T(8,128)(2,1)S(1)} all-to-all(bf16[8,8,1024]{2,1,0:T(8,128)(2,1)S(1)} %partial.2), channel_id=1, replica_groups={{0,2,4,6,8,10,12,14},{1,3,5,7,9,11,13,15},{16,18,20,22,24,26,28,30},{17..., dimensions={0} | all-to-all | bytes 262144 | tf_op jit(solution)/shard_map/all_to_all | solution.py:45
  71.1 9.8 %all_to_all.38.own_ref = bf16[8,8,1024]{2,1,0:T(8,128)(2,1)S(1)} all-to-all(bf16[8,8,1024]{2,1,0:T(8,128)(2,1)S(1)} %get-tuple-element.57), channel_id=1, replica_groups={{0,2,4,6,8,10,12,14},{1,3,5,7,9,11,13,15},{16,18,20,22,24,26,28,30},{17..., dimensions={0} | all-to-all | bytes 262144 | tf_op jit(solution)/shard_map/all_to_all | solution.py:45
  80.9 1.3 %collective-permute-done.13.other_ref = bf16[8,8,1024]{2,1,0:T(8,128)(2,1)S(1)} collective-permute-done((bf16[8,8,1024]{2,1,0:T(8,128)(2,1)S(1)}, bf16[8,8,1024]{2,1,0:T(8,128)(2,1)S(1)}, u32[]{:S(2)}, u32[]{:S(2)}) %collective-permute-start.13) | collective-permute-done | bytes 131104 | tf_op jit(solution)/shard_map/ppermute | solution.py:32
  82.3 0.8 low.3
  83.1 1.8 %collective-permute-start.15 = (bf16[16,64]{1,0:T(8,128)(2,1)S(1)}, bf16[16,64]{1,0:T(8,128)(2,1)S(1)}, u32[]{:S(2)}, u32[]{:S(2)}) collective-permute-start(bf16[16,64]{1,0:T(8,128)(2,1)S(1)} %get-tuple-element.58.refs_0_), channel_id=1, source_target_pairs={{0,2},{1,3},{2,0},{3,1},{4,6},{5,7},{6,4},{7,5},{8,10},{9,11},{10,... | collective-permute-start | bytes 6152 | tf_op jit(solution)/shard_map/ppermute | solution.py:32
  85.0 1.2 collective-permute-done.16.refs_3_
  86.7 1.4 %collective-permute-start.19 = (bf16[16,64]{1,0:T(8,128)(2,1)S(1)}, bf16[16,64]{1,0:T(8,128)(2,1)S(1)}, u32[]{:S(2)}, u32[]{:S(2)}) collective-permute-start(bf16[16,64]{1,0:T(8,128)(2,1)S(1)} %sum.3.refs_0_), channel_id=1, source_target_pairs={{0,12},{1,13},{2,14},{3,15},{4,8},{5,9},{6,10},{7,11},{8,4},{9,5},... | collective-permute-start | bytes 6152 | tf_op jit(solution)/shard_map/ppermute | solution.py:32
  88.2 1.1 collective-permute-start.18
  89.3 1.9 %collective-permute-start.17 = (bf16[16,64]{1,0:T(8,128)(2,1)S(1)}, bf16[16,64]{1,0:T(8,128)(2,1)S(1)}, u32[]{:S(2)}, u32[]{:S(2)}) collective-permute-start(bf16[16,64]{1,0:T(8,128)(2,1)S(1)} %sum.3.refs_0_), channel_id=1, source_target_pairs={{0,4},{1,5},{2,6},{3,7},{4,0},{5,1},{6,2},{7,3},{8,12},{9,13},{10,... | collective-permute-start | bytes 6152 | tf_op jit(solution)/shard_map/ppermute | solution.py:32
  91.2 1.5 %project.3 = (f32[16,512]{1,0:T(8,128)S(1)}, f32[16,128]{1,0:T(8,128)S(1)}) custom-call(bf16[16,8192]{1,0:T(8,128)(2,1)S(1)} %get-tuple-element.59.rows_ref, bf16[8192,512]{1,0:T(8,128)(2,1)S(1)} %get-tuple-element.45.query_w, bf16[8192,128]{1,0:T(8,128)(2,1)S(1)} %get-tuple-element.46.fresh_w), custom_call_target="tpu_custom_call" | custom-call | flops 167772160 | bytes 10485760 | tf_op jit(solution)/shard_map/project/pallas_call | solution.py:53
  93.4 11.2 %all_to_all.39.refs_0_ = bf16[16,8,128]{2,1,0:T(8,128)(2,1)S(1)} all-to-all(bf16[16,8,128]{2,1,0:T(8,128)(2,1)S(1)} %up.3), channel_id=1, replica_groups=mesh['groups'=2,'replica'=16] {'replica'}, dimensions={0} | all-to-all | bytes 65536 | tf_op jit(solution)/shard_map/all_to_all | solution.py:40
  104.7 0.8 attend.3
  105.5 9.1 %all_to_all.40.lines_ref = bf16[16,4,128]{2,1,0:T(4,128)(2,1)S(1)} all-to-all(bf16[16,4,128]{2,1,0:T(4,128)(2,1)S(1)} %attend.3), channel_id=1, replica_groups=mesh['groups'=2,'replica'=16] {'replica'}, dimensions={0} | all-to-all | bytes 32768 | tf_op jit(solution)/shard_map/all_to_all | solution.py:40
  114.6 1.3 %output.3 = (f32[8,8192]{1,0:T(8,128)S(1)}, bf16[8,8192]{1,0:T(8,128)(2,1)S(1)}) custom-call(bf16[16,4,128]{2,1,0:T(4,128)(2,1)S(1)} %all_to_all.40.lines_ref, s32[1]{0:T(128)} %bitcast.refs_4_.me_ref, bf16[512,8192]{1,0:T(8,128)(2,1)S(1)} %get-tuple-element.54.weight_ref), custom_call_target="tpu_custom_call" | custom-call | flops 134217728 | bytes 8388608 | tf_op jit(solution)/shard_map/output/pallas_call | solution.py:53
  115.9 1.4 %collective-permute-done.20.other_ref = bf16[8,8192]{1,0:T(8,128)(2,1)S(1)} collective-permute-done((bf16[8,8192]{1,0:T(8,128)(2,1)S(1)}, bf16[8,8192]{1,0:T(8,128)(2,1)S(1)}, u32[]{:S(2)}, u32[]{:S(2)}) %collective-permute-start.20) | collective-permute-done | bytes 131104 | tf_op jit(solution)/shard_map/ppermute | solution.py:32
  117.4 10.0 %all_to_all.41.parts_ref = bf16[8,8,1024]{2,1,0:T(8,128)(2,1)S(1)} all-to-all(bf16[8,8,1024]{2,1,0:T(8,128)(2,1)S(1)} %partial.3), channel_id=1, replica_groups={{0,2,4,6,8,10,12,14},{1,3,5,7,9,11,13,15},{16,18,20,22,24,26,28,30},{17..., dimensions={0} | all-to-all | bytes 262144 | tf_op jit(solution)/shard_map/all_to_all | solution.py:45
  (45 shorter events, 9.4 us)
Async XLA Ops:
  2.0 0.8 copy-start
  3.0 7.0 %collective-permute-start.2 = (bf16[1,8320]{1,0:T(2,128)(2,1)S(1)}, bf16[1,8320]{1,0:T(2,128)(2,1)S(1)}, u32[]{:S(2)}, u32[]{:S(2)}) collective-permute-start(bf16[1,8320]{1,0:T(2,128)(2,1)S(1)} %get-tuple-element.37), channel_id=1, source_target_pairs={{0,12},{1,13},{2,14},{3,15},{4,8},{5,9},{6,10},{7,11},{8,4},{9,5},... | collective-permute-start | bytes 49928 | tf_op jit(solution)/shard_map/ppermute | solution.py:32
  8.1 4.8 %collective-permute-start.1 = (bf16[1,8320]{1,0:T(2,128)(2,1)S(1)}, bf16[1,8320]{1,0:T(2,128)(2,1)S(1)}, u32[]{:S(2)}, u32[]{:S(2)}) collective-permute-start(bf16[1,8320]{1,0:T(2,128)(2,1)S(1)} %get-tuple-element.37), channel_id=1, source_target_pairs={{0,8},{1,9},{2,10},{3,11},{4,12},{5,13},{6,14},{7,15},{8,0},{9,1},... | collective-permute-start | bytes 49928 | tf_op jit(solution)/shard_map/ppermute | solution.py:32
  8.1 4.8 %collective-permute-start = (bf16[1,8320]{1,0:T(2,128)(2,1)S(1)}, bf16[1,8320]{1,0:T(2,128)(2,1)S(1)}, u32[]{:S(2)}, u32[]{:S(2)}) collective-permute-start(bf16[1,8320]{1,0:T(2,128)(2,1)S(1)} %get-tuple-element.37), channel_id=1, source_target_pairs={{0,4},{1,5},{2,6},{3,7},{4,0},{5,1},{6,2},{7,3},{8,12},{9,13},{10,... | collective-permute-start | bytes 49928 | tf_op jit(solution)/shard_map/ppermute | solution.py:32
  13.1 12.0 %collective-permute-start.5 = (bf16[4,8320]{1,0:T(4,128)(2,1)S(1)}, bf16[4,8320]{1,0:T(4,128)(2,1)S(1)}, u32[]{:S(2)}, u32[]{:S(2)}) collective-permute-start(bf16[4,8320]{1,0:T(4,128)(2,1)S(1)} %pad_maximum_fusion.refs_0_), channel_id=1, source_target_pairs={{0,3},{1,2},{2,1},{3,0},{4,7},{5,6},{6,5},{7,4},{8,11},{9,10},{10,... | collective-permute-start | bytes 199688 | tf_op jit(solution)/shard_map/ppermute | solution.py:32
  13.2 12.0 %collective-permute-start.4 = (bf16[4,8320]{1,0:T(4,128)(2,1)S(1)}, bf16[4,8320]{1,0:T(4,128)(2,1)S(1)}, u32[]{:S(2)}, u32[]{:S(2)}) collective-permute-start(bf16[4,8320]{1,0:T(4,128)(2,1)S(1)} %pad_maximum_fusion.refs_0_), channel_id=1, source_target_pairs={{0,2},{1,3},{2,0},{3,1},{4,6},{5,7},{6,4},{7,5},{8,10},{9,11},{10,... | collective-permute-start | bytes 199688 | tf_op jit(solution)/shard_map/ppermute | solution.py:32
  14.7 10.4 %collective-permute-start.3 = (bf16[4,8320]{1,0:T(4,128)(2,1)S(1)}, bf16[4,8320]{1,0:T(4,128)(2,1)S(1)}, u32[]{:S(2)}, u32[]{:S(2)}) collective-permute-start(bf16[4,8320]{1,0:T(4,128)(2,1)S(1)} %pad_maximum_fusion.refs_0_), channel_id=1, source_target_pairs={{0,1},{1,0},{2,3},{3,2},{4,5},{5,4},{6,7},{7,6},{8,9},{9,8},{10,11... | collective-permute-start | bytes 199688 | tf_op jit(solution)/shard_map/ppermute | solution.py:32
  15.6 9.5 %copy-start.2 = (s32[32]{0:T(128)S(1)}, s32[32]{0:T(128)}, u32[]{:S(2)}) copy-start(s32[32]{0:T(128)} %param.19) | copy-start | bytes 388
  26.2 3.1 %collective-permute-start.8 = (bf16[16,64]{1,0:T(8,128)(2,1)S(1)}, bf16[16,64]{1,0:T(8,128)(2,1)S(1)}, u32[]{:S(2)}, u32[]{:S(2)}) collective-permute-start(bf16[16,64]{1,0:T(8,128)(2,1)S(1)} %get-tuple-element.43.refs_0_), channel_id=1, source_target_pairs={{0,3},{1,2},{2,1},{3,0},{4,7},{5,6},{6,5},{7,4},{8,11},{9,10},{10,... | collective-permute-start | bytes 6152 | tf_op jit(solution)/shard_map/ppermute | solution.py:32
  27.3 3.6 %collective-permute-start.7 = (bf16[16,64]{1,0:T(8,128)(2,1)S(1)}, bf16[16,64]{1,0:T(8,128)(2,1)S(1)}, u32[]{:S(2)}, u32[]{:S(2)}) collective-permute-start(bf16[16,64]{1,0:T(8,128)(2,1)S(1)} %get-tuple-element.43.refs_0_), channel_id=1, source_target_pairs={{0,2},{1,3},{2,0},{3,1},{4,6},{5,7},{6,4},{7,5},{8,10},{9,11},{10,... | collective-permute-start | bytes 6152 | tf_op jit(solution)/shard_map/ppermute | solution.py:32
  28.0 2.9 %collective-permute-start.6 = (bf16[16,64]{1,0:T(8,128)(2,1)S(1)}, bf16[16,64]{1,0:T(8,128)(2,1)S(1)}, u32[]{:S(2)}, u32[]{:S(2)}) collective-permute-start(bf16[16,64]{1,0:T(8,128)(2,1)S(1)} %get-tuple-element.43.refs_0_), channel_id=1, source_target_pairs={{0,1},{1,0},{2,3},{3,2},{4,5},{5,4},{6,7},{7,6},{8,9},{9,8},{10,11... | collective-permute-start | bytes 6152 | tf_op jit(solution)/shard_map/ppermute | solution.py:32
  30.9 5.9 %collective-permute-start.11 = (bf16[16,64]{1,0:T(8,128)(2,1)S(1)}, bf16[16,64]{1,0:T(8,128)(2,1)S(1)}, u32[]{:S(2)}, u32[]{:S(2)}) collective-permute-start(bf16[16,64]{1,0:T(8,128)(2,1)S(1)} %sum.2.refs_0_), channel_id=1, source_target_pairs={{0,12},{1,13},{2,14},{3,15},{4,8},{5,9},{6,10},{7,11},{8,4},{9,5},... | collective-permute-start | bytes 6152 | tf_op jit(solution)/shard_map/ppermute | solution.py:32
  32.4 4.5 %collective-permute-start.10 = (bf16[16,64]{1,0:T(8,128)(2,1)S(1)}, bf16[16,64]{1,0:T(8,128)(2,1)S(1)}, u32[]{:S(2)}, u32[]{:S(2)}) collective-permute-start(bf16[16,64]{1,0:T(8,128)(2,1)S(1)} %sum.2.refs_0_), channel_id=1, source_target_pairs={{0,8},{1,9},{2,10},{3,11},{4,12},{5,13},{6,14},{7,15},{8,0},{9,1},... | collective-permute-start | bytes 6152 | tf_op jit(solution)/shard_map/ppermute | solution.py:32
  33.1 3.9 %collective-permute-start.9 = (bf16[16,64]{1,0:T(8,128)(2,1)S(1)}, bf16[16,64]{1,0:T(8,128)(2,1)S(1)}, u32[]{:S(2)}, u32[]{:S(2)}) collective-permute-start(bf16[16,64]{1,0:T(8,128)(2,1)S(1)} %sum.2.refs_0_), channel_id=1, source_target_pairs={{0,4},{1,5},{2,6},{3,7},{4,0},{5,1},{6,2},{7,3},{8,12},{9,13},{10,... | collective-permute-start | bytes 6152 | tf_op jit(solution)/shard_map/ppermute | solution.py:32
  57.9 12.8 %copy-start.1 = (bf16[1,8192]{1,0:T(2,128)(2,1)S(1)}, bf16[1,8192]{1,0:T(2,128)(2,1)}, u32[]{:S(2)}) copy-start(bf16[1,8192]{1,0:T(2,128)(2,1)} %hidden_ref.3) | copy-start | bytes 49156
  59.2 1.4 %collective-permute-start.12 = (bf16[8,8192]{1,0:T(8,128)(2,1)S(1)}, bf16[8,8192]{1,0:T(8,128)(2,1)S(1)}, u32[]{:S(2)}, u32[]{:S(2)}) collective-permute-start(bf16[8,8192]{1,0:T(8,128)(2,1)S(1)} %get-tuple-element.56), channel_id=1, source_target_pairs={{0,1},{1,0},{2,3},{3,2},{4,5},{5,4},{6,7},{7,6},{8,9},{9,8},{10,11... | collective-permute-start | bytes 393224 | tf_op jit(solution)/shard_map/ppermute | solution.py:32
  80.9 1.3 %collective-permute-start.13 = (bf16[8,8,1024]{2,1,0:T(8,128)(2,1)S(1)}, bf16[8,8,1024]{2,1,0:T(8,128)(2,1)S(1)}, u32[]{:S(2)}, u32[]{:S(2)}) collective-permute-start(bf16[8,8,1024]{2,1,0:T(8,128)(2,1)S(1)} %all_to_all.38.own_ref), channel_id=1, source_target_pairs={{0,1},{1,0},{2,3},{3,2},{4,5},{5,4},{6,7},{7,6},{8,9},{9,8},{10,11... | collective-permute-start | bytes 393224 | tf_op jit(solution)/shard_map/ppermute | solution.py:32
  83.1 3.1 %collective-permute-start.16 = (bf16[16,64]{1,0:T(8,128)(2,1)S(1)}, bf16[16,64]{1,0:T(8,128)(2,1)S(1)}, u32[]{:S(2)}, u32[]{:S(2)}) collective-permute-start(bf16[16,64]{1,0:T(8,128)(2,1)S(1)} %get-tuple-element.58.refs_0_), channel_id=1, source_target_pairs={{0,3},{1,2},{2,1},{3,0},{4,7},{5,6},{6,5},{7,4},{8,11},{9,10},{10,... | collective-permute-start | bytes 6152 | tf_op jit(solution)/shard_map/ppermute | solution.py:32
  83.1 3.7 %collective-permute-start.15 = (bf16[16,64]{1,0:T(8,128)(2,1)S(1)}, bf16[16,64]{1,0:T(8,128)(2,1)S(1)}, u32[]{:S(2)}, u32[]{:S(2)}) collective-permute-start(bf16[16,64]{1,0:T(8,128)(2,1)S(1)} %get-tuple-element.58.refs_0_), channel_id=1, source_target_pairs={{0,2},{1,3},{2,0},{3,1},{4,6},{5,7},{6,4},{7,5},{8,10},{9,11},{10,... | collective-permute-start | bytes 6152 | tf_op jit(solution)/shard_map/ppermute | solution.py:32
  84.9 1.9 %collective-permute-start.14 = (bf16[16,64]{1,0:T(8,128)(2,1)S(1)}, bf16[16,64]{1,0:T(8,128)(2,1)S(1)}, u32[]{:S(2)}, u32[]{:S(2)}) collective-permute-start(bf16[16,64]{1,0:T(8,128)(2,1)S(1)} %get-tuple-element.58.refs_0_), channel_id=1, source_target_pairs={{0,1},{1,0},{2,3},{3,2},{4,5},{5,4},{6,7},{7,6},{8,9},{9,8},{10,11... | collective-permute-start | bytes 6152 | tf_op jit(solution)/shard_map/ppermute | solution.py:32
  86.7 5.9 %collective-permute-start.19 = (bf16[16,64]{1,0:T(8,128)(2,1)S(1)}, bf16[16,64]{1,0:T(8,128)(2,1)S(1)}, u32[]{:S(2)}, u32[]{:S(2)}) collective-permute-start(bf16[16,64]{1,0:T(8,128)(2,1)S(1)} %sum.3.refs_0_), channel_id=1, source_target_pairs={{0,12},{1,13},{2,14},{3,15},{4,8},{5,9},{6,10},{7,11},{8,4},{9,5},... | collective-permute-start | bytes 6152 | tf_op jit(solution)/shard_map/ppermute | solution.py:32
  88.2 4.5 %collective-permute-start.18 = (bf16[16,64]{1,0:T(8,128)(2,1)S(1)}, bf16[16,64]{1,0:T(8,128)(2,1)S(1)}, u32[]{:S(2)}, u32[]{:S(2)}) collective-permute-start(bf16[16,64]{1,0:T(8,128)(2,1)S(1)} %sum.3.refs_0_), channel_id=1, source_target_pairs={{0,8},{1,9},{2,10},{3,11},{4,12},{5,13},{6,14},{7,15},{8,0},{9,1},... | collective-permute-start | bytes 6152 | tf_op jit(solution)/shard_map/ppermute | solution.py:32
  89.3 3.6 %collective-permute-start.17 = (bf16[16,64]{1,0:T(8,128)(2,1)S(1)}, bf16[16,64]{1,0:T(8,128)(2,1)S(1)}, u32[]{:S(2)}, u32[]{:S(2)}) collective-permute-start(bf16[16,64]{1,0:T(8,128)(2,1)S(1)} %sum.3.refs_0_), channel_id=1, source_target_pairs={{0,4},{1,5},{2,6},{3,7},{4,0},{5,1},{6,2},{7,3},{8,12},{9,13},{10,... | collective-permute-start | bytes 6152 | tf_op jit(solution)/shard_map/ppermute | solution.py:32
  115.9 1.4 %collective-permute-start.20 = (bf16[8,8192]{1,0:T(8,128)(2,1)S(1)}, bf16[8,8192]{1,0:T(8,128)(2,1)S(1)}, u32[]{:S(2)}, u32[]{:S(2)}) collective-permute-start(bf16[8,8192]{1,0:T(8,128)(2,1)S(1)} %get-tuple-element.65), channel_id=1, source_target_pairs={{0,1},{1,0},{2,3},{3,2},{4,5},{5,4},{6,7},{7,6},{8,9},{9,8},{10,11... | collective-permute-start | bytes 393224 | tf_op jit(solution)/shard_map/ppermute | solution.py:32

commit v6 on v5

--- a/solution.py
+++ b/solution.py
@@ -47,7 +47,7 @@
     )
 
 
-def call(body, outs, name, scratch=(), vmem=20 << 20, flops=1 << 20, moved=1 << 18):
+def kernel(body, outs, name, scratch=(), vmem=20 << 20, flops=1 << 20, moved=1 << 18):
     def run(*operands, specs=None):
         specs = specs or [pltpu.VMEM] * len(operands)
         return pl.pallas_call(
@@ -95,8 +95,10 @@
     out_ref[:, :width] = normalized(hidden, scale_ref[...].astype(jnp.float32))
     digit = iota((1, LANES), 1)
     adapter = adapter_ref[0]
-    high, low = adapter // 256, adapter % 256
-    digits = jnp.where(digit == 0, low, jnp.where(digit == 1, high, 0)).astype(jnp.float32)
+    length = length_ref[0]
+    digits = jnp.where(digit == 0, adapter % 256, jnp.where(digit == 1, adapter // 256, 0))
+    digits = jnp.where(digit == 2, length % 256, jnp.where(digit == 3, length // 256, digits))
+    digits = digits.astype(jnp.float32)
     out_ref[:, width:] = digits.astype(jnp.bfloat16)
 
 
@@ -114,8 +116,9 @@
 
 
 def member_kernel(near, far, width, *refs):
-    pieces, refs = refs[:near], refs[near:]
-    me_ref, storage_ref, member_ref, adapter_ref, held = refs
+    pieces = refs[:near]
+    me_ref, storage_ref = refs[near : near + 2]
+    member_ref, adapter_ref, lengths_ref, held = refs[-4:]
     kept = member_ref.shape[1]
     count = near * far
     me = me_ref[0]
@@ -125,13 +128,14 @@
             held[pl.ds(me ^ (k * near + l), 1), :] = digits[k : k + 1]
     adapter = (held[:, 0:1] + 256.0 * held[:, 1:2]).astype(jnp.int32)
     adapter_ref[...] = adapter
+    lengths_ref[...] = (held[:, 2:3] + 256.0 * held[:, 3:4]).astype(jnp.int32)
     table = storage_ref.shape[1]
     chosen = jnp.where(iota((count, table), 1) == adapter, storage_ref[...], 0)
     storage = jnp.sum(chosen.astype(jnp.float32), axis=1, keepdims=True).astype(jnp.int32)
     member_ref[...] = (storage - me * kept == iota((count, kept), 1)).astype(jnp.int32)
 
 
-def low_terms(held, member_ref, down_ref, rows_ref, low_ref):
+def low_terms(held, member_ref, down_ref, fresh_w, rows_ref, low_ref, fresh_ref):
     rows = held[...].astype(jnp.bfloat16)
     rows_ref[...] = rows
     low = jnp.zeros(low_ref.shape, jnp.float32)
@@ -139,20 +143,23 @@
         part = dot(rows, down_ref[index], LAST)
         low = jnp.where(member_ref[:, index : index + 1] > 0, part, low)
     low_ref[...] = low.astype(jnp.bfloat16)
+    fresh_ref[...] = dot(rows, fresh_w[...]).astype(jnp.bfloat16)
 
 
 def low_first_kernel(near, far, *refs):
-    pieces, refs = refs[:near], refs[near:]
-    me_ref, member_ref, down_ref, rows_ref, low_ref, held = refs
+    pieces = refs[:near]
+    me_ref, member_ref, down_ref, fresh_w = refs[near : near + 4]
+    rows_ref, low_ref, fresh_ref, held = refs[-4:]
     width = held.shape[1]
     for l in range(near):
         block = pieces[l][:, :width].astype(jnp.float32)
         for k in range(far):
             held[pl.ds(me_ref[0] ^ (k * near + l), 1), :] = block[k : k + 1]
-    low_terms(held, member_ref, down_ref, rows_ref, low_ref)
-
-
-def low_later_kernel(own_ref, other_ref, me_ref, member_ref, down_ref, rows_ref, low_ref, held):
+    low_terms(held, member_ref, down_ref, fresh_w, rows_ref, low_ref, fresh_ref)
+
+
+def low_later_kernel(own_ref, other_ref, me_ref, member_ref, down_ref, fresh_w, *refs):
+    rows_ref, low_ref, fresh_ref, held = refs
     core = me_ref[0] % CORES
     for ref, flip in ((own_ref, 0), (other_ref, 1)):
         wide = ref.shape[2]
@@ -161,23 +168,27 @@
             row = pl.ds(k * CORES + (core ^ flip), 1)
             for i in range(FOLD):
                 held[row, i * wide : (i + 1) * wide] = block[i : i + 1]
-    low_terms(held, member_ref, down_ref, rows_ref, low_ref)
-
-
-def sum_kernel(*refs):
+    low_terms(held, member_ref, down_ref, fresh_w, rows_ref, low_ref, fresh_ref)
+
+
+def join_kernel(amount, *refs):
+    rows = [ref[...].astype(jnp.float32) for ref in refs[:amount]]
+    refs[-1][...] = jnp.concatenate(rows, axis=0).astype(refs[-1].dtype)
+
+
+def sum_kernel(amount, *refs):
     total = refs[0][...].astype(jnp.float32)
-    for ref in refs[1:-1]:
+    for ref in refs[1:amount]:
         total = total + ref[...].astype(jnp.float32)
     refs[-1][...] = total.astype(refs[-1].dtype)
 
 
-def project_kernel(rows_ref, query_w, fresh_w, query_ref, fresh_ref):
+def project_kernel(rows_ref, query_w, *refs):
+    query_ref = refs[-1]
     query_ref[...] = dot(rows_ref[...], query_w[...])
-    fresh_ref[...] = dot(rows_ref[...], fresh_w[...])
-
-
-def up_kernel(parts, *refs):
-    lows, (query_ref, fresh_ref, adapter_ref, up_ref, out_ref, held) = refs[:parts], refs[parts:]
+
+
+def up_terms(lows, query_ref, adapter_ref, up_ref):
     count, columns = query_ref.shape
     rank = lows[0].shape[1]
     low = lows[0][...].astype(jnp.float32)
@@ -194,12 +205,19 @@
     for start in range(0, table, some):
         spread = jnp.where(place + start == adapter_ref[...], wide_low, 0.0).astype(jnp.bfloat16)
         query = query + dot(spread, up_ref[start : start + some].reshape(wide, columns))
+    return query
+
+
+def up_kernel(parts, *refs):
+    lows, (query_ref, fresh_ref, adapter_ref, up_ref, out_ref, held) = refs[:parts], refs[parts:]
+    count, columns = query_ref.shape
+    query = up_terms(lows, query_ref, adapter_ref, up_ref)
     line = out_ref.shape[2]
     lines = columns // line
     held[...] = jnp.zeros(held.shape, jnp.float32)
     for c in range(lines):
         held[:, c, :] = query[:, c * line : (c + 1) * line]
-    fresh = fresh_ref[...]
+    fresh = fresh_ref[...].astype(jnp.float32)
     if fresh.shape[1] < line:
         fresh = jnp.concatenate(
             [fresh, jnp.zeros((count, line - fresh.shape[1]), jnp.float32)], axis=1
@@ -307,13 +325,11 @@
             out_ref[k] = out[k : k + 1].astype(jnp.bfloat16)
 
 
-def output_kernel(lines_ref, me_ref, weight_ref, own_ref, away_ref, held):
-    count, each, line = lines_ref.shape
+def output_terms(held, each, core, weight_ref, own_ref, away_ref):
+    count = held.shape[0]
     chips = count // CORES
-    for k in range(count):
-        held[k, :each, :] = lines_ref[k].astype(jnp.float32)
     slot = iota((count, count), 0)
-    origin = (slot % chips) * CORES + ((me_ref[0] % CORES) ^ (slot // chips))
+    origin = (slot % chips) * CORES + (core ^ (slot // chips))
     order = (iota((count, count), 1) == origin).astype(jnp.bfloat16)
     rows = jnp.concatenate(
         [dot(order, held[:, c, :].astype(jnp.bfloat16)).astype(jnp.bfloat16) for c in range(each)],
@@ -326,6 +342,76 @@
         out = dot(rows, weight_ref[:, part])
         own_ref[:, part] = out[:chips]
         away_ref[:, part] = out[chips:].astype(jnp.bfloat16)
+
+
+def output_kernel(lines_ref, me_ref, weight_ref, own_ref, away_ref, held):
+    count, each, line = lines_ref.shape
+    for k in range(count):
+        held[k, :each, :] = lines_ref[k].astype(jnp.float32)
+    output_terms(held, each, me_ref[0] % CORES, weight_ref, own_ref, away_ref)
+
+
+def cut_kernel(me_ref, cache_hbm, *refs):
+    outs, sems = refs[:-1], refs[-1]
+    copies = []
+    for d, out in enumerate(outs):
+        lanes = pl.ds(pl.multiple_of(((me_ref[0] // CORES) ^ d) * HD, HD), HD)
+        copies.append(pltpu.make_async_copy(cache_hbm.at[0, :, :, lanes], out, sems.at[d]))
+    for copy in copies:
+        copy.start()
+    for copy in copies:
+        copy.wait()
+
+
+def heads_kernel(parts, steps, *refs):
+    lows, refs = refs[:parts], refs[parts:]
+    query_ref, adapter_ref, up_ref, lengths_ref, me_ref, weight_ref = refs[:6]
+    news, refs = refs[6 : 6 + 2 * steps], refs[6 + 2 * steps :]
+    own_ref, away_ref, held, mixed_ref, new_ref = refs[-5:]
+    blocks = refs[:-5]
+    count, columns = query_ref.shape
+    chips = count // CORES
+    each = columns // HD
+    lines = held.shape[1]
+    chip, core = me_ref[0] // CORES, me_ref[0] % CORES
+    query = up_terms(lows, query_ref, adapter_ref, up_ref).astype(jnp.bfloat16)
+    held[...] = jnp.zeros(held.shape, jnp.float32)
+    for c in range(each):
+        held[:, c, :] = query[:, c * HD : (c + 1) * HD].astype(jnp.float32)
+    for t in range(steps):
+        mine, other = news[2 * t][...].astype(jnp.float32), news[2 * t + 1][...].astype(jnp.float32)
+        new_ref[2 * t] = jnp.where(core == 0, mine, other)
+        new_ref[2 * t + 1] = jnp.where(core == 0, other, mine)
+    scale = 1.0 / math.sqrt(HD)
+    rows = [((chip ^ (b % chips)) * CORES) + (core ^ (b // chips)) for b in range(count)]
+    old, fresh = [], [[] for _ in range(steps)]
+    for row, block in zip(rows, blocks):
+        query = held[row]
+        score = dot(query.astype(jnp.bfloat16), block[0], LAST) * scale
+        length = lengths_ref[pl.ds(row, 1), :]
+        old.append(jnp.where(iota(score.shape, 1) < length, score, -jnp.inf))
+        for t in range(steps):
+            keys = new_ref[2 * t, pl.ds(row, 1), :]
+            fresh[t].append(jnp.sum(query * keys, axis=1, keepdims=True) * scale)
+    old = jnp.concatenate(old, axis=0)
+    fresh = [jnp.concatenate(scores, axis=0) for scores in fresh]
+    peak = jnp.max(old, axis=1, keepdims=True)
+    for scores in fresh:
+        peak = jnp.maximum(peak, scores)
+    old = jnp.exp(old - peak)
+    fresh = [jnp.exp(scores - peak) for scores in fresh]
+    total = jnp.sum(old, axis=1, keepdims=True)
+    for scores in fresh:
+        total = total + scores
+    old = (old / total).astype(jnp.bfloat16).astype(jnp.float32)
+    fresh = [(scores / total).astype(jnp.bfloat16).astype(jnp.float32) for scores in fresh]
+    for b, (row, block) in enumerate(zip(rows, blocks)):
+        part = slice(b * lines, (b + 1) * lines)
+        mixed = dot(old[part].astype(jnp.bfloat16), block[1])
+        for t in range(steps):
+            mixed = mixed + fresh[t][part] * new_ref[2 * t + 1, pl.ds(row, 1), :]
+        mixed_ref[row] = mixed
+    output_terms(mixed_ref, each, core, weight_ref, own_ref, away_ref)
 
 
 def partial_kernel(own_ref, other_ref, out_ref):
@@ -376,6 +462,7 @@
     fresh_columns = key_value_weight.shape[1]
     line = min(HD, columns)
     smem, vmem = pltpu.SMEM, pltpu.VMEM
+    call = functools.partial(kernel, vmem=min(20 << 20, (count * 3 // 4) << 20))
     me = lax.axis_index(AXIS).astype(jnp.int32).reshape(1)
     down = adapter_down_weight.transpose(0, 2, 1)
     scale = attention_norm_scale[None]
@@ -392,48 +479,14 @@
         )(token, *arrays, specs=[vmem] + [pl.ANY] * len(arrays))
         return outs[:-1], outs[-1]
 
-    hidden = hidden_state_input
-    carried, length = call(
-        first_kernel, [shape((1, width + LANES)), shape((8, LANES), jnp.int32)], "first"
-    )(hidden, scale, row_adapter_index, cache_length_per_row, specs=[vmem, vmem, smem, smem])
-    past = ()
-    for step in range(STEPS):
-        first, last = step == 0, step == STEPS - 1
-        outs = [shape((count, width)), shape((count, rank))]
-        scratch = [pltpu.VMEM((count, width), jnp.float32)]
-        if first:
-            token = jnp.zeros((8, LANES), jnp.float32)
-            (query_w, output_w, fresh_w, down_w, cache, up_w), token = stash(
-                token,
-                [query_weight, output_weight, key_value_weight, down, key_value_cache, adapter_up_weight],
-                38 << 20,
-            )
-            pieces = lax.optimization_barrier((*across(carried, far_steps, count), token))
-            carried = jnp.concatenate(pieces[:-1], axis=0)
-            pieces = across(carried, near_steps, count)
-            member, adapter = call(
-                functools.partial(member_kernel, near, far, width),
-                [shape((count, kept), jnp.int32), shape((count, 1), jnp.int32)],
-                "member",
-                [pltpu.VMEM((count, LANES), jnp.float32)],
-            )(*pieces, me, storage, specs=[vmem] * near + [smem, vmem])
-            rows, low = call(
-                functools.partial(low_first_kernel, near, far), outs, "low", scratch
-            )(*pieces, me, member, down_w, specs=[vmem] * near + [smem, vmem, vmem])
-        else:
-            own = chips_swap(carried, count)
-            rows, low = call(low_later_kernel, outs, "low", scratch)(
-                own, shift(own, 1, count), me, member, down_w, specs=[vmem, vmem, smem, vmem, vmem]
-            )
-        (low,) = call(sum_kernel, [shape((count, rank))], "sum")(*across(low, near_steps, count))
-        lows = across(low, far_steps, count)
-        query, fresh = call(
-            project_kernel,
-            [shape((count, columns), jnp.float32), shape((count, fresh_columns), jnp.float32)],
-            "project",
-            flops=2 * count * width * (columns + fresh_columns),
-            moved=2 * width * (columns + fresh_columns),
-        )(rows, query_w, fresh_w)
+    past, held_cache, moved = [], [], []
+
+    def after(*distances):
+        return [moved[d - 1] for d in distances] if moved else []
+
+
+    def by_rows(step, lows, query, fresh):
+        first = step == 0
         (lines,) = call(
             functools.partial(up_kernel, far),
             [shape((count, 8, line))],
@@ -457,12 +510,12 @@
         )(
             lines,
             length,
-            cache,
+            held_cache[0],
             *past,
             specs=[vmem] * (3 + len(past)),
         )
         if first:
-            past = tuple(outs[1:])
+            past.extend(outs[1:])
 
         lines = swap(outs[0])
         own, away = call(
@@ -473,6 +526,114 @@
             flops=2 * count * width * columns,
             moved=2 * width * columns,
         )(lines, me, output_w, specs=[vmem, smem, vmem])
+        return own, away
+
+    hidden = hidden_state_input
+    carried, length = call(
+        first_kernel, [shape((1, width + LANES)), shape((8, LANES), jnp.int32)], "first"
+    )(hidden, scale, row_adapter_index, cache_length_per_row, specs=[vmem, vmem, smem, smem])
+    news, blocks = [], []
+    by_heads = columns * CORES == GROUP * HD and count == CORES * KVH
+    for step in range(STEPS):
+        first, last = step == 0, step == STEPS - 1
+        low_outs = [shape((count, width)), shape((count, rank)), shape((count, fresh_columns))]
+        scratch = [pltpu.VMEM((count, width), jnp.float32)]
+        if first:
+            token = jnp.zeros((8, LANES), jnp.float32)
+            arrays = [query_weight, output_weight, key_value_weight, down, adapter_up_weight]
+            if by_heads:
+                blocks = call(
+                    cut_kernel,
+                    [shape((2, key_value_cache.shape[2], HD))] * chips,
+                    "cut",
+                    [pltpu.SemaphoreType.DMA((chips,))],
+                )(me, key_value_cache, specs=[smem, pl.ANY])
+                moved.extend(shift(b, CORES * d, count) for d, b in enumerate(blocks) if d)
+                blocks = [blocks[0]] + moved
+                blocks = blocks + [shift(b, 1, count) for b in blocks]
+            else:
+                arrays.append(key_value_cache)
+            outs, token = stash(token, arrays, 30 << 20)
+            query_w, output_w, fresh_w, down_w, up_w = outs[:5]
+            held_cache.append(outs[-1])
+            pieces = across(carried, far_steps, count)
+            (carried,) = call(
+                functools.partial(join_kernel, far), [shape((far, width + LANES))], "join"
+            )(*pieces, *after(1, 2), specs=[vmem] * far + [pl.ANY] * len(after(1, 2)))
+            pieces = across(carried, near_steps, count)
+            member, adapter, lengths = call(
+                functools.partial(member_kernel, near, far, width),
+                [shape((count, kept), jnp.int32)] + [shape((count, 1), jnp.int32)] * 2,
+                "member",
+                [pltpu.VMEM((count, LANES), jnp.float32)],
+            )(
+                *pieces,
+                me,
+                storage,
+                *after(4, 6),
+                specs=[vmem] * near + [smem, vmem] + [pl.ANY] * len(after(4, 6)),
+            )
+            rows, low, fresh = call(
+                functools.partial(low_first_kernel, near, far), low_outs, "low", scratch
+            )(
+                *pieces,
+                me,
+                member,
+                down_w,
+                fresh_w,
+                specs=[vmem] * near + [smem] + [vmem] * 3,
+            )
+        else:
+            own = chips_swap(carried, count)
+            rows, low, fresh = call(low_later_kernel, low_outs, "low", scratch)(
+                own,
+                shift(own, 1, count),
+                me,
+                member,
+                down_w,
+                fresh_w,
+                specs=[vmem, vmem, smem, vmem, vmem, vmem],
+            )
+        behind = after(5) if first else []
+        (low,) = call(functools.partial(sum_kernel, near), [shape((count, rank))], "sum")(
+            *across(low, near_steps, count),
+            *behind,
+            specs=[vmem] * near + [pl.ANY] * len(behind),
+        )
+        lows = across(low, far_steps, count)
+        behind = after(3) if first else []
+        (query,) = call(
+            project_kernel,
+            [shape((count, columns), jnp.float32)],
+            "project",
+            flops=2 * count * width * columns,
+            moved=2 * width * columns,
+        )(rows, query_w, *behind, specs=[vmem] * 2 + [pl.ANY] * len(behind))
+        if by_heads:
+            fresh = lax.ppermute(fresh, AXIS, [(i, 2 * (i % KVH) + i // KVH) for i in range(count)])
+            news = news + [fresh, shift(fresh, 1, count)]
+            own, away = call(
+                functools.partial(heads_kernel, far, step + 1),
+                [shape((chips, width), jnp.float32), shape((chips, width))],
+                "heads",
+                [pltpu.VMEM((count, 8, HD), jnp.float32)] * 2
+                + [pltpu.VMEM((2 * (step + 1), count, HD), jnp.float32)],
+                flops=2 * count * width * columns,
+                moved=2 * width * columns,
+            )(
+                *lows,
+                query,
+                adapter,
+                up_w,
+                lengths,
+                me,
+                output_w,
+                *news,
+                *blocks,
+                specs=[vmem] * (far + 4) + [smem] + [vmem] * (1 + len(news) + len(blocks)),
+            )
+        else:
+            own, away = by_rows(step, lows, query, fresh)
 
         (parts,) = call(partial_kernel, [shape((chips, FOLD, width // FOLD))], "partial")(
             own, shift(away, 1, count)

time: 129 us -> 140 us (1.085)
  blocking collectives: 69.7 us -> 31.8 us
  starting transfers between devices: 20.4 us -> 49.1 us
  waiting for transfers between devices: 13.3 us -> 34 us
    all_to_all x4 -> x0, blocking collectives: 39.9 us -> none  [swap(): return lax.all_to_all(blocks, AXIS, split_axis=0, concat_axis=0, tiled=True)]
    ppermute x21 -> x38, starting transfers between devices: 20.4 us -> 47.6 us  [shift(): return lax.ppermute(block, AXIS, [(i, i ^ distance) for i in range(count)])]
    ppermute x21 -> x38, waiting for transfers between devices: 13.3 us -> 34 us  [shift(): return lax.ppermute(block, AXIS, [(i, i ^ distance) for i in range(count)])]
    all_to_all x3, blocking collectives: 29.8 us -> 31.8 us  [chips_swap(): lax.all_to_all(blocks, AXIS, split_axis=0, concat_axis=0, axis_index_grou...]
    ppermute x0 -> x2, starting transfers between devices: none -> 1.5 us  [shards(): lax.ppermute(fresh, AXIS, [(i, 2 * (i % KVH) + i // KVH) for i in range(c...]
    pallas_call x19 -> x17, Pallas kernels: 21.1 us -> 21.5 us  [run(): pl.pallas_call(body, out_shape=outs, in_specs=[pl.BlockSpec(memory_space=...]
  transfers between devices with their start and end apart: 21 -> 40, of which waited for: 11 -> 16; matrix products, arithmetic and copies ran while one was open for 0% -> 0% of each run, Pallas kernels for 10% -> 9%
where the time goes in v6:
time: 140 us
  starting transfers between devices  49.1 us (35%)
  waiting for transfers between devices  34 us (24%)
  blocking collectives  31.8 us (23%)
  Pallas kernels  21.5 us (15%)
  local copies, waits for them, and re-layouts  1.62 us (1%)
  between operations  1.48 us (1%)
    ppermute x38, starting transfers between devices, shift(): return lax.ppermute(block, AXIS, [(i, i ^ distance) for i in range(count)])  47.6 us
    ppermute x38, waiting for transfers between devices, shift(): return lax.ppermute(block, AXIS, [(i, i ^ distance) for i in range(count)])  34 us
    all_to_all x3, blocking collectives, chips_swap(): lax.all_to_all(blocks, AXIS, split_axis=0, concat_axis=0, axis_index_grou...  31.8 us
    pallas_call x17, Pallas kernels, run(): pl.pallas_call(body, out_shape=outs, in_specs=[pl.BlockSpec(memory_space=...  21.5 us
  transfers between devices with their start and end apart: 40, of which 16 were waited for; matrix products, arithmetic and copies ran while one was open for 0% of the time, Pallas kernels for 9%

profile of v6, /device:TPU:0, one launch (start us, length us, event | category | flops | bytes accessed | tf_op | source)
XLA Modules:
  0.0 139.6 jit_solution(1119943428234020927)
XLA Ops:
  0.0 1.6 %copy-done = bf16[1,2,512,1024]{3,2,1,0:T(8,128)(2,1)S(1)} copy-done((bf16[1,2,512,1024]{3,2,1,0:T(8,128)(2,1)S(1)}, bf16[1,2,512,1024]{3,2,1,0:T(8,128)(2,1)}, u32[]{:S(2)}) %copy-start) | copy-done | bytes 2097176
  2.2 3.0 %collective-permute-start.3 = (bf16[2,512,128]{2,1,0:T(8,128)(2,1)S(1)}, bf16[2,512,128]{2,1,0:T(8,128)(2,1)S(1)}, u32[]{:S(2)}, u32[]{:S(2)}) collective-permute-start(bf16[2,512,128]{2,1,0:T(8,128)(2,1)S(1)} %get-tuple-element.35), channel_id=1, source_target_pairs={{0,2},{1,3},{2,0},{3,1},{4,6},{5,7},{6,4},{7,5},{8,10},{9,11},{10,... | collective-permute-start | bytes 786440 | tf_op jit(solution)/shard_map/ppermute | solution.py:32
  5.2 1.6 %collective-permute-start.4 = (bf16[2,512,128]{2,1,0:T(8,128)(2,1)S(1)}, bf16[2,512,128]{2,1,0:T(8,128)(2,1)S(1)}, u32[]{:S(2)}, u32[]{:S(2)}) collective-permute-start(bf16[2,512,128]{2,1,0:T(8,128)(2,1)S(1)} %get-tuple-element.36), channel_id=1, source_target_pairs={{0,4},{1,5},{2,6},{3,7},{4,0},{5,1},{6,2},{7,3},{8,12},{9,13},{10,... | collective-permute-start | bytes 786440 | tf_op jit(solution)/shard_map/ppermute | solution.py:32
  6.8 2.6 %collective-permute-start.8 = (bf16[2,512,128]{2,1,0:T(8,128)(2,1)S(1)}, bf16[2,512,128]{2,1,0:T(8,128)(2,1)S(1)}, u32[]{:S(2)}, u32[]{:S(2)}) collective-permute-start(bf16[2,512,128]{2,1,0:T(8,128)(2,1)S(1)} %get-tuple-element.37), channel_id=1, source_target_pairs={{0,8},{1,9},{2,10},{3,11},{4,12},{5,13},{6,14},{7,15},{8,0},{9,1},... | collective-permute-start | bytes 786440 | tf_op jit(solution)/shard_map/ppermute | solution.py:32
  11.6 1.7 %collective-permute-start.1 = (bf16[1,8320]{1,0:T(2,128)(2,1)S(1)}, bf16[1,8320]{1,0:T(2,128)(2,1)S(1)}, u32[]{:S(2)}, u32[]{:S(2)}) collective-permute-start(bf16[1,8320]{1,0:T(2,128)(2,1)S(1)} %get-tuple-element.34.refs_0_), channel_id=1, source_target_pairs={{0,8},{1,9},{2,10},{3,11},{4,12},{5,13},{6,14},{7,15},{8,0},{9,1},... | collective-permute-start | bytes 49928 | tf_op jit(solution)/shard_map/ppermute | solution.py:32
  13.3 8.5 %collective-permute-done.2.refs_3_ = bf16[1,8320]{1,0:T(2,128)(2,1)S(1)} collective-permute-done((bf16[1,8320]{1,0:T(2,128)(2,1)S(1)}, bf16[1,8320]{1,0:T(2,128)(2,1)S(1)}, u32[]{:S(2)}, u32[]{:S(2)}) %collective-permute-start.2) | collective-permute-done | bytes 16672 | tf_op jit(solution)/shard_map/ppermute | solution.py:32
  21.8 2.1 %collective-permute-start = (bf16[1,8320]{1,0:T(2,128)(2,1)S(1)}, bf16[1,8320]{1,0:T(2,128)(2,1)S(1)}, u32[]{:S(2)}, u32[]{:S(2)}) collective-permute-start(bf16[1,8320]{1,0:T(2,128)(2,1)S(1)} %get-tuple-element.34.refs_0_), channel_id=1, source_target_pairs={{0,4},{1,5},{2,6},{3,7},{4,0},{5,1},{6,2},{7,3},{8,12},{9,13},{10,... | collective-permute-start | bytes 49928 | tf_op jit(solution)/shard_map/ppermute | solution.py:32
  23.9 2.5 %collective-permute-start.9 = (bf16[2,512,128]{2,1,0:T(8,128)(2,1)S(1)}, bf16[2,512,128]{2,1,0:T(8,128)(2,1)S(1)}, u32[]{:S(2)}, u32[]{:S(2)}) collective-permute-start(bf16[2,512,128]{2,1,0:T(8,128)(2,1)S(1)} %get-tuple-element.38), channel_id=1, source_target_pairs={{0,12},{1,13},{2,14},{3,15},{4,8},{5,9},{6,10},{7,11},{8,4},{9,5},... | collective-permute-start | bytes 786440 | tf_op jit(solution)/shard_map/ppermute | solution.py:32
  26.4 2.2 %collective-permute-done.refs_1_ = bf16[1,8320]{1,0:T(2,128)(2,1)S(1)} collective-permute-done((bf16[1,8320]{1,0:T(2,128)(2,1)S(1)}, bf16[1,8320]{1,0:T(2,128)(2,1)S(1)}, u32[]{:S(2)}, u32[]{:S(2)}) %collective-permute-start) | collective-permute-done | bytes 16672 | tf_op jit(solution)/shard_map/ppermute | solution.py:32
  29.4 1.6 %collective-permute-start.6 = (bf16[4,8320]{1,0:T(4,128)(2,1)S(1)}, bf16[4,8320]{1,0:T(4,128)(2,1)S(1)}, u32[]{:S(2)}, u32[]{:S(2)}) collective-permute-start(bf16[4,8320]{1,0:T(4,128)(2,1)S(1)} %join.1.refs_0_), channel_id=1, source_target_pairs={{0,2},{1,3},{2,0},{3,1},{4,6},{5,7},{6,4},{7,5},{8,10},{9,11},{10,... | collective-permute-start | bytes 199688 | tf_op jit(solution)/shard_map/ppermute | solution.py:32
  31.3 3.1 %collective-permute-done.9.refs_7_.refs_18_.refs_20_ = bf16[2,512,128]{2,1,0:T(8,128)(2,1)S(1)} collective-permute-done((bf16[2,512,128]{2,1,0:T(8,128)(2,1)S(1)}, bf16[2,512,128]{2,1,0:T(8,128)(2,1)S(1)}, u32[]{:S(2)}, u32[]{:S(2)}) %collective-permute-start.9) | collective-permute-done | bytes 262176 | tf_op jit(solution)/shard_map/ppermute | solution.py:32
  34.4 8.7 %collective-permute-start.17 = (bf16[2,512,128]{2,1,0:T(8,128)(2,1)S(1)}, bf16[2,512,128]{2,1,0:T(8,128)(2,1)S(1)}, u32[]{:S(2)}, u32[]{:S(2)}) collective-permute-start(bf16[2,512,128]{2,1,0:T(8,128)(2,1)S(1)} %get-tuple-element.46), channel_id=1, source_target_pairs={{0,6},{1,7},{2,4},{3,5},{4,2},{5,3},{6,0},{7,1},{8,14},{9,15},{10,... | collective-permute-start | bytes 786440 | tf_op jit(solution)/shard_map/ppermute | solution.py:32
  43.0 3.4 %collective-permute-done.13.refs_4_.refs_17_.refs_19_ = bf16[2,512,128]{2,1,0:T(8,128)(2,1)S(1)} collective-permute-done((bf16[2,512,128]{2,1,0:T(8,128)(2,1)S(1)}, bf16[2,512,128]{2,1,0:T(8,128)(2,1)S(1)}, u32[]{:S(2)}, u32[]{:S(2)}) %collective-permute-start.13) | collective-permute-done | bytes 262176 | tf_op jit(solution)/shard_map/ppermute | solution.py:32
  46.4 4.3 %collective-permute-start.20 = (bf16[2,512,128]{2,1,0:T(8,128)(2,1)S(1)}, bf16[2,512,128]{2,1,0:T(8,128)(2,1)S(1)}, u32[]{:S(2)}, u32[]{:S(2)}) collective-permute-start(bf16[2,512,128]{2,1,0:T(8,128)(2,1)S(1)} %get-tuple-element.53), channel_id=1, source_target_pairs={{0,14},{1,15},{2,12},{3,13},{4,10},{5,11},{6,8},{7,9},{8,6},{9,7},... | collective-permute-start | bytes 786440 | tf_op jit(solution)/shard_map/ppermute | solution.py:32
  51.3 8.2 %stash.1 = (bf16[8192,512]{1,0:T(8,128)(2,1)S(1)}, bf16[512,8192]{1,0:T(8,128)(2,1)S(1)}, bf16[8192,128]{1,0:T(8,128)(2,1)S(1)}, bf16[2,64,8192]{2,1,0:T(8,128)(...) custom-call(f32[8,128]{1,0:T(8,128)S(1)} %broadcast_in_dim.11.token_ref, bf16[8192,512]{1,0:T(8,128)(2,1)} %refs_0_.1, ...), custom_call_target="tpu_custom_call" | custom-call | flops 1048576 | bytes 23068672 | tf_op jit(solution)/shard_map/stash/pallas_call | solution.py:53
  60.9 3.0 %collective-permute-done.12.refs_3_ = bf16[16,64]{1,0:T(8,128)(2,1)S(1)} collective-permute-done((bf16[16,64]{1,0:T(8,128)(2,1)S(1)}, bf16[16,64]{1,0:T(8,128)(2,1)S(1)}, u32[]{:S(2)}, u32[]{:S(2)}) %collective-permute-start.12) | collective-permute-done | bytes 2080 | tf_op jit(solution)/shard_map/ppermute | solution.py:32
  64.3 3.2 %collective-permute-done.11.refs_2_ = bf16[16,64]{1,0:T(8,128)(2,1)S(1)} collective-permute-done((bf16[16,64]{1,0:T(8,128)(2,1)S(1)}, bf16[16,64]{1,0:T(8,128)(2,1)S(1)}, u32[]{:S(2)}, u32[]{:S(2)}) %collective-permute-start.11) | collective-permute-done | bytes 2080 | tf_op jit(solution)/shard_map/ppermute | solution.py:32
  69.4 2.4 %collective-permute-start.16 = (bf16[16,64]{1,0:T(8,128)(2,1)S(1)}, bf16[16,64]{1,0:T(8,128)(2,1)S(1)}, u32[]{:S(2)}, u32[]{:S(2)}) collective-permute-start(bf16[16,64]{1,0:T(8,128)(2,1)S(1)} %sum.2.refs_0_), channel_id=1, source_target_pairs={{0,12},{1,13},{2,14},{3,15},{4,8},{5,9},{6,10},{7,11},{8,4},{9,5},... | collective-permute-start | bytes 6152 | tf_op jit(solution)/shard_map/ppermute | solution.py:32
  71.8 3.2 %collective-permute-start.19 = (bf16[16,128]{1,0:T(8,128)(2,1)S(1)}, bf16[16,128]{1,0:T(8,128)(2,1)S(1)}, u32[]{:S(2)}, u32[]{:S(2)}) collective-permute-start(bf16[16,128]{1,0:T(8,128)(2,1)S(1)} %collective-permute-done.18.refs_10_), channel_id=1, source_target_pairs={{0,1},{1,0},{2,3},{3,2},{4,5},{5,4},{6,7},{7,6},{8,9},{9,8},{10,11... | collective-permute-start | bytes 12296 | tf_op jit(solution)/shard_map/ppermute | solution.py:32
  75.0 2.6 %collective-permute-start.14 = (bf16[16,64]{1,0:T(8,128)(2,1)S(1)}, bf16[16,64]{1,0:T(8,128)(2,1)S(1)}, u32[]{:S(2)}, u32[]{:S(2)}) collective-permute-start(bf16[16,64]{1,0:T(8,128)(2,1)S(1)} %sum.2.refs_0_), channel_id=1, source_target_pairs={{0,4},{1,5},{2,6},{3,7},{4,0},{5,1},{6,2},{7,3},{8,12},{9,13},{10,... | collective-permute-start | bytes 6152 | tf_op jit(solution)/shard_map/ppermute | solution.py:32
  77.6 1.9 %collective-permute-done.15.refs_2_ = bf16[16,64]{1,0:T(8,128)(2,1)S(1)} collective-permute-done((bf16[16,64]{1,0:T(8,128)(2,1)S(1)}, bf16[16,64]{1,0:T(8,128)(2,1)S(1)}, u32[]{:S(2)}, u32[]{:S(2)}) %collective-permute-start.15) | collective-permute-done | bytes 2080 | tf_op jit(solution)/shard_map/ppermute | solution.py:32
  82.5 2.9 %heads.2 = (f32[8,8192]{1,0:T(8,128)S(1)}, bf16[8,8192]{1,0:T(8,128)(2,1)S(1)}) custom-call(bf16[16,64]{1,0:T(8,128)(2,1)S(1)} %sum.2.refs_0_, bf16[16,64]{1,0:T(8,128)(2,1)S(1)} %collective-permute-done.14.refs_1_, bf16[16,64]{1,0:T(8,128)(2,1)S(1)} %collective-permute-done.15.refs_2_, bf16[16,64]{1,0:T(8,128)(2,1)S(1)} %collective-permute-done.16.refs_3_, ...), custom_call_target="tpu_custom_call" | custom-call | flops 134217728 | bytes 8388608 | tf_op jit(solution)/shard_map/heads/pallas_call | solution.py:53
  85.6 1.2 collective-permute-done.29.other_ref
  87.0 10.6 %all_to_all.15.parts_ref = bf16[8,8,1024]{2,1,0:T(8,128)(2,1)S(1)} all-to-all(bf16[8,8,1024]{2,1,0:T(8,128)(2,1)S(1)} %partial.2), channel_id=1, replica_groups={{0,2,4,6,8,10,12,14},{1,3,5,7,9,11,13,15},{16,18,20,22,24,26,28,30},{17..., dimensions={0} | all-to-all | bytes 262144 | tf_op jit(solution)/shard_map/all_to_all | solution.py:45
  97.9 9.8 %all_to_all.16.own_ref = bf16[8,8,1024]{2,1,0:T(8,128)(2,1)S(1)} all-to-all(bf16[8,8,1024]{2,1,0:T(8,128)(2,1)S(1)} %get-tuple-element.56), channel_id=1, replica_groups={{0,2,4,6,8,10,12,14},{1,3,5,7,9,11,13,15},{16,18,20,22,24,26,28,30},{17..., dimensions={0} | all-to-all | bytes 262144 | tf_op jit(solution)/shard_map/all_to_all | solution.py:45
  107.7 1.3 collective-permute-done.30.other_ref
  111.0 2.3 %collective-permute-start.33 = (bf16[16,64]{1,0:T(8,128)(2,1)S(1)}, bf16[16,64]{1,0:T(8,128)(2,1)S(1)}, u32[]{:S(2)}, u32[]{:S(2)}) collective-permute-start(bf16[16,64]{1,0:T(8,128)(2,1)S(1)} %get-tuple-element.57.refs_0_), channel_id=1, source_target_pairs={{0,3},{1,2},{2,1},{3,0},{4,7},{5,6},{6,5},{7,4},{8,11},{9,10},{10,... | collective-permute-start | bytes 6152 | tf_op jit(solution)/shard_map/ppermute | solution.py:32
  114.6 2.3 %collective-permute-done.32.refs_2_ = bf16[16,64]{1,0:T(8,128)(2,1)S(1)} collective-permute-done((bf16[16,64]{1,0:T(8,128)(2,1)S(1)}, bf16[16,64]{1,0:T(8,128)(2,1)S(1)}, u32[]{:S(2)}, u32[]{:S(2)}) %collective-permute-start.32) | collective-permute-done | bytes 2080 | tf_op jit(solution)/shard_map/ppermute | solution.py:32
  117.7 1.7 %collective-permute-start.35 = (bf16[16,64]{1,0:T(8,128)(2,1)S(1)}, bf16[16,64]{1,0:T(8,128)(2,1)S(1)}, u32[]{:S(2)}, u32[]{:S(2)}) collective-permute-start(bf16[16,64]{1,0:T(8,128)(2,1)S(1)} %sum.3.refs_0_), channel_id=1, source_target_pairs={{0,8},{1,9},{2,10},{3,11},{4,12},{5,13},{6,14},{7,15},{8,0},{9,1},... | collective-permute-start | bytes 6152 | tf_op jit(solution)/shard_map/ppermute | solution.py:32
  119.4 2.0 %collective-permute-start.34 = (bf16[16,64]{1,0:T(8,128)(2,1)S(1)}, bf16[16,64]{1,0:T(8,128)(2,1)S(1)}, u32[]{:S(2)}, u32[]{:S(2)}) collective-permute-start(bf16[16,64]{1,0:T(8,128)(2,1)S(1)} %sum.3.refs_0_), channel_id=1, source_target_pairs={{0,4},{1,5},{2,6},{3,7},{4,0},{5,1},{6,2},{7,3},{8,12},{9,13},{10,... | collective-permute-start | bytes 6152 | tf_op jit(solution)/shard_map/ppermute | solution.py:32
  123.0 2.9 %heads.3 = (f32[8,8192]{1,0:T(8,128)S(1)}, bf16[8,8192]{1,0:T(8,128)(2,1)S(1)}) custom-call(bf16[16,64]{1,0:T(8,128)(2,1)S(1)} %sum.3.refs_0_, bf16[16,64]{1,0:T(8,128)(2,1)S(1)} %collective-permute-done.34.refs_1_, bf16[16,64]{1,0:T(8,128)(2,1)S(1)} %collective-permute-done.35.refs_2_, bf16[16,64]{1,0:T(8,128)(2,1)S(1)} %collective-permute-done.36.refs_3_, ...), custom_call_target="tpu_custom_call" | custom-call | flops 134217728 | bytes 8388608 | tf_op jit(solution)/shard_map/heads/pallas_call | solution.py:53
  127.4 11.5 %all_to_all.17.parts_ref = bf16[8,8,1024]{2,1,0:T(8,128)(2,1)S(1)} all-to-all(bf16[8,8,1024]{2,1,0:T(8,128)(2,1)S(1)} %partial.3), channel_id=1, replica_groups={{0,2,4,6,8,10,12,14},{1,3,5,7,9,11,13,15},{16,18,20,22,24,26,28,30},{17..., dimensions={0} | all-to-all | bytes 262144 | tf_op jit(solution)/shard_map/all_to_all | solution.py:45
  (78 shorter events, 18.3 us)
Async XLA Ops:
  2.2 27.0 %collective-permute-start.3 = (bf16[2,512,128]{2,1,0:T(8,128)(2,1)S(1)}, bf16[2,512,128]{2,1,0:T(8,128)(2,1)S(1)}, u32[]{:S(2)}, u32[]{:S(2)}) collective-permute-start(bf16[2,512,128]{2,1,0:T(8,128)(2,1)S(1)} %get-tuple-element.35), channel_id=1, source_target_pairs={{0,2},{1,3},{2,0},{3,1},{4,6},{5,7},{6,4},{7,5},{8,10},{9,11},{10,... | collective-permute-start | bytes 786440 | tf_op jit(solution)/shard_map/ppermute | solution.py:32
  5.2 24.0 %collective-permute-start.4 = (bf16[2,512,128]{2,1,0:T(8,128)(2,1)S(1)}, bf16[2,512,128]{2,1,0:T(8,128)(2,1)S(1)}, u32[]{:S(2)}, u32[]{:S(2)}) collective-permute-start(bf16[2,512,128]{2,1,0:T(8,128)(2,1)S(1)} %get-tuple-element.36), channel_id=1, source_target_pairs={{0,4},{1,5},{2,6},{3,7},{4,0},{5,1},{6,2},{7,3},{8,12},{9,13},{10,... | collective-permute-start | bytes 786440 | tf_op jit(solution)/shard_map/ppermute | solution.py:32
  6.8 24.2 %collective-permute-start.8 = (bf16[2,512,128]{2,1,0:T(8,128)(2,1)S(1)}, bf16[2,512,128]{2,1,0:T(8,128)(2,1)S(1)}, u32[]{:S(2)}, u32[]{:S(2)}) collective-permute-start(bf16[2,512,128]{2,1,0:T(8,128)(2,1)S(1)} %get-tuple-element.37), channel_id=1, source_target_pairs={{0,8},{1,9},{2,10},{3,11},{4,12},{5,13},{6,14},{7,15},{8,0},{9,1},... | collective-permute-start | bytes 786440 | tf_op jit(solution)/shard_map/ppermute | solution.py:32
  11.4 10.5 %collective-permute-start.2 = (bf16[1,8320]{1,0:T(2,128)(2,1)S(1)}, bf16[1,8320]{1,0:T(2,128)(2,1)S(1)}, u32[]{:S(2)}, u32[]{:S(2)}) collective-permute-start(bf16[1,8320]{1,0:T(2,128)(2,1)S(1)} %get-tuple-element.34.refs_0_), channel_id=1, source_target_pairs={{0,12},{1,13},{2,14},{3,15},{4,8},{5,9},{6,10},{7,11},{8,4},{9,5},... | collective-permute-start | bytes 49928 | tf_op jit(solution)/shard_map/ppermute | solution.py:32
  11.6 12.3 %collective-permute-start.1 = (bf16[1,8320]{1,0:T(2,128)(2,1)S(1)}, bf16[1,8320]{1,0:T(2,128)(2,1)S(1)}, u32[]{:S(2)}, u32[]{:S(2)}) collective-permute-start(bf16[1,8320]{1,0:T(2,128)(2,1)S(1)} %get-tuple-element.34.refs_0_), channel_id=1, source_target_pairs={{0,8},{1,9},{2,10},{3,11},{4,12},{5,13},{6,14},{7,15},{8,0},{9,1},... | collective-permute-start | bytes 49928 | tf_op jit(solution)/shard_map/ppermute | solution.py:32
  21.8 6.7 %collective-permute-start = (bf16[1,8320]{1,0:T(2,128)(2,1)S(1)}, bf16[1,8320]{1,0:T(2,128)(2,1)S(1)}, u32[]{:S(2)}, u32[]{:S(2)}) collective-permute-start(bf16[1,8320]{1,0:T(2,128)(2,1)S(1)} %get-tuple-element.34.refs_0_), channel_id=1, source_target_pairs={{0,4},{1,5},{2,6},{3,7},{4,0},{5,1},{6,2},{7,3},{8,12},{9,13},{10,... | collective-permute-start | bytes 49928 | tf_op jit(solution)/shard_map/ppermute | solution.py:32
  23.9 10.4 %collective-permute-start.9 = (bf16[2,512,128]{2,1,0:T(8,128)(2,1)S(1)}, bf16[2,512,128]{2,1,0:T(8,128)(2,1)S(1)}, u32[]{:S(2)}, u32[]{:S(2)}) collective-permute-start(bf16[2,512,128]{2,1,0:T(8,128)(2,1)S(1)} %get-tuple-element.38), channel_id=1, source_target_pairs={{0,12},{1,13},{2,14},{3,15},{4,8},{5,9},{6,10},{7,11},{8,4},{9,5},... | collective-permute-start | bytes 786440 | tf_op jit(solution)/shard_map/ppermute | solution.py:32
  28.6 17.8 %collective-permute-start.13 = (bf16[2,512,128]{2,1,0:T(8,128)(2,1)S(1)}, bf16[2,512,128]{2,1,0:T(8,128)(2,1)S(1)}, u32[]{:S(2)}, u32[]{:S(2)}) collective-permute-start(bf16[2,512,128]{2,1,0:T(8,128)(2,1)S(1)} %get-tuple-element.43), channel_id=1, source_target_pairs={{0,10},{1,11},{2,8},{3,9},{4,14},{5,15},{6,12},{7,13},{8,2},{9,3},... | collective-permute-start | bytes 786440 | tf_op jit(solution)/shard_map/ppermute | solution.py:32
  29.4 21.4 %collective-permute-start.7 = (bf16[4,8320]{1,0:T(4,128)(2,1)S(1)}, bf16[4,8320]{1,0:T(4,128)(2,1)S(1)}, u32[]{:S(2)}, u32[]{:S(2)}) collective-permute-start(bf16[4,8320]{1,0:T(4,128)(2,1)S(1)} %join.1.refs_0_), channel_id=1, source_target_pairs={{0,3},{1,2},{2,1},{3,0},{4,7},{5,6},{6,5},{7,4},{8,11},{9,10},{10,... | collective-permute-start | bytes 199688 | tf_op jit(solution)/shard_map/ppermute | solution.py:32
  29.4 21.3 %collective-permute-start.6 = (bf16[4,8320]{1,0:T(4,128)(2,1)S(1)}, bf16[4,8320]{1,0:T(4,128)(2,1)S(1)}, u32[]{:S(2)}, u32[]{:S(2)}) collective-permute-start(bf16[4,8320]{1,0:T(4,128)(2,1)S(1)} %join.1.refs_0_), channel_id=1, source_target_pairs={{0,2},{1,3},{2,0},{3,1},{4,6},{5,7},{6,4},{7,5},{8,10},{9,11},{10,... | collective-permute-start | bytes 199688 | tf_op jit(solution)/shard_map/ppermute | solution.py:32
  31.0 20.3 %collective-permute-start.5 = (bf16[4,8320]{1,0:T(4,128)(2,1)S(1)}, bf16[4,8320]{1,0:T(4,128)(2,1)S(1)}, u32[]{:S(2)}, u32[]{:S(2)}) collective-permute-start(bf16[4,8320]{1,0:T(4,128)(2,1)S(1)} %join.1.refs_0_), channel_id=1, source_target_pairs={{0,1},{1,0},{2,3},{3,2},{4,5},{5,4},{6,7},{7,6},{8,9},{9,8},{10,11... | collective-permute-start | bytes 199688 | tf_op jit(solution)/shard_map/ppermute | solution.py:32
  34.4 26.5 %collective-permute-start.17 = (bf16[2,512,128]{2,1,0:T(8,128)(2,1)S(1)}, bf16[2,512,128]{2,1,0:T(8,128)(2,1)S(1)}, u32[]{:S(2)}, u32[]{:S(2)}) collective-permute-start(bf16[2,512,128]{2,1,0:T(8,128)(2,1)S(1)} %get-tuple-element.46), channel_id=1, source_target_pairs={{0,6},{1,7},{2,4},{3,5},{4,2},{5,3},{6,0},{7,1},{8,14},{9,15},{10,... | collective-permute-start | bytes 786440 | tf_op jit(solution)/shard_map/ppermute | solution.py:32
  46.4 23.0 %collective-permute-start.20 = (bf16[2,512,128]{2,1,0:T(8,128)(2,1)S(1)}, bf16[2,512,128]{2,1,0:T(8,128)(2,1)S(1)}, u32[]{:S(2)}, u32[]{:S(2)}) collective-permute-start(bf16[2,512,128]{2,1,0:T(8,128)(2,1)S(1)} %get-tuple-element.53), channel_id=1, source_target_pairs={{0,14},{1,15},{2,12},{3,13},{4,10},{5,11},{6,8},{7,9},{8,6},{9,7},... | collective-permute-start | bytes 786440 | tf_op jit(solution)/shard_map/ppermute | solution.py:32
  50.7 24.3 %collective-permute-start.21 = (bf16[2,512,128]{2,1,0:T(8,128)(2,1)S(1)}, bf16[2,512,128]{2,1,0:T(8,128)(2,1)S(1)}, u32[]{:S(2)}, u32[]{:S(2)}) collective-permute-start(bf16[2,512,128]{2,1,0:T(8,128)(2,1)S(1)} %get-tuple-element.52.refs_12_.refs_14_), channel_id=1, source_target_pairs={{0,1},{1,0},{2,3},{3,2},{4,5},{5,4},{6,7},{7,6},{8,9},{9,8},{10,11... | collective-permute-start | bytes 786440 | tf_op jit(solution)/shard_map/ppermute | solution.py:32
  50.7 29.4 %collective-permute-start.22 = (bf16[2,512,128]{2,1,0:T(8,128)(2,1)S(1)}, bf16[2,512,128]{2,1,0:T(8,128)(2,1)S(1)}, u32[]{:S(2)}, u32[]{:S(2)}) collective-permute-start(bf16[2,512,128]{2,1,0:T(8,128)(2,1)S(1)} %collective-permute-done.3.refs_4_.refs_13_.refs_15_), channel_id=1, source_target_pairs={{0,1},{1,0},{2,3},{3,2},{4,5},{5,4},{6,7},{7,6},{8,9},{9,8},{10,11... | collective-permute-start | bytes 786440 | tf_op jit(solution)/shard_map/ppermute | solution.py:32
  51.2 29.3 %collective-permute-start.23 = (bf16[2,512,128]{2,1,0:T(8,128)(2,1)S(1)}, bf16[2,512,128]{2,1,0:T(8,128)(2,1)S(1)}, u32[]{:S(2)}, u32[]{:S(2)}) collective-permute-start(bf16[2,512,128]{2,1,0:T(8,128)(2,1)S(1)} %collective-permute-done.4.refs_5_.refs_14_.refs_16_), channel_id=1, source_target_pairs={{0,1},{1,0},{2,3},{3,2},{4,5},{5,4},{6,7},{7,6},{8,9},{9,8},{10,11... | collective-permute-start | bytes 786440 | tf_op jit(solution)/shard_map/ppermute | solution.py:32
  60.8 3.1 %collective-permute-start.12 = (bf16[16,64]{1,0:T(8,128)(2,1)S(1)}, bf16[16,64]{1,0:T(8,128)(2,1)S(1)}, u32[]{:S(2)}, u32[]{:S(2)}) collective-permute-start(bf16[16,64]{1,0:T(8,128)(2,1)S(1)} %get-tuple-element.42.refs_0_), channel_id=1, source_target_pairs={{0,3},{1,2},{2,1},{3,0},{4,7},{5,6},{6,5},{7,4},{8,11},{9,10},{10,... | collective-permute-start | bytes 6152 | tf_op jit(solution)/shard_map/ppermute | solution.py:32
  63.9 3.6 %collective-permute-start.11 = (bf16[16,64]{1,0:T(8,128)(2,1)S(1)}, bf16[16,64]{1,0:T(8,128)(2,1)S(1)}, u32[]{:S(2)}, u32[]{:S(2)}) collective-permute-start(bf16[16,64]{1,0:T(8,128)(2,1)S(1)} %get-tuple-element.42.refs_0_), channel_id=1, source_target_pairs={{0,2},{1,3},{2,0},{3,1},{4,6},{5,7},{6,4},{7,5},{8,10},{9,11},{10,... | collective-permute-start | bytes 6152 | tf_op jit(solution)/shard_map/ppermute | solution.py:32
  68.7 3.1 %collective-permute-start.18 = (bf16[16,128]{1,0:T(8,128)(2,1)S(1)}, bf16[16,128]{1,0:T(8,128)(2,1)S(1)}, u32[]{:S(2)}, u32[]{:S(2)}) collective-permute-start(bf16[16,128]{1,0:T(8,128)(2,1)S(1)} %get-tuple-element.51), channel_id=1, source_target_pairs={{0,0},{1,2},{2,4},{3,6},{4,8},{5,10},{6,12},{7,14},{8,1},{9,3},{10... | collective-permute-start | bytes 12296 | tf_op jit(solution)/shard_map/ppermute | solution.py:613
  69.4 5.6 %collective-permute-start.16 = (bf16[16,64]{1,0:T(8,128)(2,1)S(1)}, bf16[16,64]{1,0:T(8,128)(2,1)S(1)}, u32[]{:S(2)}, u32[]{:S(2)}) collective-permute-start(bf16[16,64]{1,0:T(8,128)(2,1)S(1)} %sum.2.refs_0_), channel_id=1, source_target_pairs={{0,12},{1,13},{2,14},{3,15},{4,8},{5,9},{6,10},{7,11},{8,4},{9,5},... | collective-permute-start | bytes 6152 | tf_op jit(solution)/shard_map/ppermute | solution.py:32
  71.8 8.2 %collective-permute-start.19 = (bf16[16,128]{1,0:T(8,128)(2,1)S(1)}, bf16[16,128]{1,0:T(8,128)(2,1)S(1)}, u32[]{:S(2)}, u32[]{:S(2)}) collective-permute-start(bf16[16,128]{1,0:T(8,128)(2,1)S(1)} %collective-permute-done.18.refs_10_), channel_id=1, source_target_pairs={{0,1},{1,0},{2,3},{3,2},{4,5},{5,4},{6,7},{7,6},{8,9},{9,8},{10,11... | collective-permute-start | bytes 12296 | tf_op jit(solution)/shard_map/ppermute | solution.py:32
  75.0 4.5 %collective-permute-start.15 = (bf16[16,64]{1,0:T(8,128)(2,1)S(1)}, bf16[16,64]{1,0:T(8,128)(2,1)S(1)}, u32[]{:S(2)}, u32[]{:S(2)}) collective-permute-start(bf16[16,64]{1,0:T(8,128)(2,1)S(1)} %sum.2.refs_0_), channel_id=1, source_target_pairs={{0,8},{1,9},{2,10},{3,11},{4,12},{5,13},{6,14},{7,15},{8,0},{9,1},... | collective-permute-start | bytes 6152 | tf_op jit(solution)/shard_map/ppermute | solution.py:32
  75.0 4.5 %collective-permute-start.14 = (bf16[16,64]{1,0:T(8,128)(2,1)S(1)}, bf16[16,64]{1,0:T(8,128)(2,1)S(1)}, u32[]{:S(2)}, u32[]{:S(2)}) collective-permute-start(bf16[16,64]{1,0:T(8,128)(2,1)S(1)} %sum.2.refs_0_), channel_id=1, source_target_pairs={{0,4},{1,5},{2,6},{3,7},{4,0},{5,1},{6,2},{7,3},{8,12},{9,13},{10,... | collective-permute-start | bytes 6152 | tf_op jit(solution)/shard_map/ppermute | solution.py:32
  79.5 2.3 %collective-permute-start.25 = (bf16[2,512,128]{2,1,0:T(8,128)(2,1)S(1)}, bf16[2,512,128]{2,1,0:T(8,128)(2,1)S(1)}, u32[]{:S(2)}, u32[]{:S(2)}) collective-permute-start(bf16[2,512,128]{2,1,0:T(8,128)(2,1)S(1)} %collective-permute-done.8.refs_6_.refs_16_.refs_18_), channel_id=1, source_target_pairs={{0,1},{1,0},{2,3},{3,2},{4,5},{5,4},{6,7},{7,6},{8,9},{9,8},{10,11... | collective-permute-start | bytes 786440 | tf_op jit(solution)/shard_map/ppermute | solution.py:32
  79.5 2.3 %collective-permute-start.27 = (bf16[2,512,128]{2,1,0:T(8,128)(2,1)S(1)}, bf16[2,512,128]{2,1,0:T(8,128)(2,1)S(1)}, u32[]{:S(2)}, u32[]{:S(2)}) collective-permute-start(bf16[2,512,128]{2,1,0:T(8,128)(2,1)S(1)} %collective-permute-done.9.refs_7_.refs_18_.refs_20_), channel_id=1, source_target_pairs={{0,1},{1,0},{2,3},{3,2},{4,5},{5,4},{6,7},{7,6},{8,9},{9,8},{10,11... | collective-permute-start | bytes 786440 | tf_op jit(solution)/shard_map/ppermute | solution.py:32
  110.1 11.3 %collective-permute-start.37 = (bf16[16,128]{1,0:T(8,128)(2,1)S(1)}, bf16[16,128]{1,0:T(8,128)(2,1)S(1)}, u32[]{:S(2)}, u32[]{:S(2)}) collective-permute-start(bf16[16,128]{1,0:T(8,128)(2,1)S(1)} %get-tuple-element.59), channel_id=1, source_target_pairs={{0,0},{1,2},{2,4},{3,6},{4,8},{5,10},{6,12},{7,14},{8,1},{9,3},{10... | collective-permute-start | bytes 12296 | tf_op jit(solution)/shard_map/ppermute | solution.py:613
  111.0 3.7 %collective-permute-start.33 = (bf16[16,64]{1,0:T(8,128)(2,1)S(1)}, bf16[16,64]{1,0:T(8,128)(2,1)S(1)}, u32[]{:S(2)}, u32[]{:S(2)}) collective-permute-start(bf16[16,64]{1,0:T(8,128)(2,1)S(1)} %get-tuple-element.57.refs_0_), channel_id=1, source_target_pairs={{0,3},{1,2},{2,1},{3,0},{4,7},{5,6},{6,5},{7,4},{8,11},{9,10},{10,... | collective-permute-start | bytes 6152 | tf_op jit(solution)/shard_map/ppermute | solution.py:32
  113.3 3.6 %collective-permute-start.32 = (bf16[16,64]{1,0:T(8,128)(2,1)S(1)}, bf16[16,64]{1,0:T(8,128)(2,1)S(1)}, u32[]{:S(2)}, u32[]{:S(2)}) collective-permute-start(bf16[16,64]{1,0:T(8,128)(2,1)S(1)} %get-tuple-element.57.refs_0_), channel_id=1, source_target_pairs={{0,2},{1,3},{2,0},{3,1},{4,6},{5,7},{6,4},{7,5},{8,10},{9,11},{10,... | collective-permute-start | bytes 6152 | tf_op jit(solution)/shard_map/ppermute | solution.py:32
  114.3 2.7 %collective-permute-start.31 = (bf16[16,64]{1,0:T(8,128)(2,1)S(1)}, bf16[16,64]{1,0:T(8,128)(2,1)S(1)}, u32[]{:S(2)}, u32[]{:S(2)}) collective-permute-start(bf16[16,64]{1,0:T(8,128)(2,1)S(1)} %get-tuple-element.57.refs_0_), channel_id=1, source_target_pairs={{0,1},{1,0},{2,3},{3,2},{4,5},{5,4},{6,7},{7,6},{8,9},{9,8},{10,11... | collective-permute-start | bytes 6152 | tf_op jit(solution)/shard_map/ppermute | solution.py:32
  116.9 5.6 %collective-permute-start.36 = (bf16[16,64]{1,0:T(8,128)(2,1)S(1)}, bf16[16,64]{1,0:T(8,128)(2,1)S(1)}, u32[]{:S(2)}, u32[]{:S(2)}) collective-permute-start(bf16[16,64]{1,0:T(8,128)(2,1)S(1)} %sum.3.refs_0_), channel_id=1, source_target_pairs={{0,12},{1,13},{2,14},{3,15},{4,8},{5,9},{6,10},{7,11},{8,4},{9,5},... | collective-permute-start | bytes 6152 | tf_op jit(solution)/shard_map/ppermute | solution.py:32
  117.7 4.9 %collective-permute-start.35 = (bf16[16,64]{1,0:T(8,128)(2,1)S(1)}, bf16[16,64]{1,0:T(8,128)(2,1)S(1)}, u32[]{:S(2)}, u32[]{:S(2)}) collective-permute-start(bf16[16,64]{1,0:T(8,128)(2,1)S(1)} %sum.3.refs_0_), channel_id=1, source_target_pairs={{0,8},{1,9},{2,10},{3,11},{4,12},{5,13},{6,14},{7,15},{8,0},{9,1},... | collective-permute-start | bytes 6152 | tf_op jit(solution)/shard_map/ppermute | solution.py:32
  119.4 3.6 %collective-permute-start.34 = (bf16[16,64]{1,0:T(8,128)(2,1)S(1)}, bf16[16,64]{1,0:T(8,128)(2,1)S(1)}, u32[]{:S(2)}, u32[]{:S(2)}) collective-permute-start(bf16[16,64]{1,0:T(8,128)(2,1)S(1)} %sum.3.refs_0_), channel_id=1, source_target_pairs={{0,4},{1,5},{2,6},{3,7},{4,0},{5,1},{6,2},{7,3},{8,12},{9,13},{10,... | collective-permute-start | bytes 6152 | tf_op jit(solution)/shard_map/ppermute | solution.py:32
  (12 other events, 40.8 us)

commit v7 on v6

--- a/solution.py
+++ b/solution.py
@@ -135,31 +135,38 @@
     member_ref[...] = (storage - me * kept == iota((count, kept), 1)).astype(jnp.int32)
 
 
-def low_terms(held, member_ref, down_ref, fresh_w, rows_ref, low_ref, fresh_ref):
+def low_terms(held, member_ref, down_ref, fresh_w, rows_ref, *outs):
     rows = held[...].astype(jnp.bfloat16)
     rows_ref[...] = rows
-    low = jnp.zeros(low_ref.shape, jnp.float32)
+    rank = down_ref.shape[1]
+    low = jnp.zeros((rows.shape[0], rank), jnp.float32)
     for index in range(down_ref.shape[0]):
         part = dot(rows, down_ref[index], LAST)
         low = jnp.where(member_ref[:, index : index + 1] > 0, part, low)
-    low_ref[...] = low.astype(jnp.bfloat16)
-    fresh_ref[...] = dot(rows, fresh_w[...]).astype(jnp.bfloat16)
+    fresh = dot(rows, fresh_w[...]).astype(jnp.bfloat16)
+    if len(outs) == 2:
+        outs[0][...] = low.astype(jnp.bfloat16)
+        outs[1][...] = fresh
+    else:
+        outs[0][:, :rank] = low.astype(jnp.bfloat16)
+        outs[0][:, rank:LANES] = jnp.zeros((rows.shape[0], LANES - rank), jnp.bfloat16)
+        outs[0][:, LANES:] = fresh
 
 
 def low_first_kernel(near, far, *refs):
     pieces = refs[:near]
     me_ref, member_ref, down_ref, fresh_w = refs[near : near + 4]
-    rows_ref, low_ref, fresh_ref, held = refs[-4:]
+    outs, held = refs[near + 4 : -1], refs[-1]
     width = held.shape[1]
     for l in range(near):
         block = pieces[l][:, :width].astype(jnp.float32)
         for k in range(far):
             held[pl.ds(me_ref[0] ^ (k * near + l), 1), :] = block[k : k + 1]
-    low_terms(held, member_ref, down_ref, fresh_w, rows_ref, low_ref, fresh_ref)
+    low_terms(held, member_ref, down_ref, fresh_w, *outs)
 
 
 def low_later_kernel(own_ref, other_ref, me_ref, member_ref, down_ref, fresh_w, *refs):
-    rows_ref, low_ref, fresh_ref, held = refs
+    outs, held = refs[:-1], refs[-1]
     core = me_ref[0] % CORES
     for ref, flip in ((own_ref, 0), (other_ref, 1)):
         wide = ref.shape[2]
@@ -168,7 +175,7 @@
             row = pl.ds(k * CORES + (core ^ flip), 1)
             for i in range(FOLD):
                 held[row, i * wide : (i + 1) * wide] = block[i : i + 1]
-    low_terms(held, member_ref, down_ref, fresh_w, rows_ref, low_ref, fresh_ref)
+    low_terms(held, member_ref, down_ref, fresh_w, *outs)
 
 
 def join_kernel(amount, *refs):
@@ -183,18 +190,14 @@
     refs[-1][...] = total.astype(refs[-1].dtype)
 
 
-def project_kernel(rows_ref, query_w, *refs):
-    query_ref = refs[-1]
+def project_kernel(rows_ref, query_w, query_ref):
     query_ref[...] = dot(rows_ref[...], query_w[...])
 
 
 def up_terms(lows, query_ref, adapter_ref, up_ref):
     count, columns = query_ref.shape
     rank = lows[0].shape[1]
-    low = lows[0][...].astype(jnp.float32)
-    for ref in lows[1:]:
-        low = low + ref[...].astype(jnp.float32)
-    low = low.astype(jnp.bfloat16)
+    low = functools.reduce(lambda a, b: a + b, lows).astype(jnp.bfloat16)
     query = query_ref[...]
     table = up_ref.shape[0]
     some = min(table, 32)
@@ -211,6 +214,7 @@
 def up_kernel(parts, *refs):
     lows, (query_ref, fresh_ref, adapter_ref, up_ref, out_ref, held) = refs[:parts], refs[parts:]
     count, columns = query_ref.shape
+    lows = [ref[...].astype(jnp.float32) for ref in lows]
     query = up_terms(lows, query_ref, adapter_ref, up_ref)
     line = out_ref.shape[2]
     lines = columns // line
@@ -325,16 +329,13 @@
             out_ref[k] = out[k : k + 1].astype(jnp.bfloat16)
 
 
-def output_terms(held, each, core, weight_ref, own_ref, away_ref):
-    count = held.shape[0]
+def output_terms(rows, core, weight_ref, own_ref, away_ref):
+    count = rows.shape[0]
     chips = count // CORES
     slot = iota((count, count), 0)
     origin = (slot % chips) * CORES + (core ^ (slot // chips))
     order = (iota((count, count), 1) == origin).astype(jnp.bfloat16)
-    rows = jnp.concatenate(
-        [dot(order, held[:, c, :].astype(jnp.bfloat16)).astype(jnp.bfloat16) for c in range(each)],
-        axis=1,
-    )
+    rows = dot(order, rows).astype(jnp.bfloat16)
     width = weight_ref.shape[1]
     wide = width // 8
     for c in range(8):
@@ -348,51 +349,103 @@
     count, each, line = lines_ref.shape
     for k in range(count):
         held[k, :each, :] = lines_ref[k].astype(jnp.float32)
-    output_terms(held, each, me_ref[0] % CORES, weight_ref, own_ref, away_ref)
-
-
-def cut_kernel(me_ref, cache_hbm, *refs):
+    rows = [held[:, c, :].astype(jnp.bfloat16) for c in range(each)]
+    output_terms(jnp.concatenate(rows, axis=1), me_ref[0] % CORES, weight_ref, own_ref, away_ref)
+
+
+def cut_kernel(half, me_ref, cache_hbm, *refs):
     outs, sems = refs[:-1], refs[-1]
+    chip = me_ref[0] // CORES
     copies = []
     for d, out in enumerate(outs):
-        lanes = pl.ds(pl.multiple_of(((me_ref[0] // CORES) ^ d) * HD, HD), HD)
-        copies.append(pltpu.make_async_copy(cache_hbm.at[0, :, :, lanes], out, sems.at[d]))
+        for side in range(2):
+            lanes = pl.ds(pl.multiple_of((chip ^ d ^ (side * half)) * HD, HD), HD)
+            copies.append(
+                pltpu.make_async_copy(
+                    cache_hbm.at[0, :, :, lanes], out.at[side], sems.at[2 * d + side]
+                )
+            )
     for copy in copies:
         copy.start()
     for copy in copies:
         copy.wait()
 
 
-def heads_kernel(parts, steps, *refs):
-    lows, refs = refs[:parts], refs[parts:]
-    query_ref, adapter_ref, up_ref, lengths_ref, me_ref, weight_ref = refs[:6]
-    news, refs = refs[6 : 6 + 2 * steps], refs[6 + 2 * steps :]
-    own_ref, away_ref, held, mixed_ref, new_ref = refs[-5:]
-    blocks = refs[:-5]
-    count, columns = query_ref.shape
-    chips = count // CORES
+def gate_kernel(*_):
+    pass
+
+
+def merge_kernel(amount, *refs):
+    out_ref, sems = refs[-2:]
+    copies = [pltpu.make_async_copy(refs[i], out_ref.at[i], sems.at[i]) for i in range(amount)]
+    for copy in copies:
+        copy.start()
+    for copy in copies:
+        copy.wait()
+
+
+def pack_kernel(near, *refs):
+    out_ref = refs[-1]
+    total = refs[0][:, :LANES].astype(jnp.float32)
+    for ref in refs[1:near]:
+        total = total + ref[:, :LANES].astype(jnp.float32)
+    out_ref[:, :LANES] = total.astype(jnp.bfloat16)
+    for l in range(near):
+        out_ref[:, (l + 1) * LANES : (l + 2) * LANES] = refs[l][:, LANES:]
+
+
+def ask_kernel(parts, rank, *refs):
+    lows = [ref[:, :rank].astype(jnp.float32) for ref in refs[:parts]]
+    query_ref, adapter_ref, up_ref, me_ref, own_ref, away_ref = refs[parts:]
+    query = up_terms(lows, query_ref, adapter_ref, up_ref)
+    some = own_ref.shape[0]
+    side = me_ref[0] // some
+    low, high = query[:some], query[some:]
+    own_ref[...] = jnp.where(side == 0, low, high).astype(jnp.bfloat16)
+    away_ref[...] = jnp.where(side == 0, high, low).astype(jnp.bfloat16)
+
+
+def halves_kernel(parts, near, steps, *refs):
+    own_ref, other_ref, lengths_ref, me_ref = refs[:4]
+    lows, refs = refs[4 : 4 + parts], refs[4 + parts :]
+    if steps > 1:
+        past_ref, refs = refs[0], refs[1:]
+    mine_ref, away_ref, new_ref, held, all_ref, mixed_ref = refs[-6:]
+    blocks = refs[:-6]
+    blocks = [*blocks[:-2], *(blocks[-2].at[d] for d in range(len(blocks) - 3)), blocks[-1]]
+    some, columns = own_ref.shape
     each = columns // HD
-    lines = held.shape[1]
-    chip, core = me_ref[0] // CORES, me_ref[0] % CORES
-    query = up_terms(lows, query_ref, adapter_ref, up_ref).astype(jnp.bfloat16)
+    lines = held.shape[2]
+    me = me_ref[0]
+    chip, core = me // CORES, me % CORES
+    half = KVH // 2
+    side = me // some
     held[...] = jnp.zeros(held.shape, jnp.float32)
-    for c in range(each):
-        held[:, c, :] = query[:, c * HD : (c + 1) * HD].astype(jnp.float32)
-    for t in range(steps):
-        mine, other = news[2 * t][...].astype(jnp.float32), news[2 * t + 1][...].astype(jnp.float32)
-        new_ref[2 * t] = jnp.where(core == 0, mine, other)
-        new_ref[2 * t + 1] = jnp.where(core == 0, other, mine)
+    for s, ref in enumerate((own_ref, other_ref)):
+        query = ref[...].astype(jnp.float32)
+        for c in range(each):
+            held[s, :, c, :] = query[:, c * HD : (c + 1) * HD]
+    for k in range(parts):
+        for l in range(near):
+            all_ref[k * near + l] = lows[k][:, (l + 1) * LANES : (l + 2) * LANES].astype(jnp.float32)
+    for s in range(2):
+        for v in range(2):
+            holder = (chip ^ (s * half)) + v * KVH
+            new_ref[steps - 1, s, v] = all_ref[me ^ holder, pl.ds(pl.multiple_of(side * some, some), some), :]
+    for t in range(steps - 1):
+        new_ref[t] = past_ref[t]
     scale = 1.0 / math.sqrt(HD)
-    rows = [((chip ^ (b % chips)) * CORES) + (core ^ (b // chips)) for b in range(count)]
+    rows = [((chip ^ d) % half) * CORES + (core ^ l) for l in range(CORES) for d in range(half)]
     old, fresh = [], [[] for _ in range(steps)]
     for row, block in zip(rows, blocks):
-        query = held[row]
-        score = dot(query.astype(jnp.bfloat16), block[0], LAST) * scale
-        length = lengths_ref[pl.ds(row, 1), :]
-        old.append(jnp.where(iota(score.shape, 1) < length, score, -jnp.inf))
-        for t in range(steps):
-            keys = new_ref[2 * t, pl.ds(row, 1), :]
-            fresh[t].append(jnp.sum(query * keys, axis=1, keepdims=True) * scale)
+        length = lengths_ref[pl.ds(side * some + row, 1), :]
+        for s in range(2):
+            query = held[s, row]
+            score = dot(query.astype(jnp.bfloat16), block[s, 0], LAST) * scale
+            old.append(jnp.where(iota(score.shape, 1) < length, score, -jnp.inf))
+            for t in range(steps):
+                keys = new_ref[t, s, 0, pl.ds(row, 1), :]
+                fresh[t].append(jnp.sum(query * keys, axis=1, keepdims=True) * scale)
     old = jnp.concatenate(old, axis=0)
     fresh = [jnp.concatenate(scores, axis=0) for scores in fresh]
     peak = jnp.max(old, axis=1, keepdims=True)
@@ -406,12 +459,26 @@
     old = (old / total).astype(jnp.bfloat16).astype(jnp.float32)
     fresh = [(scores / total).astype(jnp.bfloat16).astype(jnp.float32) for scores in fresh]
     for b, (row, block) in enumerate(zip(rows, blocks)):
-        part = slice(b * lines, (b + 1) * lines)
-        mixed = dot(old[part].astype(jnp.bfloat16), block[1])
-        for t in range(steps):
-            mixed = mixed + fresh[t][part] * new_ref[2 * t + 1, pl.ds(row, 1), :]
-        mixed_ref[row] = mixed
-    output_terms(mixed_ref, each, core, weight_ref, own_ref, away_ref)
+        for s in range(2):
+            part = slice((2 * b + s) * lines, (2 * b + s + 1) * lines)
+            mixed = dot(old[part].astype(jnp.bfloat16), block[s, 1])
+            for t in range(steps):
+                mixed = mixed + fresh[t][part] * new_ref[t, s, 1, pl.ds(row, 1), :]
+            mixed_ref[s, row] = mixed
+    for c in range(each):
+        part = slice(c * HD, (c + 1) * HD)
+        mine_ref[:, part] = mixed_ref[0, :, c, :].astype(jnp.bfloat16)
+        away_ref[:, part] = mixed_ref[1, :, c, :].astype(jnp.bfloat16)
+
+
+def joined_kernel(mine_ref, other_ref, me_ref, weight_ref, own_ref, away_ref):
+    some = mine_ref.shape[0]
+    mine, other = mine_ref[...].astype(jnp.float32), other_ref[...].astype(jnp.float32)
+    side = me_ref[0] // some
+    rows = jnp.concatenate(
+        [jnp.where(side == 0, mine, other), jnp.where(side == 0, other, mine)], axis=0
+    ).astype(jnp.bfloat16)
+    output_terms(rows, me_ref[0] % CORES, weight_ref, own_ref, away_ref)
 
 
 def partial_kernel(own_ref, other_ref, out_ref):
@@ -468,6 +535,17 @@
     scale = attention_norm_scale[None]
     storage = adapter_storage_index[None]
 
+    def gate(arrays, *behind):
+        return pl.pallas_call(
+            gate_kernel,
+            out_shape=[shape(a.shape, a.dtype) for a in arrays],
+            in_specs=[pl.BlockSpec(memory_space=pl.ANY)] * (len(arrays) + len(behind)),
+            out_specs=[pl.BlockSpec(memory_space=pl.ANY)] * len(arrays),
+            input_output_aliases={i: i for i in range(len(arrays))},
+            compiler_params=pltpu.CompilerParams(vmem_limit_bytes=1 << 20),
+            name="gate",
+        )(*arrays, *behind)
+
     def stash(token, arrays, limit):
         outs = call(
             functools.partial(stash_kernel, len(arrays)),
@@ -479,10 +557,10 @@
         )(token, *arrays, specs=[vmem] + [pl.ANY] * len(arrays))
         return outs[:-1], outs[-1]
 
-    past, held_cache, moved = [], [], []
-
-    def after(*distances):
-        return [moved[d - 1] for d in distances] if moved else []
+    past, held_cache, blocks = [], [], []
+
+    def after(*numbers):
+        return [blocks[d] for d in numbers] if blocks else []
 
 
     def by_rows(step, lows, query, fresh):
@@ -532,25 +610,29 @@
     carried, length = call(
         first_kernel, [shape((1, width + LANES)), shape((8, LANES), jnp.int32)], "first"
     )(hidden, scale, row_adapter_index, cache_length_per_row, specs=[vmem, vmem, smem, smem])
-    news, blocks = [], []
-    by_heads = columns * CORES == GROUP * HD and count == CORES * KVH
+    fresh_past = []
+    by_halves = columns * CORES == GROUP * HD and count == CORES * KVH and fresh_columns == LANES
     for step in range(STEPS):
         first, last = step == 0, step == STEPS - 1
-        low_outs = [shape((count, width)), shape((count, rank)), shape((count, fresh_columns))]
+        low_outs = [shape((count, width))]
+        if by_halves:
+            low_outs = low_outs + [shape((count, LANES + fresh_columns))]
+        else:
+            low_outs = low_outs + [shape((count, rank)), shape((count, fresh_columns))]
         scratch = [pltpu.VMEM((count, width), jnp.float32)]
         if first:
             token = jnp.zeros((8, LANES), jnp.float32)
             arrays = [query_weight, output_weight, key_value_weight, down, adapter_up_weight]
-            if by_heads:
-                blocks = call(
-                    cut_kernel,
-                    [shape((2, key_value_cache.shape[2], HD))] * chips,
+            if by_halves:
+                half = chips // 2
+                cut = call(
+                    functools.partial(cut_kernel, half),
+                    [shape((2, 2, key_value_cache.shape[2], HD))] * half,
                     "cut",
-                    [pltpu.SemaphoreType.DMA((chips,))],
+                    [pltpu.SemaphoreType.DMA((2 * half,))],
+                    vmem=56 << 20,
                 )(me, key_value_cache, specs=[smem, pl.ANY])
-                moved.extend(shift(b, CORES * d, count) for d, b in enumerate(blocks) if d)
-                blocks = [blocks[0]] + moved
-                blocks = blocks + [shift(b, 1, count) for b in blocks]
+                blocks.extend([cut[0]] + [shift(cut[d], CORES * d, count) for d in range(1, half - 1)])
             else:
                 arrays.append(key_value_cache)
             outs, token = stash(token, arrays, 30 << 20)
@@ -559,7 +641,17 @@
             pieces = across(carried, far_steps, count)
             (carried,) = call(
                 functools.partial(join_kernel, far), [shape((far, width + LANES))], "join"
-            )(*pieces, *after(1, 2), specs=[vmem] * far + [pl.ANY] * len(after(1, 2)))
+            )(*pieces, token, *after(1, 2), specs=[vmem] * (far + 1) + [pl.ANY] * len(after(1, 2)))
+            if by_halves:
+                (still,) = gate([cut[half - 1]], carried)
+                blocks.append(shift(still, CORES * (half - 1), count))
+                (merged,) = call(
+                    functools.partial(merge_kernel, half - 1),
+                    [shape((half - 1, *cut[0].shape))],
+                    "merge",
+                    [pltpu.SemaphoreType.DMA((half - 1,))],
+                )(*blocks[:-1], carried, specs=[pl.ANY] * half)
+                blocks.append(shift(merged, 1, count))
             pieces = across(carried, near_steps, count)
             member, adapter, lengths = call(
                 functools.partial(member_kernel, near, far, width),
@@ -570,10 +662,10 @@
                 *pieces,
                 me,
                 storage,
-                *after(4, 6),
-                specs=[vmem] * near + [smem, vmem] + [pl.ANY] * len(after(4, 6)),
+                *after(4),
+                specs=[vmem] * near + [smem, vmem] + [pl.ANY] * len(after(4)),
             )
-            rows, low, fresh = call(
+            rows, low, *fresh = call(
                 functools.partial(low_first_kernel, near, far), low_outs, "low", scratch
             )(
                 *pieces,
@@ -585,7 +677,7 @@
             )
         else:
             own = chips_swap(carried, count)
-            rows, low, fresh = call(low_later_kernel, low_outs, "low", scratch)(
+            rows, low, *fresh = call(low_later_kernel, low_outs, "low", scratch)(
                 own,
                 shift(own, 1, count),
                 me,
@@ -594,46 +686,63 @@
                 fresh_w,
                 specs=[vmem, vmem, smem, vmem, vmem, vmem],
             )
-        behind = after(5) if first else []
-        (low,) = call(functools.partial(sum_kernel, near), [shape((count, rank))], "sum")(
-            *across(low, near_steps, count),
-            *behind,
-            specs=[vmem] * near + [pl.ANY] * len(behind),
+        if first and by_halves:
+            (still,) = gate([blocks[half - 1]], rows)
+            blocks[half - 1] = still
+            blocks.append(shift(still, 1, count))
+        lows = across(low, near_steps, count)
+        behind = after(3) if first else []
+        if by_halves:
+            body, dims = pack_kernel, (count, (near + 1) * LANES)
+        else:
+            body, dims = sum_kernel, (count, rank)
+        (low,) = call(functools.partial(body, near), [shape(dims)], "sum")(
+            *lows, *behind, specs=[vmem] * near + [pl.ANY] * len(behind)
         )
         lows = across(low, far_steps, count)
-        behind = after(3) if first else []
         (query,) = call(
             project_kernel,
             [shape((count, columns), jnp.float32)],
             "project",
             flops=2 * count * width * columns,
             moved=2 * width * columns,
-        )(rows, query_w, *behind, specs=[vmem] * 2 + [pl.ANY] * len(behind))
-        if by_heads:
-            fresh = lax.ppermute(fresh, AXIS, [(i, 2 * (i % KVH) + i // KVH) for i in range(count)])
-            news = news + [fresh, shift(fresh, 1, count)]
+        )(rows, query_w)
+        if by_halves:
+            some = count // 2
+            rows_half = shape((some, columns))
+            own, away = call(functools.partial(ask_kernel, far, rank), [rows_half] * 2, "ask")(
+                *lows, query, adapter, up_w, me, specs=[vmem] * (far + 3) + [smem]
+            )
+            new = (step + 1, 2, 2, some, HD)
+            mine, away, *fresh_past = call(
+                functools.partial(halves_kernel, far, near, step + 1),
+                [rows_half, rows_half, shape(new, jnp.float32)],
+                "attend",
+                [
+                    pltpu.VMEM((2, some, 8, HD), jnp.float32),
+                    pltpu.VMEM((count, count, LANES), jnp.float32),
+                    pltpu.VMEM((2, some, 8, HD), jnp.float32),
+                ],
+                moved=4 << 20,
+            )(
+                own,
+                shift(away, some, count),
+                lengths,
+                me,
+                *lows,
+                *fresh_past,
+                *blocks,
+                specs=[vmem] * 3 + [smem] + [vmem] * (far + len(fresh_past) + len(blocks)),
+            )
             own, away = call(
-                functools.partial(heads_kernel, far, step + 1),
+                joined_kernel,
                 [shape((chips, width), jnp.float32), shape((chips, width))],
-                "heads",
-                [pltpu.VMEM((count, 8, HD), jnp.float32)] * 2
-                + [pltpu.VMEM((2 * (step + 1), count, HD), jnp.float32)],
+                "output",
                 flops=2 * count * width * columns,
                 moved=2 * width * columns,
-            )(
-                *lows,
-                query,
-                adapter,
-                up_w,
-                lengths,
-                me,
-                output_w,
-                *news,
-                *blocks,
-                specs=[vmem] * (far + 4) + [smem] + [vmem] * (1 + len(news) + len(blocks)),
-            )
+            )(mine, shift(away, some, count), me, output_w, specs=[vmem, vmem, smem, vmem])
         else:
-            own, away = by_rows(step, lows, query, fresh)
+            own, away = by_rows(step, lows, query, fresh[0])
 
         (parts,) = call(partial_kernel, [shape((chips, FOLD, width // FOLD))], "partial")(
             own, shift(away, 1, count)

time: 140 us -> 131 us (0.936)
  starting transfers between devices: 49.1 us -> 24.8 us
  waiting for transfers between devices: 34 us -> 46.5 us
  Pallas kernels: 21.5 us -> 23.7 us
  blocking collectives: 31.8 us -> 33.4 us
    ppermute x38 -> x30, starting transfers between devices: 47.6 us -> 24.8 us  [shift(): return lax.ppermute(block, AXIS, [(i, i ^ distance) for i in range(count)])]
    ppermute x38 -> x30, waiting for transfers between devices: 34 us -> 46.5 us  [shift(): return lax.ppermute(block, AXIS, [(i, i ^ distance) for i in range(count)])]
    pallas_call x17 -> x22, Pallas kernels: 21.5 us -> 23.7 us  [run(): pl.pallas_call(body, out_shape=outs, in_specs=[pl.BlockSpec(memory_space=...]
    all_to_all x3, blocking collectives: 31.8 us -> 33.4 us  [chips_swap(): lax.all_to_all(blocks, AXIS, split_axis=0, concat_axis=0, axis_index_grou...]
    ppermute x2 -> x0, starting transfers between devices: 1.5 us -> none  [shards(): lax.ppermute(fresh, AXIS, [(i, 2 * (i % KVH) + i // KVH) for i in range(c...]
  transfers between devices with their start and end apart: 40 -> 30, of which waited for: 16 -> 15; matrix products, arithmetic and copies ran while one was open for 0% -> 0% of each run, Pallas kernels for 9% -> 9%
where the time goes in v7:
time: 131 us
  waiting for transfers between devices  46.5 us (35%)
  blocking collectives  33.4 us (25%)
  starting transfers between devices  24.8 us (19%)
  Pallas kernels  23.7 us (18%)
  between operations  1.47 us (1%)
    ppermute x30, waiting for transfers between devices, shift(): return lax.ppermute(block, AXIS, [(i, i ^ distance) for i in range(count)])  46.5 us
    all_to_all x3, blocking collectives, chips_swap(): lax.all_to_all(blocks, AXIS, split_axis=0, concat_axis=0, axis_index_grou...  33.4 us
    ppermute x30, starting transfers between devices, shift(): return lax.ppermute(block, AXIS, [(i, i ^ distance) for i in range(count)])  24.8 us
    pallas_call x22, Pallas kernels, run(): pl.pallas_call(body, out_shape=outs, in_specs=[pl.BlockSpec(memory_space=...  23.7 us
  transfers between devices with their start and end apart: 30, of which 15 were waited for; matrix products, arithmetic and copies ran while one was open for 0% of the time, Pallas kernels for 9%

profile of v7, /device:TPU:0, one launch (start us, length us, event | category | flops | bytes accessed | tf_op | source)
XLA Modules:
  0.0 130.5 jit_solution(3326593526990159683)
XLA Ops:
  0.0 3.0 %cut.1 = (bf16[2,2,512,128]{3,2,1,0:T(8,128)(2,1)}, bf16[2,2,512,128]{3,2,1,0:T(8,128)(2,1)}, bf16[2,2,512,128]{3,2,1,0:T(8,128)(2,1)}, bf16[2,2,512,128]{3,2,1,0:T(8,128)(2,1)}) custom-call(s32[1]{0:T(128)} %bitcast.1.me_ref.refs_4_.refs_7_.refs_3_, bf16[1,2,512,1024]{3,2,1,0:T(8,128)(2,1)} %cache_hbm.1), custom_call_target="tpu_custom_call" | custom-call | flops 1048576 | bytes 262144 | tf_op jit(solution)/shard_map/cut/pallas_call | solution.py:53
  3.0 3.0 %collective-permute-start.3 = (bf16[2,2,512,128]{3,2,1,0:T(8,128)(2,1)}, bf16[2,2,512,128]{3,2,1,0:T(8,128)(2,1)S(1)}, u32[]{:S(2)}, u32[]{:S(2)}) collective-permute-start(bf16[2,2,512,128]{3,2,1,0:T(8,128)(2,1)} %get-tuple-element.40), channel_id=1, source_target_pairs={{0,2},{1,3},{2,0},{3,1},{4,6},{5,7},{6,4},{7,5},{8,10},{9,11},{10,... | collective-permute-start | bytes 1572872 | tf_op jit(solution)/shard_map/ppermute | solution.py:32
  6.0 1.6 %collective-permute-start.4 = (bf16[2,2,512,128]{3,2,1,0:T(8,128)(2,1)}, bf16[2,2,512,128]{3,2,1,0:T(8,128)(2,1)S(1)}, u32[]{:S(2)}, u32[]{:S(2)}) collective-permute-start(bf16[2,2,512,128]{3,2,1,0:T(8,128)(2,1)} %get-tuple-element.41), channel_id=1, source_target_pairs={{0,4},{1,5},{2,6},{3,7},{4,0},{5,1},{6,2},{7,3},{8,12},{9,13},{10,... | collective-permute-start | bytes 1572872 | tf_op jit(solution)/shard_map/ppermute | solution.py:32
  10.0 2.6 %collective-permute-start.1 = (bf16[1,8320]{1,0:T(2,128)(2,1)S(1)}, bf16[1,8320]{1,0:T(2,128)(2,1)S(1)}, u32[]{:S(2)}, u32[]{:S(2)}) collective-permute-start(bf16[1,8320]{1,0:T(2,128)(2,1)S(1)} %get-tuple-element.38.refs_0_), channel_id=1, source_target_pairs={{0,8},{1,9},{2,10},{3,11},{4,12},{5,13},{6,14},{7,15},{8,0},{9,1},... | collective-permute-start | bytes 49928 | tf_op jit(solution)/shard_map/ppermute | solution.py:32
  12.6 1.3 %collective-permute-start.2 = (bf16[1,8320]{1,0:T(2,128)(2,1)S(1)}, bf16[1,8320]{1,0:T(2,128)(2,1)S(1)}, u32[]{:S(2)}, u32[]{:S(2)}) collective-permute-start(bf16[1,8320]{1,0:T(2,128)(2,1)S(1)} %get-tuple-element.38.refs_0_), channel_id=1, source_target_pairs={{0,12},{1,13},{2,14},{3,15},{4,8},{5,9},{6,10},{7,11},{8,4},{9,5},... | collective-permute-start | bytes 49928 | tf_op jit(solution)/shard_map/ppermute | solution.py:32
  13.9 7.7 %stash.1 = (bf16[8192,512]{1,0:T(8,128)(2,1)S(1)}, bf16[512,8192]{1,0:T(8,128)(2,1)S(1)}, bf16[8192,128]{1,0:T(8,128)(2,1)S(1)}, bf16[2,64,8192]{2,1,0:T(8,128)(...) custom-call(f32[8,128]{1,0:T(8,128)S(1)} %broadcast_in_dim.10.token_ref, bf16[8192,512]{1,0:T(8,128)(2,1)} %refs_0_.1, ...), custom_call_target="tpu_custom_call" | custom-call | flops 1048576 | bytes 23068672 | tf_op jit(solution)/shard_map/stash/pallas_call | solution.py:53
  21.6 2.2 %collective-permute-done.2.refs_3_ = bf16[1,8320]{1,0:T(2,128)(2,1)S(1)} collective-permute-done((bf16[1,8320]{1,0:T(2,128)(2,1)S(1)}, bf16[1,8320]{1,0:T(2,128)(2,1)S(1)}, u32[]{:S(2)}, u32[]{:S(2)}) %collective-permute-start.2) | collective-permute-done | bytes 16672 | tf_op jit(solution)/shard_map/ppermute | solution.py:32
  25.0 1.5 %collective-permute-start.6 = (bf16[4,8320]{1,0:T(4,128)(2,1)S(1)}, bf16[4,8320]{1,0:T(4,128)(2,1)S(1)}, u32[]{:S(2)}, u32[]{:S(2)}) collective-permute-start(bf16[4,8320]{1,0:T(4,128)(2,1)S(1)} %join.1.refs_3_.refs_0_.__1_), channel_id=1, source_target_pairs={{0,2},{1,3},{2,0},{3,1},{4,6},{5,7},{6,4},{7,5},{8,10},{9,11},{10,... | collective-permute-start | bytes 199688 | tf_op jit(solution)/shard_map/ppermute | solution.py:32
  27.6 13.3 %collective-permute-done.6.refs_2_ = bf16[4,8320]{1,0:T(4,128)(2,1)S(1)} collective-permute-done((bf16[4,8320]{1,0:T(4,128)(2,1)S(1)}, bf16[4,8320]{1,0:T(4,128)(2,1)S(1)}, u32[]{:S(2)}, u32[]{:S(2)}) %collective-permute-start.6) | collective-permute-done | bytes 66592 | tf_op jit(solution)/shard_map/ppermute | solution.py:32
  40.9 1.2 collective-permute-done.7.refs_3_
  45.8 1.6 %collective-permute-done.10.refs_2_ = bf16[16,256]{1,0:T(8,128)(2,1)S(1)} collective-permute-done((bf16[16,256]{1,0:T(8,128)(2,1)S(1)}, bf16[16,256]{1,0:T(8,128)(2,1)S(1)}, u32[]{:S(2)}, u32[]{:S(2)}) %collective-permute-start.10) | collective-permute-done | bytes 8224 | tf_op jit(solution)/shard_map/ppermute | solution.py:32
  47.7 1.8 %collective-permute-start.14 = (bf16[16,640]{1,0:T(8,128)(2,1)S(1)}, bf16[16,640]{1,0:T(8,128)(2,1)S(1)}, u32[]{:S(2)}, u32[]{:S(2)}) collective-permute-start(bf16[16,640]{1,0:T(8,128)(2,1)S(1)} %sum.2.refs_0_.refs_4_), channel_id=1, source_target_pairs={{0,8},{1,9},{2,10},{3,11},{4,12},{5,13},{6,14},{7,15},{8,0},{9,1},... | collective-permute-start | bytes 61448 | tf_op jit(solution)/shard_map/ppermute | solution.py:32
  49.5 2.3 %collective-permute-start.15 = (bf16[16,640]{1,0:T(8,128)(2,1)S(1)}, bf16[16,640]{1,0:T(8,128)(2,1)S(1)}, u32[]{:S(2)}, u32[]{:S(2)}) collective-permute-start(bf16[16,640]{1,0:T(8,128)(2,1)S(1)} %sum.2.refs_0_.refs_4_), channel_id=1, source_target_pairs={{0,12},{1,13},{2,14},{3,15},{4,8},{5,9},{6,10},{7,11},{8,4},{9,5},... | collective-permute-start | bytes 61448 | tf_op jit(solution)/shard_map/ppermute | solution.py:32
  53.0 2.1 %collective-permute-done.15.refs_3_.refs_7_ = bf16[16,640]{1,0:T(8,128)(2,1)S(1)} collective-permute-done((bf16[16,640]{1,0:T(8,128)(2,1)S(1)}, bf16[16,640]{1,0:T(8,128)(2,1)S(1)}, u32[]{:S(2)}, u32[]{:S(2)}) %collective-permute-start.15) | collective-permute-done | bytes 20512 | tf_op jit(solution)/shard_map/ppermute | solution.py:32
  55.6 4.6 %collective-permute-done.16.refs_1_ = bf16[8,512]{1,0:T(8,128)(2,1)S(1)} collective-permute-done((bf16[8,512]{1,0:T(8,128)(2,1)S(1)}, bf16[8,512]{1,0:T(8,128)(2,1)S(1)}, u32[]{:S(2)}, u32[]{:S(2)}) %collective-permute-start.16) | collective-permute-done | bytes 8224 | tf_op jit(solution)/shard_map/ppermute | solution.py:32
  61.4 4.5 %collective-permute-done.18.other_ref = bf16[8,512]{1,0:T(8,128)(2,1)S(1)} collective-permute-done((bf16[8,512]{1,0:T(8,128)(2,1)S(1)}, bf16[8,512]{1,0:T(8,128)(2,1)S(1)}, u32[]{:S(2)}, u32[]{:S(2)}) %collective-permute-start.18) | collective-permute-done | bytes 8224 | tf_op jit(solution)/shard_map/ppermute | solution.py:32
  66.0 1.3 output.2
  67.3 1.4 %collective-permute-done.19.other_ref = bf16[8,8192]{1,0:T(8,128)(2,1)S(1)} collective-permute-done((bf16[8,8192]{1,0:T(8,128)(2,1)S(1)}, bf16[8,8192]{1,0:T(8,128)(2,1)S(1)}, u32[]{:S(2)}, u32[]{:S(2)}) %collective-permute-start.19) | collective-permute-done | bytes 131104 | tf_op jit(solution)/shard_map/ppermute | solution.py:32
  68.8 11.5 %all_to_all.15.parts_ref = bf16[8,8,1024]{2,1,0:T(8,128)(2,1)S(1)} all-to-all(bf16[8,8,1024]{2,1,0:T(8,128)(2,1)S(1)} %partial.2), channel_id=1, replica_groups={{0,2,4,6,8,10,12,14},{1,3,5,7,9,11,13,15},{16,18,20,22,24,26,28,30},{17..., dimensions={0} | all-to-all | bytes 262144 | tf_op jit(solution)/shard_map/all_to_all | solution.py:45
  80.7 9.8 %all_to_all.16.own_ref = bf16[8,8,1024]{2,1,0:T(8,128)(2,1)S(1)} all-to-all(bf16[8,8,1024]{2,1,0:T(8,128)(2,1)S(1)} %get-tuple-element.60), channel_id=1, replica_groups={{0,2,4,6,8,10,12,14},{1,3,5,7,9,11,13,15},{16,18,20,22,24,26,28,30},{17..., dimensions={0} | all-to-all | bytes 262144 | tf_op jit(solution)/shard_map/all_to_all | solution.py:45
  90.5 1.3 %collective-permute-done.20.other_ref = bf16[8,8,1024]{2,1,0:T(8,128)(2,1)S(1)} collective-permute-done((bf16[8,8,1024]{2,1,0:T(8,128)(2,1)S(1)}, bf16[8,8,1024]{2,1,0:T(8,128)(2,1)S(1)}, u32[]{:S(2)}, u32[]{:S(2)}) %collective-permute-start.20) | collective-permute-done | bytes 131104 | tf_op jit(solution)/shard_map/ppermute | solution.py:32
  93.3 1.5 %collective-permute-start.23 = (bf16[16,256]{1,0:T(8,128)(2,1)S(1)}, bf16[16,256]{1,0:T(8,128)(2,1)S(1)}, u32[]{:S(2)}, u32[]{:S(2)}) collective-permute-start(bf16[16,256]{1,0:T(8,128)(2,1)S(1)} %get-tuple-element.61.refs_0_), channel_id=1, source_target_pairs={{0,3},{1,2},{2,1},{3,0},{4,7},{5,6},{6,5},{7,4},{8,11},{9,10},{10,... | collective-permute-start | bytes 24584 | tf_op jit(solution)/shard_map/ppermute | solution.py:32
  94.8 2.0 %collective-permute-done.22.refs_2_ = bf16[16,256]{1,0:T(8,128)(2,1)S(1)} collective-permute-done((bf16[16,256]{1,0:T(8,128)(2,1)S(1)}, bf16[16,256]{1,0:T(8,128)(2,1)S(1)}, u32[]{:S(2)}, u32[]{:S(2)}) %collective-permute-start.22) | collective-permute-done | bytes 8224 | tf_op jit(solution)/shard_map/ppermute | solution.py:32
  98.4 2.8 %collective-permute-start.26 = (bf16[16,640]{1,0:T(8,128)(2,1)S(1)}, bf16[16,640]{1,0:T(8,128)(2,1)S(1)}, u32[]{:S(2)}, u32[]{:S(2)}) collective-permute-start(bf16[16,640]{1,0:T(8,128)(2,1)S(1)} %sum.3.refs_0_.refs_4_), channel_id=1, source_target_pairs={{0,12},{1,13},{2,14},{3,15},{4,8},{5,9},{6,10},{7,11},{8,4},{9,5},... | collective-permute-start | bytes 61448 | tf_op jit(solution)/shard_map/ppermute | solution.py:32
  101.2 1.2 project.3.refs_4_
  102.4 1.6 %collective-permute-done.26.refs_3_.refs_7_ = bf16[16,640]{1,0:T(8,128)(2,1)S(1)} collective-permute-done((bf16[16,640]{1,0:T(8,128)(2,1)S(1)}, bf16[16,640]{1,0:T(8,128)(2,1)S(1)}, u32[]{:S(2)}, u32[]{:S(2)}) %collective-permute-start.26) | collective-permute-done | bytes 20512 | tf_op jit(solution)/shard_map/ppermute | solution.py:32
  104.7 4.3 %collective-permute-done.27.refs_1_ = bf16[8,512]{1,0:T(8,128)(2,1)S(1)} collective-permute-done((bf16[8,512]{1,0:T(8,128)(2,1)S(1)}, bf16[8,512]{1,0:T(8,128)(2,1)S(1)}, u32[]{:S(2)}, u32[]{:S(2)}) %collective-permute-start.27) | collective-permute-done | bytes 8224 | tf_op jit(solution)/shard_map/ppermute | solution.py:32
  109.0 1.4 %attend.3 = (bf16[8,512]{1,0:T(8,128)(2,1)S(1)}, bf16[8,512]{1,0:T(8,128)(2,1)S(1)}, f32[2,2,2,8,128]{4,3,2,1,0:T(8,128)}) custom-call(bf16[8,512]{1,0:T(8,128)(2,1)S(1)} %get-tuple-element.63.refs_0_, bf16[8,512]{1,0:T(8,128)(2,1)S(1)} %collective-permute-done.27.refs_1_, s32[16,1]{1,0:T(8,128)S(1)} %get-tuple-element.54.refs_2_, ...), custom_call_target="tpu_custom_call" | custom-call | flops 1048576 | bytes 4194304 | tf_op jit(solution)/shard_map/attend/pallas_call | solution.py:53
  110.6 4.3 %collective-permute-done.28.other_ref = bf16[8,512]{1,0:T(8,128)(2,1)S(1)} collective-permute-done((bf16[8,512]{1,0:T(8,128)(2,1)S(1)}, bf16[8,512]{1,0:T(8,128)(2,1)S(1)}, u32[]{:S(2)}, u32[]{:S(2)}) %collective-permute-start.28) | collective-permute-done | bytes 8224 | tf_op jit(solution)/shard_map/ppermute | solution.py:32
  114.9 1.3 output.3
  116.2 1.4 %collective-permute-done.29.other_ref = bf16[8,8192]{1,0:T(8,128)(2,1)S(1)} collective-permute-done((bf16[8,8192]{1,0:T(8,128)(2,1)S(1)}, bf16[8,8192]{1,0:T(8,128)(2,1)S(1)}, u32[]{:S(2)}, u32[]{:S(2)}) %collective-permute-start.29) | collective-permute-done | bytes 131104 | tf_op jit(solution)/shard_map/ppermute | solution.py:32
  117.7 12.1 %all_to_all.17.parts_ref = bf16[8,8,1024]{2,1,0:T(8,128)(2,1)S(1)} all-to-all(bf16[8,8,1024]{2,1,0:T(8,128)(2,1)S(1)} %partial.3), channel_id=1, replica_groups={{0,2,4,6,8,10,12,14},{1,3,5,7,9,11,13,15},{16,18,20,22,24,26,28,30},{17..., dimensions={0} | all-to-all | bytes 262144 | tf_op jit(solution)/shard_map/all_to_all | solution.py:45
  (67 shorter events, 15.9 us)
Async XLA Ops:
  3.0 20.8 %collective-permute-start.3 = (bf16[2,2,512,128]{3,2,1,0:T(8,128)(2,1)}, bf16[2,2,512,128]{3,2,1,0:T(8,128)(2,1)S(1)}, u32[]{:S(2)}, u32[]{:S(2)}) collective-permute-start(bf16[2,2,512,128]{3,2,1,0:T(8,128)(2,1)} %get-tuple-element.40), channel_id=1, source_target_pairs={{0,2},{1,3},{2,0},{3,1},{4,6},{5,7},{6,4},{7,5},{8,10},{9,11},{10,... | collective-permute-start | bytes 1572872 | tf_op jit(solution)/shard_map/ppermute | solution.py:32
  6.0 17.8 %collective-permute-start.4 = (bf16[2,2,512,128]{3,2,1,0:T(8,128)(2,1)}, bf16[2,2,512,128]{3,2,1,0:T(8,128)(2,1)S(1)}, u32[]{:S(2)}, u32[]{:S(2)}) collective-permute-start(bf16[2,2,512,128]{3,2,1,0:T(8,128)(2,1)} %get-tuple-element.41), channel_id=1, source_target_pairs={{0,4},{1,5},{2,6},{3,7},{4,0},{5,1},{6,2},{7,3},{8,12},{9,13},{10,... | collective-permute-start | bytes 1572872 | tf_op jit(solution)/shard_map/ppermute | solution.py:32
  9.5 12.1 %collective-permute-start = (bf16[1,8320]{1,0:T(2,128)(2,1)S(1)}, bf16[1,8320]{1,0:T(2,128)(2,1)S(1)}, u32[]{:S(2)}, u32[]{:S(2)}) collective-permute-start(bf16[1,8320]{1,0:T(2,128)(2,1)S(1)} %get-tuple-element.38.refs_0_), channel_id=1, source_target_pairs={{0,4},{1,5},{2,6},{3,7},{4,0},{5,1},{6,2},{7,3},{8,12},{9,13},{10,... | collective-permute-start | bytes 49928 | tf_op jit(solution)/shard_map/ppermute | solution.py:32
  10.0 11.6 %collective-permute-start.1 = (bf16[1,8320]{1,0:T(2,128)(2,1)S(1)}, bf16[1,8320]{1,0:T(2,128)(2,1)S(1)}, u32[]{:S(2)}, u32[]{:S(2)}) collective-permute-start(bf16[1,8320]{1,0:T(2,128)(2,1)S(1)} %get-tuple-element.38.refs_0_), channel_id=1, source_target_pairs={{0,8},{1,9},{2,10},{3,11},{4,12},{5,13},{6,14},{7,15},{8,0},{9,1},... | collective-permute-start | bytes 49928 | tf_op jit(solution)/shard_map/ppermute | solution.py:32
  12.6 11.2 %collective-permute-start.2 = (bf16[1,8320]{1,0:T(2,128)(2,1)S(1)}, bf16[1,8320]{1,0:T(2,128)(2,1)S(1)}, u32[]{:S(2)}, u32[]{:S(2)}) collective-permute-start(bf16[1,8320]{1,0:T(2,128)(2,1)S(1)} %get-tuple-element.38.refs_0_), channel_id=1, source_target_pairs={{0,12},{1,13},{2,14},{3,15},{4,8},{5,9},{6,10},{7,11},{8,4},{9,5},... | collective-permute-start | bytes 49928 | tf_op jit(solution)/shard_map/ppermute | solution.py:32
  13.9 10.0 %copy-start = (bf16[2,2,512,128]{3,2,1,0:T(8,128)(2,1)S(1)}, bf16[2,2,512,128]{3,2,1,0:T(8,128)(2,1)}, u32[]{:S(2)}) copy-start(bf16[2,2,512,128]{3,2,1,0:T(8,128)(2,1)} %get-tuple-element.42.refs_0_.refs_8_.refs_9_) | copy-start | bytes 1572868
  23.9 18.2 %copy-start.3 = (s32[32]{0:T(128)S(1)}, s32[32]{0:T(128)}, u32[]{:S(2)}) copy-start(s32[32]{0:T(128)} %param.19) | copy-start | bytes 388
  24.1 18.0 %collective-permute-start.8 = (bf16[3,2,2,512,128]{4,3,2,1,0:T(8,128)(2,1)S(1)}, bf16[3,2,2,512,128]{4,3,2,1,0:T(8,128)(2,1)S(1)}, u32[]{:S(2)}, u32[]{:S(2)}) collective-permute-start(bf16[3,2,2,512,128]{4,3,2,1,0:T(8,128)(2,1)S(1)} %merge.1), channel_id=1, source_target_pairs={{0,1},{1,0},{2,3},{3,2},{4,5},{5,4},{6,7},{7,6},{8,9},{9,8},{10,11... | collective-permute-start | bytes 4718600 | tf_op jit(solution)/shard_map/ppermute | solution.py:32
  24.8 18.6 %collective-permute-start.12 = (bf16[2,2,512,128]{3,2,1,0:T(8,128)(2,1)S(1)}, bf16[2,2,512,128]{3,2,1,0:T(8,128)(2,1)S(1)}, u32[]{:S(2)}, u32[]{:S(2)}) collective-permute-start(bf16[2,2,512,128]{3,2,1,0:T(8,128)(2,1)S(1)} %gate.2), channel_id=1, source_target_pairs={{0,6},{1,7},{2,4},{3,5},{4,2},{5,3},{6,0},{7,1},{8,14},{9,15},{10,... | collective-permute-start | bytes 1572872 | tf_op jit(solution)/shard_map/ppermute | solution.py:32
  25.0 2.6 %collective-permute-start.5 = (bf16[4,8320]{1,0:T(4,128)(2,1)S(1)}, bf16[4,8320]{1,0:T(4,128)(2,1)S(1)}, u32[]{:S(2)}, u32[]{:S(2)}) collective-permute-start(bf16[4,8320]{1,0:T(4,128)(2,1)S(1)} %join.1.refs_3_.refs_0_.__1_), channel_id=1, source_target_pairs={{0,1},{1,0},{2,3},{3,2},{4,5},{5,4},{6,7},{7,6},{8,9},{9,8},{10,11... | collective-permute-start | bytes 199688 | tf_op jit(solution)/shard_map/ppermute | solution.py:32
  25.0 15.9 %collective-permute-start.6 = (bf16[4,8320]{1,0:T(4,128)(2,1)S(1)}, bf16[4,8320]{1,0:T(4,128)(2,1)S(1)}, u32[]{:S(2)}, u32[]{:S(2)}) collective-permute-start(bf16[4,8320]{1,0:T(4,128)(2,1)S(1)} %join.1.refs_3_.refs_0_.__1_), channel_id=1, source_target_pairs={{0,2},{1,3},{2,0},{3,1},{4,6},{5,7},{6,4},{7,5},{8,10},{9,11},{10,... | collective-permute-start | bytes 199688 | tf_op jit(solution)/shard_map/ppermute | solution.py:32
  26.5 15.6 %collective-permute-start.7 = (bf16[4,8320]{1,0:T(4,128)(2,1)S(1)}, bf16[4,8320]{1,0:T(4,128)(2,1)S(1)}, u32[]{:S(2)}, u32[]{:S(2)}) collective-permute-start(bf16[4,8320]{1,0:T(4,128)(2,1)S(1)} %join.1.refs_3_.refs_0_.__1_), channel_id=1, source_target_pairs={{0,3},{1,2},{2,1},{3,0},{4,7},{5,6},{6,5},{7,4},{8,11},{9,10},{10,... | collective-permute-start | bytes 199688 | tf_op jit(solution)/shard_map/ppermute | solution.py:32
  43.4 16.8 %collective-permute-start.17 = (bf16[2,2,512,128]{3,2,1,0:T(8,128)(2,1)S(1)}, bf16[2,2,512,128]{3,2,1,0:T(8,128)(2,1)S(1)}, u32[]{:S(2)}, u32[]{:S(2)}) collective-permute-start(bf16[2,2,512,128]{3,2,1,0:T(8,128)(2,1)S(1)} %gate.3.refs_4_.refs_11_.refs_12_), channel_id=1, source_target_pairs={{0,1},{1,0},{2,3},{3,2},{4,5},{5,4},{6,7},{7,6},{8,9},{9,8},{10,11... | collective-permute-start | bytes 1572872 | tf_op jit(solution)/shard_map/ppermute | solution.py:32
  43.6 3.7 %collective-permute-start.10 = (bf16[16,256]{1,0:T(8,128)(2,1)S(1)}, bf16[16,256]{1,0:T(8,128)(2,1)S(1)}, u32[]{:S(2)}, u32[]{:S(2)}) collective-permute-start(bf16[16,256]{1,0:T(8,128)(2,1)S(1)} %get-tuple-element.46.refs_0_), channel_id=1, source_target_pairs={{0,2},{1,3},{2,0},{3,1},{4,6},{5,7},{6,4},{7,5},{8,10},{9,11},{10,... | collective-permute-start | bytes 24584 | tf_op jit(solution)/shard_map/ppermute | solution.py:32
  44.2 3.1 %collective-permute-start.11 = (bf16[16,256]{1,0:T(8,128)(2,1)S(1)}, bf16[16,256]{1,0:T(8,128)(2,1)S(1)}, u32[]{:S(2)}, u32[]{:S(2)}) collective-permute-start(bf16[16,256]{1,0:T(8,128)(2,1)S(1)} %get-tuple-element.46.refs_0_), channel_id=1, source_target_pairs={{0,3},{1,2},{2,1},{3,0},{4,7},{5,6},{6,5},{7,4},{8,11},{9,10},{10,... | collective-permute-start | bytes 24584 | tf_op jit(solution)/shard_map/ppermute | solution.py:32
  45.3 2.0 %collective-permute-start.9 = (bf16[16,256]{1,0:T(8,128)(2,1)S(1)}, bf16[16,256]{1,0:T(8,128)(2,1)S(1)}, u32[]{:S(2)}, u32[]{:S(2)}) collective-permute-start(bf16[16,256]{1,0:T(8,128)(2,1)S(1)} %get-tuple-element.46.refs_0_), channel_id=1, source_target_pairs={{0,1},{1,0},{2,3},{3,2},{4,5},{5,4},{6,7},{7,6},{8,9},{9,8},{10,11... | collective-permute-start | bytes 24584 | tf_op jit(solution)/shard_map/ppermute | solution.py:32
  47.4 5.6 %collective-permute-start.13 = (bf16[16,640]{1,0:T(8,128)(2,1)S(1)}, bf16[16,640]{1,0:T(8,128)(2,1)S(1)}, u32[]{:S(2)}, u32[]{:S(2)}) collective-permute-start(bf16[16,640]{1,0:T(8,128)(2,1)S(1)} %sum.2.refs_0_.refs_4_), channel_id=1, source_target_pairs={{0,4},{1,5},{2,6},{3,7},{4,0},{5,1},{6,2},{7,3},{8,12},{9,13},{10,... | collective-permute-start | bytes 61448 | tf_op jit(solution)/shard_map/ppermute | solution.py:32
  47.7 5.3 %collective-permute-start.14 = (bf16[16,640]{1,0:T(8,128)(2,1)S(1)}, bf16[16,640]{1,0:T(8,128)(2,1)S(1)}, u32[]{:S(2)}, u32[]{:S(2)}) collective-permute-start(bf16[16,640]{1,0:T(8,128)(2,1)S(1)} %sum.2.refs_0_.refs_4_), channel_id=1, source_target_pairs={{0,8},{1,9},{2,10},{3,11},{4,12},{5,13},{6,14},{7,15},{8,0},{9,1},... | collective-permute-start | bytes 61448 | tf_op jit(solution)/shard_map/ppermute | solution.py:32
  49.5 5.6 %collective-permute-start.15 = (bf16[16,640]{1,0:T(8,128)(2,1)S(1)}, bf16[16,640]{1,0:T(8,128)(2,1)S(1)}, u32[]{:S(2)}, u32[]{:S(2)}) collective-permute-start(bf16[16,640]{1,0:T(8,128)(2,1)S(1)} %sum.2.refs_0_.refs_4_), channel_id=1, source_target_pairs={{0,12},{1,13},{2,14},{3,15},{4,8},{5,9},{6,10},{7,11},{8,4},{9,5},... | collective-permute-start | bytes 61448 | tf_op jit(solution)/shard_map/ppermute | solution.py:32
  55.6 4.6 %collective-permute-start.16 = (bf16[8,512]{1,0:T(8,128)(2,1)S(1)}, bf16[8,512]{1,0:T(8,128)(2,1)S(1)}, u32[]{:S(2)}, u32[]{:S(2)}) collective-permute-start(bf16[8,512]{1,0:T(8,128)(2,1)S(1)} %get-tuple-element.53), channel_id=1, source_target_pairs={{0,8},{1,9},{2,10},{3,11},{4,12},{5,13},{6,14},{7,15},{8,0},{9,1},... | collective-permute-start | bytes 24584 | tf_op jit(solution)/shard_map/ppermute | solution.py:32
  61.4 4.6 %collective-permute-start.18 = (bf16[8,512]{1,0:T(8,128)(2,1)S(1)}, bf16[8,512]{1,0:T(8,128)(2,1)S(1)}, u32[]{:S(2)}, u32[]{:S(2)}) collective-permute-start(bf16[8,512]{1,0:T(8,128)(2,1)S(1)} %get-tuple-element.56), channel_id=1, source_target_pairs={{0,8},{1,9},{2,10},{3,11},{4,12},{5,13},{6,14},{7,15},{8,0},{9,1},... | collective-permute-start | bytes 24584 | tf_op jit(solution)/shard_map/ppermute | solution.py:32
  67.3 1.4 %collective-permute-start.19 = (bf16[8,8192]{1,0:T(8,128)(2,1)S(1)}, bf16[8,8192]{1,0:T(8,128)(2,1)S(1)}, u32[]{:S(2)}, u32[]{:S(2)}) collective-permute-start(bf16[8,8192]{1,0:T(8,128)(2,1)S(1)} %get-tuple-element.59), channel_id=1, source_target_pairs={{0,1},{1,0},{2,3},{3,2},{4,5},{5,4},{6,7},{7,6},{8,9},{9,8},{10,11... | collective-permute-start | bytes 393224 | tf_op jit(solution)/shard_map/ppermute | solution.py:32
  90.5 1.3 %collective-permute-start.20 = (bf16[8,8,1024]{2,1,0:T(8,128)(2,1)S(1)}, bf16[8,8,1024]{2,1,0:T(8,128)(2,1)S(1)}, u32[]{:S(2)}, u32[]{:S(2)}) collective-permute-start(bf16[8,8,1024]{2,1,0:T(8,128)(2,1)S(1)} %all_to_all.16.own_ref), channel_id=1, source_target_pairs={{0,1},{1,0},{2,3},{3,2},{4,5},{5,4},{6,7},{7,6},{8,9},{9,8},{10,11... | collective-permute-start | bytes 393224 | tf_op jit(solution)/shard_map/ppermute | solution.py:32
  92.9 1.9 %collective-permute-start.21 = (bf16[16,256]{1,0:T(8,128)(2,1)S(1)}, bf16[16,256]{1,0:T(8,128)(2,1)S(1)}, u32[]{:S(2)}, u32[]{:S(2)}) collective-permute-start(bf16[16,256]{1,0:T(8,128)(2,1)S(1)} %get-tuple-element.61.refs_0_), channel_id=1, source_target_pairs={{0,1},{1,0},{2,3},{3,2},{4,5},{5,4},{6,7},{7,6},{8,9},{9,8},{10,11... | collective-permute-start | bytes 24584 | tf_op jit(solution)/shard_map/ppermute | solution.py:32
  93.1 3.7 %collective-permute-start.22 = (bf16[16,256]{1,0:T(8,128)(2,1)S(1)}, bf16[16,256]{1,0:T(8,128)(2,1)S(1)}, u32[]{:S(2)}, u32[]{:S(2)}) collective-permute-start(bf16[16,256]{1,0:T(8,128)(2,1)S(1)} %get-tuple-element.61.refs_0_), channel_id=1, source_target_pairs={{0,2},{1,3},{2,0},{3,1},{4,6},{5,7},{6,4},{7,5},{8,10},{9,11},{10,... | collective-permute-start | bytes 24584 | tf_op jit(solution)/shard_map/ppermute | solution.py:32
  93.3 3.4 %collective-permute-start.23 = (bf16[16,256]{1,0:T(8,128)(2,1)S(1)}, bf16[16,256]{1,0:T(8,128)(2,1)S(1)}, u32[]{:S(2)}, u32[]{:S(2)}) collective-permute-start(bf16[16,256]{1,0:T(8,128)(2,1)S(1)} %get-tuple-element.61.refs_0_), channel_id=1, source_target_pairs={{0,3},{1,2},{2,1},{3,0},{4,7},{5,6},{6,5},{7,4},{8,11},{9,10},{10,... | collective-permute-start | bytes 24584 | tf_op jit(solution)/shard_map/ppermute | solution.py:32
  96.8 5.6 %collective-permute-start.24 = (bf16[16,640]{1,0:T(8,128)(2,1)S(1)}, bf16[16,640]{1,0:T(8,128)(2,1)S(1)}, u32[]{:S(2)}, u32[]{:S(2)}) collective-permute-start(bf16[16,640]{1,0:T(8,128)(2,1)S(1)} %sum.3.refs_0_.refs_4_), channel_id=1, source_target_pairs={{0,4},{1,5},{2,6},{3,7},{4,0},{5,1},{6,2},{7,3},{8,12},{9,13},{10,... | collective-permute-start | bytes 61448 | tf_op jit(solution)/shard_map/ppermute | solution.py:32
  97.5 4.9 %collective-permute-start.25 = (bf16[16,640]{1,0:T(8,128)(2,1)S(1)}, bf16[16,640]{1,0:T(8,128)(2,1)S(1)}, u32[]{:S(2)}, u32[]{:S(2)}) collective-permute-start(bf16[16,640]{1,0:T(8,128)(2,1)S(1)} %sum.3.refs_0_.refs_4_), channel_id=1, source_target_pairs={{0,8},{1,9},{2,10},{3,11},{4,12},{5,13},{6,14},{7,15},{8,0},{9,1},... | collective-permute-start | bytes 61448 | tf_op jit(solution)/shard_map/ppermute | solution.py:32
  98.4 5.6 %collective-permute-start.26 = (bf16[16,640]{1,0:T(8,128)(2,1)S(1)}, bf16[16,640]{1,0:T(8,128)(2,1)S(1)}, u32[]{:S(2)}, u32[]{:S(2)}) collective-permute-start(bf16[16,640]{1,0:T(8,128)(2,1)S(1)} %sum.3.refs_0_.refs_4_), channel_id=1, source_target_pairs={{0,12},{1,13},{2,14},{3,15},{4,8},{5,9},{6,10},{7,11},{8,4},{9,5},... | collective-permute-start | bytes 61448 | tf_op jit(solution)/shard_map/ppermute | solution.py:32
  104.5 4.6 %collective-permute-start.27 = (bf16[8,512]{1,0:T(8,128)(2,1)S(1)}, bf16[8,512]{1,0:T(8,128)(2,1)S(1)}, u32[]{:S(2)}, u32[]{:S(2)}) collective-permute-start(bf16[8,512]{1,0:T(8,128)(2,1)S(1)} %get-tuple-element.64), channel_id=1, source_target_pairs={{0,8},{1,9},{2,10},{3,11},{4,12},{5,13},{6,14},{7,15},{8,0},{9,1},... | collective-permute-start | bytes 24584 | tf_op jit(solution)/shard_map/ppermute | solution.py:32
  110.4 4.5 %collective-permute-start.28 = (bf16[8,512]{1,0:T(8,128)(2,1)S(1)}, bf16[8,512]{1,0:T(8,128)(2,1)S(1)}, u32[]{:S(2)}, u32[]{:S(2)}) collective-permute-start(bf16[8,512]{1,0:T(8,128)(2,1)S(1)} %get-tuple-element.67), channel_id=1, source_target_pairs={{0,8},{1,9},{2,10},{3,11},{4,12},{5,13},{6,14},{7,15},{8,0},{9,1},... | collective-permute-start | bytes 24584 | tf_op jit(solution)/shard_map/ppermute | solution.py:32
  116.2 1.4 %collective-permute-start.29 = (bf16[8,8192]{1,0:T(8,128)(2,1)S(1)}, bf16[8,8192]{1,0:T(8,128)(2,1)S(1)}, u32[]{:S(2)}, u32[]{:S(2)}) collective-permute-start(bf16[8,8192]{1,0:T(8,128)(2,1)S(1)} %get-tuple-element.69), channel_id=1, source_target_pairs={{0,1},{1,0},{2,3},{3,2},{4,5},{5,4},{6,7},{7,6},{8,9},{9,8},{10,11... | collective-permute-start | bytes 393224 | tf_op jit(solution)/shard_map/ppermute | solution.py:32
  (3 other events, 17.6 us)

commit v8 on v7

--- a/solution.py
+++ b/solution.py
@@ -371,8 +371,8 @@
         copy.wait()
 
 
-def gate_kernel(*_):
-    pass
+def late_kernel(row_ref, _, out_ref):
+    out_ref[...] = row_ref[...]
 
 
 def merge_kernel(amount, *refs):
@@ -412,7 +412,7 @@
         past_ref, refs = refs[0], refs[1:]
     mine_ref, away_ref, new_ref, held, all_ref, mixed_ref = refs[-6:]
     blocks = refs[:-6]
-    blocks = [*blocks[:-2], *(blocks[-2].at[d] for d in range(len(blocks) - 3)), blocks[-1]]
+    blocks = [*blocks[:-1], *(blocks[-1].at[d] for d in range(len(blocks) - 1))]
     some, columns = own_ref.shape
     each = columns // HD
     lines = held.shape[2]
@@ -535,17 +535,6 @@
     scale = attention_norm_scale[None]
     storage = adapter_storage_index[None]
 
-    def gate(arrays, *behind):
-        return pl.pallas_call(
-            gate_kernel,
-            out_shape=[shape(a.shape, a.dtype) for a in arrays],
-            in_specs=[pl.BlockSpec(memory_space=pl.ANY)] * (len(arrays) + len(behind)),
-            out_specs=[pl.BlockSpec(memory_space=pl.ANY)] * len(arrays),
-            input_output_aliases={i: i for i in range(len(arrays))},
-            compiler_params=pltpu.CompilerParams(vmem_limit_bytes=1 << 20),
-            name="gate",
-        )(*arrays, *behind)
-
     def stash(token, arrays, limit):
         outs = call(
             functools.partial(stash_kernel, len(arrays)),
@@ -627,31 +616,25 @@
                 half = chips // 2
                 cut = call(
                     functools.partial(cut_kernel, half),
-                    [shape((2, 2, key_value_cache.shape[2], HD))] * half,
+                    [pltpu.VMEM((2, 2, key_value_cache.shape[2], HD), jnp.bfloat16)] * half,
                     "cut",
                     [pltpu.SemaphoreType.DMA((2 * half,))],
-                    vmem=56 << 20,
+                    vmem=58 << 20,
                 )(me, key_value_cache, specs=[smem, pl.ANY])
-                blocks.extend([cut[0]] + [shift(cut[d], CORES * d, count) for d in range(1, half - 1)])
+                blocks.extend([cut[0]] + [shift(cut[d], CORES * d, count) for d in range(1, half)])
             else:
                 arrays.append(key_value_cache)
             outs, token = stash(token, arrays, 30 << 20)
             query_w, output_w, fresh_w, down_w, up_w = outs[:5]
             held_cache.append(outs[-1])
-            pieces = across(carried, far_steps, count)
+            late = carried
+            if by_halves:
+                (late,) = call(late_kernel, [shape(carried.shape)], "late")(carried, token)
+            pieces = [carried, shift(late, near, count)]
+            pieces = pieces + [shift(carried, d, count) for d in far_steps[1:]]
             (carried,) = call(
                 functools.partial(join_kernel, far), [shape((far, width + LANES))], "join"
-            )(*pieces, token, *after(1, 2), specs=[vmem] * (far + 1) + [pl.ANY] * len(after(1, 2)))
-            if by_halves:
-                (still,) = gate([cut[half - 1]], carried)
-                blocks.append(shift(still, CORES * (half - 1), count))
-                (merged,) = call(
-                    functools.partial(merge_kernel, half - 1),
-                    [shape((half - 1, *cut[0].shape))],
-                    "merge",
-                    [pltpu.SemaphoreType.DMA((half - 1,))],
-                )(*blocks[:-1], carried, specs=[pl.ANY] * half)
-                blocks.append(shift(merged, 1, count))
+            )(*pieces, token, *after(1, 2, 3), specs=[vmem] * (far + 1) + [pl.ANY] * len(after(1, 2, 3)))
             pieces = across(carried, near_steps, count)
             member, adapter, lengths = call(
                 functools.partial(member_kernel, near, far, width),
@@ -662,9 +645,17 @@
                 *pieces,
                 me,
                 storage,
-                *after(4),
-                specs=[vmem] * near + [smem, vmem] + [pl.ANY] * len(after(4)),
+                *after(),
+                specs=[vmem] * near + [smem, vmem] + [pl.ANY] * len(after()),
             )
+            if by_halves:
+                (merged,) = call(
+                    functools.partial(merge_kernel, half),
+                    [shape((half, *cut[0].shape))],
+                    "merge",
+                    [pltpu.SemaphoreType.DMA((half,))],
+                )(*blocks, member, specs=[pl.ANY] * (half + 1))
+                blocks.append(shift(merged, 1, count))
             rows, low, *fresh = call(
                 functools.partial(low_first_kernel, near, far), low_outs, "low", scratch
             )(
@@ -686,12 +677,8 @@
                 fresh_w,
                 specs=[vmem, vmem, smem, vmem, vmem, vmem],
             )
-        if first and by_halves:
-            (still,) = gate([blocks[half - 1]], rows)
-            blocks[half - 1] = still
-            blocks.append(shift(still, 1, count))
         lows = across(low, near_steps, count)
-        behind = after(3) if first else []
+        behind = after() if first else []
         if by_halves:
             body, dims = pack_kernel, (count, (near + 1) * LANES)
         else:

time: 131 us -> 128 us (0.977)
  starting transfers between devices: 24.8 us -> 31 us
  waiting for transfers between devices: 46.5 us -> 40.9 us
  Pallas kernels: 23.7 us -> 22.3 us
    ppermute x30 -> x29, starting transfers between devices: 24.8 us -> 31 us  [shift(): return lax.ppermute(block, AXIS, [(i, i ^ distance) for i in range(count)])]
    ppermute x30 -> x29, waiting for transfers between devices: 46.5 us -> 40.9 us  [shift(): return lax.ppermute(block, AXIS, [(i, i ^ distance) for i in range(count)])]
    pallas_call x22 -> x23, Pallas kernels: 23.7 us -> 22.3 us  [run(): pl.pallas_call(body, out_shape=outs, in_specs=[pl.BlockSpec(memory_space=...]
  transfers between devices with their start and end apart: 30 -> 29, of which waited for: 15 -> 19; matrix products, arithmetic and copies ran while one was open for 0% -> 0% of each run, Pallas kernels for 9% -> 9%
where the time goes in v8:
time: 128 us
  waiting for transfers between devices  40.9 us (32%)
  blocking collectives  32.3 us (25%)
  starting transfers between devices  31 us (24%)
  Pallas kernels  22.3 us (17%)
  between operations  1.44 us (1%)
    ppermute x29, waiting for transfers between devices, shift(): return lax.ppermute(block, AXIS, [(i, i ^ distance) for i in range(count)])  40.9 us
    all_to_all x3, blocking collectives, chips_swap(): lax.all_to_all(blocks, AXIS, split_axis=0, concat_axis=0, axis_index_grou...  32.3 us
    ppermute x29, starting transfers between devices, shift(): return lax.ppermute(block, AXIS, [(i, i ^ distance) for i in range(count)])  31 us
    pallas_call x23, Pallas kernels, run(): pl.pallas_call(body, out_shape=outs, in_specs=[pl.BlockSpec(memory_space=...  22.3 us
  transfers between devices with their start and end apart: 29, of which 19 were waited for; matrix products, arithmetic and copies ran while one was open for 0% of the time, Pallas kernels for 9%

profile of v8, /device:TPU:0, one launch (start us, length us, event | category | flops | bytes accessed | tf_op | source)
XLA Modules:
  0.0 127.9 jit_solution(11872541578827089479)
XLA Ops:
  0.0 1.6 %cut.1 = (bf16[2,2,512,128]{3,2,1,0:T(8,128)(2,1)S(1)}, bf16[2,2,512,128]{3,2,1,0:T(8,128)(2,1)S(1)}, bf16[2,2,512,128]{3,2,1,0:T(8,128)(2,1)S(1)}, bf16[2,2,512,128]{3,2,1,0:T(8,128)(2,1)S(1)}) custom-call(s32[1]{0:T(128)} %bitcast.1.me_ref.refs_4_.refs_7_.refs_3_, bf16[1,2,512,1024]{3,2,1,0:T(8,128)(2,1)} %cache_hbm.1), custom_call_target="tpu_custom_call" | custom-call | flops 1048576 | bytes 262144 | tf_op jit(solution)/shard_map/cut/pallas_call | solution.py:53
  1.7 3.0 %collective-permute-start.3 = (bf16[2,2,512,128]{3,2,1,0:T(8,128)(2,1)S(1)}, bf16[2,2,512,128]{3,2,1,0:T(8,128)(2,1)S(1)}, u32[]{:S(2)}, u32[]{:S(2)}) collective-permute-start(bf16[2,2,512,128]{3,2,1,0:T(8,128)(2,1)S(1)} %get-tuple-element.40), channel_id=1, source_target_pairs={{0,2},{1,3},{2,0},{3,1},{4,6},{5,7},{6,4},{7,5},{8,10},{9,11},{10,... | collective-permute-start | bytes 1572872 | tf_op jit(solution)/shard_map/ppermute | solution.py:32
  4.7 1.6 %collective-permute-start.4 = (bf16[2,2,512,128]{3,2,1,0:T(8,128)(2,1)S(1)}, bf16[2,2,512,128]{3,2,1,0:T(8,128)(2,1)S(1)}, u32[]{:S(2)}, u32[]{:S(2)}) collective-permute-start(bf16[2,2,512,128]{3,2,1,0:T(8,128)(2,1)S(1)} %get-tuple-element.41), channel_id=1, source_target_pairs={{0,4},{1,5},{2,6},{3,7},{4,0},{5,1},{6,2},{7,3},{8,12},{9,13},{10,... | collective-permute-start | bytes 1572872 | tf_op jit(solution)/shard_map/ppermute | solution.py:32
  8.2 4.0 %collective-permute-start.2 = (bf16[1,8320]{1,0:T(2,128)(2,1)S(1)}, bf16[1,8320]{1,0:T(2,128)(2,1)S(1)}, u32[]{:S(2)}, u32[]{:S(2)}) collective-permute-start(bf16[1,8320]{1,0:T(2,128)(2,1)S(1)} %get-tuple-element.38.row_ref.refs_0_), channel_id=1, source_target_pairs={{0,12},{1,13},{2,14},{3,15},{4,8},{5,9},{6,10},{7,11},{8,4},{9,5},... | collective-permute-start | bytes 49928 | tf_op jit(solution)/shard_map/ppermute | solution.py:32
  12.2 7.6 %stash.1 = (bf16[8192,512]{1,0:T(8,128)(2,1)S(1)}, bf16[512,8192]{1,0:T(8,128)(2,1)S(1)}, bf16[8192,128]{1,0:T(8,128)(2,1)S(1)}, bf16[2,64,8192]{2,1,0:T(8,128)(...) custom-call(f32[8,128]{1,0:T(8,128)S(1)} %broadcast_in_dim.10.token_ref, bf16[8192,512]{1,0:T(8,128)(2,1)} %refs_0_.1, ...), custom_call_target="tpu_custom_call" | custom-call | flops 1048576 | bytes 23068672 | tf_op jit(solution)/shard_map/stash/pallas_call | solution.py:53
  19.9 12.5 %collective-permute-done.2.refs_3_ = bf16[1,8320]{1,0:T(2,128)(2,1)S(1)} collective-permute-done((bf16[1,8320]{1,0:T(2,128)(2,1)S(1)}, bf16[1,8320]{1,0:T(2,128)(2,1)S(1)}, u32[]{:S(2)}, u32[]{:S(2)}) %collective-permute-start.2) | collective-permute-done | bytes 16672 | tf_op jit(solution)/shard_map/ppermute | solution.py:32
  32.4 3.9 %collective-permute-done.refs_1_ = bf16[1,8320]{1,0:T(2,128)(2,1)S(1)} collective-permute-done((bf16[1,8320]{1,0:T(2,128)(2,1)S(1)}, bf16[1,8320]{1,0:T(2,128)(2,1)S(1)}, u32[]{:S(2)}, u32[]{:S(2)}) %collective-permute-start) | collective-permute-done | bytes 16672 | tf_op jit(solution)/shard_map/ppermute | solution.py:32
  38.3 1.9 %collective-permute-done.8.refs_3_ = bf16[4,8320]{1,0:T(4,128)(2,1)S(1)} collective-permute-done((bf16[4,8320]{1,0:T(4,128)(2,1)S(1)}, bf16[4,8320]{1,0:T(4,128)(2,1)S(1)}, u32[]{:S(2)}, u32[]{:S(2)}) %collective-permute-start.8) | collective-permute-done | bytes 66592 | tf_op jit(solution)/shard_map/ppermute | solution.py:32
  43.1 1.4 %collective-permute-start.11 = (bf16[16,256]{1,0:T(8,128)(2,1)S(1)}, bf16[16,256]{1,0:T(8,128)(2,1)S(1)}, u32[]{:S(2)}, u32[]{:S(2)}) collective-permute-start(bf16[16,256]{1,0:T(8,128)(2,1)S(1)} %get-tuple-element.46.refs_0_), channel_id=1, source_target_pairs={{0,3},{1,2},{2,1},{3,0},{4,7},{5,6},{6,5},{7,4},{8,11},{9,10},{10,... | collective-permute-start | bytes 24584 | tf_op jit(solution)/shard_map/ppermute | solution.py:32
  46.3 1.9 %collective-permute-done.10.refs_2_ = bf16[16,256]{1,0:T(8,128)(2,1)S(1)} collective-permute-done((bf16[16,256]{1,0:T(8,128)(2,1)S(1)}, bf16[16,256]{1,0:T(8,128)(2,1)S(1)}, u32[]{:S(2)}, u32[]{:S(2)}) %collective-permute-start.10) | collective-permute-done | bytes 8224 | tf_op jit(solution)/shard_map/ppermute | solution.py:32
  48.2 1.5 %collective-permute-start.14 = (bf16[16,640]{1,0:T(8,128)(2,1)S(1)}, bf16[16,640]{1,0:T(8,128)(2,1)S(1)}, u32[]{:S(2)}, u32[]{:S(2)}) collective-permute-start(bf16[16,640]{1,0:T(8,128)(2,1)S(1)} %sum.2.refs_0_.refs_4_), channel_id=1, source_target_pairs={{0,12},{1,13},{2,14},{3,15},{4,8},{5,9},{6,10},{7,11},{8,4},{9,5},... | collective-permute-start | bytes 61448 | tf_op jit(solution)/shard_map/ppermute | solution.py:32
  49.8 2.9 %collective-permute-start.12 = (bf16[16,640]{1,0:T(8,128)(2,1)S(1)}, bf16[16,640]{1,0:T(8,128)(2,1)S(1)}, u32[]{:S(2)}, u32[]{:S(2)}) collective-permute-start(bf16[16,640]{1,0:T(8,128)(2,1)S(1)} %sum.2.refs_0_.refs_4_), channel_id=1, source_target_pairs={{0,4},{1,5},{2,6},{3,7},{4,0},{5,1},{6,2},{7,3},{8,12},{9,13},{10,... | collective-permute-start | bytes 61448 | tf_op jit(solution)/shard_map/ppermute | solution.py:32
  55.1 1.8 %collective-permute-start.15 = (bf16[8,512]{1,0:T(8,128)(2,1)S(1)}, bf16[8,512]{1,0:T(8,128)(2,1)S(1)}, u32[]{:S(2)}, u32[]{:S(2)}) collective-permute-start(bf16[8,512]{1,0:T(8,128)(2,1)S(1)} %get-tuple-element.52), channel_id=1, source_target_pairs={{0,8},{1,9},{2,10},{3,11},{4,12},{5,13},{6,14},{7,15},{8,0},{9,1},... | collective-permute-start | bytes 24584 | tf_op jit(solution)/shard_map/ppermute | solution.py:32
  56.9 2.7 %collective-permute-done.15.refs_1_ = bf16[8,512]{1,0:T(8,128)(2,1)S(1)} collective-permute-done((bf16[8,512]{1,0:T(8,128)(2,1)S(1)}, bf16[8,512]{1,0:T(8,128)(2,1)S(1)}, u32[]{:S(2)}, u32[]{:S(2)}) %collective-permute-start.15) | collective-permute-done | bytes 8224 | tf_op jit(solution)/shard_map/ppermute | solution.py:32
  60.9 1.9 %collective-permute-start.17 = (bf16[8,512]{1,0:T(8,128)(2,1)S(1)}, bf16[8,512]{1,0:T(8,128)(2,1)S(1)}, u32[]{:S(2)}, u32[]{:S(2)}) collective-permute-start(bf16[8,512]{1,0:T(8,128)(2,1)S(1)} %get-tuple-element.56), channel_id=1, source_target_pairs={{0,8},{1,9},{2,10},{3,11},{4,12},{5,13},{6,14},{7,15},{8,0},{9,1},... | collective-permute-start | bytes 24584 | tf_op jit(solution)/shard_map/ppermute | solution.py:32
  62.7 2.7 %collective-permute-done.17.other_ref = bf16[8,512]{1,0:T(8,128)(2,1)S(1)} collective-permute-done((bf16[8,512]{1,0:T(8,128)(2,1)S(1)}, bf16[8,512]{1,0:T(8,128)(2,1)S(1)}, u32[]{:S(2)}, u32[]{:S(2)}) %collective-permute-start.17) | collective-permute-done | bytes 8224 | tf_op jit(solution)/shard_map/ppermute | solution.py:32
  65.5 1.3 %output.2 = (f32[8,8192]{1,0:T(8,128)S(1)}, bf16[8,8192]{1,0:T(8,128)(2,1)S(1)}) custom-call(bf16[8,512]{1,0:T(8,128)(2,1)S(1)} %get-tuple-element.55.mine_ref, bf16[8,512]{1,0:T(8,128)(2,1)S(1)} %collective-permute-done.17.other_ref, s32[1]{0:T(128)} %bitcast.1.me_ref.refs_4_.refs_7_.refs_3_, bf16[512,8192]{1,0:T(8,128)(2,1)S(1)} %get-tuple-element.57.weight_ref), custom_call_target="tpu_custom_call" | custom-call | flops 134217728 | bytes 8388608 | tf_op jit(solution)/shard_map/output/pallas_call | solution.py:53
  66.8 1.4 %collective-permute-done.18.other_ref = bf16[8,8192]{1,0:T(8,128)(2,1)S(1)} collective-permute-done((bf16[8,8192]{1,0:T(8,128)(2,1)S(1)}, bf16[8,8192]{1,0:T(8,128)(2,1)S(1)}, u32[]{:S(2)}, u32[]{:S(2)}) %collective-permute-start.18) | collective-permute-done | bytes 131104 | tf_op jit(solution)/shard_map/ppermute | solution.py:32
  68.3 10.7 %all_to_all.15.parts_ref = bf16[8,8,1024]{2,1,0:T(8,128)(2,1)S(1)} all-to-all(bf16[8,8,1024]{2,1,0:T(8,128)(2,1)S(1)} %partial.2), channel_id=1, replica_groups={{0,2,4,6,8,10,12,14},{1,3,5,7,9,11,13,15},{16,18,20,22,24,26,28,30},{17..., dimensions={0} | all-to-all | bytes 262144 | tf_op jit(solution)/shard_map/all_to_all | solution.py:45
  79.4 9.8 %all_to_all.16.own_ref = bf16[8,8,1024]{2,1,0:T(8,128)(2,1)S(1)} all-to-all(bf16[8,8,1024]{2,1,0:T(8,128)(2,1)S(1)} %get-tuple-element.60), channel_id=1, replica_groups={{0,2,4,6,8,10,12,14},{1,3,5,7,9,11,13,15},{16,18,20,22,24,26,28,30},{17..., dimensions={0} | all-to-all | bytes 262144 | tf_op jit(solution)/shard_map/all_to_all | solution.py:45
  89.2 1.3 %collective-permute-done.19.other_ref = bf16[8,8,1024]{2,1,0:T(8,128)(2,1)S(1)} collective-permute-done((bf16[8,8,1024]{2,1,0:T(8,128)(2,1)S(1)}, bf16[8,8,1024]{2,1,0:T(8,128)(2,1)S(1)}, u32[]{:S(2)}, u32[]{:S(2)}) %collective-permute-start.19) | collective-permute-done | bytes 131104 | tf_op jit(solution)/shard_map/ppermute | solution.py:32
  91.7 1.8 %collective-permute-start.21 = (bf16[16,256]{1,0:T(8,128)(2,1)S(1)}, bf16[16,256]{1,0:T(8,128)(2,1)S(1)}, u32[]{:S(2)}, u32[]{:S(2)}) collective-permute-start(bf16[16,256]{1,0:T(8,128)(2,1)S(1)} %get-tuple-element.61.refs_0_), channel_id=1, source_target_pairs={{0,2},{1,3},{2,0},{3,1},{4,6},{5,7},{6,4},{7,5},{8,10},{9,11},{10,... | collective-permute-start | bytes 24584 | tf_op jit(solution)/shard_map/ppermute | solution.py:32
  95.4 1.4 %collective-permute-start.25 = (bf16[16,640]{1,0:T(8,128)(2,1)S(1)}, bf16[16,640]{1,0:T(8,128)(2,1)S(1)}, u32[]{:S(2)}, u32[]{:S(2)}) collective-permute-start(bf16[16,640]{1,0:T(8,128)(2,1)S(1)} %sum.3.refs_0_.refs_4_), channel_id=1, source_target_pairs={{0,12},{1,13},{2,14},{3,15},{4,8},{5,9},{6,10},{7,11},{8,4},{9,5},... | collective-permute-start | bytes 61448 | tf_op jit(solution)/shard_map/ppermute | solution.py:32
  97.9 1.9 %collective-permute-start.23 = (bf16[16,640]{1,0:T(8,128)(2,1)S(1)}, bf16[16,640]{1,0:T(8,128)(2,1)S(1)}, u32[]{:S(2)}, u32[]{:S(2)}) collective-permute-start(bf16[16,640]{1,0:T(8,128)(2,1)S(1)} %sum.3.refs_0_.refs_4_), channel_id=1, source_target_pairs={{0,4},{1,5},{2,6},{3,7},{4,0},{5,1},{6,2},{7,3},{8,12},{9,13},{10,... | collective-permute-start | bytes 61448 | tf_op jit(solution)/shard_map/ppermute | solution.py:32
  102.2 1.8 %collective-permute-start.26 = (bf16[8,512]{1,0:T(8,128)(2,1)S(1)}, bf16[8,512]{1,0:T(8,128)(2,1)S(1)}, u32[]{:S(2)}, u32[]{:S(2)}) collective-permute-start(bf16[8,512]{1,0:T(8,128)(2,1)S(1)} %get-tuple-element.64), channel_id=1, source_target_pairs={{0,8},{1,9},{2,10},{3,11},{4,12},{5,13},{6,14},{7,15},{8,0},{9,1},... | collective-permute-start | bytes 24584 | tf_op jit(solution)/shard_map/ppermute | solution.py:32
  104.0 2.7 %collective-permute-done.26.refs_1_ = bf16[8,512]{1,0:T(8,128)(2,1)S(1)} collective-permute-done((bf16[8,512]{1,0:T(8,128)(2,1)S(1)}, bf16[8,512]{1,0:T(8,128)(2,1)S(1)}, u32[]{:S(2)}, u32[]{:S(2)}) %collective-permute-start.26) | collective-permute-done | bytes 8224 | tf_op jit(solution)/shard_map/ppermute | solution.py:32
  106.7 1.3 attend.3
  108.0 1.8 %collective-permute-start.27 = (bf16[8,512]{1,0:T(8,128)(2,1)S(1)}, bf16[8,512]{1,0:T(8,128)(2,1)S(1)}, u32[]{:S(2)}, u32[]{:S(2)}) collective-permute-start(bf16[8,512]{1,0:T(8,128)(2,1)S(1)} %get-tuple-element.67), channel_id=1, source_target_pairs={{0,8},{1,9},{2,10},{3,11},{4,12},{5,13},{6,14},{7,15},{8,0},{9,1},... | collective-permute-start | bytes 24584 | tf_op jit(solution)/shard_map/ppermute | solution.py:32
  109.8 2.7 %collective-permute-done.27.other_ref = bf16[8,512]{1,0:T(8,128)(2,1)S(1)} collective-permute-done((bf16[8,512]{1,0:T(8,128)(2,1)S(1)}, bf16[8,512]{1,0:T(8,128)(2,1)S(1)}, u32[]{:S(2)}, u32[]{:S(2)}) %collective-permute-start.27) | collective-permute-done | bytes 8224 | tf_op jit(solution)/shard_map/ppermute | solution.py:32
  112.6 1.3 %output.3 = (f32[8,8192]{1,0:T(8,128)S(1)}, bf16[8,8192]{1,0:T(8,128)(2,1)S(1)}) custom-call(bf16[8,512]{1,0:T(8,128)(2,1)S(1)} %get-tuple-element.66.mine_ref, bf16[8,512]{1,0:T(8,128)(2,1)S(1)} %collective-permute-done.27.other_ref, s32[1]{0:T(128)} %bitcast.1.me_ref.refs_4_.refs_7_.refs_3_, bf16[512,8192]{1,0:T(8,128)(2,1)S(1)} %get-tuple-element.57.weight_ref), custom_call_target="tpu_custom_call" | custom-call | flops 134217728 | bytes 8388608 | tf_op jit(solution)/shard_map/output/pallas_call | solution.py:53
  113.9 1.4 %collective-permute-done.28.other_ref = bf16[8,8192]{1,0:T(8,128)(2,1)S(1)} collective-permute-done((bf16[8,8192]{1,0:T(8,128)(2,1)S(1)}, bf16[8,8192]{1,0:T(8,128)(2,1)S(1)}, u32[]{:S(2)}, u32[]{:S(2)}) %collective-permute-start.28) | collective-permute-done | bytes 131104 | tf_op jit(solution)/shard_map/ppermute | solution.py:32
  115.4 11.8 %all_to_all.17.parts_ref = bf16[8,8,1024]{2,1,0:T(8,128)(2,1)S(1)} all-to-all(bf16[8,8,1024]{2,1,0:T(8,128)(2,1)S(1)} %partial.3), channel_id=1, replica_groups={{0,2,4,6,8,10,12,14},{1,3,5,7,9,11,13,15},{16,18,20,22,24,26,28,30},{17..., dimensions={0} | all-to-all | bytes 262144 | tf_op jit(solution)/shard_map/all_to_all | solution.py:45
  (60 shorter events, 18.9 us)
Async XLA Ops:
  0.0 7.5 %copy-start.2 = (bf16[8192]{0:T(1024)(128)(2,1)S(1)}, bf16[8192]{0:T(1024)(128)(2,1)}, u32[]{:S(2)}) copy-start(bf16[8192]{0:T(1024)(128)(2,1)} %param.12) | copy-start | bytes 49156
  0.0 7.6 %copy-start = (bf16[1,8192]{1,0:T(2,128)(2,1)S(1)}, bf16[1,8192]{1,0:T(2,128)(2,1)}, u32[]{:S(2)}) copy-start(bf16[1,8192]{1,0:T(2,128)(2,1)} %hidden_ref.3) | copy-start | bytes 49156
  1.7 34.6 %collective-permute-start.3 = (bf16[2,2,512,128]{3,2,1,0:T(8,128)(2,1)S(1)}, bf16[2,2,512,128]{3,2,1,0:T(8,128)(2,1)S(1)}, u32[]{:S(2)}, u32[]{:S(2)}) collective-permute-start(bf16[2,2,512,128]{3,2,1,0:T(8,128)(2,1)S(1)} %get-tuple-element.40), channel_id=1, source_target_pairs={{0,2},{1,3},{2,0},{3,1},{4,6},{5,7},{6,4},{7,5},{8,10},{9,11},{10,... | collective-permute-start | bytes 1572872 | tf_op jit(solution)/shard_map/ppermute | solution.py:32
  4.7 31.6 %collective-permute-start.4 = (bf16[2,2,512,128]{3,2,1,0:T(8,128)(2,1)S(1)}, bf16[2,2,512,128]{3,2,1,0:T(8,128)(2,1)S(1)}, u32[]{:S(2)}, u32[]{:S(2)}) collective-permute-start(bf16[2,2,512,128]{3,2,1,0:T(8,128)(2,1)S(1)} %get-tuple-element.41), channel_id=1, source_target_pairs={{0,4},{1,5},{2,6},{3,7},{4,0},{5,1},{6,2},{7,3},{8,12},{9,13},{10,... | collective-permute-start | bytes 1572872 | tf_op jit(solution)/shard_map/ppermute | solution.py:32
  6.2 30.1 %collective-permute-start.5 = (bf16[2,2,512,128]{3,2,1,0:T(8,128)(2,1)S(1)}, bf16[2,2,512,128]{3,2,1,0:T(8,128)(2,1)S(1)}, u32[]{:S(2)}, u32[]{:S(2)}) collective-permute-start(bf16[2,2,512,128]{3,2,1,0:T(8,128)(2,1)S(1)} %get-tuple-element.42), channel_id=1, source_target_pairs={{0,6},{1,7},{2,4},{3,5},{4,2},{5,3},{6,0},{7,1},{8,14},{9,15},{10,... | collective-permute-start | bytes 1572872 | tf_op jit(solution)/shard_map/ppermute | solution.py:32
  8.2 24.2 %collective-permute-start.2 = (bf16[1,8320]{1,0:T(2,128)(2,1)S(1)}, bf16[1,8320]{1,0:T(2,128)(2,1)S(1)}, u32[]{:S(2)}, u32[]{:S(2)}) collective-permute-start(bf16[1,8320]{1,0:T(2,128)(2,1)S(1)} %get-tuple-element.38.row_ref.refs_0_), channel_id=1, source_target_pairs={{0,12},{1,13},{2,14},{3,15},{4,8},{5,9},{6,10},{7,11},{8,4},{9,5},... | collective-permute-start | bytes 49928 | tf_op jit(solution)/shard_map/ppermute | solution.py:32
  12.2 20.2 %collective-permute-start.1 = (bf16[1,8320]{1,0:T(2,128)(2,1)S(1)}, bf16[1,8320]{1,0:T(2,128)(2,1)S(1)}, u32[]{:S(2)}, u32[]{:S(2)}) collective-permute-start(bf16[1,8320]{1,0:T(2,128)(2,1)S(1)} %get-tuple-element.38.row_ref.refs_0_), channel_id=1, source_target_pairs={{0,8},{1,9},{2,10},{3,11},{4,12},{5,13},{6,14},{7,15},{8,0},{9,1},... | collective-permute-start | bytes 49928 | tf_op jit(solution)/shard_map/ppermute | solution.py:32
  12.2 29.3 %copy-start.1 = (s32[32]{0:T(128)S(1)}, s32[32]{0:T(128)}, u32[]{:S(2)}) copy-start(s32[32]{0:T(128)} %param.19) | copy-start | bytes 388
  32.4 3.9 %collective-permute-start = (bf16[1,8320]{1,0:T(2,128)(2,1)S(1)}, bf16[1,8320]{1,0:T(2,128)(2,1)S(1)}, u32[]{:S(2)}, u32[]{:S(2)}) collective-permute-start(bf16[1,8320]{1,0:T(2,128)(2,1)S(1)} %late.1), channel_id=1, source_target_pairs={{0,4},{1,5},{2,6},{3,7},{4,0},{5,1},{6,2},{7,3},{8,12},{9,13},{10,... | collective-permute-start | bytes 49928 | tf_op jit(solution)/shard_map/ppermute | solution.py:32
  36.4 3.9 %collective-permute-start.8 = (bf16[4,8320]{1,0:T(4,128)(2,1)S(1)}, bf16[4,8320]{1,0:T(4,128)(2,1)S(1)}, u32[]{:S(2)}, u32[]{:S(2)}) collective-permute-start(bf16[4,8320]{1,0:T(4,128)(2,1)S(1)} %join.1.refs_0_), channel_id=1, source_target_pairs={{0,3},{1,2},{2,1},{3,0},{4,7},{5,6},{6,5},{7,4},{8,11},{9,10},{10,... | collective-permute-start | bytes 199688 | tf_op jit(solution)/shard_map/ppermute | solution.py:32
  36.5 5.0 %collective-permute-start.7 = (bf16[4,8320]{1,0:T(4,128)(2,1)S(1)}, bf16[4,8320]{1,0:T(4,128)(2,1)S(1)}, u32[]{:S(2)}, u32[]{:S(2)}) collective-permute-start(bf16[4,8320]{1,0:T(4,128)(2,1)S(1)} %join.1.refs_0_), channel_id=1, source_target_pairs={{0,2},{1,3},{2,0},{3,1},{4,6},{5,7},{6,4},{7,5},{8,10},{9,11},{10,... | collective-permute-start | bytes 199688 | tf_op jit(solution)/shard_map/ppermute | solution.py:32
  37.1 4.4 %collective-permute-start.6 = (bf16[4,8320]{1,0:T(4,128)(2,1)S(1)}, bf16[4,8320]{1,0:T(4,128)(2,1)S(1)}, u32[]{:S(2)}, u32[]{:S(2)}) collective-permute-start(bf16[4,8320]{1,0:T(4,128)(2,1)S(1)} %join.1.refs_0_), channel_id=1, source_target_pairs={{0,1},{1,0},{2,3},{3,2},{4,5},{5,4},{6,7},{7,6},{8,9},{9,8},{10,11... | collective-permute-start | bytes 199688 | tf_op jit(solution)/shard_map/ppermute | solution.py:32
  41.9 17.8 %collective-permute-start.16 = (bf16[4,2,2,512,128]{4,3,2,1,0:T(8,128)(2,1)S(1)}, bf16[4,2,2,512,128]{4,3,2,1,0:T(8,128)(2,1)S(1)}, u32[]{:S(2)}, u32[]{:S(2)}) collective-permute-start(bf16[4,2,2,512,128]{4,3,2,1,0:T(8,128)(2,1)S(1)} %merge.1), channel_id=1, source_target_pairs={{0,1},{1,0},{2,3},{3,2},{4,5},{5,4},{6,7},{7,6},{8,9},{9,8},{10,11... | collective-permute-start | bytes 6291464 | tf_op jit(solution)/shard_map/ppermute | solution.py:32
  43.1 3.2 %collective-permute-start.11 = (bf16[16,256]{1,0:T(8,128)(2,1)S(1)}, bf16[16,256]{1,0:T(8,128)(2,1)S(1)}, u32[]{:S(2)}, u32[]{:S(2)}) collective-permute-start(bf16[16,256]{1,0:T(8,128)(2,1)S(1)} %get-tuple-element.46.refs_0_), channel_id=1, source_target_pairs={{0,3},{1,2},{2,1},{3,0},{4,7},{5,6},{6,5},{7,4},{8,11},{9,10},{10,... | collective-permute-start | bytes 24584 | tf_op jit(solution)/shard_map/ppermute | solution.py:32
  44.6 3.7 %collective-permute-start.10 = (bf16[16,256]{1,0:T(8,128)(2,1)S(1)}, bf16[16,256]{1,0:T(8,128)(2,1)S(1)}, u32[]{:S(2)}, u32[]{:S(2)}) collective-permute-start(bf16[16,256]{1,0:T(8,128)(2,1)S(1)} %get-tuple-element.46.refs_0_), channel_id=1, source_target_pairs={{0,2},{1,3},{2,0},{3,1},{4,6},{5,7},{6,4},{7,5},{8,10},{9,11},{10,... | collective-permute-start | bytes 24584 | tf_op jit(solution)/shard_map/ppermute | solution.py:32
  45.2 3.0 %collective-permute-start.9 = (bf16[16,256]{1,0:T(8,128)(2,1)S(1)}, bf16[16,256]{1,0:T(8,128)(2,1)S(1)}, u32[]{:S(2)}, u32[]{:S(2)}) collective-permute-start(bf16[16,256]{1,0:T(8,128)(2,1)S(1)} %get-tuple-element.46.refs_0_), channel_id=1, source_target_pairs={{0,1},{1,0},{2,3},{3,2},{4,5},{5,4},{6,7},{7,6},{8,9},{9,8},{10,11... | collective-permute-start | bytes 24584 | tf_op jit(solution)/shard_map/ppermute | solution.py:32
  48.2 5.6 %collective-permute-start.14 = (bf16[16,640]{1,0:T(8,128)(2,1)S(1)}, bf16[16,640]{1,0:T(8,128)(2,1)S(1)}, u32[]{:S(2)}, u32[]{:S(2)}) collective-permute-start(bf16[16,640]{1,0:T(8,128)(2,1)S(1)} %sum.2.refs_0_.refs_4_), channel_id=1, source_target_pairs={{0,12},{1,13},{2,14},{3,15},{4,8},{5,9},{6,10},{7,11},{8,4},{9,5},... | collective-permute-start | bytes 61448 | tf_op jit(solution)/shard_map/ppermute | solution.py:32
  49.7 4.7 %collective-permute-start.13 = (bf16[16,640]{1,0:T(8,128)(2,1)S(1)}, bf16[16,640]{1,0:T(8,128)(2,1)S(1)}, u32[]{:S(2)}, u32[]{:S(2)}) collective-permute-start(bf16[16,640]{1,0:T(8,128)(2,1)S(1)} %sum.2.refs_0_.refs_4_), channel_id=1, source_target_pairs={{0,8},{1,9},{2,10},{3,11},{4,12},{5,13},{6,14},{7,15},{8,0},{9,1},... | collective-permute-start | bytes 61448 | tf_op jit(solution)/shard_map/ppermute | solution.py:32
  49.8 4.9 %collective-permute-start.12 = (bf16[16,640]{1,0:T(8,128)(2,1)S(1)}, bf16[16,640]{1,0:T(8,128)(2,1)S(1)}, u32[]{:S(2)}, u32[]{:S(2)}) collective-permute-start(bf16[16,640]{1,0:T(8,128)(2,1)S(1)} %sum.2.refs_0_.refs_4_), channel_id=1, source_target_pairs={{0,4},{1,5},{2,6},{3,7},{4,0},{5,1},{6,2},{7,3},{8,12},{9,13},{10,... | collective-permute-start | bytes 61448 | tf_op jit(solution)/shard_map/ppermute | solution.py:32
  55.1 4.6 %collective-permute-start.15 = (bf16[8,512]{1,0:T(8,128)(2,1)S(1)}, bf16[8,512]{1,0:T(8,128)(2,1)S(1)}, u32[]{:S(2)}, u32[]{:S(2)}) collective-permute-start(bf16[8,512]{1,0:T(8,128)(2,1)S(1)} %get-tuple-element.52), channel_id=1, source_target_pairs={{0,8},{1,9},{2,10},{3,11},{4,12},{5,13},{6,14},{7,15},{8,0},{9,1},... | collective-permute-start | bytes 24584 | tf_op jit(solution)/shard_map/ppermute | solution.py:32
  60.9 4.6 %collective-permute-start.17 = (bf16[8,512]{1,0:T(8,128)(2,1)S(1)}, bf16[8,512]{1,0:T(8,128)(2,1)S(1)}, u32[]{:S(2)}, u32[]{:S(2)}) collective-permute-start(bf16[8,512]{1,0:T(8,128)(2,1)S(1)} %get-tuple-element.56), channel_id=1, source_target_pairs={{0,8},{1,9},{2,10},{3,11},{4,12},{5,13},{6,14},{7,15},{8,0},{9,1},... | collective-permute-start | bytes 24584 | tf_op jit(solution)/shard_map/ppermute | solution.py:32
  66.8 1.4 %collective-permute-start.18 = (bf16[8,8192]{1,0:T(8,128)(2,1)S(1)}, bf16[8,8192]{1,0:T(8,128)(2,1)S(1)}, u32[]{:S(2)}, u32[]{:S(2)}) collective-permute-start(bf16[8,8192]{1,0:T(8,128)(2,1)S(1)} %get-tuple-element.59), channel_id=1, source_target_pairs={{0,1},{1,0},{2,3},{3,2},{4,5},{5,4},{6,7},{7,6},{8,9},{9,8},{10,11... | collective-permute-start | bytes 393224 | tf_op jit(solution)/shard_map/ppermute | solution.py:32
  89.2 1.3 %collective-permute-start.19 = (bf16[8,8,1024]{2,1,0:T(8,128)(2,1)S(1)}, bf16[8,8,1024]{2,1,0:T(8,128)(2,1)S(1)}, u32[]{:S(2)}, u32[]{:S(2)}) collective-permute-start(bf16[8,8,1024]{2,1,0:T(8,128)(2,1)S(1)} %all_to_all.16.own_ref), channel_id=1, source_target_pairs={{0,1},{1,0},{2,3},{3,2},{4,5},{5,4},{6,7},{7,6},{8,9},{9,8},{10,11... | collective-permute-start | bytes 393224 | tf_op jit(solution)/shard_map/ppermute | solution.py:32
  91.6 3.1 %collective-permute-start.22 = (bf16[16,256]{1,0:T(8,128)(2,1)S(1)}, bf16[16,256]{1,0:T(8,128)(2,1)S(1)}, u32[]{:S(2)}, u32[]{:S(2)}) collective-permute-start(bf16[16,256]{1,0:T(8,128)(2,1)S(1)} %get-tuple-element.61.refs_0_), channel_id=1, source_target_pairs={{0,3},{1,2},{2,1},{3,0},{4,7},{5,6},{6,5},{7,4},{8,11},{9,10},{10,... | collective-permute-start | bytes 24584 | tf_op jit(solution)/shard_map/ppermute | solution.py:32
  91.7 3.7 %collective-permute-start.21 = (bf16[16,256]{1,0:T(8,128)(2,1)S(1)}, bf16[16,256]{1,0:T(8,128)(2,1)S(1)}, u32[]{:S(2)}, u32[]{:S(2)}) collective-permute-start(bf16[16,256]{1,0:T(8,128)(2,1)S(1)} %get-tuple-element.61.refs_0_), channel_id=1, source_target_pairs={{0,2},{1,3},{2,0},{3,1},{4,6},{5,7},{6,4},{7,5},{8,10},{9,11},{10,... | collective-permute-start | bytes 24584 | tf_op jit(solution)/shard_map/ppermute | solution.py:32
  93.4 1.9 %collective-permute-start.20 = (bf16[16,256]{1,0:T(8,128)(2,1)S(1)}, bf16[16,256]{1,0:T(8,128)(2,1)S(1)}, u32[]{:S(2)}, u32[]{:S(2)}) collective-permute-start(bf16[16,256]{1,0:T(8,128)(2,1)S(1)} %get-tuple-element.61.refs_0_), channel_id=1, source_target_pairs={{0,1},{1,0},{2,3},{3,2},{4,5},{5,4},{6,7},{7,6},{8,9},{9,8},{10,11... | collective-permute-start | bytes 24584 | tf_op jit(solution)/shard_map/ppermute | solution.py:32
  95.4 5.6 %collective-permute-start.25 = (bf16[16,640]{1,0:T(8,128)(2,1)S(1)}, bf16[16,640]{1,0:T(8,128)(2,1)S(1)}, u32[]{:S(2)}, u32[]{:S(2)}) collective-permute-start(bf16[16,640]{1,0:T(8,128)(2,1)S(1)} %sum.3.refs_0_.refs_4_), channel_id=1, source_target_pairs={{0,12},{1,13},{2,14},{3,15},{4,8},{5,9},{6,10},{7,11},{8,4},{9,5},... | collective-permute-start | bytes 61448 | tf_op jit(solution)/shard_map/ppermute | solution.py:32
  96.8 4.7 %collective-permute-start.24 = (bf16[16,640]{1,0:T(8,128)(2,1)S(1)}, bf16[16,640]{1,0:T(8,128)(2,1)S(1)}, u32[]{:S(2)}, u32[]{:S(2)}) collective-permute-start(bf16[16,640]{1,0:T(8,128)(2,1)S(1)} %sum.3.refs_0_.refs_4_), channel_id=1, source_target_pairs={{0,8},{1,9},{2,10},{3,11},{4,12},{5,13},{6,14},{7,15},{8,0},{9,1},... | collective-permute-start | bytes 61448 | tf_op jit(solution)/shard_map/ppermute | solution.py:32
  97.9 3.8 %collective-permute-start.23 = (bf16[16,640]{1,0:T(8,128)(2,1)S(1)}, bf16[16,640]{1,0:T(8,128)(2,1)S(1)}, u32[]{:S(2)}, u32[]{:S(2)}) collective-permute-start(bf16[16,640]{1,0:T(8,128)(2,1)S(1)} %sum.3.refs_0_.refs_4_), channel_id=1, source_target_pairs={{0,4},{1,5},{2,6},{3,7},{4,0},{5,1},{6,2},{7,3},{8,12},{9,13},{10,... | collective-permute-start | bytes 61448 | tf_op jit(solution)/shard_map/ppermute | solution.py:32
  102.2 4.6 %collective-permute-start.26 = (bf16[8,512]{1,0:T(8,128)(2,1)S(1)}, bf16[8,512]{1,0:T(8,128)(2,1)S(1)}, u32[]{:S(2)}, u32[]{:S(2)}) collective-permute-start(bf16[8,512]{1,0:T(8,128)(2,1)S(1)} %get-tuple-element.64), channel_id=1, source_target_pairs={{0,8},{1,9},{2,10},{3,11},{4,12},{5,13},{6,14},{7,15},{8,0},{9,1},... | collective-permute-start | bytes 24584 | tf_op jit(solution)/shard_map/ppermute | solution.py:32
  108.0 4.6 %collective-permute-start.27 = (bf16[8,512]{1,0:T(8,128)(2,1)S(1)}, bf16[8,512]{1,0:T(8,128)(2,1)S(1)}, u32[]{:S(2)}, u32[]{:S(2)}) collective-permute-start(bf16[8,512]{1,0:T(8,128)(2,1)S(1)} %get-tuple-element.67), channel_id=1, source_target_pairs={{0,8},{1,9},{2,10},{3,11},{4,12},{5,13},{6,14},{7,15},{8,0},{9,1},... | collective-permute-start | bytes 24584 | tf_op jit(solution)/shard_map/ppermute | solution.py:32
  113.9 1.4 %collective-permute-start.28 = (bf16[8,8192]{1,0:T(8,128)(2,1)S(1)}, bf16[8,8192]{1,0:T(8,128)(2,1)S(1)}, u32[]{:S(2)}, u32[]{:S(2)}) collective-permute-start(bf16[8,8192]{1,0:T(8,128)(2,1)S(1)} %get-tuple-element.69), channel_id=1, source_target_pairs={{0,1},{1,0},{2,3},{3,2},{4,5},{5,4},{6,7},{7,6},{8,9},{9,8},{10,11... | collective-permute-start | bytes 393224 | tf_op jit(solution)/shard_map/ppermute | solution.py:32

commit v9 on v5

--- a/solution.py
+++ b/solution.py
@@ -81,6 +81,11 @@
     return (hidden * factor * scale).astype(jnp.bfloat16)
 
 
+def row_of(ref):
+    lines = ref[...].astype(jnp.float32)
+    return jnp.concatenate([lines[i : i + 1] for i in range(lines.shape[0])], axis=1)
+
+
 def folded(out_ref, row):
     wide = row.shape[1] // FOLD
     for k in range(out_ref.shape[0]):
@@ -92,7 +97,7 @@
     length_out[...] = jnp.full(length_out.shape, length_ref[0], jnp.int32)
     width = hidden_ref.shape[1]
     hidden = hidden_ref[...].astype(jnp.float32)
-    out_ref[:, :width] = normalized(hidden, scale_ref[...].astype(jnp.float32))
+    out_ref[:, :width] = normalized(hidden, row_of(scale_ref))
     digit = iota((1, LANES), 1)
     adapter = adapter_ref[0]
     high, low = adapter // 256, adapter % 256
@@ -108,14 +113,14 @@
     ]
     for copy in copies:
         copy.start()
-    out_token[...] = token_ref[...] * 0.0
+    out_token[...] = token_ref[...]
     for copy in copies:
         copy.wait()
 
 
 def member_kernel(near, far, width, *refs):
     pieces, refs = refs[:near], refs[near:]
-    me_ref, storage_ref, member_ref, adapter_ref, held = refs
+    me_ref, storage_ref, _, member_ref, adapter_ref, held = refs
     kept = member_ref.shape[1]
     count = near * far
     me = me_ref[0]
@@ -162,6 +167,11 @@
             for i in range(FOLD):
                 held[row, i * wide : (i + 1) * wide] = block[i : i + 1]
     low_terms(held, member_ref, down_ref, rows_ref, low_ref)
+
+
+def join_kernel(amount, *refs):
+    rows = [ref[...].astype(jnp.float32) for ref in refs[:amount]]
+    refs[-1][...] = jnp.concatenate(rows, axis=0).astype(refs[-1].dtype)
 
 
 def sum_kernel(*refs):
@@ -350,7 +360,7 @@
         out_ref[...] = jnp.concatenate([before, hidden], axis=0).astype(jnp.bfloat16)
     else:
         out_ref[...] = hidden.astype(jnp.bfloat16)
-        folded(spread[0], normalized(hidden, scale_ref[...].astype(jnp.float32)).astype(jnp.float32))
+        folded(spread[0], normalized(hidden, row_of(scale_ref)).astype(jnp.float32))
 
 
 def shards(
@@ -378,18 +388,21 @@
     smem, vmem = pltpu.SMEM, pltpu.VMEM
     me = lax.axis_index(AXIS).astype(jnp.int32).reshape(1)
     down = adapter_down_weight.transpose(0, 2, 1)
-    scale = attention_norm_scale[None]
+    scale = attention_norm_scale.reshape(-1, LANES)
     storage = adapter_storage_index[None]
 
-    def stash(token, arrays, limit):
+    def stash(token, arrays):
         outs = call(
             functools.partial(stash_kernel, len(arrays)),
-            [pltpu.VMEM(a.shape, a.dtype) for a in arrays] + [shape((8, LANES), jnp.float32)],
+            [pltpu.VMEM(a.shape, a.dtype) for a in arrays] + [shape((8, LANES), jnp.int32)],
             "stash",
             [pltpu.SemaphoreType.DMA((len(arrays),))],
-            vmem=limit,
             moved=sum(2 * a.size for a in arrays),
-        )(token, *arrays, specs=[vmem] + [pl.ANY] * len(arrays))
+        )(
+            token,
+            *(pltpu.with_memory_space_constraint(a, pltpu.HBM) for a in arrays),
+            specs=[vmem] + [pltpu.HBM] * len(arrays),
+        )
         return outs[:-1], outs[-1]
 
     hidden = hidden_state_input
@@ -402,21 +415,21 @@
         outs = [shape((count, width)), shape((count, rank))]
         scratch = [pltpu.VMEM((count, width), jnp.float32)]
         if first:
-            token = jnp.zeros((8, LANES), jnp.float32)
-            (query_w, output_w, fresh_w, down_w, cache, up_w), token = stash(
-                token,
-                [query_weight, output_weight, key_value_weight, down, key_value_cache, adapter_up_weight],
-                38 << 20,
-            )
-            pieces = lax.optimization_barrier((*across(carried, far_steps, count), token))
-            carried = jnp.concatenate(pieces[:-1], axis=0)
+            early = [query_weight, key_value_weight, down]
+            (query_w, fresh_w, down_w), token = stash(length, early)
+            pieces = across(carried, far_steps, count)
+            (carried,) = call(
+                functools.partial(join_kernel, far), [shape((far, width + LANES))], "join"
+            )(*pieces, token)
+            later = [output_weight, key_value_cache, adapter_up_weight]
+            (output_w, cache, up_w), token = stash(token, later)
             pieces = across(carried, near_steps, count)
             member, adapter = call(
                 functools.partial(member_kernel, near, far, width),
                 [shape((count, kept), jnp.int32), shape((count, 1), jnp.int32)],
                 "member",
                 [pltpu.VMEM((count, LANES), jnp.float32)],
-            )(*pieces, me, storage, specs=[vmem] * near + [smem, vmem])
+            )(*pieces, me, storage, token, specs=[vmem] * near + [smem, vmem, vmem])
             rows, low = call(
                 functools.partial(low_first_kernel, near, far), outs, "low", scratch
             )(*pieces, me, member, down_w, specs=[vmem] * near + [smem, vmem, vmem])

time: 129 us -> 133 us (1.031)
  local copies, waits for them, and re-layouts: 2.09 us -> 9.47 us
  waiting for transfers between devices: 13.3 us -> 8.97 us
    unnamed x6 -> x22, local copies, waits for them, and re-layouts: 0.76 us -> 9.47 us
    ppermute x21, waiting for transfers between devices: 13.3 us -> 8.97 us  [shift(): return lax.ppermute(block, AXIS, [(i, i ^ distance) for i in range(count)])]
    broadcast_in_dim x2 -> x0, local copies, waits for them, and re-layouts: 1.33 us -> none  [the longest x1 0.74 us: shards(): scale = attention_norm_scale[None]]
    pallas_call x19 -> x21, Pallas kernels: 21.1 us -> 20.9 us  [run(): pl.pallas_call(body, out_shape=outs, in_specs=[pl.BlockSpec(memory_space=...]
  transfers between devices with their start and end apart: 21 -> 21, of which waited for: 11 -> 8; matrix products, arithmetic and copies ran while one was open for 0% -> 0% of each run, Pallas kernels for 10% -> 9%
where the time goes in v9:
time: 133 us; the launch traced here: 132 us
  blocking collectives  70.9 us (53%)
  Pallas kernels  20.9 us (16%)
  starting transfers between devices  20.5 us (15%)
  local copies, waits for them, and re-layouts  9.47 us (7%)
  waiting for transfers between devices  8.97 us (7%)
  between operations  1.48 us (1%)
    all_to_all x4, blocking collectives, swap(): return lax.all_to_all(blocks, AXIS, split_axis=0, concat_axis=0, tiled=True)  41.1 us
    all_to_all x3, blocking collectives, chips_swap(): lax.all_to_all(blocks, AXIS, split_axis=0, concat_axis=0, axis_index_grou...  29.8 us
    pallas_call x21, Pallas kernels, run(): pl.pallas_call(body, out_shape=outs, in_specs=[pl.BlockSpec(memory_space=...  20.9 us
    ppermute x21, starting transfers between devices, shift(): return lax.ppermute(block, AXIS, [(i, i ^ distance) for i in range(count)])  20.5 us
    unnamed x22, local copies, waits for them, and re-layouts  9.47 us
    ppermute x21, waiting for transfers between devices, shift(): return lax.ppermute(block, AXIS, [(i, i ^ distance) for i in range(count)])  8.97 us
  transfers between devices with their start and end apart: 21, of which 8 were waited for; matrix products, arithmetic and copies ran while one was open for 0% of the time, Pallas kernels for 9%

profile of v9, /device:TPU:0, one launch (start us, length us, event | category | flops | bytes accessed | tf_op | source)
XLA Modules:
  0.0 132.2 jit_solution(12994719611390772649)
XLA Ops:
  3.0 5.1 %collective-permute-start.2 = (bf16[1,8320]{1,0:T(2,128)(2,1)S(1)}, bf16[1,8320]{1,0:T(2,128)(2,1)S(1)}, u32[]{:S(2)}, u32[]{:S(2)}) collective-permute-start(bf16[1,8320]{1,0:T(2,128)(2,1)S(1)} %get-tuple-element.34.refs_0_), channel_id=1, source_target_pairs={{0,12},{1,13},{2,14},{3,15},{4,8},{5,9},{6,10},{7,11},{8,4},{9,5},... | collective-permute-start | bytes 49928 | tf_op jit(solution)/shard_map/ppermute | solution.py:32
  8.7 4.6 %stash.2 = (bf16[8192,512]{1,0:T(8,128)(2,1)S(1)}, bf16[8192,128]{1,0:T(8,128)(2,1)S(1)}, bf16[2,64,8192]{2,1,0:T(8,128)(2,1)S(1)}, s32[8,128]{1,0:T(8,128)S(1)}) custom-call(s32[8,128]{1,0:T(8,128)S(1)} %get-tuple-element.35.token_ref.refs_1_, bf16[8192,512]{1,0:T(8,128)(2,1)} %refs_0_.2, bf16[8192,128]{1,0:T(8,128)(2,1)} %refs_1_.2, ...), custom_call_target="tpu_custom_call" | custom-call | flops 1048576 | bytes 12582912 | tf_op jit(solution)/shard_map/stash/pallas_call | solution.py:53
  13.3 3.3 %copy-done = bf16[8192,512]{1,0:T(8,128)(2,1)} copy-done((bf16[8192,512]{1,0:T(8,128)(2,1)}, bf16[8192,512]{1,0:T(8,128)(2,1)S(1)}, u32[]{:S(2)}) %copy-start) | copy-done | bytes 8388632
  16.6 1.3 %copy-done.2 = bf16[8192,128]{1,0:T(8,128)(2,1)} copy-done((bf16[8192,128]{1,0:T(8,128)(2,1)}, bf16[8192,128]{1,0:T(8,128)(2,1)S(1)}, u32[]{:S(2)}) %copy-start.2) | copy-done | bytes 2097176
  18.5 1.3 %collective-permute-start.4 = (bf16[4,8320]{1,0:T(4,128)(2,1)S(1)}, bf16[4,8320]{1,0:T(4,128)(2,1)S(1)}, u32[]{:S(2)}, u32[]{:S(2)}) collective-permute-start(bf16[4,8320]{1,0:T(4,128)(2,1)S(1)} %join.1.refs_0_), channel_id=1, source_target_pairs={{0,2},{1,3},{2,0},{3,1},{4,6},{5,7},{6,4},{7,5},{8,10},{9,11},{10,... | collective-permute-start | bytes 199688 | tf_op jit(solution)/shard_map/ppermute | solution.py:32
  20.0 4.6 %stash.3 = (bf16[512,8192]{1,0:T(8,128)(2,1)S(1)}, bf16[1,2,512,1024]{3,2,1,0:T(8,128)(2,1)S(1)}, bf16[32,64,512]{2,1,0:T(8,128)(2,1)S(1)}, s32[8,128]{1,0:T(8,128)S(1)}) custom-call(s32[8,128]{1,0:T(8,128)S(1)} %get-tuple-element.36.refs_4_.token_ref, bf16[512,8192]{1,0:T(8,128)(2,1)} %refs_0_.3, bf16[1,2,512,1024]{3,2,1,0:T(8,128)(2,1)} %refs_1_.3, ...), custom_call_target="tpu_custom_call" | custom-call | flops 1048576 | bytes 12582912 | tf_op jit(solution)/shard_map/stash/pallas_call | solution.py:53
  25.7 1.3 collective-permute-start.8
  27.7 1.1 collective-permute-done.8.refs_3_
  28.7 1.8 %collective-permute-done.7.refs_2_ = bf16[16,64]{1,0:T(8,128)(2,1)S(1)} collective-permute-done((bf16[16,64]{1,0:T(8,128)(2,1)S(1)}, bf16[16,64]{1,0:T(8,128)(2,1)S(1)}, u32[]{:S(2)}, u32[]{:S(2)}) %collective-permute-start.7) | collective-permute-done | bytes 2080 | tf_op jit(solution)/shard_map/ppermute | solution.py:32
  30.5 3.7 %collective-permute-start.11 = (bf16[16,64]{1,0:T(8,128)(2,1)S(1)}, bf16[16,64]{1,0:T(8,128)(2,1)S(1)}, u32[]{:S(2)}, u32[]{:S(2)}) collective-permute-start(bf16[16,64]{1,0:T(8,128)(2,1)S(1)} %sum.2.refs_0_), channel_id=1, source_target_pairs={{0,12},{1,13},{2,14},{3,15},{4,8},{5,9},{6,10},{7,11},{8,4},{9,5},... | collective-permute-start | bytes 6152 | tf_op jit(solution)/shard_map/ppermute | solution.py:32
  35.0 3.4 %copy-done.1 = bf16[8192,512]{1,0:T(8,128)(2,1)S(1)} copy-done((bf16[8192,512]{1,0:T(8,128)(2,1)S(1)}, bf16[8192,512]{1,0:T(8,128)(2,1)}, u32[]{:S(2)}) %copy-start.1) | copy-done | bytes 8388632
  38.4 1.4 %project.2 = (f32[16,512]{1,0:T(8,128)S(1)}, f32[16,128]{1,0:T(8,128)S(1)}) custom-call(bf16[16,8192]{1,0:T(8,128)(2,1)S(1)} %get-tuple-element.41.rows_ref, bf16[8192,512]{1,0:T(8,128)(2,1)S(1)} %copy-done.1, bf16[8192,128]{1,0:T(8,128)(2,1)S(1)} %copy-done.3), custom_call_target="tpu_custom_call" | custom-call | flops 167772160 | bytes 10485760 | tf_op jit(solution)/shard_map/project/pallas_call | solution.py:53
  40.4 11.7 %all_to_all.35.refs_0_ = bf16[16,8,128]{2,1,0:T(8,128)(2,1)S(1)} all-to-all(bf16[16,8,128]{2,1,0:T(8,128)(2,1)S(1)} %up.2), channel_id=1, replica_groups=mesh['groups'=2,'replica'=16] {'replica'}, dimensions={0} | all-to-all | bytes 65536 | tf_op jit(solution)/shard_map/all_to_all | solution.py:40
  52.1 0.8 attend.2
  52.9 9.1 %all_to_all.36.lines_ref = bf16[16,4,128]{2,1,0:T(4,128)(2,1)S(1)} all-to-all(bf16[16,4,128]{2,1,0:T(4,128)(2,1)S(1)} %get-tuple-element.49), channel_id=1, replica_groups=mesh['groups'=2,'replica'=16] {'replica'}, dimensions={0} | all-to-all | bytes 32768 | tf_op jit(solution)/shard_map/all_to_all | solution.py:40
  62.0 1.3 output.2
  63.3 1.4 %collective-permute-done.12.other_ref = bf16[8,8192]{1,0:T(8,128)(2,1)S(1)} collective-permute-done((bf16[8,8192]{1,0:T(8,128)(2,1)S(1)}, bf16[8,8192]{1,0:T(8,128)(2,1)S(1)}, u32[]{:S(2)}, u32[]{:S(2)}) %collective-permute-start.12) | collective-permute-done | bytes 131104 | tf_op jit(solution)/shard_map/ppermute | solution.py:32
  64.9 10.0 %all_to_all.37.parts_ref = bf16[8,8,1024]{2,1,0:T(8,128)(2,1)S(1)} all-to-all(bf16[8,8,1024]{2,1,0:T(8,128)(2,1)S(1)} %partial.2), channel_id=1, replica_groups={{0,2,4,6,8,10,12,14},{1,3,5,7,9,11,13,15},{16,18,20,22,24,26,28,30},{17..., dimensions={0} | all-to-all | bytes 262144 | tf_op jit(solution)/shard_map/all_to_all | solution.py:45
  75.2 9.8 %all_to_all.38.own_ref = bf16[8,8,1024]{2,1,0:T(8,128)(2,1)S(1)} all-to-all(bf16[8,8,1024]{2,1,0:T(8,128)(2,1)S(1)} %get-tuple-element.53), channel_id=1, replica_groups={{0,2,4,6,8,10,12,14},{1,3,5,7,9,11,13,15},{16,18,20,22,24,26,28,30},{17..., dimensions={0} | all-to-all | bytes 262144 | tf_op jit(solution)/shard_map/all_to_all | solution.py:45
  85.1 1.3 %collective-permute-done.13.other_ref = bf16[8,8,1024]{2,1,0:T(8,128)(2,1)S(1)} collective-permute-done((bf16[8,8,1024]{2,1,0:T(8,128)(2,1)S(1)}, bf16[8,8,1024]{2,1,0:T(8,128)(2,1)S(1)}, u32[]{:S(2)}, u32[]{:S(2)}) %collective-permute-start.13) | collective-permute-done | bytes 131104 | tf_op jit(solution)/shard_map/ppermute | solution.py:32
  87.2 1.8 %collective-permute-start.15 = (bf16[16,64]{1,0:T(8,128)(2,1)S(1)}, bf16[16,64]{1,0:T(8,128)(2,1)S(1)}, u32[]{:S(2)}, u32[]{:S(2)}) collective-permute-start(bf16[16,64]{1,0:T(8,128)(2,1)S(1)} %get-tuple-element.54.refs_0_), channel_id=1, source_target_pairs={{0,2},{1,3},{2,0},{3,1},{4,6},{5,7},{6,4},{7,5},{8,10},{9,11},{10,... | collective-permute-start | bytes 6152 | tf_op jit(solution)/shard_map/ppermute | solution.py:32
  89.1 1.2 collective-permute-done.16.refs_3_
  90.9 1.4 %collective-permute-start.19 = (bf16[16,64]{1,0:T(8,128)(2,1)S(1)}, bf16[16,64]{1,0:T(8,128)(2,1)S(1)}, u32[]{:S(2)}, u32[]{:S(2)}) collective-permute-start(bf16[16,64]{1,0:T(8,128)(2,1)S(1)} %sum.3.refs_0_), channel_id=1, source_target_pairs={{0,12},{1,13},{2,14},{3,15},{4,8},{5,9},{6,10},{7,11},{8,4},{9,5},... | collective-permute-start | bytes 6152 | tf_op jit(solution)/shard_map/ppermute | solution.py:32
  92.3 1.1 collective-permute-start.18
  93.4 1.9 %collective-permute-start.17 = (bf16[16,64]{1,0:T(8,128)(2,1)S(1)}, bf16[16,64]{1,0:T(8,128)(2,1)S(1)}, u32[]{:S(2)}, u32[]{:S(2)}) collective-permute-start(bf16[16,64]{1,0:T(8,128)(2,1)S(1)} %sum.3.refs_0_), channel_id=1, source_target_pairs={{0,4},{1,5},{2,6},{3,7},{4,0},{5,1},{6,2},{7,3},{8,12},{9,13},{10,... | collective-permute-start | bytes 6152 | tf_op jit(solution)/shard_map/ppermute | solution.py:32
  95.3 1.5 %project.3 = (f32[16,512]{1,0:T(8,128)S(1)}, f32[16,128]{1,0:T(8,128)S(1)}) custom-call(bf16[16,8192]{1,0:T(8,128)(2,1)S(1)} %get-tuple-element.55.rows_ref, bf16[8192,512]{1,0:T(8,128)(2,1)S(1)} %bitcast.6, bf16[8192,128]{1,0:T(8,128)(2,1)S(1)} %copy-done.3), custom_call_target="tpu_custom_call" | custom-call | flops 167772160 | bytes 10485760 | tf_op jit(solution)/shard_map/project/pallas_call | solution.py:53
  97.5 11.2 %all_to_all.39.refs_0_ = bf16[16,8,128]{2,1,0:T(8,128)(2,1)S(1)} all-to-all(bf16[16,8,128]{2,1,0:T(8,128)(2,1)S(1)} %up.3), channel_id=1, replica_groups=mesh['groups'=2,'replica'=16] {'replica'}, dimensions={0} | all-to-all | bytes 65536 | tf_op jit(solution)/shard_map/all_to_all | solution.py:40
  108.8 0.8 attend.3
  109.6 9.1 %all_to_all.40.lines_ref = bf16[16,4,128]{2,1,0:T(4,128)(2,1)S(1)} all-to-all(bf16[16,4,128]{2,1,0:T(4,128)(2,1)S(1)} %attend.3), channel_id=1, replica_groups=mesh['groups'=2,'replica'=16] {'replica'}, dimensions={0} | all-to-all | bytes 32768 | tf_op jit(solution)/shard_map/all_to_all | solution.py:40
  118.7 1.3 output.3
  120.0 1.4 %collective-permute-done.20.other_ref = bf16[8,8192]{1,0:T(8,128)(2,1)S(1)} collective-permute-done((bf16[8,8192]{1,0:T(8,128)(2,1)S(1)}, bf16[8,8192]{1,0:T(8,128)(2,1)S(1)}, u32[]{:S(2)}, u32[]{:S(2)}) %collective-permute-start.20) | collective-permute-done | bytes 131104 | tf_op jit(solution)/shard_map/ppermute | solution.py:32
  121.5 10.0 %all_to_all.41.parts_ref = bf16[8,8,1024]{2,1,0:T(8,128)(2,1)S(1)} all-to-all(bf16[8,8,1024]{2,1,0:T(8,128)(2,1)S(1)} %partial.3), channel_id=1, replica_groups={{0,2,4,6,8,10,12,14},{1,3,5,7,9,11,13,15},{16,18,20,22,24,26,28,30},{17..., dimensions={0} | all-to-all | bytes 262144 | tf_op jit(solution)/shard_map/all_to_all | solution.py:45
  (61 shorter events, 9.8 us)
Async XLA Ops:
  1.3 0.7 copy-start.4
  2.0 0.8 copy-start.6
  3.0 15.0 %collective-permute-start.2 = (bf16[1,8320]{1,0:T(2,128)(2,1)S(1)}, bf16[1,8320]{1,0:T(2,128)(2,1)S(1)}, u32[]{:S(2)}, u32[]{:S(2)}) collective-permute-start(bf16[1,8320]{1,0:T(2,128)(2,1)S(1)} %get-tuple-element.34.refs_0_), channel_id=1, source_target_pairs={{0,12},{1,13},{2,14},{3,15},{4,8},{5,9},{6,10},{7,11},{8,4},{9,5},... | collective-permute-start | bytes 49928 | tf_op jit(solution)/shard_map/ppermute | solution.py:32
  8.1 9.9 %collective-permute-start.1 = (bf16[1,8320]{1,0:T(2,128)(2,1)S(1)}, bf16[1,8320]{1,0:T(2,128)(2,1)S(1)}, u32[]{:S(2)}, u32[]{:S(2)}) collective-permute-start(bf16[1,8320]{1,0:T(2,128)(2,1)S(1)} %get-tuple-element.34.refs_0_), channel_id=1, source_target_pairs={{0,8},{1,9},{2,10},{3,11},{4,12},{5,13},{6,14},{7,15},{8,0},{9,1},... | collective-permute-start | bytes 49928 | tf_op jit(solution)/shard_map/ppermute | solution.py:32
  8.1 9.9 %collective-permute-start = (bf16[1,8320]{1,0:T(2,128)(2,1)S(1)}, bf16[1,8320]{1,0:T(2,128)(2,1)S(1)}, u32[]{:S(2)}, u32[]{:S(2)}) collective-permute-start(bf16[1,8320]{1,0:T(2,128)(2,1)S(1)} %get-tuple-element.34.refs_0_), channel_id=1, source_target_pairs={{0,4},{1,5},{2,6},{3,7},{4,0},{5,1},{6,2},{7,3},{8,12},{9,13},{10,... | collective-permute-start | bytes 49928 | tf_op jit(solution)/shard_map/ppermute | solution.py:32
  13.3 3.3 %copy-start = (bf16[8192,512]{1,0:T(8,128)(2,1)}, bf16[8192,512]{1,0:T(8,128)(2,1)S(1)}, u32[]{:S(2)}) copy-start(bf16[8192,512]{1,0:T(8,128)(2,1)S(1)} %get-tuple-element.42.query_w) | copy-start | bytes 25165828
  16.6 1.3 %copy-start.2 = (bf16[8192,128]{1,0:T(8,128)(2,1)}, bf16[8192,128]{1,0:T(8,128)(2,1)S(1)}, u32[]{:S(2)}) copy-start(bf16[8192,128]{1,0:T(8,128)(2,1)S(1)} %get-tuple-element.43.fresh_w) | copy-start | bytes 6291460
  18.0 6.6 %collective-permute-start.5 = (bf16[4,8320]{1,0:T(4,128)(2,1)S(1)}, bf16[4,8320]{1,0:T(4,128)(2,1)S(1)}, u32[]{:S(2)}, u32[]{:S(2)}) collective-permute-start(bf16[4,8320]{1,0:T(4,128)(2,1)S(1)} %join.1.refs_0_), channel_id=1, source_target_pairs={{0,3},{1,2},{2,1},{3,0},{4,7},{5,6},{6,5},{7,4},{8,11},{9,10},{10,... | collective-permute-start | bytes 199688 | tf_op jit(solution)/shard_map/ppermute | solution.py:32
  18.5 6.2 %collective-permute-start.4 = (bf16[4,8320]{1,0:T(4,128)(2,1)S(1)}, bf16[4,8320]{1,0:T(4,128)(2,1)S(1)}, u32[]{:S(2)}, u32[]{:S(2)}) collective-permute-start(bf16[4,8320]{1,0:T(4,128)(2,1)S(1)} %join.1.refs_0_), channel_id=1, source_target_pairs={{0,2},{1,3},{2,0},{3,1},{4,6},{5,7},{6,4},{7,5},{8,10},{9,11},{10,... | collective-permute-start | bytes 199688 | tf_op jit(solution)/shard_map/ppermute | solution.py:32
  19.8 4.8 %collective-permute-start.3 = (bf16[4,8320]{1,0:T(4,128)(2,1)S(1)}, bf16[4,8320]{1,0:T(4,128)(2,1)S(1)}, u32[]{:S(2)}, u32[]{:S(2)}) collective-permute-start(bf16[4,8320]{1,0:T(4,128)(2,1)S(1)} %join.1.refs_0_), channel_id=1, source_target_pairs={{0,1},{1,0},{2,3},{3,2},{4,5},{5,4},{6,7},{7,6},{8,9},{9,8},{10,11... | collective-permute-start | bytes 199688 | tf_op jit(solution)/shard_map/ppermute | solution.py:32
  20.0 4.7 %copy-start.8 = (s32[32]{0:T(128)S(1)}, s32[32]{0:T(128)}, u32[]{:S(2)}) copy-start(s32[32]{0:T(128)} %param.19) | copy-start | bytes 388
  24.6 10.4 %copy-start.3 = (bf16[8192,128]{1,0:T(8,128)(2,1)S(1)}, bf16[8192,128]{1,0:T(8,128)(2,1)}, u32[]{:S(2)}) copy-start(bf16[8192,128]{1,0:T(8,128)(2,1)} %copy-done.2) | copy-start | bytes 6291460
  25.7 3.1 %collective-permute-start.8 = (bf16[16,64]{1,0:T(8,128)(2,1)S(1)}, bf16[16,64]{1,0:T(8,128)(2,1)S(1)}, u32[]{:S(2)}, u32[]{:S(2)}) collective-permute-start(bf16[16,64]{1,0:T(8,128)(2,1)S(1)} %get-tuple-element.40.refs_0_), channel_id=1, source_target_pairs={{0,3},{1,2},{2,1},{3,0},{4,7},{5,6},{6,5},{7,4},{8,11},{9,10},{10,... | collective-permute-start | bytes 6152 | tf_op jit(solution)/shard_map/ppermute | solution.py:32
  26.9 3.6 %collective-permute-start.7 = (bf16[16,64]{1,0:T(8,128)(2,1)S(1)}, bf16[16,64]{1,0:T(8,128)(2,1)S(1)}, u32[]{:S(2)}, u32[]{:S(2)}) collective-permute-start(bf16[16,64]{1,0:T(8,128)(2,1)S(1)} %get-tuple-element.40.refs_0_), channel_id=1, source_target_pairs={{0,2},{1,3},{2,0},{3,1},{4,6},{5,7},{6,4},{7,5},{8,10},{9,11},{10,... | collective-permute-start | bytes 6152 | tf_op jit(solution)/shard_map/ppermute | solution.py:32
  27.7 2.9 %collective-permute-start.6 = (bf16[16,64]{1,0:T(8,128)(2,1)S(1)}, bf16[16,64]{1,0:T(8,128)(2,1)S(1)}, u32[]{:S(2)}, u32[]{:S(2)}) collective-permute-start(bf16[16,64]{1,0:T(8,128)(2,1)S(1)} %get-tuple-element.40.refs_0_), channel_id=1, source_target_pairs={{0,1},{1,0},{2,3},{3,2},{4,5},{5,4},{6,7},{7,6},{8,9},{9,8},{10,11... | collective-permute-start | bytes 6152 | tf_op jit(solution)/shard_map/ppermute | solution.py:32
  30.5 9.3 %collective-permute-start.11 = (bf16[16,64]{1,0:T(8,128)(2,1)S(1)}, bf16[16,64]{1,0:T(8,128)(2,1)S(1)}, u32[]{:S(2)}, u32[]{:S(2)}) collective-permute-start(bf16[16,64]{1,0:T(8,128)(2,1)S(1)} %sum.2.refs_0_), channel_id=1, source_target_pairs={{0,12},{1,13},{2,14},{3,15},{4,8},{5,9},{6,10},{7,11},{8,4},{9,5},... | collective-permute-start | bytes 6152 | tf_op jit(solution)/shard_map/ppermute | solution.py:32
  34.2 5.6 %collective-permute-start.10 = (bf16[16,64]{1,0:T(8,128)(2,1)S(1)}, bf16[16,64]{1,0:T(8,128)(2,1)S(1)}, u32[]{:S(2)}, u32[]{:S(2)}) collective-permute-start(bf16[16,64]{1,0:T(8,128)(2,1)S(1)} %sum.2.refs_0_), channel_id=1, source_target_pairs={{0,8},{1,9},{2,10},{3,11},{4,12},{5,13},{6,14},{7,15},{8,0},{9,1},... | collective-permute-start | bytes 6152 | tf_op jit(solution)/shard_map/ppermute | solution.py:32
  34.2 5.7 %collective-permute-start.9 = (bf16[16,64]{1,0:T(8,128)(2,1)S(1)}, bf16[16,64]{1,0:T(8,128)(2,1)S(1)}, u32[]{:S(2)}, u32[]{:S(2)}) collective-permute-start(bf16[16,64]{1,0:T(8,128)(2,1)S(1)} %sum.2.refs_0_), channel_id=1, source_target_pairs={{0,4},{1,5},{2,6},{3,7},{4,0},{5,1},{6,2},{7,3},{8,12},{9,13},{10,... | collective-permute-start | bytes 6152 | tf_op jit(solution)/shard_map/ppermute | solution.py:32
  35.0 3.4 %copy-start.1 = (bf16[8192,512]{1,0:T(8,128)(2,1)S(1)}, bf16[8192,512]{1,0:T(8,128)(2,1)}, u32[]{:S(2)}) copy-start(bf16[8192,512]{1,0:T(8,128)(2,1)} %copy-done) | copy-start | bytes 25165828
  39.9 55.4 %slice-start = ((s8[8388608]{0:T(1024)(128)(4,1)}), s8[4194304]{0:T(1024)(128)(4,1)S(1)}, s32[]{:S(2)}) async-start(s8[8388608]{0:T(1024)(128)(4,1)} %bitcast.5), calls=%async_computation.7 | async-start | bytes 8388608
  62.0 12.8 %copy-start.5 = (bf16[8192]{0:T(1024)(128)(2,1)S(1)}, bf16[8192]{0:T(1024)(128)(2,1)}, u32[]{:S(2)}) copy-start(bf16[8192]{0:T(1024)(128)(2,1)} %param.12) | copy-start | bytes 49156
  62.0 12.8 %copy-start.7 = (bf16[1,8192]{1,0:T(2,128)(2,1)S(1)}, bf16[1,8192]{1,0:T(2,128)(2,1)}, u32[]{:S(2)}) copy-start(bf16[1,8192]{1,0:T(2,128)(2,1)} %hidden_ref.3) | copy-start | bytes 49156
  62.0 33.3 %slice-start.1 = ((s8[8388608]{0:T(1024)(128)(4,1)}), s8[4194304]{0:T(1024)(128)(4,1)S(1)}, s32[]{:S(2)}) async-start(s8[8388608]{0:T(1024)(128)(4,1)} %bitcast.5), calls=%async_computation.8 | async-start | bytes 8388608
  63.3 1.4 %collective-permute-start.12 = (bf16[8,8192]{1,0:T(8,128)(2,1)S(1)}, bf16[8,8192]{1,0:T(8,128)(2,1)S(1)}, u32[]{:S(2)}, u32[]{:S(2)}) collective-permute-start(bf16[8,8192]{1,0:T(8,128)(2,1)S(1)} %get-tuple-element.52), channel_id=1, source_target_pairs={{0,1},{1,0},{2,3},{3,2},{4,5},{5,4},{6,7},{7,6},{8,9},{9,8},{10,11... | collective-permute-start | bytes 393224 | tf_op jit(solution)/shard_map/ppermute | solution.py:32
  85.1 1.3 %collective-permute-start.13 = (bf16[8,8,1024]{2,1,0:T(8,128)(2,1)S(1)}, bf16[8,8,1024]{2,1,0:T(8,128)(2,1)S(1)}, u32[]{:S(2)}, u32[]{:S(2)}) collective-permute-start(bf16[8,8,1024]{2,1,0:T(8,128)(2,1)S(1)} %all_to_all.38.own_ref), channel_id=1, source_target_pairs={{0,1},{1,0},{2,3},{3,2},{4,5},{5,4},{6,7},{7,6},{8,9},{9,8},{10,11... | collective-permute-start | bytes 393224 | tf_op jit(solution)/shard_map/ppermute | solution.py:32
  87.2 3.1 %collective-permute-start.16 = (bf16[16,64]{1,0:T(8,128)(2,1)S(1)}, bf16[16,64]{1,0:T(8,128)(2,1)S(1)}, u32[]{:S(2)}, u32[]{:S(2)}) collective-permute-start(bf16[16,64]{1,0:T(8,128)(2,1)S(1)} %get-tuple-element.54.refs_0_), channel_id=1, source_target_pairs={{0,3},{1,2},{2,1},{3,0},{4,7},{5,6},{6,5},{7,4},{8,11},{9,10},{10,... | collective-permute-start | bytes 6152 | tf_op jit(solution)/shard_map/ppermute | solution.py:32
  87.2 3.7 %collective-permute-start.15 = (bf16[16,64]{1,0:T(8,128)(2,1)S(1)}, bf16[16,64]{1,0:T(8,128)(2,1)S(1)}, u32[]{:S(2)}, u32[]{:S(2)}) collective-permute-start(bf16[16,64]{1,0:T(8,128)(2,1)S(1)} %get-tuple-element.54.refs_0_), channel_id=1, source_target_pairs={{0,2},{1,3},{2,0},{3,1},{4,6},{5,7},{6,4},{7,5},{8,10},{9,11},{10,... | collective-permute-start | bytes 6152 | tf_op jit(solution)/shard_map/ppermute | solution.py:32
  89.0 1.9 %collective-permute-start.14 = (bf16[16,64]{1,0:T(8,128)(2,1)S(1)}, bf16[16,64]{1,0:T(8,128)(2,1)S(1)}, u32[]{:S(2)}, u32[]{:S(2)}) collective-permute-start(bf16[16,64]{1,0:T(8,128)(2,1)S(1)} %get-tuple-element.54.refs_0_), channel_id=1, source_target_pairs={{0,1},{1,0},{2,3},{3,2},{4,5},{5,4},{6,7},{7,6},{8,9},{9,8},{10,11... | collective-permute-start | bytes 6152 | tf_op jit(solution)/shard_map/ppermute | solution.py:32
  90.9 5.9 %collective-permute-start.19 = (bf16[16,64]{1,0:T(8,128)(2,1)S(1)}, bf16[16,64]{1,0:T(8,128)(2,1)S(1)}, u32[]{:S(2)}, u32[]{:S(2)}) collective-permute-start(bf16[16,64]{1,0:T(8,128)(2,1)S(1)} %sum.3.refs_0_), channel_id=1, source_target_pairs={{0,12},{1,13},{2,14},{3,15},{4,8},{5,9},{6,10},{7,11},{8,4},{9,5},... | collective-permute-start | bytes 6152 | tf_op jit(solution)/shard_map/ppermute | solution.py:32
  92.3 4.5 %collective-permute-start.18 = (bf16[16,64]{1,0:T(8,128)(2,1)S(1)}, bf16[16,64]{1,0:T(8,128)(2,1)S(1)}, u32[]{:S(2)}, u32[]{:S(2)}) collective-permute-start(bf16[16,64]{1,0:T(8,128)(2,1)S(1)} %sum.3.refs_0_), channel_id=1, source_target_pairs={{0,8},{1,9},{2,10},{3,11},{4,12},{5,13},{6,14},{7,15},{8,0},{9,1},... | collective-permute-start | bytes 6152 | tf_op jit(solution)/shard_map/ppermute | solution.py:32
  93.4 3.6 %collective-permute-start.17 = (bf16[16,64]{1,0:T(8,128)(2,1)S(1)}, bf16[16,64]{1,0:T(8,128)(2,1)S(1)}, u32[]{:S(2)}, u32[]{:S(2)}) collective-permute-start(bf16[16,64]{1,0:T(8,128)(2,1)S(1)} %sum.3.refs_0_), channel_id=1, source_target_pairs={{0,4},{1,5},{2,6},{3,7},{4,0},{5,1},{6,2},{7,3},{8,12},{9,13},{10,... | collective-permute-start | bytes 6152 | tf_op jit(solution)/shard_map/ppermute | solution.py:32
  120.0 1.4 %collective-permute-start.20 = (bf16[8,8192]{1,0:T(8,128)(2,1)S(1)}, bf16[8,8192]{1,0:T(8,128)(2,1)S(1)}, u32[]{:S(2)}, u32[]{:S(2)}) collective-permute-start(bf16[8,8192]{1,0:T(8,128)(2,1)S(1)} %get-tuple-element.61), channel_id=1, source_target_pairs={{0,1},{1,0},{2,3},{3,2},{4,5},{5,4},{6,7},{7,6},{8,9},{9,8},{10,11... | collective-permute-start | bytes 393224 | tf_op jit(solution)/shard_map/ppermute | solution.py:32

commit v10 on v9

--- a/solution.py
+++ b/solution.py
@@ -93,7 +93,7 @@
             out_ref[k, i : i + 1, :wide] = row[:, i * wide : (i + 1) * wide].astype(out_ref.dtype)
 
 
-def first_kernel(hidden_ref, scale_ref, adapter_ref, length_ref, out_ref, length_out):
+def first_kernel(hidden_ref, scale_ref, adapter_ref, length_ref, _, out_ref, length_out):
     length_out[...] = jnp.full(length_out.shape, length_ref[0], jnp.int32)
     width = hidden_ref.shape[1]
     hidden = hidden_ref[...].astype(jnp.float32)
@@ -408,7 +408,14 @@
     hidden = hidden_state_input
     carried, length = call(
         first_kernel, [shape((1, width + LANES)), shape((8, LANES), jnp.int32)], "first"
-    )(hidden, scale, row_adapter_index, cache_length_per_row, specs=[vmem, vmem, smem, smem])
+    )(
+        hidden,
+        scale,
+        row_adapter_index,
+        cache_length_per_row,
+        me,
+        specs=[vmem, vmem, smem, smem, smem],
+    )
     past = ()
     for step in range(STEPS):
         first, last = step == 0, step == STEPS - 1

time: 133 us -> 125 us (0.940)
  local copies, waits for them, and re-layouts: 9.47 us -> 1.48 us
  waiting for transfers between devices: 8.97 us -> 11.2 us
  blocking collectives: 70.9 us -> 69.2 us
    unnamed x22 -> x10, local copies, waits for them, and re-layouts: 9.47 us -> 1.48 us
    ppermute x21, waiting for transfers between devices: 8.97 us -> 11.2 us  [shift(): return lax.ppermute(block, AXIS, [(i, i ^ distance) for i in range(count)])]
    all_to_all x4, blocking collectives: 41.1 us -> 39.4 us  [swap(): return lax.all_to_all(blocks, AXIS, split_axis=0, concat_axis=0, tiled=True)]
  transfers between devices with their start and end apart: 21 -> 21, of which waited for: 8 -> 9; matrix products, arithmetic and copies ran while one was open for 0% -> 0% of each run, Pallas kernels for 9% -> 10%
where the time goes in v10:
time: 125 us
  blocking collectives  69.2 us (55%)
  Pallas kernels  20.9 us (17%)
  starting transfers between devices  20.5 us (16%)
  waiting for transfers between devices  11.2 us (9%)
  local copies, waits for them, and re-layouts  1.48 us (1%)
  between operations  1.46 us (1%)
    all_to_all x4, blocking collectives, swap(): return lax.all_to_all(blocks, AXIS, split_axis=0, concat_axis=0, tiled=True)  39.4 us
    all_to_all x3, blocking collectives, chips_swap(): lax.all_to_all(blocks, AXIS, split_axis=0, concat_axis=0, axis_index_grou...  29.8 us
    pallas_call x21, Pallas kernels, run(): pl.pallas_call(body, out_shape=outs, in_specs=[pl.BlockSpec(memory_space=...  20.9 us
    ppermute x21, starting transfers between devices, shift(): return lax.ppermute(block, AXIS, [(i, i ^ distance) for i in range(count)])  20.5 us
    ppermute x21, waiting for transfers between devices, shift(): return lax.ppermute(block, AXIS, [(i, i ^ distance) for i in range(count)])  11.2 us
  transfers between devices with their start and end apart: 21, of which 9 were waited for; matrix products, arithmetic and copies ran while one was open for 0% of the time, Pallas kernels for 10%

profile of v10, /device:TPU:0, one launch (start us, length us, event | category | flops | bytes accessed | tf_op | source)
XLA Modules:
  0.0 124.7 jit_solution(10518572914170546136)
XLA Ops:
  3.0 5.1 %collective-permute-start.2 = (bf16[1,8320]{1,0:T(2,128)(2,1)S(1)}, bf16[1,8320]{1,0:T(2,128)(2,1)S(1)}, u32[]{:S(2)}, u32[]{:S(2)}) collective-permute-start(bf16[1,8320]{1,0:T(2,128)(2,1)S(1)} %get-tuple-element.34.refs_0_), channel_id=1, source_target_pairs={{0,12},{1,13},{2,14},{3,15},{4,8},{5,9},{6,10},{7,11},{8,4},{9,5},... | collective-permute-start | bytes 49928 | tf_op jit(solution)/shard_map/ppermute | solution.py:32
  8.7 4.6 %stash.2 = (bf16[8192,512]{1,0:T(8,128)(2,1)S(1)}, bf16[8192,128]{1,0:T(8,128)(2,1)S(1)}, bf16[2,64,8192]{2,1,0:T(8,128)(2,1)S(1)}, s32[8,128]{1,0:T(8,128)S(1)}) custom-call(s32[8,128]{1,0:T(8,128)S(1)} %get-tuple-element.35.token_ref.refs_1_, bf16[8192,512]{1,0:T(8,128)(2,1)} %refs_0_.2, bf16[8192,128]{1,0:T(8,128)(2,1)} %refs_1_.2, ...), custom_call_target="tpu_custom_call" | custom-call | flops 1048576 | bytes 12582912 | tf_op jit(solution)/shard_map/stash/pallas_call | solution.py:53
  13.9 1.3 %collective-permute-start.4 = (bf16[4,8320]{1,0:T(4,128)(2,1)S(1)}, bf16[4,8320]{1,0:T(4,128)(2,1)S(1)}, u32[]{:S(2)}, u32[]{:S(2)}) collective-permute-start(bf16[4,8320]{1,0:T(4,128)(2,1)S(1)} %join.1.refs_0_), channel_id=1, source_target_pairs={{0,2},{1,3},{2,0},{3,1},{4,6},{5,7},{6,4},{7,5},{8,10},{9,11},{10,... | collective-permute-start | bytes 199688 | tf_op jit(solution)/shard_map/ppermute | solution.py:32
  15.4 4.6 %stash.3 = (bf16[512,8192]{1,0:T(8,128)(2,1)S(1)}, bf16[1,2,512,1024]{3,2,1,0:T(8,128)(2,1)S(1)}, bf16[32,64,512]{2,1,0:T(8,128)(2,1)S(1)}, s32[8,128]{1,0:T(8,128)S(1)}) custom-call(s32[8,128]{1,0:T(8,128)S(1)} %get-tuple-element.36.refs_4_.token_ref, bf16[512,8192]{1,0:T(8,128)(2,1)} %refs_0_.3, bf16[1,2,512,1024]{3,2,1,0:T(8,128)(2,1)} %refs_1_.3, ...), custom_call_target="tpu_custom_call" | custom-call | flops 1048576 | bytes 12582912 | tf_op jit(solution)/shard_map/stash/pallas_call | solution.py:53
  21.1 1.3 %collective-permute-start.8 = (bf16[16,64]{1,0:T(8,128)(2,1)S(1)}, bf16[16,64]{1,0:T(8,128)(2,1)S(1)}, u32[]{:S(2)}, u32[]{:S(2)}) collective-permute-start(bf16[16,64]{1,0:T(8,128)(2,1)S(1)} %get-tuple-element.40.refs_0_), channel_id=1, source_target_pairs={{0,3},{1,2},{2,1},{3,0},{4,7},{5,6},{6,5},{7,4},{8,11},{9,10},{10,... | collective-permute-start | bytes 6152 | tf_op jit(solution)/shard_map/ppermute | solution.py:32
  23.1 1.1 collective-permute-done.8.refs_3_
  24.1 1.8 %collective-permute-done.7.refs_2_ = bf16[16,64]{1,0:T(8,128)(2,1)S(1)} collective-permute-done((bf16[16,64]{1,0:T(8,128)(2,1)S(1)}, bf16[16,64]{1,0:T(8,128)(2,1)S(1)}, u32[]{:S(2)}, u32[]{:S(2)}) %collective-permute-start.7) | collective-permute-done | bytes 2080 | tf_op jit(solution)/shard_map/ppermute | solution.py:32
  25.9 3.7 %collective-permute-start.11 = (bf16[16,64]{1,0:T(8,128)(2,1)S(1)}, bf16[16,64]{1,0:T(8,128)(2,1)S(1)}, u32[]{:S(2)}, u32[]{:S(2)}) collective-permute-start(bf16[16,64]{1,0:T(8,128)(2,1)S(1)} %sum.2.refs_0_), channel_id=1, source_target_pairs={{0,12},{1,13},{2,14},{3,15},{4,8},{5,9},{6,10},{7,11},{8,4},{9,5},... | collective-permute-start | bytes 6152 | tf_op jit(solution)/shard_map/ppermute | solution.py:32
  29.6 0.8 collective-permute-start.9
  30.4 1.5 %project.2 = (f32[16,512]{1,0:T(8,128)S(1)}, f32[16,128]{1,0:T(8,128)S(1)}) custom-call(bf16[16,8192]{1,0:T(8,128)(2,1)S(1)} %get-tuple-element.41.rows_ref, bf16[8192,512]{1,0:T(8,128)(2,1)S(1)} %get-tuple-element.42.query_w, bf16[8192,128]{1,0:T(8,128)(2,1)S(1)} %get-tuple-element.43.fresh_w), custom_call_target="tpu_custom_call" | custom-call | flops 167772160 | bytes 10485760 | tf_op jit(solution)/shard_map/project/pallas_call | solution.py:53
  31.9 2.3 %collective-permute-done.10.refs_2_ = bf16[16,64]{1,0:T(8,128)(2,1)S(1)} collective-permute-done((bf16[16,64]{1,0:T(8,128)(2,1)S(1)}, bf16[16,64]{1,0:T(8,128)(2,1)S(1)}, u32[]{:S(2)}, u32[]{:S(2)}) %collective-permute-start.10) | collective-permute-done | bytes 2080 | tf_op jit(solution)/shard_map/ppermute | solution.py:32
  34.6 10.0 %all_to_all.35.refs_0_ = bf16[16,8,128]{2,1,0:T(8,128)(2,1)S(1)} all-to-all(bf16[16,8,128]{2,1,0:T(8,128)(2,1)S(1)} %up.2), channel_id=1, replica_groups=mesh['groups'=2,'replica'=16] {'replica'}, dimensions={0} | all-to-all | bytes 65536 | tf_op jit(solution)/shard_map/all_to_all | solution.py:40
  44.7 0.8 attend.2
  45.5 9.1 %all_to_all.36.lines_ref = bf16[16,4,128]{2,1,0:T(4,128)(2,1)S(1)} all-to-all(bf16[16,4,128]{2,1,0:T(4,128)(2,1)S(1)} %get-tuple-element.49), channel_id=1, replica_groups=mesh['groups'=2,'replica'=16] {'replica'}, dimensions={0} | all-to-all | bytes 32768 | tf_op jit(solution)/shard_map/all_to_all | solution.py:40
  54.6 1.3 %output.2 = (f32[8,8192]{1,0:T(8,128)S(1)}, bf16[8,8192]{1,0:T(8,128)(2,1)S(1)}) custom-call(bf16[16,4,128]{2,1,0:T(4,128)(2,1)S(1)} %all_to_all.36.lines_ref, s32[1]{0:T(128)} %bitcast.1._.refs_4_.me_ref, bf16[512,8192]{1,0:T(8,128)(2,1)S(1)} %get-tuple-element.50.weight_ref), custom_call_target="tpu_custom_call" | custom-call | flops 134217728 | bytes 8388608 | tf_op jit(solution)/shard_map/output/pallas_call | solution.py:53
  55.9 1.4 %collective-permute-done.12.other_ref = bf16[8,8192]{1,0:T(8,128)(2,1)S(1)} collective-permute-done((bf16[8,8192]{1,0:T(8,128)(2,1)S(1)}, bf16[8,8192]{1,0:T(8,128)(2,1)S(1)}, u32[]{:S(2)}, u32[]{:S(2)}) %collective-permute-start.12) | collective-permute-done | bytes 131104 | tf_op jit(solution)/shard_map/ppermute | solution.py:32
  57.4 10.0 %all_to_all.37.parts_ref = bf16[8,8,1024]{2,1,0:T(8,128)(2,1)S(1)} all-to-all(bf16[8,8,1024]{2,1,0:T(8,128)(2,1)S(1)} %partial.2), channel_id=1, replica_groups={{0,2,4,6,8,10,12,14},{1,3,5,7,9,11,13,15},{16,18,20,22,24,26,28,30},{17..., dimensions={0} | all-to-all | bytes 262144 | tf_op jit(solution)/shard_map/all_to_all | solution.py:45
  67.7 9.8 %all_to_all.38.own_ref = bf16[8,8,1024]{2,1,0:T(8,128)(2,1)S(1)} all-to-all(bf16[8,8,1024]{2,1,0:T(8,128)(2,1)S(1)} %get-tuple-element.53), channel_id=1, replica_groups={{0,2,4,6,8,10,12,14},{1,3,5,7,9,11,13,15},{16,18,20,22,24,26,28,30},{17..., dimensions={0} | all-to-all | bytes 262144 | tf_op jit(solution)/shard_map/all_to_all | solution.py:45
  77.6 1.3 %collective-permute-done.13.other_ref = bf16[8,8,1024]{2,1,0:T(8,128)(2,1)S(1)} collective-permute-done((bf16[8,8,1024]{2,1,0:T(8,128)(2,1)S(1)}, bf16[8,8,1024]{2,1,0:T(8,128)(2,1)S(1)}, u32[]{:S(2)}, u32[]{:S(2)}) %collective-permute-start.13) | collective-permute-done | bytes 131104 | tf_op jit(solution)/shard_map/ppermute | solution.py:32
  78.9 0.8 low.3
  79.7 1.8 %collective-permute-start.15 = (bf16[16,64]{1,0:T(8,128)(2,1)S(1)}, bf16[16,64]{1,0:T(8,128)(2,1)S(1)}, u32[]{:S(2)}, u32[]{:S(2)}) collective-permute-start(bf16[16,64]{1,0:T(8,128)(2,1)S(1)} %get-tuple-element.54.refs_0_), channel_id=1, source_target_pairs={{0,2},{1,3},{2,0},{3,1},{4,6},{5,7},{6,4},{7,5},{8,10},{9,11},{10,... | collective-permute-start | bytes 6152 | tf_op jit(solution)/shard_map/ppermute | solution.py:32
  81.6 1.2 collective-permute-done.16.refs_3_
  83.4 1.4 %collective-permute-start.19 = (bf16[16,64]{1,0:T(8,128)(2,1)S(1)}, bf16[16,64]{1,0:T(8,128)(2,1)S(1)}, u32[]{:S(2)}, u32[]{:S(2)}) collective-permute-start(bf16[16,64]{1,0:T(8,128)(2,1)S(1)} %sum.3.refs_0_), channel_id=1, source_target_pairs={{0,12},{1,13},{2,14},{3,15},{4,8},{5,9},{6,10},{7,11},{8,4},{9,5},... | collective-permute-start | bytes 6152 | tf_op jit(solution)/shard_map/ppermute | solution.py:32
  84.8 1.1 collective-permute-start.18
  85.9 1.9 %collective-permute-start.17 = (bf16[16,64]{1,0:T(8,128)(2,1)S(1)}, bf16[16,64]{1,0:T(8,128)(2,1)S(1)}, u32[]{:S(2)}, u32[]{:S(2)}) collective-permute-start(bf16[16,64]{1,0:T(8,128)(2,1)S(1)} %sum.3.refs_0_), channel_id=1, source_target_pairs={{0,4},{1,5},{2,6},{3,7},{4,0},{5,1},{6,2},{7,3},{8,12},{9,13},{10,... | collective-permute-start | bytes 6152 | tf_op jit(solution)/shard_map/ppermute | solution.py:32
  87.8 1.5 %project.3 = (f32[16,512]{1,0:T(8,128)S(1)}, f32[16,128]{1,0:T(8,128)S(1)}) custom-call(bf16[16,8192]{1,0:T(8,128)(2,1)S(1)} %get-tuple-element.55.rows_ref, bf16[8192,512]{1,0:T(8,128)(2,1)S(1)} %get-tuple-element.42.query_w, bf16[8192,128]{1,0:T(8,128)(2,1)S(1)} %get-tuple-element.43.fresh_w), custom_call_target="tpu_custom_call" | custom-call | flops 167772160 | bytes 10485760 | tf_op jit(solution)/shard_map/project/pallas_call | solution.py:53
  90.1 11.2 %all_to_all.39.refs_0_ = bf16[16,8,128]{2,1,0:T(8,128)(2,1)S(1)} all-to-all(bf16[16,8,128]{2,1,0:T(8,128)(2,1)S(1)} %up.3), channel_id=1, replica_groups=mesh['groups'=2,'replica'=16] {'replica'}, dimensions={0} | all-to-all | bytes 65536 | tf_op jit(solution)/shard_map/all_to_all | solution.py:40
  101.3 0.8 attend.3
  102.1 9.1 %all_to_all.40.lines_ref = bf16[16,4,128]{2,1,0:T(4,128)(2,1)S(1)} all-to-all(bf16[16,4,128]{2,1,0:T(4,128)(2,1)S(1)} %attend.3), channel_id=1, replica_groups=mesh['groups'=2,'replica'=16] {'replica'}, dimensions={0} | all-to-all | bytes 32768 | tf_op jit(solution)/shard_map/all_to_all | solution.py:40
  111.2 1.3 %output.3 = (f32[8,8192]{1,0:T(8,128)S(1)}, bf16[8,8192]{1,0:T(8,128)(2,1)S(1)}) custom-call(bf16[16,4,128]{2,1,0:T(4,128)(2,1)S(1)} %all_to_all.40.lines_ref, s32[1]{0:T(128)} %bitcast.1._.refs_4_.me_ref, bf16[512,8192]{1,0:T(8,128)(2,1)S(1)} %get-tuple-element.50.weight_ref), custom_call_target="tpu_custom_call" | custom-call | flops 134217728 | bytes 8388608 | tf_op jit(solution)/shard_map/output/pallas_call | solution.py:53
  112.5 1.4 %collective-permute-done.20.other_ref = bf16[8,8192]{1,0:T(8,128)(2,1)S(1)} collective-permute-done((bf16[8,8192]{1,0:T(8,128)(2,1)S(1)}, bf16[8,8192]{1,0:T(8,128)(2,1)S(1)}, u32[]{:S(2)}, u32[]{:S(2)}) %collective-permute-start.20) | collective-permute-done | bytes 131104 | tf_op jit(solution)/shard_map/ppermute | solution.py:32
  114.0 10.0 %all_to_all.41.parts_ref = bf16[8,8,1024]{2,1,0:T(8,128)(2,1)S(1)} all-to-all(bf16[8,8,1024]{2,1,0:T(8,128)(2,1)S(1)} %partial.3), channel_id=1, replica_groups={{0,2,4,6,8,10,12,14},{1,3,5,7,9,11,13,15},{16,18,20,22,24,26,28,30},{17..., dimensions={0} | all-to-all | bytes 262144 | tf_op jit(solution)/shard_map/all_to_all | solution.py:45
  (48 shorter events, 8.2 us)
Async XLA Ops:
  1.3 0.7 copy-start
  2.0 0.8 copy-start.2
  3.0 10.4 %collective-permute-start.2 = (bf16[1,8320]{1,0:T(2,128)(2,1)S(1)}, bf16[1,8320]{1,0:T(2,128)(2,1)S(1)}, u32[]{:S(2)}, u32[]{:S(2)}) collective-permute-start(bf16[1,8320]{1,0:T(2,128)(2,1)S(1)} %get-tuple-element.34.refs_0_), channel_id=1, source_target_pairs={{0,12},{1,13},{2,14},{3,15},{4,8},{5,9},{6,10},{7,11},{8,4},{9,5},... | collective-permute-start | bytes 49928 | tf_op jit(solution)/shard_map/ppermute | solution.py:32
  8.1 5.3 %collective-permute-start.1 = (bf16[1,8320]{1,0:T(2,128)(2,1)S(1)}, bf16[1,8320]{1,0:T(2,128)(2,1)S(1)}, u32[]{:S(2)}, u32[]{:S(2)}) collective-permute-start(bf16[1,8320]{1,0:T(2,128)(2,1)S(1)} %get-tuple-element.34.refs_0_), channel_id=1, source_target_pairs={{0,8},{1,9},{2,10},{3,11},{4,12},{5,13},{6,14},{7,15},{8,0},{9,1},... | collective-permute-start | bytes 49928 | tf_op jit(solution)/shard_map/ppermute | solution.py:32
  8.1 5.3 %collective-permute-start = (bf16[1,8320]{1,0:T(2,128)(2,1)S(1)}, bf16[1,8320]{1,0:T(2,128)(2,1)S(1)}, u32[]{:S(2)}, u32[]{:S(2)}) collective-permute-start(bf16[1,8320]{1,0:T(2,128)(2,1)S(1)} %get-tuple-element.34.refs_0_), channel_id=1, source_target_pairs={{0,4},{1,5},{2,6},{3,7},{4,0},{5,1},{6,2},{7,3},{8,12},{9,13},{10,... | collective-permute-start | bytes 49928 | tf_op jit(solution)/shard_map/ppermute | solution.py:32
  13.5 6.6 %copy-start.4 = (s32[32]{0:T(128)S(1)}, s32[32]{0:T(128)}, u32[]{:S(2)}) copy-start(s32[32]{0:T(128)} %param.19) | copy-start | bytes 388
  13.5 6.6 %collective-permute-start.5 = (bf16[4,8320]{1,0:T(4,128)(2,1)S(1)}, bf16[4,8320]{1,0:T(4,128)(2,1)S(1)}, u32[]{:S(2)}, u32[]{:S(2)}) collective-permute-start(bf16[4,8320]{1,0:T(4,128)(2,1)S(1)} %join.1.refs_0_), channel_id=1, source_target_pairs={{0,3},{1,2},{2,1},{3,0},{4,7},{5,6},{6,5},{7,4},{8,11},{9,10},{10,... | collective-permute-start | bytes 199688 | tf_op jit(solution)/shard_map/ppermute | solution.py:32
  13.9 6.1 %collective-permute-start.4 = (bf16[4,8320]{1,0:T(4,128)(2,1)S(1)}, bf16[4,8320]{1,0:T(4,128)(2,1)S(1)}, u32[]{:S(2)}, u32[]{:S(2)}) collective-permute-start(bf16[4,8320]{1,0:T(4,128)(2,1)S(1)} %join.1.refs_0_), channel_id=1, source_target_pairs={{0,2},{1,3},{2,0},{3,1},{4,6},{5,7},{6,4},{7,5},{8,10},{9,11},{10,... | collective-permute-start | bytes 199688 | tf_op jit(solution)/shard_map/ppermute | solution.py:32
  15.2 4.8 %collective-permute-start.3 = (bf16[4,8320]{1,0:T(4,128)(2,1)S(1)}, bf16[4,8320]{1,0:T(4,128)(2,1)S(1)}, u32[]{:S(2)}, u32[]{:S(2)}) collective-permute-start(bf16[4,8320]{1,0:T(4,128)(2,1)S(1)} %join.1.refs_0_), channel_id=1, source_target_pairs={{0,1},{1,0},{2,3},{3,2},{4,5},{5,4},{6,7},{7,6},{8,9},{9,8},{10,11... | collective-permute-start | bytes 199688 | tf_op jit(solution)/shard_map/ppermute | solution.py:32
  21.1 3.1 %collective-permute-start.8 = (bf16[16,64]{1,0:T(8,128)(2,1)S(1)}, bf16[16,64]{1,0:T(8,128)(2,1)S(1)}, u32[]{:S(2)}, u32[]{:S(2)}) collective-permute-start(bf16[16,64]{1,0:T(8,128)(2,1)S(1)} %get-tuple-element.40.refs_0_), channel_id=1, source_target_pairs={{0,3},{1,2},{2,1},{3,0},{4,7},{5,6},{6,5},{7,4},{8,11},{9,10},{10,... | collective-permute-start | bytes 6152 | tf_op jit(solution)/shard_map/ppermute | solution.py:32
  22.3 3.6 %collective-permute-start.7 = (bf16[16,64]{1,0:T(8,128)(2,1)S(1)}, bf16[16,64]{1,0:T(8,128)(2,1)S(1)}, u32[]{:S(2)}, u32[]{:S(2)}) collective-permute-start(bf16[16,64]{1,0:T(8,128)(2,1)S(1)} %get-tuple-element.40.refs_0_), channel_id=1, source_target_pairs={{0,2},{1,3},{2,0},{3,1},{4,6},{5,7},{6,4},{7,5},{8,10},{9,11},{10,... | collective-permute-start | bytes 6152 | tf_op jit(solution)/shard_map/ppermute | solution.py:32
  23.1 2.9 %collective-permute-start.6 = (bf16[16,64]{1,0:T(8,128)(2,1)S(1)}, bf16[16,64]{1,0:T(8,128)(2,1)S(1)}, u32[]{:S(2)}, u32[]{:S(2)}) collective-permute-start(bf16[16,64]{1,0:T(8,128)(2,1)S(1)} %get-tuple-element.40.refs_0_), channel_id=1, source_target_pairs={{0,1},{1,0},{2,3},{3,2},{4,5},{5,4},{6,7},{7,6},{8,9},{9,8},{10,11... | collective-permute-start | bytes 6152 | tf_op jit(solution)/shard_map/ppermute | solution.py:32
  25.9 5.9 %collective-permute-start.11 = (bf16[16,64]{1,0:T(8,128)(2,1)S(1)}, bf16[16,64]{1,0:T(8,128)(2,1)S(1)}, u32[]{:S(2)}, u32[]{:S(2)}) collective-permute-start(bf16[16,64]{1,0:T(8,128)(2,1)S(1)} %sum.2.refs_0_), channel_id=1, source_target_pairs={{0,12},{1,13},{2,14},{3,15},{4,8},{5,9},{6,10},{7,11},{8,4},{9,5},... | collective-permute-start | bytes 6152 | tf_op jit(solution)/shard_map/ppermute | solution.py:32
  29.6 4.5 %collective-permute-start.10 = (bf16[16,64]{1,0:T(8,128)(2,1)S(1)}, bf16[16,64]{1,0:T(8,128)(2,1)S(1)}, u32[]{:S(2)}, u32[]{:S(2)}) collective-permute-start(bf16[16,64]{1,0:T(8,128)(2,1)S(1)} %sum.2.refs_0_), channel_id=1, source_target_pairs={{0,8},{1,9},{2,10},{3,11},{4,12},{5,13},{6,14},{7,15},{8,0},{9,1},... | collective-permute-start | bytes 6152 | tf_op jit(solution)/shard_map/ppermute | solution.py:32
  29.6 4.5 %collective-permute-start.9 = (bf16[16,64]{1,0:T(8,128)(2,1)S(1)}, bf16[16,64]{1,0:T(8,128)(2,1)S(1)}, u32[]{:S(2)}, u32[]{:S(2)}) collective-permute-start(bf16[16,64]{1,0:T(8,128)(2,1)S(1)} %sum.2.refs_0_), channel_id=1, source_target_pairs={{0,4},{1,5},{2,6},{3,7},{4,0},{5,1},{6,2},{7,3},{8,12},{9,13},{10,... | collective-permute-start | bytes 6152 | tf_op jit(solution)/shard_map/ppermute | solution.py:32
  54.5 12.8 %copy-start.1 = (bf16[8192]{0:T(1024)(128)(2,1)S(1)}, bf16[8192]{0:T(1024)(128)(2,1)}, u32[]{:S(2)}) copy-start(bf16[8192]{0:T(1024)(128)(2,1)} %param.12) | copy-start | bytes 49156
  54.5 12.8 %copy-start.3 = (bf16[1,8192]{1,0:T(2,128)(2,1)S(1)}, bf16[1,8192]{1,0:T(2,128)(2,1)}, u32[]{:S(2)}) copy-start(bf16[1,8192]{1,0:T(2,128)(2,1)} %hidden_ref.3) | copy-start | bytes 49156
  55.9 1.4 %collective-permute-start.12 = (bf16[8,8192]{1,0:T(8,128)(2,1)S(1)}, bf16[8,8192]{1,0:T(8,128)(2,1)S(1)}, u32[]{:S(2)}, u32[]{:S(2)}) collective-permute-start(bf16[8,8192]{1,0:T(8,128)(2,1)S(1)} %get-tuple-element.52), channel_id=1, source_target_pairs={{0,1},{1,0},{2,3},{3,2},{4,5},{5,4},{6,7},{7,6},{8,9},{9,8},{10,11... | collective-permute-start | bytes 393224 | tf_op jit(solution)/shard_map/ppermute | solution.py:32
  77.6 1.3 %collective-permute-start.13 = (bf16[8,8,1024]{2,1,0:T(8,128)(2,1)S(1)}, bf16[8,8,1024]{2,1,0:T(8,128)(2,1)S(1)}, u32[]{:S(2)}, u32[]{:S(2)}) collective-permute-start(bf16[8,8,1024]{2,1,0:T(8,128)(2,1)S(1)} %all_to_all.38.own_ref), channel_id=1, source_target_pairs={{0,1},{1,0},{2,3},{3,2},{4,5},{5,4},{6,7},{7,6},{8,9},{9,8},{10,11... | collective-permute-start | bytes 393224 | tf_op jit(solution)/shard_map/ppermute | solution.py:32
  79.7 3.1 %collective-permute-start.16 = (bf16[16,64]{1,0:T(8,128)(2,1)S(1)}, bf16[16,64]{1,0:T(8,128)(2,1)S(1)}, u32[]{:S(2)}, u32[]{:S(2)}) collective-permute-start(bf16[16,64]{1,0:T(8,128)(2,1)S(1)} %get-tuple-element.54.refs_0_), channel_id=1, source_target_pairs={{0,3},{1,2},{2,1},{3,0},{4,7},{5,6},{6,5},{7,4},{8,11},{9,10},{10,... | collective-permute-start | bytes 6152 | tf_op jit(solution)/shard_map/ppermute | solution.py:32
  79.7 3.7 %collective-permute-start.15 = (bf16[16,64]{1,0:T(8,128)(2,1)S(1)}, bf16[16,64]{1,0:T(8,128)(2,1)S(1)}, u32[]{:S(2)}, u32[]{:S(2)}) collective-permute-start(bf16[16,64]{1,0:T(8,128)(2,1)S(1)} %get-tuple-element.54.refs_0_), channel_id=1, source_target_pairs={{0,2},{1,3},{2,0},{3,1},{4,6},{5,7},{6,4},{7,5},{8,10},{9,11},{10,... | collective-permute-start | bytes 6152 | tf_op jit(solution)/shard_map/ppermute | solution.py:32
  81.5 1.9 %collective-permute-start.14 = (bf16[16,64]{1,0:T(8,128)(2,1)S(1)}, bf16[16,64]{1,0:T(8,128)(2,1)S(1)}, u32[]{:S(2)}, u32[]{:S(2)}) collective-permute-start(bf16[16,64]{1,0:T(8,128)(2,1)S(1)} %get-tuple-element.54.refs_0_), channel_id=1, source_target_pairs={{0,1},{1,0},{2,3},{3,2},{4,5},{5,4},{6,7},{7,6},{8,9},{9,8},{10,11... | collective-permute-start | bytes 6152 | tf_op jit(solution)/shard_map/ppermute | solution.py:32
  83.4 5.9 %collective-permute-start.19 = (bf16[16,64]{1,0:T(8,128)(2,1)S(1)}, bf16[16,64]{1,0:T(8,128)(2,1)S(1)}, u32[]{:S(2)}, u32[]{:S(2)}) collective-permute-start(bf16[16,64]{1,0:T(8,128)(2,1)S(1)} %sum.3.refs_0_), channel_id=1, source_target_pairs={{0,12},{1,13},{2,14},{3,15},{4,8},{5,9},{6,10},{7,11},{8,4},{9,5},... | collective-permute-start | bytes 6152 | tf_op jit(solution)/shard_map/ppermute | solution.py:32
  84.8 4.5 %collective-permute-start.18 = (bf16[16,64]{1,0:T(8,128)(2,1)S(1)}, bf16[16,64]{1,0:T(8,128)(2,1)S(1)}, u32[]{:S(2)}, u32[]{:S(2)}) collective-permute-start(bf16[16,64]{1,0:T(8,128)(2,1)S(1)} %sum.3.refs_0_), channel_id=1, source_target_pairs={{0,8},{1,9},{2,10},{3,11},{4,12},{5,13},{6,14},{7,15},{8,0},{9,1},... | collective-permute-start | bytes 6152 | tf_op jit(solution)/shard_map/ppermute | solution.py:32
  85.9 3.6 %collective-permute-start.17 = (bf16[16,64]{1,0:T(8,128)(2,1)S(1)}, bf16[16,64]{1,0:T(8,128)(2,1)S(1)}, u32[]{:S(2)}, u32[]{:S(2)}) collective-permute-start(bf16[16,64]{1,0:T(8,128)(2,1)S(1)} %sum.3.refs_0_), channel_id=1, source_target_pairs={{0,4},{1,5},{2,6},{3,7},{4,0},{5,1},{6,2},{7,3},{8,12},{9,13},{10,... | collective-permute-start | bytes 6152 | tf_op jit(solution)/shard_map/ppermute | solution.py:32
  112.5 1.4 %collective-permute-start.20 = (bf16[8,8192]{1,0:T(8,128)(2,1)S(1)}, bf16[8,8192]{1,0:T(8,128)(2,1)S(1)}, u32[]{:S(2)}, u32[]{:S(2)}) collective-permute-start(bf16[8,8192]{1,0:T(8,128)(2,1)S(1)} %get-tuple-element.61), channel_id=1, source_target_pairs={{0,1},{1,0},{2,3},{3,2},{4,5},{5,4},{6,7},{7,6},{8,9},{9,8},{10,11... | collective-permute-start | bytes 393224 | tf_op jit(solution)/shard_map/ppermute | solution.py:32

commit v11 on v8

--- a/solution.py
+++ b/solution.py
@@ -47,7 +47,7 @@
     )
 
 
-def kernel(body, outs, name, scratch=(), vmem=20 << 20, flops=1 << 20, moved=1 << 18):
+def call(body, outs, name, scratch=(), vmem=20 << 20, flops=1 << 20, moved=1 << 18):
     def run(*operands, specs=None):
         specs = specs or [pltpu.VMEM] * len(operands)
         return pl.pallas_call(
@@ -81,6 +81,11 @@
     return (hidden * factor * scale).astype(jnp.bfloat16)
 
 
+def row_of(ref):
+    lines = ref[...].astype(jnp.float32)
+    return jnp.concatenate([lines[i : i + 1] for i in range(lines.shape[0])], axis=1)
+
+
 def folded(out_ref, row):
     wide = row.shape[1] // FOLD
     for k in range(out_ref.shape[0]):
@@ -88,11 +93,11 @@
             out_ref[k, i : i + 1, :wide] = row[:, i * wide : (i + 1) * wide].astype(out_ref.dtype)
 
 
-def first_kernel(hidden_ref, scale_ref, adapter_ref, length_ref, out_ref, length_out):
+def first_kernel(hidden_ref, scale_ref, adapter_ref, length_ref, _, out_ref, length_out):
     length_out[...] = jnp.full(length_out.shape, length_ref[0], jnp.int32)
     width = hidden_ref.shape[1]
     hidden = hidden_ref[...].astype(jnp.float32)
-    out_ref[:, :width] = normalized(hidden, scale_ref[...].astype(jnp.float32))
+    out_ref[:, :width] = normalized(hidden, row_of(scale_ref))
     digit = iota((1, LANES), 1)
     adapter = adapter_ref[0]
     length = length_ref[0]
@@ -110,22 +115,22 @@
     ]
     for copy in copies:
         copy.start()
-    out_token[...] = token_ref[...] * 0.0
+    out_token[...] = token_ref[...]
     for copy in copies:
         copy.wait()
 
 
-def member_kernel(near, far, width, *refs):
-    pieces = refs[:near]
-    me_ref, storage_ref = refs[near : near + 2]
+def member_kernel(near, far, width, strides, *refs):
+    amount = far if strides[0] > 1 else near
+    pieces, (me_ref, storage_ref) = refs[:amount], refs[amount : amount + 2]
     member_ref, adapter_ref, lengths_ref, held = refs[-4:]
     kept = member_ref.shape[1]
     count = near * far
     me = me_ref[0]
-    for l in range(near):
-        digits = pieces[l][:, width:].astype(jnp.float32)
-        for k in range(far):
-            held[pl.ds(me ^ (k * near + l), 1), :] = digits[k : k + 1]
+    for l, piece in enumerate(pieces):
+        digits = piece[:, width:].astype(jnp.float32)
+        for k in range(digits.shape[0]):
+            held[pl.ds(me ^ (l * strides[0] + k * strides[1]), 1), :] = digits[k : k + 1]
     adapter = (held[:, 0:1] + 256.0 * held[:, 1:2]).astype(jnp.int32)
     adapter_ref[...] = adapter
     lengths_ref[...] = (held[:, 2:3] + 256.0 * held[:, 3:4]).astype(jnp.int32)
@@ -153,15 +158,14 @@
         outs[0][:, LANES:] = fresh
 
 
-def low_first_kernel(near, far, *refs):
-    pieces = refs[:near]
-    me_ref, member_ref, down_ref, fresh_w = refs[near : near + 4]
-    outs, held = refs[near + 4 : -1], refs[-1]
+def low_first_kernel(amount, strides, *refs):
+    pieces, (me_ref, member_ref, down_ref, fresh_w) = refs[:amount], refs[amount : amount + 4]
+    outs, held = refs[amount + 4 : -1], refs[-1]
     width = held.shape[1]
-    for l in range(near):
-        block = pieces[l][:, :width].astype(jnp.float32)
-        for k in range(far):
-            held[pl.ds(me_ref[0] ^ (k * near + l), 1), :] = block[k : k + 1]
+    for l, piece in enumerate(pieces):
+        block = piece[:, :width].astype(jnp.float32)
+        for k in range(block.shape[0]):
+            held[pl.ds(me_ref[0] ^ (l * strides[0] + k * strides[1]), 1), :] = block[k : k + 1]
     low_terms(held, member_ref, down_ref, fresh_w, *outs)
 
 
@@ -214,8 +218,7 @@
 def up_kernel(parts, *refs):
     lows, (query_ref, fresh_ref, adapter_ref, up_ref, out_ref, held) = refs[:parts], refs[parts:]
     count, columns = query_ref.shape
-    lows = [ref[...].astype(jnp.float32) for ref in lows]
-    query = up_terms(lows, query_ref, adapter_ref, up_ref)
+    query = up_terms([ref[...].astype(jnp.float32) for ref in lows], query_ref, adapter_ref, up_ref)
     line = out_ref.shape[2]
     lines = columns // line
     held[...] = jnp.zeros(held.shape, jnp.float32)
@@ -353,17 +356,17 @@
     output_terms(jnp.concatenate(rows, axis=1), me_ref[0] % CORES, weight_ref, own_ref, away_ref)
 
 
-def cut_kernel(half, me_ref, cache_hbm, *refs):
+def cut_kernel(sides, pair, me_ref, cache_hbm, *refs):
     outs, sems = refs[:-1], refs[-1]
     chip = me_ref[0] // CORES
+    group = len(outs) * pair // sides
     copies = []
-    for d, out in enumerate(outs):
-        for side in range(2):
-            lanes = pl.ds(pl.multiple_of((chip ^ d ^ (side * half)) * HD, HD), HD)
+    for d in range(group):
+        for s in range(sides):
+            lanes = pl.ds(pl.multiple_of((chip ^ d ^ (s * group)) * HD, HD), HD)
+            out = outs[d * (sides // pair) + s // pair].at[s % pair]
             copies.append(
-                pltpu.make_async_copy(
-                    cache_hbm.at[0, :, :, lanes], out.at[side], sems.at[2 * d + side]
-                )
+                pltpu.make_async_copy(cache_hbm.at[0, :, :, lanes], out, sems.at[d * sides + s])
             )
     for copy in copies:
         copy.start()
@@ -371,17 +374,8 @@
         copy.wait()
 
 
-def late_kernel(row_ref, _, out_ref):
-    out_ref[...] = row_ref[...]
-
-
-def merge_kernel(amount, *refs):
-    out_ref, sems = refs[-2:]
-    copies = [pltpu.make_async_copy(refs[i], out_ref.at[i], sems.at[i]) for i in range(amount)]
-    for copy in copies:
-        copy.start()
-    for copy in copies:
-        copy.wait()
+def gate_kernel(*_):
+    pass
 
 
 def pack_kernel(near, *refs):
@@ -394,58 +388,68 @@
         out_ref[:, (l + 1) * LANES : (l + 2) * LANES] = refs[l][:, LANES:]
 
 
-def ask_kernel(parts, rank, *refs):
-    lows = [ref[:, :rank].astype(jnp.float32) for ref in refs[:parts]]
-    query_ref, adapter_ref, up_ref, me_ref, own_ref, away_ref = refs[parts:]
+def ask_kernel(sides, rank, *refs):
+    lows = [ref[:, :rank].astype(jnp.float32) for ref in refs[:sides]]
+    query_ref, adapter_ref, up_ref, me_ref = refs[sides : sides + 4]
+    outs, held = refs[sides + 4 : -1], refs[-1]
     query = up_terms(lows, query_ref, adapter_ref, up_ref)
-    some = own_ref.shape[0]
-    side = me_ref[0] // some
-    low, high = query[:some], query[some:]
-    own_ref[...] = jnp.where(side == 0, low, high).astype(jnp.bfloat16)
-    away_ref[...] = jnp.where(side == 0, high, low).astype(jnp.bfloat16)
-
-
-def halves_kernel(parts, near, steps, *refs):
-    own_ref, other_ref, lengths_ref, me_ref = refs[:4]
-    lows, refs = refs[4 : 4 + parts], refs[4 + parts :]
+    some = outs[0].shape[0]
+    for s in range(sides):
+        held[s, :some] = query[s * some : (s + 1) * some]
+    for s in range(sides):
+        outs[s][...] = held[(me_ref[0] // some) ^ s, :some].astype(jnp.bfloat16)
+
+
+def group_kernel(sides, near, steps, *refs):
+    asked, refs = refs[:sides], refs[sides:]
+    lows, refs = refs[:sides], refs[sides:]
+    lengths_ref, me_ref, refs = refs[0], refs[1], refs[2:]
     if steps > 1:
         past_ref, refs = refs[0], refs[1:]
-    mine_ref, away_ref, new_ref, held, all_ref, mixed_ref = refs[-6:]
-    blocks = refs[:-6]
-    blocks = [*blocks[:-1], *(blocks[-1].at[d] for d in range(len(blocks) - 1))]
-    some, columns = own_ref.shape
+    new_ref, held, all_ref, mixed_ref = refs[-4:]
+    outs, blocks = refs[-4 - sides : -4], refs[: -4 - sides]
+    some, columns = asked[0].shape
     each = columns // HD
     lines = held.shape[2]
     me = me_ref[0]
     chip, core = me // CORES, me % CORES
-    half = KVH // 2
-    side = me // some
+    mine = me // some
+    group = some // CORES
     held[...] = jnp.zeros(held.shape, jnp.float32)
-    for s, ref in enumerate((own_ref, other_ref)):
+    for s, ref in enumerate(asked):
         query = ref[...].astype(jnp.float32)
         for c in range(each):
             held[s, :, c, :] = query[:, c * HD : (c + 1) * HD]
-    for k in range(parts):
+    for k in range(sides):
         for l in range(near):
             all_ref[k * near + l] = lows[k][:, (l + 1) * LANES : (l + 2) * LANES].astype(jnp.float32)
-    for s in range(2):
+    for s in range(sides):
         for v in range(2):
-            holder = (chip ^ (s * half)) + v * KVH
-            new_ref[steps - 1, s, v] = all_ref[me ^ holder, pl.ds(pl.multiple_of(side * some, some), some), :]
+            holder = me ^ ((chip ^ (s * group)) + v * KVH)
+            for row in range(some):
+                new_ref[steps - 1, s, v, row : row + 1, :] = all_ref[
+                    holder, pl.ds(mine * some + row, 1), :
+                ]
     for t in range(steps - 1):
         new_ref[t] = past_ref[t]
     scale = 1.0 / math.sqrt(HD)
-    rows = [((chip ^ d) % half) * CORES + (core ^ l) for l in range(CORES) for d in range(half)]
+    pair = blocks[0].shape[0]
+    where = []
+    for l in range(CORES):
+        for d in range(group):
+            row = ((chip ^ d) % group) * CORES + (core ^ l)
+            for s in range(sides):
+                number = (l * group + d) * (sides // pair) + s // pair
+                where.append((row, s, blocks[number].at[s % pair]))
     old, fresh = [], [[] for _ in range(steps)]
-    for row, block in zip(rows, blocks):
-        length = lengths_ref[pl.ds(side * some + row, 1), :]
-        for s in range(2):
-            query = held[s, row]
-            score = dot(query.astype(jnp.bfloat16), block[s, 0], LAST) * scale
-            old.append(jnp.where(iota(score.shape, 1) < length, score, -jnp.inf))
-            for t in range(steps):
-                keys = new_ref[t, s, 0, pl.ds(row, 1), :]
-                fresh[t].append(jnp.sum(query * keys, axis=1, keepdims=True) * scale)
+    for row, s, block in where:
+        length = lengths_ref[pl.ds(mine * some + row, 1), :]
+        query = held[s, row]
+        score = dot(query.astype(jnp.bfloat16), block[0], LAST) * scale
+        old.append(jnp.where(iota(score.shape, 1) < length, score, -jnp.inf))
+        for t in range(steps):
+            keys = new_ref[t, s, 0, pl.ds(row, 1), :]
+            fresh[t].append(jnp.sum(query * keys, axis=1, keepdims=True) * scale)
     old = jnp.concatenate(old, axis=0)
     fresh = [jnp.concatenate(scores, axis=0) for scores in fresh]
     peak = jnp.max(old, axis=1, keepdims=True)
@@ -458,27 +462,25 @@
         total = total + scores
     old = (old / total).astype(jnp.bfloat16).astype(jnp.float32)
     fresh = [(scores / total).astype(jnp.bfloat16).astype(jnp.float32) for scores in fresh]
-    for b, (row, block) in enumerate(zip(rows, blocks)):
-        for s in range(2):
-            part = slice((2 * b + s) * lines, (2 * b + s + 1) * lines)
-            mixed = dot(old[part].astype(jnp.bfloat16), block[s, 1])
-            for t in range(steps):
-                mixed = mixed + fresh[t][part] * new_ref[t, s, 1, pl.ds(row, 1), :]
-            mixed_ref[s, row] = mixed
-    for c in range(each):
-        part = slice(c * HD, (c + 1) * HD)
-        mine_ref[:, part] = mixed_ref[0, :, c, :].astype(jnp.bfloat16)
-        away_ref[:, part] = mixed_ref[1, :, c, :].astype(jnp.bfloat16)
-
-
-def joined_kernel(mine_ref, other_ref, me_ref, weight_ref, own_ref, away_ref):
-    some = mine_ref.shape[0]
-    mine, other = mine_ref[...].astype(jnp.float32), other_ref[...].astype(jnp.float32)
-    side = me_ref[0] // some
-    rows = jnp.concatenate(
-        [jnp.where(side == 0, mine, other), jnp.where(side == 0, other, mine)], axis=0
-    ).astype(jnp.bfloat16)
-    output_terms(rows, me_ref[0] % CORES, weight_ref, own_ref, away_ref)
+    for b, (row, s, block) in enumerate(where):
+        part = slice(b * lines, (b + 1) * lines)
+        mixed = dot(old[part].astype(jnp.bfloat16), block[1])
+        for t in range(steps):
+            mixed = mixed + fresh[t][part] * new_ref[t, s, 1, pl.ds(row, 1), :]
+        mixed_ref[s, row] = mixed
+    for s in range(sides):
+        for c in range(each):
+            outs[s][:, c * HD : (c + 1) * HD] = mixed_ref[s, :, c, :].astype(jnp.bfloat16)
+
+
+def joined_kernel(sides, *refs):
+    pieces, (me_ref, weight_ref, own_ref, away_ref, held) = refs[:sides], refs[sides:]
+    some = pieces[0].shape[0]
+    for s in range(sides):
+        piece = pieces[s][...].astype(jnp.float32)
+        for row in range(some):
+            held[pl.ds(((me_ref[0] // some) ^ s) * some + row, 1), :] = piece[row : row + 1]
+    output_terms(held[...].astype(jnp.bfloat16), me_ref[0] % CORES, weight_ref, own_ref, away_ref)
 
 
 def partial_kernel(own_ref, other_ref, out_ref):
@@ -503,7 +505,7 @@
         out_ref[...] = jnp.concatenate([before, hidden], axis=0).astype(jnp.bfloat16)
     else:
         out_ref[...] = hidden.astype(jnp.bfloat16)
-        folded(spread[0], normalized(hidden, scale_ref[...].astype(jnp.float32)).astype(jnp.float32))
+        folded(spread[0], normalized(hidden, row_of(scale_ref)).astype(jnp.float32))
 
 
 def shards(
@@ -529,28 +531,35 @@
     fresh_columns = key_value_weight.shape[1]
     line = min(HD, columns)
     smem, vmem = pltpu.SMEM, pltpu.VMEM
-    call = functools.partial(kernel, vmem=min(20 << 20, (count * 3 // 4) << 20))
     me = lax.axis_index(AXIS).astype(jnp.int32).reshape(1)
     down = adapter_down_weight.transpose(0, 2, 1)
-    scale = attention_norm_scale[None]
+    scale = attention_norm_scale.reshape(-1, LANES)
     storage = adapter_storage_index[None]
 
-    def stash(token, arrays, limit):
+    def stash(token, arrays):
         outs = call(
             functools.partial(stash_kernel, len(arrays)),
-            [pltpu.VMEM(a.shape, a.dtype) for a in arrays] + [shape((8, LANES), jnp.float32)],
+            [pltpu.VMEM(a.shape, a.dtype) for a in arrays] + [shape((8, LANES), jnp.int32)],
             "stash",
             [pltpu.SemaphoreType.DMA((len(arrays),))],
-            vmem=limit,
             moved=sum(2 * a.size for a in arrays),
-        )(token, *arrays, specs=[vmem] + [pl.ANY] * len(arrays))
+        )(
+            token,
+            *(pltpu.with_memory_space_constraint(a, pltpu.HBM) for a in arrays),
+            specs=[vmem] + [pltpu.HBM] * len(arrays),
+        )
         return outs[:-1], outs[-1]
 
-    past, held_cache, blocks = [], [], []
-
-    def after(*numbers):
-        return [blocks[d] for d in numbers] if blocks else []
-
+    def gate(array, *behind):
+        return pl.pallas_call(
+            gate_kernel,
+            out_shape=shape(array.shape, array.dtype),
+            in_specs=[pl.BlockSpec(memory_space=pl.ANY)] * (1 + len(behind)),
+            out_specs=pl.BlockSpec(memory_space=pl.ANY),
+            input_output_aliases={0: 0},
+            compiler_params=pltpu.CompilerParams(vmem_limit_bytes=1 << 20),
+            name="gate",
+        )(array, *behind)
 
     def by_rows(step, lows, query, fresh):
         first = step == 0
@@ -595,49 +604,114 @@
         )(lines, me, output_w, specs=[vmem, smem, vmem])
         return own, away
 
+    def by_groups(step, lows, query):
+        rows_group = shape((near, columns))
+        asked = call(
+            functools.partial(ask_kernel, far, rank),
+            [rows_group] * far,
+            "ask",
+            [pltpu.VMEM((far, 8, columns), jnp.float32)],
+        )(*lows, query, adapter, up_w, me, specs=[vmem] * (far + 3) + [smem])
+        asked = [asked[0]] + [shift(a, d, count) for a, d in zip(asked[1:], far_steps)]
+        if not blocks:
+            still = gate(parts[-1], asked[1])
+            blocks.extend([*parts[:-1], still, *sibs, shift(still, 1, count)])
+        new = (step + 1, far, 2, near, HD)
+        outs = call(
+            functools.partial(group_kernel, far, near, step + 1),
+            [rows_group] * far + [shape(new, jnp.float32)],
+            "attend",
+            [
+                pltpu.VMEM((far, near, 8, HD), jnp.float32),
+                pltpu.VMEM((count, count, LANES), jnp.float32),
+                pltpu.VMEM((far, near, 8, HD), jnp.float32),
+            ],
+            moved=4 << 20,
+        )(
+            *asked,
+            *lows,
+            lengths,
+            me,
+            *past,
+            *blocks,
+            specs=[vmem] * (2 * far + 1) + [smem] + [vmem] * (len(past) + len(blocks)),
+        )
+        past[:] = [outs[-1]]
+        pieces = [outs[0]] + [shift(a, d, count) for a, d in zip(outs[1:far], far_steps)]
+        return call(
+            functools.partial(joined_kernel, far),
+            [shape((chips, width), jnp.float32), shape((chips, width))],
+            "output",
+            [pltpu.VMEM((count, columns), jnp.float32)],
+            flops=2 * count * width * columns,
+            moved=2 * width * columns,
+        )(*pieces, me, output_w, specs=[vmem] * far + [smem, vmem])
+
+    by_heads = (
+        columns * CORES == GROUP * HD and count == CORES * KVH and fresh_columns == LANES
+    )
+    past, held_cache, blocks = [], [], []
     hidden = hidden_state_input
     carried, length = call(
         first_kernel, [shape((1, width + LANES)), shape((8, LANES), jnp.int32)], "first"
-    )(hidden, scale, row_adapter_index, cache_length_per_row, specs=[vmem, vmem, smem, smem])
-    fresh_past = []
-    by_halves = columns * CORES == GROUP * HD and count == CORES * KVH and fresh_columns == LANES
+    )(
+        hidden,
+        scale,
+        row_adapter_index,
+        cache_length_per_row,
+        me,
+        specs=[vmem, vmem, smem, smem, smem],
+    )
     for step in range(STEPS):
         first, last = step == 0, step == STEPS - 1
         low_outs = [shape((count, width))]
-        if by_halves:
+        if by_heads:
             low_outs = low_outs + [shape((count, LANES + fresh_columns))]
         else:
             low_outs = low_outs + [shape((count, rank)), shape((count, fresh_columns))]
         scratch = [pltpu.VMEM((count, width), jnp.float32)]
+        behind = []
         if first:
-            token = jnp.zeros((8, LANES), jnp.float32)
-            arrays = [query_weight, output_weight, key_value_weight, down, adapter_up_weight]
-            if by_halves:
-                half = chips // 2
+            steps = (near_steps, far_steps) if by_heads else (far_steps, near_steps)
+            strides = (near, 1) if by_heads else (1, near)
+            amount = len(steps[1]) + 1
+            early = [query_weight, key_value_weight, down]
+            later = [output_weight, adapter_up_weight]
+            if by_heads:
+                group = near // CORES
+                pair = far // 2
                 cut = call(
-                    functools.partial(cut_kernel, half),
-                    [pltpu.VMEM((2, 2, key_value_cache.shape[2], HD), jnp.bfloat16)] * half,
+                    functools.partial(cut_kernel, far, pair),
+                    [pltpu.VMEM((pair, 2, key_value_cache.shape[2], HD), jnp.bfloat16)]
+                    * (group * 2),
                     "cut",
-                    [pltpu.SemaphoreType.DMA((2 * half,))],
-                    vmem=58 << 20,
-                )(me, key_value_cache, specs=[smem, pl.ANY])
-                blocks.extend([cut[0]] + [shift(cut[d], CORES * d, count) for d in range(1, half)])
+                    [pltpu.SemaphoreType.DMA((group * far,))],
+                )(
+                    me,
+                    pltpu.with_memory_space_constraint(key_value_cache, pltpu.HBM),
+                    specs=[smem, pltpu.HBM],
+                )
             else:
-                arrays.append(key_value_cache)
-            outs, token = stash(token, arrays, 30 << 20)
-            query_w, output_w, fresh_w, down_w, up_w = outs[:5]
-            held_cache.append(outs[-1])
-            late = carried
-            if by_halves:
-                (late,) = call(late_kernel, [shape(carried.shape)], "late")(carried, token)
-            pieces = [carried, shift(late, near, count)]
-            pieces = pieces + [shift(carried, d, count) for d in far_steps[1:]]
+                later = later + [key_value_cache]
+                (query_w, fresh_w, down_w), token = stash(length, early)
+            pieces = across(carried, steps[0], count)
+            ordered = [] if by_heads else [token]
             (carried,) = call(
-                functools.partial(join_kernel, far), [shape((far, width + LANES))], "join"
-            )(*pieces, token, *after(1, 2, 3), specs=[vmem] * (far + 1) + [pl.ANY] * len(after(1, 2, 3)))
-            pieces = across(carried, near_steps, count)
+                functools.partial(join_kernel, len(pieces)),
+                [shape((len(pieces), width + LANES))],
+                "join",
+            )(*pieces, *ordered)
+            if by_heads:
+                (query_w, fresh_w, down_w), token = stash(length, early)
+                there = shift(gate(cut[2], carried), CORES, count)
+                parts = [gate(cut[0], carried)]
+                beside = shift(parts[0], 1, count)
+                behind = [there, beside]
+            (output_w, up_w, *cached), token = stash(token, later)
+            held_cache.extend(cached)
+            pieces = across(carried, steps[1], count)
             member, adapter, lengths = call(
-                functools.partial(member_kernel, near, far, width),
+                functools.partial(member_kernel, near, far, width, strides),
                 [shape((count, kept), jnp.int32)] + [shape((count, 1), jnp.int32)] * 2,
                 "member",
                 [pltpu.VMEM((count, LANES), jnp.float32)],
@@ -645,27 +719,19 @@
                 *pieces,
                 me,
                 storage,
-                *after(),
-                specs=[vmem] * near + [smem, vmem] + [pl.ANY] * len(after()),
+                token,
+                *behind,
+                specs=[vmem] * amount + [smem, vmem, vmem] + [pl.ANY] * len(behind),
             )
-            if by_halves:
-                (merged,) = call(
-                    functools.partial(merge_kernel, half),
-                    [shape((half, *cut[0].shape))],
-                    "merge",
-                    [pltpu.SemaphoreType.DMA((half,))],
-                )(*blocks, member, specs=[pl.ANY] * (half + 1))
-                blocks.append(shift(merged, 1, count))
             rows, low, *fresh = call(
-                functools.partial(low_first_kernel, near, far), low_outs, "low", scratch
-            )(
-                *pieces,
-                me,
-                member,
-                down_w,
-                fresh_w,
-                specs=[vmem] * near + [smem] + [vmem] * 3,
-            )
+                functools.partial(low_first_kernel, amount, strides), low_outs, "low", scratch
+            )(*pieces, me, member, down_w, fresh_w, specs=[vmem] * amount + [smem] + [vmem] * 3)
+            behind = []
+            if by_heads:
+                still = gate(there, rows)
+                parts = parts + [gate(cut[1], rows), still]
+                sibs = [beside] + [shift(p, 1, count) for p in parts[1:]]
+                behind = sibs[1:]
         else:
             own = chips_swap(carried, count)
             rows, low, *fresh = call(low_later_kernel, low_outs, "low", scratch)(
@@ -677,15 +743,17 @@
                 fresh_w,
                 specs=[vmem, vmem, smem, vmem, vmem, vmem],
             )
-        lows = across(low, near_steps, count)
-        behind = after() if first else []
-        if by_halves:
+        if by_heads:
             body, dims = pack_kernel, (count, (near + 1) * LANES)
         else:
             body, dims = sum_kernel, (count, rank)
         (low,) = call(functools.partial(body, near), [shape(dims)], "sum")(
-            *lows, *behind, specs=[vmem] * near + [pl.ANY] * len(behind)
+            *across(low, near_steps, count),
+            *behind,
+            specs=[vmem] * near + [pl.ANY] * len(behind),
         )
+        if first and by_heads:
+            parts = parts + [shift(gate(cut[3], low), CORES, count)]
         lows = across(low, far_steps, count)
         (query,) = call(
             project_kernel,
@@ -694,40 +762,8 @@
             flops=2 * count * width * columns,
             moved=2 * width * columns,
         )(rows, query_w)
-        if by_halves:
-            some = count // 2
-            rows_half = shape((some, columns))
-            own, away = call(functools.partial(ask_kernel, far, rank), [rows_half] * 2, "ask")(
-                *lows, query, adapter, up_w, me, specs=[vmem] * (far + 3) + [smem]
-            )
-            new = (step + 1, 2, 2, some, HD)
-            mine, away, *fresh_past = call(
-                functools.partial(halves_kernel, far, near, step + 1),
-                [rows_half, rows_half, shape(new, jnp.float32)],
-                "attend",
-                [
-                    pltpu.VMEM((2, some, 8, HD), jnp.float32),
-                    pltpu.VMEM((count, count, LANES), jnp.float32),
-                    pltpu.VMEM((2, some, 8, HD), jnp.float32),
-                ],
-                moved=4 << 20,
-            )(
-                own,
-                shift(away, some, count),
-                lengths,
-                me,
-                *lows,
-                *fresh_past,
-                *blocks,
-                specs=[vmem] * 3 + [smem] + [vmem] * (far + len(fresh_past) + len(blocks)),
-            )
-            own, away = call(
-                joined_kernel,
-                [shape((chips, width), jnp.float32), shape((chips, width))],
-                "output",
-                flops=2 * count * width * columns,
-                moved=2 * width * columns,
-            )(mine, shift(away, some, count), me, output_w, specs=[vmem, vmem, smem, vmem])
+        if by_heads:
+            own, away = by_groups(step, lows, query)
         else:
             own, away = by_rows(step, lows, query, fresh[0])
 

time: 128 us -> 131 us (1.023)
  waiting for transfers between devices: 40.9 us -> 31.2 us
  starting transfers between devices: 31 us -> 39.9 us
  local copies, waits for them, and re-layouts: 0.03 us -> 1.48 us
    ppermute x29 -> x39, waiting for transfers between devices: 40.9 us -> 31.2 us  [shift(): return lax.ppermute(block, AXIS, [(i, i ^ distance) for i in range(count)])]
    ppermute x29 -> x39, starting transfers between devices: 31 us -> 39.9 us  [shift(): return lax.ppermute(block, AXIS, [(i, i ^ distance) for i in range(count)])]
    unnamed x6 -> x10, local copies, waits for them, and re-layouts: 0.01 us -> 1.48 us
    pallas_call x23 -> x22, Pallas kernels: 22.3 us -> 23.1 us  [run(): pl.pallas_call(body, out_shape=outs, in_specs=[pl.BlockSpec(memory_space=...]
  transfers between devices with their start and end apart: 29 -> 39, of which waited for: 19 -> 21; matrix products, arithmetic and copies ran while one was open for 0% -> 0% of each run, Pallas kernels for 9% -> 10%
where the time goes in v11:
time: 131 us; the launch traced here: 130 us
  starting transfers between devices  39.9 us (30%)
  blocking collectives  33 us (25%)
  waiting for transfers between devices  31.2 us (24%)
  Pallas kernels  23.1 us (18%)
  between operations  1.55 us (1%)
  local copies, waits for them, and re-layouts  1.48 us (1%)
    ppermute x39, starting transfers between devices, shift(): return lax.ppermute(block, AXIS, [(i, i ^ distance) for i in range(count)])  39.9 us
    all_to_all x3, blocking collectives, chips_swap(): lax.all_to_all(blocks, AXIS, split_axis=0, concat_axis=0, axis_index_grou...  33 us
    ppermute x39, waiting for transfers between devices, shift(): return lax.ppermute(block, AXIS, [(i, i ^ distance) for i in range(count)])  31.2 us
    pallas_call x22, Pallas kernels, run(): pl.pallas_call(body, out_shape=outs, in_specs=[pl.BlockSpec(memory_space=...  23.1 us
  transfers between devices with their start and end apart: 39, of which 21 were waited for; matrix products, arithmetic and copies ran while one was open for 0% of the time, Pallas kernels for 10%

profile of v11, /device:TPU:0, one launch (start us, length us, event | category | flops | bytes accessed | tf_op | source)
XLA Modules:
  0.0 130.2 jit_solution(9818084048937952057)
XLA Ops:
  3.0 2.4 %collective-permute-start.2 = (bf16[1,8320]{1,0:T(2,128)(2,1)S(1)}, bf16[1,8320]{1,0:T(2,128)(2,1)S(1)}, u32[]{:S(2)}, u32[]{:S(2)}) collective-permute-start(bf16[1,8320]{1,0:T(2,128)(2,1)S(1)} %get-tuple-element.48.refs_0_), channel_id=1, source_target_pairs={{0,3},{1,2},{2,1},{3,0},{4,7},{5,6},{6,5},{7,4},{8,11},{9,10},{10,... | collective-permute-start | bytes 49928 | tf_op jit(solution)/shard_map/ppermute | solution.py:32
  6.1 1.6 %cut.1 = (bf16[2,2,512,128]{3,2,1,0:T(8,128)(2,1)S(1)}, bf16[2,2,512,128]{3,2,1,0:T(8,128)(2,1)S(1)}, bf16[2,2,512,128]{3,2,1,0:T(8,128)(2,1)S(1)}, bf16[2,2,512,128]{3,2,1,0:T(8,128)(2,1)S(1)}) custom-call(s32[1]{0:T(128)} %bitcast.1._.me_ref.refs_4_.refs_7_.refs_9_, bf16[1,2,512,1024]{3,2,1,0:T(8,128)(2,1)} %cache_hbm.1), custom_call_target="tpu_custom_call" | custom-call | flops 1048576 | bytes 262144 | tf_op jit(solution)/shard_map/cut/pallas_call | solution.py:53
  7.7 1.7 %collective-permute-done.1.refs_2_ = bf16[1,8320]{1,0:T(2,128)(2,1)S(1)} collective-permute-done((bf16[1,8320]{1,0:T(2,128)(2,1)S(1)}, bf16[1,8320]{1,0:T(2,128)(2,1)S(1)}, u32[]{:S(2)}, u32[]{:S(2)}) %collective-permute-start.1) | collective-permute-done | bytes 16672 | tf_op jit(solution)/shard_map/ppermute | solution.py:32
  10.7 3.6 %collective-permute-start.5 = (bf16[4,8320]{1,0:T(4,128)(2,1)S(1)}, bf16[4,8320]{1,0:T(4,128)(2,1)S(1)}, u32[]{:S(2)}, u32[]{:S(2)}) collective-permute-start(bf16[4,8320]{1,0:T(4,128)(2,1)S(1)} %join.1.__1_.refs_0_), channel_id=1, source_target_pairs={{0,12},{1,13},{2,14},{3,15},{4,8},{5,9},{6,10},{7,11},{8,4},{9,5},... | collective-permute-start | bytes 199688 | tf_op jit(solution)/shard_map/ppermute | solution.py:32
  15.1 4.6 %stash.2 = (bf16[8192,512]{1,0:T(8,128)(2,1)S(1)}, bf16[8192,128]{1,0:T(8,128)(2,1)S(1)}, bf16[2,64,8192]{2,1,0:T(8,128)(2,1)S(1)}, s32[8,128]{1,0:T(8,128)S(1)}) custom-call(s32[8,128]{1,0:T(8,128)S(1)} %get-tuple-element.49.token_ref, bf16[8192,512]{1,0:T(8,128)(2,1)} %refs_0_.2, bf16[8192,128]{1,0:T(8,128)(2,1)} %refs_1_.2, bf16[2,64,8192]{2,1,0:T(8,128)(2,1)} %bitcast.9), custom_call_target="tpu_custom_call" | custom-call | flops 1048576 | bytes 12582912 | tf_op jit(solution)/shard_map/stash/pallas_call | solution.py:53
  19.7 4.0 %stash.3 = (bf16[512,8192]{1,0:T(8,128)(2,1)S(1)}, bf16[32,64,512]{2,1,0:T(8,128)(2,1)S(1)}, s32[8,128]{1,0:T(8,128)S(1)}) custom-call(s32[8,128]{1,0:T(8,128)S(1)} %get-tuple-element.50.token_ref, bf16[512,8192]{1,0:T(8,128)(2,1)} %refs_0_.3, bf16[32,64,512]{2,1,0:T(8,128)(2,1)} %refs_1_.3), custom_call_target="tpu_custom_call" | custom-call | flops 1048576 | bytes 10485760 | tf_op jit(solution)/shard_map/stash/pallas_call | solution.py:53
  31.3 3.6 %collective-permute-start.15 = (bf16[16,640]{1,0:T(8,128)(2,1)S(1)}, bf16[16,640]{1,0:T(8,128)(2,1)S(1)}, u32[]{:S(2)}, u32[]{:S(2)}) collective-permute-start(bf16[16,640]{1,0:T(8,128)(2,1)S(1)} %sum.2.refs_0_.__1_.refs_4_), channel_id=1, source_target_pairs={{0,12},{1,13},{2,14},{3,15},{4,8},{5,9},{6,10},{7,11},{8,4},{9,5},... | collective-permute-start | bytes 61448 | tf_op jit(solution)/shard_map/ppermute | solution.py:32
  36.8 2.7 %collective-permute-done.14.refs_2_.refs_6_ = bf16[16,640]{1,0:T(8,128)(2,1)S(1)} collective-permute-done((bf16[16,640]{1,0:T(8,128)(2,1)S(1)}, bf16[16,640]{1,0:T(8,128)(2,1)S(1)}, u32[]{:S(2)}, u32[]{:S(2)}) %collective-permute-start.14) | collective-permute-done | bytes 20512 | tf_op jit(solution)/shard_map/ppermute | solution.py:32
  40.1 3.6 %collective-permute-done.16.__1_.refs_1_ = bf16[4,512]{1,0:T(4,128)(2,1)S(1)} collective-permute-done((bf16[4,512]{1,0:T(4,128)(2,1)S(1)}, bf16[4,512]{1,0:T(4,128)(2,1)S(1)}, u32[]{:S(2)}, u32[]{:S(2)}) %collective-permute-start.16) | collective-permute-done | bytes 4128 | tf_op jit(solution)/shard_map/ppermute | solution.py:32
  43.7 2.2 %collective-permute-start.17 = (bf16[4,512]{1,0:T(4,128)(2,1)S(1)}, bf16[4,512]{1,0:T(4,128)(2,1)S(1)}, u32[]{:S(2)}, u32[]{:S(2)}) collective-permute-start(bf16[4,512]{1,0:T(4,128)(2,1)S(1)} %get-tuple-element.65), channel_id=1, source_target_pairs={{0,8},{1,9},{2,10},{3,11},{4,12},{5,13},{6,14},{7,15},{8,0},{9,1},... | collective-permute-start | bytes 12296 | tf_op jit(solution)/shard_map/ppermute | solution.py:32
  45.9 1.3 %collective-permute-start.18 = (bf16[4,512]{1,0:T(4,128)(2,1)S(1)}, bf16[4,512]{1,0:T(4,128)(2,1)S(1)}, u32[]{:S(2)}, u32[]{:S(2)}) collective-permute-start(bf16[4,512]{1,0:T(4,128)(2,1)S(1)} %get-tuple-element.66), channel_id=1, source_target_pairs={{0,12},{1,13},{2,14},{3,15},{4,8},{5,9},{6,10},{7,11},{8,4},{9,5},... | collective-permute-start | bytes 12296 | tf_op jit(solution)/shard_map/ppermute | solution.py:32
  48.3 3.0 %collective-permute-done.18.refs_3_ = bf16[4,512]{1,0:T(4,128)(2,1)S(1)} collective-permute-done((bf16[4,512]{1,0:T(4,128)(2,1)S(1)}, bf16[4,512]{1,0:T(4,128)(2,1)S(1)}, u32[]{:S(2)}, u32[]{:S(2)}) %collective-permute-start.18) | collective-permute-done | bytes 4128 | tf_op jit(solution)/shard_map/ppermute | solution.py:32
  52.6 1.9 %collective-permute-start.22 = (bf16[4,512]{1,0:T(4,128)(2,1)S(1)}, bf16[4,512]{1,0:T(4,128)(2,1)S(1)}, u32[]{:S(2)}, u32[]{:S(2)}) collective-permute-start(bf16[4,512]{1,0:T(4,128)(2,1)S(1)} %get-tuple-element.71), channel_id=1, source_target_pairs={{0,8},{1,9},{2,10},{3,11},{4,12},{5,13},{6,14},{7,15},{8,0},{9,1},... | collective-permute-start | bytes 12296 | tf_op jit(solution)/shard_map/ppermute | solution.py:32
  54.5 2.5 %collective-permute-start.23 = (bf16[4,512]{1,0:T(4,128)(2,1)S(1)}, bf16[4,512]{1,0:T(4,128)(2,1)S(1)}, u32[]{:S(2)}, u32[]{:S(2)}) collective-permute-start(bf16[4,512]{1,0:T(4,128)(2,1)S(1)} %get-tuple-element.72), channel_id=1, source_target_pairs={{0,12},{1,13},{2,14},{3,15},{4,8},{5,9},{6,10},{7,11},{8,4},{9,5},... | collective-permute-start | bytes 12296 | tf_op jit(solution)/shard_map/ppermute | solution.py:32
  57.2 2.7 %collective-permute-done.23.refs_3_ = bf16[4,512]{1,0:T(4,128)(2,1)S(1)} collective-permute-done((bf16[4,512]{1,0:T(4,128)(2,1)S(1)}, bf16[4,512]{1,0:T(4,128)(2,1)S(1)}, u32[]{:S(2)}, u32[]{:S(2)}) %collective-permute-start.23) | collective-permute-done | bytes 4128 | tf_op jit(solution)/shard_map/ppermute | solution.py:32
  61.2 1.4 %collective-permute-done.24.other_ref = bf16[8,8192]{1,0:T(8,128)(2,1)S(1)} collective-permute-done((bf16[8,8192]{1,0:T(8,128)(2,1)S(1)}, bf16[8,8192]{1,0:T(8,128)(2,1)S(1)}, u32[]{:S(2)}, u32[]{:S(2)}) %collective-permute-start.24) | collective-permute-done | bytes 131104 | tf_op jit(solution)/shard_map/ppermute | solution.py:32
  62.7 11.4 %all_to_all.15.parts_ref = bf16[8,8,1024]{2,1,0:T(8,128)(2,1)S(1)} all-to-all(bf16[8,8,1024]{2,1,0:T(8,128)(2,1)S(1)} %partial.2), channel_id=1, replica_groups={{0,2,4,6,8,10,12,14},{1,3,5,7,9,11,13,15},{16,18,20,22,24,26,28,30},{17..., dimensions={0} | all-to-all | bytes 262144 | tf_op jit(solution)/shard_map/all_to_all | solution.py:45
  74.5 9.8 %all_to_all.16.own_ref = bf16[8,8,1024]{2,1,0:T(8,128)(2,1)S(1)} all-to-all(bf16[8,8,1024]{2,1,0:T(8,128)(2,1)S(1)} %get-tuple-element.76), channel_id=1, replica_groups={{0,2,4,6,8,10,12,14},{1,3,5,7,9,11,13,15},{16,18,20,22,24,26,28,30},{17..., dimensions={0} | all-to-all | bytes 262144 | tf_op jit(solution)/shard_map/all_to_all | solution.py:45
  84.3 1.3 %collective-permute-done.25.other_ref = bf16[8,8,1024]{2,1,0:T(8,128)(2,1)S(1)} collective-permute-done((bf16[8,8,1024]{2,1,0:T(8,128)(2,1)S(1)}, bf16[8,8,1024]{2,1,0:T(8,128)(2,1)S(1)}, u32[]{:S(2)}, u32[]{:S(2)}) %collective-permute-start.25) | collective-permute-done | bytes 131104 | tf_op jit(solution)/shard_map/ppermute | solution.py:32
  86.8 1.8 %collective-permute-start.27 = (bf16[16,256]{1,0:T(8,128)(2,1)S(1)}, bf16[16,256]{1,0:T(8,128)(2,1)S(1)}, u32[]{:S(2)}, u32[]{:S(2)}) collective-permute-start(bf16[16,256]{1,0:T(8,128)(2,1)S(1)} %get-tuple-element.77.refs_0_), channel_id=1, source_target_pairs={{0,2},{1,3},{2,0},{3,1},{4,6},{5,7},{6,4},{7,5},{8,10},{9,11},{10,... | collective-permute-start | bytes 24584 | tf_op jit(solution)/shard_map/ppermute | solution.py:32
  90.5 1.4 %collective-permute-start.31 = (bf16[16,640]{1,0:T(8,128)(2,1)S(1)}, bf16[16,640]{1,0:T(8,128)(2,1)S(1)}, u32[]{:S(2)}, u32[]{:S(2)}) collective-permute-start(bf16[16,640]{1,0:T(8,128)(2,1)S(1)} %sum.3.refs_0_.refs_4_), channel_id=1, source_target_pairs={{0,12},{1,13},{2,14},{3,15},{4,8},{5,9},{6,10},{7,11},{8,4},{9,5},... | collective-permute-start | bytes 61448 | tf_op jit(solution)/shard_map/ppermute | solution.py:32
  93.0 1.9 %collective-permute-start.29 = (bf16[16,640]{1,0:T(8,128)(2,1)S(1)}, bf16[16,640]{1,0:T(8,128)(2,1)S(1)}, u32[]{:S(2)}, u32[]{:S(2)}) collective-permute-start(bf16[16,640]{1,0:T(8,128)(2,1)S(1)} %sum.3.refs_0_.refs_4_), channel_id=1, source_target_pairs={{0,4},{1,5},{2,6},{3,7},{4,0},{5,1},{6,2},{7,3},{8,12},{9,13},{10,... | collective-permute-start | bytes 61448 | tf_op jit(solution)/shard_map/ppermute | solution.py:32
  97.3 2.0 %collective-permute-start.32 = (bf16[4,512]{1,0:T(4,128)(2,1)S(1)}, bf16[4,512]{1,0:T(4,128)(2,1)S(1)}, u32[]{:S(2)}, u32[]{:S(2)}) collective-permute-start(bf16[4,512]{1,0:T(4,128)(2,1)S(1)} %get-tuple-element.80), channel_id=1, source_target_pairs={{0,4},{1,5},{2,6},{3,7},{4,0},{5,1},{6,2},{7,3},{8,12},{9,13},{10,... | collective-permute-start | bytes 12296 | tf_op jit(solution)/shard_map/ppermute | solution.py:32
  100.2 1.6 %collective-permute-start.34 = (bf16[4,512]{1,0:T(4,128)(2,1)S(1)}, bf16[4,512]{1,0:T(4,128)(2,1)S(1)}, u32[]{:S(2)}, u32[]{:S(2)}) collective-permute-start(bf16[4,512]{1,0:T(4,128)(2,1)S(1)} %get-tuple-element.82), channel_id=1, source_target_pairs={{0,12},{1,13},{2,14},{3,15},{4,8},{5,9},{6,10},{7,11},{8,4},{9,5},... | collective-permute-start | bytes 12296 | tf_op jit(solution)/shard_map/ppermute | solution.py:32
  101.8 2.0 %collective-permute-done.33.refs_2_ = bf16[4,512]{1,0:T(4,128)(2,1)S(1)} collective-permute-done((bf16[4,512]{1,0:T(4,128)(2,1)S(1)}, bf16[4,512]{1,0:T(4,128)(2,1)S(1)}, u32[]{:S(2)}, u32[]{:S(2)}) %collective-permute-start.33) | collective-permute-done | bytes 4128 | tf_op jit(solution)/shard_map/ppermute | solution.py:32
  103.8 1.8 %collective-permute-done.34.refs_3_ = bf16[4,512]{1,0:T(4,128)(2,1)S(1)} collective-permute-done((bf16[4,512]{1,0:T(4,128)(2,1)S(1)}, bf16[4,512]{1,0:T(4,128)(2,1)S(1)}, u32[]{:S(2)}, u32[]{:S(2)}) %collective-permute-start.34) | collective-permute-done | bytes 4128 | tf_op jit(solution)/shard_map/ppermute | solution.py:32
  105.6 1.7 %attend.3 = (bf16[4,512]{1,0:T(4,128)(2,1)S(1)}, bf16[4,512]{1,0:T(4,128)(2,1)S(1)}, bf16[4,512]{1,0:T(4,128)(2,1)S(1)}, bf16[4,512]{1,0:T(4,128)(2,1)S(1)}, f32[2,4,2,4,128]{4,3,2,1,0:T(4,128)}) custom-call(bf16[4,512]{1,0:T(4,128)(2,1)S(1)} %get-tuple-element.79.refs_0_, bf16[4,512]{1,0:T(4,128)(2,1)S(1)} %collective-permute-done.32.refs_1_, ...), custom_call_target="tpu_custom_call" | custom-call | flops 1048576 | bytes 4194304 | tf_op jit(solution)/shard_map/attend/pallas_call | solution.py:53
  107.3 2.1 %collective-permute-start.36 = (bf16[4,512]{1,0:T(4,128)(2,1)S(1)}, bf16[4,512]{1,0:T(4,128)(2,1)S(1)}, u32[]{:S(2)}, u32[]{:S(2)}) collective-permute-start(bf16[4,512]{1,0:T(4,128)(2,1)S(1)} %get-tuple-element.86), channel_id=1, source_target_pairs={{0,8},{1,9},{2,10},{3,11},{4,12},{5,13},{6,14},{7,15},{8,0},{9,1},... | collective-permute-start | bytes 12296 | tf_op jit(solution)/shard_map/ppermute | solution.py:32
  109.4 2.3 %collective-permute-start.37 = (bf16[4,512]{1,0:T(4,128)(2,1)S(1)}, bf16[4,512]{1,0:T(4,128)(2,1)S(1)}, u32[]{:S(2)}, u32[]{:S(2)}) collective-permute-start(bf16[4,512]{1,0:T(4,128)(2,1)S(1)} %get-tuple-element.87), channel_id=1, source_target_pairs={{0,12},{1,13},{2,14},{3,15},{4,8},{5,9},{6,10},{7,11},{8,4},{9,5},... | collective-permute-start | bytes 12296 | tf_op jit(solution)/shard_map/ppermute | solution.py:32
  111.8 3.0 %collective-permute-done.37.refs_3_ = bf16[4,512]{1,0:T(4,128)(2,1)S(1)} collective-permute-done((bf16[4,512]{1,0:T(4,128)(2,1)S(1)}, bf16[4,512]{1,0:T(4,128)(2,1)S(1)}, u32[]{:S(2)}, u32[]{:S(2)}) %collective-permute-start.37) | collective-permute-done | bytes 4128 | tf_op jit(solution)/shard_map/ppermute | solution.py:32
  116.1 1.4 %collective-permute-done.38.other_ref = bf16[8,8192]{1,0:T(8,128)(2,1)S(1)} collective-permute-done((bf16[8,8192]{1,0:T(8,128)(2,1)S(1)}, bf16[8,8192]{1,0:T(8,128)(2,1)S(1)}, u32[]{:S(2)}, u32[]{:S(2)}) %collective-permute-start.38) | collective-permute-done | bytes 131104 | tf_op jit(solution)/shard_map/ppermute | solution.py:32
  117.7 11.8 %all_to_all.17.parts_ref = bf16[8,8,1024]{2,1,0:T(8,128)(2,1)S(1)} all-to-all(bf16[8,8,1024]{2,1,0:T(8,128)(2,1)S(1)} %partial.3), channel_id=1, replica_groups={{0,2,4,6,8,10,12,14},{1,3,5,7,9,11,13,15},{16,18,20,22,24,26,28,30},{17..., dimensions={0} | all-to-all | bytes 262144 | tf_op jit(solution)/shard_map/all_to_all | solution.py:45
  (87 shorter events, 28.5 us)
Async XLA Ops:
  3.0 4.8 %collective-permute-start.2 = (bf16[1,8320]{1,0:T(2,128)(2,1)S(1)}, bf16[1,8320]{1,0:T(2,128)(2,1)S(1)}, u32[]{:S(2)}, u32[]{:S(2)}) collective-permute-start(bf16[1,8320]{1,0:T(2,128)(2,1)S(1)} %get-tuple-element.48.refs_0_), channel_id=1, source_target_pairs={{0,3},{1,2},{2,1},{3,0},{4,7},{5,6},{6,5},{7,4},{8,11},{9,10},{10,... | collective-permute-start | bytes 49928 | tf_op jit(solution)/shard_map/ppermute | solution.py:32
  5.4 4.0 %collective-permute-start.1 = (bf16[1,8320]{1,0:T(2,128)(2,1)S(1)}, bf16[1,8320]{1,0:T(2,128)(2,1)S(1)}, u32[]{:S(2)}, u32[]{:S(2)}) collective-permute-start(bf16[1,8320]{1,0:T(2,128)(2,1)S(1)} %get-tuple-element.48.refs_0_), channel_id=1, source_target_pairs={{0,2},{1,3},{2,0},{3,1},{4,6},{5,7},{6,4},{7,5},{8,10},{9,11},{10,... | collective-permute-start | bytes 49928 | tf_op jit(solution)/shard_map/ppermute | solution.py:32
  6.0 3.3 %collective-permute-start = (bf16[1,8320]{1,0:T(2,128)(2,1)S(1)}, bf16[1,8320]{1,0:T(2,128)(2,1)S(1)}, u32[]{:S(2)}, u32[]{:S(2)}) collective-permute-start(bf16[1,8320]{1,0:T(2,128)(2,1)S(1)} %get-tuple-element.48.refs_0_), channel_id=1, source_target_pairs={{0,1},{1,0},{2,3},{3,2},{4,5},{5,4},{6,7},{7,6},{8,9},{9,8},{10,11... | collective-permute-start | bytes 49928 | tf_op jit(solution)/shard_map/ppermute | solution.py:32
  9.5 14.2 %collective-permute-start.7 = (bf16[2,2,512,128]{3,2,1,0:T(8,128)(2,1)S(1)}, bf16[2,2,512,128]{3,2,1,0:T(8,128)(2,1)S(1)}, u32[]{:S(2)}, u32[]{:S(2)}) collective-permute-start(bf16[2,2,512,128]{3,2,1,0:T(8,128)(2,1)S(1)} %gate.7.refs_10_.refs_11_), channel_id=1, source_target_pairs={{0,1},{1,0},{2,3},{3,2},{4,5},{5,4},{6,7},{7,6},{8,9},{9,8},{10,11... | collective-permute-start | bytes 1572872 | tf_op jit(solution)/shard_map/ppermute | solution.py:32
  9.6 14.3 %collective-permute-start.6 = (bf16[2,2,512,128]{3,2,1,0:T(8,128)(2,1)S(1)}, bf16[2,2,512,128]{3,2,1,0:T(8,128)(2,1)S(1)}, u32[]{:S(2)}, u32[]{:S(2)}) collective-permute-start(bf16[2,2,512,128]{3,2,1,0:T(8,128)(2,1)S(1)} %gate.6), channel_id=1, source_target_pairs={{0,2},{1,3},{2,0},{3,1},{4,6},{5,7},{6,4},{7,5},{8,10},{9,11},{10,... | collective-permute-start | bytes 1572872 | tf_op jit(solution)/shard_map/ppermute | solution.py:32
  10.7 13.0 %collective-permute-start.5 = (bf16[4,8320]{1,0:T(4,128)(2,1)S(1)}, bf16[4,8320]{1,0:T(4,128)(2,1)S(1)}, u32[]{:S(2)}, u32[]{:S(2)}) collective-permute-start(bf16[4,8320]{1,0:T(4,128)(2,1)S(1)} %join.1.__1_.refs_0_), channel_id=1, source_target_pairs={{0,12},{1,13},{2,14},{3,15},{4,8},{5,9},{6,10},{7,11},{8,4},{9,5},... | collective-permute-start | bytes 199688 | tf_op jit(solution)/shard_map/ppermute | solution.py:32
  14.3 9.4 %collective-permute-start.4 = (bf16[4,8320]{1,0:T(4,128)(2,1)S(1)}, bf16[4,8320]{1,0:T(4,128)(2,1)S(1)}, u32[]{:S(2)}, u32[]{:S(2)}) collective-permute-start(bf16[4,8320]{1,0:T(4,128)(2,1)S(1)} %join.1.__1_.refs_0_), channel_id=1, source_target_pairs={{0,8},{1,9},{2,10},{3,11},{4,12},{5,13},{6,14},{7,15},{8,0},{9,1},... | collective-permute-start | bytes 199688 | tf_op jit(solution)/shard_map/ppermute | solution.py:32
  14.3 9.4 %collective-permute-start.3 = (bf16[4,8320]{1,0:T(4,128)(2,1)S(1)}, bf16[4,8320]{1,0:T(4,128)(2,1)S(1)}, u32[]{:S(2)}, u32[]{:S(2)}) collective-permute-start(bf16[4,8320]{1,0:T(4,128)(2,1)S(1)} %join.1.__1_.refs_0_), channel_id=1, source_target_pairs={{0,4},{1,5},{2,6},{3,7},{4,0},{5,1},{6,2},{7,3},{8,12},{9,13},{10,... | collective-permute-start | bytes 199688 | tf_op jit(solution)/shard_map/ppermute | solution.py:32
  25.2 4.9 %collective-permute-start.11 = (bf16[2,2,512,128]{3,2,1,0:T(8,128)(2,1)S(1)}, bf16[2,2,512,128]{3,2,1,0:T(8,128)(2,1)S(1)}, u32[]{:S(2)}, u32[]{:S(2)}) collective-permute-start(bf16[2,2,512,128]{3,2,1,0:T(8,128)(2,1)S(1)} %gate.8.refs_11_.refs_12_), channel_id=1, source_target_pairs={{0,1},{1,0},{2,3},{3,2},{4,5},{5,4},{6,7},{7,6},{8,9},{9,8},{10,11... | collective-permute-start | bytes 1572872 | tf_op jit(solution)/shard_map/ppermute | solution.py:32
  25.3 4.8 %collective-permute-start.12 = (bf16[2,2,512,128]{3,2,1,0:T(8,128)(2,1)S(1)}, bf16[2,2,512,128]{3,2,1,0:T(8,128)(2,1)S(1)}, u32[]{:S(2)}, u32[]{:S(2)}) collective-permute-start(bf16[2,2,512,128]{3,2,1,0:T(8,128)(2,1)S(1)} %gate.9.refs_12_.refs_13_), channel_id=1, source_target_pairs={{0,1},{1,0},{2,3},{3,2},{4,5},{5,4},{6,7},{7,6},{8,9},{9,8},{10,11... | collective-permute-start | bytes 1572872 | tf_op jit(solution)/shard_map/ppermute | solution.py:32
  26.5 3.7 %collective-permute-start.9 = (bf16[16,256]{1,0:T(8,128)(2,1)S(1)}, bf16[16,256]{1,0:T(8,128)(2,1)S(1)}, u32[]{:S(2)}, u32[]{:S(2)}) collective-permute-start(bf16[16,256]{1,0:T(8,128)(2,1)S(1)} %get-tuple-element.57.refs_0_), channel_id=1, source_target_pairs={{0,2},{1,3},{2,0},{3,1},{4,6},{5,7},{6,4},{7,5},{8,10},{9,11},{10,... | collective-permute-start | bytes 24584 | tf_op jit(solution)/shard_map/ppermute | solution.py:32
  30.2 13.6 %collective-permute-start.19 = (bf16[2,2,512,128]{3,2,1,0:T(8,128)(2,1)S(1)}, bf16[2,2,512,128]{3,2,1,0:T(8,128)(2,1)S(1)}, u32[]{:S(2)}, u32[]{:S(2)}) collective-permute-start(bf16[2,2,512,128]{3,2,1,0:T(8,128)(2,1)S(1)} %gate.10), channel_id=1, source_target_pairs={{0,2},{1,3},{2,0},{3,1},{4,6},{5,7},{6,4},{7,5},{8,10},{9,11},{10,... | collective-permute-start | bytes 1572872 | tf_op jit(solution)/shard_map/ppermute | solution.py:32
  31.3 5.6 %collective-permute-start.15 = (bf16[16,640]{1,0:T(8,128)(2,1)S(1)}, bf16[16,640]{1,0:T(8,128)(2,1)S(1)}, u32[]{:S(2)}, u32[]{:S(2)}) collective-permute-start(bf16[16,640]{1,0:T(8,128)(2,1)S(1)} %sum.2.refs_0_.__1_.refs_4_), channel_id=1, source_target_pairs={{0,12},{1,13},{2,14},{3,15},{4,8},{5,9},{6,10},{7,11},{8,4},{9,5},... | collective-permute-start | bytes 61448 | tf_op jit(solution)/shard_map/ppermute | solution.py:32
  34.9 4.7 %collective-permute-start.14 = (bf16[16,640]{1,0:T(8,128)(2,1)S(1)}, bf16[16,640]{1,0:T(8,128)(2,1)S(1)}, u32[]{:S(2)}, u32[]{:S(2)}) collective-permute-start(bf16[16,640]{1,0:T(8,128)(2,1)S(1)} %sum.2.refs_0_.__1_.refs_4_), channel_id=1, source_target_pairs={{0,8},{1,9},{2,10},{3,11},{4,12},{5,13},{6,14},{7,15},{8,0},{9,1},... | collective-permute-start | bytes 61448 | tf_op jit(solution)/shard_map/ppermute | solution.py:32
  34.9 4.7 %collective-permute-start.13 = (bf16[16,640]{1,0:T(8,128)(2,1)S(1)}, bf16[16,640]{1,0:T(8,128)(2,1)S(1)}, u32[]{:S(2)}, u32[]{:S(2)}) collective-permute-start(bf16[16,640]{1,0:T(8,128)(2,1)S(1)} %sum.2.refs_0_.__1_.refs_4_), channel_id=1, source_target_pairs={{0,4},{1,5},{2,6},{3,7},{4,0},{5,1},{6,2},{7,3},{8,12},{9,13},{10,... | collective-permute-start | bytes 61448 | tf_op jit(solution)/shard_map/ppermute | solution.py:32
  40.1 3.7 %collective-permute-start.16 = (bf16[4,512]{1,0:T(4,128)(2,1)S(1)}, bf16[4,512]{1,0:T(4,128)(2,1)S(1)}, u32[]{:S(2)}, u32[]{:S(2)}) collective-permute-start(bf16[4,512]{1,0:T(4,128)(2,1)S(1)} %get-tuple-element.64), channel_id=1, source_target_pairs={{0,4},{1,5},{2,6},{3,7},{4,0},{5,1},{6,2},{7,3},{8,12},{9,13},{10,... | collective-permute-start | bytes 12296 | tf_op jit(solution)/shard_map/ppermute | solution.py:32
  43.7 7.6 %collective-permute-start.20 = (bf16[2,2,512,128]{3,2,1,0:T(8,128)(2,1)S(1)}, bf16[2,2,512,128]{3,2,1,0:T(8,128)(2,1)S(1)}, u32[]{:S(2)}, u32[]{:S(2)}) collective-permute-start(bf16[2,2,512,128]{3,2,1,0:T(8,128)(2,1)S(1)} %gate.11.refs_13_.refs_14_), channel_id=1, source_target_pairs={{0,1},{1,0},{2,3},{3,2},{4,5},{5,4},{6,7},{7,6},{8,9},{9,8},{10,11... | collective-permute-start | bytes 1572872 | tf_op jit(solution)/shard_map/ppermute | solution.py:32
  43.7 4.6 %collective-permute-start.17 = (bf16[4,512]{1,0:T(4,128)(2,1)S(1)}, bf16[4,512]{1,0:T(4,128)(2,1)S(1)}, u32[]{:S(2)}, u32[]{:S(2)}) collective-permute-start(bf16[4,512]{1,0:T(4,128)(2,1)S(1)} %get-tuple-element.65), channel_id=1, source_target_pairs={{0,8},{1,9},{2,10},{3,11},{4,12},{5,13},{6,14},{7,15},{8,0},{9,1},... | collective-permute-start | bytes 12296 | tf_op jit(solution)/shard_map/ppermute | solution.py:32
  45.9 5.4 %collective-permute-start.18 = (bf16[4,512]{1,0:T(4,128)(2,1)S(1)}, bf16[4,512]{1,0:T(4,128)(2,1)S(1)}, u32[]{:S(2)}, u32[]{:S(2)}) collective-permute-start(bf16[4,512]{1,0:T(4,128)(2,1)S(1)} %get-tuple-element.66), channel_id=1, source_target_pairs={{0,12},{1,13},{2,14},{3,15},{4,8},{5,9},{6,10},{7,11},{8,4},{9,5},... | collective-permute-start | bytes 12296 | tf_op jit(solution)/shard_map/ppermute | solution.py:32
  52.5 4.5 %collective-permute-start.21 = (bf16[4,512]{1,0:T(4,128)(2,1)S(1)}, bf16[4,512]{1,0:T(4,128)(2,1)S(1)}, u32[]{:S(2)}, u32[]{:S(2)}) collective-permute-start(bf16[4,512]{1,0:T(4,128)(2,1)S(1)} %get-tuple-element.70), channel_id=1, source_target_pairs={{0,4},{1,5},{2,6},{3,7},{4,0},{5,1},{6,2},{7,3},{8,12},{9,13},{10,... | collective-permute-start | bytes 12296 | tf_op jit(solution)/shard_map/ppermute | solution.py:32
  52.6 4.6 %collective-permute-start.22 = (bf16[4,512]{1,0:T(4,128)(2,1)S(1)}, bf16[4,512]{1,0:T(4,128)(2,1)S(1)}, u32[]{:S(2)}, u32[]{:S(2)}) collective-permute-start(bf16[4,512]{1,0:T(4,128)(2,1)S(1)} %get-tuple-element.71), channel_id=1, source_target_pairs={{0,8},{1,9},{2,10},{3,11},{4,12},{5,13},{6,14},{7,15},{8,0},{9,1},... | collective-permute-start | bytes 12296 | tf_op jit(solution)/shard_map/ppermute | solution.py:32
  54.5 5.4 %collective-permute-start.23 = (bf16[4,512]{1,0:T(4,128)(2,1)S(1)}, bf16[4,512]{1,0:T(4,128)(2,1)S(1)}, u32[]{:S(2)}, u32[]{:S(2)}) collective-permute-start(bf16[4,512]{1,0:T(4,128)(2,1)S(1)} %get-tuple-element.72), channel_id=1, source_target_pairs={{0,12},{1,13},{2,14},{3,15},{4,8},{5,9},{6,10},{7,11},{8,4},{9,5},... | collective-permute-start | bytes 12296 | tf_op jit(solution)/shard_map/ppermute | solution.py:32
  86.8 3.7 %collective-permute-start.27 = (bf16[16,256]{1,0:T(8,128)(2,1)S(1)}, bf16[16,256]{1,0:T(8,128)(2,1)S(1)}, u32[]{:S(2)}, u32[]{:S(2)}) collective-permute-start(bf16[16,256]{1,0:T(8,128)(2,1)S(1)} %get-tuple-element.77.refs_0_), channel_id=1, source_target_pairs={{0,2},{1,3},{2,0},{3,1},{4,6},{5,7},{6,4},{7,5},{8,10},{9,11},{10,... | collective-permute-start | bytes 24584 | tf_op jit(solution)/shard_map/ppermute | solution.py:32
  90.5 5.6 %collective-permute-start.31 = (bf16[16,640]{1,0:T(8,128)(2,1)S(1)}, bf16[16,640]{1,0:T(8,128)(2,1)S(1)}, u32[]{:S(2)}, u32[]{:S(2)}) collective-permute-start(bf16[16,640]{1,0:T(8,128)(2,1)S(1)} %sum.3.refs_0_.refs_4_), channel_id=1, source_target_pairs={{0,12},{1,13},{2,14},{3,15},{4,8},{5,9},{6,10},{7,11},{8,4},{9,5},... | collective-permute-start | bytes 61448 | tf_op jit(solution)/shard_map/ppermute | solution.py:32
  91.9 4.7 %collective-permute-start.30 = (bf16[16,640]{1,0:T(8,128)(2,1)S(1)}, bf16[16,640]{1,0:T(8,128)(2,1)S(1)}, u32[]{:S(2)}, u32[]{:S(2)}) collective-permute-start(bf16[16,640]{1,0:T(8,128)(2,1)S(1)} %sum.3.refs_0_.refs_4_), channel_id=1, source_target_pairs={{0,8},{1,9},{2,10},{3,11},{4,12},{5,13},{6,14},{7,15},{8,0},{9,1},... | collective-permute-start | bytes 61448 | tf_op jit(solution)/shard_map/ppermute | solution.py:32
  93.0 3.8 %collective-permute-start.29 = (bf16[16,640]{1,0:T(8,128)(2,1)S(1)}, bf16[16,640]{1,0:T(8,128)(2,1)S(1)}, u32[]{:S(2)}, u32[]{:S(2)}) collective-permute-start(bf16[16,640]{1,0:T(8,128)(2,1)S(1)} %sum.3.refs_0_.refs_4_), channel_id=1, source_target_pairs={{0,4},{1,5},{2,6},{3,7},{4,0},{5,1},{6,2},{7,3},{8,12},{9,13},{10,... | collective-permute-start | bytes 61448 | tf_op jit(solution)/shard_map/ppermute | solution.py:32
  97.3 4.5 %collective-permute-start.32 = (bf16[4,512]{1,0:T(4,128)(2,1)S(1)}, bf16[4,512]{1,0:T(4,128)(2,1)S(1)}, u32[]{:S(2)}, u32[]{:S(2)}) collective-permute-start(bf16[4,512]{1,0:T(4,128)(2,1)S(1)} %get-tuple-element.80), channel_id=1, source_target_pairs={{0,4},{1,5},{2,6},{3,7},{4,0},{5,1},{6,2},{7,3},{8,12},{9,13},{10,... | collective-permute-start | bytes 12296 | tf_op jit(solution)/shard_map/ppermute | solution.py:32
  99.3 4.5 %collective-permute-start.33 = (bf16[4,512]{1,0:T(4,128)(2,1)S(1)}, bf16[4,512]{1,0:T(4,128)(2,1)S(1)}, u32[]{:S(2)}, u32[]{:S(2)}) collective-permute-start(bf16[4,512]{1,0:T(4,128)(2,1)S(1)} %get-tuple-element.81), channel_id=1, source_target_pairs={{0,8},{1,9},{2,10},{3,11},{4,12},{5,13},{6,14},{7,15},{8,0},{9,1},... | collective-permute-start | bytes 12296 | tf_op jit(solution)/shard_map/ppermute | solution.py:32
  100.2 5.4 %collective-permute-start.34 = (bf16[4,512]{1,0:T(4,128)(2,1)S(1)}, bf16[4,512]{1,0:T(4,128)(2,1)S(1)}, u32[]{:S(2)}, u32[]{:S(2)}) collective-permute-start(bf16[4,512]{1,0:T(4,128)(2,1)S(1)} %get-tuple-element.82), channel_id=1, source_target_pairs={{0,12},{1,13},{2,14},{3,15},{4,8},{5,9},{6,10},{7,11},{8,4},{9,5},... | collective-permute-start | bytes 12296 | tf_op jit(solution)/shard_map/ppermute | solution.py:32
  107.3 4.4 %collective-permute-start.35 = (bf16[4,512]{1,0:T(4,128)(2,1)S(1)}, bf16[4,512]{1,0:T(4,128)(2,1)S(1)}, u32[]{:S(2)}, u32[]{:S(2)}) collective-permute-start(bf16[4,512]{1,0:T(4,128)(2,1)S(1)} %get-tuple-element.85), channel_id=1, source_target_pairs={{0,4},{1,5},{2,6},{3,7},{4,0},{5,1},{6,2},{7,3},{8,12},{9,13},{10,... | collective-permute-start | bytes 12296 | tf_op jit(solution)/shard_map/ppermute | solution.py:32
  107.3 4.5 %collective-permute-start.36 = (bf16[4,512]{1,0:T(4,128)(2,1)S(1)}, bf16[4,512]{1,0:T(4,128)(2,1)S(1)}, u32[]{:S(2)}, u32[]{:S(2)}) collective-permute-start(bf16[4,512]{1,0:T(4,128)(2,1)S(1)} %get-tuple-element.86), channel_id=1, source_target_pairs={{0,8},{1,9},{2,10},{3,11},{4,12},{5,13},{6,14},{7,15},{8,0},{9,1},... | collective-permute-start | bytes 12296 | tf_op jit(solution)/shard_map/ppermute | solution.py:32
  109.4 5.4 %collective-permute-start.37 = (bf16[4,512]{1,0:T(4,128)(2,1)S(1)}, bf16[4,512]{1,0:T(4,128)(2,1)S(1)}, u32[]{:S(2)}, u32[]{:S(2)}) collective-permute-start(bf16[4,512]{1,0:T(4,128)(2,1)S(1)} %get-tuple-element.87), channel_id=1, source_target_pairs={{0,12},{1,13},{2,14},{3,15},{4,8},{5,9},{6,10},{7,11},{8,4},{9,5},... | collective-permute-start | bytes 12296 | tf_op jit(solution)/shard_map/ppermute | solution.py:32
  (12 other events, 49.0 us)

commit v12 on v10

--- a/solution.py
+++ b/solution.py
@@ -86,18 +86,10 @@
     return jnp.concatenate([lines[i : i + 1] for i in range(lines.shape[0])], axis=1)
 
 
-def folded(out_ref, row):
-    wide = row.shape[1] // FOLD
-    for k in range(out_ref.shape[0]):
-        for i in range(FOLD):
-            out_ref[k, i : i + 1, :wide] = row[:, i * wide : (i + 1) * wide].astype(out_ref.dtype)
-
-
-def first_kernel(hidden_ref, scale_ref, adapter_ref, length_ref, _, out_ref, length_out):
+def first_kernel(hidden_ref, adapter_ref, length_ref, _, out_ref, length_out):
     length_out[...] = jnp.full(length_out.shape, length_ref[0], jnp.int32)
     width = hidden_ref.shape[1]
-    hidden = hidden_ref[...].astype(jnp.float32)
-    out_ref[:, :width] = normalized(hidden, row_of(scale_ref))
+    out_ref[:, :width] = hidden_ref[...]
     digit = iota((1, LANES), 1)
     adapter = adapter_ref[0]
     high, low = adapter // 256, adapter % 256
@@ -157,21 +149,65 @@
     low_terms(held, member_ref, down_ref, rows_ref, low_ref)
 
 
-def low_later_kernel(own_ref, other_ref, me_ref, member_ref, down_ref, rows_ref, low_ref, held):
-    core = me_ref[0] % CORES
-    for ref, flip in ((own_ref, 0), (other_ref, 1)):
-        wide = ref.shape[2]
-        for k in range(ref.shape[0]):
-            block = ref[k].astype(jnp.float32)
-            row = pl.ds(k * CORES + (core ^ flip), 1)
-            for i in range(FOLD):
-                held[row, i * wide : (i + 1) * wide] = block[i : i + 1]
+def low_later_kernel(near, far, own_ref, other_ref, me_ref, member_ref, down_ref, rows_ref, low_ref, held):
+    half = own_ref.shape[0]
+    for start, ref in ((0, own_ref), (half, other_ref)):
+        block = ref[...].astype(jnp.float32)
+        for k in range(half):
+            row = me_ref[0] ^ distance(start + k, near, far)
+            held[pl.ds(row, 1), :] = block[k : k + 1]
     low_terms(held, member_ref, down_ref, rows_ref, low_ref)
 
 
 def join_kernel(amount, *refs):
+    scale_ref, _, hidden_ref, out_ref = refs[amount:]
+    width = hidden_ref.shape[1]
     rows = [ref[...].astype(jnp.float32) for ref in refs[:amount]]
+    rows = jnp.concatenate(rows, axis=0)
+    hidden = rows[:, :width]
+    hidden_ref[...] = hidden.astype(jnp.bfloat16)
+    out_ref[:, :width] = normalized(hidden, row_of(scale_ref))
+    out_ref[:, width:] = rows[:, width:].astype(jnp.bfloat16)
+
+
+def stack_kernel(*refs):
+    rows = [ref[...].astype(jnp.float32) for ref in refs[:-1]]
     refs[-1][...] = jnp.concatenate(rows, axis=0).astype(refs[-1].dtype)
+
+
+def distance(slot, near, far):
+    size, total = near * far, (slot % far) * near
+    bit = 1
+    while bit < near:
+        size //= 2
+        total = total + ((slot // size) % 2) * bit
+        bit *= 2
+    return total
+
+
+def fold_kernel(own_ref, other_ref, keep_ref, away_ref):
+    total = own_ref[...] + other_ref[...].astype(jnp.float32)
+    half = keep_ref.shape[0]
+    keep_ref[...] = total[:half]
+    away_ref[...] = total[half:].astype(jnp.bfloat16)
+
+
+def folded_kernel(own_ref, other_ref, out_ref):
+    out_ref[...] = (own_ref[...] + other_ref[...].astype(jnp.float32)).astype(jnp.bfloat16)
+
+
+def next_kernel(far, *refs):
+    pieces, (hidden_ref, scale_ref, own_ref, out_ref) = refs[:far], refs[far:]
+    sums = []
+    for k in range(far):
+        piece = pieces[k][...].astype(jnp.float32)
+        sums.append(jnp.concatenate([piece[j ^ k : (j ^ k) + 1] for j in range(far)], axis=0))
+    while len(sums) > 1:
+        sums = [sums[i] + sums[i + 1] for i in range(0, len(sums), 2)]
+    total = sums[0].astype(jnp.bfloat16).astype(jnp.float32)
+    hidden = (hidden_ref[...].astype(jnp.float32) + total).astype(jnp.bfloat16)
+    own_ref[...] = hidden.astype(jnp.float32)[:1].astype(jnp.bfloat16)
+    out_ref[...] = normalized(hidden.astype(jnp.float32), row_of(scale_ref))
 
 
 def sum_kernel(*refs):
@@ -317,13 +353,16 @@
             out_ref[k] = out[k : k + 1].astype(jnp.bfloat16)
 
 
-def output_kernel(lines_ref, me_ref, weight_ref, own_ref, away_ref, held):
+def output_kernel(split, lines_ref, me_ref, weight_ref, own_ref, away_ref, held):
     count, each, line = lines_ref.shape
     chips = count // CORES
     for k in range(count):
         held[k, :each, :] = lines_ref[k].astype(jnp.float32)
     slot = iota((count, count), 0)
-    origin = (slot % chips) * CORES + ((me_ref[0] % CORES) ^ (slot // chips))
+    if split:
+        origin = me_ref[0] ^ distance(slot, *split)
+    else:
+        origin = (slot % chips) * CORES + ((me_ref[0] % CORES) ^ (slot // chips))
     order = (iota((count, count), 1) == origin).astype(jnp.bfloat16)
     rows = jnp.concatenate(
         [dot(order, held[:, c, :].astype(jnp.bfloat16)).astype(jnp.bfloat16) for c in range(each)],
@@ -348,19 +387,14 @@
             )
 
 
-def finish_kernel(last, parts_ref, hidden_ref, scale_ref, out_ref, *spread):
+def finish_kernel(parts_ref, hidden_ref, out_ref):
     total = parts_ref[0].astype(jnp.float32)
     for k in range(1, parts_ref.shape[0]):
         total = total + parts_ref[k].astype(jnp.float32)
     total = jnp.concatenate([total[i : i + 1] for i in range(FOLD)], axis=1)
     total = total.astype(jnp.bfloat16).astype(jnp.float32)
     before = hidden_ref[...].astype(jnp.float32)
-    hidden = (before + total).astype(jnp.bfloat16).astype(jnp.float32)
-    if last:
-        out_ref[...] = jnp.concatenate([before, hidden], axis=0).astype(jnp.bfloat16)
-    else:
-        out_ref[...] = hidden.astype(jnp.bfloat16)
-        folded(spread[0], normalized(hidden, row_of(scale_ref)).astype(jnp.float32))
+    out_ref[...] = jnp.concatenate([before, before + total], axis=0).astype(jnp.bfloat16)
 
 
 def shards(
@@ -410,11 +444,10 @@
         first_kernel, [shape((1, width + LANES)), shape((8, LANES), jnp.int32)], "first"
     )(
         hidden,
-        scale,
         row_adapter_index,
         cache_length_per_row,
         me,
-        specs=[vmem, vmem, smem, smem, smem],
+        specs=[vmem, smem, smem, smem],
     )
     past = ()
     for step in range(STEPS):
@@ -425,9 +458,11 @@
             early = [query_weight, key_value_weight, down]
             (query_w, fresh_w, down_w), token = stash(length, early)
             pieces = across(carried, far_steps, count)
-            (carried,) = call(
-                functools.partial(join_kernel, far), [shape((far, width + LANES))], "join"
-            )(*pieces, token)
+            column, carried = call(
+                functools.partial(join_kernel, far),
+                [shape((far, width)), shape((far, width + LANES))],
+                "join",
+            )(*pieces, scale, token)
             later = [output_weight, key_value_cache, adapter_up_weight]
             (output_w, cache, up_w), token = stash(token, later)
             pieces = across(carried, near_steps, count)
@@ -441,9 +476,13 @@
                 functools.partial(low_first_kernel, near, far), outs, "low", scratch
             )(*pieces, me, member, down_w, specs=[vmem] * near + [smem, vmem, vmem])
         else:
-            own = chips_swap(carried, count)
-            rows, low = call(low_later_kernel, outs, "low", scratch)(
-                own, shift(own, 1, count), me, member, down_w, specs=[vmem, vmem, smem, vmem, vmem]
+            rows, low = call(functools.partial(low_later_kernel, near, far), outs, "low", scratch)(
+                carried,
+                shift(carried, 1, count),
+                me,
+                member,
+                down_w,
+                specs=[vmem, vmem, smem, vmem, vmem],
             )
         (low,) = call(sum_kernel, [shape((count, rank))], "sum")(*across(low, near_steps, count))
         lows = across(low, far_steps, count)
@@ -486,7 +525,7 @@
 
         lines = swap(outs[0])
         own, away = call(
-            output_kernel,
+            functools.partial(output_kernel, None if last else (near, far)),
             [shape((chips, width), jnp.float32), shape((chips, width))],
             "output",
             [pltpu.VMEM((count, 8, line), jnp.float32)],
@@ -494,17 +533,29 @@
             moved=2 * width * columns,
         )(lines, me, output_w, specs=[vmem, smem, vmem])
 
-        (parts,) = call(partial_kernel, [shape((chips, FOLD, width // FOLD))], "partial")(
-            own, shift(away, 1, count)
-        )
-        parts = chips_swap(parts, count)
-        outs = [shape((2 if last else 1, width))]
-        if not last:
-            outs = outs + [shape((chips, FOLD, width // FOLD))]
-        outs = call(functools.partial(finish_kernel, last), outs, "finish")(parts, hidden, scale)
         if last:
-            return outs[0].reshape(STEPS, 1, width)
-        hidden, carried = outs
+            (parts,) = call(partial_kernel, [shape((chips, FOLD, width // FOLD))], "partial")(
+                own, shift(away, 1, count)
+            )
+            parts = chips_swap(parts, count)
+            (out,) = call(finish_kernel, [shape((STEPS, width))], "finish")(parts, hidden)
+            return out.reshape(STEPS, 1, width)
+        bit = 1
+        while bit < near // 2:
+            half = own.shape[0] // 2
+            own, away = call(
+                fold_kernel, [shape((half, width), jnp.float32), shape((half, width))], "fold"
+            )(own, shift(away, bit, count))
+            bit *= 2
+        (own,) = call(folded_kernel, [shape((far, width))], "fold")(own, shift(away, bit, count))
+        hidden, carried = call(
+            functools.partial(next_kernel, far), [shape((1, width)), shape((far, width))], "next"
+        )(*across(own, far_steps, count), column, scale)
+        while bit > 1:
+            (carried,) = call(stack_kernel, [shape((2 * carried.shape[0], width))], "stack")(
+                carried, shift(carried, bit, count)
+            )
+            bit //= 2
 
 
 def solution(mesh):

time: 125 us -> 121 us (0.968)
  blocking collectives: 69.2 us -> 49.1 us
  waiting for transfers between devices: 11.2 us -> 22.2 us
  starting transfers between devices: 20.5 us -> 26.1 us
    all_to_all x3 -> x1, blocking collectives: 29.8 us -> 9.97 us  [chips_swap(): lax.all_to_all(blocks, AXIS, split_axis=0, concat_axis=0, axis_index_grou...]
    ppermute x21 -> x26, waiting for transfers between devices: 11.2 us -> 22.2 us  [shift(): return lax.ppermute(block, AXIS, [(i, i ^ distance) for i in range(count)])]
    ppermute x21 -> x26, starting transfers between devices: 20.5 us -> 26.1 us  [shift(): return lax.ppermute(block, AXIS, [(i, i ^ distance) for i in range(count)])]
    pallas_call x21 -> x23, Pallas kernels: 20.9 us -> 21.2 us  [run(): pl.pallas_call(body, out_shape=outs, in_specs=[pl.BlockSpec(memory_space=...]
  transfers between devices with their start and end apart: 21 -> 26, of which waited for: 9 -> 13; matrix products, arithmetic and copies ran while one was open for 0% -> 0% of each run, Pallas kernels for 10% -> 10%
where the time goes in v12:
time: 121 us
  blocking collectives  49.1 us (41%)
  starting transfers between devices  26.1 us (22%)
  waiting for transfers between devices  22.2 us (18%)
  Pallas kernels  21.2 us (18%)
  between operations  1.48 us (1%)
    all_to_all x4, blocking collectives, swap(): return lax.all_to_all(blocks, AXIS, split_axis=0, concat_axis=0, tiled=True)  39.2 us
    ppermute x26, starting transfers between devices, shift(): return lax.ppermute(block, AXIS, [(i, i ^ distance) for i in range(count)])  26.1 us
    ppermute x26, waiting for transfers between devices, shift(): return lax.ppermute(block, AXIS, [(i, i ^ distance) for i in range(count)])  22.2 us
    pallas_call x23, Pallas kernels, run(): pl.pallas_call(body, out_shape=outs, in_specs=[pl.BlockSpec(memory_space=...  21.2 us
    all_to_all x1, blocking collectives, chips_swap(): lax.all_to_all(blocks, AXIS, split_axis=0, concat_axis=0, axis_index_grou...  9.97 us
  transfers between devices with their start and end apart: 26, of which 13 were waited for; matrix products, arithmetic and copies ran while one was open for 0% of the time, Pallas kernels for 10%

profile of v12, /device:TPU:0, one launch (start us, length us, event | category | flops | bytes accessed | tf_op | source)
XLA Modules:
  0.0 120.9 jit_solution(9236501129724000229)
XLA Ops:
  2.1 5.1 %collective-permute-start.2 = (bf16[1,8320]{1,0:T(2,128)(2,1)S(1)}, bf16[1,8320]{1,0:T(2,128)(2,1)S(1)}, u32[]{:S(2)}, u32[]{:S(2)}) collective-permute-start(bf16[1,8320]{1,0:T(2,128)(2,1)S(1)} %get-tuple-element.38.refs_0_), channel_id=1, source_target_pairs={{0,12},{1,13},{2,14},{3,15},{4,8},{5,9},{6,10},{7,11},{8,4},{9,5},... | collective-permute-start | bytes 49928 | tf_op jit(solution)/shard_map/ppermute | solution.py:32
  7.8 4.6 %stash.2 = (bf16[8192,512]{1,0:T(8,128)(2,1)S(1)}, bf16[8192,128]{1,0:T(8,128)(2,1)S(1)}, bf16[2,64,8192]{2,1,0:T(8,128)(2,1)S(1)}, s32[8,128]{1,0:T(8,128)S(1)}) custom-call(s32[8,128]{1,0:T(8,128)S(1)} %get-tuple-element.39.token_ref.refs_1_, bf16[8192,512]{1,0:T(8,128)(2,1)} %refs_0_.2, bf16[8192,128]{1,0:T(8,128)(2,1)} %refs_1_.2, ...), custom_call_target="tpu_custom_call" | custom-call | flops 1048576 | bytes 12582912 | tf_op jit(solution)/shard_map/stash/pallas_call | solution.py:53
  13.2 1.3 %collective-permute-start.4 = (bf16[4,8320]{1,0:T(4,128)(2,1)S(1)}, bf16[4,8320]{1,0:T(4,128)(2,1)S(1)}, u32[]{:S(2)}, u32[]{:S(2)}) collective-permute-start(bf16[4,8320]{1,0:T(4,128)(2,1)S(1)} %get-tuple-element.41.refs_0_), channel_id=1, source_target_pairs={{0,2},{1,3},{2,0},{3,1},{4,6},{5,7},{6,4},{7,5},{8,10},{9,11},{10,... | collective-permute-start | bytes 199688 | tf_op jit(solution)/shard_map/ppermute | solution.py:32
  14.8 4.6 %stash.3 = (bf16[512,8192]{1,0:T(8,128)(2,1)S(1)}, bf16[1,2,512,1024]{3,2,1,0:T(8,128)(2,1)S(1)}, bf16[32,64,512]{2,1,0:T(8,128)(2,1)S(1)}, s32[8,128]{1,0:T(8,128)S(1)}) custom-call(s32[8,128]{1,0:T(8,128)S(1)} %get-tuple-element.40.refs_5_.token_ref, bf16[512,8192]{1,0:T(8,128)(2,1)} %refs_0_.3, bf16[1,2,512,1024]{3,2,1,0:T(8,128)(2,1)} %refs_1_.3, ...), custom_call_target="tpu_custom_call" | custom-call | flops 1048576 | bytes 12582912 | tf_op jit(solution)/shard_map/stash/pallas_call | solution.py:53
  20.4 1.3 %collective-permute-start.8 = (bf16[16,64]{1,0:T(8,128)(2,1)S(1)}, bf16[16,64]{1,0:T(8,128)(2,1)S(1)}, u32[]{:S(2)}, u32[]{:S(2)}) collective-permute-start(bf16[16,64]{1,0:T(8,128)(2,1)S(1)} %get-tuple-element.45.refs_0_), channel_id=1, source_target_pairs={{0,3},{1,2},{2,1},{3,0},{4,7},{5,6},{6,5},{7,4},{8,11},{9,10},{10,... | collective-permute-start | bytes 6152 | tf_op jit(solution)/shard_map/ppermute | solution.py:32
  22.4 1.1 collective-permute-done.8.refs_3_
  23.5 1.8 %collective-permute-done.7.refs_2_ = bf16[16,64]{1,0:T(8,128)(2,1)S(1)} collective-permute-done((bf16[16,64]{1,0:T(8,128)(2,1)S(1)}, bf16[16,64]{1,0:T(8,128)(2,1)S(1)}, u32[]{:S(2)}, u32[]{:S(2)}) %collective-permute-start.7) | collective-permute-done | bytes 2080 | tf_op jit(solution)/shard_map/ppermute | solution.py:32
  25.3 3.7 %collective-permute-start.11 = (bf16[16,64]{1,0:T(8,128)(2,1)S(1)}, bf16[16,64]{1,0:T(8,128)(2,1)S(1)}, u32[]{:S(2)}, u32[]{:S(2)}) collective-permute-start(bf16[16,64]{1,0:T(8,128)(2,1)S(1)} %sum.2.refs_0_), channel_id=1, source_target_pairs={{0,12},{1,13},{2,14},{3,15},{4,8},{5,9},{6,10},{7,11},{8,4},{9,5},... | collective-permute-start | bytes 6152 | tf_op jit(solution)/shard_map/ppermute | solution.py:32
  29.7 1.5 %project.2 = (f32[16,512]{1,0:T(8,128)S(1)}, f32[16,128]{1,0:T(8,128)S(1)}) custom-call(bf16[16,8192]{1,0:T(8,128)(2,1)S(1)} %get-tuple-element.46.rows_ref, bf16[8192,512]{1,0:T(8,128)(2,1)S(1)} %get-tuple-element.47.query_w, bf16[8192,128]{1,0:T(8,128)(2,1)S(1)} %get-tuple-element.48.fresh_w), custom_call_target="tpu_custom_call" | custom-call | flops 167772160 | bytes 10485760 | tf_op jit(solution)/shard_map/project/pallas_call | solution.py:53
  31.2 2.3 %collective-permute-done.10.refs_2_ = bf16[16,64]{1,0:T(8,128)(2,1)S(1)} collective-permute-done((bf16[16,64]{1,0:T(8,128)(2,1)S(1)}, bf16[16,64]{1,0:T(8,128)(2,1)S(1)}, u32[]{:S(2)}, u32[]{:S(2)}) %collective-permute-start.10) | collective-permute-done | bytes 2080 | tf_op jit(solution)/shard_map/ppermute | solution.py:32
  34.0 10.0 %all_to_all.25.refs_0_ = bf16[16,8,128]{2,1,0:T(8,128)(2,1)S(1)} all-to-all(bf16[16,8,128]{2,1,0:T(8,128)(2,1)S(1)} %up.2), channel_id=1, replica_groups=mesh['groups'=2,'replica'=16] {'replica'}, dimensions={0} | all-to-all | bytes 65536 | tf_op jit(solution)/shard_map/all_to_all | solution.py:40
  44.8 9.1 %all_to_all.26.lines_ref = bf16[16,4,128]{2,1,0:T(4,128)(2,1)S(1)} all-to-all(bf16[16,4,128]{2,1,0:T(4,128)(2,1)S(1)} %get-tuple-element.54), channel_id=1, replica_groups=mesh['groups'=2,'replica'=16] {'replica'}, dimensions={0} | all-to-all | bytes 32768 | tf_op jit(solution)/shard_map/all_to_all | solution.py:40
  53.9 1.3 %output.2 = (f32[8,8192]{1,0:T(8,128)S(1)}, bf16[8,8192]{1,0:T(8,128)(2,1)S(1)}) custom-call(bf16[16,4,128]{2,1,0:T(4,128)(2,1)S(1)} %all_to_all.26.lines_ref, s32[1]{0:T(128)} %bitcast._.refs_4_.me_ref, bf16[512,8192]{1,0:T(8,128)(2,1)S(1)} %get-tuple-element.55.weight_ref), custom_call_target="tpu_custom_call" | custom-call | flops 134217728 | bytes 8388608 | tf_op jit(solution)/shard_map/output/pallas_call | solution.py:53
  55.2 1.4 %collective-permute-done.12.other_ref = bf16[8,8192]{1,0:T(8,128)(2,1)S(1)} collective-permute-done((bf16[8,8192]{1,0:T(8,128)(2,1)S(1)}, bf16[8,8192]{1,0:T(8,128)(2,1)S(1)}, u32[]{:S(2)}, u32[]{:S(2)}) %collective-permute-start.12) | collective-permute-done | bytes 131104 | tf_op jit(solution)/shard_map/ppermute | solution.py:32
  57.1 3.8 %collective-permute-done.13.other_ref = bf16[4,8192]{1,0:T(4,128)(2,1)S(1)} collective-permute-done((bf16[4,8192]{1,0:T(4,128)(2,1)S(1)}, bf16[4,8192]{1,0:T(4,128)(2,1)S(1)}, u32[]{:S(2)}, u32[]{:S(2)}) %collective-permute-start.13) | collective-permute-done | bytes 65568 | tf_op jit(solution)/shard_map/ppermute | solution.py:32
  61.5 1.4 %collective-permute-start.15 = (bf16[4,8192]{1,0:T(4,128)(2,1)S(1)}, bf16[4,8192]{1,0:T(4,128)(2,1)S(1)}, u32[]{:S(2)}, u32[]{:S(2)}) collective-permute-start(bf16[4,8192]{1,0:T(4,128)(2,1)S(1)} %fold.3.refs_0_), channel_id=1, source_target_pairs={{0,8},{1,9},{2,10},{3,11},{4,12},{5,13},{6,14},{7,15},{8,0},{9,1},... | collective-permute-start | bytes 196616 | tf_op jit(solution)/shard_map/ppermute | solution.py:32
  63.0 2.5 %collective-permute-start.14 = (bf16[4,8192]{1,0:T(4,128)(2,1)S(1)}, bf16[4,8192]{1,0:T(4,128)(2,1)S(1)}, u32[]{:S(2)}, u32[]{:S(2)}) collective-permute-start(bf16[4,8192]{1,0:T(4,128)(2,1)S(1)} %fold.3.refs_0_), channel_id=1, source_target_pairs={{0,4},{1,5},{2,6},{3,7},{4,0},{5,1},{6,2},{7,3},{8,12},{9,13},{10,... | collective-permute-start | bytes 196616 | tf_op jit(solution)/shard_map/ppermute | solution.py:32
  65.4 2.0 %collective-permute-done.16.refs_3_ = bf16[4,8192]{1,0:T(4,128)(2,1)S(1)} collective-permute-done((bf16[4,8192]{1,0:T(4,128)(2,1)S(1)}, bf16[4,8192]{1,0:T(4,128)(2,1)S(1)}, u32[]{:S(2)}, u32[]{:S(2)}) %collective-permute-start.16) | collective-permute-done | bytes 65568 | tf_op jit(solution)/shard_map/ppermute | solution.py:32
  67.4 1.3 %collective-permute-done.15.refs_2_ = bf16[4,8192]{1,0:T(4,128)(2,1)S(1)} collective-permute-done((bf16[4,8192]{1,0:T(4,128)(2,1)S(1)}, bf16[4,8192]{1,0:T(4,128)(2,1)S(1)}, u32[]{:S(2)}, u32[]{:S(2)}) %collective-permute-start.15) | collective-permute-done | bytes 65568 | tf_op jit(solution)/shard_map/ppermute | solution.py:32
  69.9 3.7 %collective-permute-done.17.refs_1_ = bf16[4,8192]{1,0:T(4,128)(2,1)S(1)} collective-permute-done((bf16[4,8192]{1,0:T(4,128)(2,1)S(1)}, bf16[4,8192]{1,0:T(4,128)(2,1)S(1)}, u32[]{:S(2)}, u32[]{:S(2)}) %collective-permute-start.17) | collective-permute-done | bytes 65568 | tf_op jit(solution)/shard_map/ppermute | solution.py:32
  73.8 1.3 %collective-permute-done.18.other_ref = bf16[8,8192]{1,0:T(8,128)(2,1)S(1)} collective-permute-done((bf16[8,8192]{1,0:T(8,128)(2,1)S(1)}, bf16[8,8192]{1,0:T(8,128)(2,1)S(1)}, u32[]{:S(2)}, u32[]{:S(2)}) %collective-permute-start.18) | collective-permute-done | bytes 131104 | tf_op jit(solution)/shard_map/ppermute | solution.py:32
  76.2 1.5 %collective-permute-start.20 = (bf16[16,64]{1,0:T(8,128)(2,1)S(1)}, bf16[16,64]{1,0:T(8,128)(2,1)S(1)}, u32[]{:S(2)}, u32[]{:S(2)}) collective-permute-start(bf16[16,64]{1,0:T(8,128)(2,1)S(1)} %get-tuple-element.62.refs_0_), channel_id=1, source_target_pairs={{0,2},{1,3},{2,0},{3,1},{4,6},{5,7},{6,4},{7,5},{8,10},{9,11},{10,... | collective-permute-start | bytes 6152 | tf_op jit(solution)/shard_map/ppermute | solution.py:32
  77.8 1.2 collective-permute-done.21.refs_3_
  78.9 0.9 collective-permute-done.20.refs_2_
  79.9 1.6 %collective-permute-start.24 = (bf16[16,64]{1,0:T(8,128)(2,1)S(1)}, bf16[16,64]{1,0:T(8,128)(2,1)S(1)}, u32[]{:S(2)}, u32[]{:S(2)}) collective-permute-start(bf16[16,64]{1,0:T(8,128)(2,1)S(1)} %sum.3.refs_0_), channel_id=1, source_target_pairs={{0,12},{1,13},{2,14},{3,15},{4,8},{5,9},{6,10},{7,11},{8,4},{9,5},... | collective-permute-start | bytes 6152 | tf_op jit(solution)/shard_map/ppermute | solution.py:32
  82.3 2.0 %collective-permute-start.22 = (bf16[16,64]{1,0:T(8,128)(2,1)S(1)}, bf16[16,64]{1,0:T(8,128)(2,1)S(1)}, u32[]{:S(2)}, u32[]{:S(2)}) collective-permute-start(bf16[16,64]{1,0:T(8,128)(2,1)S(1)} %sum.3.refs_0_), channel_id=1, source_target_pairs={{0,4},{1,5},{2,6},{3,7},{4,0},{5,1},{6,2},{7,3},{8,12},{9,13},{10,... | collective-permute-start | bytes 6152 | tf_op jit(solution)/shard_map/ppermute | solution.py:32
  84.3 1.5 %project.3 = (f32[16,512]{1,0:T(8,128)S(1)}, f32[16,128]{1,0:T(8,128)S(1)}) custom-call(bf16[16,8192]{1,0:T(8,128)(2,1)S(1)} %get-tuple-element.63.rows_ref, bf16[8192,512]{1,0:T(8,128)(2,1)S(1)} %get-tuple-element.47.query_w, bf16[8192,128]{1,0:T(8,128)(2,1)S(1)} %get-tuple-element.48.fresh_w), custom_call_target="tpu_custom_call" | custom-call | flops 167772160 | bytes 10485760 | tf_op jit(solution)/shard_map/project/pallas_call | solution.py:53
  86.5 11.0 %all_to_all.27.refs_0_ = bf16[16,8,128]{2,1,0:T(8,128)(2,1)S(1)} all-to-all(bf16[16,8,128]{2,1,0:T(8,128)(2,1)S(1)} %up.3), channel_id=1, replica_groups=mesh['groups'=2,'replica'=16] {'replica'}, dimensions={0} | all-to-all | bytes 65536 | tf_op jit(solution)/shard_map/all_to_all | solution.py:40
  98.3 9.1 %all_to_all.28.lines_ref = bf16[16,4,128]{2,1,0:T(4,128)(2,1)S(1)} all-to-all(bf16[16,4,128]{2,1,0:T(4,128)(2,1)S(1)} %attend.3), channel_id=1, replica_groups=mesh['groups'=2,'replica'=16] {'replica'}, dimensions={0} | all-to-all | bytes 32768 | tf_op jit(solution)/shard_map/all_to_all | solution.py:40
  107.4 1.3 %output.3 = (f32[8,8192]{1,0:T(8,128)S(1)}, bf16[8,8192]{1,0:T(8,128)(2,1)S(1)}) custom-call(bf16[16,4,128]{2,1,0:T(4,128)(2,1)S(1)} %all_to_all.28.lines_ref, s32[1]{0:T(128)} %bitcast._.refs_4_.me_ref, bf16[512,8192]{1,0:T(8,128)(2,1)S(1)} %get-tuple-element.55.weight_ref), custom_call_target="tpu_custom_call" | custom-call | flops 134217728 | bytes 8388608 | tf_op jit(solution)/shard_map/output/pallas_call | solution.py:53
  108.7 1.4 %collective-permute-done.25.other_ref = bf16[8,8192]{1,0:T(8,128)(2,1)S(1)} collective-permute-done((bf16[8,8192]{1,0:T(8,128)(2,1)S(1)}, bf16[8,8192]{1,0:T(8,128)(2,1)S(1)}, u32[]{:S(2)}, u32[]{:S(2)}) %collective-permute-start.25) | collective-permute-done | bytes 131104 | tf_op jit(solution)/shard_map/ppermute | solution.py:32
  110.2 10.0 %all_to_all.29.parts_ref = bf16[8,8,1024]{2,1,0:T(8,128)(2,1)S(1)} all-to-all(bf16[8,8,1024]{2,1,0:T(8,128)(2,1)S(1)} %partial.1), channel_id=1, replica_groups={{0,2,4,6,8,10,12,14},{1,3,5,7,9,11,13,15},{16,18,20,22,24,26,28,30},{17..., dimensions={0} | all-to-all | bytes 262144 | tf_op jit(solution)/shard_map/all_to_all | solution.py:45
  (54 shorter events, 13.2 us)
Async XLA Ops:
  1.3 0.8 copy-start.1
  2.1 10.4 %collective-permute-start.2 = (bf16[1,8320]{1,0:T(2,128)(2,1)S(1)}, bf16[1,8320]{1,0:T(2,128)(2,1)S(1)}, u32[]{:S(2)}, u32[]{:S(2)}) collective-permute-start(bf16[1,8320]{1,0:T(2,128)(2,1)S(1)} %get-tuple-element.38.refs_0_), channel_id=1, source_target_pairs={{0,12},{1,13},{2,14},{3,15},{4,8},{5,9},{6,10},{7,11},{8,4},{9,5},... | collective-permute-start | bytes 49928 | tf_op jit(solution)/shard_map/ppermute | solution.py:32
  7.2 5.3 %collective-permute-start.1 = (bf16[1,8320]{1,0:T(2,128)(2,1)S(1)}, bf16[1,8320]{1,0:T(2,128)(2,1)S(1)}, u32[]{:S(2)}, u32[]{:S(2)}) collective-permute-start(bf16[1,8320]{1,0:T(2,128)(2,1)S(1)} %get-tuple-element.38.refs_0_), channel_id=1, source_target_pairs={{0,8},{1,9},{2,10},{3,11},{4,12},{5,13},{6,14},{7,15},{8,0},{9,1},... | collective-permute-start | bytes 49928 | tf_op jit(solution)/shard_map/ppermute | solution.py:32
  7.2 5.3 %collective-permute-start = (bf16[1,8320]{1,0:T(2,128)(2,1)S(1)}, bf16[1,8320]{1,0:T(2,128)(2,1)S(1)}, u32[]{:S(2)}, u32[]{:S(2)}) collective-permute-start(bf16[1,8320]{1,0:T(2,128)(2,1)S(1)} %get-tuple-element.38.refs_0_), channel_id=1, source_target_pairs={{0,4},{1,5},{2,6},{3,7},{4,0},{5,1},{6,2},{7,3},{8,12},{9,13},{10,... | collective-permute-start | bytes 49928 | tf_op jit(solution)/shard_map/ppermute | solution.py:32
  7.8 4.7 %copy-start = (bf16[8192]{0:T(1024)(128)(2,1)S(1)}, bf16[8192]{0:T(1024)(128)(2,1)}, u32[]{:S(2)}) copy-start(bf16[8192]{0:T(1024)(128)(2,1)} %param.12) | copy-start | bytes 49156
  12.8 6.6 %copy-start.2 = (s32[32]{0:T(128)S(1)}, s32[32]{0:T(128)}, u32[]{:S(2)}) copy-start(s32[32]{0:T(128)} %param.19) | copy-start | bytes 388
  12.8 6.6 %collective-permute-start.5 = (bf16[4,8320]{1,0:T(4,128)(2,1)S(1)}, bf16[4,8320]{1,0:T(4,128)(2,1)S(1)}, u32[]{:S(2)}, u32[]{:S(2)}) collective-permute-start(bf16[4,8320]{1,0:T(4,128)(2,1)S(1)} %get-tuple-element.41.refs_0_), channel_id=1, source_target_pairs={{0,3},{1,2},{2,1},{3,0},{4,7},{5,6},{6,5},{7,4},{8,11},{9,10},{10,... | collective-permute-start | bytes 199688 | tf_op jit(solution)/shard_map/ppermute | solution.py:32
  13.2 6.1 %collective-permute-start.4 = (bf16[4,8320]{1,0:T(4,128)(2,1)S(1)}, bf16[4,8320]{1,0:T(4,128)(2,1)S(1)}, u32[]{:S(2)}, u32[]{:S(2)}) collective-permute-start(bf16[4,8320]{1,0:T(4,128)(2,1)S(1)} %get-tuple-element.41.refs_0_), channel_id=1, source_target_pairs={{0,2},{1,3},{2,0},{3,1},{4,6},{5,7},{6,4},{7,5},{8,10},{9,11},{10,... | collective-permute-start | bytes 199688 | tf_op jit(solution)/shard_map/ppermute | solution.py:32
  14.6 4.8 %collective-permute-start.3 = (bf16[4,8320]{1,0:T(4,128)(2,1)S(1)}, bf16[4,8320]{1,0:T(4,128)(2,1)S(1)}, u32[]{:S(2)}, u32[]{:S(2)}) collective-permute-start(bf16[4,8320]{1,0:T(4,128)(2,1)S(1)} %get-tuple-element.41.refs_0_), channel_id=1, source_target_pairs={{0,1},{1,0},{2,3},{3,2},{4,5},{5,4},{6,7},{7,6},{8,9},{9,8},{10,11... | collective-permute-start | bytes 199688 | tf_op jit(solution)/shard_map/ppermute | solution.py:32
  20.4 3.1 %collective-permute-start.8 = (bf16[16,64]{1,0:T(8,128)(2,1)S(1)}, bf16[16,64]{1,0:T(8,128)(2,1)S(1)}, u32[]{:S(2)}, u32[]{:S(2)}) collective-permute-start(bf16[16,64]{1,0:T(8,128)(2,1)S(1)} %get-tuple-element.45.refs_0_), channel_id=1, source_target_pairs={{0,3},{1,2},{2,1},{3,0},{4,7},{5,6},{6,5},{7,4},{8,11},{9,10},{10,... | collective-permute-start | bytes 6152 | tf_op jit(solution)/shard_map/ppermute | solution.py:32
  21.7 3.6 %collective-permute-start.7 = (bf16[16,64]{1,0:T(8,128)(2,1)S(1)}, bf16[16,64]{1,0:T(8,128)(2,1)S(1)}, u32[]{:S(2)}, u32[]{:S(2)}) collective-permute-start(bf16[16,64]{1,0:T(8,128)(2,1)S(1)} %get-tuple-element.45.refs_0_), channel_id=1, source_target_pairs={{0,2},{1,3},{2,0},{3,1},{4,6},{5,7},{6,4},{7,5},{8,10},{9,11},{10,... | collective-permute-start | bytes 6152 | tf_op jit(solution)/shard_map/ppermute | solution.py:32
  22.4 2.9 %collective-permute-start.6 = (bf16[16,64]{1,0:T(8,128)(2,1)S(1)}, bf16[16,64]{1,0:T(8,128)(2,1)S(1)}, u32[]{:S(2)}, u32[]{:S(2)}) collective-permute-start(bf16[16,64]{1,0:T(8,128)(2,1)S(1)} %get-tuple-element.45.refs_0_), channel_id=1, source_target_pairs={{0,1},{1,0},{2,3},{3,2},{4,5},{5,4},{6,7},{7,6},{8,9},{9,8},{10,11... | collective-permute-start | bytes 6152 | tf_op jit(solution)/shard_map/ppermute | solution.py:32
  25.3 5.9 %collective-permute-start.11 = (bf16[16,64]{1,0:T(8,128)(2,1)S(1)}, bf16[16,64]{1,0:T(8,128)(2,1)S(1)}, u32[]{:S(2)}, u32[]{:S(2)}) collective-permute-start(bf16[16,64]{1,0:T(8,128)(2,1)S(1)} %sum.2.refs_0_), channel_id=1, source_target_pairs={{0,12},{1,13},{2,14},{3,15},{4,8},{5,9},{6,10},{7,11},{8,4},{9,5},... | collective-permute-start | bytes 6152 | tf_op jit(solution)/shard_map/ppermute | solution.py:32
  28.9 4.5 %collective-permute-start.10 = (bf16[16,64]{1,0:T(8,128)(2,1)S(1)}, bf16[16,64]{1,0:T(8,128)(2,1)S(1)}, u32[]{:S(2)}, u32[]{:S(2)}) collective-permute-start(bf16[16,64]{1,0:T(8,128)(2,1)S(1)} %sum.2.refs_0_), channel_id=1, source_target_pairs={{0,8},{1,9},{2,10},{3,11},{4,12},{5,13},{6,14},{7,15},{8,0},{9,1},... | collective-permute-start | bytes 6152 | tf_op jit(solution)/shard_map/ppermute | solution.py:32
  28.9 4.5 %collective-permute-start.9 = (bf16[16,64]{1,0:T(8,128)(2,1)S(1)}, bf16[16,64]{1,0:T(8,128)(2,1)S(1)}, u32[]{:S(2)}, u32[]{:S(2)}) collective-permute-start(bf16[16,64]{1,0:T(8,128)(2,1)S(1)} %sum.2.refs_0_), channel_id=1, source_target_pairs={{0,4},{1,5},{2,6},{3,7},{4,0},{5,1},{6,2},{7,3},{8,12},{9,13},{10,... | collective-permute-start | bytes 6152 | tf_op jit(solution)/shard_map/ppermute | solution.py:32
  55.2 1.4 %collective-permute-start.12 = (bf16[8,8192]{1,0:T(8,128)(2,1)S(1)}, bf16[8,8192]{1,0:T(8,128)(2,1)S(1)}, u32[]{:S(2)}, u32[]{:S(2)}) collective-permute-start(bf16[8,8192]{1,0:T(8,128)(2,1)S(1)} %get-tuple-element.57), channel_id=1, source_target_pairs={{0,1},{1,0},{2,3},{3,2},{4,5},{5,4},{6,7},{7,6},{8,9},{9,8},{10,11... | collective-permute-start | bytes 393224 | tf_op jit(solution)/shard_map/ppermute | solution.py:32
  56.6 4.3 %collective-permute-start.13 = (bf16[4,8192]{1,0:T(4,128)(2,1)S(1)}, bf16[4,8192]{1,0:T(4,128)(2,1)S(1)}, u32[]{:S(2)}, u32[]{:S(2)}) collective-permute-start(bf16[4,8192]{1,0:T(4,128)(2,1)S(1)} %get-tuple-element.59), channel_id=1, source_target_pairs={{0,2},{1,3},{2,0},{3,1},{4,6},{5,7},{6,4},{7,5},{8,10},{9,11},{10,... | collective-permute-start | bytes 196616 | tf_op jit(solution)/shard_map/ppermute | solution.py:32
  61.0 6.4 %collective-permute-start.16 = (bf16[4,8192]{1,0:T(4,128)(2,1)S(1)}, bf16[4,8192]{1,0:T(4,128)(2,1)S(1)}, u32[]{:S(2)}, u32[]{:S(2)}) collective-permute-start(bf16[4,8192]{1,0:T(4,128)(2,1)S(1)} %fold.3.refs_0_), channel_id=1, source_target_pairs={{0,12},{1,13},{2,14},{3,15},{4,8},{5,9},{6,10},{7,11},{8,4},{9,5},... | collective-permute-start | bytes 196616 | tf_op jit(solution)/shard_map/ppermute | solution.py:32
  61.5 7.1 %collective-permute-start.15 = (bf16[4,8192]{1,0:T(4,128)(2,1)S(1)}, bf16[4,8192]{1,0:T(4,128)(2,1)S(1)}, u32[]{:S(2)}, u32[]{:S(2)}) collective-permute-start(bf16[4,8192]{1,0:T(4,128)(2,1)S(1)} %fold.3.refs_0_), channel_id=1, source_target_pairs={{0,8},{1,9},{2,10},{3,11},{4,12},{5,13},{6,14},{7,15},{8,0},{9,1},... | collective-permute-start | bytes 196616 | tf_op jit(solution)/shard_map/ppermute | solution.py:32
  63.0 5.7 %collective-permute-start.14 = (bf16[4,8192]{1,0:T(4,128)(2,1)S(1)}, bf16[4,8192]{1,0:T(4,128)(2,1)S(1)}, u32[]{:S(2)}, u32[]{:S(2)}) collective-permute-start(bf16[4,8192]{1,0:T(4,128)(2,1)S(1)} %fold.3.refs_0_), channel_id=1, source_target_pairs={{0,4},{1,5},{2,6},{3,7},{4,0},{5,1},{6,2},{7,3},{8,12},{9,13},{10,... | collective-permute-start | bytes 196616 | tf_op jit(solution)/shard_map/ppermute | solution.py:32
  69.3 4.3 %collective-permute-start.17 = (bf16[4,8192]{1,0:T(4,128)(2,1)S(1)}, bf16[4,8192]{1,0:T(4,128)(2,1)S(1)}, u32[]{:S(2)}, u32[]{:S(2)}) collective-permute-start(bf16[4,8192]{1,0:T(4,128)(2,1)S(1)} %get-tuple-element.61.refs_0_), channel_id=1, source_target_pairs={{0,2},{1,3},{2,0},{3,1},{4,6},{5,7},{6,4},{7,5},{8,10},{9,11},{10,... | collective-permute-start | bytes 196616 | tf_op jit(solution)/shard_map/ppermute | solution.py:32
  73.7 1.4 %collective-permute-start.18 = (bf16[8,8192]{1,0:T(8,128)(2,1)S(1)}, bf16[8,8192]{1,0:T(8,128)(2,1)S(1)}, u32[]{:S(2)}, u32[]{:S(2)}) collective-permute-start(bf16[8,8192]{1,0:T(8,128)(2,1)S(1)} %stack.1.own_ref), channel_id=1, source_target_pairs={{0,1},{1,0},{2,3},{3,2},{4,5},{5,4},{6,7},{7,6},{8,9},{9,8},{10,11... | collective-permute-start | bytes 393224 | tf_op jit(solution)/shard_map/ppermute | solution.py:32
  75.9 3.1 %collective-permute-start.21 = (bf16[16,64]{1,0:T(8,128)(2,1)S(1)}, bf16[16,64]{1,0:T(8,128)(2,1)S(1)}, u32[]{:S(2)}, u32[]{:S(2)}) collective-permute-start(bf16[16,64]{1,0:T(8,128)(2,1)S(1)} %get-tuple-element.62.refs_0_), channel_id=1, source_target_pairs={{0,3},{1,2},{2,1},{3,0},{4,7},{5,6},{6,5},{7,4},{8,11},{9,10},{10,... | collective-permute-start | bytes 6152 | tf_op jit(solution)/shard_map/ppermute | solution.py:32
  76.2 3.6 %collective-permute-start.20 = (bf16[16,64]{1,0:T(8,128)(2,1)S(1)}, bf16[16,64]{1,0:T(8,128)(2,1)S(1)}, u32[]{:S(2)}, u32[]{:S(2)}) collective-permute-start(bf16[16,64]{1,0:T(8,128)(2,1)S(1)} %get-tuple-element.62.refs_0_), channel_id=1, source_target_pairs={{0,2},{1,3},{2,0},{3,1},{4,6},{5,7},{6,4},{7,5},{8,10},{9,11},{10,... | collective-permute-start | bytes 6152 | tf_op jit(solution)/shard_map/ppermute | solution.py:32
  77.7 2.1 %collective-permute-start.19 = (bf16[16,64]{1,0:T(8,128)(2,1)S(1)}, bf16[16,64]{1,0:T(8,128)(2,1)S(1)}, u32[]{:S(2)}, u32[]{:S(2)}) collective-permute-start(bf16[16,64]{1,0:T(8,128)(2,1)S(1)} %get-tuple-element.62.refs_0_), channel_id=1, source_target_pairs={{0,1},{1,0},{2,3},{3,2},{4,5},{5,4},{6,7},{7,6},{8,9},{9,8},{10,11... | collective-permute-start | bytes 6152 | tf_op jit(solution)/shard_map/ppermute | solution.py:32
  79.9 5.9 %collective-permute-start.24 = (bf16[16,64]{1,0:T(8,128)(2,1)S(1)}, bf16[16,64]{1,0:T(8,128)(2,1)S(1)}, u32[]{:S(2)}, u32[]{:S(2)}) collective-permute-start(bf16[16,64]{1,0:T(8,128)(2,1)S(1)} %sum.3.refs_0_), channel_id=1, source_target_pairs={{0,12},{1,13},{2,14},{3,15},{4,8},{5,9},{6,10},{7,11},{8,4},{9,5},... | collective-permute-start | bytes 6152 | tf_op jit(solution)/shard_map/ppermute | solution.py:32
  81.5 4.5 %collective-permute-start.23 = (bf16[16,64]{1,0:T(8,128)(2,1)S(1)}, bf16[16,64]{1,0:T(8,128)(2,1)S(1)}, u32[]{:S(2)}, u32[]{:S(2)}) collective-permute-start(bf16[16,64]{1,0:T(8,128)(2,1)S(1)} %sum.3.refs_0_), channel_id=1, source_target_pairs={{0,8},{1,9},{2,10},{3,11},{4,12},{5,13},{6,14},{7,15},{8,0},{9,1},... | collective-permute-start | bytes 6152 | tf_op jit(solution)/shard_map/ppermute | solution.py:32
  82.3 3.7 %collective-permute-start.22 = (bf16[16,64]{1,0:T(8,128)(2,1)S(1)}, bf16[16,64]{1,0:T(8,128)(2,1)S(1)}, u32[]{:S(2)}, u32[]{:S(2)}) collective-permute-start(bf16[16,64]{1,0:T(8,128)(2,1)S(1)} %sum.3.refs_0_), channel_id=1, source_target_pairs={{0,4},{1,5},{2,6},{3,7},{4,0},{5,1},{6,2},{7,3},{8,12},{9,13},{10,... | collective-permute-start | bytes 6152 | tf_op jit(solution)/shard_map/ppermute | solution.py:32
  108.7 1.4 %collective-permute-start.25 = (bf16[8,8192]{1,0:T(8,128)(2,1)S(1)}, bf16[8,8192]{1,0:T(8,128)(2,1)S(1)}, u32[]{:S(2)}, u32[]{:S(2)}) collective-permute-start(bf16[8,8192]{1,0:T(8,128)(2,1)S(1)} %get-tuple-element.69), channel_id=1, source_target_pairs={{0,1},{1,0},{2,3},{3,2},{4,5},{5,4},{6,7},{7,6},{8,9},{9,8},{10,11... | collective-permute-start | bytes 393224 | tf_op jit(solution)/shard_map/ppermute | solution.py:32

commit v13 on v12

--- a/solution.py
+++ b/solution.py
@@ -99,7 +99,7 @@
 
 def stash_kernel(amount, token_ref, *refs):
     sources, refs = refs[:amount], refs[amount:]
-    outs, out_token, sems = refs[:amount], refs[amount], refs[-1]
+    outs, out_token, sems = refs[-2 - amount : -2], refs[-2], refs[-1]
     copies = [
         pltpu.make_async_copy(sources[i], outs[i], sems.at[i]) for i in range(amount)
     ]
@@ -138,7 +138,7 @@
     low_ref[...] = low.astype(jnp.bfloat16)
 
 
-def low_first_kernel(near, far, *refs):
+def low_kernel(near, far, *refs):
     pieces, refs = refs[:near], refs[near:]
     me_ref, member_ref, down_ref, rows_ref, low_ref, held = refs
     width = held.shape[1]
@@ -146,16 +146,6 @@
         block = pieces[l][:, :width].astype(jnp.float32)
         for k in range(far):
             held[pl.ds(me_ref[0] ^ (k * near + l), 1), :] = block[k : k + 1]
-    low_terms(held, member_ref, down_ref, rows_ref, low_ref)
-
-
-def low_later_kernel(near, far, own_ref, other_ref, me_ref, member_ref, down_ref, rows_ref, low_ref, held):
-    half = own_ref.shape[0]
-    for start, ref in ((0, own_ref), (half, other_ref)):
-        block = ref[...].astype(jnp.float32)
-        for k in range(half):
-            row = me_ref[0] ^ distance(start + k, near, far)
-            held[pl.ds(row, 1), :] = block[k : k + 1]
     low_terms(held, member_ref, down_ref, rows_ref, low_ref)
 
 
@@ -168,11 +158,6 @@
     hidden_ref[...] = hidden.astype(jnp.bfloat16)
     out_ref[:, :width] = normalized(hidden, row_of(scale_ref))
     out_ref[:, width:] = rows[:, width:].astype(jnp.bfloat16)
-
-
-def stack_kernel(*refs):
-    rows = [ref[...].astype(jnp.float32) for ref in refs[:-1]]
-    refs[-1][...] = jnp.concatenate(rows, axis=0).astype(refs[-1].dtype)
 
 
 def distance(slot, near, far):
@@ -210,9 +195,9 @@
     out_ref[...] = normalized(hidden.astype(jnp.float32), row_of(scale_ref))
 
 
-def sum_kernel(*refs):
+def sum_kernel(amount, *refs):
     total = refs[0][...].astype(jnp.float32)
-    for ref in refs[1:-1]:
+    for ref in refs[1:amount]:
         total = total + ref[...].astype(jnp.float32)
     refs[-1][...] = total.astype(refs[-1].dtype)
 
@@ -425,7 +410,7 @@
     scale = attention_norm_scale.reshape(-1, LANES)
     storage = adapter_storage_index[None]
 
-    def stash(token, arrays):
+    def stash(token, arrays, *behind):
         outs = call(
             functools.partial(stash_kernel, len(arrays)),
             [pltpu.VMEM(a.shape, a.dtype) for a in arrays] + [shape((8, LANES), jnp.int32)],
@@ -435,7 +420,8 @@
         )(
             token,
             *(pltpu.with_memory_space_constraint(a, pltpu.HBM) for a in arrays),
-            specs=[vmem] + [pltpu.HBM] * len(arrays),
+            *behind,
+            specs=[vmem] + [pltpu.HBM] * len(arrays) + [pl.ANY] * len(behind),
         )
         return outs[:-1], outs[-1]
 
@@ -455,16 +441,14 @@
         outs = [shape((count, width)), shape((count, rank))]
         scratch = [pltpu.VMEM((count, width), jnp.float32)]
         if first:
-            early = [query_weight, key_value_weight, down]
-            (query_w, fresh_w, down_w), token = stash(length, early)
+            (query_w, down_w), token = stash(length, [query_weight, down])
             pieces = across(carried, far_steps, count)
             column, carried = call(
                 functools.partial(join_kernel, far),
                 [shape((far, width)), shape((far, width + LANES))],
                 "join",
             )(*pieces, scale, token)
-            later = [output_weight, key_value_cache, adapter_up_weight]
-            (output_w, cache, up_w), token = stash(token, later)
+            (output_w,), token = stash(token, [output_weight])
             pieces = across(carried, near_steps, count)
             member, adapter = call(
                 functools.partial(member_kernel, near, far, width),
@@ -472,19 +456,19 @@
                 "member",
                 [pltpu.VMEM((count, LANES), jnp.float32)],
             )(*pieces, me, storage, token, specs=[vmem] * near + [smem, vmem, vmem])
-            rows, low = call(
-                functools.partial(low_first_kernel, near, far), outs, "low", scratch
-            )(*pieces, me, member, down_w, specs=[vmem] * near + [smem, vmem, vmem])
         else:
-            rows, low = call(functools.partial(low_later_kernel, near, far), outs, "low", scratch)(
-                carried,
-                shift(carried, 1, count),
-                me,
-                member,
-                down_w,
-                specs=[vmem, vmem, smem, vmem, vmem],
-            )
-        (low,) = call(sum_kernel, [shape((count, rank))], "sum")(*across(low, near_steps, count))
+            pieces = across(carried, near_steps, count)
+        rows, low = call(functools.partial(low_kernel, near, far), outs, "low", scratch)(
+            *pieces, me, member, down_w, specs=[vmem] * near + [smem, vmem, vmem]
+        )
+        behind = []
+        if first:
+            rest = [key_value_weight, adapter_up_weight, key_value_cache]
+            (fresh_w, up_w, cache), token = stash(token, rest, low)
+            behind = [token]
+        (low,) = call(functools.partial(sum_kernel, near), [shape((count, rank))], "sum")(
+            *across(low, near_steps, count), *behind
+        )
         lows = across(low, far_steps, count)
         query, fresh = call(
             project_kernel,
@@ -551,11 +535,6 @@
         hidden, carried = call(
             functools.partial(next_kernel, far), [shape((1, width)), shape((far, width))], "next"
         )(*across(own, far_steps, count), column, scale)
-        while bit > 1:
-            (carried,) = call(stack_kernel, [shape((2 * carried.shape[0], width))], "stack")(
-                carried, shift(carried, bit, count)
-            )
-            bit //= 2
 
 
 def solution(mesh):

time: 121 us -> 120 us (level)
  waiting for transfers between devices: 22.2 us -> 18.9 us
    ppermute x26 -> x27, waiting for transfers between devices: 22.2 us -> 18.9 us  [shift(): return lax.ppermute(block, AXIS, [(i, i ^ distance) for i in range(count)])]
    ppermute x26 -> x27, starting transfers between devices: 26.1 us -> 27.3 us  [shift(): return lax.ppermute(block, AXIS, [(i, i ^ distance) for i in range(count)])]
  transfers between devices with their start and end apart: 26 -> 27, of which waited for: 13 -> 13; matrix products, arithmetic and copies ran while one was open for 0% -> 0% of each run, Pallas kernels for 10% -> 11%
where the time goes in v13:
time: 120 us; the launch traced here: 119 us
  blocking collectives  48.6 us (40%)
  starting transfers between devices  27.3 us (23%)
  Pallas kernels  22.2 us (18%)
  waiting for transfers between devices  18.9 us (16%)
  between operations  1.47 us (1%)
    all_to_all x4, blocking collectives, swap(): return lax.all_to_all(blocks, AXIS, split_axis=0, concat_axis=0, tiled=True)  38.6 us
    ppermute x27, starting transfers between devices, shift(): return lax.ppermute(block, AXIS, [(i, i ^ distance) for i in range(count)])  27.3 us
    pallas_call x23, Pallas kernels, run(): pl.pallas_call(body, out_shape=outs, in_specs=[pl.BlockSpec(memory_space=...  22.2 us
    ppermute x27, waiting for transfers between devices, shift(): return lax.ppermute(block, AXIS, [(i, i ^ distance) for i in range(count)])  18.9 us
    all_to_all x1, blocking collectives, chips_swap(): lax.all_to_all(blocks, AXIS, split_axis=0, concat_axis=0, axis_index_grou...  9.97 us
  transfers between devices with their start and end apart: 27, of which 13 were waited for; matrix products, arithmetic and copies ran while one was open for 0% of the time, Pallas kernels for 11%

profile of v13, /device:TPU:0, one launch (start us, length us, event | category | flops | bytes accessed | tf_op | source)
XLA Modules:
  0.0 119.1 jit_solution(15301722901631591741)
XLA Ops:
  2.1 5.1 %collective-permute-start.2 = (bf16[1,8320]{1,0:T(2,128)(2,1)S(1)}, bf16[1,8320]{1,0:T(2,128)(2,1)S(1)}, u32[]{:S(2)}, u32[]{:S(2)}) collective-permute-start(bf16[1,8320]{1,0:T(2,128)(2,1)S(1)} %get-tuple-element.39.refs_0_), channel_id=1, source_target_pairs={{0,12},{1,13},{2,14},{3,15},{4,8},{5,9},{6,10},{7,11},{8,4},{9,5},... | collective-permute-start | bytes 49928 | tf_op jit(solution)/shard_map/ppermute | solution.py:32
  7.8 4.0 %stash.3 = (bf16[8192,512]{1,0:T(8,128)(2,1)S(1)}, bf16[2,64,8192]{2,1,0:T(8,128)(2,1)S(1)}, s32[8,128]{1,0:T(8,128)S(1)}) custom-call(s32[8,128]{1,0:T(8,128)S(1)} %get-tuple-element.40.token_ref.refs_1_, bf16[8192,512]{1,0:T(8,128)(2,1)} %refs_0_.3, bf16[2,64,8192]{2,1,0:T(8,128)(2,1)} %bitcast.8), custom_call_target="tpu_custom_call" | custom-call | flops 1048576 | bytes 10485760 | tf_op jit(solution)/shard_map/stash/pallas_call | solution.py:53
  12.6 1.3 %collective-permute-start.4 = (bf16[4,8320]{1,0:T(4,128)(2,1)S(1)}, bf16[4,8320]{1,0:T(4,128)(2,1)S(1)}, u32[]{:S(2)}, u32[]{:S(2)}) collective-permute-start(bf16[4,8320]{1,0:T(4,128)(2,1)S(1)} %get-tuple-element.42.refs_0_), channel_id=1, source_target_pairs={{0,2},{1,3},{2,0},{3,1},{4,6},{5,7},{6,4},{7,5},{8,10},{9,11},{10,... | collective-permute-start | bytes 199688 | tf_op jit(solution)/shard_map/ppermute | solution.py:32
  14.3 3.4 %stash.4 = (bf16[512,8192]{1,0:T(8,128)(2,1)S(1)}, s32[8,128]{1,0:T(8,128)S(1)}) custom-call(s32[8,128]{1,0:T(8,128)S(1)} %get-tuple-element.41.refs_5_.token_ref, bf16[512,8192]{1,0:T(8,128)(2,1)} %refs_0_.4), custom_call_target="tpu_custom_call" | custom-call | flops 1048576 | bytes 8388608 | tf_op jit(solution)/shard_map/stash/pallas_call | solution.py:53
  19.8 1.1 collective-permute-start.7
  21.1 2.9 %stash.5 = (bf16[8192,128]{1,0:T(8,128)(2,1)S(1)}, bf16[32,64,512]{2,1,0:T(8,128)(2,1)S(1)}, bf16[1,2,512,1024]{3,2,1,0:T(8,128)(2,1)S(1)}, s32[8,128]{1,0:T(8,128)S(1)}) custom-call(s32[8,128]{1,0:T(8,128)S(1)} %get-tuple-element.43.refs_6_.token_ref, bf16[8192,128]{1,0:T(8,128)(2,1)} %refs_0_.5, bf16[32,64,512]{2,1,0:T(8,128)(2,1)} %refs_1_.1, ...), custom_call_target="tpu_custom_call" | custom-call | flops 1048576 | bytes 6291456 | tf_op jit(solution)/shard_map/stash/pallas_call | solution.py:53
  24.1 3.7 %collective-permute-start.11 = (bf16[16,64]{1,0:T(8,128)(2,1)S(1)}, bf16[16,64]{1,0:T(8,128)(2,1)S(1)}, u32[]{:S(2)}, u32[]{:S(2)}) collective-permute-start(bf16[16,64]{1,0:T(8,128)(2,1)S(1)} %sum.2.refs_0_), channel_id=1, source_target_pairs={{0,12},{1,13},{2,14},{3,15},{4,8},{5,9},{6,10},{7,11},{8,4},{9,5},... | collective-permute-start | bytes 6152 | tf_op jit(solution)/shard_map/ppermute | solution.py:32
  28.5 1.5 %project.2 = (f32[16,512]{1,0:T(8,128)S(1)}, f32[16,128]{1,0:T(8,128)S(1)}) custom-call(bf16[16,8192]{1,0:T(8,128)(2,1)S(1)} %get-tuple-element.48.rows_ref, bf16[8192,512]{1,0:T(8,128)(2,1)S(1)} %get-tuple-element.49.query_w, bf16[8192,128]{1,0:T(8,128)(2,1)S(1)} %get-tuple-element.50.fresh_w), custom_call_target="tpu_custom_call" | custom-call | flops 167772160 | bytes 10485760 | tf_op jit(solution)/shard_map/project/pallas_call | solution.py:53
  30.0 2.3 %collective-permute-done.10.refs_2_ = bf16[16,64]{1,0:T(8,128)(2,1)S(1)} collective-permute-done((bf16[16,64]{1,0:T(8,128)(2,1)S(1)}, bf16[16,64]{1,0:T(8,128)(2,1)S(1)}, u32[]{:S(2)}, u32[]{:S(2)}) %collective-permute-start.10) | collective-permute-done | bytes 2080 | tf_op jit(solution)/shard_map/ppermute | solution.py:32
  32.8 10.2 %all_to_all.25.refs_0_ = bf16[16,8,128]{2,1,0:T(8,128)(2,1)S(1)} all-to-all(bf16[16,8,128]{2,1,0:T(8,128)(2,1)S(1)} %up.2), channel_id=1, replica_groups=mesh['groups'=2,'replica'=16] {'replica'}, dimensions={0} | all-to-all | bytes 65536 | tf_op jit(solution)/shard_map/all_to_all | solution.py:40
  43.8 9.1 %all_to_all.26.lines_ref = bf16[16,4,128]{2,1,0:T(4,128)(2,1)S(1)} all-to-all(bf16[16,4,128]{2,1,0:T(4,128)(2,1)S(1)} %get-tuple-element.56), channel_id=1, replica_groups=mesh['groups'=2,'replica'=16] {'replica'}, dimensions={0} | all-to-all | bytes 32768 | tf_op jit(solution)/shard_map/all_to_all | solution.py:40
  52.9 1.3 %output.2 = (f32[8,8192]{1,0:T(8,128)S(1)}, bf16[8,8192]{1,0:T(8,128)(2,1)S(1)}) custom-call(bf16[16,4,128]{2,1,0:T(4,128)(2,1)S(1)} %all_to_all.26.lines_ref, s32[1]{0:T(128)} %bitcast._.refs_4_.me_ref, bf16[512,8192]{1,0:T(8,128)(2,1)S(1)} %get-tuple-element.57.weight_ref), custom_call_target="tpu_custom_call" | custom-call | flops 134217728 | bytes 8388608 | tf_op jit(solution)/shard_map/output/pallas_call | solution.py:53
  54.2 1.4 %collective-permute-done.12.other_ref = bf16[8,8192]{1,0:T(8,128)(2,1)S(1)} collective-permute-done((bf16[8,8192]{1,0:T(8,128)(2,1)S(1)}, bf16[8,8192]{1,0:T(8,128)(2,1)S(1)}, u32[]{:S(2)}, u32[]{:S(2)}) %collective-permute-start.12) | collective-permute-done | bytes 131104 | tf_op jit(solution)/shard_map/ppermute | solution.py:32
  56.1 3.8 %collective-permute-done.13.other_ref = bf16[4,8192]{1,0:T(4,128)(2,1)S(1)} collective-permute-done((bf16[4,8192]{1,0:T(4,128)(2,1)S(1)}, bf16[4,8192]{1,0:T(4,128)(2,1)S(1)}, u32[]{:S(2)}, u32[]{:S(2)}) %collective-permute-start.13) | collective-permute-done | bytes 65568 | tf_op jit(solution)/shard_map/ppermute | solution.py:32
  60.5 1.4 %collective-permute-start.15 = (bf16[4,8192]{1,0:T(4,128)(2,1)S(1)}, bf16[4,8192]{1,0:T(4,128)(2,1)S(1)}, u32[]{:S(2)}, u32[]{:S(2)}) collective-permute-start(bf16[4,8192]{1,0:T(4,128)(2,1)S(1)} %fold.3.refs_0_), channel_id=1, source_target_pairs={{0,8},{1,9},{2,10},{3,11},{4,12},{5,13},{6,14},{7,15},{8,0},{9,1},... | collective-permute-start | bytes 196616 | tf_op jit(solution)/shard_map/ppermute | solution.py:32
  62.0 2.5 %collective-permute-start.14 = (bf16[4,8192]{1,0:T(4,128)(2,1)S(1)}, bf16[4,8192]{1,0:T(4,128)(2,1)S(1)}, u32[]{:S(2)}, u32[]{:S(2)}) collective-permute-start(bf16[4,8192]{1,0:T(4,128)(2,1)S(1)} %fold.3.refs_0_), channel_id=1, source_target_pairs={{0,4},{1,5},{2,6},{3,7},{4,0},{5,1},{6,2},{7,3},{8,12},{9,13},{10,... | collective-permute-start | bytes 196616 | tf_op jit(solution)/shard_map/ppermute | solution.py:32
  64.4 2.0 %collective-permute-done.16.refs_3_ = bf16[4,8192]{1,0:T(4,128)(2,1)S(1)} collective-permute-done((bf16[4,8192]{1,0:T(4,128)(2,1)S(1)}, bf16[4,8192]{1,0:T(4,128)(2,1)S(1)}, u32[]{:S(2)}, u32[]{:S(2)}) %collective-permute-start.16) | collective-permute-done | bytes 65568 | tf_op jit(solution)/shard_map/ppermute | solution.py:32
  66.4 1.3 %collective-permute-done.15.refs_2_ = bf16[4,8192]{1,0:T(4,128)(2,1)S(1)} collective-permute-done((bf16[4,8192]{1,0:T(4,128)(2,1)S(1)}, bf16[4,8192]{1,0:T(4,128)(2,1)S(1)}, u32[]{:S(2)}, u32[]{:S(2)}) %collective-permute-start.15) | collective-permute-done | bytes 65568 | tf_op jit(solution)/shard_map/ppermute | solution.py:32
  69.0 1.2 %collective-permute-start.17 = (bf16[4,8192]{1,0:T(4,128)(2,1)S(1)}, bf16[4,8192]{1,0:T(4,128)(2,1)S(1)}, u32[]{:S(2)}, u32[]{:S(2)}) collective-permute-start(bf16[4,8192]{1,0:T(4,128)(2,1)S(1)} %get-tuple-element.63.refs_0_), channel_id=1, source_target_pairs={{0,1},{1,0},{2,3},{3,2},{4,5},{5,4},{6,7},{7,6},{8,9},{9,8},{10,11... | collective-permute-start | bytes 196616 | tf_op jit(solution)/shard_map/ppermute | solution.py:32
  70.2 1.9 %collective-permute-done.19.refs_3_ = bf16[4,8192]{1,0:T(4,128)(2,1)S(1)} collective-permute-done((bf16[4,8192]{1,0:T(4,128)(2,1)S(1)}, bf16[4,8192]{1,0:T(4,128)(2,1)S(1)}, u32[]{:S(2)}, u32[]{:S(2)}) %collective-permute-start.19) | collective-permute-done | bytes 65568 | tf_op jit(solution)/shard_map/ppermute | solution.py:32
  72.2 1.2 %collective-permute-done.18.refs_2_ = bf16[4,8192]{1,0:T(4,128)(2,1)S(1)} collective-permute-done((bf16[4,8192]{1,0:T(4,128)(2,1)S(1)}, bf16[4,8192]{1,0:T(4,128)(2,1)S(1)}, u32[]{:S(2)}, u32[]{:S(2)}) %collective-permute-start.18) | collective-permute-done | bytes 65568 | tf_op jit(solution)/shard_map/ppermute | solution.py:32
  74.1 1.1 collective-permute-start.22
  76.1 1.1 collective-permute-done.22.refs_3_
  77.2 1.6 %collective-permute-done.21.refs_2_ = bf16[16,64]{1,0:T(8,128)(2,1)S(1)} collective-permute-done((bf16[16,64]{1,0:T(8,128)(2,1)S(1)}, bf16[16,64]{1,0:T(8,128)(2,1)S(1)}, u32[]{:S(2)}, u32[]{:S(2)}) %collective-permute-start.21) | collective-permute-done | bytes 2080 | tf_op jit(solution)/shard_map/ppermute | solution.py:32
  78.8 1.6 %collective-permute-start.25 = (bf16[16,64]{1,0:T(8,128)(2,1)S(1)}, bf16[16,64]{1,0:T(8,128)(2,1)S(1)}, u32[]{:S(2)}, u32[]{:S(2)}) collective-permute-start(bf16[16,64]{1,0:T(8,128)(2,1)S(1)} %sum.3.refs_0_), channel_id=1, source_target_pairs={{0,12},{1,13},{2,14},{3,15},{4,8},{5,9},{6,10},{7,11},{8,4},{9,5},... | collective-permute-start | bytes 6152 | tf_op jit(solution)/shard_map/ppermute | solution.py:32
  81.2 2.1 %collective-permute-start.23 = (bf16[16,64]{1,0:T(8,128)(2,1)S(1)}, bf16[16,64]{1,0:T(8,128)(2,1)S(1)}, u32[]{:S(2)}, u32[]{:S(2)}) collective-permute-start(bf16[16,64]{1,0:T(8,128)(2,1)S(1)} %sum.3.refs_0_), channel_id=1, source_target_pairs={{0,4},{1,5},{2,6},{3,7},{4,0},{5,1},{6,2},{7,3},{8,12},{9,13},{10,... | collective-permute-start | bytes 6152 | tf_op jit(solution)/shard_map/ppermute | solution.py:32
  83.3 1.5 %project.3 = (f32[16,512]{1,0:T(8,128)S(1)}, f32[16,128]{1,0:T(8,128)S(1)}) custom-call(bf16[16,8192]{1,0:T(8,128)(2,1)S(1)} %get-tuple-element.65.rows_ref, bf16[8192,512]{1,0:T(8,128)(2,1)S(1)} %get-tuple-element.49.query_w, bf16[8192,128]{1,0:T(8,128)(2,1)S(1)} %get-tuple-element.50.fresh_w), custom_call_target="tpu_custom_call" | custom-call | flops 167772160 | bytes 10485760 | tf_op jit(solution)/shard_map/project/pallas_call | solution.py:53
  85.5 10.2 %all_to_all.27.refs_0_ = bf16[16,8,128]{2,1,0:T(8,128)(2,1)S(1)} all-to-all(bf16[16,8,128]{2,1,0:T(8,128)(2,1)S(1)} %up.3), channel_id=1, replica_groups=mesh['groups'=2,'replica'=16] {'replica'}, dimensions={0} | all-to-all | bytes 65536 | tf_op jit(solution)/shard_map/all_to_all | solution.py:40
  96.5 9.1 %all_to_all.28.lines_ref = bf16[16,4,128]{2,1,0:T(4,128)(2,1)S(1)} all-to-all(bf16[16,4,128]{2,1,0:T(4,128)(2,1)S(1)} %attend.3), channel_id=1, replica_groups=mesh['groups'=2,'replica'=16] {'replica'}, dimensions={0} | all-to-all | bytes 32768 | tf_op jit(solution)/shard_map/all_to_all | solution.py:40
  105.6 1.3 %output.3 = (f32[8,8192]{1,0:T(8,128)S(1)}, bf16[8,8192]{1,0:T(8,128)(2,1)S(1)}) custom-call(bf16[16,4,128]{2,1,0:T(4,128)(2,1)S(1)} %all_to_all.28.lines_ref, s32[1]{0:T(128)} %bitcast._.refs_4_.me_ref, bf16[512,8192]{1,0:T(8,128)(2,1)S(1)} %get-tuple-element.57.weight_ref), custom_call_target="tpu_custom_call" | custom-call | flops 134217728 | bytes 8388608 | tf_op jit(solution)/shard_map/output/pallas_call | solution.py:53
  106.9 1.4 %collective-permute-done.26.other_ref = bf16[8,8192]{1,0:T(8,128)(2,1)S(1)} collective-permute-done((bf16[8,8192]{1,0:T(8,128)(2,1)S(1)}, bf16[8,8192]{1,0:T(8,128)(2,1)S(1)}, u32[]{:S(2)}, u32[]{:S(2)}) %collective-permute-start.26) | collective-permute-done | bytes 131104 | tf_op jit(solution)/shard_map/ppermute | solution.py:32
  108.4 10.0 %all_to_all.29.parts_ref = bf16[8,8,1024]{2,1,0:T(8,128)(2,1)S(1)} all-to-all(bf16[8,8,1024]{2,1,0:T(8,128)(2,1)S(1)} %partial.1), channel_id=1, replica_groups={{0,2,4,6,8,10,12,14},{1,3,5,7,9,11,13,15},{16,18,20,22,24,26,28,30},{17..., dimensions={0} | all-to-all | bytes 262144 | tf_op jit(solution)/shard_map/all_to_all | solution.py:45
  (56 shorter events, 14.2 us)
Async XLA Ops:
  1.3 0.8 copy-start.1
  2.1 9.8 %collective-permute-start.2 = (bf16[1,8320]{1,0:T(2,128)(2,1)S(1)}, bf16[1,8320]{1,0:T(2,128)(2,1)S(1)}, u32[]{:S(2)}, u32[]{:S(2)}) collective-permute-start(bf16[1,8320]{1,0:T(2,128)(2,1)S(1)} %get-tuple-element.39.refs_0_), channel_id=1, source_target_pairs={{0,12},{1,13},{2,14},{3,15},{4,8},{5,9},{6,10},{7,11},{8,4},{9,5},... | collective-permute-start | bytes 49928 | tf_op jit(solution)/shard_map/ppermute | solution.py:32
  7.2 4.8 %collective-permute-start.1 = (bf16[1,8320]{1,0:T(2,128)(2,1)S(1)}, bf16[1,8320]{1,0:T(2,128)(2,1)S(1)}, u32[]{:S(2)}, u32[]{:S(2)}) collective-permute-start(bf16[1,8320]{1,0:T(2,128)(2,1)S(1)} %get-tuple-element.39.refs_0_), channel_id=1, source_target_pairs={{0,8},{1,9},{2,10},{3,11},{4,12},{5,13},{6,14},{7,15},{8,0},{9,1},... | collective-permute-start | bytes 49928 | tf_op jit(solution)/shard_map/ppermute | solution.py:32
  7.2 4.8 %collective-permute-start = (bf16[1,8320]{1,0:T(2,128)(2,1)S(1)}, bf16[1,8320]{1,0:T(2,128)(2,1)S(1)}, u32[]{:S(2)}, u32[]{:S(2)}) collective-permute-start(bf16[1,8320]{1,0:T(2,128)(2,1)S(1)} %get-tuple-element.39.refs_0_), channel_id=1, source_target_pairs={{0,4},{1,5},{2,6},{3,7},{4,0},{5,1},{6,2},{7,3},{8,12},{9,13},{10,... | collective-permute-start | bytes 49928 | tf_op jit(solution)/shard_map/ppermute | solution.py:32
  7.8 4.2 %copy-start = (bf16[8192]{0:T(1024)(128)(2,1)S(1)}, bf16[8192]{0:T(1024)(128)(2,1)}, u32[]{:S(2)}) copy-start(bf16[8192]{0:T(1024)(128)(2,1)} %param.12) | copy-start | bytes 49156
  12.3 5.9 %copy-start.2 = (s32[32]{0:T(128)S(1)}, s32[32]{0:T(128)}, u32[]{:S(2)}) copy-start(s32[32]{0:T(128)} %param.19) | copy-start | bytes 388
  12.3 5.3 %collective-permute-start.5 = (bf16[4,8320]{1,0:T(4,128)(2,1)S(1)}, bf16[4,8320]{1,0:T(4,128)(2,1)S(1)}, u32[]{:S(2)}, u32[]{:S(2)}) collective-permute-start(bf16[4,8320]{1,0:T(4,128)(2,1)S(1)} %get-tuple-element.42.refs_0_), channel_id=1, source_target_pairs={{0,3},{1,2},{2,1},{3,0},{4,7},{5,6},{6,5},{7,4},{8,11},{9,10},{10,... | collective-permute-start | bytes 199688 | tf_op jit(solution)/shard_map/ppermute | solution.py:32
  12.6 5.6 %collective-permute-start.4 = (bf16[4,8320]{1,0:T(4,128)(2,1)S(1)}, bf16[4,8320]{1,0:T(4,128)(2,1)S(1)}, u32[]{:S(2)}, u32[]{:S(2)}) collective-permute-start(bf16[4,8320]{1,0:T(4,128)(2,1)S(1)} %get-tuple-element.42.refs_0_), channel_id=1, source_target_pairs={{0,2},{1,3},{2,0},{3,1},{4,6},{5,7},{6,4},{7,5},{8,10},{9,11},{10,... | collective-permute-start | bytes 199688 | tf_op jit(solution)/shard_map/ppermute | solution.py:32
  14.0 4.3 %collective-permute-start.3 = (bf16[4,8320]{1,0:T(4,128)(2,1)S(1)}, bf16[4,8320]{1,0:T(4,128)(2,1)S(1)}, u32[]{:S(2)}, u32[]{:S(2)}) collective-permute-start(bf16[4,8320]{1,0:T(4,128)(2,1)S(1)} %get-tuple-element.42.refs_0_), channel_id=1, source_target_pairs={{0,1},{1,0},{2,3},{3,2},{4,5},{5,4},{6,7},{7,6},{8,9},{9,8},{10,11... | collective-permute-start | bytes 199688 | tf_op jit(solution)/shard_map/ppermute | solution.py:32
  19.2 4.8 %collective-permute-start.8 = (bf16[16,64]{1,0:T(8,128)(2,1)S(1)}, bf16[16,64]{1,0:T(8,128)(2,1)S(1)}, u32[]{:S(2)}, u32[]{:S(2)}) collective-permute-start(bf16[16,64]{1,0:T(8,128)(2,1)S(1)} %get-tuple-element.46.refs_3_.refs_0_), channel_id=1, source_target_pairs={{0,3},{1,2},{2,1},{3,0},{4,7},{5,6},{6,5},{7,4},{8,11},{9,10},{10,... | collective-permute-start | bytes 6152 | tf_op jit(solution)/shard_map/ppermute | solution.py:32
  19.8 4.2 %collective-permute-start.7 = (bf16[16,64]{1,0:T(8,128)(2,1)S(1)}, bf16[16,64]{1,0:T(8,128)(2,1)S(1)}, u32[]{:S(2)}, u32[]{:S(2)}) collective-permute-start(bf16[16,64]{1,0:T(8,128)(2,1)S(1)} %get-tuple-element.46.refs_3_.refs_0_), channel_id=1, source_target_pairs={{0,2},{1,3},{2,0},{3,1},{4,6},{5,7},{6,4},{7,5},{8,10},{9,11},{10,... | collective-permute-start | bytes 6152 | tf_op jit(solution)/shard_map/ppermute | solution.py:32
  20.9 3.1 %collective-permute-start.6 = (bf16[16,64]{1,0:T(8,128)(2,1)S(1)}, bf16[16,64]{1,0:T(8,128)(2,1)S(1)}, u32[]{:S(2)}, u32[]{:S(2)}) collective-permute-start(bf16[16,64]{1,0:T(8,128)(2,1)S(1)} %get-tuple-element.46.refs_3_.refs_0_), channel_id=1, source_target_pairs={{0,1},{1,0},{2,3},{3,2},{4,5},{5,4},{6,7},{7,6},{8,9},{9,8},{10,11... | collective-permute-start | bytes 6152 | tf_op jit(solution)/shard_map/ppermute | solution.py:32
  24.1 5.9 %collective-permute-start.11 = (bf16[16,64]{1,0:T(8,128)(2,1)S(1)}, bf16[16,64]{1,0:T(8,128)(2,1)S(1)}, u32[]{:S(2)}, u32[]{:S(2)}) collective-permute-start(bf16[16,64]{1,0:T(8,128)(2,1)S(1)} %sum.2.refs_0_), channel_id=1, source_target_pairs={{0,12},{1,13},{2,14},{3,15},{4,8},{5,9},{6,10},{7,11},{8,4},{9,5},... | collective-permute-start | bytes 6152 | tf_op jit(solution)/shard_map/ppermute | solution.py:32
  27.8 4.5 %collective-permute-start.10 = (bf16[16,64]{1,0:T(8,128)(2,1)S(1)}, bf16[16,64]{1,0:T(8,128)(2,1)S(1)}, u32[]{:S(2)}, u32[]{:S(2)}) collective-permute-start(bf16[16,64]{1,0:T(8,128)(2,1)S(1)} %sum.2.refs_0_), channel_id=1, source_target_pairs={{0,8},{1,9},{2,10},{3,11},{4,12},{5,13},{6,14},{7,15},{8,0},{9,1},... | collective-permute-start | bytes 6152 | tf_op jit(solution)/shard_map/ppermute | solution.py:32
  27.8 4.5 %collective-permute-start.9 = (bf16[16,64]{1,0:T(8,128)(2,1)S(1)}, bf16[16,64]{1,0:T(8,128)(2,1)S(1)}, u32[]{:S(2)}, u32[]{:S(2)}) collective-permute-start(bf16[16,64]{1,0:T(8,128)(2,1)S(1)} %sum.2.refs_0_), channel_id=1, source_target_pairs={{0,4},{1,5},{2,6},{3,7},{4,0},{5,1},{6,2},{7,3},{8,12},{9,13},{10,... | collective-permute-start | bytes 6152 | tf_op jit(solution)/shard_map/ppermute | solution.py:32
  54.2 1.4 %collective-permute-start.12 = (bf16[8,8192]{1,0:T(8,128)(2,1)S(1)}, bf16[8,8192]{1,0:T(8,128)(2,1)S(1)}, u32[]{:S(2)}, u32[]{:S(2)}) collective-permute-start(bf16[8,8192]{1,0:T(8,128)(2,1)S(1)} %get-tuple-element.59), channel_id=1, source_target_pairs={{0,1},{1,0},{2,3},{3,2},{4,5},{5,4},{6,7},{7,6},{8,9},{9,8},{10,11... | collective-permute-start | bytes 393224 | tf_op jit(solution)/shard_map/ppermute | solution.py:32
  55.6 4.3 %collective-permute-start.13 = (bf16[4,8192]{1,0:T(4,128)(2,1)S(1)}, bf16[4,8192]{1,0:T(4,128)(2,1)S(1)}, u32[]{:S(2)}, u32[]{:S(2)}) collective-permute-start(bf16[4,8192]{1,0:T(4,128)(2,1)S(1)} %get-tuple-element.61), channel_id=1, source_target_pairs={{0,2},{1,3},{2,0},{3,1},{4,6},{5,7},{6,4},{7,5},{8,10},{9,11},{10,... | collective-permute-start | bytes 196616 | tf_op jit(solution)/shard_map/ppermute | solution.py:32
  60.0 6.4 %collective-permute-start.16 = (bf16[4,8192]{1,0:T(4,128)(2,1)S(1)}, bf16[4,8192]{1,0:T(4,128)(2,1)S(1)}, u32[]{:S(2)}, u32[]{:S(2)}) collective-permute-start(bf16[4,8192]{1,0:T(4,128)(2,1)S(1)} %fold.3.refs_0_), channel_id=1, source_target_pairs={{0,12},{1,13},{2,14},{3,15},{4,8},{5,9},{6,10},{7,11},{8,4},{9,5},... | collective-permute-start | bytes 196616 | tf_op jit(solution)/shard_map/ppermute | solution.py:32
  60.5 7.1 %collective-permute-start.15 = (bf16[4,8192]{1,0:T(4,128)(2,1)S(1)}, bf16[4,8192]{1,0:T(4,128)(2,1)S(1)}, u32[]{:S(2)}, u32[]{:S(2)}) collective-permute-start(bf16[4,8192]{1,0:T(4,128)(2,1)S(1)} %fold.3.refs_0_), channel_id=1, source_target_pairs={{0,8},{1,9},{2,10},{3,11},{4,12},{5,13},{6,14},{7,15},{8,0},{9,1},... | collective-permute-start | bytes 196616 | tf_op jit(solution)/shard_map/ppermute | solution.py:32
  62.0 5.7 %collective-permute-start.14 = (bf16[4,8192]{1,0:T(4,128)(2,1)S(1)}, bf16[4,8192]{1,0:T(4,128)(2,1)S(1)}, u32[]{:S(2)}, u32[]{:S(2)}) collective-permute-start(bf16[4,8192]{1,0:T(4,128)(2,1)S(1)} %fold.3.refs_0_), channel_id=1, source_target_pairs={{0,4},{1,5},{2,6},{3,7},{4,0},{5,1},{6,2},{7,3},{8,12},{9,13},{10,... | collective-permute-start | bytes 196616 | tf_op jit(solution)/shard_map/ppermute | solution.py:32
  68.3 3.8 %collective-permute-start.19 = (bf16[4,8192]{1,0:T(4,128)(2,1)S(1)}, bf16[4,8192]{1,0:T(4,128)(2,1)S(1)}, u32[]{:S(2)}, u32[]{:S(2)}) collective-permute-start(bf16[4,8192]{1,0:T(4,128)(2,1)S(1)} %get-tuple-element.63.refs_0_), channel_id=1, source_target_pairs={{0,3},{1,2},{2,1},{3,0},{4,7},{5,6},{6,5},{7,4},{8,11},{9,10},{10,... | collective-permute-start | bytes 196616 | tf_op jit(solution)/shard_map/ppermute | solution.py:32
  68.4 5.0 %collective-permute-start.18 = (bf16[4,8192]{1,0:T(4,128)(2,1)S(1)}, bf16[4,8192]{1,0:T(4,128)(2,1)S(1)}, u32[]{:S(2)}, u32[]{:S(2)}) collective-permute-start(bf16[4,8192]{1,0:T(4,128)(2,1)S(1)} %get-tuple-element.63.refs_0_), channel_id=1, source_target_pairs={{0,2},{1,3},{2,0},{3,1},{4,6},{5,7},{6,4},{7,5},{8,10},{9,11},{10,... | collective-permute-start | bytes 196616 | tf_op jit(solution)/shard_map/ppermute | solution.py:32
  69.0 4.4 %collective-permute-start.17 = (bf16[4,8192]{1,0:T(4,128)(2,1)S(1)}, bf16[4,8192]{1,0:T(4,128)(2,1)S(1)}, u32[]{:S(2)}, u32[]{:S(2)}) collective-permute-start(bf16[4,8192]{1,0:T(4,128)(2,1)S(1)} %get-tuple-element.63.refs_0_), channel_id=1, source_target_pairs={{0,1},{1,0},{2,3},{3,2},{4,5},{5,4},{6,7},{7,6},{8,9},{9,8},{10,11... | collective-permute-start | bytes 196616 | tf_op jit(solution)/shard_map/ppermute | solution.py:32
  74.1 3.1 %collective-permute-start.22 = (bf16[16,64]{1,0:T(8,128)(2,1)S(1)}, bf16[16,64]{1,0:T(8,128)(2,1)S(1)}, u32[]{:S(2)}, u32[]{:S(2)}) collective-permute-start(bf16[16,64]{1,0:T(8,128)(2,1)S(1)} %get-tuple-element.64.refs_0_), channel_id=1, source_target_pairs={{0,3},{1,2},{2,1},{3,0},{4,7},{5,6},{6,5},{7,4},{8,11},{9,10},{10,... | collective-permute-start | bytes 6152 | tf_op jit(solution)/shard_map/ppermute | solution.py:32
  75.2 3.6 %collective-permute-start.21 = (bf16[16,64]{1,0:T(8,128)(2,1)S(1)}, bf16[16,64]{1,0:T(8,128)(2,1)S(1)}, u32[]{:S(2)}, u32[]{:S(2)}) collective-permute-start(bf16[16,64]{1,0:T(8,128)(2,1)S(1)} %get-tuple-element.64.refs_0_), channel_id=1, source_target_pairs={{0,2},{1,3},{2,0},{3,1},{4,6},{5,7},{6,4},{7,5},{8,10},{9,11},{10,... | collective-permute-start | bytes 6152 | tf_op jit(solution)/shard_map/ppermute | solution.py:32
  75.9 2.9 %collective-permute-start.20 = (bf16[16,64]{1,0:T(8,128)(2,1)S(1)}, bf16[16,64]{1,0:T(8,128)(2,1)S(1)}, u32[]{:S(2)}, u32[]{:S(2)}) collective-permute-start(bf16[16,64]{1,0:T(8,128)(2,1)S(1)} %get-tuple-element.64.refs_0_), channel_id=1, source_target_pairs={{0,1},{1,0},{2,3},{3,2},{4,5},{5,4},{6,7},{7,6},{8,9},{9,8},{10,11... | collective-permute-start | bytes 6152 | tf_op jit(solution)/shard_map/ppermute | solution.py:32
  78.8 5.9 %collective-permute-start.25 = (bf16[16,64]{1,0:T(8,128)(2,1)S(1)}, bf16[16,64]{1,0:T(8,128)(2,1)S(1)}, u32[]{:S(2)}, u32[]{:S(2)}) collective-permute-start(bf16[16,64]{1,0:T(8,128)(2,1)S(1)} %sum.3.refs_0_), channel_id=1, source_target_pairs={{0,12},{1,13},{2,14},{3,15},{4,8},{5,9},{6,10},{7,11},{8,4},{9,5},... | collective-permute-start | bytes 6152 | tf_op jit(solution)/shard_map/ppermute | solution.py:32
  80.4 4.5 %collective-permute-start.24 = (bf16[16,64]{1,0:T(8,128)(2,1)S(1)}, bf16[16,64]{1,0:T(8,128)(2,1)S(1)}, u32[]{:S(2)}, u32[]{:S(2)}) collective-permute-start(bf16[16,64]{1,0:T(8,128)(2,1)S(1)} %sum.3.refs_0_), channel_id=1, source_target_pairs={{0,8},{1,9},{2,10},{3,11},{4,12},{5,13},{6,14},{7,15},{8,0},{9,1},... | collective-permute-start | bytes 6152 | tf_op jit(solution)/shard_map/ppermute | solution.py:32
  81.2 3.7 %collective-permute-start.23 = (bf16[16,64]{1,0:T(8,128)(2,1)S(1)}, bf16[16,64]{1,0:T(8,128)(2,1)S(1)}, u32[]{:S(2)}, u32[]{:S(2)}) collective-permute-start(bf16[16,64]{1,0:T(8,128)(2,1)S(1)} %sum.3.refs_0_), channel_id=1, source_target_pairs={{0,4},{1,5},{2,6},{3,7},{4,0},{5,1},{6,2},{7,3},{8,12},{9,13},{10,... | collective-permute-start | bytes 6152 | tf_op jit(solution)/shard_map/ppermute | solution.py:32
  106.9 1.4 %collective-permute-start.26 = (bf16[8,8192]{1,0:T(8,128)(2,1)S(1)}, bf16[8,8192]{1,0:T(8,128)(2,1)S(1)}, u32[]{:S(2)}, u32[]{:S(2)}) collective-permute-start(bf16[8,8192]{1,0:T(8,128)(2,1)S(1)} %get-tuple-element.71), channel_id=1, source_target_pairs={{0,1},{1,0},{2,3},{3,2},{4,5},{5,4},{6,7},{7,6},{8,9},{9,8},{10,11... | collective-permute-start | bytes 393224 | tf_op jit(solution)/shard_map/ppermute | solution.py:32

commit v14 on v13

--- a/solution.py
+++ b/solution.py
@@ -110,24 +110,6 @@
         copy.wait()
 
 
-def member_kernel(near, far, width, *refs):
-    pieces, refs = refs[:near], refs[near:]
-    me_ref, storage_ref, _, member_ref, adapter_ref, held = refs
-    kept = member_ref.shape[1]
-    count = near * far
-    me = me_ref[0]
-    for l in range(near):
-        digits = pieces[l][:, width:].astype(jnp.float32)
-        for k in range(far):
-            held[pl.ds(me ^ (k * near + l), 1), :] = digits[k : k + 1]
-    adapter = (held[:, 0:1] + 256.0 * held[:, 1:2]).astype(jnp.int32)
-    adapter_ref[...] = adapter
-    table = storage_ref.shape[1]
-    chosen = jnp.where(iota((count, table), 1) == adapter, storage_ref[...], 0)
-    storage = jnp.sum(chosen.astype(jnp.float32), axis=1, keepdims=True).astype(jnp.int32)
-    member_ref[...] = (storage - me * kept == iota((count, kept), 1)).astype(jnp.int32)
-
-
 def low_terms(held, member_ref, down_ref, rows_ref, low_ref):
     rows = held[...].astype(jnp.bfloat16)
     rows_ref[...] = rows
@@ -138,14 +120,40 @@
     low_ref[...] = low.astype(jnp.bfloat16)
 
 
-def low_kernel(near, far, *refs):
-    pieces, refs = refs[:near], refs[near:]
-    me_ref, member_ref, down_ref, rows_ref, low_ref, held = refs
+def gathered(near, far, pieces, me, held):
     width = held.shape[1]
     for l in range(near):
         block = pieces[l][:, :width].astype(jnp.float32)
         for k in range(far):
-            held[pl.ds(me_ref[0] ^ (k * near + l), 1), :] = block[k : k + 1]
+            held[pl.ds(me ^ (k * near + l), 1), :] = block[k : k + 1]
+
+
+def low_kernel(near, far, *refs):
+    pieces, refs = refs[:near], refs[near:]
+    me_ref, member_ref, down_ref, rows_ref, low_ref, held = refs
+    gathered(near, far, pieces, me_ref[0], held)
+    low_terms(held, member_ref, down_ref, rows_ref, low_ref)
+
+
+def low_first_kernel(near, far, *refs):
+    pieces, refs = refs[:near], refs[near:]
+    me_ref, storage_ref, down_ref, _, rows_ref, low_ref, member_ref, adapter_ref = refs[:8]
+    held, digits = refs[-2:]
+    width = held.shape[1]
+    me = me_ref[0]
+    kept = member_ref.shape[1]
+    count = near * far
+    for l in range(near):
+        block = pieces[l][:, width:].astype(jnp.float32)
+        for k in range(far):
+            digits[pl.ds(me ^ (k * near + l), 1), :] = block[k : k + 1]
+    adapter = (digits[:, 0:1] + 256.0 * digits[:, 1:2]).astype(jnp.int32)
+    adapter_ref[...] = adapter
+    table = storage_ref.shape[1]
+    chosen = jnp.where(iota((count, table), 1) == adapter, storage_ref[...], 0)
+    storage = jnp.sum(chosen.astype(jnp.float32), axis=1, keepdims=True).astype(jnp.int32)
+    member_ref[...] = (storage - me * kept == iota((count, kept), 1)).astype(jnp.int32)
+    gathered(near, far, pieces, me, held)
     low_terms(held, member_ref, down_ref, rows_ref, low_ref)
 
 
@@ -160,25 +168,11 @@
     out_ref[:, width:] = rows[:, width:].astype(jnp.bfloat16)
 
 
-def distance(slot, near, far):
-    size, total = near * far, (slot % far) * near
-    bit = 1
-    while bit < near:
-        size //= 2
-        total = total + ((slot // size) % 2) * bit
-        bit *= 2
-    return total
-
-
-def fold_kernel(own_ref, other_ref, keep_ref, away_ref):
-    total = own_ref[...] + other_ref[...].astype(jnp.float32)
-    half = keep_ref.shape[0]
-    keep_ref[...] = total[:half]
-    away_ref[...] = total[half:].astype(jnp.bfloat16)
-
-
-def folded_kernel(own_ref, other_ref, out_ref):
-    out_ref[...] = (own_ref[...] + other_ref[...].astype(jnp.float32)).astype(jnp.bfloat16)
+def fold_kernel(*refs):
+    total = refs[0][...]
+    for ref in refs[1:-1]:
+        total = total + ref[...].astype(jnp.float32)
+    refs[-1][...] = total.astype(jnp.bfloat16)
 
 
 def next_kernel(far, *refs):
@@ -219,8 +213,9 @@
     table = up_ref.shape[0]
     some = min(table, 32)
     wide = some * rank
-    repeat = (iota((rank, wide), 1) % rank == iota((rank, wide), 0)).astype(jnp.bfloat16)
-    wide_low = dot(low, repeat)
+    low = low.astype(jnp.float32)
+    wide_low = jnp.concatenate([low] * max(1, LANES // rank), axis=1)
+    wide_low = jnp.concatenate([wide_low] * (wide // wide_low.shape[1]), axis=1)
     place = iota((count, wide), 1) // rank
     for start in range(0, table, some):
         spread = jnp.where(place + start == adapter_ref[...], wide_low, 0.0).astype(jnp.bfloat16)
@@ -338,14 +333,16 @@
             out_ref[k] = out[k : k + 1].astype(jnp.bfloat16)
 
 
-def output_kernel(split, lines_ref, me_ref, weight_ref, own_ref, away_ref, held):
+def output_kernel(split, lines_ref, me_ref, weight_ref, own_ref, *refs):
+    aways, held = refs[:-1], refs[-1]
     count, each, line = lines_ref.shape
     chips = count // CORES
     for k in range(count):
         held[k, :each, :] = lines_ref[k].astype(jnp.float32)
     slot = iota((count, count), 0)
     if split:
-        origin = me_ref[0] ^ distance(slot, *split)
+        near, far = split
+        origin = me_ref[0] ^ ((slot % far) * near + slot // far)
     else:
         origin = (slot % chips) * CORES + ((me_ref[0] % CORES) ^ (slot // chips))
     order = (iota((count, count), 1) == origin).astype(jnp.bfloat16)
@@ -358,8 +355,10 @@
     for c in range(8):
         part = slice(c * wide, (c + 1) * wide)
         out = dot(rows, weight_ref[:, part])
-        own_ref[:, part] = out[:chips]
-        away_ref[:, part] = out[chips:].astype(jnp.bfloat16)
+        some = own_ref.shape[0]
+        own_ref[:, part] = out[:some]
+        for l, ref in enumerate(aways):
+            ref[:, part] = out[(l + 1) * some : (l + 2) * some].astype(jnp.bfloat16)
 
 
 def partial_kernel(own_ref, other_ref, out_ref):
@@ -450,17 +449,25 @@
             )(*pieces, scale, token)
             (output_w,), token = stash(token, [output_weight])
             pieces = across(carried, near_steps, count)
-            member, adapter = call(
-                functools.partial(member_kernel, near, far, width),
-                [shape((count, kept), jnp.int32), shape((count, 1), jnp.int32)],
-                "member",
-                [pltpu.VMEM((count, LANES), jnp.float32)],
-            )(*pieces, me, storage, token, specs=[vmem] * near + [smem, vmem, vmem])
+            outs = outs + [shape((count, kept), jnp.int32), shape((count, 1), jnp.int32)]
+            rows, low, member, adapter = call(
+                functools.partial(low_first_kernel, near, far),
+                outs,
+                "low",
+                scratch + [pltpu.VMEM((count, LANES), jnp.float32)],
+            )(
+                *pieces,
+                me,
+                storage,
+                down_w,
+                token,
+                specs=[vmem] * near + [smem] + [vmem] * 3,
+            )
         else:
             pieces = across(carried, near_steps, count)
-        rows, low = call(functools.partial(low_kernel, near, far), outs, "low", scratch)(
-            *pieces, me, member, down_w, specs=[vmem] * near + [smem, vmem, vmem]
-        )
+            rows, low = call(functools.partial(low_kernel, near, far), outs, "low", scratch)(
+                *pieces, me, member, down_w, specs=[vmem] * near + [smem, vmem, vmem]
+            )
         behind = []
         if first:
             rest = [key_value_weight, adapter_up_weight, key_value_cache]
@@ -508,9 +515,10 @@
             past = tuple(outs[1:])
 
         lines = swap(outs[0])
-        own, away = call(
+        some = chips if last else far
+        own, *aways = call(
             functools.partial(output_kernel, None if last else (near, far)),
-            [shape((chips, width), jnp.float32), shape((chips, width))],
+            [shape((some, width), jnp.float32)] + [shape((some, width))] * (count // some - 1),
             "output",
             [pltpu.VMEM((count, 8, line), jnp.float32)],
             flops=2 * count * width * columns,
@@ -519,19 +527,13 @@
 
         if last:
             (parts,) = call(partial_kernel, [shape((chips, FOLD, width // FOLD))], "partial")(
-                own, shift(away, 1, count)
+                own, shift(aways[0], 1, count)
             )
             parts = chips_swap(parts, count)
             (out,) = call(finish_kernel, [shape((STEPS, width))], "finish")(parts, hidden)
             return out.reshape(STEPS, 1, width)
-        bit = 1
-        while bit < near // 2:
-            half = own.shape[0] // 2
-            own, away = call(
-                fold_kernel, [shape((half, width), jnp.float32), shape((half, width))], "fold"
-            )(own, shift(away, bit, count))
-            bit *= 2
-        (own,) = call(folded_kernel, [shape((far, width))], "fold")(own, shift(away, bit, count))
+        aways = [shift(a, d, count) for a, d in zip(aways, near_steps)]
+        (own,) = call(fold_kernel, [shape((far, width))], "fold")(own, *aways)
         hidden, carried = call(
             functools.partial(next_kernel, far), [shape((1, width)), shape((far, width))], "next"
         )(*across(own, far_steps, count), column, scale)

time: 120 us -> 120 us (level)
  starting transfers between devices: 27.3 us -> 28.6 us
    ppermute x27 -> x28, starting transfers between devices: 27.3 us -> 28.6 us  [shift(): return lax.ppermute(block, AXIS, [(i, i ^ distance) for i in range(count)])]
    ppermute x27 -> x28, waiting for transfers between devices: 18.9 us -> 18 us  [shift(): return lax.ppermute(block, AXIS, [(i, i ^ distance) for i in range(count)])]
    pallas_call x23 -> x21, Pallas kernels: 22.2 us -> 21.8 us  [run(): pl.pallas_call(body, out_shape=outs, in_specs=[pl.BlockSpec(memory_space=...]
  transfers between devices with their start and end apart: 27 -> 28, of which waited for: 13 -> 13; matrix products, arithmetic and copies ran while one was open for 0% -> 0% of each run, Pallas kernels for 11% -> 11%
where the time goes in v14:
time: 120 us
  blocking collectives  48.9 us (41%)
  starting transfers between devices  28.6 us (24%)
  Pallas kernels  21.8 us (18%)
  waiting for transfers between devices  18 us (15%)
  between operations  1.47 us (1%)
    all_to_all x4, blocking collectives, swap(): return lax.all_to_all(blocks, AXIS, split_axis=0, concat_axis=0, tiled=True)  38.9 us
    ppermute x28, starting transfers between devices, shift(): return lax.ppermute(block, AXIS, [(i, i ^ distance) for i in range(count)])  28.6 us
    pallas_call x21, Pallas kernels, run(): pl.pallas_call(body, out_shape=outs, in_specs=[pl.BlockSpec(memory_space=...  21.8 us
    ppermute x28, waiting for transfers between devices, shift(): return lax.ppermute(block, AXIS, [(i, i ^ distance) for i in range(count)])  18 us
    all_to_all x1, blocking collectives, chips_swap(): lax.all_to_all(blocks, AXIS, split_axis=0, concat_axis=0, axis_index_grou...  9.97 us
  transfers between devices with their start and end apart: 28, of which 13 were waited for; matrix products, arithmetic and copies ran while one was open for 0% of the time, Pallas kernels for 11%

profile of v14, /device:TPU:0, one launch (start us, length us, event | category | flops | bytes accessed | tf_op | source)
XLA Modules:
  0.0 119.6 jit_solution(2988337547953734542)
XLA Ops:
  2.1 5.1 %collective-permute-start.2 = (bf16[1,8320]{1,0:T(2,128)(2,1)S(1)}, bf16[1,8320]{1,0:T(2,128)(2,1)S(1)}, u32[]{:S(2)}, u32[]{:S(2)}) collective-permute-start(bf16[1,8320]{1,0:T(2,128)(2,1)S(1)} %get-tuple-element.39.refs_0_), channel_id=1, source_target_pairs={{0,12},{1,13},{2,14},{3,15},{4,8},{5,9},{6,10},{7,11},{8,4},{9,5},... | collective-permute-start | bytes 49928 | tf_op jit(solution)/shard_map/ppermute | solution.py:32
  7.8 4.0 %stash.3 = (bf16[8192,512]{1,0:T(8,128)(2,1)S(1)}, bf16[2,64,8192]{2,1,0:T(8,128)(2,1)S(1)}, s32[8,128]{1,0:T(8,128)S(1)}) custom-call(s32[8,128]{1,0:T(8,128)S(1)} %get-tuple-element.40.token_ref.refs_1_, bf16[8192,512]{1,0:T(8,128)(2,1)} %refs_0_.3, bf16[2,64,8192]{2,1,0:T(8,128)(2,1)} %bitcast.8), custom_call_target="tpu_custom_call" | custom-call | flops 1048576 | bytes 10485760 | tf_op jit(solution)/shard_map/stash/pallas_call | solution.py:53
  12.6 1.3 %collective-permute-start.4 = (bf16[4,8320]{1,0:T(4,128)(2,1)S(1)}, bf16[4,8320]{1,0:T(4,128)(2,1)S(1)}, u32[]{:S(2)}, u32[]{:S(2)}) collective-permute-start(bf16[4,8320]{1,0:T(4,128)(2,1)S(1)} %get-tuple-element.42.refs_0_), channel_id=1, source_target_pairs={{0,2},{1,3},{2,0},{3,1},{4,6},{5,7},{6,4},{7,5},{8,10},{9,11},{10,... | collective-permute-start | bytes 199688 | tf_op jit(solution)/shard_map/ppermute | solution.py:32
  14.3 3.4 %stash.4 = (bf16[512,8192]{1,0:T(8,128)(2,1)S(1)}, s32[8,128]{1,0:T(8,128)S(1)}) custom-call(s32[8,128]{1,0:T(8,128)S(1)} %get-tuple-element.41.refs_5_.token_ref, bf16[512,8192]{1,0:T(8,128)(2,1)} %refs_0_.4), custom_call_target="tpu_custom_call" | custom-call | flops 1048576 | bytes 8388608 | tf_op jit(solution)/shard_map/stash/pallas_call | solution.py:53
  19.6 1.1 collective-permute-start.7
  20.9 2.9 %stash.5 = (bf16[8192,128]{1,0:T(8,128)(2,1)S(1)}, bf16[32,64,512]{2,1,0:T(8,128)(2,1)S(1)}, bf16[1,2,512,1024]{3,2,1,0:T(8,128)(2,1)S(1)}, s32[8,128]{1,0:T(8,128)S(1)}) custom-call(s32[8,128]{1,0:T(8,128)S(1)} %get-tuple-element.44.refs_7_.token_ref, bf16[8192,128]{1,0:T(8,128)(2,1)} %refs_0_.5, bf16[32,64,512]{2,1,0:T(8,128)(2,1)} %refs_1_.1, ...), custom_call_target="tpu_custom_call" | custom-call | flops 1048576 | bytes 6291456 | tf_op jit(solution)/shard_map/stash/pallas_call | solution.py:53
  23.8 3.7 %collective-permute-start.11 = (bf16[16,64]{1,0:T(8,128)(2,1)S(1)}, bf16[16,64]{1,0:T(8,128)(2,1)S(1)}, u32[]{:S(2)}, u32[]{:S(2)}) collective-permute-start(bf16[16,64]{1,0:T(8,128)(2,1)S(1)} %sum.2.refs_0_), channel_id=1, source_target_pairs={{0,12},{1,13},{2,14},{3,15},{4,8},{5,9},{6,10},{7,11},{8,4},{9,5},... | collective-permute-start | bytes 6152 | tf_op jit(solution)/shard_map/ppermute | solution.py:32
  28.3 1.5 %project.2 = (f32[16,512]{1,0:T(8,128)S(1)}, f32[16,128]{1,0:T(8,128)S(1)}) custom-call(bf16[16,8192]{1,0:T(8,128)(2,1)S(1)} %get-tuple-element.47.rows_ref, bf16[8192,512]{1,0:T(8,128)(2,1)S(1)} %get-tuple-element.48.query_w, bf16[8192,128]{1,0:T(8,128)(2,1)S(1)} %get-tuple-element.49.fresh_w), custom_call_target="tpu_custom_call" | custom-call | flops 167772160 | bytes 10485760 | tf_op jit(solution)/shard_map/project/pallas_call | solution.py:53
  29.8 2.3 %collective-permute-done.10.refs_2_ = bf16[16,64]{1,0:T(8,128)(2,1)S(1)} collective-permute-done((bf16[16,64]{1,0:T(8,128)(2,1)S(1)}, bf16[16,64]{1,0:T(8,128)(2,1)S(1)}, u32[]{:S(2)}, u32[]{:S(2)}) %collective-permute-start.10) | collective-permute-done | bytes 2080 | tf_op jit(solution)/shard_map/ppermute | solution.py:32
  32.5 10.2 %all_to_all.25.refs_0_ = bf16[16,8,128]{2,1,0:T(8,128)(2,1)S(1)} all-to-all(bf16[16,8,128]{2,1,0:T(8,128)(2,1)S(1)} %up.2), channel_id=1, replica_groups=mesh['groups'=2,'replica'=16] {'replica'}, dimensions={0} | all-to-all | bytes 65536 | tf_op jit(solution)/shard_map/all_to_all | solution.py:40
  43.5 9.1 %all_to_all.26.lines_ref = bf16[16,4,128]{2,1,0:T(4,128)(2,1)S(1)} all-to-all(bf16[16,4,128]{2,1,0:T(4,128)(2,1)S(1)} %get-tuple-element.55), channel_id=1, replica_groups=mesh['groups'=2,'replica'=16] {'replica'}, dimensions={0} | all-to-all | bytes 32768 | tf_op jit(solution)/shard_map/all_to_all | solution.py:40
  52.6 1.3 %output.2 = (f32[4,8192]{1,0:T(4,128)S(1)}, bf16[4,8192]{1,0:T(4,128)(2,1)S(1)}, bf16[4,8192]{1,0:T(4,128)(2,1)S(1)}, bf16[4,8192]{1,0:T(4,128)(2,1)S(1)}) custom-call(bf16[16,4,128]{2,1,0:T(4,128)(2,1)S(1)} %all_to_all.26.lines_ref, s32[1]{0:T(128)} %bitcast._.refs_4_.me_ref, bf16[512,8192]{1,0:T(8,128)(2,1)S(1)} %get-tuple-element.56.weight_ref), custom_call_target="tpu_custom_call" | custom-call | flops 134217728 | bytes 8388608 | tf_op jit(solution)/shard_map/output/pallas_call | solution.py:53
  54.5 1.3 %collective-permute-start.14 = (bf16[4,8192]{1,0:T(4,128)(2,1)S(1)}, bf16[4,8192]{1,0:T(4,128)(2,1)S(1)}, u32[]{:S(2)}, u32[]{:S(2)}) collective-permute-start(bf16[4,8192]{1,0:T(4,128)(2,1)S(1)} %get-tuple-element.60), channel_id=1, source_target_pairs={{0,3},{1,2},{2,1},{3,0},{4,7},{5,6},{6,5},{7,4},{8,11},{9,10},{10,... | collective-permute-start | bytes 196616 | tf_op jit(solution)/shard_map/ppermute | solution.py:32
  55.8 3.1 %collective-permute-done.13.refs_2_ = bf16[4,8192]{1,0:T(4,128)(2,1)S(1)} collective-permute-done((bf16[4,8192]{1,0:T(4,128)(2,1)S(1)}, bf16[4,8192]{1,0:T(4,128)(2,1)S(1)}, u32[]{:S(2)}, u32[]{:S(2)}) %collective-permute-start.13) | collective-permute-done | bytes 65568 | tf_op jit(solution)/shard_map/ppermute | solution.py:32
  60.0 1.3 %collective-permute-start.16 = (bf16[4,8192]{1,0:T(4,128)(2,1)S(1)}, bf16[4,8192]{1,0:T(4,128)(2,1)S(1)}, u32[]{:S(2)}, u32[]{:S(2)}) collective-permute-start(bf16[4,8192]{1,0:T(4,128)(2,1)S(1)} %fold.1.refs_0_), channel_id=1, source_target_pairs={{0,8},{1,9},{2,10},{3,11},{4,12},{5,13},{6,14},{7,15},{8,0},{9,1},... | collective-permute-start | bytes 196616 | tf_op jit(solution)/shard_map/ppermute | solution.py:32
  61.3 2.6 %collective-permute-start.15 = (bf16[4,8192]{1,0:T(4,128)(2,1)S(1)}, bf16[4,8192]{1,0:T(4,128)(2,1)S(1)}, u32[]{:S(2)}, u32[]{:S(2)}) collective-permute-start(bf16[4,8192]{1,0:T(4,128)(2,1)S(1)} %fold.1.refs_0_), channel_id=1, source_target_pairs={{0,4},{1,5},{2,6},{3,7},{4,0},{5,1},{6,2},{7,3},{8,12},{9,13},{10,... | collective-permute-start | bytes 196616 | tf_op jit(solution)/shard_map/ppermute | solution.py:32
  63.9 2.4 %collective-permute-done.17.refs_3_ = bf16[4,8192]{1,0:T(4,128)(2,1)S(1)} collective-permute-done((bf16[4,8192]{1,0:T(4,128)(2,1)S(1)}, bf16[4,8192]{1,0:T(4,128)(2,1)S(1)}, u32[]{:S(2)}, u32[]{:S(2)}) %collective-permute-start.17) | collective-permute-done | bytes 65568 | tf_op jit(solution)/shard_map/ppermute | solution.py:32
  66.3 1.5 %collective-permute-done.16.refs_2_ = bf16[4,8192]{1,0:T(4,128)(2,1)S(1)} collective-permute-done((bf16[4,8192]{1,0:T(4,128)(2,1)S(1)}, bf16[4,8192]{1,0:T(4,128)(2,1)S(1)}, u32[]{:S(2)}, u32[]{:S(2)}) %collective-permute-start.16) | collective-permute-done | bytes 65568 | tf_op jit(solution)/shard_map/ppermute | solution.py:32
  68.6 1.1 collective-permute-start.19
  70.5 2.5 %collective-permute-done.20.refs_3_ = bf16[4,8192]{1,0:T(4,128)(2,1)S(1)} collective-permute-done((bf16[4,8192]{1,0:T(4,128)(2,1)S(1)}, bf16[4,8192]{1,0:T(4,128)(2,1)S(1)}, u32[]{:S(2)}, u32[]{:S(2)}) %collective-permute-start.20) | collective-permute-done | bytes 65568 | tf_op jit(solution)/shard_map/ppermute | solution.py:32
  75.3 1.0 collective-permute-start.22
  76.4 1.2 collective-permute-done.23.refs_3_
  77.6 1.3 %collective-permute-done.22.refs_2_ = bf16[16,64]{1,0:T(8,128)(2,1)S(1)} collective-permute-done((bf16[16,64]{1,0:T(8,128)(2,1)S(1)}, bf16[16,64]{1,0:T(8,128)(2,1)S(1)}, u32[]{:S(2)}, u32[]{:S(2)}) %collective-permute-start.22) | collective-permute-done | bytes 2080 | tf_op jit(solution)/shard_map/ppermute | solution.py:32
  78.9 1.7 %collective-permute-start.26 = (bf16[16,64]{1,0:T(8,128)(2,1)S(1)}, bf16[16,64]{1,0:T(8,128)(2,1)S(1)}, u32[]{:S(2)}, u32[]{:S(2)}) collective-permute-start(bf16[16,64]{1,0:T(8,128)(2,1)S(1)} %sum.3.refs_0_), channel_id=1, source_target_pairs={{0,12},{1,13},{2,14},{3,15},{4,8},{5,9},{6,10},{7,11},{8,4},{9,5},... | collective-permute-start | bytes 6152 | tf_op jit(solution)/shard_map/ppermute | solution.py:32
  81.0 2.4 %collective-permute-start.24 = (bf16[16,64]{1,0:T(8,128)(2,1)S(1)}, bf16[16,64]{1,0:T(8,128)(2,1)S(1)}, u32[]{:S(2)}, u32[]{:S(2)}) collective-permute-start(bf16[16,64]{1,0:T(8,128)(2,1)S(1)} %sum.3.refs_0_), channel_id=1, source_target_pairs={{0,4},{1,5},{2,6},{3,7},{4,0},{5,1},{6,2},{7,3},{8,12},{9,13},{10,... | collective-permute-start | bytes 6152 | tf_op jit(solution)/shard_map/ppermute | solution.py:32
  83.4 1.5 %project.3 = (f32[16,512]{1,0:T(8,128)S(1)}, f32[16,128]{1,0:T(8,128)S(1)}) custom-call(bf16[16,8192]{1,0:T(8,128)(2,1)S(1)} %get-tuple-element.65.rows_ref, bf16[8192,512]{1,0:T(8,128)(2,1)S(1)} %get-tuple-element.48.query_w, bf16[8192,128]{1,0:T(8,128)(2,1)S(1)} %get-tuple-element.49.fresh_w), custom_call_target="tpu_custom_call" | custom-call | flops 167772160 | bytes 10485760 | tf_op jit(solution)/shard_map/project/pallas_call | solution.py:53
  85.6 10.6 %all_to_all.27.refs_0_ = bf16[16,8,128]{2,1,0:T(8,128)(2,1)S(1)} all-to-all(bf16[16,8,128]{2,1,0:T(8,128)(2,1)S(1)} %up.3), channel_id=1, replica_groups=mesh['groups'=2,'replica'=16] {'replica'}, dimensions={0} | all-to-all | bytes 65536 | tf_op jit(solution)/shard_map/all_to_all | solution.py:40
  96.2 0.8 attend.3
  97.0 9.1 %all_to_all.28.lines_ref = bf16[16,4,128]{2,1,0:T(4,128)(2,1)S(1)} all-to-all(bf16[16,4,128]{2,1,0:T(4,128)(2,1)S(1)} %attend.3), channel_id=1, replica_groups=mesh['groups'=2,'replica'=16] {'replica'}, dimensions={0} | all-to-all | bytes 32768 | tf_op jit(solution)/shard_map/all_to_all | solution.py:40
  106.1 1.3 %output.3 = (f32[8,8192]{1,0:T(8,128)S(1)}, bf16[8,8192]{1,0:T(8,128)(2,1)S(1)}) custom-call(bf16[16,4,128]{2,1,0:T(4,128)(2,1)S(1)} %all_to_all.28.lines_ref, s32[1]{0:T(128)} %bitcast._.refs_4_.me_ref, bf16[512,8192]{1,0:T(8,128)(2,1)S(1)} %get-tuple-element.56.weight_ref), custom_call_target="tpu_custom_call" | custom-call | flops 134217728 | bytes 8388608 | tf_op jit(solution)/shard_map/output/pallas_call | solution.py:53
  107.4 1.4 %collective-permute-done.27.other_ref = bf16[8,8192]{1,0:T(8,128)(2,1)S(1)} collective-permute-done((bf16[8,8192]{1,0:T(8,128)(2,1)S(1)}, bf16[8,8192]{1,0:T(8,128)(2,1)S(1)}, u32[]{:S(2)}, u32[]{:S(2)}) %collective-permute-start.27) | collective-permute-done | bytes 131104 | tf_op jit(solution)/shard_map/ppermute | solution.py:32
  108.9 10.0 %all_to_all.29.parts_ref = bf16[8,8,1024]{2,1,0:T(8,128)(2,1)S(1)} all-to-all(bf16[8,8,1024]{2,1,0:T(8,128)(2,1)S(1)} %partial.1), channel_id=1, replica_groups={{0,2,4,6,8,10,12,14},{1,3,5,7,9,11,13,15},{16,18,20,22,24,26,28,30},{17..., dimensions={0} | all-to-all | bytes 262144 | tf_op jit(solution)/shard_map/all_to_all | solution.py:45
  (56 shorter events, 14.2 us)
Async XLA Ops:
  1.3 0.8 copy-start.1
  2.1 9.8 %collective-permute-start.2 = (bf16[1,8320]{1,0:T(2,128)(2,1)S(1)}, bf16[1,8320]{1,0:T(2,128)(2,1)S(1)}, u32[]{:S(2)}, u32[]{:S(2)}) collective-permute-start(bf16[1,8320]{1,0:T(2,128)(2,1)S(1)} %get-tuple-element.39.refs_0_), channel_id=1, source_target_pairs={{0,12},{1,13},{2,14},{3,15},{4,8},{5,9},{6,10},{7,11},{8,4},{9,5},... | collective-permute-start | bytes 49928 | tf_op jit(solution)/shard_map/ppermute | solution.py:32
  7.2 4.8 %collective-permute-start.1 = (bf16[1,8320]{1,0:T(2,128)(2,1)S(1)}, bf16[1,8320]{1,0:T(2,128)(2,1)S(1)}, u32[]{:S(2)}, u32[]{:S(2)}) collective-permute-start(bf16[1,8320]{1,0:T(2,128)(2,1)S(1)} %get-tuple-element.39.refs_0_), channel_id=1, source_target_pairs={{0,8},{1,9},{2,10},{3,11},{4,12},{5,13},{6,14},{7,15},{8,0},{9,1},... | collective-permute-start | bytes 49928 | tf_op jit(solution)/shard_map/ppermute | solution.py:32
  7.2 4.8 %collective-permute-start = (bf16[1,8320]{1,0:T(2,128)(2,1)S(1)}, bf16[1,8320]{1,0:T(2,128)(2,1)S(1)}, u32[]{:S(2)}, u32[]{:S(2)}) collective-permute-start(bf16[1,8320]{1,0:T(2,128)(2,1)S(1)} %get-tuple-element.39.refs_0_), channel_id=1, source_target_pairs={{0,4},{1,5},{2,6},{3,7},{4,0},{5,1},{6,2},{7,3},{8,12},{9,13},{10,... | collective-permute-start | bytes 49928 | tf_op jit(solution)/shard_map/ppermute | solution.py:32
  7.8 4.2 %copy-start = (bf16[8192]{0:T(1024)(128)(2,1)S(1)}, bf16[8192]{0:T(1024)(128)(2,1)}, u32[]{:S(2)}) copy-start(bf16[8192]{0:T(1024)(128)(2,1)} %param.12) | copy-start | bytes 49156
  12.3 5.9 %copy-start.2 = (s32[32]{0:T(128)S(1)}, s32[32]{0:T(128)}, u32[]{:S(2)}) copy-start(s32[32]{0:T(128)} %param.19) | copy-start | bytes 388
  12.3 5.3 %collective-permute-start.5 = (bf16[4,8320]{1,0:T(4,128)(2,1)S(1)}, bf16[4,8320]{1,0:T(4,128)(2,1)S(1)}, u32[]{:S(2)}, u32[]{:S(2)}) collective-permute-start(bf16[4,8320]{1,0:T(4,128)(2,1)S(1)} %get-tuple-element.42.refs_0_), channel_id=1, source_target_pairs={{0,3},{1,2},{2,1},{3,0},{4,7},{5,6},{6,5},{7,4},{8,11},{9,10},{10,... | collective-permute-start | bytes 199688 | tf_op jit(solution)/shard_map/ppermute | solution.py:32
  12.6 5.6 %collective-permute-start.4 = (bf16[4,8320]{1,0:T(4,128)(2,1)S(1)}, bf16[4,8320]{1,0:T(4,128)(2,1)S(1)}, u32[]{:S(2)}, u32[]{:S(2)}) collective-permute-start(bf16[4,8320]{1,0:T(4,128)(2,1)S(1)} %get-tuple-element.42.refs_0_), channel_id=1, source_target_pairs={{0,2},{1,3},{2,0},{3,1},{4,6},{5,7},{6,4},{7,5},{8,10},{9,11},{10,... | collective-permute-start | bytes 199688 | tf_op jit(solution)/shard_map/ppermute | solution.py:32
  14.0 4.3 %collective-permute-start.3 = (bf16[4,8320]{1,0:T(4,128)(2,1)S(1)}, bf16[4,8320]{1,0:T(4,128)(2,1)S(1)}, u32[]{:S(2)}, u32[]{:S(2)}) collective-permute-start(bf16[4,8320]{1,0:T(4,128)(2,1)S(1)} %get-tuple-element.42.refs_0_), channel_id=1, source_target_pairs={{0,1},{1,0},{2,3},{3,2},{4,5},{5,4},{6,7},{7,6},{8,9},{9,8},{10,11... | collective-permute-start | bytes 199688 | tf_op jit(solution)/shard_map/ppermute | solution.py:32
  19.0 4.8 %collective-permute-start.8 = (bf16[16,64]{1,0:T(8,128)(2,1)S(1)}, bf16[16,64]{1,0:T(8,128)(2,1)S(1)}, u32[]{:S(2)}, u32[]{:S(2)}) collective-permute-start(bf16[16,64]{1,0:T(8,128)(2,1)S(1)} %get-tuple-element.45.refs_3_.refs_0_), channel_id=1, source_target_pairs={{0,3},{1,2},{2,1},{3,0},{4,7},{5,6},{6,5},{7,4},{8,11},{9,10},{10,... | collective-permute-start | bytes 6152 | tf_op jit(solution)/shard_map/ppermute | solution.py:32
  19.6 4.2 %collective-permute-start.7 = (bf16[16,64]{1,0:T(8,128)(2,1)S(1)}, bf16[16,64]{1,0:T(8,128)(2,1)S(1)}, u32[]{:S(2)}, u32[]{:S(2)}) collective-permute-start(bf16[16,64]{1,0:T(8,128)(2,1)S(1)} %get-tuple-element.45.refs_3_.refs_0_), channel_id=1, source_target_pairs={{0,2},{1,3},{2,0},{3,1},{4,6},{5,7},{6,4},{7,5},{8,10},{9,11},{10,... | collective-permute-start | bytes 6152 | tf_op jit(solution)/shard_map/ppermute | solution.py:32
  20.7 3.1 %collective-permute-start.6 = (bf16[16,64]{1,0:T(8,128)(2,1)S(1)}, bf16[16,64]{1,0:T(8,128)(2,1)S(1)}, u32[]{:S(2)}, u32[]{:S(2)}) collective-permute-start(bf16[16,64]{1,0:T(8,128)(2,1)S(1)} %get-tuple-element.45.refs_3_.refs_0_), channel_id=1, source_target_pairs={{0,1},{1,0},{2,3},{3,2},{4,5},{5,4},{6,7},{7,6},{8,9},{9,8},{10,11... | collective-permute-start | bytes 6152 | tf_op jit(solution)/shard_map/ppermute | solution.py:32
  23.8 5.9 %collective-permute-start.11 = (bf16[16,64]{1,0:T(8,128)(2,1)S(1)}, bf16[16,64]{1,0:T(8,128)(2,1)S(1)}, u32[]{:S(2)}, u32[]{:S(2)}) collective-permute-start(bf16[16,64]{1,0:T(8,128)(2,1)S(1)} %sum.2.refs_0_), channel_id=1, source_target_pairs={{0,12},{1,13},{2,14},{3,15},{4,8},{5,9},{6,10},{7,11},{8,4},{9,5},... | collective-permute-start | bytes 6152 | tf_op jit(solution)/shard_map/ppermute | solution.py:32
  27.5 4.5 %collective-permute-start.10 = (bf16[16,64]{1,0:T(8,128)(2,1)S(1)}, bf16[16,64]{1,0:T(8,128)(2,1)S(1)}, u32[]{:S(2)}, u32[]{:S(2)}) collective-permute-start(bf16[16,64]{1,0:T(8,128)(2,1)S(1)} %sum.2.refs_0_), channel_id=1, source_target_pairs={{0,8},{1,9},{2,10},{3,11},{4,12},{5,13},{6,14},{7,15},{8,0},{9,1},... | collective-permute-start | bytes 6152 | tf_op jit(solution)/shard_map/ppermute | solution.py:32
  27.5 4.5 %collective-permute-start.9 = (bf16[16,64]{1,0:T(8,128)(2,1)S(1)}, bf16[16,64]{1,0:T(8,128)(2,1)S(1)}, u32[]{:S(2)}, u32[]{:S(2)}) collective-permute-start(bf16[16,64]{1,0:T(8,128)(2,1)S(1)} %sum.2.refs_0_), channel_id=1, source_target_pairs={{0,4},{1,5},{2,6},{3,7},{4,0},{5,1},{6,2},{7,3},{8,12},{9,13},{10,... | collective-permute-start | bytes 6152 | tf_op jit(solution)/shard_map/ppermute | solution.py:32
  53.9 1.9 %collective-permute-start.12 = (bf16[4,8192]{1,0:T(4,128)(2,1)S(1)}, bf16[4,8192]{1,0:T(4,128)(2,1)S(1)}, u32[]{:S(2)}, u32[]{:S(2)}) collective-permute-start(bf16[4,8192]{1,0:T(4,128)(2,1)S(1)} %get-tuple-element.58), channel_id=1, source_target_pairs={{0,1},{1,0},{2,3},{3,2},{4,5},{5,4},{6,7},{7,6},{8,9},{9,8},{10,11... | collective-permute-start | bytes 196616 | tf_op jit(solution)/shard_map/ppermute | solution.py:32
  53.9 5.0 %collective-permute-start.13 = (bf16[4,8192]{1,0:T(4,128)(2,1)S(1)}, bf16[4,8192]{1,0:T(4,128)(2,1)S(1)}, u32[]{:S(2)}, u32[]{:S(2)}) collective-permute-start(bf16[4,8192]{1,0:T(4,128)(2,1)S(1)} %get-tuple-element.59), channel_id=1, source_target_pairs={{0,2},{1,3},{2,0},{3,1},{4,6},{5,7},{6,4},{7,5},{8,10},{9,11},{10,... | collective-permute-start | bytes 196616 | tf_op jit(solution)/shard_map/ppermute | solution.py:32
  54.5 4.9 %collective-permute-start.14 = (bf16[4,8192]{1,0:T(4,128)(2,1)S(1)}, bf16[4,8192]{1,0:T(4,128)(2,1)S(1)}, u32[]{:S(2)}, u32[]{:S(2)}) collective-permute-start(bf16[4,8192]{1,0:T(4,128)(2,1)S(1)} %get-tuple-element.60), channel_id=1, source_target_pairs={{0,3},{1,2},{2,1},{3,0},{4,7},{5,6},{6,5},{7,4},{8,11},{9,10},{10,... | collective-permute-start | bytes 196616 | tf_op jit(solution)/shard_map/ppermute | solution.py:32
  59.5 6.9 %collective-permute-start.17 = (bf16[4,8192]{1,0:T(4,128)(2,1)S(1)}, bf16[4,8192]{1,0:T(4,128)(2,1)S(1)}, u32[]{:S(2)}, u32[]{:S(2)}) collective-permute-start(bf16[4,8192]{1,0:T(4,128)(2,1)S(1)} %fold.1.refs_0_), channel_id=1, source_target_pairs={{0,12},{1,13},{2,14},{3,15},{4,8},{5,9},{6,10},{7,11},{8,4},{9,5},... | collective-permute-start | bytes 196616 | tf_op jit(solution)/shard_map/ppermute | solution.py:32
  60.0 7.9 %collective-permute-start.16 = (bf16[4,8192]{1,0:T(4,128)(2,1)S(1)}, bf16[4,8192]{1,0:T(4,128)(2,1)S(1)}, u32[]{:S(2)}, u32[]{:S(2)}) collective-permute-start(bf16[4,8192]{1,0:T(4,128)(2,1)S(1)} %fold.1.refs_0_), channel_id=1, source_target_pairs={{0,8},{1,9},{2,10},{3,11},{4,12},{5,13},{6,14},{7,15},{8,0},{9,1},... | collective-permute-start | bytes 196616 | tf_op jit(solution)/shard_map/ppermute | solution.py:32
  61.3 6.5 %collective-permute-start.15 = (bf16[4,8192]{1,0:T(4,128)(2,1)S(1)}, bf16[4,8192]{1,0:T(4,128)(2,1)S(1)}, u32[]{:S(2)}, u32[]{:S(2)}) collective-permute-start(bf16[4,8192]{1,0:T(4,128)(2,1)S(1)} %fold.1.refs_0_), channel_id=1, source_target_pairs={{0,4},{1,5},{2,6},{3,7},{4,0},{5,1},{6,2},{7,3},{8,12},{9,13},{10,... | collective-permute-start | bytes 196616 | tf_op jit(solution)/shard_map/ppermute | solution.py:32
  68.5 4.5 %collective-permute-start.20 = (bf16[4,8192]{1,0:T(4,128)(2,1)S(1)}, bf16[4,8192]{1,0:T(4,128)(2,1)S(1)}, u32[]{:S(2)}, u32[]{:S(2)}) collective-permute-start(bf16[4,8192]{1,0:T(4,128)(2,1)S(1)} %get-tuple-element.62.refs_0_), channel_id=1, source_target_pairs={{0,3},{1,2},{2,1},{3,0},{4,7},{5,6},{6,5},{7,4},{8,11},{9,10},{10,... | collective-permute-start | bytes 196616 | tf_op jit(solution)/shard_map/ppermute | solution.py:32
  68.6 5.1 %collective-permute-start.19 = (bf16[4,8192]{1,0:T(4,128)(2,1)S(1)}, bf16[4,8192]{1,0:T(4,128)(2,1)S(1)}, u32[]{:S(2)}, u32[]{:S(2)}) collective-permute-start(bf16[4,8192]{1,0:T(4,128)(2,1)S(1)} %get-tuple-element.62.refs_0_), channel_id=1, source_target_pairs={{0,2},{1,3},{2,0},{3,1},{4,6},{5,7},{6,4},{7,5},{8,10},{9,11},{10,... | collective-permute-start | bytes 196616 | tf_op jit(solution)/shard_map/ppermute | solution.py:32
  69.7 4.0 %collective-permute-start.18 = (bf16[4,8192]{1,0:T(4,128)(2,1)S(1)}, bf16[4,8192]{1,0:T(4,128)(2,1)S(1)}, u32[]{:S(2)}, u32[]{:S(2)}) collective-permute-start(bf16[4,8192]{1,0:T(4,128)(2,1)S(1)} %get-tuple-element.62.refs_0_), channel_id=1, source_target_pairs={{0,1},{1,0},{2,3},{3,2},{4,5},{5,4},{6,7},{7,6},{8,9},{9,8},{10,11... | collective-permute-start | bytes 196616 | tf_op jit(solution)/shard_map/ppermute | solution.py:32
  74.5 3.1 %collective-permute-start.23 = (bf16[16,64]{1,0:T(8,128)(2,1)S(1)}, bf16[16,64]{1,0:T(8,128)(2,1)S(1)}, u32[]{:S(2)}, u32[]{:S(2)}) collective-permute-start(bf16[16,64]{1,0:T(8,128)(2,1)S(1)} %get-tuple-element.64.refs_0_), channel_id=1, source_target_pairs={{0,3},{1,2},{2,1},{3,0},{4,7},{5,6},{6,5},{7,4},{8,11},{9,10},{10,... | collective-permute-start | bytes 6152 | tf_op jit(solution)/shard_map/ppermute | solution.py:32
  75.3 3.6 %collective-permute-start.22 = (bf16[16,64]{1,0:T(8,128)(2,1)S(1)}, bf16[16,64]{1,0:T(8,128)(2,1)S(1)}, u32[]{:S(2)}, u32[]{:S(2)}) collective-permute-start(bf16[16,64]{1,0:T(8,128)(2,1)S(1)} %get-tuple-element.64.refs_0_), channel_id=1, source_target_pairs={{0,2},{1,3},{2,0},{3,1},{4,6},{5,7},{6,4},{7,5},{8,10},{9,11},{10,... | collective-permute-start | bytes 6152 | tf_op jit(solution)/shard_map/ppermute | solution.py:32
  76.3 2.6 %collective-permute-start.21 = (bf16[16,64]{1,0:T(8,128)(2,1)S(1)}, bf16[16,64]{1,0:T(8,128)(2,1)S(1)}, u32[]{:S(2)}, u32[]{:S(2)}) collective-permute-start(bf16[16,64]{1,0:T(8,128)(2,1)S(1)} %get-tuple-element.64.refs_0_), channel_id=1, source_target_pairs={{0,1},{1,0},{2,3},{3,2},{4,5},{5,4},{6,7},{7,6},{8,9},{9,8},{10,11... | collective-permute-start | bytes 6152 | tf_op jit(solution)/shard_map/ppermute | solution.py:32
  78.9 5.9 %collective-permute-start.26 = (bf16[16,64]{1,0:T(8,128)(2,1)S(1)}, bf16[16,64]{1,0:T(8,128)(2,1)S(1)}, u32[]{:S(2)}, u32[]{:S(2)}) collective-permute-start(bf16[16,64]{1,0:T(8,128)(2,1)S(1)} %sum.3.refs_0_), channel_id=1, source_target_pairs={{0,12},{1,13},{2,14},{3,15},{4,8},{5,9},{6,10},{7,11},{8,4},{9,5},... | collective-permute-start | bytes 6152 | tf_op jit(solution)/shard_map/ppermute | solution.py:32
  80.6 4.5 %collective-permute-start.25 = (bf16[16,64]{1,0:T(8,128)(2,1)S(1)}, bf16[16,64]{1,0:T(8,128)(2,1)S(1)}, u32[]{:S(2)}, u32[]{:S(2)}) collective-permute-start(bf16[16,64]{1,0:T(8,128)(2,1)S(1)} %sum.3.refs_0_), channel_id=1, source_target_pairs={{0,8},{1,9},{2,10},{3,11},{4,12},{5,13},{6,14},{7,15},{8,0},{9,1},... | collective-permute-start | bytes 6152 | tf_op jit(solution)/shard_map/ppermute | solution.py:32
  81.0 4.2 %collective-permute-start.24 = (bf16[16,64]{1,0:T(8,128)(2,1)S(1)}, bf16[16,64]{1,0:T(8,128)(2,1)S(1)}, u32[]{:S(2)}, u32[]{:S(2)}) collective-permute-start(bf16[16,64]{1,0:T(8,128)(2,1)S(1)} %sum.3.refs_0_), channel_id=1, source_target_pairs={{0,4},{1,5},{2,6},{3,7},{4,0},{5,1},{6,2},{7,3},{8,12},{9,13},{10,... | collective-permute-start | bytes 6152 | tf_op jit(solution)/shard_map/ppermute | solution.py:32
  107.4 1.4 %collective-permute-start.27 = (bf16[8,8192]{1,0:T(8,128)(2,1)S(1)}, bf16[8,8192]{1,0:T(8,128)(2,1)S(1)}, u32[]{:S(2)}, u32[]{:S(2)}) collective-permute-start(bf16[8,8192]{1,0:T(8,128)(2,1)S(1)} %get-tuple-element.71), channel_id=1, source_target_pairs={{0,1},{1,0},{2,3},{3,2},{4,5},{5,4},{6,7},{7,6},{8,9},{9,8},{10,11... | collective-permute-start | bytes 393224 | tf_op jit(solution)/shard_map/ppermute | solution.py:32

commit v15 on v14

--- a/solution.py
+++ b/solution.py
@@ -168,11 +168,25 @@
     out_ref[:, width:] = rows[:, width:].astype(jnp.bfloat16)
 
 
-def fold_kernel(*refs):
-    total = refs[0][...]
-    for ref in refs[1:-1]:
-        total = total + ref[...].astype(jnp.float32)
-    refs[-1][...] = total.astype(jnp.bfloat16)
+def distance(slot, near, far):
+    size, total = near * far, (slot % far) * near
+    bit = 1
+    while bit < near:
+        size //= 2
+        total = total + ((slot // size) % 2) * bit
+        bit *= 2
+    return total
+
+
+def fold_kernel(own_ref, other_ref, keep_ref, away_ref):
+    total = own_ref[...] + other_ref[...].astype(jnp.float32)
+    half = keep_ref.shape[0]
+    keep_ref[...] = total[:half]
+    away_ref[...] = total[half:].astype(jnp.bfloat16)
+
+
+def folded_kernel(own_ref, other_ref, out_ref):
+    out_ref[...] = (own_ref[...] + other_ref[...].astype(jnp.float32)).astype(jnp.bfloat16)
 
 
 def next_kernel(far, *refs):
@@ -333,16 +347,14 @@
             out_ref[k] = out[k : k + 1].astype(jnp.bfloat16)
 
 
-def output_kernel(split, lines_ref, me_ref, weight_ref, own_ref, *refs):
-    aways, held = refs[:-1], refs[-1]
+def output_kernel(split, lines_ref, me_ref, weight_ref, own_ref, away_ref, held):
     count, each, line = lines_ref.shape
     chips = count // CORES
     for k in range(count):
         held[k, :each, :] = lines_ref[k].astype(jnp.float32)
     slot = iota((count, count), 0)
     if split:
-        near, far = split
-        origin = me_ref[0] ^ ((slot % far) * near + slot // far)
+        origin = me_ref[0] ^ distance(slot, *split)
     else:
         origin = (slot % chips) * CORES + ((me_ref[0] % CORES) ^ (slot // chips))
     order = (iota((count, count), 1) == origin).astype(jnp.bfloat16)
@@ -355,10 +367,8 @@
     for c in range(8):
         part = slice(c * wide, (c + 1) * wide)
         out = dot(rows, weight_ref[:, part])
-        some = own_ref.shape[0]
-        own_ref[:, part] = out[:some]
-        for l, ref in enumerate(aways):
-            ref[:, part] = out[(l + 1) * some : (l + 2) * some].astype(jnp.bfloat16)
+        own_ref[:, part] = out[:chips]
+        away_ref[:, part] = out[chips:].astype(jnp.bfloat16)
 
 
 def partial_kernel(own_ref, other_ref, out_ref):
@@ -515,10 +525,9 @@
             past = tuple(outs[1:])
 
         lines = swap(outs[0])
-        some = chips if last else far
-        own, *aways = call(
+        own, away = call(
             functools.partial(output_kernel, None if last else (near, far)),
-            [shape((some, width), jnp.float32)] + [shape((some, width))] * (count // some - 1),
+            [shape((chips, width), jnp.float32), shape((chips, width))],
             "output",
             [pltpu.VMEM((count, 8, line), jnp.float32)],
             flops=2 * count * width * columns,
@@ -527,13 +536,19 @@
 
         if last:
             (parts,) = call(partial_kernel, [shape((chips, FOLD, width // FOLD))], "partial")(
-                own, shift(aways[0], 1, count)
+                own, shift(away, 1, count)
             )
             parts = chips_swap(parts, count)
             (out,) = call(finish_kernel, [shape((STEPS, width))], "finish")(parts, hidden)
             return out.reshape(STEPS, 1, width)
-        aways = [shift(a, d, count) for a, d in zip(aways, near_steps)]
-        (own,) = call(fold_kernel, [shape((far, width))], "fold")(own, *aways)
+        bit = 1
+        while bit < near // 2:
+            half = own.shape[0] // 2
+            own, away = call(
+                fold_kernel, [shape((half, width), jnp.float32), shape((half, width))], "fold"
+            )(own, shift(away, bit, count))
+            bit *= 2
+        (own,) = call(folded_kernel, [shape((far, width))], "fold")(own, shift(away, bit, count))
         hidden, carried = call(
             functools.partial(next_kernel, far), [shape((1, width)), shape((far, width))], "next"
         )(*across(own, far_steps, count), column, scale)

time: 120 us -> 119 us (level)
  starting transfers between devices: 28.6 us -> 27.3 us
    ppermute x28 -> x27, starting transfers between devices: 28.6 us -> 27.3 us  [shift(): return lax.ppermute(block, AXIS, [(i, i ^ distance) for i in range(count)])]
    ppermute x28 -> x27, waiting for transfers between devices: 18 us -> 18.9 us  [shift(): return lax.ppermute(block, AXIS, [(i, i ^ distance) for i in range(count)])]
    pallas_call x21 -> x22, Pallas kernels: 21.8 us -> 21.8 us  [run(): pl.pallas_call(body, out_shape=outs, in_specs=[pl.BlockSpec(memory_space=...]
  transfers between devices with their start and end apart: 28 -> 27, of which waited for: 13 -> 13; matrix products, arithmetic and copies ran while one was open for 0% -> 0% of each run, Pallas kernels for 11% -> 11%
where the time goes in v15:
time: 119 us
  blocking collectives  48.6 us (41%)
  starting transfers between devices  27.3 us (23%)
  Pallas kernels  21.8 us (18%)
  waiting for transfers between devices  18.9 us (16%)
  between operations  1.47 us (1%)
    all_to_all x4, blocking collectives, swap(): return lax.all_to_all(blocks, AXIS, split_axis=0, concat_axis=0, tiled=True)  38.6 us
    ppermute x27, starting transfers between devices, shift(): return lax.ppermute(block, AXIS, [(i, i ^ distance) for i in range(count)])  27.3 us
    pallas_call x22, Pallas kernels, run(): pl.pallas_call(body, out_shape=outs, in_specs=[pl.BlockSpec(memory_space=...  21.8 us
    ppermute x27, waiting for transfers between devices, shift(): return lax.ppermute(block, AXIS, [(i, i ^ distance) for i in range(count)])  18.9 us
    all_to_all x1, blocking collectives, chips_swap(): lax.all_to_all(blocks, AXIS, split_axis=0, concat_axis=0, axis_index_grou...  9.97 us
  transfers between devices with their start and end apart: 27, of which 13 were waited for; matrix products, arithmetic and copies ran while one was open for 0% of the time, Pallas kernels for 11%

profile of v15, /device:TPU:0, one launch (start us, length us, event | category | flops | bytes accessed | tf_op | source)
XLA Modules:
  0.0 118.8 jit_solution(8431928152061099121)
XLA Ops:
  2.1 5.1 %collective-permute-start.2 = (bf16[1,8320]{1,0:T(2,128)(2,1)S(1)}, bf16[1,8320]{1,0:T(2,128)(2,1)S(1)}, u32[]{:S(2)}, u32[]{:S(2)}) collective-permute-start(bf16[1,8320]{1,0:T(2,128)(2,1)S(1)} %get-tuple-element.39.refs_0_), channel_id=1, source_target_pairs={{0,12},{1,13},{2,14},{3,15},{4,8},{5,9},{6,10},{7,11},{8,4},{9,5},... | collective-permute-start | bytes 49928 | tf_op jit(solution)/shard_map/ppermute | solution.py:32
  7.8 4.0 %stash.3 = (bf16[8192,512]{1,0:T(8,128)(2,1)S(1)}, bf16[2,64,8192]{2,1,0:T(8,128)(2,1)S(1)}, s32[8,128]{1,0:T(8,128)S(1)}) custom-call(s32[8,128]{1,0:T(8,128)S(1)} %get-tuple-element.40.token_ref.refs_1_, bf16[8192,512]{1,0:T(8,128)(2,1)} %refs_0_.3, bf16[2,64,8192]{2,1,0:T(8,128)(2,1)} %bitcast.8), custom_call_target="tpu_custom_call" | custom-call | flops 1048576 | bytes 10485760 | tf_op jit(solution)/shard_map/stash/pallas_call | solution.py:53
  12.6 1.3 %collective-permute-start.4 = (bf16[4,8320]{1,0:T(4,128)(2,1)S(1)}, bf16[4,8320]{1,0:T(4,128)(2,1)S(1)}, u32[]{:S(2)}, u32[]{:S(2)}) collective-permute-start(bf16[4,8320]{1,0:T(4,128)(2,1)S(1)} %get-tuple-element.42.refs_0_), channel_id=1, source_target_pairs={{0,2},{1,3},{2,0},{3,1},{4,6},{5,7},{6,4},{7,5},{8,10},{9,11},{10,... | collective-permute-start | bytes 199688 | tf_op jit(solution)/shard_map/ppermute | solution.py:32
  14.3 3.4 %stash.4 = (bf16[512,8192]{1,0:T(8,128)(2,1)S(1)}, s32[8,128]{1,0:T(8,128)S(1)}) custom-call(s32[8,128]{1,0:T(8,128)S(1)} %get-tuple-element.41.refs_5_.token_ref, bf16[512,8192]{1,0:T(8,128)(2,1)} %refs_0_.4), custom_call_target="tpu_custom_call" | custom-call | flops 1048576 | bytes 8388608 | tf_op jit(solution)/shard_map/stash/pallas_call | solution.py:53
  19.6 1.1 collective-permute-start.7
  20.9 2.9 %stash.5 = (bf16[8192,128]{1,0:T(8,128)(2,1)S(1)}, bf16[32,64,512]{2,1,0:T(8,128)(2,1)S(1)}, bf16[1,2,512,1024]{3,2,1,0:T(8,128)(2,1)S(1)}, s32[8,128]{1,0:T(8,128)S(1)}) custom-call(s32[8,128]{1,0:T(8,128)S(1)} %get-tuple-element.44.refs_7_.token_ref, bf16[8192,128]{1,0:T(8,128)(2,1)} %refs_0_.5, bf16[32,64,512]{2,1,0:T(8,128)(2,1)} %refs_1_.1, ...), custom_call_target="tpu_custom_call" | custom-call | flops 1048576 | bytes 6291456 | tf_op jit(solution)/shard_map/stash/pallas_call | solution.py:53
  23.8 3.7 %collective-permute-start.11 = (bf16[16,64]{1,0:T(8,128)(2,1)S(1)}, bf16[16,64]{1,0:T(8,128)(2,1)S(1)}, u32[]{:S(2)}, u32[]{:S(2)}) collective-permute-start(bf16[16,64]{1,0:T(8,128)(2,1)S(1)} %sum.2.refs_0_), channel_id=1, source_target_pairs={{0,12},{1,13},{2,14},{3,15},{4,8},{5,9},{6,10},{7,11},{8,4},{9,5},... | collective-permute-start | bytes 6152 | tf_op jit(solution)/shard_map/ppermute | solution.py:32
  28.3 1.5 %project.2 = (f32[16,512]{1,0:T(8,128)S(1)}, f32[16,128]{1,0:T(8,128)S(1)}) custom-call(bf16[16,8192]{1,0:T(8,128)(2,1)S(1)} %get-tuple-element.47.rows_ref, bf16[8192,512]{1,0:T(8,128)(2,1)S(1)} %get-tuple-element.48.query_w, bf16[8192,128]{1,0:T(8,128)(2,1)S(1)} %get-tuple-element.49.fresh_w), custom_call_target="tpu_custom_call" | custom-call | flops 167772160 | bytes 10485760 | tf_op jit(solution)/shard_map/project/pallas_call | solution.py:53
  29.8 2.3 %collective-permute-done.10.refs_2_ = bf16[16,64]{1,0:T(8,128)(2,1)S(1)} collective-permute-done((bf16[16,64]{1,0:T(8,128)(2,1)S(1)}, bf16[16,64]{1,0:T(8,128)(2,1)S(1)}, u32[]{:S(2)}, u32[]{:S(2)}) %collective-permute-start.10) | collective-permute-done | bytes 2080 | tf_op jit(solution)/shard_map/ppermute | solution.py:32
  32.5 10.2 %all_to_all.25.refs_0_ = bf16[16,8,128]{2,1,0:T(8,128)(2,1)S(1)} all-to-all(bf16[16,8,128]{2,1,0:T(8,128)(2,1)S(1)} %up.2), channel_id=1, replica_groups=mesh['groups'=2,'replica'=16] {'replica'}, dimensions={0} | all-to-all | bytes 65536 | tf_op jit(solution)/shard_map/all_to_all | solution.py:40
  43.5 9.1 %all_to_all.26.lines_ref = bf16[16,4,128]{2,1,0:T(4,128)(2,1)S(1)} all-to-all(bf16[16,4,128]{2,1,0:T(4,128)(2,1)S(1)} %get-tuple-element.55), channel_id=1, replica_groups=mesh['groups'=2,'replica'=16] {'replica'}, dimensions={0} | all-to-all | bytes 32768 | tf_op jit(solution)/shard_map/all_to_all | solution.py:40
  52.6 1.3 %output.2 = (f32[8,8192]{1,0:T(8,128)S(1)}, bf16[8,8192]{1,0:T(8,128)(2,1)S(1)}) custom-call(bf16[16,4,128]{2,1,0:T(4,128)(2,1)S(1)} %all_to_all.26.lines_ref, s32[1]{0:T(128)} %bitcast._.refs_4_.me_ref, bf16[512,8192]{1,0:T(8,128)(2,1)S(1)} %get-tuple-element.56.weight_ref), custom_call_target="tpu_custom_call" | custom-call | flops 134217728 | bytes 8388608 | tf_op jit(solution)/shard_map/output/pallas_call | solution.py:53
  53.9 1.4 %collective-permute-done.12.other_ref = bf16[8,8192]{1,0:T(8,128)(2,1)S(1)} collective-permute-done((bf16[8,8192]{1,0:T(8,128)(2,1)S(1)}, bf16[8,8192]{1,0:T(8,128)(2,1)S(1)}, u32[]{:S(2)}, u32[]{:S(2)}) %collective-permute-start.12) | collective-permute-done | bytes 131104 | tf_op jit(solution)/shard_map/ppermute | solution.py:32
  55.8 3.8 %collective-permute-done.13.other_ref = bf16[4,8192]{1,0:T(4,128)(2,1)S(1)} collective-permute-done((bf16[4,8192]{1,0:T(4,128)(2,1)S(1)}, bf16[4,8192]{1,0:T(4,128)(2,1)S(1)}, u32[]{:S(2)}, u32[]{:S(2)}) %collective-permute-start.13) | collective-permute-done | bytes 65568 | tf_op jit(solution)/shard_map/ppermute | solution.py:32
  60.2 1.4 %collective-permute-start.15 = (bf16[4,8192]{1,0:T(4,128)(2,1)S(1)}, bf16[4,8192]{1,0:T(4,128)(2,1)S(1)}, u32[]{:S(2)}, u32[]{:S(2)}) collective-permute-start(bf16[4,8192]{1,0:T(4,128)(2,1)S(1)} %fold.3.refs_0_), channel_id=1, source_target_pairs={{0,8},{1,9},{2,10},{3,11},{4,12},{5,13},{6,14},{7,15},{8,0},{9,1},... | collective-permute-start | bytes 196616 | tf_op jit(solution)/shard_map/ppermute | solution.py:32
  61.7 2.5 %collective-permute-start.14 = (bf16[4,8192]{1,0:T(4,128)(2,1)S(1)}, bf16[4,8192]{1,0:T(4,128)(2,1)S(1)}, u32[]{:S(2)}, u32[]{:S(2)}) collective-permute-start(bf16[4,8192]{1,0:T(4,128)(2,1)S(1)} %fold.3.refs_0_), channel_id=1, source_target_pairs={{0,4},{1,5},{2,6},{3,7},{4,0},{5,1},{6,2},{7,3},{8,12},{9,13},{10,... | collective-permute-start | bytes 196616 | tf_op jit(solution)/shard_map/ppermute | solution.py:32
  64.1 2.0 %collective-permute-done.16.refs_3_ = bf16[4,8192]{1,0:T(4,128)(2,1)S(1)} collective-permute-done((bf16[4,8192]{1,0:T(4,128)(2,1)S(1)}, bf16[4,8192]{1,0:T(4,128)(2,1)S(1)}, u32[]{:S(2)}, u32[]{:S(2)}) %collective-permute-start.16) | collective-permute-done | bytes 65568 | tf_op jit(solution)/shard_map/ppermute | solution.py:32
  66.1 1.3 %collective-permute-done.15.refs_2_ = bf16[4,8192]{1,0:T(4,128)(2,1)S(1)} collective-permute-done((bf16[4,8192]{1,0:T(4,128)(2,1)S(1)}, bf16[4,8192]{1,0:T(4,128)(2,1)S(1)}, u32[]{:S(2)}, u32[]{:S(2)}) %collective-permute-start.15) | collective-permute-done | bytes 65568 | tf_op jit(solution)/shard_map/ppermute | solution.py:32
  68.7 1.2 %collective-permute-start.17 = (bf16[4,8192]{1,0:T(4,128)(2,1)S(1)}, bf16[4,8192]{1,0:T(4,128)(2,1)S(1)}, u32[]{:S(2)}, u32[]{:S(2)}) collective-permute-start(bf16[4,8192]{1,0:T(4,128)(2,1)S(1)} %get-tuple-element.62.refs_0_), channel_id=1, source_target_pairs={{0,1},{1,0},{2,3},{3,2},{4,5},{5,4},{6,7},{7,6},{8,9},{9,8},{10,11... | collective-permute-start | bytes 196616 | tf_op jit(solution)/shard_map/ppermute | solution.py:32
  69.9 1.9 %collective-permute-done.19.refs_3_ = bf16[4,8192]{1,0:T(4,128)(2,1)S(1)} collective-permute-done((bf16[4,8192]{1,0:T(4,128)(2,1)S(1)}, bf16[4,8192]{1,0:T(4,128)(2,1)S(1)}, u32[]{:S(2)}, u32[]{:S(2)}) %collective-permute-start.19) | collective-permute-done | bytes 65568 | tf_op jit(solution)/shard_map/ppermute | solution.py:32
  71.9 1.2 %collective-permute-done.18.refs_2_ = bf16[4,8192]{1,0:T(4,128)(2,1)S(1)} collective-permute-done((bf16[4,8192]{1,0:T(4,128)(2,1)S(1)}, bf16[4,8192]{1,0:T(4,128)(2,1)S(1)}, u32[]{:S(2)}, u32[]{:S(2)}) %collective-permute-start.18) | collective-permute-done | bytes 65568 | tf_op jit(solution)/shard_map/ppermute | solution.py:32
  73.8 1.1 collective-permute-start.22
  75.8 1.1 collective-permute-done.22.refs_3_
  76.9 1.6 %collective-permute-done.21.refs_2_ = bf16[16,64]{1,0:T(8,128)(2,1)S(1)} collective-permute-done((bf16[16,64]{1,0:T(8,128)(2,1)S(1)}, bf16[16,64]{1,0:T(8,128)(2,1)S(1)}, u32[]{:S(2)}, u32[]{:S(2)}) %collective-permute-start.21) | collective-permute-done | bytes 2080 | tf_op jit(solution)/shard_map/ppermute | solution.py:32
  78.5 1.6 %collective-permute-start.25 = (bf16[16,64]{1,0:T(8,128)(2,1)S(1)}, bf16[16,64]{1,0:T(8,128)(2,1)S(1)}, u32[]{:S(2)}, u32[]{:S(2)}) collective-permute-start(bf16[16,64]{1,0:T(8,128)(2,1)S(1)} %sum.3.refs_0_), channel_id=1, source_target_pairs={{0,12},{1,13},{2,14},{3,15},{4,8},{5,9},{6,10},{7,11},{8,4},{9,5},... | collective-permute-start | bytes 6152 | tf_op jit(solution)/shard_map/ppermute | solution.py:32
  80.9 2.1 %collective-permute-start.23 = (bf16[16,64]{1,0:T(8,128)(2,1)S(1)}, bf16[16,64]{1,0:T(8,128)(2,1)S(1)}, u32[]{:S(2)}, u32[]{:S(2)}) collective-permute-start(bf16[16,64]{1,0:T(8,128)(2,1)S(1)} %sum.3.refs_0_), channel_id=1, source_target_pairs={{0,4},{1,5},{2,6},{3,7},{4,0},{5,1},{6,2},{7,3},{8,12},{9,13},{10,... | collective-permute-start | bytes 6152 | tf_op jit(solution)/shard_map/ppermute | solution.py:32
  83.0 1.5 %project.3 = (f32[16,512]{1,0:T(8,128)S(1)}, f32[16,128]{1,0:T(8,128)S(1)}) custom-call(bf16[16,8192]{1,0:T(8,128)(2,1)S(1)} %get-tuple-element.65.rows_ref, bf16[8192,512]{1,0:T(8,128)(2,1)S(1)} %get-tuple-element.48.query_w, bf16[8192,128]{1,0:T(8,128)(2,1)S(1)} %get-tuple-element.49.fresh_w), custom_call_target="tpu_custom_call" | custom-call | flops 167772160 | bytes 10485760 | tf_op jit(solution)/shard_map/project/pallas_call | solution.py:53
  85.1 10.2 %all_to_all.27.refs_0_ = bf16[16,8,128]{2,1,0:T(8,128)(2,1)S(1)} all-to-all(bf16[16,8,128]{2,1,0:T(8,128)(2,1)S(1)} %up.3), channel_id=1, replica_groups=mesh['groups'=2,'replica'=16] {'replica'}, dimensions={0} | all-to-all | bytes 65536 | tf_op jit(solution)/shard_map/all_to_all | solution.py:40
  96.2 9.1 %all_to_all.28.lines_ref = bf16[16,4,128]{2,1,0:T(4,128)(2,1)S(1)} all-to-all(bf16[16,4,128]{2,1,0:T(4,128)(2,1)S(1)} %attend.3), channel_id=1, replica_groups=mesh['groups'=2,'replica'=16] {'replica'}, dimensions={0} | all-to-all | bytes 32768 | tf_op jit(solution)/shard_map/all_to_all | solution.py:40
  105.2 1.3 %output.3 = (f32[8,8192]{1,0:T(8,128)S(1)}, bf16[8,8192]{1,0:T(8,128)(2,1)S(1)}) custom-call(bf16[16,4,128]{2,1,0:T(4,128)(2,1)S(1)} %all_to_all.28.lines_ref, s32[1]{0:T(128)} %bitcast._.refs_4_.me_ref, bf16[512,8192]{1,0:T(8,128)(2,1)S(1)} %get-tuple-element.56.weight_ref), custom_call_target="tpu_custom_call" | custom-call | flops 134217728 | bytes 8388608 | tf_op jit(solution)/shard_map/output/pallas_call | solution.py:53
  106.6 1.4 %collective-permute-done.26.other_ref = bf16[8,8192]{1,0:T(8,128)(2,1)S(1)} collective-permute-done((bf16[8,8192]{1,0:T(8,128)(2,1)S(1)}, bf16[8,8192]{1,0:T(8,128)(2,1)S(1)}, u32[]{:S(2)}, u32[]{:S(2)}) %collective-permute-start.26) | collective-permute-done | bytes 131104 | tf_op jit(solution)/shard_map/ppermute | solution.py:32
  108.1 10.0 %all_to_all.29.parts_ref = bf16[8,8,1024]{2,1,0:T(8,128)(2,1)S(1)} all-to-all(bf16[8,8,1024]{2,1,0:T(8,128)(2,1)S(1)} %partial.1), channel_id=1, replica_groups={{0,2,4,6,8,10,12,14},{1,3,5,7,9,11,13,15},{16,18,20,22,24,26,28,30},{17..., dimensions={0} | all-to-all | bytes 262144 | tf_op jit(solution)/shard_map/all_to_all | solution.py:45
  (55 shorter events, 13.9 us)
Async XLA Ops:
  1.3 0.8 copy-start.1
  2.1 9.8 %collective-permute-start.2 = (bf16[1,8320]{1,0:T(2,128)(2,1)S(1)}, bf16[1,8320]{1,0:T(2,128)(2,1)S(1)}, u32[]{:S(2)}, u32[]{:S(2)}) collective-permute-start(bf16[1,8320]{1,0:T(2,128)(2,1)S(1)} %get-tuple-element.39.refs_0_), channel_id=1, source_target_pairs={{0,12},{1,13},{2,14},{3,15},{4,8},{5,9},{6,10},{7,11},{8,4},{9,5},... | collective-permute-start | bytes 49928 | tf_op jit(solution)/shard_map/ppermute | solution.py:32
  7.2 4.8 %collective-permute-start.1 = (bf16[1,8320]{1,0:T(2,128)(2,1)S(1)}, bf16[1,8320]{1,0:T(2,128)(2,1)S(1)}, u32[]{:S(2)}, u32[]{:S(2)}) collective-permute-start(bf16[1,8320]{1,0:T(2,128)(2,1)S(1)} %get-tuple-element.39.refs_0_), channel_id=1, source_target_pairs={{0,8},{1,9},{2,10},{3,11},{4,12},{5,13},{6,14},{7,15},{8,0},{9,1},... | collective-permute-start | bytes 49928 | tf_op jit(solution)/shard_map/ppermute | solution.py:32
  7.2 4.8 %collective-permute-start = (bf16[1,8320]{1,0:T(2,128)(2,1)S(1)}, bf16[1,8320]{1,0:T(2,128)(2,1)S(1)}, u32[]{:S(2)}, u32[]{:S(2)}) collective-permute-start(bf16[1,8320]{1,0:T(2,128)(2,1)S(1)} %get-tuple-element.39.refs_0_), channel_id=1, source_target_pairs={{0,4},{1,5},{2,6},{3,7},{4,0},{5,1},{6,2},{7,3},{8,12},{9,13},{10,... | collective-permute-start | bytes 49928 | tf_op jit(solution)/shard_map/ppermute | solution.py:32
  7.8 4.2 %copy-start = (bf16[8192]{0:T(1024)(128)(2,1)S(1)}, bf16[8192]{0:T(1024)(128)(2,1)}, u32[]{:S(2)}) copy-start(bf16[8192]{0:T(1024)(128)(2,1)} %param.12) | copy-start | bytes 49156
  12.3 5.9 %copy-start.2 = (s32[32]{0:T(128)S(1)}, s32[32]{0:T(128)}, u32[]{:S(2)}) copy-start(s32[32]{0:T(128)} %param.19) | copy-start | bytes 388
  12.3 5.3 %collective-permute-start.5 = (bf16[4,8320]{1,0:T(4,128)(2,1)S(1)}, bf16[4,8320]{1,0:T(4,128)(2,1)S(1)}, u32[]{:S(2)}, u32[]{:S(2)}) collective-permute-start(bf16[4,8320]{1,0:T(4,128)(2,1)S(1)} %get-tuple-element.42.refs_0_), channel_id=1, source_target_pairs={{0,3},{1,2},{2,1},{3,0},{4,7},{5,6},{6,5},{7,4},{8,11},{9,10},{10,... | collective-permute-start | bytes 199688 | tf_op jit(solution)/shard_map/ppermute | solution.py:32
  12.6 5.6 %collective-permute-start.4 = (bf16[4,8320]{1,0:T(4,128)(2,1)S(1)}, bf16[4,8320]{1,0:T(4,128)(2,1)S(1)}, u32[]{:S(2)}, u32[]{:S(2)}) collective-permute-start(bf16[4,8320]{1,0:T(4,128)(2,1)S(1)} %get-tuple-element.42.refs_0_), channel_id=1, source_target_pairs={{0,2},{1,3},{2,0},{3,1},{4,6},{5,7},{6,4},{7,5},{8,10},{9,11},{10,... | collective-permute-start | bytes 199688 | tf_op jit(solution)/shard_map/ppermute | solution.py:32
  14.0 4.3 %collective-permute-start.3 = (bf16[4,8320]{1,0:T(4,128)(2,1)S(1)}, bf16[4,8320]{1,0:T(4,128)(2,1)S(1)}, u32[]{:S(2)}, u32[]{:S(2)}) collective-permute-start(bf16[4,8320]{1,0:T(4,128)(2,1)S(1)} %get-tuple-element.42.refs_0_), channel_id=1, source_target_pairs={{0,1},{1,0},{2,3},{3,2},{4,5},{5,4},{6,7},{7,6},{8,9},{9,8},{10,11... | collective-permute-start | bytes 199688 | tf_op jit(solution)/shard_map/ppermute | solution.py:32
  19.0 4.8 %collective-permute-start.8 = (bf16[16,64]{1,0:T(8,128)(2,1)S(1)}, bf16[16,64]{1,0:T(8,128)(2,1)S(1)}, u32[]{:S(2)}, u32[]{:S(2)}) collective-permute-start(bf16[16,64]{1,0:T(8,128)(2,1)S(1)} %get-tuple-element.45.refs_3_.refs_0_), channel_id=1, source_target_pairs={{0,3},{1,2},{2,1},{3,0},{4,7},{5,6},{6,5},{7,4},{8,11},{9,10},{10,... | collective-permute-start | bytes 6152 | tf_op jit(solution)/shard_map/ppermute | solution.py:32
  19.6 4.2 %collective-permute-start.7 = (bf16[16,64]{1,0:T(8,128)(2,1)S(1)}, bf16[16,64]{1,0:T(8,128)(2,1)S(1)}, u32[]{:S(2)}, u32[]{:S(2)}) collective-permute-start(bf16[16,64]{1,0:T(8,128)(2,1)S(1)} %get-tuple-element.45.refs_3_.refs_0_), channel_id=1, source_target_pairs={{0,2},{1,3},{2,0},{3,1},{4,6},{5,7},{6,4},{7,5},{8,10},{9,11},{10,... | collective-permute-start | bytes 6152 | tf_op jit(solution)/shard_map/ppermute | solution.py:32
  20.7 3.1 %collective-permute-start.6 = (bf16[16,64]{1,0:T(8,128)(2,1)S(1)}, bf16[16,64]{1,0:T(8,128)(2,1)S(1)}, u32[]{:S(2)}, u32[]{:S(2)}) collective-permute-start(bf16[16,64]{1,0:T(8,128)(2,1)S(1)} %get-tuple-element.45.refs_3_.refs_0_), channel_id=1, source_target_pairs={{0,1},{1,0},{2,3},{3,2},{4,5},{5,4},{6,7},{7,6},{8,9},{9,8},{10,11... | collective-permute-start | bytes 6152 | tf_op jit(solution)/shard_map/ppermute | solution.py:32
  23.8 5.9 %collective-permute-start.11 = (bf16[16,64]{1,0:T(8,128)(2,1)S(1)}, bf16[16,64]{1,0:T(8,128)(2,1)S(1)}, u32[]{:S(2)}, u32[]{:S(2)}) collective-permute-start(bf16[16,64]{1,0:T(8,128)(2,1)S(1)} %sum.2.refs_0_), channel_id=1, source_target_pairs={{0,12},{1,13},{2,14},{3,15},{4,8},{5,9},{6,10},{7,11},{8,4},{9,5},... | collective-permute-start | bytes 6152 | tf_op jit(solution)/shard_map/ppermute | solution.py:32
  27.5 4.5 %collective-permute-start.10 = (bf16[16,64]{1,0:T(8,128)(2,1)S(1)}, bf16[16,64]{1,0:T(8,128)(2,1)S(1)}, u32[]{:S(2)}, u32[]{:S(2)}) collective-permute-start(bf16[16,64]{1,0:T(8,128)(2,1)S(1)} %sum.2.refs_0_), channel_id=1, source_target_pairs={{0,8},{1,9},{2,10},{3,11},{4,12},{5,13},{6,14},{7,15},{8,0},{9,1},... | collective-permute-start | bytes 6152 | tf_op jit(solution)/shard_map/ppermute | solution.py:32
  27.5 4.5 %collective-permute-start.9 = (bf16[16,64]{1,0:T(8,128)(2,1)S(1)}, bf16[16,64]{1,0:T(8,128)(2,1)S(1)}, u32[]{:S(2)}, u32[]{:S(2)}) collective-permute-start(bf16[16,64]{1,0:T(8,128)(2,1)S(1)} %sum.2.refs_0_), channel_id=1, source_target_pairs={{0,4},{1,5},{2,6},{3,7},{4,0},{5,1},{6,2},{7,3},{8,12},{9,13},{10,... | collective-permute-start | bytes 6152 | tf_op jit(solution)/shard_map/ppermute | solution.py:32
  53.9 1.4 %collective-permute-start.12 = (bf16[8,8192]{1,0:T(8,128)(2,1)S(1)}, bf16[8,8192]{1,0:T(8,128)(2,1)S(1)}, u32[]{:S(2)}, u32[]{:S(2)}) collective-permute-start(bf16[8,8192]{1,0:T(8,128)(2,1)S(1)} %get-tuple-element.58), channel_id=1, source_target_pairs={{0,1},{1,0},{2,3},{3,2},{4,5},{5,4},{6,7},{7,6},{8,9},{9,8},{10,11... | collective-permute-start | bytes 393224 | tf_op jit(solution)/shard_map/ppermute | solution.py:32
  55.3 4.3 %collective-permute-start.13 = (bf16[4,8192]{1,0:T(4,128)(2,1)S(1)}, bf16[4,8192]{1,0:T(4,128)(2,1)S(1)}, u32[]{:S(2)}, u32[]{:S(2)}) collective-permute-start(bf16[4,8192]{1,0:T(4,128)(2,1)S(1)} %get-tuple-element.60), channel_id=1, source_target_pairs={{0,2},{1,3},{2,0},{3,1},{4,6},{5,7},{6,4},{7,5},{8,10},{9,11},{10,... | collective-permute-start | bytes 196616 | tf_op jit(solution)/shard_map/ppermute | solution.py:32
  59.7 6.4 %collective-permute-start.16 = (bf16[4,8192]{1,0:T(4,128)(2,1)S(1)}, bf16[4,8192]{1,0:T(4,128)(2,1)S(1)}, u32[]{:S(2)}, u32[]{:S(2)}) collective-permute-start(bf16[4,8192]{1,0:T(4,128)(2,1)S(1)} %fold.3.refs_0_), channel_id=1, source_target_pairs={{0,12},{1,13},{2,14},{3,15},{4,8},{5,9},{6,10},{7,11},{8,4},{9,5},... | collective-permute-start | bytes 196616 | tf_op jit(solution)/shard_map/ppermute | solution.py:32
  60.2 7.1 %collective-permute-start.15 = (bf16[4,8192]{1,0:T(4,128)(2,1)S(1)}, bf16[4,8192]{1,0:T(4,128)(2,1)S(1)}, u32[]{:S(2)}, u32[]{:S(2)}) collective-permute-start(bf16[4,8192]{1,0:T(4,128)(2,1)S(1)} %fold.3.refs_0_), channel_id=1, source_target_pairs={{0,8},{1,9},{2,10},{3,11},{4,12},{5,13},{6,14},{7,15},{8,0},{9,1},... | collective-permute-start | bytes 196616 | tf_op jit(solution)/shard_map/ppermute | solution.py:32
  61.7 5.7 %collective-permute-start.14 = (bf16[4,8192]{1,0:T(4,128)(2,1)S(1)}, bf16[4,8192]{1,0:T(4,128)(2,1)S(1)}, u32[]{:S(2)}, u32[]{:S(2)}) collective-permute-start(bf16[4,8192]{1,0:T(4,128)(2,1)S(1)} %fold.3.refs_0_), channel_id=1, source_target_pairs={{0,4},{1,5},{2,6},{3,7},{4,0},{5,1},{6,2},{7,3},{8,12},{9,13},{10,... | collective-permute-start | bytes 196616 | tf_op jit(solution)/shard_map/ppermute | solution.py:32
  68.0 3.8 %collective-permute-start.19 = (bf16[4,8192]{1,0:T(4,128)(2,1)S(1)}, bf16[4,8192]{1,0:T(4,128)(2,1)S(1)}, u32[]{:S(2)}, u32[]{:S(2)}) collective-permute-start(bf16[4,8192]{1,0:T(4,128)(2,1)S(1)} %get-tuple-element.62.refs_0_), channel_id=1, source_target_pairs={{0,3},{1,2},{2,1},{3,0},{4,7},{5,6},{6,5},{7,4},{8,11},{9,10},{10,... | collective-permute-start | bytes 196616 | tf_op jit(solution)/shard_map/ppermute | solution.py:32
  68.1 5.0 %collective-permute-start.18 = (bf16[4,8192]{1,0:T(4,128)(2,1)S(1)}, bf16[4,8192]{1,0:T(4,128)(2,1)S(1)}, u32[]{:S(2)}, u32[]{:S(2)}) collective-permute-start(bf16[4,8192]{1,0:T(4,128)(2,1)S(1)} %get-tuple-element.62.refs_0_), channel_id=1, source_target_pairs={{0,2},{1,3},{2,0},{3,1},{4,6},{5,7},{6,4},{7,5},{8,10},{9,11},{10,... | collective-permute-start | bytes 196616 | tf_op jit(solution)/shard_map/ppermute | solution.py:32
  68.7 4.4 %collective-permute-start.17 = (bf16[4,8192]{1,0:T(4,128)(2,1)S(1)}, bf16[4,8192]{1,0:T(4,128)(2,1)S(1)}, u32[]{:S(2)}, u32[]{:S(2)}) collective-permute-start(bf16[4,8192]{1,0:T(4,128)(2,1)S(1)} %get-tuple-element.62.refs_0_), channel_id=1, source_target_pairs={{0,1},{1,0},{2,3},{3,2},{4,5},{5,4},{6,7},{7,6},{8,9},{9,8},{10,11... | collective-permute-start | bytes 196616 | tf_op jit(solution)/shard_map/ppermute | solution.py:32
  73.8 3.1 %collective-permute-start.22 = (bf16[16,64]{1,0:T(8,128)(2,1)S(1)}, bf16[16,64]{1,0:T(8,128)(2,1)S(1)}, u32[]{:S(2)}, u32[]{:S(2)}) collective-permute-start(bf16[16,64]{1,0:T(8,128)(2,1)S(1)} %get-tuple-element.64.refs_0_), channel_id=1, source_target_pairs={{0,3},{1,2},{2,1},{3,0},{4,7},{5,6},{6,5},{7,4},{8,11},{9,10},{10,... | collective-permute-start | bytes 6152 | tf_op jit(solution)/shard_map/ppermute | solution.py:32
  74.9 3.6 %collective-permute-start.21 = (bf16[16,64]{1,0:T(8,128)(2,1)S(1)}, bf16[16,64]{1,0:T(8,128)(2,1)S(1)}, u32[]{:S(2)}, u32[]{:S(2)}) collective-permute-start(bf16[16,64]{1,0:T(8,128)(2,1)S(1)} %get-tuple-element.64.refs_0_), channel_id=1, source_target_pairs={{0,2},{1,3},{2,0},{3,1},{4,6},{5,7},{6,4},{7,5},{8,10},{9,11},{10,... | collective-permute-start | bytes 6152 | tf_op jit(solution)/shard_map/ppermute | solution.py:32
  75.6 2.9 %collective-permute-start.20 = (bf16[16,64]{1,0:T(8,128)(2,1)S(1)}, bf16[16,64]{1,0:T(8,128)(2,1)S(1)}, u32[]{:S(2)}, u32[]{:S(2)}) collective-permute-start(bf16[16,64]{1,0:T(8,128)(2,1)S(1)} %get-tuple-element.64.refs_0_), channel_id=1, source_target_pairs={{0,1},{1,0},{2,3},{3,2},{4,5},{5,4},{6,7},{7,6},{8,9},{9,8},{10,11... | collective-permute-start | bytes 6152 | tf_op jit(solution)/shard_map/ppermute | solution.py:32
  78.5 5.9 %collective-permute-start.25 = (bf16[16,64]{1,0:T(8,128)(2,1)S(1)}, bf16[16,64]{1,0:T(8,128)(2,1)S(1)}, u32[]{:S(2)}, u32[]{:S(2)}) collective-permute-start(bf16[16,64]{1,0:T(8,128)(2,1)S(1)} %sum.3.refs_0_), channel_id=1, source_target_pairs={{0,12},{1,13},{2,14},{3,15},{4,8},{5,9},{6,10},{7,11},{8,4},{9,5},... | collective-permute-start | bytes 6152 | tf_op jit(solution)/shard_map/ppermute | solution.py:32
  80.1 4.5 %collective-permute-start.24 = (bf16[16,64]{1,0:T(8,128)(2,1)S(1)}, bf16[16,64]{1,0:T(8,128)(2,1)S(1)}, u32[]{:S(2)}, u32[]{:S(2)}) collective-permute-start(bf16[16,64]{1,0:T(8,128)(2,1)S(1)} %sum.3.refs_0_), channel_id=1, source_target_pairs={{0,8},{1,9},{2,10},{3,11},{4,12},{5,13},{6,14},{7,15},{8,0},{9,1},... | collective-permute-start | bytes 6152 | tf_op jit(solution)/shard_map/ppermute | solution.py:32
  80.9 3.7 %collective-permute-start.23 = (bf16[16,64]{1,0:T(8,128)(2,1)S(1)}, bf16[16,64]{1,0:T(8,128)(2,1)S(1)}, u32[]{:S(2)}, u32[]{:S(2)}) collective-permute-start(bf16[16,64]{1,0:T(8,128)(2,1)S(1)} %sum.3.refs_0_), channel_id=1, source_target_pairs={{0,4},{1,5},{2,6},{3,7},{4,0},{5,1},{6,2},{7,3},{8,12},{9,13},{10,... | collective-permute-start | bytes 6152 | tf_op jit(solution)/shard_map/ppermute | solution.py:32
  106.6 1.4 %collective-permute-start.26 = (bf16[8,8192]{1,0:T(8,128)(2,1)S(1)}, bf16[8,8192]{1,0:T(8,128)(2,1)S(1)}, u32[]{:S(2)}, u32[]{:S(2)}) collective-permute-start(bf16[8,8192]{1,0:T(8,128)(2,1)S(1)} %get-tuple-element.71), channel_id=1, source_target_pairs={{0,1},{1,0},{2,3},{3,2},{4,5},{5,4},{6,7},{7,6},{8,9},{9,8},{10,11... | collective-permute-start | bytes 393224 | tf_op jit(solution)/shard_map/ppermute | solution.py:32

commit v16 on v15

--- a/solution.py
+++ b/solution.py
@@ -483,10 +483,10 @@
             rest = [key_value_weight, adapter_up_weight, key_value_cache]
             (fresh_w, up_w, cache), token = stash(token, rest, low)
             behind = [token]
-        (low,) = call(functools.partial(sum_kernel, near), [shape((count, rank))], "sum")(
-            *across(low, near_steps, count), *behind
+        (low,) = call(functools.partial(sum_kernel, far), [shape((count, rank))], "sum")(
+            *across(low, far_steps, count), *behind
         )
-        lows = across(low, far_steps, count)
+        lows = across(low, near_steps, count)
         query, fresh = call(
             project_kernel,
             [shape((count, columns), jnp.float32), shape((count, fresh_columns), jnp.float32)],
@@ -495,7 +495,7 @@
             moved=2 * width * (columns + fresh_columns),
         )(rows, query_w, fresh_w)
         (lines,) = call(
-            functools.partial(up_kernel, far),
+            functools.partial(up_kernel, near),
             [shape((count, 8, line))],
             "up",
             [pltpu.VMEM((count, 8, line), jnp.float32)],

time: 119 us -> 119 us (level)
  waiting for transfers between devices: 18.9 us -> 17 us
  blocking collectives: 48.6 us -> 49.9 us
    ppermute x27, waiting for transfers between devices: 18.9 us -> 17 us  [shift(): return lax.ppermute(block, AXIS, [(i, i ^ distance) for i in range(count)])]
    all_to_all x4, blocking collectives: 38.6 us -> 40 us  [swap(): return lax.all_to_all(blocks, AXIS, split_axis=0, concat_axis=0, tiled=True)]
  transfers between devices with their start and end apart: 27 -> 27, of which waited for: 13 -> 14; matrix products, arithmetic and copies ran while one was open for 0% -> 0% of each run, Pallas kernels for 11% -> 11%
where the time goes in v16:
time: 119 us; the launch traced here: 118 us
  blocking collectives  49.9 us (42%)
  starting transfers between devices  27.2 us (23%)
  Pallas kernels  21.8 us (18%)
  waiting for transfers between devices  17 us (14%)
  between operations  1.47 us (1%)
    all_to_all x4, blocking collectives, swap(): return lax.all_to_all(blocks, AXIS, split_axis=0, concat_axis=0, tiled=True)  40 us
    ppermute x27, starting transfers between devices, shift(): return lax.ppermute(block, AXIS, [(i, i ^ distance) for i in range(count)])  27.2 us
    pallas_call x22, Pallas kernels, run(): pl.pallas_call(body, out_shape=outs, in_specs=[pl.BlockSpec(memory_space=...  21.8 us
    ppermute x27, waiting for transfers between devices, shift(): return lax.ppermute(block, AXIS, [(i, i ^ distance) for i in range(count)])  17 us
    all_to_all x1, blocking collectives, chips_swap(): lax.all_to_all(blocks, AXIS, split_axis=0, concat_axis=0, axis_index_grou...  9.97 us
  transfers between devices with their start and end apart: 27, of which 14 were waited for; matrix products, arithmetic and copies ran while one was open for 0% of the time, Pallas kernels for 11%

profile of v16, /device:TPU:0, one launch (start us, length us, event | category | flops | bytes accessed | tf_op | source)
XLA Modules:
  0.0 118.1 jit_solution(4896847838283513682)
XLA Ops:
  2.1 5.1 %collective-permute-start.2 = (bf16[1,8320]{1,0:T(2,128)(2,1)S(1)}, bf16[1,8320]{1,0:T(2,128)(2,1)S(1)}, u32[]{:S(2)}, u32[]{:S(2)}) collective-permute-start(bf16[1,8320]{1,0:T(2,128)(2,1)S(1)} %get-tuple-element.39.refs_0_), channel_id=1, source_target_pairs={{0,12},{1,13},{2,14},{3,15},{4,8},{5,9},{6,10},{7,11},{8,4},{9,5},... | collective-permute-start | bytes 49928 | tf_op jit(solution)/shard_map/ppermute | solution.py:32
  7.8 4.0 %stash.3 = (bf16[8192,512]{1,0:T(8,128)(2,1)S(1)}, bf16[2,64,8192]{2,1,0:T(8,128)(2,1)S(1)}, s32[8,128]{1,0:T(8,128)S(1)}) custom-call(s32[8,128]{1,0:T(8,128)S(1)} %get-tuple-element.40.token_ref.refs_1_, bf16[8192,512]{1,0:T(8,128)(2,1)} %refs_0_.3, bf16[2,64,8192]{2,1,0:T(8,128)(2,1)} %bitcast.8), custom_call_target="tpu_custom_call" | custom-call | flops 1048576 | bytes 10485760 | tf_op jit(solution)/shard_map/stash/pallas_call | solution.py:53
  12.6 1.3 %collective-permute-start.4 = (bf16[4,8320]{1,0:T(4,128)(2,1)S(1)}, bf16[4,8320]{1,0:T(4,128)(2,1)S(1)}, u32[]{:S(2)}, u32[]{:S(2)}) collective-permute-start(bf16[4,8320]{1,0:T(4,128)(2,1)S(1)} %get-tuple-element.42.refs_0_), channel_id=1, source_target_pairs={{0,2},{1,3},{2,0},{3,1},{4,6},{5,7},{6,4},{7,5},{8,10},{9,11},{10,... | collective-permute-start | bytes 199688 | tf_op jit(solution)/shard_map/ppermute | solution.py:32
  14.3 3.4 %stash.4 = (bf16[512,8192]{1,0:T(8,128)(2,1)S(1)}, s32[8,128]{1,0:T(8,128)S(1)}) custom-call(s32[8,128]{1,0:T(8,128)S(1)} %get-tuple-element.41.refs_5_.token_ref, bf16[512,8192]{1,0:T(8,128)(2,1)} %refs_0_.4), custom_call_target="tpu_custom_call" | custom-call | flops 1048576 | bytes 8388608 | tf_op jit(solution)/shard_map/stash/pallas_call | solution.py:53
  19.0 3.6 %collective-permute-start.8 = (bf16[16,64]{1,0:T(8,128)(2,1)S(1)}, bf16[16,64]{1,0:T(8,128)(2,1)S(1)}, u32[]{:S(2)}, u32[]{:S(2)}) collective-permute-start(bf16[16,64]{1,0:T(8,128)(2,1)S(1)} %get-tuple-element.45.refs_3_.refs_0_), channel_id=1, source_target_pairs={{0,12},{1,13},{2,14},{3,15},{4,8},{5,9},{6,10},{7,11},{8,4},{9,5},... | collective-permute-start | bytes 6152 | tf_op jit(solution)/shard_map/ppermute | solution.py:32
  23.4 2.9 %stash.5 = (bf16[8192,128]{1,0:T(8,128)(2,1)S(1)}, bf16[32,64,512]{2,1,0:T(8,128)(2,1)S(1)}, bf16[1,2,512,1024]{3,2,1,0:T(8,128)(2,1)S(1)}, s32[8,128]{1,0:T(8,128)S(1)}) custom-call(s32[8,128]{1,0:T(8,128)S(1)} %get-tuple-element.44.refs_7_.token_ref, bf16[8192,128]{1,0:T(8,128)(2,1)} %refs_0_.5, bf16[32,64,512]{2,1,0:T(8,128)(2,1)} %refs_1_.1, ...), custom_call_target="tpu_custom_call" | custom-call | flops 1048576 | bytes 6291456 | tf_op jit(solution)/shard_map/stash/pallas_call | solution.py:53
  26.3 0.8 collective-permute-done.7.refs_2_
  27.3 1.0 collective-permute-start.10
  29.1 1.5 %project.2 = (f32[16,512]{1,0:T(8,128)S(1)}, f32[16,128]{1,0:T(8,128)S(1)}) custom-call(bf16[16,8192]{1,0:T(8,128)(2,1)S(1)} %get-tuple-element.47.rows_ref, bf16[8192,512]{1,0:T(8,128)(2,1)S(1)} %get-tuple-element.48.query_w, bf16[8192,128]{1,0:T(8,128)(2,1)S(1)} %get-tuple-element.49.fresh_w), custom_call_target="tpu_custom_call" | custom-call | flops 167772160 | bytes 10485760 | tf_op jit(solution)/shard_map/project/pallas_call | solution.py:53
  31.4 11.0 %all_to_all.25.refs_0_ = bf16[16,8,128]{2,1,0:T(8,128)(2,1)S(1)} all-to-all(bf16[16,8,128]{2,1,0:T(8,128)(2,1)S(1)} %up.2), channel_id=1, replica_groups=mesh['groups'=2,'replica'=16] {'replica'}, dimensions={0} | all-to-all | bytes 65536 | tf_op jit(solution)/shard_map/all_to_all | solution.py:40
  43.2 9.1 %all_to_all.26.lines_ref = bf16[16,4,128]{2,1,0:T(4,128)(2,1)S(1)} all-to-all(bf16[16,4,128]{2,1,0:T(4,128)(2,1)S(1)} %get-tuple-element.55), channel_id=1, replica_groups=mesh['groups'=2,'replica'=16] {'replica'}, dimensions={0} | all-to-all | bytes 32768 | tf_op jit(solution)/shard_map/all_to_all | solution.py:40
  52.3 1.3 %output.2 = (f32[8,8192]{1,0:T(8,128)S(1)}, bf16[8,8192]{1,0:T(8,128)(2,1)S(1)}) custom-call(bf16[16,4,128]{2,1,0:T(4,128)(2,1)S(1)} %all_to_all.26.lines_ref, s32[1]{0:T(128)} %bitcast._.refs_4_.me_ref, bf16[512,8192]{1,0:T(8,128)(2,1)S(1)} %get-tuple-element.56.weight_ref), custom_call_target="tpu_custom_call" | custom-call | flops 134217728 | bytes 8388608 | tf_op jit(solution)/shard_map/output/pallas_call | solution.py:53
  53.6 1.4 %collective-permute-done.12.other_ref = bf16[8,8192]{1,0:T(8,128)(2,1)S(1)} collective-permute-done((bf16[8,8192]{1,0:T(8,128)(2,1)S(1)}, bf16[8,8192]{1,0:T(8,128)(2,1)S(1)}, u32[]{:S(2)}, u32[]{:S(2)}) %collective-permute-start.12) | collective-permute-done | bytes 131104 | tf_op jit(solution)/shard_map/ppermute | solution.py:32
  55.5 3.8 %collective-permute-done.13.other_ref = bf16[4,8192]{1,0:T(4,128)(2,1)S(1)} collective-permute-done((bf16[4,8192]{1,0:T(4,128)(2,1)S(1)}, bf16[4,8192]{1,0:T(4,128)(2,1)S(1)}, u32[]{:S(2)}, u32[]{:S(2)}) %collective-permute-start.13) | collective-permute-done | bytes 65568 | tf_op jit(solution)/shard_map/ppermute | solution.py:32
  59.9 1.4 %collective-permute-start.15 = (bf16[4,8192]{1,0:T(4,128)(2,1)S(1)}, bf16[4,8192]{1,0:T(4,128)(2,1)S(1)}, u32[]{:S(2)}, u32[]{:S(2)}) collective-permute-start(bf16[4,8192]{1,0:T(4,128)(2,1)S(1)} %fold.3.refs_0_), channel_id=1, source_target_pairs={{0,8},{1,9},{2,10},{3,11},{4,12},{5,13},{6,14},{7,15},{8,0},{9,1},... | collective-permute-start | bytes 196616 | tf_op jit(solution)/shard_map/ppermute | solution.py:32
  61.4 2.5 %collective-permute-start.14 = (bf16[4,8192]{1,0:T(4,128)(2,1)S(1)}, bf16[4,8192]{1,0:T(4,128)(2,1)S(1)}, u32[]{:S(2)}, u32[]{:S(2)}) collective-permute-start(bf16[4,8192]{1,0:T(4,128)(2,1)S(1)} %fold.3.refs_0_), channel_id=1, source_target_pairs={{0,4},{1,5},{2,6},{3,7},{4,0},{5,1},{6,2},{7,3},{8,12},{9,13},{10,... | collective-permute-start | bytes 196616 | tf_op jit(solution)/shard_map/ppermute | solution.py:32
  63.8 2.0 %collective-permute-done.16.refs_3_ = bf16[4,8192]{1,0:T(4,128)(2,1)S(1)} collective-permute-done((bf16[4,8192]{1,0:T(4,128)(2,1)S(1)}, bf16[4,8192]{1,0:T(4,128)(2,1)S(1)}, u32[]{:S(2)}, u32[]{:S(2)}) %collective-permute-start.16) | collective-permute-done | bytes 65568 | tf_op jit(solution)/shard_map/ppermute | solution.py:32
  65.8 1.3 %collective-permute-done.15.refs_2_ = bf16[4,8192]{1,0:T(4,128)(2,1)S(1)} collective-permute-done((bf16[4,8192]{1,0:T(4,128)(2,1)S(1)}, bf16[4,8192]{1,0:T(4,128)(2,1)S(1)}, u32[]{:S(2)}, u32[]{:S(2)}) %collective-permute-start.15) | collective-permute-done | bytes 65568 | tf_op jit(solution)/shard_map/ppermute | solution.py:32
  68.4 1.2 %collective-permute-start.17 = (bf16[4,8192]{1,0:T(4,128)(2,1)S(1)}, bf16[4,8192]{1,0:T(4,128)(2,1)S(1)}, u32[]{:S(2)}, u32[]{:S(2)}) collective-permute-start(bf16[4,8192]{1,0:T(4,128)(2,1)S(1)} %get-tuple-element.62.refs_0_), channel_id=1, source_target_pairs={{0,1},{1,0},{2,3},{3,2},{4,5},{5,4},{6,7},{7,6},{8,9},{9,8},{10,11... | collective-permute-start | bytes 196616 | tf_op jit(solution)/shard_map/ppermute | solution.py:32
  69.6 1.9 %collective-permute-done.19.refs_3_ = bf16[4,8192]{1,0:T(4,128)(2,1)S(1)} collective-permute-done((bf16[4,8192]{1,0:T(4,128)(2,1)S(1)}, bf16[4,8192]{1,0:T(4,128)(2,1)S(1)}, u32[]{:S(2)}, u32[]{:S(2)}) %collective-permute-start.19) | collective-permute-done | bytes 65568 | tf_op jit(solution)/shard_map/ppermute | solution.py:32
  71.6 1.2 %collective-permute-done.18.refs_2_ = bf16[4,8192]{1,0:T(4,128)(2,1)S(1)} collective-permute-done((bf16[4,8192]{1,0:T(4,128)(2,1)S(1)}, bf16[4,8192]{1,0:T(4,128)(2,1)S(1)}, u32[]{:S(2)}, u32[]{:S(2)}) %collective-permute-start.18) | collective-permute-done | bytes 65568 | tf_op jit(solution)/shard_map/ppermute | solution.py:32
  73.5 1.6 %collective-permute-start.22 = (bf16[16,64]{1,0:T(8,128)(2,1)S(1)}, bf16[16,64]{1,0:T(8,128)(2,1)S(1)}, u32[]{:S(2)}, u32[]{:S(2)}) collective-permute-start(bf16[16,64]{1,0:T(8,128)(2,1)S(1)} %get-tuple-element.64.refs_0_), channel_id=1, source_target_pairs={{0,12},{1,13},{2,14},{3,15},{4,8},{5,9},{6,10},{7,11},{8,4},{9,5},... | collective-permute-start | bytes 6152 | tf_op jit(solution)/shard_map/ppermute | solution.py:32
  75.1 0.9 collective-permute-start.21
  76.1 1.9 %collective-permute-start.20 = (bf16[16,64]{1,0:T(8,128)(2,1)S(1)}, bf16[16,64]{1,0:T(8,128)(2,1)S(1)}, u32[]{:S(2)}, u32[]{:S(2)}) collective-permute-start(bf16[16,64]{1,0:T(8,128)(2,1)S(1)} %get-tuple-element.64.refs_0_), channel_id=1, source_target_pairs={{0,4},{1,5},{2,6},{3,7},{4,0},{5,1},{6,2},{7,3},{8,12},{9,13},{10,... | collective-permute-start | bytes 6152 | tf_op jit(solution)/shard_map/ppermute | solution.py:32
  77.9 1.0 collective-permute-done.22.refs_3_
  79.7 1.4 %collective-permute-start.24 = (bf16[16,64]{1,0:T(8,128)(2,1)S(1)}, bf16[16,64]{1,0:T(8,128)(2,1)S(1)}, u32[]{:S(2)}, u32[]{:S(2)}) collective-permute-start(bf16[16,64]{1,0:T(8,128)(2,1)S(1)} %sum.3.refs_0_), channel_id=1, source_target_pairs={{0,2},{1,3},{2,0},{3,1},{4,6},{5,7},{6,4},{7,5},{8,10},{9,11},{10,... | collective-permute-start | bytes 6152 | tf_op jit(solution)/shard_map/ppermute | solution.py:32
  81.6 1.5 %project.3 = (f32[16,512]{1,0:T(8,128)S(1)}, f32[16,128]{1,0:T(8,128)S(1)}) custom-call(bf16[16,8192]{1,0:T(8,128)(2,1)S(1)} %get-tuple-element.65.rows_ref, bf16[8192,512]{1,0:T(8,128)(2,1)S(1)} %get-tuple-element.48.query_w, bf16[8192,128]{1,0:T(8,128)(2,1)S(1)} %get-tuple-element.49.fresh_w), custom_call_target="tpu_custom_call" | custom-call | flops 167772160 | bytes 10485760 | tf_op jit(solution)/shard_map/project/pallas_call | solution.py:53
  83.9 10.8 %all_to_all.27.refs_0_ = bf16[16,8,128]{2,1,0:T(8,128)(2,1)S(1)} all-to-all(bf16[16,8,128]{2,1,0:T(8,128)(2,1)S(1)} %up.3), channel_id=1, replica_groups=mesh['groups'=2,'replica'=16] {'replica'}, dimensions={0} | all-to-all | bytes 65536 | tf_op jit(solution)/shard_map/all_to_all | solution.py:40
  95.5 9.1 %all_to_all.28.lines_ref = bf16[16,4,128]{2,1,0:T(4,128)(2,1)S(1)} all-to-all(bf16[16,4,128]{2,1,0:T(4,128)(2,1)S(1)} %attend.3), channel_id=1, replica_groups=mesh['groups'=2,'replica'=16] {'replica'}, dimensions={0} | all-to-all | bytes 32768 | tf_op jit(solution)/shard_map/all_to_all | solution.py:40
  104.6 1.3 %output.3 = (f32[8,8192]{1,0:T(8,128)S(1)}, bf16[8,8192]{1,0:T(8,128)(2,1)S(1)}) custom-call(bf16[16,4,128]{2,1,0:T(4,128)(2,1)S(1)} %all_to_all.28.lines_ref, s32[1]{0:T(128)} %bitcast._.refs_4_.me_ref, bf16[512,8192]{1,0:T(8,128)(2,1)S(1)} %get-tuple-element.56.weight_ref), custom_call_target="tpu_custom_call" | custom-call | flops 134217728 | bytes 8388608 | tf_op jit(solution)/shard_map/output/pallas_call | solution.py:53
  105.9 1.4 %collective-permute-done.26.other_ref = bf16[8,8192]{1,0:T(8,128)(2,1)S(1)} collective-permute-done((bf16[8,8192]{1,0:T(8,128)(2,1)S(1)}, bf16[8,8192]{1,0:T(8,128)(2,1)S(1)}, u32[]{:S(2)}, u32[]{:S(2)}) %collective-permute-start.26) | collective-permute-done | bytes 131104 | tf_op jit(solution)/shard_map/ppermute | solution.py:32
  107.4 10.0 %all_to_all.29.parts_ref = bf16[8,8,1024]{2,1,0:T(8,128)(2,1)S(1)} all-to-all(bf16[8,8,1024]{2,1,0:T(8,128)(2,1)S(1)} %partial.1), channel_id=1, replica_groups={{0,2,4,6,8,10,12,14},{1,3,5,7,9,11,13,15},{16,18,20,22,24,26,28,30},{17..., dimensions={0} | all-to-all | bytes 262144 | tf_op jit(solution)/shard_map/all_to_all | solution.py:45
  (55 shorter events, 14.1 us)
Async XLA Ops:
  1.3 0.8 copy-start.1
  2.1 9.8 %collective-permute-start.2 = (bf16[1,8320]{1,0:T(2,128)(2,1)S(1)}, bf16[1,8320]{1,0:T(2,128)(2,1)S(1)}, u32[]{:S(2)}, u32[]{:S(2)}) collective-permute-start(bf16[1,8320]{1,0:T(2,128)(2,1)S(1)} %get-tuple-element.39.refs_0_), channel_id=1, source_target_pairs={{0,12},{1,13},{2,14},{3,15},{4,8},{5,9},{6,10},{7,11},{8,4},{9,5},... | collective-permute-start | bytes 49928 | tf_op jit(solution)/shard_map/ppermute | solution.py:32
  7.2 4.8 %collective-permute-start.1 = (bf16[1,8320]{1,0:T(2,128)(2,1)S(1)}, bf16[1,8320]{1,0:T(2,128)(2,1)S(1)}, u32[]{:S(2)}, u32[]{:S(2)}) collective-permute-start(bf16[1,8320]{1,0:T(2,128)(2,1)S(1)} %get-tuple-element.39.refs_0_), channel_id=1, source_target_pairs={{0,8},{1,9},{2,10},{3,11},{4,12},{5,13},{6,14},{7,15},{8,0},{9,1},... | collective-permute-start | bytes 49928 | tf_op jit(solution)/shard_map/ppermute | solution.py:32
  7.2 4.8 %collective-permute-start = (bf16[1,8320]{1,0:T(2,128)(2,1)S(1)}, bf16[1,8320]{1,0:T(2,128)(2,1)S(1)}, u32[]{:S(2)}, u32[]{:S(2)}) collective-permute-start(bf16[1,8320]{1,0:T(2,128)(2,1)S(1)} %get-tuple-element.39.refs_0_), channel_id=1, source_target_pairs={{0,4},{1,5},{2,6},{3,7},{4,0},{5,1},{6,2},{7,3},{8,12},{9,13},{10,... | collective-permute-start | bytes 49928 | tf_op jit(solution)/shard_map/ppermute | solution.py:32
  7.8 4.2 %copy-start = (bf16[8192]{0:T(1024)(128)(2,1)S(1)}, bf16[8192]{0:T(1024)(128)(2,1)}, u32[]{:S(2)}) copy-start(bf16[8192]{0:T(1024)(128)(2,1)} %param.12) | copy-start | bytes 49156
  12.3 5.9 %copy-start.2 = (s32[32]{0:T(128)S(1)}, s32[32]{0:T(128)}, u32[]{:S(2)}) copy-start(s32[32]{0:T(128)} %param.19) | copy-start | bytes 388
  12.3 5.3 %collective-permute-start.5 = (bf16[4,8320]{1,0:T(4,128)(2,1)S(1)}, bf16[4,8320]{1,0:T(4,128)(2,1)S(1)}, u32[]{:S(2)}, u32[]{:S(2)}) collective-permute-start(bf16[4,8320]{1,0:T(4,128)(2,1)S(1)} %get-tuple-element.42.refs_0_), channel_id=1, source_target_pairs={{0,3},{1,2},{2,1},{3,0},{4,7},{5,6},{6,5},{7,4},{8,11},{9,10},{10,... | collective-permute-start | bytes 199688 | tf_op jit(solution)/shard_map/ppermute | solution.py:32
  12.6 5.6 %collective-permute-start.4 = (bf16[4,8320]{1,0:T(4,128)(2,1)S(1)}, bf16[4,8320]{1,0:T(4,128)(2,1)S(1)}, u32[]{:S(2)}, u32[]{:S(2)}) collective-permute-start(bf16[4,8320]{1,0:T(4,128)(2,1)S(1)} %get-tuple-element.42.refs_0_), channel_id=1, source_target_pairs={{0,2},{1,3},{2,0},{3,1},{4,6},{5,7},{6,4},{7,5},{8,10},{9,11},{10,... | collective-permute-start | bytes 199688 | tf_op jit(solution)/shard_map/ppermute | solution.py:32
  14.0 4.3 %collective-permute-start.3 = (bf16[4,8320]{1,0:T(4,128)(2,1)S(1)}, bf16[4,8320]{1,0:T(4,128)(2,1)S(1)}, u32[]{:S(2)}, u32[]{:S(2)}) collective-permute-start(bf16[4,8320]{1,0:T(4,128)(2,1)S(1)} %get-tuple-element.42.refs_0_), channel_id=1, source_target_pairs={{0,1},{1,0},{2,3},{3,2},{4,5},{5,4},{6,7},{7,6},{8,9},{9,8},{10,11... | collective-permute-start | bytes 199688 | tf_op jit(solution)/shard_map/ppermute | solution.py:32
  19.0 7.3 %collective-permute-start.8 = (bf16[16,64]{1,0:T(8,128)(2,1)S(1)}, bf16[16,64]{1,0:T(8,128)(2,1)S(1)}, u32[]{:S(2)}, u32[]{:S(2)}) collective-permute-start(bf16[16,64]{1,0:T(8,128)(2,1)S(1)} %get-tuple-element.45.refs_3_.refs_0_), channel_id=1, source_target_pairs={{0,12},{1,13},{2,14},{3,15},{4,8},{5,9},{6,10},{7,11},{8,4},{9,5},... | collective-permute-start | bytes 6152 | tf_op jit(solution)/shard_map/ppermute | solution.py:32
  22.7 4.5 %collective-permute-start.7 = (bf16[16,64]{1,0:T(8,128)(2,1)S(1)}, bf16[16,64]{1,0:T(8,128)(2,1)S(1)}, u32[]{:S(2)}, u32[]{:S(2)}) collective-permute-start(bf16[16,64]{1,0:T(8,128)(2,1)S(1)} %get-tuple-element.45.refs_3_.refs_0_), channel_id=1, source_target_pairs={{0,8},{1,9},{2,10},{3,11},{4,12},{5,13},{6,14},{7,15},{8,0},{9,1},... | collective-permute-start | bytes 6152 | tf_op jit(solution)/shard_map/ppermute | solution.py:32
  22.7 4.5 %collective-permute-start.6 = (bf16[16,64]{1,0:T(8,128)(2,1)S(1)}, bf16[16,64]{1,0:T(8,128)(2,1)S(1)}, u32[]{:S(2)}, u32[]{:S(2)}) collective-permute-start(bf16[16,64]{1,0:T(8,128)(2,1)S(1)} %get-tuple-element.45.refs_3_.refs_0_), channel_id=1, source_target_pairs={{0,4},{1,5},{2,6},{3,7},{4,0},{5,1},{6,2},{7,3},{8,12},{9,13},{10,... | collective-permute-start | bytes 6152 | tf_op jit(solution)/shard_map/ppermute | solution.py:32
  27.2 3.4 %collective-permute-start.11 = (bf16[16,64]{1,0:T(8,128)(2,1)S(1)}, bf16[16,64]{1,0:T(8,128)(2,1)S(1)}, u32[]{:S(2)}, u32[]{:S(2)}) collective-permute-start(bf16[16,64]{1,0:T(8,128)(2,1)S(1)} %sum.2.refs_0_), channel_id=1, source_target_pairs={{0,3},{1,2},{2,1},{3,0},{4,7},{5,6},{6,5},{7,4},{8,11},{9,10},{10,... | collective-permute-start | bytes 6152 | tf_op jit(solution)/shard_map/ppermute | solution.py:32
  27.3 3.7 %collective-permute-start.10 = (bf16[16,64]{1,0:T(8,128)(2,1)S(1)}, bf16[16,64]{1,0:T(8,128)(2,1)S(1)}, u32[]{:S(2)}, u32[]{:S(2)}) collective-permute-start(bf16[16,64]{1,0:T(8,128)(2,1)S(1)} %sum.2.refs_0_), channel_id=1, source_target_pairs={{0,2},{1,3},{2,0},{3,1},{4,6},{5,7},{6,4},{7,5},{8,10},{9,11},{10,... | collective-permute-start | bytes 6152 | tf_op jit(solution)/shard_map/ppermute | solution.py:32
  28.3 2.7 %collective-permute-start.9 = (bf16[16,64]{1,0:T(8,128)(2,1)S(1)}, bf16[16,64]{1,0:T(8,128)(2,1)S(1)}, u32[]{:S(2)}, u32[]{:S(2)}) collective-permute-start(bf16[16,64]{1,0:T(8,128)(2,1)S(1)} %sum.2.refs_0_), channel_id=1, source_target_pairs={{0,1},{1,0},{2,3},{3,2},{4,5},{5,4},{6,7},{7,6},{8,9},{9,8},{10,11... | collective-permute-start | bytes 6152 | tf_op jit(solution)/shard_map/ppermute | solution.py:32
  53.6 1.4 %collective-permute-start.12 = (bf16[8,8192]{1,0:T(8,128)(2,1)S(1)}, bf16[8,8192]{1,0:T(8,128)(2,1)S(1)}, u32[]{:S(2)}, u32[]{:S(2)}) collective-permute-start(bf16[8,8192]{1,0:T(8,128)(2,1)S(1)} %get-tuple-element.58), channel_id=1, source_target_pairs={{0,1},{1,0},{2,3},{3,2},{4,5},{5,4},{6,7},{7,6},{8,9},{9,8},{10,11... | collective-permute-start | bytes 393224 | tf_op jit(solution)/shard_map/ppermute | solution.py:32
  55.0 4.3 %collective-permute-start.13 = (bf16[4,8192]{1,0:T(4,128)(2,1)S(1)}, bf16[4,8192]{1,0:T(4,128)(2,1)S(1)}, u32[]{:S(2)}, u32[]{:S(2)}) collective-permute-start(bf16[4,8192]{1,0:T(4,128)(2,1)S(1)} %get-tuple-element.60), channel_id=1, source_target_pairs={{0,2},{1,3},{2,0},{3,1},{4,6},{5,7},{6,4},{7,5},{8,10},{9,11},{10,... | collective-permute-start | bytes 196616 | tf_op jit(solution)/shard_map/ppermute | solution.py:32
  59.4 6.4 %collective-permute-start.16 = (bf16[4,8192]{1,0:T(4,128)(2,1)S(1)}, bf16[4,8192]{1,0:T(4,128)(2,1)S(1)}, u32[]{:S(2)}, u32[]{:S(2)}) collective-permute-start(bf16[4,8192]{1,0:T(4,128)(2,1)S(1)} %fold.3.refs_0_), channel_id=1, source_target_pairs={{0,12},{1,13},{2,14},{3,15},{4,8},{5,9},{6,10},{7,11},{8,4},{9,5},... | collective-permute-start | bytes 196616 | tf_op jit(solution)/shard_map/ppermute | solution.py:32
  59.9 7.1 %collective-permute-start.15 = (bf16[4,8192]{1,0:T(4,128)(2,1)S(1)}, bf16[4,8192]{1,0:T(4,128)(2,1)S(1)}, u32[]{:S(2)}, u32[]{:S(2)}) collective-permute-start(bf16[4,8192]{1,0:T(4,128)(2,1)S(1)} %fold.3.refs_0_), channel_id=1, source_target_pairs={{0,8},{1,9},{2,10},{3,11},{4,12},{5,13},{6,14},{7,15},{8,0},{9,1},... | collective-permute-start | bytes 196616 | tf_op jit(solution)/shard_map/ppermute | solution.py:32
  61.4 5.7 %collective-permute-start.14 = (bf16[4,8192]{1,0:T(4,128)(2,1)S(1)}, bf16[4,8192]{1,0:T(4,128)(2,1)S(1)}, u32[]{:S(2)}, u32[]{:S(2)}) collective-permute-start(bf16[4,8192]{1,0:T(4,128)(2,1)S(1)} %fold.3.refs_0_), channel_id=1, source_target_pairs={{0,4},{1,5},{2,6},{3,7},{4,0},{5,1},{6,2},{7,3},{8,12},{9,13},{10,... | collective-permute-start | bytes 196616 | tf_op jit(solution)/shard_map/ppermute | solution.py:32
  67.7 3.8 %collective-permute-start.19 = (bf16[4,8192]{1,0:T(4,128)(2,1)S(1)}, bf16[4,8192]{1,0:T(4,128)(2,1)S(1)}, u32[]{:S(2)}, u32[]{:S(2)}) collective-permute-start(bf16[4,8192]{1,0:T(4,128)(2,1)S(1)} %get-tuple-element.62.refs_0_), channel_id=1, source_target_pairs={{0,3},{1,2},{2,1},{3,0},{4,7},{5,6},{6,5},{7,4},{8,11},{9,10},{10,... | collective-permute-start | bytes 196616 | tf_op jit(solution)/shard_map/ppermute | solution.py:32
  67.8 5.0 %collective-permute-start.18 = (bf16[4,8192]{1,0:T(4,128)(2,1)S(1)}, bf16[4,8192]{1,0:T(4,128)(2,1)S(1)}, u32[]{:S(2)}, u32[]{:S(2)}) collective-permute-start(bf16[4,8192]{1,0:T(4,128)(2,1)S(1)} %get-tuple-element.62.refs_0_), channel_id=1, source_target_pairs={{0,2},{1,3},{2,0},{3,1},{4,6},{5,7},{6,4},{7,5},{8,10},{9,11},{10,... | collective-permute-start | bytes 196616 | tf_op jit(solution)/shard_map/ppermute | solution.py:32
  68.4 4.4 %collective-permute-start.17 = (bf16[4,8192]{1,0:T(4,128)(2,1)S(1)}, bf16[4,8192]{1,0:T(4,128)(2,1)S(1)}, u32[]{:S(2)}, u32[]{:S(2)}) collective-permute-start(bf16[4,8192]{1,0:T(4,128)(2,1)S(1)} %get-tuple-element.62.refs_0_), channel_id=1, source_target_pairs={{0,1},{1,0},{2,3},{3,2},{4,5},{5,4},{6,7},{7,6},{8,9},{9,8},{10,11... | collective-permute-start | bytes 196616 | tf_op jit(solution)/shard_map/ppermute | solution.py:32
  73.5 5.4 %collective-permute-start.22 = (bf16[16,64]{1,0:T(8,128)(2,1)S(1)}, bf16[16,64]{1,0:T(8,128)(2,1)S(1)}, u32[]{:S(2)}, u32[]{:S(2)}) collective-permute-start(bf16[16,64]{1,0:T(8,128)(2,1)S(1)} %get-tuple-element.64.refs_0_), channel_id=1, source_target_pairs={{0,12},{1,13},{2,14},{3,15},{4,8},{5,9},{6,10},{7,11},{8,4},{9,5},... | collective-permute-start | bytes 6152 | tf_op jit(solution)/shard_map/ppermute | solution.py:32
  75.1 4.5 %collective-permute-start.21 = (bf16[16,64]{1,0:T(8,128)(2,1)S(1)}, bf16[16,64]{1,0:T(8,128)(2,1)S(1)}, u32[]{:S(2)}, u32[]{:S(2)}) collective-permute-start(bf16[16,64]{1,0:T(8,128)(2,1)S(1)} %get-tuple-element.64.refs_0_), channel_id=1, source_target_pairs={{0,8},{1,9},{2,10},{3,11},{4,12},{5,13},{6,14},{7,15},{8,0},{9,1},... | collective-permute-start | bytes 6152 | tf_op jit(solution)/shard_map/ppermute | solution.py:32
  76.1 3.6 %collective-permute-start.20 = (bf16[16,64]{1,0:T(8,128)(2,1)S(1)}, bf16[16,64]{1,0:T(8,128)(2,1)S(1)}, u32[]{:S(2)}, u32[]{:S(2)}) collective-permute-start(bf16[16,64]{1,0:T(8,128)(2,1)S(1)} %get-tuple-element.64.refs_0_), channel_id=1, source_target_pairs={{0,4},{1,5},{2,6},{3,7},{4,0},{5,1},{6,2},{7,3},{8,12},{9,13},{10,... | collective-permute-start | bytes 6152 | tf_op jit(solution)/shard_map/ppermute | solution.py:32
  79.7 3.4 %collective-permute-start.25 = (bf16[16,64]{1,0:T(8,128)(2,1)S(1)}, bf16[16,64]{1,0:T(8,128)(2,1)S(1)}, u32[]{:S(2)}, u32[]{:S(2)}) collective-permute-start(bf16[16,64]{1,0:T(8,128)(2,1)S(1)} %sum.3.refs_0_), channel_id=1, source_target_pairs={{0,3},{1,2},{2,1},{3,0},{4,7},{5,6},{6,5},{7,4},{8,11},{9,10},{10,... | collective-permute-start | bytes 6152 | tf_op jit(solution)/shard_map/ppermute | solution.py:32
  79.7 3.7 %collective-permute-start.24 = (bf16[16,64]{1,0:T(8,128)(2,1)S(1)}, bf16[16,64]{1,0:T(8,128)(2,1)S(1)}, u32[]{:S(2)}, u32[]{:S(2)}) collective-permute-start(bf16[16,64]{1,0:T(8,128)(2,1)S(1)} %sum.3.refs_0_), channel_id=1, source_target_pairs={{0,2},{1,3},{2,0},{3,1},{4,6},{5,7},{6,4},{7,5},{8,10},{9,11},{10,... | collective-permute-start | bytes 6152 | tf_op jit(solution)/shard_map/ppermute | solution.py:32
  81.1 2.3 %collective-permute-start.23 = (bf16[16,64]{1,0:T(8,128)(2,1)S(1)}, bf16[16,64]{1,0:T(8,128)(2,1)S(1)}, u32[]{:S(2)}, u32[]{:S(2)}) collective-permute-start(bf16[16,64]{1,0:T(8,128)(2,1)S(1)} %sum.3.refs_0_), channel_id=1, source_target_pairs={{0,1},{1,0},{2,3},{3,2},{4,5},{5,4},{6,7},{7,6},{8,9},{9,8},{10,11... | collective-permute-start | bytes 6152 | tf_op jit(solution)/shard_map/ppermute | solution.py:32
  105.9 1.4 %collective-permute-start.26 = (bf16[8,8192]{1,0:T(8,128)(2,1)S(1)}, bf16[8,8192]{1,0:T(8,128)(2,1)S(1)}, u32[]{:S(2)}, u32[]{:S(2)}) collective-permute-start(bf16[8,8192]{1,0:T(8,128)(2,1)S(1)} %get-tuple-element.71), channel_id=1, source_target_pairs={{0,1},{1,0},{2,3},{3,2},{4,5},{5,4},{6,7},{7,6},{8,9},{9,8},{10,11... | collective-permute-start | bytes 393224 | tf_op jit(solution)/shard_map/ppermute | solution.py:32

commit v17 on v16

--- a/solution.py
+++ b/solution.py
@@ -158,7 +158,8 @@
 
 
 def join_kernel(amount, *refs):
-    scale_ref, _, hidden_ref, out_ref = refs[amount:]
+    scale_ref, _, hidden_ref, out_ref, row_ref = refs[amount:]
+    row_ref[...] = row_of(scale_ref)
     width = hidden_ref.shape[1]
     rows = [ref[...].astype(jnp.float32) for ref in refs[:amount]]
     rows = jnp.concatenate(rows, axis=0)
@@ -200,7 +201,7 @@
     total = sums[0].astype(jnp.bfloat16).astype(jnp.float32)
     hidden = (hidden_ref[...].astype(jnp.float32) + total).astype(jnp.bfloat16)
     own_ref[...] = hidden.astype(jnp.float32)[:1].astype(jnp.bfloat16)
-    out_ref[...] = normalized(hidden.astype(jnp.float32), row_of(scale_ref))
+    out_ref[...] = normalized(hidden.astype(jnp.float32), scale_ref[...])
 
 
 def sum_kernel(amount, *refs):
@@ -452,9 +453,13 @@
         if first:
             (query_w, down_w), token = stash(length, [query_weight, down])
             pieces = across(carried, far_steps, count)
-            column, carried = call(
+            column, carried, scale_row = call(
                 functools.partial(join_kernel, far),
-                [shape((far, width)), shape((far, width + LANES))],
+                [
+                    shape((far, width)),
+                    shape((far, width + LANES)),
+                    shape((1, width), jnp.float32),
+                ],
                 "join",
             )(*pieces, scale, token)
             (output_w,), token = stash(token, [output_weight])
@@ -551,7 +556,7 @@
         (own,) = call(folded_kernel, [shape((far, width))], "fold")(own, shift(away, bit, count))
         hidden, carried = call(
             functools.partial(next_kernel, far), [shape((1, width)), shape((far, width))], "next"
-        )(*across(own, far_steps, count), column, scale)
+        )(*across(own, far_steps, count), column, scale_row)
 
 
 def solution(mesh):

time: 119 us -> 119 us (level)
  no operation moved by 1% of the time
where the time goes in v17:
time: 119 us; the launch traced here: 118 us
  blocking collectives  49.9 us (42%)
  starting transfers between devices  27.2 us (23%)
  Pallas kernels  21.8 us (18%)
  waiting for transfers between devices  17 us (14%)
  between operations  1.47 us (1%)
    all_to_all x4, blocking collectives, swap(): return lax.all_to_all(blocks, AXIS, split_axis=0, concat_axis=0, tiled=True)  40 us
    ppermute x27, starting transfers between devices, shift(): return lax.ppermute(block, AXIS, [(i, i ^ distance) for i in range(count)])  27.2 us
    pallas_call x22, Pallas kernels, run(): pl.pallas_call(body, out_shape=outs, in_specs=[pl.BlockSpec(memory_space=...  21.8 us
    ppermute x27, waiting for transfers between devices, shift(): return lax.ppermute(block, AXIS, [(i, i ^ distance) for i in range(count)])  17 us
    all_to_all x1, blocking collectives, chips_swap(): lax.all_to_all(blocks, AXIS, split_axis=0, concat_axis=0, axis_index_grou...  9.97 us
  transfers between devices with their start and end apart: 27, of which 14 were waited for; matrix products, arithmetic and copies ran while one was open for 0% of the time, Pallas kernels for 11%

profile of v17, /device:TPU:0, one launch (start us, length us, event | category | flops | bytes accessed | tf_op | source)
XLA Modules:
  0.0 118.2 jit_solution(3179835312849643128)
XLA Ops:
  2.1 5.1 %collective-permute-start.2 = (bf16[1,8320]{1,0:T(2,128)(2,1)S(1)}, bf16[1,8320]{1,0:T(2,128)(2,1)S(1)}, u32[]{:S(2)}, u32[]{:S(2)}) collective-permute-start(bf16[1,8320]{1,0:T(2,128)(2,1)S(1)} %get-tuple-element.40.refs_0_), channel_id=1, source_target_pairs={{0,12},{1,13},{2,14},{3,15},{4,8},{5,9},{6,10},{7,11},{8,4},{9,5},... | collective-permute-start | bytes 49928 | tf_op jit(solution)/shard_map/ppermute | solution.py:32
  7.8 4.0 %stash.3 = (bf16[8192,512]{1,0:T(8,128)(2,1)S(1)}, bf16[2,64,8192]{2,1,0:T(8,128)(2,1)S(1)}, s32[8,128]{1,0:T(8,128)S(1)}) custom-call(s32[8,128]{1,0:T(8,128)S(1)} %get-tuple-element.41.token_ref.refs_1_, bf16[8192,512]{1,0:T(8,128)(2,1)} %refs_0_.3, bf16[2,64,8192]{2,1,0:T(8,128)(2,1)} %bitcast.7), custom_call_target="tpu_custom_call" | custom-call | flops 1048576 | bytes 10485760 | tf_op jit(solution)/shard_map/stash/pallas_call | solution.py:53
  12.7 1.3 %collective-permute-start.4 = (bf16[4,8320]{1,0:T(4,128)(2,1)S(1)}, bf16[4,8320]{1,0:T(4,128)(2,1)S(1)}, u32[]{:S(2)}, u32[]{:S(2)}) collective-permute-start(bf16[4,8320]{1,0:T(4,128)(2,1)S(1)} %get-tuple-element.43.refs_0_), channel_id=1, source_target_pairs={{0,2},{1,3},{2,0},{3,1},{4,6},{5,7},{6,4},{7,5},{8,10},{9,11},{10,... | collective-permute-start | bytes 199688 | tf_op jit(solution)/shard_map/ppermute | solution.py:32
  14.3 3.4 %stash.4 = (bf16[512,8192]{1,0:T(8,128)(2,1)S(1)}, s32[8,128]{1,0:T(8,128)S(1)}) custom-call(s32[8,128]{1,0:T(8,128)S(1)} %get-tuple-element.42.refs_5_.token_ref, bf16[512,8192]{1,0:T(8,128)(2,1)} %refs_0_.4), custom_call_target="tpu_custom_call" | custom-call | flops 1048576 | bytes 8388608 | tf_op jit(solution)/shard_map/stash/pallas_call | solution.py:53
  19.0 3.6 %collective-permute-start.8 = (bf16[16,64]{1,0:T(8,128)(2,1)S(1)}, bf16[16,64]{1,0:T(8,128)(2,1)S(1)}, u32[]{:S(2)}, u32[]{:S(2)}) collective-permute-start(bf16[16,64]{1,0:T(8,128)(2,1)S(1)} %get-tuple-element.46.refs_3_.refs_0_), channel_id=1, source_target_pairs={{0,12},{1,13},{2,14},{3,15},{4,8},{5,9},{6,10},{7,11},{8,4},{9,5},... | collective-permute-start | bytes 6152 | tf_op jit(solution)/shard_map/ppermute | solution.py:32
  23.4 2.9 %stash.5 = (bf16[8192,128]{1,0:T(8,128)(2,1)S(1)}, bf16[32,64,512]{2,1,0:T(8,128)(2,1)S(1)}, bf16[1,2,512,1024]{3,2,1,0:T(8,128)(2,1)S(1)}, s32[8,128]{1,0:T(8,128)S(1)}) custom-call(s32[8,128]{1,0:T(8,128)S(1)} %get-tuple-element.45.refs_7_.token_ref, bf16[8192,128]{1,0:T(8,128)(2,1)} %refs_0_.5, bf16[32,64,512]{2,1,0:T(8,128)(2,1)} %refs_1_.1, ...), custom_call_target="tpu_custom_call" | custom-call | flops 1048576 | bytes 6291456 | tf_op jit(solution)/shard_map/stash/pallas_call | solution.py:53
  26.3 0.8 collective-permute-done.7.refs_2_
  27.3 1.0 collective-permute-start.10
  29.1 1.5 %project.2 = (f32[16,512]{1,0:T(8,128)S(1)}, f32[16,128]{1,0:T(8,128)S(1)}) custom-call(bf16[16,8192]{1,0:T(8,128)(2,1)S(1)} %get-tuple-element.48.rows_ref, bf16[8192,512]{1,0:T(8,128)(2,1)S(1)} %get-tuple-element.49.query_w, bf16[8192,128]{1,0:T(8,128)(2,1)S(1)} %get-tuple-element.50.fresh_w), custom_call_target="tpu_custom_call" | custom-call | flops 167772160 | bytes 10485760 | tf_op jit(solution)/shard_map/project/pallas_call | solution.py:53
  31.4 11.0 %all_to_all.25.refs_0_ = bf16[16,8,128]{2,1,0:T(8,128)(2,1)S(1)} all-to-all(bf16[16,8,128]{2,1,0:T(8,128)(2,1)S(1)} %up.2), channel_id=1, replica_groups=mesh['groups'=2,'replica'=16] {'replica'}, dimensions={0} | all-to-all | bytes 65536 | tf_op jit(solution)/shard_map/all_to_all | solution.py:40
  43.2 9.1 %all_to_all.26.lines_ref = bf16[16,4,128]{2,1,0:T(4,128)(2,1)S(1)} all-to-all(bf16[16,4,128]{2,1,0:T(4,128)(2,1)S(1)} %get-tuple-element.56), channel_id=1, replica_groups=mesh['groups'=2,'replica'=16] {'replica'}, dimensions={0} | all-to-all | bytes 32768 | tf_op jit(solution)/shard_map/all_to_all | solution.py:40
  52.3 1.3 %output.2 = (f32[8,8192]{1,0:T(8,128)S(1)}, bf16[8,8192]{1,0:T(8,128)(2,1)S(1)}) custom-call(bf16[16,4,128]{2,1,0:T(4,128)(2,1)S(1)} %all_to_all.26.lines_ref, s32[1]{0:T(128)} %bitcast._.refs_4_.me_ref, bf16[512,8192]{1,0:T(8,128)(2,1)S(1)} %get-tuple-element.57.weight_ref), custom_call_target="tpu_custom_call" | custom-call | flops 134217728 | bytes 8388608 | tf_op jit(solution)/shard_map/output/pallas_call | solution.py:53
  53.6 1.4 %collective-permute-done.12.other_ref = bf16[8,8192]{1,0:T(8,128)(2,1)S(1)} collective-permute-done((bf16[8,8192]{1,0:T(8,128)(2,1)S(1)}, bf16[8,8192]{1,0:T(8,128)(2,1)S(1)}, u32[]{:S(2)}, u32[]{:S(2)}) %collective-permute-start.12) | collective-permute-done | bytes 131104 | tf_op jit(solution)/shard_map/ppermute | solution.py:32
  55.5 3.8 %collective-permute-done.13.other_ref = bf16[4,8192]{1,0:T(4,128)(2,1)S(1)} collective-permute-done((bf16[4,8192]{1,0:T(4,128)(2,1)S(1)}, bf16[4,8192]{1,0:T(4,128)(2,1)S(1)}, u32[]{:S(2)}, u32[]{:S(2)}) %collective-permute-start.13) | collective-permute-done | bytes 65568 | tf_op jit(solution)/shard_map/ppermute | solution.py:32
  60.0 1.4 %collective-permute-start.15 = (bf16[4,8192]{1,0:T(4,128)(2,1)S(1)}, bf16[4,8192]{1,0:T(4,128)(2,1)S(1)}, u32[]{:S(2)}, u32[]{:S(2)}) collective-permute-start(bf16[4,8192]{1,0:T(4,128)(2,1)S(1)} %fold.3.refs_0_), channel_id=1, source_target_pairs={{0,8},{1,9},{2,10},{3,11},{4,12},{5,13},{6,14},{7,15},{8,0},{9,1},... | collective-permute-start | bytes 196616 | tf_op jit(solution)/shard_map/ppermute | solution.py:32
  61.4 2.5 %collective-permute-start.14 = (bf16[4,8192]{1,0:T(4,128)(2,1)S(1)}, bf16[4,8192]{1,0:T(4,128)(2,1)S(1)}, u32[]{:S(2)}, u32[]{:S(2)}) collective-permute-start(bf16[4,8192]{1,0:T(4,128)(2,1)S(1)} %fold.3.refs_0_), channel_id=1, source_target_pairs={{0,4},{1,5},{2,6},{3,7},{4,0},{5,1},{6,2},{7,3},{8,12},{9,13},{10,... | collective-permute-start | bytes 196616 | tf_op jit(solution)/shard_map/ppermute | solution.py:32
  63.9 2.0 %collective-permute-done.16.refs_3_ = bf16[4,8192]{1,0:T(4,128)(2,1)S(1)} collective-permute-done((bf16[4,8192]{1,0:T(4,128)(2,1)S(1)}, bf16[4,8192]{1,0:T(4,128)(2,1)S(1)}, u32[]{:S(2)}, u32[]{:S(2)}) %collective-permute-start.16) | collective-permute-done | bytes 65568 | tf_op jit(solution)/shard_map/ppermute | solution.py:32
  65.8 1.3 %collective-permute-done.15.refs_2_ = bf16[4,8192]{1,0:T(4,128)(2,1)S(1)} collective-permute-done((bf16[4,8192]{1,0:T(4,128)(2,1)S(1)}, bf16[4,8192]{1,0:T(4,128)(2,1)S(1)}, u32[]{:S(2)}, u32[]{:S(2)}) %collective-permute-start.15) | collective-permute-done | bytes 65568 | tf_op jit(solution)/shard_map/ppermute | solution.py:32
  68.4 1.2 %collective-permute-start.17 = (bf16[4,8192]{1,0:T(4,128)(2,1)S(1)}, bf16[4,8192]{1,0:T(4,128)(2,1)S(1)}, u32[]{:S(2)}, u32[]{:S(2)}) collective-permute-start(bf16[4,8192]{1,0:T(4,128)(2,1)S(1)} %get-tuple-element.64.refs_0_), channel_id=1, source_target_pairs={{0,1},{1,0},{2,3},{3,2},{4,5},{5,4},{6,7},{7,6},{8,9},{9,8},{10,11... | collective-permute-start | bytes 196616 | tf_op jit(solution)/shard_map/ppermute | solution.py:32
  69.7 1.9 %collective-permute-done.19.refs_3_ = bf16[4,8192]{1,0:T(4,128)(2,1)S(1)} collective-permute-done((bf16[4,8192]{1,0:T(4,128)(2,1)S(1)}, bf16[4,8192]{1,0:T(4,128)(2,1)S(1)}, u32[]{:S(2)}, u32[]{:S(2)}) %collective-permute-start.19) | collective-permute-done | bytes 65568 | tf_op jit(solution)/shard_map/ppermute | solution.py:32
  71.6 1.2 %collective-permute-done.18.refs_2_ = bf16[4,8192]{1,0:T(4,128)(2,1)S(1)} collective-permute-done((bf16[4,8192]{1,0:T(4,128)(2,1)S(1)}, bf16[4,8192]{1,0:T(4,128)(2,1)S(1)}, u32[]{:S(2)}, u32[]{:S(2)}) %collective-permute-start.18) | collective-permute-done | bytes 65568 | tf_op jit(solution)/shard_map/ppermute | solution.py:32
  73.6 1.6 %collective-permute-start.22 = (bf16[16,64]{1,0:T(8,128)(2,1)S(1)}, bf16[16,64]{1,0:T(8,128)(2,1)S(1)}, u32[]{:S(2)}, u32[]{:S(2)}) collective-permute-start(bf16[16,64]{1,0:T(8,128)(2,1)S(1)} %get-tuple-element.66.refs_0_), channel_id=1, source_target_pairs={{0,12},{1,13},{2,14},{3,15},{4,8},{5,9},{6,10},{7,11},{8,4},{9,5},... | collective-permute-start | bytes 6152 | tf_op jit(solution)/shard_map/ppermute | solution.py:32
  75.1 0.9 collective-permute-start.21
  76.1 1.9 %collective-permute-start.20 = (bf16[16,64]{1,0:T(8,128)(2,1)S(1)}, bf16[16,64]{1,0:T(8,128)(2,1)S(1)}, u32[]{:S(2)}, u32[]{:S(2)}) collective-permute-start(bf16[16,64]{1,0:T(8,128)(2,1)S(1)} %get-tuple-element.66.refs_0_), channel_id=1, source_target_pairs={{0,4},{1,5},{2,6},{3,7},{4,0},{5,1},{6,2},{7,3},{8,12},{9,13},{10,... | collective-permute-start | bytes 6152 | tf_op jit(solution)/shard_map/ppermute | solution.py:32
  78.0 1.0 collective-permute-done.22.refs_3_
  79.8 1.4 %collective-permute-start.24 = (bf16[16,64]{1,0:T(8,128)(2,1)S(1)}, bf16[16,64]{1,0:T(8,128)(2,1)S(1)}, u32[]{:S(2)}, u32[]{:S(2)}) collective-permute-start(bf16[16,64]{1,0:T(8,128)(2,1)S(1)} %sum.3.refs_0_), channel_id=1, source_target_pairs={{0,2},{1,3},{2,0},{3,1},{4,6},{5,7},{6,4},{7,5},{8,10},{9,11},{10,... | collective-permute-start | bytes 6152 | tf_op jit(solution)/shard_map/ppermute | solution.py:32
  81.6 1.5 %project.3 = (f32[16,512]{1,0:T(8,128)S(1)}, f32[16,128]{1,0:T(8,128)S(1)}) custom-call(bf16[16,8192]{1,0:T(8,128)(2,1)S(1)} %get-tuple-element.67.rows_ref, bf16[8192,512]{1,0:T(8,128)(2,1)S(1)} %get-tuple-element.49.query_w, bf16[8192,128]{1,0:T(8,128)(2,1)S(1)} %get-tuple-element.50.fresh_w), custom_call_target="tpu_custom_call" | custom-call | flops 167772160 | bytes 10485760 | tf_op jit(solution)/shard_map/project/pallas_call | solution.py:53
  83.9 10.8 %all_to_all.27.refs_0_ = bf16[16,8,128]{2,1,0:T(8,128)(2,1)S(1)} all-to-all(bf16[16,8,128]{2,1,0:T(8,128)(2,1)S(1)} %up.3), channel_id=1, replica_groups=mesh['groups'=2,'replica'=16] {'replica'}, dimensions={0} | all-to-all | bytes 65536 | tf_op jit(solution)/shard_map/all_to_all | solution.py:40
  95.6 9.1 %all_to_all.28.lines_ref = bf16[16,4,128]{2,1,0:T(4,128)(2,1)S(1)} all-to-all(bf16[16,4,128]{2,1,0:T(4,128)(2,1)S(1)} %attend.3), channel_id=1, replica_groups=mesh['groups'=2,'replica'=16] {'replica'}, dimensions={0} | all-to-all | bytes 32768 | tf_op jit(solution)/shard_map/all_to_all | solution.py:40
  104.6 1.3 %output.3 = (f32[8,8192]{1,0:T(8,128)S(1)}, bf16[8,8192]{1,0:T(8,128)(2,1)S(1)}) custom-call(bf16[16,4,128]{2,1,0:T(4,128)(2,1)S(1)} %all_to_all.28.lines_ref, s32[1]{0:T(128)} %bitcast._.refs_4_.me_ref, bf16[512,8192]{1,0:T(8,128)(2,1)S(1)} %get-tuple-element.57.weight_ref), custom_call_target="tpu_custom_call" | custom-call | flops 134217728 | bytes 8388608 | tf_op jit(solution)/shard_map/output/pallas_call | solution.py:53
  106.0 1.4 %collective-permute-done.26.other_ref = bf16[8,8192]{1,0:T(8,128)(2,1)S(1)} collective-permute-done((bf16[8,8192]{1,0:T(8,128)(2,1)S(1)}, bf16[8,8192]{1,0:T(8,128)(2,1)S(1)}, u32[]{:S(2)}, u32[]{:S(2)}) %collective-permute-start.26) | collective-permute-done | bytes 131104 | tf_op jit(solution)/shard_map/ppermute | solution.py:32
  107.5 10.0 %all_to_all.29.parts_ref = bf16[8,8,1024]{2,1,0:T(8,128)(2,1)S(1)} all-to-all(bf16[8,8,1024]{2,1,0:T(8,128)(2,1)S(1)} %partial.1), channel_id=1, replica_groups={{0,2,4,6,8,10,12,14},{1,3,5,7,9,11,13,15},{16,18,20,22,24,26,28,30},{17..., dimensions={0} | all-to-all | bytes 262144 | tf_op jit(solution)/shard_map/all_to_all | solution.py:45
  (55 shorter events, 14.1 us)
Async XLA Ops:
  1.3 0.8 copy-start
  2.1 9.8 %collective-permute-start.2 = (bf16[1,8320]{1,0:T(2,128)(2,1)S(1)}, bf16[1,8320]{1,0:T(2,128)(2,1)S(1)}, u32[]{:S(2)}, u32[]{:S(2)}) collective-permute-start(bf16[1,8320]{1,0:T(2,128)(2,1)S(1)} %get-tuple-element.40.refs_0_), channel_id=1, source_target_pairs={{0,12},{1,13},{2,14},{3,15},{4,8},{5,9},{6,10},{7,11},{8,4},{9,5},... | collective-permute-start | bytes 49928 | tf_op jit(solution)/shard_map/ppermute | solution.py:32
  7.2 4.8 %collective-permute-start.1 = (bf16[1,8320]{1,0:T(2,128)(2,1)S(1)}, bf16[1,8320]{1,0:T(2,128)(2,1)S(1)}, u32[]{:S(2)}, u32[]{:S(2)}) collective-permute-start(bf16[1,8320]{1,0:T(2,128)(2,1)S(1)} %get-tuple-element.40.refs_0_), channel_id=1, source_target_pairs={{0,8},{1,9},{2,10},{3,11},{4,12},{5,13},{6,14},{7,15},{8,0},{9,1},... | collective-permute-start | bytes 49928 | tf_op jit(solution)/shard_map/ppermute | solution.py:32
  7.2 4.8 %collective-permute-start = (bf16[1,8320]{1,0:T(2,128)(2,1)S(1)}, bf16[1,8320]{1,0:T(2,128)(2,1)S(1)}, u32[]{:S(2)}, u32[]{:S(2)}) collective-permute-start(bf16[1,8320]{1,0:T(2,128)(2,1)S(1)} %get-tuple-element.40.refs_0_), channel_id=1, source_target_pairs={{0,4},{1,5},{2,6},{3,7},{4,0},{5,1},{6,2},{7,3},{8,12},{9,13},{10,... | collective-permute-start | bytes 49928 | tf_op jit(solution)/shard_map/ppermute | solution.py:32
  7.8 4.2 %copy-start.1 = (bf16[8192]{0:T(1024)(128)(2,1)S(1)}, bf16[8192]{0:T(1024)(128)(2,1)}, u32[]{:S(2)}) copy-start(bf16[8192]{0:T(1024)(128)(2,1)} %param.12) | copy-start | bytes 49156
  12.3 5.9 %copy-start.2 = (s32[32]{0:T(128)S(1)}, s32[32]{0:T(128)}, u32[]{:S(2)}) copy-start(s32[32]{0:T(128)} %param.19) | copy-start | bytes 388
  12.3 5.3 %collective-permute-start.5 = (bf16[4,8320]{1,0:T(4,128)(2,1)S(1)}, bf16[4,8320]{1,0:T(4,128)(2,1)S(1)}, u32[]{:S(2)}, u32[]{:S(2)}) collective-permute-start(bf16[4,8320]{1,0:T(4,128)(2,1)S(1)} %get-tuple-element.43.refs_0_), channel_id=1, source_target_pairs={{0,3},{1,2},{2,1},{3,0},{4,7},{5,6},{6,5},{7,4},{8,11},{9,10},{10,... | collective-permute-start | bytes 199688 | tf_op jit(solution)/shard_map/ppermute | solution.py:32
  12.7 5.6 %collective-permute-start.4 = (bf16[4,8320]{1,0:T(4,128)(2,1)S(1)}, bf16[4,8320]{1,0:T(4,128)(2,1)S(1)}, u32[]{:S(2)}, u32[]{:S(2)}) collective-permute-start(bf16[4,8320]{1,0:T(4,128)(2,1)S(1)} %get-tuple-element.43.refs_0_), channel_id=1, source_target_pairs={{0,2},{1,3},{2,0},{3,1},{4,6},{5,7},{6,4},{7,5},{8,10},{9,11},{10,... | collective-permute-start | bytes 199688 | tf_op jit(solution)/shard_map/ppermute | solution.py:32
  14.0 4.3 %collective-permute-start.3 = (bf16[4,8320]{1,0:T(4,128)(2,1)S(1)}, bf16[4,8320]{1,0:T(4,128)(2,1)S(1)}, u32[]{:S(2)}, u32[]{:S(2)}) collective-permute-start(bf16[4,8320]{1,0:T(4,128)(2,1)S(1)} %get-tuple-element.43.refs_0_), channel_id=1, source_target_pairs={{0,1},{1,0},{2,3},{3,2},{4,5},{5,4},{6,7},{7,6},{8,9},{9,8},{10,11... | collective-permute-start | bytes 199688 | tf_op jit(solution)/shard_map/ppermute | solution.py:32
  19.0 7.3 %collective-permute-start.8 = (bf16[16,64]{1,0:T(8,128)(2,1)S(1)}, bf16[16,64]{1,0:T(8,128)(2,1)S(1)}, u32[]{:S(2)}, u32[]{:S(2)}) collective-permute-start(bf16[16,64]{1,0:T(8,128)(2,1)S(1)} %get-tuple-element.46.refs_3_.refs_0_), channel_id=1, source_target_pairs={{0,12},{1,13},{2,14},{3,15},{4,8},{5,9},{6,10},{7,11},{8,4},{9,5},... | collective-permute-start | bytes 6152 | tf_op jit(solution)/shard_map/ppermute | solution.py:32
  22.7 4.5 %collective-permute-start.7 = (bf16[16,64]{1,0:T(8,128)(2,1)S(1)}, bf16[16,64]{1,0:T(8,128)(2,1)S(1)}, u32[]{:S(2)}, u32[]{:S(2)}) collective-permute-start(bf16[16,64]{1,0:T(8,128)(2,1)S(1)} %get-tuple-element.46.refs_3_.refs_0_), channel_id=1, source_target_pairs={{0,8},{1,9},{2,10},{3,11},{4,12},{5,13},{6,14},{7,15},{8,0},{9,1},... | collective-permute-start | bytes 6152 | tf_op jit(solution)/shard_map/ppermute | solution.py:32
  22.7 4.5 %collective-permute-start.6 = (bf16[16,64]{1,0:T(8,128)(2,1)S(1)}, bf16[16,64]{1,0:T(8,128)(2,1)S(1)}, u32[]{:S(2)}, u32[]{:S(2)}) collective-permute-start(bf16[16,64]{1,0:T(8,128)(2,1)S(1)} %get-tuple-element.46.refs_3_.refs_0_), channel_id=1, source_target_pairs={{0,4},{1,5},{2,6},{3,7},{4,0},{5,1},{6,2},{7,3},{8,12},{9,13},{10,... | collective-permute-start | bytes 6152 | tf_op jit(solution)/shard_map/ppermute | solution.py:32
  27.2 3.4 %collective-permute-start.11 = (bf16[16,64]{1,0:T(8,128)(2,1)S(1)}, bf16[16,64]{1,0:T(8,128)(2,1)S(1)}, u32[]{:S(2)}, u32[]{:S(2)}) collective-permute-start(bf16[16,64]{1,0:T(8,128)(2,1)S(1)} %sum.2.refs_0_), channel_id=1, source_target_pairs={{0,3},{1,2},{2,1},{3,0},{4,7},{5,6},{6,5},{7,4},{8,11},{9,10},{10,... | collective-permute-start | bytes 6152 | tf_op jit(solution)/shard_map/ppermute | solution.py:32
  27.3 3.7 %collective-permute-start.10 = (bf16[16,64]{1,0:T(8,128)(2,1)S(1)}, bf16[16,64]{1,0:T(8,128)(2,1)S(1)}, u32[]{:S(2)}, u32[]{:S(2)}) collective-permute-start(bf16[16,64]{1,0:T(8,128)(2,1)S(1)} %sum.2.refs_0_), channel_id=1, source_target_pairs={{0,2},{1,3},{2,0},{3,1},{4,6},{5,7},{6,4},{7,5},{8,10},{9,11},{10,... | collective-permute-start | bytes 6152 | tf_op jit(solution)/shard_map/ppermute | solution.py:32
  28.3 2.7 %collective-permute-start.9 = (bf16[16,64]{1,0:T(8,128)(2,1)S(1)}, bf16[16,64]{1,0:T(8,128)(2,1)S(1)}, u32[]{:S(2)}, u32[]{:S(2)}) collective-permute-start(bf16[16,64]{1,0:T(8,128)(2,1)S(1)} %sum.2.refs_0_), channel_id=1, source_target_pairs={{0,1},{1,0},{2,3},{3,2},{4,5},{5,4},{6,7},{7,6},{8,9},{9,8},{10,11... | collective-permute-start | bytes 6152 | tf_op jit(solution)/shard_map/ppermute | solution.py:32
  53.6 1.4 %collective-permute-start.12 = (bf16[8,8192]{1,0:T(8,128)(2,1)S(1)}, bf16[8,8192]{1,0:T(8,128)(2,1)S(1)}, u32[]{:S(2)}, u32[]{:S(2)}) collective-permute-start(bf16[8,8192]{1,0:T(8,128)(2,1)S(1)} %get-tuple-element.59), channel_id=1, source_target_pairs={{0,1},{1,0},{2,3},{3,2},{4,5},{5,4},{6,7},{7,6},{8,9},{9,8},{10,11... | collective-permute-start | bytes 393224 | tf_op jit(solution)/shard_map/ppermute | solution.py:32
  55.0 4.3 %collective-permute-start.13 = (bf16[4,8192]{1,0:T(4,128)(2,1)S(1)}, bf16[4,8192]{1,0:T(4,128)(2,1)S(1)}, u32[]{:S(2)}, u32[]{:S(2)}) collective-permute-start(bf16[4,8192]{1,0:T(4,128)(2,1)S(1)} %get-tuple-element.61), channel_id=1, source_target_pairs={{0,2},{1,3},{2,0},{3,1},{4,6},{5,7},{6,4},{7,5},{8,10},{9,11},{10,... | collective-permute-start | bytes 196616 | tf_op jit(solution)/shard_map/ppermute | solution.py:32
  59.4 6.4 %collective-permute-start.16 = (bf16[4,8192]{1,0:T(4,128)(2,1)S(1)}, bf16[4,8192]{1,0:T(4,128)(2,1)S(1)}, u32[]{:S(2)}, u32[]{:S(2)}) collective-permute-start(bf16[4,8192]{1,0:T(4,128)(2,1)S(1)} %fold.3.refs_0_), channel_id=1, source_target_pairs={{0,12},{1,13},{2,14},{3,15},{4,8},{5,9},{6,10},{7,11},{8,4},{9,5},... | collective-permute-start | bytes 196616 | tf_op jit(solution)/shard_map/ppermute | solution.py:32
  60.0 7.1 %collective-permute-start.15 = (bf16[4,8192]{1,0:T(4,128)(2,1)S(1)}, bf16[4,8192]{1,0:T(4,128)(2,1)S(1)}, u32[]{:S(2)}, u32[]{:S(2)}) collective-permute-start(bf16[4,8192]{1,0:T(4,128)(2,1)S(1)} %fold.3.refs_0_), channel_id=1, source_target_pairs={{0,8},{1,9},{2,10},{3,11},{4,12},{5,13},{6,14},{7,15},{8,0},{9,1},... | collective-permute-start | bytes 196616 | tf_op jit(solution)/shard_map/ppermute | solution.py:32
  61.4 5.7 %collective-permute-start.14 = (bf16[4,8192]{1,0:T(4,128)(2,1)S(1)}, bf16[4,8192]{1,0:T(4,128)(2,1)S(1)}, u32[]{:S(2)}, u32[]{:S(2)}) collective-permute-start(bf16[4,8192]{1,0:T(4,128)(2,1)S(1)} %fold.3.refs_0_), channel_id=1, source_target_pairs={{0,4},{1,5},{2,6},{3,7},{4,0},{5,1},{6,2},{7,3},{8,12},{9,13},{10,... | collective-permute-start | bytes 196616 | tf_op jit(solution)/shard_map/ppermute | solution.py:32
  67.7 3.8 %collective-permute-start.19 = (bf16[4,8192]{1,0:T(4,128)(2,1)S(1)}, bf16[4,8192]{1,0:T(4,128)(2,1)S(1)}, u32[]{:S(2)}, u32[]{:S(2)}) collective-permute-start(bf16[4,8192]{1,0:T(4,128)(2,1)S(1)} %get-tuple-element.64.refs_0_), channel_id=1, source_target_pairs={{0,3},{1,2},{2,1},{3,0},{4,7},{5,6},{6,5},{7,4},{8,11},{9,10},{10,... | collective-permute-start | bytes 196616 | tf_op jit(solution)/shard_map/ppermute | solution.py:32
  67.8 5.0 %collective-permute-start.18 = (bf16[4,8192]{1,0:T(4,128)(2,1)S(1)}, bf16[4,8192]{1,0:T(4,128)(2,1)S(1)}, u32[]{:S(2)}, u32[]{:S(2)}) collective-permute-start(bf16[4,8192]{1,0:T(4,128)(2,1)S(1)} %get-tuple-element.64.refs_0_), channel_id=1, source_target_pairs={{0,2},{1,3},{2,0},{3,1},{4,6},{5,7},{6,4},{7,5},{8,10},{9,11},{10,... | collective-permute-start | bytes 196616 | tf_op jit(solution)/shard_map/ppermute | solution.py:32
  68.4 4.4 %collective-permute-start.17 = (bf16[4,8192]{1,0:T(4,128)(2,1)S(1)}, bf16[4,8192]{1,0:T(4,128)(2,1)S(1)}, u32[]{:S(2)}, u32[]{:S(2)}) collective-permute-start(bf16[4,8192]{1,0:T(4,128)(2,1)S(1)} %get-tuple-element.64.refs_0_), channel_id=1, source_target_pairs={{0,1},{1,0},{2,3},{3,2},{4,5},{5,4},{6,7},{7,6},{8,9},{9,8},{10,11... | collective-permute-start | bytes 196616 | tf_op jit(solution)/shard_map/ppermute | solution.py:32
  73.6 5.4 %collective-permute-start.22 = (bf16[16,64]{1,0:T(8,128)(2,1)S(1)}, bf16[16,64]{1,0:T(8,128)(2,1)S(1)}, u32[]{:S(2)}, u32[]{:S(2)}) collective-permute-start(bf16[16,64]{1,0:T(8,128)(2,1)S(1)} %get-tuple-element.66.refs_0_), channel_id=1, source_target_pairs={{0,12},{1,13},{2,14},{3,15},{4,8},{5,9},{6,10},{7,11},{8,4},{9,5},... | collective-permute-start | bytes 6152 | tf_op jit(solution)/shard_map/ppermute | solution.py:32
  75.1 4.5 %collective-permute-start.21 = (bf16[16,64]{1,0:T(8,128)(2,1)S(1)}, bf16[16,64]{1,0:T(8,128)(2,1)S(1)}, u32[]{:S(2)}, u32[]{:S(2)}) collective-permute-start(bf16[16,64]{1,0:T(8,128)(2,1)S(1)} %get-tuple-element.66.refs_0_), channel_id=1, source_target_pairs={{0,8},{1,9},{2,10},{3,11},{4,12},{5,13},{6,14},{7,15},{8,0},{9,1},... | collective-permute-start | bytes 6152 | tf_op jit(solution)/shard_map/ppermute | solution.py:32
  76.1 3.6 %collective-permute-start.20 = (bf16[16,64]{1,0:T(8,128)(2,1)S(1)}, bf16[16,64]{1,0:T(8,128)(2,1)S(1)}, u32[]{:S(2)}, u32[]{:S(2)}) collective-permute-start(bf16[16,64]{1,0:T(8,128)(2,1)S(1)} %get-tuple-element.66.refs_0_), channel_id=1, source_target_pairs={{0,4},{1,5},{2,6},{3,7},{4,0},{5,1},{6,2},{7,3},{8,12},{9,13},{10,... | collective-permute-start | bytes 6152 | tf_op jit(solution)/shard_map/ppermute | solution.py:32
  79.7 3.4 %collective-permute-start.25 = (bf16[16,64]{1,0:T(8,128)(2,1)S(1)}, bf16[16,64]{1,0:T(8,128)(2,1)S(1)}, u32[]{:S(2)}, u32[]{:S(2)}) collective-permute-start(bf16[16,64]{1,0:T(8,128)(2,1)S(1)} %sum.3.refs_0_), channel_id=1, source_target_pairs={{0,3},{1,2},{2,1},{3,0},{4,7},{5,6},{6,5},{7,4},{8,11},{9,10},{10,... | collective-permute-start | bytes 6152 | tf_op jit(solution)/shard_map/ppermute | solution.py:32
  79.8 3.7 %collective-permute-start.24 = (bf16[16,64]{1,0:T(8,128)(2,1)S(1)}, bf16[16,64]{1,0:T(8,128)(2,1)S(1)}, u32[]{:S(2)}, u32[]{:S(2)}) collective-permute-start(bf16[16,64]{1,0:T(8,128)(2,1)S(1)} %sum.3.refs_0_), channel_id=1, source_target_pairs={{0,2},{1,3},{2,0},{3,1},{4,6},{5,7},{6,4},{7,5},{8,10},{9,11},{10,... | collective-permute-start | bytes 6152 | tf_op jit(solution)/shard_map/ppermute | solution.py:32
  81.2 2.3 %collective-permute-start.23 = (bf16[16,64]{1,0:T(8,128)(2,1)S(1)}, bf16[16,64]{1,0:T(8,128)(2,1)S(1)}, u32[]{:S(2)}, u32[]{:S(2)}) collective-permute-start(bf16[16,64]{1,0:T(8,128)(2,1)S(1)} %sum.3.refs_0_), channel_id=1, source_target_pairs={{0,1},{1,0},{2,3},{3,2},{4,5},{5,4},{6,7},{7,6},{8,9},{9,8},{10,11... | collective-permute-start | bytes 6152 | tf_op jit(solution)/shard_map/ppermute | solution.py:32
  106.0 1.4 %collective-permute-start.26 = (bf16[8,8192]{1,0:T(8,128)(2,1)S(1)}, bf16[8,8192]{1,0:T(8,128)(2,1)S(1)}, u32[]{:S(2)}, u32[]{:S(2)}) collective-permute-start(bf16[8,8192]{1,0:T(8,128)(2,1)S(1)} %get-tuple-element.73), channel_id=1, source_target_pairs={{0,1},{1,0},{2,3},{3,2},{4,5},{5,4},{6,7},{7,6},{8,9},{9,8},{10,11... | collective-permute-start | bytes 393224 | tf_op jit(solution)/shard_map/ppermute | solution.py:32
